TPU v7x, 32 devices: a whole 2x2x4 slice. The times are simulated.
32 devices in a mesh: dp: 4 (over y, core), expert: 8 (over z, x).
Axes of the slice: x: 2, y: 2, z: 4, core: 2. Of those that a mesh axis runs over, the one named last changes fastest.
Arguments:
- tokens: bfloat16 [4096, 768], P(('dp', 'expert')), may hold values from -6 to 6
- seg_ids: int32 [32, 128], P(('dp', 'expert')), may hold values from 0 to 3, never falling along the last dimension, each value on 1 to 96 neighbouring positions
- routes: int32 [4096, 1], P(('dp', 'expert')), may hold values from 0 to 15
- attn_gain: bfloat16 [768], replicated, may hold values from 0.099609375 to 1.8984375
- w_query: bfloat16 [768, 768], P('dp', 'expert'), may hold values from -0.21875 to 0.21875
- w_key: bfloat16 [768, 768], P('dp', 'expert'), may hold values from -0.21875 to 0.21875
- w_value: bfloat16 [768, 768], P('dp', 'expert'), may hold values from -0.21875 to 0.21875
- w_output: bfloat16 [768, 768], P('dp', 'expert'), may hold values from -1.25 to 1.25
- rel_bias: bfloat16 [32, 12], replicated, may hold values from -4 to 4
- ffn_gain: bfloat16 [768], replicated, may hold values from 0.099609375 to 1.8984375
- w_router: bfloat16 [768, 16], replicated, may hold values from -0.1796875 to 0.1796875
- w_in: bfloat16 [16, 768, 3072], P('expert', None, 'dp'), may hold values from -0.21875 to 0.21875
- w_out: bfloat16 [16, 3072, 768], P('expert', 'dp'), may hold values from -2.5 to 2.5
- d_out: bfloat16 [4096, 768], P(('dp', 'expert')), may hold values from -6 to 6
Outputs:
- output: bfloat16 [4096, 768], P(('dp', 'expert'))
- d_input: float32 [4096, 768], P(('dp', 'expert'))
- g_attn_gain: float32 [768], replicated
- g_query: float32 [768, 768], P('dp', 'expert')
- g_key: float32 [768, 768], P('dp', 'expert')
- g_value: float32 [768, 768], P('dp', 'expert')
- g_output: float32 [768, 768], P('dp', 'expert')
- g_rel_bias: float32 [32, 12], replicated
- g_ffn_gain: float32 [768], replicated
- g_router: float32 [768, 16], replicated
- g_in: float32 [16, 768, 3072], P('expert', None, 'dp')
- g_out: float32 [16, 3072, 768], P('expert', 'dp')
Inputs may be any that keep to these rules, and one draw needn't show every extreme that they name: `seg_ids`: document numbers of one packed sequence, never falling, each document at most 96 tokens, and one document of every block exactly that long.
All inputs are finite; a program needn't handle non-finite values.
Results may differ from a plain program's by a relative error of at most 0.02.
Values may be sent and summed in bfloat16 or wider, within the bound.
No kernel may reach another device: no remote copies, remote signals or barrier semaphores. Data moves between devices by JAX's collectives and lax.ppermute only.
A program may use at most 128 MiB of HBM per device.

v0:
```python
import jax
import jax.numpy as jnp
from jax import lax
from jax.sharding import PartitionSpec as P

EPSILON = 1e-06
LIMITS = (12, 16, 23, 32, 46, 64, 91)
MASKED = -1000000000.0
HIGHEST = lax.Precision.HIGHEST


def bucket_table(length):
    spots = jnp.arange(length, dtype=jnp.int32)
    delta = spots[None, :] - spots[:, None]
    magnitude = jnp.abs(delta)
    distant = jnp.full_like(magnitude, 8)
    for threshold in LIMITS:
        distant = distant + (magnitude >= threshold).astype(jnp.int32)
    return jnp.where(delta > 0, 16, 0).astype(jnp.int32) + jnp.where(
        magnitude < 8, magnitude, distant
    )


def normalize(matrix, gain_vec):
    scale = lax.rsqrt(jnp.mean(matrix * matrix, axis=-1, keepdims=True) + EPSILON)
    return (matrix * scale * gain_vec, scale)


def norm_back(matrix, scale, gain_vec, incoming):
    weighted = incoming * gain_vec
    average = jnp.mean(matrix * weighted, axis=-1, keepdims=True)
    return (
        scale * weighted - matrix * (scale * scale * scale) * average,
        jnp.sum(incoming * matrix * scale, axis=0),
    )


def contract_rows(left, right, precision=None):
    return lax.dot_general(
        left,
        right,
        (((0,), (0,)), ((), ())),
        precision=precision,
        preferred_element_type=jnp.float32,
    )


def contract_cols(left, right, precision=None):
    return lax.dot_general(
        left,
        right,
        (((1,), (1,)), ((), ())),
        precision=precision,
        preferred_element_type=jnp.float32,
    )


def smooth(values):
    return jax.nn.gelu(values, approximate=True)


def expert_forward(slot_rows, first_w, second_w):
    pre_act = jnp.einsum("secd,edf->secf", slot_rows, first_w, preferred_element_type=jnp.float32)
    activated_f, gelu_back = jax.vjp(smooth, pre_act)
    activated = activated_f.astype(jnp.bfloat16)
    partial_out = jnp.einsum(
        "secf,efd->secd", activated, second_w, preferred_element_type=jnp.float32
    )
    return (activated, gelu_back, partial_out)


def expert_backward(slot_rows, activated, gelu_back, grad_rows, first_w, second_w):
    act_grad = jnp.einsum("secd,efd->secf", grad_rows, second_w, preferred_element_type=jnp.float32)
    pre_grad = gelu_back(act_grad)[0].astype(jnp.bfloat16)
    first_grad = jnp.einsum(
        "secd,secf->edf", slot_rows, pre_grad, preferred_element_type=jnp.float32
    )
    second_grad = jnp.einsum(
        "secf,secd->efd", activated, grad_rows, preferred_element_type=jnp.float32
    )
    input_part = jnp.einsum("secf,edf->secd", pre_grad, first_w, preferred_element_type=jnp.float32)
    return (first_grad, second_grad, input_part)


def per_device(
    tokens,
    seg_ids,
    routes,
    attn_gain,
    w_query,
    w_key,
    w_value,
    w_output,
    rel_bias,
    ffn_gain,
    w_router,
    w_in,
    w_out,
    d_out,
):
    inputs = tokens.astype(jnp.float32)
    length, model_width = inputs.shape
    head_count = rel_bias.shape[1]
    bucket_count = rel_bias.shape[0]
    row_parts = (
        lax.all_gather(w_query, "dp", axis=0, tiled=True),
        lax.all_gather(w_key, "dp", axis=0, tiled=True),
        lax.all_gather(w_value, "dp", axis=0, tiled=True),
        lax.all_gather(w_output, "dp", axis=0, tiled=True),
    )
    query_w, key_w, value_w, output_w = (
        lax.all_gather(row_parts[0], "expert", axis=1, tiled=True),
        lax.all_gather(row_parts[1], "expert", axis=1, tiled=True),
        lax.all_gather(row_parts[2], "expert", axis=1, tiled=True),
        lax.all_gather(row_parts[3], "expert", axis=1, tiled=True),
    )
    inner_width = query_w.shape[1]
    head_size = inner_width // head_count
    factor = head_size ** (-0.5)
    gain_one = attn_gain.astype(jnp.float32)
    normed_one, scale_one = normalize(inputs, gain_one)
    normed_low = normed_one.astype(jnp.bfloat16)
    query_rows = jnp.dot(normed_low, query_w, preferred_element_type=jnp.float32).astype(
        jnp.bfloat16
    )
    key_rows = jnp.dot(normed_low, key_w, preferred_element_type=jnp.float32).astype(jnp.bfloat16)
    value_rows = jnp.dot(normed_low, value_w, preferred_element_type=jnp.float32).astype(
        jnp.bfloat16
    )
    query_heads = query_rows.reshape(length, head_count, head_size)
    key_heads = key_rows.reshape(length, head_count, head_size)
    value_heads = value_rows.reshape(length, head_count, head_size)
    bucket_ids = bucket_table(length)
    onehot_buckets = (
        bucket_ids[:, :, None] == jnp.arange(bucket_count, dtype=jnp.int32)[None, None, :]
    ).astype(jnp.bfloat16)
    bias_full = jnp.einsum(
        "ijb,bh->hij", onehot_buckets, rel_bias, preferred_element_type=jnp.float32
    )
    segment_row = seg_ids[0]
    same_doc = (segment_row[:, None] == segment_row[None, :])[None, :, :]
    scores = (
        jnp.einsum("ihd,jhd->hij", query_heads, key_heads, preferred_element_type=jnp.float32)
        * factor
        + bias_full
    )
    weights = jax.nn.softmax(jnp.where(same_doc, scores, MASKED), axis=-1)
    weights_low = weights.astype(jnp.bfloat16)
    attended = jnp.einsum(
        "hij,jhd->ihd", weights_low, value_heads, preferred_element_type=jnp.float32
    )
    attended = attended.reshape(length, inner_width).astype(jnp.bfloat16)
    hidden = inputs + jnp.dot(attended, output_w, preferred_element_type=jnp.float32)
    gain_two = ffn_gain.astype(jnp.float32)
    normed_two, scale_two = normalize(hidden, gain_two)
    router_w = w_router.astype(jnp.float32)
    experts_total = router_w.shape[1]
    chance = jax.nn.softmax(jnp.dot(normed_two, router_w, precision=HIGHEST), axis=-1)
    route_hits = (routes == jnp.arange(experts_total, dtype=jnp.int32)[None, :]).astype(jnp.int32)
    placed = jnp.sum(jnp.cumsum(route_hits, axis=0) * route_hits, axis=1) - 1
    capacity = length * 5 // (4 * experts_total)
    slot_total = experts_total * capacity
    slot_index = jnp.where(placed < capacity, routes[:, 0] * capacity + placed, slot_total)
    slot_mask = (slot_index[:, None] == jnp.arange(slot_total, dtype=jnp.int32)[None, :]).astype(
        jnp.bfloat16
    )
    hits_float = route_hits.astype(jnp.float32)
    gate_value = jnp.sum(chance * hits_float, axis=1)
    local_experts = w_in.shape[0]
    expert_ranks = lax.axis_size("expert")
    outgoing = contract_rows(slot_mask, normed_two.astype(jnp.bfloat16)).astype(jnp.bfloat16)
    outgoing = outgoing.reshape(expert_ranks, local_experts * capacity, model_width)
    arrived = lax.all_to_all(outgoing, "expert", split_axis=0, concat_axis=0, tiled=True)
    dp_ranks = lax.axis_size("dp")
    gathered = lax.all_gather(arrived, "dp", axis=0, tiled=True)
    slot_rows = gathered.reshape(dp_ranks * expert_ranks, local_experts, capacity, model_width)
    activated, gelu_back, partial_out = expert_forward(slot_rows, w_in, w_out)
    partial_out = partial_out.reshape(
        dp_ranks * expert_ranks, local_experts * capacity, model_width
    )
    returned = lax.psum_scatter(
        partial_out.astype(jnp.bfloat16), "dp", scatter_dimension=0, tiled=True
    )
    back_rows = lax.all_to_all(returned, "expert", split_axis=0, concat_axis=0, tiled=True)
    fetched = jnp.dot(
        slot_mask, back_rows.reshape(slot_total, model_width), preferred_element_type=jnp.float32
    )
    output = (hidden + gate_value[:, None] * fetched).astype(jnp.bfloat16)
    upstream = d_out.astype(jnp.float32)
    gate_grad = jnp.sum(upstream * fetched, axis=1)
    logit_grad = chance * (hits_float - gate_value[:, None]) * gate_grad[:, None]
    router_grad = contract_rows(normed_two, logit_grad, HIGHEST)
    slot_grad_tok = (gate_value[:, None] * upstream).astype(jnp.bfloat16)
    outgoing_grad = contract_rows(slot_mask, slot_grad_tok).astype(jnp.bfloat16)
    outgoing_grad = outgoing_grad.reshape(expert_ranks, local_experts * capacity, model_width)
    arrived_grad = lax.all_to_all(outgoing_grad, "expert", split_axis=0, concat_axis=0, tiled=True)
    grad_rows = lax.all_gather(arrived_grad, "dp", axis=0, tiled=True)
    grad_rows = grad_rows.reshape(dp_ranks * expert_ranks, local_experts, capacity, model_width)
    kept_rows = lax.all_gather(arrived, "dp", axis=0, tiled=True)
    kept_rows = kept_rows.reshape(dp_ranks * expert_ranks, local_experts, capacity, model_width)
    first_grad, second_grad, input_part = expert_backward(
        kept_rows, activated, gelu_back, grad_rows, w_in, w_out
    )
    input_part = input_part.reshape(dp_ranks * expert_ranks, local_experts * capacity, model_width)
    input_grad = lax.psum_scatter(
        input_part.astype(jnp.bfloat16), "dp", scatter_dimension=0, tiled=True
    )
    dispatch_back = lax.all_to_all(input_grad, "expert", split_axis=0, concat_axis=0, tiled=True)
    normed_two_grad = contract_cols(logit_grad, router_w, HIGHEST)
    normed_two_grad = normed_two_grad + jnp.dot(
        slot_mask,
        dispatch_back.reshape(slot_total, model_width),
        preferred_element_type=jnp.float32,
    )
    hidden_part, ffn_gain_grad = norm_back(hidden, scale_two, gain_two, normed_two_grad)
    hidden_grad = upstream + hidden_part
    branch_grad = hidden_grad.astype(jnp.bfloat16)
    output_grad = contract_rows(attended, branch_grad)
    attended_grad = (
        contract_cols(branch_grad, output_w)
        .astype(jnp.bfloat16)
        .reshape(length, head_count, head_size)
    )
    value_grad = jnp.einsum(
        "hij,ihd->jhd", weights_low, attended_grad, preferred_element_type=jnp.float32
    )
    value_grad = value_grad.reshape(length, inner_width).astype(jnp.bfloat16)
    prob_grad = jnp.einsum(
        "ihd,jhd->hij", attended_grad, value_heads, preferred_element_type=jnp.float32
    )
    score_grad = (
        weights * (prob_grad - jnp.sum(prob_grad * weights, axis=-1, keepdims=True))
    ).astype(jnp.bfloat16)
    query_grad = (
        jnp.einsum("hij,jhd->ihd", score_grad, key_heads, preferred_element_type=jnp.float32)
        * factor
    )
    query_grad = query_grad.reshape(length, inner_width).astype(jnp.bfloat16)
    key_grad = (
        jnp.einsum("hij,ihd->jhd", score_grad, query_heads, preferred_element_type=jnp.float32)
        * factor
    )
    key_grad = key_grad.reshape(length, inner_width).astype(jnp.bfloat16)
    bias_grad = jnp.einsum(
        "hij,ijb->bh", score_grad, onehot_buckets, preferred_element_type=jnp.float32
    )
    query_w_grad = contract_rows(normed_low, query_grad)
    key_w_grad = contract_rows(normed_low, key_grad)
    value_w_grad = contract_rows(normed_low, value_grad)
    normed_one_grad = (
        contract_cols(query_grad, query_w)
        + contract_cols(key_grad, key_w)
        + contract_cols(value_grad, value_w)
    )
    input_norm_grad, attn_gain_grad = norm_back(inputs, scale_one, gain_one, normed_one_grad)
    d_input = hidden_grad + input_norm_grad
    column_parts = (
        lax.psum_scatter(
            query_w_grad.astype(jnp.bfloat16), "expert", scatter_dimension=1, tiled=True
        ).astype(jnp.float32),
        lax.psum_scatter(
            key_w_grad.astype(jnp.bfloat16), "expert", scatter_dimension=1, tiled=True
        ).astype(jnp.float32),
        lax.psum_scatter(
            value_w_grad.astype(jnp.bfloat16), "expert", scatter_dimension=1, tiled=True
        ).astype(jnp.float32),
        lax.psum_scatter(
            output_grad.astype(jnp.bfloat16), "expert", scatter_dimension=1, tiled=True
        ).astype(jnp.float32),
    )
    g_query, g_key, g_value, g_output = (
        lax.psum_scatter(
            column_parts[0].astype(jnp.bfloat16), "dp", scatter_dimension=0, tiled=True
        ).astype(jnp.float32),
        lax.psum_scatter(
            column_parts[1].astype(jnp.bfloat16), "dp", scatter_dimension=0, tiled=True
        ).astype(jnp.float32),
        lax.psum_scatter(
            column_parts[2].astype(jnp.bfloat16), "dp", scatter_dimension=0, tiled=True
        ).astype(jnp.float32),
        lax.psum_scatter(
            column_parts[3].astype(jnp.bfloat16), "dp", scatter_dimension=0, tiled=True
        ).astype(jnp.float32),
    )
    g_attn_gain, g_ffn_gain, g_rel_bias, g_router = lax.psum(
        (attn_gain_grad, ffn_gain_grad, bias_grad, router_grad), ("dp", "expert")
    )
    return (
        output,
        d_input,
        g_attn_gain,
        g_query,
        g_key,
        g_value,
        g_output,
        g_rel_bias,
        g_ffn_gain,
        g_router,
        first_grad,
        second_grad,
    )


def solution(mesh):
    return jax.shard_map(
        per_device,
        mesh=mesh,
        in_specs=(
            P(("dp", "expert"), None),
            P(("dp", "expert"), None),
            P(("dp", "expert"), None),
            P(),
            P("dp", "expert"),
            P("dp", "expert"),
            P("dp", "expert"),
            P("dp", "expert"),
            P(),
            P(),
            P(),
            P("expert", None, "dp"),
            P("expert", "dp", None),
            P(("dp", "expert"), None),
        ),
        out_specs=(
            P(("dp", "expert"), None),
            P(("dp", "expert"), None),
            P(),
            P("dp", "expert"),
            P("dp", "expert"),
            P("dp", "expert"),
            P("dp", "expert"),
            P(),
            P(),
            P(),
            P("expert", None, "dp"),
            P("expert", "dp", None),
        ),
        check_vma=False,
    )
```

profile of v0, /device:TPU:0, one launch (start us, length us, event | category | flops | bytes accessed | tf_op | source)
XLA Modules:
  0.0 655.2 jit_solution(4438276847205637439)
XLA Ops:
  7.3 7.2 %all_gather.33 = bf16[768,96]{1,0:T(8,128)(2,1)S(1)} all-gather(bf16[192,96]{1,0:T(8,128)(2,1)} %param.18), channel_id=1, replica_groups=mesh['dp'=4,'expert'=8] {'dp'}, dimensions={0}, use_global_device_ids=true | all-gather | bytes 184320 | tf_op jit(solution)/shard_map/all_gather | solution.py:106
  15.4 5.8 all_gather.35
  22.1 5.8 all_gather.31
  28.8 5.6 all_gather.37
  37.8 2.4 copy.98
  40.3 17.7 %all-gather.7.cloned.1.call-done = bf16[768,768]{0,1:T(8,128)(2,1)} async-done(((bf16[768,96]{0,1:T(8,128)(2,1)}), bf16[768,768]{0,1:T(8,128)(2,1)}) %all-gather.7.cloned.1.call-update) | async-done | bytes 1179664 | tf_op jit(solution)/shard_map/all_gather | solution.py:112
  58.0 1.8 convolution_convert_fusion.10
  60.0 40.0 %all-gather.9.cloned.1.call-done = bf16[768,768]{0,1:T(8,128)(2,1)} async-done(((bf16[768,96]{0,1:T(8,128)(2,1)}), bf16[768,768]{0,1:T(8,128)(2,1)}) %all-gather.9.cloned.1.call-update) | async-done | bytes 1179664 | tf_op jit(solution)/shard_map/all_gather | solution.py:113
  100.0 1.8 convolution_convert_fusion.9
  102.0 40.6 %all-gather.5.cloned.1.call-done = bf16[768,768]{0,1:T(8,128)(2,1)} async-done(((bf16[768,96]{0,1:T(8,128)(2,1)}), bf16[768,768]{0,1:T(8,128)(2,1)}) %all-gather.5.cloned.1.call-update) | async-done | bytes 1179664 | tf_op jit(solution)/shard_map/all_gather | solution.py:114
  142.6 1.8 convolution_convert_fusion.11
  148.2 1.8 convolution_convert_fusion.8
  150.0 34.6 %all-gather.11.cloned.1.call-done = bf16[768,768]{0,1:T(8,128)(2,1)} async-done(((bf16[768,96]{0,1:T(8,128)(2,1)}), bf16[768,768]{0,1:T(8,128)(2,1)}) %all-gather.11.cloned.1.call-update) | async-done | bytes 1179664 | tf_op jit(solution)/shard_map/all_gather | solution.py:115
  184.5 1.9 multiply_reduce_fusion.3
  188.1 3.4 all-to-all-start
  192.1 8.1 %all-to-all-done = bf16[8,20,768]{2,1,0:T(8,128)(2,1)S(1)} async-done(((bf16[8,20,768]{2,1,0:T(8,128)(2,1)}), bf16[8,20,768]{2,1,0:T(8,128)(2,1)S(1)}, u32[]{:S(2)}, u32[]{:S(2)}) %all-to-all-start) | async-done | bytes 245792 | tf_op jit(solution)/shard_map/all_to_all | solution.py:173
  200.2 9.6 %all_gather.39 = bf16[32,20,768]{2,0,1:T(8,128)(2,1)S(1)} all-gather(bf16[8,20,768]{2,0,1:T(8,128)(2,1)S(1)} %copy.103), channel_id=1, replica_groups=mesh['dp'=4,'expert'=8] {'dp'}, dimensions={0}, use_global_device_ids=true | all-gather | bytes 1228800 | tf_op jit(solution)/shard_map/all_gather | solution.py:175
  210.8 2.6 fusion.3
  218.4 14.3 %all_to_all.20 = bf16[8,20,768]{2,1,0:T(8,128)(2,1)S(1)} all-to-all(bf16[8,20,768]{2,1,0:T(8,128)(2,1)S(1)} %reshape.202), channel_id=1, replica_groups=mesh['dp'=4,'expert'=8] {'expert'}, dimensions={0} | all-to-all | bytes 491520 | tf_op jit(solution)/shard_map/all_to_all | solution.py:196
  232.7 12.6 %all_gather.40 = bf16[32,20,768]{2,0,1:T(8,128)(2,1)S(1)} all-gather(bf16[8,20,768]{2,0,1:T(8,128)(2,1)S(1)} %copy.105), channel_id=1, replica_groups=mesh['dp'=4,'expert'=8] {'dp'}, dimensions={0}, use_global_device_ids=true | all-gather | bytes 1228800 | tf_op jit(solution)/shard_map/all_gather | solution.py:197
  245.4 1.8 fusion.17
  250.0 5.4 all-to-all-start.1
  255.4 20.4 %reduce-scatter.21.cloned.1.call-done = bf16[8,20,768]{2,1,0:T(8,128)(2,1)} async-done(((bf16[32,20,768]{2,1,0:T(8,128)(2,1)}), bf16[8,20,768]{2,1,0:T(8,128)(2,1)}) %reduce-scatter.21.cloned.1.call-update) | async-done | bytes 245776 | tf_op jit(solution)/shard_map/reduce_scatter | solution.py:205
  275.7 5.5 all-to-all-start.3
  282.1 1.9 fusion.39
  285.6 5.4 all-to-all-done.3
  291.0 1.7 reshape.204
  292.7 2.0 multiply_reduce_fusion.1
  294.7 1.9 convert_add_fusion
  300.6 1.9 convolution_convert_fusion.6
  302.5 2.2 convolution_convert_fusion
  304.8 1.7 multiply_reduce_fusion
  311.5 2.2 convolution_convert_fusion.2
  313.8 5.5 convolution_bitcast_fusion
  319.3 41.2 %reduce-scatter.29.cloned.1.call-done = bf16[768,96]{0,1:T(8,128)(2,1)} async-done(((bf16[768,768]{0,1:T(8,128)(2,1)}), bf16[768,96]{0,1:T(8,128)(2,1)}) %reduce-scatter.29.cloned.1.call-update) | async-done | bytes 147472 | tf_op jit(solution)/shard_map/reduce_scatter | solution.py:267
  360.5 1.7 copy.130
  362.3 5.2 convolution_bitcast_fusion.1
  368.7 58.3 %reduce-scatter.27.cloned.1.call-done = bf16[768,96]{0,1:T(8,128)(2,1)} async-done(((bf16[768,768]{0,1:T(8,128)(2,1)}), bf16[768,96]{0,1:T(8,128)(2,1)}) %reduce-scatter.27.cloned.1.call-update) | async-done | bytes 147472 | tf_op jit(solution)/shard_map/reduce_scatter | solution.py:264
  426.9 1.7 copy.128
  429.0 1.8 convolution_add_fusion.1
  432.1 61.3 %reduce-scatter.25.cloned.1.call-done = bf16[768,96]{0,1:T(8,128)(2,1)} async-done(((bf16[768,768]{0,1:T(8,128)(2,1)}), bf16[768,96]{0,1:T(8,128)(2,1)}) %reduce-scatter.25.cloned.1.call-update) | async-done | bytes 147472 | tf_op jit(solution)/shard_map/reduce_scatter | solution.py:261
  493.4 1.7 copy.126
  495.2 2.2 copy.111
  497.9 61.7 %reduce-scatter.23.cloned.1.call-done = bf16[768,96]{0,1:T(8,128)(2,1)} async-done(((bf16[768,768]{0,1:T(8,128)(2,1)}), bf16[768,96]{0,1:T(8,128)(2,1)}) %reduce-scatter.23.cloned.1.call-update) | async-done | bytes 147472 | tf_op jit(solution)/shard_map/reduce_scatter | solution.py:258
  559.6 1.7 copy.124
  562.8 41.0 %all-reduce = (f32[768]{0:T(1024)}, f32[32,12]{0,1:T(8,128)}, f32[768]{0:T(1024)}, f32[768,16]{0,1:T(8,128)}) all-reduce(f32[768]{0:T(1024)S(1)} %get-tuple-element.62, f32[32,12]{0,1:T(8,128)S(1)} %fusion.36, f32[768]{0:T(1024)S(1)} %copy-done.34, f32[768,16]{0,1:T(8,128)S(1)} %fusion.50), channel_id=1, replica_groups=mesh['dp'=4,'expert'=8] {'dp','expert'}, use_global_device_ids=true, to_apply=%region_16.17 | all-reduce | flops 14208 | bytes 113664 | tf_op jit(solution)/shard_map/psum | solution.py:285
  608.0 17.0 %reduce-scatter.33.cloned.1.call-done = bf16[192,96]{1,0:T(8,128)(2,1)} async-done(((bf16[768,96]{1,0:T(8,128)(2,1)}), bf16[192,96]{1,0:T(8,128)(2,1)}) %reduce-scatter.33.cloned.1.call-update) | async-done | bytes 36880
  626.6 20.4 %reduce-scatter.31.cloned.1.call-done = bf16[192,96]{1,0:T(8,128)(2,1)} async-done(((bf16[768,96]{1,0:T(8,128)(2,1)}), bf16[192,96]{1,0:T(8,128)(2,1)}) %reduce-scatter.31.cloned.1.call-update) | async-done | bytes 36880
  (202 shorter events, 44.4 us)
Async XLA Ops:
  7.2 206.2 %copy-start = (bf16[2,768,768]{2,1,0:T(8,128)(2,1)S(1)}, bf16[2,768,768]{2,1,0:T(8,128)(2,1)}, u32[]{:S(2)}) copy-start(bf16[2,768,768]{2,1,0:T(8,128)(2,1)} %param.26) | copy-start | bytes 7077892
  7.2 21.6 %copy-start.27 = (bf16[192,96]{1,0:T(8,128)(2,1)S(1)}, bf16[192,96]{1,0:T(8,128)(2,1)}, u32[]{:S(2)}) copy-start(bf16[192,96]{1,0:T(8,128)(2,1)} %param.21) | copy-start | bytes 110596
  7.2 28.1 %copy-start.1 = (bf16[128,768]{1,0:T(8,128)(2,1)S(1)}, bf16[128,768]{1,0:T(8,128)(2,1)}, u32[]{:S(2)}) copy-start(bf16[128,768]{1,0:T(8,128)(2,1)} %param.14) | copy-start | bytes 589828
  7.2 28.7 %copy-start.41 = (s32[128,1]{0,1:T(1,128)S(1)}, s32[128,1]{0,1:T(1,128)}, u32[]{:S(2)}) copy-start(s32[128,1]{0,1:T(1,128)} %param.16) | copy-start | bytes 1540
  7.2 29.1 %copy-start.49 = (bf16[32,12]{0,1:T(8,128)(2,1)S(1)}, bf16[32,12]{0,1:T(8,128)(2,1)}, u32[]{:S(2)}) copy-start(bf16[32,12]{0,1:T(8,128)(2,1)} %param.22) | copy-start | bytes 2308
  7.2 50.8 %all-gather.7.cloned.1.call-start = ((), (), s32[]{:S(2)}) async-start(), calls=%async_computation.15 | async-start | bytes 1327104 | tf_op jit(solution)/shard_map/all_gather | solution.py:112
  15.3 22.4 %copy-start.50 = (bf16[768]{0:T(1024)(128)(2,1)S(1)}, bf16[768]{0:T(1024)(128)(2,1)}, u32[]{:S(2)}) copy-start(bf16[768]{0:T(1024)(128)(2,1)} %param.17) | copy-start | bytes 4612
  15.3 22.4 %copy-start.51 = (bf16[768]{0:T(1024)(128)(2,1)S(1)}, bf16[768]{0:T(1024)(128)(2,1)}, u32[]{:S(2)}) copy-start(bf16[768]{0:T(1024)(128)(2,1)} %param.23) | copy-start | bytes 4612
  15.3 84.7 %all-gather.9.cloned.1.call-start = ((), (), s32[]{:S(2)}) async-start(), calls=%async_computation.16 | async-start | bytes 1327104 | tf_op jit(solution)/shard_map/all_gather | solution.py:113
  22.0 120.6 %all-gather.5.cloned.1.call-start = ((), (), s32[]{:S(2)}) async-start(), calls=%async_computation.14 | async-start | bytes 1327104 | tf_op jit(solution)/shard_map/all_gather | solution.py:114
  28.7 155.8 %all-gather.11.cloned.1.call-start = ((), (), s32[]{:S(2)}) async-start(), calls=%async_computation.17 | async-start | bytes 1327104 | tf_op jit(solution)/shard_map/all_gather | solution.py:115
  35.3 22.7 %copy-start.23 = (s32[128,128]{1,0:T(8,128)}, s32[128,128]{1,0:T(8,128)S(1)}, u32[]{:S(2)}) copy-start(s32[128,128]{1,0:T(8,128)S(1)} %fusion.67) | copy-start | bytes 196612
  36.0 106.7 %copy-start.30 = (f32[128]{0:T(128)}, f32[128]{0:T(128)S(1)}, u32[]{:S(2)}) copy-start(f32[128]{0:T(128)S(1)} %get-tuple-element.71) | copy-start | bytes 1540
  40.2 146.8 %copy-start.43 = (s32[128]{0:T(128)}, s32[128]{0:T(128)S(1)}, u32[]{:S(2)}) copy-start(s32[128]{0:T(128)S(1)} %fusion.92) | copy-start | bytes 1540
  60.0 84.7 %copy-start.15 = (bf16[128,768]{0,1:T(8,128)(2,1)}, bf16[128,768]{0,1:T(8,128)(2,1)S(1)}, u32[]{:S(2)}) copy-start(bf16[128,768]{0,1:T(8,128)(2,1)S(1)} %copy.95) | copy-start | bytes 589828
  102.0 44.2 %copy-start.14 = (bf16[128,768]{0,1:T(8,128)(2,1)}, bf16[128,768]{0,1:T(8,128)(2,1)S(1)}, u32[]{:S(2)}) copy-start(bf16[128,768]{0,1:T(8,128)(2,1)S(1)} %copy.97) | copy-start | bytes 589828
  148.2 38.3 %copy-start.28 = (f32[12,128]{1,0:T(8,128)}, f32[12,128]{1,0:T(8,128)S(1)}, u32[]{:S(2)}) copy-start(f32[12,128]{1,0:T(8,128)S(1)} %get-tuple-element.74) | copy-start | bytes 18436
  150.0 37.0 %copy-start.19 = (bf16[12,64,128]{2,1,0:T(8,128)(2,1)}, bf16[12,64,128]{2,1,0:T(8,128)(2,1)S(1)}, u32[]{:S(2)}) copy-start(bf16[12,64,128]{2,1,0:T(8,128)(2,1)S(1)} %convolution_convert_fusion.8) | copy-start | bytes 589828
  150.0 41.6 %copy-start.26 = (bf16[768,16]{0,1:T(8,128)(2,1)S(1)}, bf16[768,16]{0,1:T(8,128)(2,1)}, u32[]{:S(2)}) copy-start(bf16[768,16]{0,1:T(8,128)(2,1)} %param.24) | copy-start | bytes 73732
  187.0 22.9 %copy-start.35 = (f32[128]{0:T(128)}, f32[128]{0:T(128)S(1)}, u32[]{:S(2)}) copy-start(f32[128]{0:T(128)S(1)} %get-tuple-element.73) | copy-start | bytes 1540
  188.1 12.1 %all-to-all-start = ((bf16[8,20,768]{2,1,0:T(8,128)(2,1)}), bf16[8,20,768]{2,1,0:T(8,128)(2,1)S(1)}, u32[]{:S(2)}, u32[]{:S(2)}) async-start(bf16[8,20,768]{2,1,0:T(8,128)(2,1)} %reshape.199), calls=%async_computation | async-start | bytes 589824 | tf_op jit(solution)/shard_map/all_to_all | solution.py:173
  191.5 58.4 %reduce-scatter.19.cloned.1.call-start = ((), (), s32[]{:S(2)}) async-start(), calls=%async_computation.18 | async-start | bytes 1474560 | tf_op jit(solution)/shard_map/reduce_scatter | solution.py:181
  192.0 21.4 %copy-start.39 = (f32[128]{0:T(128)}, f32[128]{0:T(128)S(1)}, u32[]{:S(2)}) copy-start(f32[128]{0:T(128)S(1)} %get-tuple-element.80) | copy-start | bytes 1540
  192.0 21.4 %copy-start.45 = (f32[128]{0:T(128)}, f32[128]{0:T(128)S(1)}, u32[]{:S(2)}) copy-start(f32[128]{0:T(128)S(1)} %fusion.83) | copy-start | bytes 1540
  192.1 24.3 %copy-start.37 = (f32[128]{0:T(128)}, f32[128]{0:T(128)S(1)}, u32[]{:S(2)}) copy-start(f32[128]{0:T(128)S(1)} %multiply_reduce_fusion.4) | copy-start | bytes 1540
  216.3 59.5 %reduce-scatter.21.cloned.1.call-start = ((), (), s32[]{:S(2)}) async-start(), calls=%async_computation.19 | async-start | bytes 1474560 | tf_op jit(solution)/shard_map/reduce_scatter | solution.py:205
  218.4 26.9 %copy-start.10 = (f32[2,32,10,768]{3,1,2,0:T(8,128)S(1)}, f32[2,32,10,768]{3,1,2,0:T(8,128)}, u32[]{:S(2)}) copy-start(f32[2,32,10,768]{3,1,2,0:T(8,128)} %copy-done.9) | copy-start | bytes 5898244
  250.0 25.8 %all-to-all-start.1 = ((bf16[8,20,768]{2,1,0:T(8,128)(2,1)}), bf16[8,20,768]{2,1,0:T(8,128)(2,1)S(1)}, u32[]{:S(2)}, u32[]{:S(2)}) async-start(bf16[8,20,768]{2,1,0:T(8,128)(2,1)} %reduce-scatter.19.cloned.1.call-done), calls=%async_computation.2 | async-start | bytes 589824 | tf_op jit(solution)/shard_map/all_to_all | solution.py:184
  275.7 15.2 %all-to-all-start.3 = ((bf16[8,20,768]{2,1,0:T(8,128)(2,1)}), bf16[8,20,768]{2,1,0:T(8,128)(2,1)}, u32[]{:S(2)}, u32[]{:S(2)}) async-start(bf16[8,20,768]{2,1,0:T(8,128)(2,1)} %reduce-scatter.21.cloned.1.call-done), calls=%async_computation.5 | async-start | bytes 589824 | tf_op jit(solution)/shard_map/all_to_all | solution.py:208
  281.3 79.2 %reduce-scatter.29.cloned.1.call-start = ((), (), s32[]{:S(2)}) async-start(), calls=%async_computation.23 | async-start | bytes 1327104 | tf_op jit(solution)/shard_map/reduce_scatter | solution.py:267
  298.2 128.8 %reduce-scatter.27.cloned.1.call-start = ((), (), s32[]{:S(2)}) async-start(), calls=%async_computation.22 | async-start | bytes 1327104 | tf_op jit(solution)/shard_map/reduce_scatter | solution.py:264
  304.7 188.7 %reduce-scatter.25.cloned.1.call-start = ((), (), s32[]{:S(2)}) async-start(), calls=%async_computation.21 | async-start | bytes 1327104 | tf_op jit(solution)/shard_map/reduce_scatter | solution.py:261
  309.4 250.1 %reduce-scatter.23.cloned.1.call-start = ((), (), s32[]{:S(2)}) async-start(), calls=%async_computation.20 | async-start | bytes 1327104 | tf_op jit(solution)/shard_map/reduce_scatter | solution.py:258
  313.7 291.0 %reduce-scatter.37.cloned.1.call-start = ((), (), s32[]{:S(2)}) async-start(), calls=%async_computation.27 | async-start | bytes 245760
  362.3 244.1 %reduce-scatter.35.cloned.1.call-start = ((), (), s32[]{:S(2)}) async-start(), calls=%async_computation.26 | async-start | bytes 245760
  428.7 196.3 %reduce-scatter.33.cloned.1.call-start = ((), (), s32[]{:S(2)}) async-start(), calls=%async_computation.25 | async-start | bytes 245760
  430.8 66.6 %copy-start.36 = (f32[128]{0:T(128)S(1)}, f32[128]{0:T(128)}, u32[]{:S(2)}) copy-start(f32[128]{0:T(128)} %copy-done.35) | copy-start | bytes 1540
  430.8 66.6 %copy-start.38 = (f32[128]{0:T(128)S(1)}, f32[128]{0:T(128)}, u32[]{:S(2)}) copy-start(f32[128]{0:T(128)} %copy-done.37) | copy-start | bytes 1540
  430.8 66.6 %copy-start.40 = (f32[128]{0:T(128)S(1)}, f32[128]{0:T(128)}, u32[]{:S(2)}) copy-start(f32[128]{0:T(128)} %copy-done.39) | copy-start | bytes 1540
  430.8 66.6 %copy-start.42 = (s32[128,1]{0,1:T(1,128)S(1)}, s32[128,1]{0,1:T(1,128)}, u32[]{:S(2)}) copy-start(s32[128,1]{0,1:T(1,128)} %param.16) | copy-start | bytes 1540
  430.9 66.6 %copy-start.46 = (f32[128]{0:T(128)S(1)}, f32[128]{0:T(128)}, u32[]{:S(2)}) copy-start(f32[128]{0:T(128)} %copy-done.45) | copy-start | bytes 1540
  430.9 66.6 %copy-start.48 = (f32[128]{0:T(128)S(1)}, f32[128]{0:T(128)}, u32[]{:S(2)}) copy-start(f32[128]{0:T(128)} %copy-done.47) | copy-start | bytes 1540
  430.9 130.4 %copy-start.24 = (s32[128,128]{1,0:T(8,128)S(1)}, s32[128,128]{1,0:T(8,128)}, u32[]{:S(2)}) copy-start(s32[128,128]{1,0:T(8,128)} %copy-done.23) | copy-start | bytes 196612
  432.1 130.7 %copy-start.34 = (f32[768]{0:T(1024)S(1)}, f32[768]{0:T(1024)}, u32[]{:S(2)}) copy-start(f32[768]{0:T(1024)} %get-tuple-element.60) | copy-start | bytes 9220
  432.1 171.8 %copy-start.33 = (f32[128]{0:T(128)S(1)}, f32[128]{0:T(128)}, u32[]{:S(2)}) copy-start(f32[128]{0:T(128)} %copy-done.30) | copy-start | bytes 1540
  432.1 171.8 %copy-start.53 = (f32[128]{0:T(128)S(1)}, f32[128]{0:T(128)}, u32[]{:S(2)}) copy-start(f32[128]{0:T(128)} %get-tuple-element.70) | copy-start | bytes 1540
  495.1 151.9 %reduce-scatter.31.cloned.1.call-start = ((), (), s32[]{:S(2)}) async-start(), calls=%async_computation.24 | async-start | bytes 245760
  497.9 106.0 %copy-start.17 = (f32[128,768]{1,0:T(8,128)S(1)}, f32[128,768]{1,0:T(8,128)}, u32[]{:S(2)}) copy-start(f32[128,768]{1,0:T(8,128)} %get-tuple-element.85) | copy-start | bytes 1179652
  (24 other events, 55.7 us)
Sparse Core Ops, SparseCore 0:
  15.4 42.5 all-gather.6
  60.2 39.8 all-gather.8
  102.8 39.8 all-gather.4
  144.7 39.8 all-gather.10
  216.4 27.1 reduce-scatter.18
  250.1 25.6 reduce-scatter.20
  298.3 62.1 reduce-scatter.28
  363.9 62.9 reduce-scatter.26
  430.3 62.9 reduce-scatter.24
  496.6 62.9 reduce-scatter.22
  562.0 18.7 reduce-scatter.36
  583.1 19.8 reduce-scatter.34
  605.4 19.5 reduce-scatter.32
  627.3 19.7 reduce-scatter.30
where the time goes:
time: 657 us; the launch traced here: 655 us
  waiting for transfers between devices  427 us (65%)
  blocking collectives  102 us (16%)
  matrix products  56.5 us (9%)
  local copies, waits for them, and re-layouts  34.3 us (5%)
  starting transfers between devices  15.1 us (2%)
  between operations  14.7 us (2%)
    reduce_scatter x1, waiting for transfers between devices, per_device(): lax.psum_scatter(query_w_grad.astype(jnp.bfloat16), 'expert', scatter_dim...  61.7 us
    reduce_scatter x1, waiting for transfers between devices, per_device(): lax.psum_scatter(key_w_grad.astype(jnp.bfloat16), 'expert', scatter_dimen...  61.3 us
    reduce_scatter x1, waiting for transfers between devices, per_device(): lax.psum_scatter(value_w_grad.astype(jnp.bfloat16), 'expert', scatter_dim...  58.3 us
    reduce_scatter x1, waiting for transfers between devices, per_device(): lax.psum_scatter(output_grad.astype(jnp.bfloat16), 'expert', scatter_dime...  41.2 us
    psum x1, blocking collectives, per_device(): lax.psum((attn_gain_grad, ffn_gain_grad, bias_grad, router_grad), ('dp',...  41 us
    all_gather x1, waiting for transfers between devices, per_device(): lax.all_gather(row_parts[2], 'expert', axis=1, tiled=True)  40.6 us
    all_gather x1, waiting for transfers between devices, per_device(): lax.all_gather(row_parts[1], 'expert', axis=1, tiled=True)  40 us
    unnamed x18, waiting for transfers between devices  37.6 us
  transfers between devices with their start and end apart: 17, of which 13 were waited for; matrix products, arithmetic and copies ran while one was open for 11% of the time, Pallas kernels for 0%

commit v1 on v0

v1 whole, which is shorter than its diff:
```python
import jax
import jax.numpy as jnp
from jax import lax
from jax.sharding import PartitionSpec as P

EPSILON = 1e-06
LIMITS = (12, 16, 23, 32, 46, 64, 91)
MASKED = -1000000000.0
HIGHEST = lax.Precision.HIGHEST
LOW = jnp.bfloat16
FULL = jnp.float32


def bucket_table(length):
    spots = jnp.arange(length, dtype=jnp.int32)
    delta = spots[None, :] - spots[:, None]
    magnitude = jnp.abs(delta)
    distant = jnp.full_like(magnitude, 8)
    for threshold in LIMITS:
        distant = distant + (magnitude >= threshold).astype(jnp.int32)
    return jnp.where(delta > 0, 16, 0).astype(jnp.int32) + jnp.where(
        magnitude < 8, magnitude, distant
    )


def normalize(matrix, gain_vec):
    scale = lax.rsqrt(jnp.mean(matrix * matrix, axis=-1, keepdims=True) + EPSILON)
    return (matrix * scale * gain_vec, scale)


def norm_back(matrix, scale, gain_vec, incoming):
    weighted = incoming * gain_vec
    average = jnp.mean(matrix * weighted, axis=-1, keepdims=True)
    return (
        scale * weighted - matrix * (scale * scale * scale) * average,
        jnp.sum(incoming * matrix * scale, axis=0),
    )


def contract_rows(left, right, precision=None):
    return lax.dot_general(
        left, right, (((0,), (0,)), ((), ())), precision=precision, preferred_element_type=FULL
    )


def contract_cols(left, right, precision=None):
    return lax.dot_general(
        left, right, (((1,), (1,)), ((), ())), precision=precision, preferred_element_type=FULL
    )


def smooth(values):
    return jax.nn.gelu(values, approximate=True)


def swap(value, axis, mask):
    count = lax.axis_size(axis)
    return lax.ppermute(value, axis, [(i, i ^ mask) for i in range(count)])


def gather_bits(value, axis, masks):
    return jnp.concatenate([value] + [swap(value, axis, mask) for mask in masks], axis=0)


def absolute(stacked, position):
    count = stacked.shape[0]
    return jnp.concatenate(
        [lax.dynamic_index_in_dim(stacked, position ^ j, 0, keepdims=True) for j in range(count)],
        axis=0,
    )


def scatter_sum(stacked, axis):
    bit = 1
    while stacked.shape[0] > 1:
        pairs = stacked.reshape((stacked.shape[0] // 2, 2) + stacked.shape[1:])
        taken = swap(pairs[:, 1], axis, bit)
        stacked = (pairs[:, 0].astype(FULL) + taken.astype(FULL)).astype(stacked.dtype)
        bit = bit * 2
    return stacked[0]


def gather_rel(value, axis):
    count = lax.axis_size(axis)
    stacked = value[None]
    bit = count // 2
    parts = []
    while bit >= 1:
        other = swap(stacked, axis, bit)
        stacked = jnp.concatenate([stacked, other], axis=0)
        parts.append(bit)
        bit = bit // 2
    bits = len(parts)
    stacked = stacked.reshape((2,) * bits + value.shape)
    stacked = stacked.transpose(tuple(reversed(range(bits))) + tuple(range(bits, stacked.ndim)))
    return stacked.reshape((count,) + value.shape)


def gather_weights(payload):
    ranks, dps = lax.axis_size("expert"), lax.axis_size("dp")
    half = payload.shape[0] // 2
    low_masks = list(range(2, ranks, 2))
    high_dp = list(range(2, dps, 2))
    halves = []
    for part, order in ((payload[:half], "xy"), (payload[half:], "yx")):
        value = part[None]
        value = gather_bits(value, "expert", low_masks)
        for letter in order:
            if letter == "x":
                value = gather_bits(value[None], "expert", [1])
            else:
                value = gather_bits(value[None], "dp", high_dp)
        value = gather_bits(value[None], "dp", [1])
        if order == "xy":
            value = value.transpose(3, 2, 1, 0, 4, 5)
        else:
            value = value.transpose(3, 1, 2, 0, 4, 5)
        halves.append(value.reshape((ranks, dps) + part.shape))
    stacked = jnp.concatenate(halves, axis=2)
    stacked = absolute(stacked, lax.axis_index("expert"))
    stacked = absolute(jnp.swapaxes(stacked, 0, 1), lax.axis_index("dp"))
    return jnp.swapaxes(stacked, 0, 1)


def per_device(
    tokens,
    seg_ids,
    routes,
    attn_gain,
    w_query,
    w_key,
    w_value,
    w_output,
    rel_bias,
    ffn_gain,
    w_router,
    w_in,
    w_out,
    d_out,
):
    inputs = tokens.astype(FULL)
    length, model_width = inputs.shape
    bucket_count, head_count = rel_bias.shape
    experts_total = w_router.shape[1]
    local_experts = w_in.shape[0]
    ranks, dps = lax.axis_size("expert"), lax.axis_size("dp")
    capacity = length * 5 // (4 * experts_total)
    slot_total = experts_total * capacity
    rank_slots = local_experts * capacity
    blocks = ranks * dps

    route_hits = (routes == jnp.arange(experts_total, dtype=jnp.int32)[None, :]).astype(jnp.int32)
    placed = jnp.sum(jnp.cumsum(route_hits, axis=0) * route_hits, axis=1) - 1
    slot_index = jnp.where(placed < capacity, routes[:, 0] * capacity + placed, slot_total)
    slot_mask = (slot_index[:, None] == jnp.arange(slot_total, dtype=jnp.int32)[None, :]).astype(
        LOW
    )
    hits_float = route_hits.astype(FULL)

    payload = jnp.concatenate([w_query, w_key, w_value, w_output], axis=1)
    rows_here, columns_here = w_query.shape
    weights_all = gather_weights(payload)
    weights_all = weights_all.reshape(ranks, dps * rows_here, 4, columns_here)
    full_w = weights_all.transpose(2, 1, 0, 3).reshape(4, dps * rows_here, ranks * columns_here)
    query_w, key_w, value_w, output_w = full_w[0], full_w[1], full_w[2], full_w[3]

    upstream = d_out.astype(FULL)
    up_out = contract_rows(slot_mask, d_out).astype(LOW).reshape(ranks, rank_slots, model_width)
    up_arrived = lax.all_to_all(up_out, "expert", split_axis=0, concat_axis=0, tiled=True)
    up_rows = gather_rel(up_arrived, "dp").reshape(blocks, local_experts, capacity, model_width)
    up_act = jnp.einsum("secd,efd->secf", up_rows, w_out, preferred_element_type=FULL)

    inner_width = query_w.shape[1]
    head_size = inner_width // head_count
    factor = head_size ** (-0.5)
    gain_one = attn_gain.astype(FULL)
    normed_one, scale_one = normalize(inputs, gain_one)
    normed_low = normed_one.astype(LOW)
    normed_all = lax.all_gather(normed_low, "expert", axis=0, tiled=True)
    query_rows = jnp.dot(normed_low, query_w, preferred_element_type=FULL).astype(LOW)
    key_rows = jnp.dot(normed_low, key_w, preferred_element_type=FULL).astype(LOW)
    value_rows = jnp.dot(normed_low, value_w, preferred_element_type=FULL).astype(LOW)
    query_heads = query_rows.reshape(length, head_count, head_size)
    key_heads = key_rows.reshape(length, head_count, head_size)
    value_heads = value_rows.reshape(length, head_count, head_size)
    bucket_ids = bucket_table(length)
    onehot_buckets = (
        bucket_ids[:, :, None] == jnp.arange(bucket_count, dtype=jnp.int32)[None, None, :]
    ).astype(LOW)
    bias_full = jnp.einsum("ijb,bh->hij", onehot_buckets, rel_bias, preferred_element_type=FULL)
    segment_row = seg_ids[0]
    same_doc = (segment_row[:, None] == segment_row[None, :])[None, :, :]
    scores = (
        jnp.einsum("ihd,jhd->hij", query_heads, key_heads, preferred_element_type=FULL) * factor
        + bias_full
    )
    weights = jax.nn.softmax(jnp.where(same_doc, scores, MASKED), axis=-1)
    weights_low = weights.astype(LOW)
    attended = jnp.einsum("hij,jhd->ihd", weights_low, value_heads, preferred_element_type=FULL)
    attended = attended.reshape(length, inner_width).astype(LOW)
    attended_all = lax.all_gather(attended, "expert", axis=0, tiled=True)
    hidden = inputs + jnp.dot(attended, output_w, preferred_element_type=FULL)
    gain_two = ffn_gain.astype(FULL)
    normed_two, scale_two = normalize(hidden, gain_two)
    router_w = w_router.astype(FULL)
    chance = jax.nn.softmax(jnp.dot(normed_two, router_w, precision=HIGHEST), axis=-1)
    gate_value = jnp.sum(chance * hits_float, axis=1)

    outgoing = contract_rows(slot_mask, normed_two.astype(LOW)).astype(LOW)
    gate_slots = jnp.sum(slot_mask.astype(FULL) * gate_value[:, None], axis=0)
    gate_slots = gate_slots.reshape(ranks, 1, rank_slots)
    gate_high = gate_slots.astype(LOW)
    gate_low = (gate_slots - gate_high.astype(FULL)).astype(LOW)
    gate_row = jnp.concatenate(
        [gate_high, gate_low, jnp.zeros((ranks, 1, model_width - 2 * rank_slots), LOW)], axis=2
    )
    outgoing = jnp.concatenate(
        [outgoing.reshape(ranks, rank_slots, model_width), gate_row], axis=1
    )
    arrived = lax.all_to_all(outgoing, "expert", split_axis=0, concat_axis=0, tiled=True)
    gathered = gather_rel(arrived, "dp").reshape(blocks, rank_slots + 1, model_width)
    slot_rows = gathered[:, :rank_slots].reshape(blocks, local_experts, capacity, model_width)
    gate_rows = gathered[:, rank_slots, :rank_slots].astype(FULL) + gathered[
        :, rank_slots, rank_slots : 2 * rank_slots
    ].astype(FULL)
    gate_rows = gate_rows.reshape(blocks, local_experts, capacity, 1)

    pre_act = jnp.einsum("secd,edf->secf", slot_rows, w_in, preferred_element_type=FULL)
    activated_f, gelu_back = jax.vjp(smooth, pre_act)
    activated = activated_f.astype(LOW)
    gate_part = jnp.sum(activated.astype(FULL) * up_act, axis=3)
    pre_grad = gelu_back(up_act * gate_rows)[0].astype(LOW)
    input_part = jnp.einsum("secf,edf->secd", pre_grad, w_in, preferred_element_type=FULL)
    gate_part = gate_part.reshape(blocks, 1, rank_slots).astype(LOW)
    gate_part = jnp.pad(gate_part, ((0, 0), (0, 0), (0, model_width - rank_slots)))
    back = jnp.concatenate(
        [input_part.astype(LOW).reshape(blocks, rank_slots, model_width), gate_part], axis=1
    )
    back = scatter_sum(back.reshape(dps, ranks, rank_slots + 1, model_width), "dp")
    dispatch_back = lax.all_to_all(back, "expert", split_axis=0, concat_axis=0, tiled=True)

    partial_out = jnp.einsum("secf,efd->secd", activated, w_out, preferred_element_type=FULL)
    returned = scatter_sum(
        partial_out.astype(LOW).reshape(dps, ranks, rank_slots, model_width), "dp"
    )
    back_rows = lax.all_to_all(returned, "expert", split_axis=0, concat_axis=0, tiled=True)
    first_grad = jnp.einsum("secd,secf->edf", slot_rows, pre_grad, preferred_element_type=FULL)
    grad_rows = (up_rows.astype(FULL) * gate_rows).astype(LOW)
    second_grad = jnp.einsum("secf,secd->efd", activated, grad_rows, preferred_element_type=FULL)

    fetched = jnp.dot(
        slot_mask, back_rows.reshape(slot_total, model_width), preferred_element_type=FULL
    )
    output = (hidden + gate_value[:, None] * fetched).astype(LOW)

    gate_slots_grad = dispatch_back[:, rank_slots, :rank_slots].astype(FULL).reshape(1, slot_total)
    gate_grad = jnp.sum(slot_mask.astype(FULL) * gate_slots_grad, axis=1)
    logit_grad = chance * (hits_float - gate_value[:, None]) * gate_grad[:, None]
    router_grad = contract_rows(normed_two, logit_grad, HIGHEST)
    normed_two_grad = contract_cols(logit_grad, router_w, HIGHEST)
    normed_two_grad = normed_two_grad + jnp.dot(
        slot_mask,
        dispatch_back[:, :rank_slots].reshape(slot_total, model_width),
        preferred_element_type=FULL,
    )
    hidden_part, ffn_gain_grad = norm_back(hidden, scale_two, gain_two, normed_two_grad)
    g_ffn_gain, g_router = lax.psum((ffn_gain_grad, router_grad), ("dp", "expert"))
    hidden_grad = upstream + hidden_part
    branch_grad = hidden_grad.astype(LOW)
    attended_grad = (
        contract_cols(branch_grad, output_w).astype(LOW).reshape(length, head_count, head_size)
    )
    value_grad = jnp.einsum("hij,ihd->jhd", weights_low, attended_grad, preferred_element_type=FULL)
    value_grad = value_grad.reshape(length, inner_width).astype(LOW)
    prob_grad = jnp.einsum("ihd,jhd->hij", attended_grad, value_heads, preferred_element_type=FULL)
    score_grad = (
        weights * (prob_grad - jnp.sum(prob_grad * weights, axis=-1, keepdims=True))
    ).astype(LOW)
    query_grad = (
        jnp.einsum("hij,jhd->ihd", score_grad, key_heads, preferred_element_type=FULL) * factor
    )
    query_grad = query_grad.reshape(length, inner_width).astype(LOW)
    key_grad = (
        jnp.einsum("hij,ihd->jhd", score_grad, query_heads, preferred_element_type=FULL) * factor
    )
    key_grad = key_grad.reshape(length, inner_width).astype(LOW)
    bias_grad = jnp.einsum("hij,ijb->bh", score_grad, onehot_buckets, preferred_element_type=FULL)

    factors = jnp.concatenate(
        [
            item.reshape(length, ranks, columns_here).transpose(1, 2, 0)
            for item in (query_grad, key_grad, value_grad, branch_grad)
        ],
        axis=1,
    )
    factors = lax.all_to_all(factors, "expert", split_axis=0, concat_axis=0, tiled=True)
    factors = factors.transpose(0, 2, 1).reshape(ranks * length, 4 * columns_here)
    grads_qkv = contract_rows(normed_all, factors[:, : 3 * columns_here])
    grads_out = contract_rows(attended_all, factors[:, 3 * columns_here :])
    grads = jnp.concatenate([grads_qkv, grads_out], axis=1).astype(LOW)
    grads = grads.reshape(dps, rows_here, 4 * columns_here)
    grads = scatter_sum(absolute(grads, lax.axis_index("dp")), "dp").astype(FULL)
    g_query, g_key, g_value, g_output = (
        grads[:, i * columns_here : (i + 1) * columns_here] for i in range(4)
    )

    normed_one_grad = (
        contract_cols(query_grad, query_w)
        + contract_cols(key_grad, key_w)
        + contract_cols(value_grad, value_w)
    )
    input_norm_grad, attn_gain_grad = norm_back(inputs, scale_one, gain_one, normed_one_grad)
    d_input = hidden_grad + input_norm_grad
    g_attn_gain, g_rel_bias = lax.psum((attn_gain_grad, bias_grad), ("dp", "expert"))
    return (
        output,
        d_input,
        g_attn_gain,
        g_query,
        g_key,
        g_value,
        g_output,
        g_rel_bias,
        g_ffn_gain,
        g_router,
        first_grad,
        second_grad,
    )


def solution(mesh):
    return jax.shard_map(
        per_device,
        mesh=mesh,
        in_specs=(
            P(("dp", "expert"), None),
            P(("dp", "expert"), None),
            P(("dp", "expert"), None),
            P(),
            P("dp", "expert"),
            P("dp", "expert"),
            P("dp", "expert"),
            P("dp", "expert"),
            P(),
            P(),
            P(),
            P("expert", None, "dp"),
            P("expert", "dp", None),
            P(("dp", "expert"), None),
        ),
        out_specs=(
            P(("dp", "expert"), None),
            P(("dp", "expert"), None),
            P(),
            P("dp", "expert"),
            P("dp", "expert"),
            P("dp", "expert"),
            P("dp", "expert"),
            P(),
            P(),
            P(),
            P("expert", None, "dp"),
            P("expert", "dp", None),
        ),
        check_vma=False,
    )
```

time: 657 us -> 336 us (0.51)
  waiting for transfers between devices: 427 us -> 39.3 us
  blocking collectives: 102 us -> 39.2 us
  local copies, waits for them, and re-layouts: 34.3 us -> 92.3 us
  starting transfers between devices: 15.1 us -> 55.4 us
  other arithmetic: 5.61 us -> 35.3 us
    reduce_scatter x6 -> x0, waiting for transfers between devices: 243 us -> none  [the longest x1 61.7 us: per_device(): lax.psum_scatter(query_w_grad.astype(jnp.bfloat16), 'expert', scatter_dim...]
    all_gather x4 -> x2, waiting for transfers between devices: 133 us -> 0.04 us  [the longest x1 0.02 us: per_device(): normed_all = lax.all_gather(normed_low, 'expert', axis=0, tiled=True)]
    slice x0 -> x8, local copies, waits for them, and re-layouts: none -> 50.8 us  [the longest x2 27.2 us: per_device(): full_w[3]]
    all_gather x6 -> x0, blocking collectives: 46.7 us -> none  [the longest x1 12.6 us: per_device(): grad_rows = lax.all_gather(arrived_grad, 'dp', axis=0, tiled=True)]
    unnamed x18 -> x2, waiting for transfers between devices: 37.6 us -> 0.03 us
    ppermute x0 -> x22, starting transfers between devices: none -> 27.6 us  [swap(): return lax.ppermute(value, axis, [(i, i ^ mask) for i in range(count)])]
    ppermute x0 -> x22, waiting for transfers between devices: none -> 21.2 us  [swap(): return lax.ppermute(value, axis, [(i, i ^ mask) for i in range(count)])]
    all_to_all x1 -> x0, blocking collectives: 14.3 us -> none  [per_device(): lax.all_to_all(outgoing_grad, 'expert', split_axis=0, concat_axis=0, tile...]
  transfers between devices with their start and end apart: 17 -> 29, of which waited for: 13 -> 12; matrix products, arithmetic and copies ran while one was open for 11% -> 52% of each run, Pallas kernels for 0% -> 0%
where the time goes in v1:
time: 336 us; the launch traced here: 333 us
  local copies, waits for them, and re-layouts  92.3 us (27%)
  matrix products  56.8 us (17%)
  starting transfers between devices  55.4 us (16%)
  waiting for transfers between devices  39.3 us (12%)
  blocking collectives  39.2 us (12%)
  other arithmetic  35.3 us (11%)
  between operations  15.2 us (5%)
    psum x1, blocking collectives, per_device(): lax.psum((attn_gain_grad, bias_grad), ('dp', 'expert'))  39.2 us
    ppermute x22, starting transfers between devices, swap(): return lax.ppermute(value, axis, [(i, i ^ mask) for i in range(count)])  27.6 us
    slice x2, local copies, waits for them, and re-layouts, per_device(): full_w[3]  27.2 us
    ppermute x22, waiting for transfers between devices, swap(): return lax.ppermute(value, axis, [(i, i ^ mask) for i in range(count)])  21.2 us
    reshape x1, local copies, waits for them, and re-layouts, per_device(): weights_all = weights_all.reshape(ranks, dps * rows_here, 4, columns_here)  12.4 us
    dot_general x5, matrix products, contract_rows(): lax.dot_general(left, right, (((0,), (0,)), ((), ())), precision=precisio...  8.91 us
    slice x1, local copies, waits for them, and re-layouts, per_device(): full_w[0]  8.14 us
    all_to_all x1, waiting for transfers between devices, per_device(): lax.all_to_all(outgoing, 'expert', split_axis=0, concat_axis=0, tiled=True)  7.91 us
  transfers between devices with their start and end apart: 29, of which 12 were waited for; matrix products, arithmetic and copies ran while one was open for 52% of the time, Pallas kernels for 0%

profile of v1, /device:TPU:0, one launch (start us, length us, event | category | flops | bytes accessed | tf_op | source)
XLA Modules:
  0.0 333.4 jit_solution(13492369566615135108)
XLA Ops:
  8.4 5.1 %collective-permute-start.8 = (bf16[1,96,384]{2,1,0:T(8,128)(2,1)S(1)}, bf16[1,96,384]{2,1,0:T(8,128)(2,1)S(1)}, u32[]{:S(2)}, u32[]{:S(2)}) collective-permute-start(bf16[1,96,384]{2,1,0:T(8,128)(2,1)S(1)} %get-tuple-element.45), channel_id=1, source_target_pairs={{0,6},{1,7},{2,4},{3,5},{4,2},{5,3},{6,0},{7,1},{8,14},{9,15},{10,... | collective-permute-start | bytes 221192 | tf_op jit(solution)/shard_map/ppermute | solution.py:58
  14.2 3.7 %collective-permute-start.2 = (bf16[1,96,384]{2,1,0:T(8,128)(2,1)S(1)}, bf16[1,96,384]{2,1,0:T(8,128)(2,1)S(1)}, u32[]{:S(2)}, u32[]{:S(2)}) collective-permute-start(bf16[1,96,384]{2,1,0:T(8,128)(2,1)S(1)} %get-tuple-element.44), channel_id=1, source_target_pairs={{0,6},{1,7},{2,4},{3,5},{4,2},{5,3},{6,0},{7,1},{8,14},{9,15},{10,... | collective-permute-start | bytes 221192 | tf_op jit(solution)/shard_map/ppermute | solution.py:58
  17.9 2.7 collective-permute-start
  20.6 3.0 collective-permute-done.7
  32.9 4.2 %collective-permute-done.3 = bf16[1,4,96,384]{3,2,0,1:T(8,128)(2,1)} collective-permute-done((bf16[1,4,96,384]{3,2,0,1:T(8,128)(2,1)}, bf16[1,4,96,384]{3,2,0,1:T(8,128)(2,1)}, u32[]{:S(2)}, u32[]{:S(2)}) %collective-permute-start.3) | collective-permute-done | bytes 294944 | tf_op jit(solution)/shard_map/ppermute | solution.py:58
  37.1 1.9 maximum_bitcast_fusion.4
  42.9 4.9 %all-to-all-start.2 = ((bf16[8,20,768]{2,1,0:T(8,128)(2,1)}), bf16[8,20,768]{2,1,0:T(8,128)(2,1)}, u32[]{:S(2)}, u32[]{:S(2)}) async-start(bf16[8,20,768]{2,1,0:T(8,128)(2,1)} %reshape.391), calls=%async_computation.2 | async-start | bytes 589824 | tf_op jit(solution)/shard_map/all_to_all | solution.py:169
  49.3 2.2 maximum_bitcast_fusion.3
  51.7 2.4 maximum_bitcast_fusion.2
  59.6 1.9 maximum_bitcast_fusion.1
  61.9 1.9 pad_maximum_fusion
  65.3 2.6 maximum_bitcast_fusion
  67.9 12.4 %reshape.381 = bf16[8,768,4,96]{3,2,1,0:T(4,128)(2,1)} reshape(bf16[8,4,192,384]{3,2,1,0:T(8,128)(2,1)} %maximum_bitcast_fusion) | data formatting | bytes 9437184 | tf_op jit(solution)/shard_map/reshape | solution.py:163
  80.3 19.1 %fusion.132 = (bf16[1,768,8,96]{3,0,1,2:T(2,128)(2,1)}, bf16[1,768,8,96]{3,0,1,2:T(2,128)(2,1)}, bf16[1,768,8,96]{3,0,1,2:T(2,128)(2,1)}, bf16[1,768,8,96]{3,0,1,2:T(2,128)(2,1)}) fusion(bf16[4,768,8,96]{3,0,1,2:T(4,128)(2,1)} %bitcast.287), kind=kLoop, calls=%fused_computation.254 | loop fusion | bytes 9437184 | tf_op jit(solution)/shard_map/slice | solution.py:165
  99.3 6.7 %copy.226 = bf16[1,768,8,96]{1,3,2,0:T(8,128)(2,1)S(1)} copy(bf16[1,768,8,96]{3,0,1,2:T(2,128)(2,1)} %get-tuple-element.25) | data formatting | bytes 2359296 | tf_op jit(solution)/shard_map/slice | solution.py:165
  106.1 2.4 convolution_convert_fusion.8
  110.2 8.1 %copy.228 = bf16[1,768,8,96]{1,3,2,0:T(8,128)(2,1)} copy(bf16[1,768,8,96]{3,0,1,2:T(2,128)(2,1)} %get-tuple-element.24) | data formatting | bytes 2359296 | tf_op jit(solution)/shard_map/slice | solution.py:165
  118.3 1.9 convolution_convert_fusion.7
  121.1 6.7 %copy.230 = bf16[1,768,8,96]{1,3,2,0:T(8,128)(2,1)S(1)} copy(bf16[1,768,8,96]{3,0,1,2:T(2,128)(2,1)} %get-tuple-element.23) | data formatting | bytes 2359296 | tf_op jit(solution)/shard_map/slice | solution.py:165
  127.8 2.4 convolution_convert_fusion.6
  134.8 8.1 %copy.234 = bf16[1,768,8,96]{1,3,2,0:T(8,128)(2,1)} copy(bf16[1,768,8,96]{3,0,1,2:T(2,128)(2,1)} %get-tuple-element.22) | data formatting | bytes 2359296 | tf_op jit(solution)/shard_map/slice | solution.py:165
  142.9 1.8 convolution_convert_fusion.5
  144.7 2.0 multiply_reduce_fusion.3
  151.3 4.9 %all-to-all-start = ((bf16[8,21,768]{2,1,0:T(8,128)(2,1)}), bf16[8,21,768]{2,1,0:T(8,128)(2,1)S(1)}, u32[]{:S(2)}, u32[]{:S(2)}) async-start(bf16[8,21,768]{2,1,0:T(8,128)(2,1)} %maximum_maximum_fusion), calls=%async_computation | async-start | bytes 589824 | tf_op jit(solution)/shard_map/all_to_all | solution.py:220
  157.9 7.9 %all-to-all-done = bf16[8,21,768]{2,1,0:T(8,128)(2,1)S(1)} async-done(((bf16[8,21,768]{2,1,0:T(8,128)(2,1)}), bf16[8,21,768]{2,1,0:T(8,128)(2,1)S(1)}, u32[]{:S(2)}, u32[]{:S(2)}) %all-to-all-start) | async-done | bytes 258080 | tf_op jit(solution)/shard_map/all_to_all | solution.py:220
  168.7 4.0 %collective-permute-done.12 = bf16[1,8,21,768]{3,2,1,0:T(8,128)(2,1)S(1)} collective-permute-done((bf16[1,8,21,768]{3,2,1,0:T(8,128)(2,1)S(1)}, bf16[1,8,21,768]{3,2,1,0:T(8,128)(2,1)S(1)}, u32[]{:S(2)}, u32[]{:S(2)}) %collective-permute-start.12) | collective-permute-done | bytes 258080 | tf_op jit(solution)/shard_map/ppermute | solution.py:58
  180.4 3.0 fusion.3
  183.5 2.2 fusion.17
  185.9 1.9 fusion.25
  195.5 5.3 %collective-permute-done.19 = bf16[1,8,21,768]{3,1,2,0:T(8,128)(2,1)S(1)} collective-permute-done((bf16[1,8,21,768]{3,1,2,0:T(8,128)(2,1)S(1)}, bf16[1,8,21,768]{3,1,2,0:T(8,128)(2,1)S(1)}, u32[]{:S(2)}, u32[]{:S(2)}) %collective-permute-start.19) | collective-permute-done | bytes 258080 | tf_op jit(solution)/shard_map/ppermute | solution.py:58
  201.6 5.1 %all-to-all-start.3 = ((bf16[8,21,768]{2,1,0:T(8,128)(2,1)}), bf16[8,21,768]{2,1,0:T(8,128)(2,1)S(1)}, u32[]{:S(2)}, u32[]{:S(2)}) async-start(bf16[8,21,768]{2,1,0:T(8,128)(2,1)} %copy.252), calls=%async_computation.3 | async-start | bytes 589824 | tf_op jit(solution)/shard_map/all_to_all | solution.py:240
  206.8 5.7 %convolution_bitcast_fusion = f32[2,768,768]{2,1,0:T(8,128)} fusion(bf16[32,2,10,768]{3,0,2,1:T(8,128)(2,1)} %bitcast.319, f32[32,2,10]{0,2,1:T(8,128)S(1)} %add.243, f32[2,32,10,768]{3,1,2,0:T(8,128)} %copy-done.13), kind=kOutput, calls=%fused_computation.30 | convolution fusion | flops 760872960 | bytes 7670272 | tf_op jit(solution)/shard_map/secf,secd->efd/dot_general | solution.py:249
  214.3 6.8 %all-to-all-done.3 = bf16[8,21,768]{2,1,0:T(8,128)(2,1)S(1)} async-done(((bf16[8,21,768]{2,1,0:T(8,128)(2,1)}), bf16[8,21,768]{2,1,0:T(8,128)(2,1)S(1)}, u32[]{:S(2)}, u32[]{:S(2)}) %all-to-all-start.3) | async-done | bytes 258080 | tf_op jit(solution)/shard_map/all_to_all | solution.py:240
  221.1 6.6 %all-to-all-start.1 = ((bf16[8,20,768]{2,1,0:T(8,128)(2,1)}), bf16[8,20,768]{2,1,0:T(8,128)(2,1)}, u32[]{:S(2)}, u32[]{:S(2)}) async-start(bf16[8,20,768]{2,1,0:T(8,128)(2,1)} %copy.243), calls=%async_computation.1 | async-start | bytes 589824 | tf_op jit(solution)/shard_map/all_to_all | solution.py:246
  229.8 2.2 multiply_reduce_fusion.1
  232.0 1.8 fusion.131
  237.1 2.5 convolution_convert_fusion.3
  242.4 2.1 pad_maximum_fusion.3
  244.5 6.0 %all-to-all-start.4 = ((bf16[8,384,128]{2,1,0:T(8,128)(2,1)}), bf16[8,384,128]{2,1,0:T(8,128)(2,1)}, u32[]{:S(2)}, u32[]{:S(2)}) async-start(bf16[8,384,128]{2,1,0:T(8,128)(2,1)} %pad_maximum_fusion.3), calls=%async_computation.4 | async-start | bytes 1572864 | tf_op jit(solution)/shard_map/all_to_all | solution.py:296
  250.5 5.1 %convolution_bitcast_fusion.1 = f32[2,768,768]{2,1,0:T(8,128)} fusion(bf16[32,2,10,768]{3,0,2,1:T(8,128)(2,1)} %bitcast.300, bf16[32,2,10,768]{3,0,2,1:T(8,128)(2,1)} %copy-done.62), kind=kOutput, calls=%fused_computation.31 | convolution fusion | flops 754974720 | bytes 6684672 | tf_op jit(solution)/shard_map/secd,secf->edf/dot_general | solution.py:247
  257.4 1.9 fusion.35
  260.5 1.9 fusion.74
  266.3 3.3 all-to-all-done.4
  272.0 2.8 convolution_convert_fusion
  276.1 2.1 convolution_convert_fusion.9
  280.0 39.2 %all-reduce.1 = (f32[768]{0:T(1024)}, f32[32,12]{0,1:T(8,128)}, f32[768]{0:T(1024)}, f32[768,16]{0,1:T(8,128)}) all-reduce(f32[768]{0:T(1024)S(1)} %copy-done.40, f32[32,12]{0,1:T(8,128)S(1)} %fusion.36, f32[768]{0:T(1024)S(1)} %copy-done.39, f32[768,16]{0,1:T(8,128)S(1)} %copy-done.29), channel_id=1, replica_groups=mesh['dp'=4,'expert'=8] {'dp','expert'}, use_global_device_ids=true, to_apply=%region_16.17 | all-reduce | flops 14208 | bytes 113664 | tf_op jit(solution)/shard_map/psum | solution.py:314
  320.2 2.3 collective-permute-start.21
  322.6 2.0 fusion.70
  (281 shorter events, 81.5 us)
Async XLA Ops:
  7.2 176.3 %copy-start = (bf16[2,768,768]{2,1,0:T(8,128)(2,1)S(1)}, bf16[2,768,768]{2,1,0:T(8,128)(2,1)}, u32[]{:S(2)}) copy-start(bf16[2,768,768]{2,1,0:T(8,128)(2,1)} %param.26) | copy-start | bytes 7077892
  7.2 22.1 %copy-start.47 = (s32[128,1]{0,1:T(1,128)S(1)}, s32[128,1]{0,1:T(1,128)}, u32[]{:S(2)}) copy-start(s32[128,1]{0,1:T(1,128)} %param.16) | copy-start | bytes 1540
  8.4 9.5 %collective-permute-start.8 = (bf16[1,96,384]{2,1,0:T(8,128)(2,1)S(1)}, bf16[1,96,384]{2,1,0:T(8,128)(2,1)S(1)}, u32[]{:S(2)}, u32[]{:S(2)}) collective-permute-start(bf16[1,96,384]{2,1,0:T(8,128)(2,1)S(1)} %get-tuple-element.45), channel_id=1, source_target_pairs={{0,6},{1,7},{2,4},{3,5},{4,2},{5,3},{6,0},{7,1},{8,14},{9,15},{10,... | collective-permute-start | bytes 221192 | tf_op jit(solution)/shard_map/ppermute | solution.py:58
  13.5 10.1 %collective-permute-start.7 = (bf16[1,96,384]{2,1,0:T(8,128)(2,1)S(1)}, bf16[1,96,384]{2,1,0:T(8,128)(2,1)S(1)}, u32[]{:S(2)}, u32[]{:S(2)}) collective-permute-start(bf16[1,96,384]{2,1,0:T(8,128)(2,1)S(1)} %get-tuple-element.45), channel_id=1, source_target_pairs={{0,4},{1,5},{2,6},{3,7},{4,0},{5,1},{6,2},{7,3},{8,12},{9,13},{10,... | collective-permute-start | bytes 221192 | tf_op jit(solution)/shard_map/ppermute | solution.py:58
  13.5 10.1 %collective-permute-start.6 = (bf16[1,96,384]{2,1,0:T(8,128)(2,1)S(1)}, bf16[1,96,384]{2,1,0:T(8,128)(2,1)S(1)}, u32[]{:S(2)}, u32[]{:S(2)}) collective-permute-start(bf16[1,96,384]{2,1,0:T(8,128)(2,1)S(1)} %get-tuple-element.45), channel_id=1, source_target_pairs={{0,2},{1,3},{2,0},{3,1},{4,6},{5,7},{6,4},{7,5},{8,10},{9,11},{10,... | collective-permute-start | bytes 221192 | tf_op jit(solution)/shard_map/ppermute | solution.py:58
  14.2 10.8 %collective-permute-start.2 = (bf16[1,96,384]{2,1,0:T(8,128)(2,1)S(1)}, bf16[1,96,384]{2,1,0:T(8,128)(2,1)S(1)}, u32[]{:S(2)}, u32[]{:S(2)}) collective-permute-start(bf16[1,96,384]{2,1,0:T(8,128)(2,1)S(1)} %get-tuple-element.44), channel_id=1, source_target_pairs={{0,6},{1,7},{2,4},{3,5},{4,2},{5,3},{6,0},{7,1},{8,14},{9,15},{10,... | collective-permute-start | bytes 221192 | tf_op jit(solution)/shard_map/ppermute | solution.py:58
  17.9 8.1 %collective-permute-start.1 = (bf16[1,96,384]{2,1,0:T(8,128)(2,1)S(1)}, bf16[1,96,384]{2,1,0:T(8,128)(2,1)S(1)}, u32[]{:S(2)}, u32[]{:S(2)}) collective-permute-start(bf16[1,96,384]{2,1,0:T(8,128)(2,1)S(1)} %get-tuple-element.44), channel_id=1, source_target_pairs={{0,4},{1,5},{2,6},{3,7},{4,0},{5,1},{6,2},{7,3},{8,12},{9,13},{10,... | collective-permute-start | bytes 221192 | tf_op jit(solution)/shard_map/ppermute | solution.py:58
  17.9 8.1 %collective-permute-start = (bf16[1,96,384]{2,1,0:T(8,128)(2,1)S(1)}, bf16[1,96,384]{2,1,0:T(8,128)(2,1)S(1)}, u32[]{:S(2)}, u32[]{:S(2)}) collective-permute-start(bf16[1,96,384]{2,1,0:T(8,128)(2,1)S(1)} %get-tuple-element.44), channel_id=1, source_target_pairs={{0,2},{1,3},{2,0},{3,1},{4,6},{5,7},{6,4},{7,5},{8,10},{9,11},{10,... | collective-permute-start | bytes 221192 | tf_op jit(solution)/shard_map/ppermute | solution.py:58
  23.6 6.9 %collective-permute-start.9 = (bf16[1,4,96,384]{3,2,1,0:T(8,128)(2,1)S(1)}, bf16[1,4,96,384]{3,2,1,0:T(8,128)(2,1)}, u32[]{:S(2)}, u32[]{:S(2)}) collective-permute-start(bf16[1,4,96,384]{3,2,1,0:T(8,128)(2,1)S(1)} %maximum_bitcast_fusion.7), channel_id=1, source_target_pairs={{0,16},{8,24},{16,0},{24,8},{1,17},{9,25},{17,1},{25,9},{2,18},{10... | collective-permute-start | bytes 884744 | tf_op jit(solution)/shard_map/ppermute | solution.py:58
  26.8 10.3 %collective-permute-start.3 = (bf16[1,4,96,384]{3,2,0,1:T(8,128)(2,1)}, bf16[1,4,96,384]{3,2,0,1:T(8,128)(2,1)}, u32[]{:S(2)}, u32[]{:S(2)}) collective-permute-start(bf16[1,4,96,384]{3,2,0,1:T(8,128)(2,1)} %maximum_bitcast_fusion.6), channel_id=1, source_target_pairs={{0,1},{1,0},{2,3},{3,2},{4,5},{5,4},{6,7},{7,6},{8,9},{9,8},{10,11... | collective-permute-start | bytes 884744 | tf_op jit(solution)/shard_map/ppermute | solution.py:58
  29.3 18.6 %copy-start.57 = (bf16[768]{0:T(1024)(128)(2,1)S(1)}, bf16[768]{0:T(1024)(128)(2,1)}, u32[]{:S(2)}) copy-start(bf16[768]{0:T(1024)(128)(2,1)} %param.17) | copy-start | bytes 4612
  29.3 18.6 %copy-start.6 = (bf16[128,768]{1,0:T(8,128)(2,1)S(1)}, bf16[128,768]{1,0:T(8,128)(2,1)}, u32[]{:S(2)}) copy-start(bf16[128,768]{1,0:T(8,128)(2,1)} %param.14) | copy-start | bytes 589828
  31.5 17.8 %collective-permute-start.10 = (bf16[1,2,4,96,384]{4,3,2,1,0:T(8,128)(2,1)S(1)}, bf16[1,2,4,96,384]{4,3,2,1,0:T(8,128)(2,1)}, u32[]{:S(2)}, u32[]{:S(2)}) collective-permute-start(bf16[1,2,4,96,384]{4,3,2,1,0:T(8,128)(2,1)S(1)} %maximum_bitcast_fusion.5), channel_id=1, source_target_pairs={{0,1},{1,0},{2,3},{3,2},{4,5},{5,4},{6,7},{7,6},{8,9},{9,8},{10,11... | collective-permute-start | bytes 1769480 | tf_op jit(solution)/shard_map/ppermute | solution.py:58
  39.0 12.7 %collective-permute-start.4 = (bf16[1,2,4,96,384]{4,3,0,1,2:T(8,128)(2,1)}, bf16[1,2,4,96,384]{4,3,0,1,2:T(8,128)(2,1)}, u32[]{:S(2)}, u32[]{:S(2)}) collective-permute-start(bf16[1,2,4,96,384]{4,3,0,1,2:T(8,128)(2,1)} %maximum_bitcast_fusion.4), channel_id=1, source_target_pairs={{0,16},{8,24},{16,0},{24,8},{1,17},{9,25},{17,1},{25,9},{2,18},{10... | collective-permute-start | bytes 1769480 | tf_op jit(solution)/shard_map/ppermute | solution.py:58
  42.9 108.3 %all-to-all-start.2 = ((bf16[8,20,768]{2,1,0:T(8,128)(2,1)}), bf16[8,20,768]{2,1,0:T(8,128)(2,1)}, u32[]{:S(2)}, u32[]{:S(2)}) async-start(bf16[8,20,768]{2,1,0:T(8,128)(2,1)} %reshape.391), calls=%async_computation.2 | async-start | bytes 589824 | tf_op jit(solution)/shard_map/all_to_all | solution.py:169
  47.9 223.2 %all-gather.3.cloned.1.call-start = ((), (), s32[]{:S(2)}) async-start(), calls=%async_computation.5 | async-start | bytes 1769472 | tf_op jit(solution)/shard_map/all_gather | solution.py:179
  48.0 216.5 %copy-start.32 = (f32[768]{0:T(1024)}, f32[768]{0:T(1024)S(1)}, u32[]{:S(2)}) copy-start(f32[768]{0:T(1024)S(1)} %convert_element_type.390) | copy-start | bytes 9220
  51.5 8.1 %collective-permute-start.11 = (bf16[1,2,2,4,96,384]{5,4,3,2,1,0:T(8,128)(2,1)}, bf16[1,2,2,4,96,384]{5,4,3,2,1,0:T(8,128)(2,1)}, u32[]{:S(2)}, u32[]{:S(2)}) collective-permute-start(bf16[1,2,2,4,96,384]{5,4,3,2,1,0:T(8,128)(2,1)} %maximum_bitcast_fusion.3), channel_id=1, source_target_pairs={{0,8},{8,0},{16,24},{24,16},{1,9},{9,1},{17,25},{25,17},{2,10},{10... | collective-permute-start | bytes 3538952 | tf_op jit(solution)/shard_map/ppermute | solution.py:58
  54.1 7.8 %collective-permute-start.5 = (bf16[1,2,2,4,96,384]{5,4,0,1,2,3:T(8,128)(2,1)}, bf16[1,2,2,4,96,384]{5,4,0,1,2,3:T(8,128)(2,1)}, u32[]{:S(2)}, u32[]{:S(2)}) collective-permute-start(bf16[1,2,2,4,96,384]{5,4,0,1,2,3:T(8,128)(2,1)} %maximum_bitcast_fusion.2), channel_id=1, source_target_pairs={{0,8},{8,0},{16,24},{24,16},{1,9},{9,1},{17,25},{25,17},{2,10},{10... | collective-permute-start | bytes 3538952 | tf_op jit(solution)/shard_map/ppermute | solution.py:58
  106.1 12.3 %copy-start.1 = (bf16[1,768,8,96]{1,3,2,0:T(8,128)(2,1)}, bf16[1,768,8,96]{1,3,2,0:T(8,128)(2,1)S(1)}, u32[]{:S(2)}) copy-start(bf16[1,768,8,96]{1,3,2,0:T(8,128)(2,1)S(1)} %copy.226) | copy-start | bytes 3538948
  134.8 8.1 %copy-start.34 = (f32[12,128]{1,0:T(8,128)}, f32[12,128]{1,0:T(8,128)S(1)}, u32[]{:S(2)}) copy-start(f32[12,128]{1,0:T(8,128)S(1)} %get-tuple-element.52) | copy-start | bytes 18436
  134.8 8.1 %copy-start.27 = (bf16[128,768]{0,1:T(8,128)(2,1)S(1)}, bf16[128,768]{0,1:T(8,128)(2,1)}, u32[]{:S(2)}) copy-start(bf16[128,768]{0,1:T(8,128)(2,1)} %copy.227) | copy-start | bytes 589828
  147.7 20.9 %copy-start.50 = (f32[128]{0:T(128)}, f32[128]{0:T(128)S(1)}, u32[]{:S(2)}) copy-start(f32[128]{0:T(128)S(1)} %fusion.116) | copy-start | bytes 1540
  151.3 14.6 %all-to-all-start = ((bf16[8,21,768]{2,1,0:T(8,128)(2,1)}), bf16[8,21,768]{2,1,0:T(8,128)(2,1)S(1)}, u32[]{:S(2)}, u32[]{:S(2)}) async-start(bf16[8,21,768]{2,1,0:T(8,128)(2,1)} %maximum_maximum_fusion), calls=%async_computation | async-start | bytes 589824 | tf_op jit(solution)/shard_map/all_to_all | solution.py:220
  156.1 120.0 %all-gather.5.cloned.1.call-start = ((), (), s32[]{:S(2)}) async-start(), calls=%async_computation.6 | async-start | bytes 1769472 | tf_op jit(solution)/shard_map/all_gather | solution.py:201
  156.4 11.0 %collective-permute-start.16 = (bf16[1,8,20,768]{3,2,1,0:T(8,128)(2,1)}, bf16[1,8,20,768]{3,2,1,0:T(8,128)(2,1)}, u32[]{:S(2)}, u32[]{:S(2)}) collective-permute-start(bf16[1,8,20,768]{3,2,1,0:T(8,128)(2,1)} %bitcast.52), channel_id=1, source_target_pairs={{0,16},{8,24},{16,0},{24,8},{1,17},{9,25},{17,1},{25,9},{2,18},{10... | collective-permute-start | bytes 737288 | tf_op jit(solution)/shard_map/ppermute | solution.py:58
  165.8 6.8 %collective-permute-start.12 = (bf16[1,8,21,768]{3,2,1,0:T(8,128)(2,1)S(1)}, bf16[1,8,21,768]{3,2,1,0:T(8,128)(2,1)S(1)}, u32[]{:S(2)}, u32[]{:S(2)}) collective-permute-start(bf16[1,8,21,768]{3,2,1,0:T(8,128)(2,1)S(1)} %bitcast.302), channel_id=1, source_target_pairs={{0,16},{8,24},{16,0},{24,8},{1,17},{9,25},{17,1},{25,9},{2,18},{10... | collective-permute-start | bytes 774152 | tf_op jit(solution)/shard_map/ppermute | solution.py:58
  168.6 7.1 %collective-permute-start.17 = (bf16[2,8,20,768]{3,1,2,0:T(8,128)(2,1)S(1)}, bf16[2,8,20,768]{3,1,2,0:T(8,128)(2,1)S(1)}, u32[]{:S(2)}, u32[]{:S(2)}) collective-permute-start(bf16[2,8,20,768]{3,1,2,0:T(8,128)(2,1)S(1)} %copy.244), channel_id=1, source_target_pairs={{0,8},{8,0},{16,24},{24,16},{1,9},{9,1},{17,25},{25,17},{2,10},{10... | collective-permute-start | bytes 1474568 | tf_op jit(solution)/shard_map/ppermute | solution.py:58
  173.6 4.3 %collective-permute-start.13 = (bf16[2,8,21,768]{3,1,2,0:T(8,128)(2,1)}, bf16[2,8,21,768]{3,1,2,0:T(8,128)(2,1)}, u32[]{:S(2)}, u32[]{:S(2)}) collective-permute-start(bf16[2,8,21,768]{3,1,2,0:T(8,128)(2,1)} %copy.237), channel_id=1, source_target_pairs={{0,8},{8,0},{16,24},{24,16},{1,9},{9,1},{17,25},{25,17},{2,10},{10... | collective-permute-start | bytes 1548296 | tf_op jit(solution)/shard_map/ppermute | solution.py:58
  189.4 2.1 collective-permute-start.18
  191.1 2.2 collective-permute-start.14
  191.7 9.1 %collective-permute-start.19 = (bf16[1,8,21,768]{3,1,2,0:T(8,128)(2,1)S(1)}, bf16[1,8,21,768]{3,1,2,0:T(8,128)(2,1)S(1)}, u32[]{:S(2)}, u32[]{:S(2)}) collective-permute-start(bf16[1,8,21,768]{3,1,2,0:T(8,128)(2,1)S(1)} %slice_bitcast_fusion.2), channel_id=1, source_target_pairs={{0,16},{8,24},{16,0},{24,8},{1,17},{9,25},{17,1},{25,9},{2,18},{10... | collective-permute-start | bytes 774152 | tf_op jit(solution)/shard_map/ppermute | solution.py:58
  194.2 18.3 %collective-permute-start.15 = (bf16[1,8,20,768]{3,1,2,0:T(8,128)(2,1)}, bf16[1,8,20,768]{3,1,2,0:T(8,128)(2,1)}, u32[]{:S(2)}, u32[]{:S(2)}) collective-permute-start(bf16[1,8,20,768]{3,1,2,0:T(8,128)(2,1)} %slice_bitcast_fusion.4), channel_id=1, source_target_pairs={{0,16},{8,24},{16,0},{24,8},{1,17},{9,25},{17,1},{25,9},{2,18},{10... | collective-permute-start | bytes 737288 | tf_op jit(solution)/shard_map/ppermute | solution.py:58
  201.6 19.4 %all-to-all-start.3 = ((bf16[8,21,768]{2,1,0:T(8,128)(2,1)}), bf16[8,21,768]{2,1,0:T(8,128)(2,1)S(1)}, u32[]{:S(2)}, u32[]{:S(2)}) async-start(bf16[8,21,768]{2,1,0:T(8,128)(2,1)} %copy.252), calls=%async_computation.3 | async-start | bytes 589824 | tf_op jit(solution)/shard_map/all_to_all | solution.py:240
  206.8 21.1 %copy-start.44 = (f32[128]{0:T(128)S(1)}, f32[128]{0:T(128)}, u32[]{:S(2)}) copy-start(f32[128]{0:T(128)} %copy-done.43) | copy-start | bytes 1540
  206.8 21.1 %copy-start.46 = (f32[128]{0:T(128)S(1)}, f32[128]{0:T(128)}, u32[]{:S(2)}) copy-start(f32[128]{0:T(128)} %copy-done.45) | copy-start | bytes 1540
  206.8 21.1 %copy-start.49 = (s32[128,1]{0,1:T(1,128)S(1)}, s32[128,1]{0,1:T(1,128)}, u32[]{:S(2)}) copy-start(s32[128,1]{0,1:T(1,128)} %param.16) | copy-start | bytes 1540
  206.8 21.1 %copy-start.51 = (f32[128]{0:T(128)S(1)}, f32[128]{0:T(128)}, u32[]{:S(2)}) copy-start(f32[128]{0:T(128)} %copy-done.50) | copy-start | bytes 1540
  212.5 17.3 %copy-start.38 = (s32[128]{0:T(128)S(1)}, s32[128]{0:T(128)}, u32[]{:S(2)}) copy-start(s32[128]{0:T(128)} %copy-done.36) | copy-start | bytes 1540
  212.5 17.3 %copy-start.42 = (f32[128]{0:T(128)S(1)}, f32[128]{0:T(128)}, u32[]{:S(2)}) copy-start(f32[128]{0:T(128)} %copy-done.41) | copy-start | bytes 1540
  221.1 23.5 %all-to-all-start.1 = ((bf16[8,20,768]{2,1,0:T(8,128)(2,1)}), bf16[8,20,768]{2,1,0:T(8,128)(2,1)}, u32[]{:S(2)}, u32[]{:S(2)}) async-start(bf16[8,20,768]{2,1,0:T(8,128)(2,1)} %copy.243), calls=%async_computation.1 | async-start | bytes 589824 | tf_op jit(solution)/shard_map/all_to_all | solution.py:246
  244.5 25.1 %all-to-all-start.4 = ((bf16[8,384,128]{2,1,0:T(8,128)(2,1)}), bf16[8,384,128]{2,1,0:T(8,128)(2,1)}, u32[]{:S(2)}, u32[]{:S(2)}) async-start(bf16[8,384,128]{2,1,0:T(8,128)(2,1)} %pad_maximum_fusion.3), calls=%async_computation.4 | async-start | bytes 1572864 | tf_op jit(solution)/shard_map/all_to_all | solution.py:296
  278.5 40.7 %copy-start.61 = (f32[128]{0:T(128)S(1)}, f32[128]{0:T(128)}, u32[]{:S(2)}) copy-start(f32[128]{0:T(128)} %get-tuple-element.15) | copy-start | bytes 1540
  278.6 43.9 %copy-start.33 = (f32[768]{0:T(1024)S(1)}, f32[768]{0:T(1024)}, u32[]{:S(2)}) copy-start(f32[768]{0:T(1024)} %copy-done.32) | copy-start | bytes 9220
  278.7 43.9 %copy-start.54 = (f32[128]{0:T(128)S(1)}, f32[128]{0:T(128)}, u32[]{:S(2)}) copy-start(f32[128]{0:T(128)} %copy-done.52) | copy-start | bytes 1540
  278.7 43.9 %copy-start.60 = (f32[128]{0:T(128)S(1)}, f32[128]{0:T(128)}, u32[]{:S(2)}) copy-start(f32[128]{0:T(128)} %get-tuple-element.48) | copy-start | bytes 1540
  279.5 39.6 %collective-permute-start.20 = (bf16[2,192,384]{2,1,0:T(8,128)(2,1)}, bf16[2,192,384]{2,1,0:T(8,128)(2,1)}, u32[]{:S(2)}, u32[]{:S(2)}) collective-permute-start(bf16[2,192,384]{2,1,0:T(8,128)(2,1)} %slice_bitcast_fusion), channel_id=1, source_target_pairs={{0,8},{8,0},{16,24},{24,16},{1,9},{9,1},{17,25},{25,17},{2,10},{10... | collective-permute-start | bytes 884744 | tf_op jit(solution)/shard_map/ppermute | solution.py:58
  320.2 5.5 %collective-permute-start.21 = (bf16[1,192,384]{2,1,0:T(8,128)(2,1)S(1)}, bf16[1,192,384]{2,1,0:T(8,128)(2,1)S(1)}, u32[]{:S(2)}, u32[]{:S(2)}) collective-permute-start(bf16[1,192,384]{2,1,0:T(8,128)(2,1)S(1)} %slice_bitcast_fusion.6), channel_id=1, source_target_pairs={{0,16},{8,24},{16,0},{24,8},{1,17},{9,25},{17,1},{25,9},{2,18},{10... | collective-permute-start | bytes 442376 | tf_op jit(solution)/shard_map/ppermute | solution.py:58
  (44 other events, 121.1 us)
Sparse Core Ops, SparseCore 0:
  55.9 44.4 all-gather.2
  177.0 50.1 all-gather.4

commit v2 on v1

v2 whole, which is shorter than its diff:
```python
import functools

import jax
import jax.numpy as jnp
from jax import lax
from jax.experimental import pallas as pl
from jax.experimental.pallas import tpu as pltpu
from jax.sharding import PartitionSpec as P

EPSILON = 1e-06
LIMITS = (12, 16, 23, 32, 46, 64, 91)
MASKED = -1000000000.0
HIGHEST = lax.Precision.HIGHEST
LOW = jnp.bfloat16
FULL = jnp.float32


def bucket_table(length):
    spots = jnp.arange(length, dtype=jnp.int32)
    delta = spots[None, :] - spots[:, None]
    magnitude = jnp.abs(delta)
    distant = jnp.full_like(magnitude, 8)
    for threshold in LIMITS:
        distant = distant + (magnitude >= threshold).astype(jnp.int32)
    return jnp.where(delta > 0, 16, 0).astype(jnp.int32) + jnp.where(
        magnitude < 8, magnitude, distant
    )


def normalize(matrix, gain_vec):
    scale = lax.rsqrt(jnp.mean(matrix * matrix, axis=-1, keepdims=True) + EPSILON)
    return (matrix * scale * gain_vec, scale)


def norm_back(matrix, scale, gain_vec, incoming):
    weighted = incoming * gain_vec
    average = jnp.mean(matrix * weighted, axis=-1, keepdims=True)
    return (
        scale * weighted - matrix * (scale * scale * scale) * average,
        jnp.sum(incoming * matrix * scale, axis=0),
    )


def contract_rows(left, right, precision=None):
    return lax.dot_general(
        left, right, (((0,), (0,)), ((), ())), precision=precision, preferred_element_type=FULL
    )


def contract_cols(left, right, precision=None):
    return lax.dot_general(
        left, right, (((1,), (1,)), ((), ())), precision=precision, preferred_element_type=FULL
    )


def smooth(values):
    return jax.nn.gelu(values, approximate=True)


def swap(value, axis, mask):
    count = lax.axis_size(axis)
    return lax.ppermute(value, axis, [(i, i ^ mask) for i in range(count)])


def gather_bits(value, axis, masks):
    return jnp.concatenate([value] + [swap(value, axis, mask) for mask in masks], axis=0)


def absolute(stacked, position):
    count = stacked.shape[0]
    return jnp.concatenate(
        [lax.dynamic_index_in_dim(stacked, position ^ j, 0, keepdims=True) for j in range(count)],
        axis=0,
    )


def scatter_sum(stacked, axis):
    bit = 1
    while stacked.shape[0] > 1:
        pairs = stacked.reshape((stacked.shape[0] // 2, 2) + stacked.shape[1:])
        taken = swap(pairs[:, 1], axis, bit)
        stacked = (pairs[:, 0].astype(FULL) + taken.astype(FULL)).astype(stacked.dtype)
        bit = bit * 2
    return stacked[0]


def gather_rel(value, axis):
    count = lax.axis_size(axis)
    stacked = value[None]
    bit = count // 2
    parts = []
    while bit >= 1:
        other = swap(stacked, axis, bit)
        stacked = jnp.concatenate([stacked, other], axis=0)
        parts.append(bit)
        bit = bit // 2
    bits = len(parts)
    stacked = stacked.reshape((2,) * bits + value.shape)
    stacked = stacked.transpose(tuple(reversed(range(bits))) + tuple(range(bits, stacked.ndim)))
    return stacked.reshape((count,) + value.shape)


def all_sum(value):
    for axis in ("dp", "expert"):
        bit = 1
        while bit < lax.axis_size(axis):
            value = value + swap(value, axis, bit)
            bit = bit * 2
    return value


def gather_pieces(payload):
    ranks, dps = lax.axis_size("expert"), lax.axis_size("dp")
    half = payload.shape[0] // 2
    far = list(range(0, ranks, 2))
    sides = {"x": ("expert", [0, 1]), "y": ("dp", list(range(0, dps, 2)))}
    pieces, places = [], []
    for index, order in enumerate(("xy", "yx")):
        value = payload[index * half : (index + 1) * half][None]
        value = gather_bits(value, "expert", far[1:])
        axis, masks = sides[order[0]]
        value = gather_bits(value[None], axis, masks[1:])
        other_axis, other_masks = sides[order[1]]
        found = [(value, 0)] + [(swap(value, other_axis, m), m) for m in other_masks[1:]]
        found = [(v, m, 0) for v, m in found] + [(swap(v, "dp", 1), m, 1) for v, m in found]
        for piece, mask, core in found:
            offsets = []
            for first in masks:
                for low in far:
                    x_mask, y_mask = (first, mask) if order == "xy" else (mask, first)
                    offsets.append((low ^ x_mask, y_mask ^ core))
            pieces.append(piece)
            places.append((index, offsets))
    return pieces, places


def place_weights(places, piece_refs, w_ref, sem):
    my_expert, my_dp = lax.axis_index("expert"), lax.axis_index("dp")
    copies = []
    for ref, (half, offsets) in zip(piece_refs, places):
        low_count, rows = ref.shape[1], ref.shape[2]
        for index, (e_mask, d_mask) in enumerate(offsets):
            start = (my_dp ^ d_mask) * (2 * rows) + half * rows
            copies.append(
                pltpu.make_async_copy(
                    ref.at[index // low_count, index % low_count],
                    w_ref.at[my_expert ^ e_mask, pl.ds(pl.multiple_of(start, 16), rows), :],
                    sem,
                )
            )
    for copy in copies:
        copy.start()
    return copies


def dot(left, right, dims=((1,), (0,)), precision=None):
    return lax.dot_general(
        left, right, (dims, ((), ())), precision=precision, preferred_element_type=FULL
    )


NT = ((1,), (1,))
TN = ((0,), (0,))


def forward_kernel(
    places, slab, rank_slots, tokens_ref, normed_ref, seg_col_ref, seg_row_ref, bias_ref, gain_ref,
    router_ref, hits_ref, mask_t_ref, *rest
):
    count = len(places)
    piece_refs, rest = rest[:count], rest[count:]
    (heads_ref, weights_ref, attended_ref, hidden_ref, chance_ref, slabs_ref,
     w_ref, qkv_ref, att_t_ref, sem) = rest
    copies = place_weights(places, piece_refs, w_ref, sem)
    ranks, width, columns = w_ref.shape
    cols = columns // 4
    head_count = weights_ref.shape[0]
    head = width // head_count
    same_doc = seg_col_ref[...] == seg_row_ref[...]
    normed = normed_ref[...]
    for copy in copies:
        copy.wait()
    for e in range(ranks):
        turned = dot(normed, w_ref[e]).T
        for m in range(3):
            qkv_ref[m, e * cols : (e + 1) * cols, :] = turned[m * cols : (m + 1) * cols]
    heads_ref[...] = qkv_ref[...].astype(LOW)
    for h in range(head_count):
        rows = slice(h * head, (h + 1) * head)
        scores = dot(heads_ref[0, rows, :], heads_ref[1, rows, :], TN) * head ** (-0.5)
        scores = jnp.where(same_doc, scores + bias_ref[h], MASKED)
        grown = jnp.exp(scores - jnp.max(scores, axis=1, keepdims=True))
        weights = grown / jnp.sum(grown, axis=1, keepdims=True)
        weights_ref[h] = weights
        att_t_ref[rows, :] = dot(heads_ref[2, rows, :], weights.astype(LOW), NT)
    attended = att_t_ref[...].T.astype(LOW)
    attended_ref[...] = attended
    low_lane = 3 * cols // 128 * 128
    for e in range(ranks):
        turned = dot(attended, w_ref[e, :, low_lane:]).T
        att_t_ref[e * cols : (e + 1) * cols, :] = turned[3 * cols - low_lane :]
    hidden = tokens_ref[...].astype(FULL) + att_t_ref[...].T
    hidden_ref[...] = hidden
    normed_two, _ = normalize(hidden, gain_ref[...].astype(FULL))
    logits = dot(normed_two, router_ref[...].astype(FULL), precision=HIGHEST)
    grown = jnp.exp(logits - jnp.max(logits, axis=1, keepdims=True))
    chance = grown / jnp.sum(grown, axis=1, keepdims=True)
    chance_ref[...] = chance
    gate = jnp.sum(chance * hits_ref[...], axis=1, keepdims=True)
    mask_t = mask_t_ref[...]
    slots = dot(mask_t, normed_two.astype(LOW))
    gates = dot(mask_t.astype(FULL), jnp.broadcast_to(gate, (gate.shape[0], 128)), precision=HIGHEST)
    sub = lax.broadcasted_iota(jnp.int32, (slab, 128), 0)
    lane = lax.broadcasted_iota(jnp.int32, (slab, 128), 1)
    for r in range(ranks):
        mine = gates[r * slab : (r + 1) * slab]
        high = mine.astype(LOW).astype(FULL)
        spread = jnp.where(lane == sub, high, 0.0) + jnp.where(lane == sub + 64, mine - high, 0.0)
        row = jnp.sum(spread, axis=0, keepdims=True)
        rows = slots[r * slab : (r + 1) * slab]
        start = rows[:, :128] + jnp.where(sub == rank_slots, row, 0.0)
        slabs_ref[r, :, :128] = start.astype(LOW)
        slabs_ref[r, :, 128:] = rows[:, 128:].astype(LOW)


def backward_kernel(
    places, rank_slots, tokens_ref, gain_one_ref, gain_two_ref, router_t_ref, hits_ref, mask_ref,
    back_ref, up_ref, hidden_ref, chance_ref, heads_ref, weights_ref, *rest
):
    count = len(places)
    piece_refs, rest = rest[:count], rest[count:]
    (d_input_ref, factors_ref, score_grad_ref, router_grad_ref, gains_ref,
     w_ref, turned_ref, grads_ref, sem) = rest
    copies = place_weights(places, piece_refs, w_ref, sem)
    ranks, width, columns = w_ref.shape
    cols = columns // 4
    head_count = weights_ref.shape[0]
    head = width // head_count
    factor = head ** (-0.5)
    slab = back_ref.shape[1]
    hidden = hidden_ref[...]
    gain_two = gain_two_ref[...].astype(FULL)
    normed_two, scale_two = normalize(hidden, gain_two)
    mask = mask_ref[...]
    chance, hits = chance_ref[...], hits_ref[...]
    gate = jnp.sum(chance * hits, axis=1, keepdims=True)
    back = back_ref[...].reshape(ranks * slab, width)
    sub = lax.broadcasted_iota(jnp.int32, (slab, 128), 0)
    lane = lax.broadcasted_iota(jnp.int32, (slab, 128), 1)
    spread = []
    for r in range(ranks):
        row = back_ref[r, :, :128].astype(FULL)[rank_slots : rank_slots + 1]
        column = jnp.sum(jnp.where(lane == sub, row, 0.0), axis=1, keepdims=True)
        spread.append(jnp.broadcast_to(column, (slab, 128)))
    spread = jnp.concatenate(spread, axis=0).astype(LOW)
    gate_grad = dot(mask, spread)[:, :1]
    logit_grad = chance * (hits - gate) * gate_grad
    router_grad_ref[...] = dot(logit_grad, normed_two, TN, HIGHEST)
    router_t = router_t_ref[...].astype(FULL)
    normed_two_grad = dot(logit_grad, router_t, precision=HIGHEST) + dot(mask, back)
    hidden_part, ffn_gain_grad = norm_back(hidden, scale_two, gain_two, normed_two_grad)
    hidden_grad = up_ref[...].astype(FULL) + hidden_part
    turned_ref[...] = hidden_grad.astype(LOW).astype(FULL).T
    for copy in copies:
        copy.wait()
    low_lane = 3 * cols // 128 * 128
    att_grad = None
    for e in range(ranks):
        own = turned_ref[e * cols : (e + 1) * cols, :]
        if 3 * cols > low_lane:
            own = jnp.concatenate([jnp.zeros((3 * cols - low_lane, 128), FULL), own], axis=0)
        part = dot(w_ref[e, :, low_lane:], own.astype(LOW))
        att_grad = part if att_grad is None else att_grad + part
    att_grad = att_grad.astype(LOW)
    for h in range(head_count):
        rows = slice(h * head, (h + 1) * head)
        own = att_grad[rows]
        weights = weights_ref[h]
        grads_ref[2, rows, :] = dot(own, weights.astype(LOW))
        prob_grad = dot(own, heads_ref[2, rows, :], TN)
        score_grad = weights * (prob_grad - jnp.sum(prob_grad * weights, axis=1, keepdims=True))
        score_grad = score_grad.astype(LOW)
        score_grad_ref[h] = score_grad
        grads_ref[0, rows, :] = dot(heads_ref[1, rows, :], score_grad, NT) * factor
        grads_ref[1, rows, :] = dot(heads_ref[0, rows, :], score_grad) * factor
    total = None
    for e in range(ranks):
        span = slice(e * cols, (e + 1) * cols)
        own = [grads_ref[m, span, :] for m in range(3)]
        factors_ref[e] = jnp.concatenate(own + [turned_ref[span, :]], axis=0).astype(LOW)
        held = jnp.concatenate(own + [jnp.zeros((cols, 128), FULL)], axis=0).astype(LOW)
        part = dot(w_ref[e], held)
        total = part if total is None else total + part
    inputs = tokens_ref[...].astype(FULL)
    gain_one = gain_one_ref[...].astype(FULL)
    _, scale_one = normalize(inputs, gain_one)
    norm_part, attn_gain_grad = norm_back(inputs, scale_one, gain_one, total.T)
    d_input_ref[...] = hidden_grad + norm_part
    gains_ref[0:1, :] = ffn_gain_grad.reshape(1, width)
    gains_ref[1:2, :] = attn_gain_grad.reshape(1, width)


VMEM = pl.BlockSpec(memory_space=pltpu.VMEM)
ANY = pl.BlockSpec(memory_space=pl.ANY)
LIMIT = 40 * 1024 * 1024


def shaped(dtype, *shape):
    return jax.ShapeDtypeStruct(shape, dtype)


def per_device(
    tokens,
    seg_ids,
    routes,
    attn_gain,
    w_query,
    w_key,
    w_value,
    w_output,
    rel_bias,
    ffn_gain,
    w_router,
    w_in,
    w_out,
    d_out,
):
    inputs = tokens.astype(FULL)
    length, model_width = inputs.shape
    bucket_count, head_count = rel_bias.shape
    experts_total = w_router.shape[1]
    local_experts = w_in.shape[0]
    ranks, dps = lax.axis_size("expert"), lax.axis_size("dp")
    capacity = length * 5 // (4 * experts_total)
    slot_total = experts_total * capacity
    rank_slots = local_experts * capacity
    blocks = ranks * dps

    slab = -(-(rank_slots + 1) // 8) * 8

    payload = jnp.concatenate([w_query, w_key, w_value, w_output], axis=1)
    rows_here, columns_here = w_query.shape
    pieces, places = gather_pieces(payload)

    route_hits = (routes == jnp.arange(experts_total, dtype=jnp.int32)[None, :]).astype(jnp.int32)
    placed = jnp.sum(jnp.cumsum(route_hits, axis=0) * route_hits, axis=1) - 1
    slot_index = jnp.where(placed < capacity, routes[:, 0] * capacity + placed, slot_total)
    slot_mask = (slot_index[:, None] == jnp.arange(slot_total, dtype=jnp.int32)[None, :]).astype(
        LOW
    )
    hits_float = route_hits.astype(FULL)
    slab_mask = jnp.pad(
        slot_mask.reshape(length, ranks, rank_slots), ((0, 0), (0, 0), (0, slab - rank_slots))
    ).reshape(length, ranks * slab)

    upstream = d_out.astype(FULL)
    up_out = contract_rows(slot_mask, d_out).astype(LOW).reshape(ranks, rank_slots, model_width)
    up_arrived = lax.all_to_all(up_out, "expert", split_axis=0, concat_axis=0, tiled=True)
    up_rows = gather_rel(up_arrived, "dp").reshape(blocks, local_experts, capacity, model_width)
    up_act = jnp.einsum("secd,efd->secf", up_rows, w_out, preferred_element_type=FULL)

    inner_width = dps * rows_here
    gain_one = attn_gain.astype(FULL)
    normed_low = normalize(inputs, gain_one)[0].astype(LOW)
    normed_all = lax.all_gather(normed_low, "expert", axis=0, tiled=True)
    bucket_ids = bucket_table(length)
    onehot_buckets = (
        bucket_ids[:, :, None] == jnp.arange(bucket_count, dtype=jnp.int32)[None, None, :]
    ).astype(LOW)
    bias_full = jnp.einsum("ijb,bh->hij", onehot_buckets, rel_bias, preferred_element_type=FULL)
    w_shape = (ranks, inner_width, 4 * columns_here)
    heads, weights, attended, hidden, chance, outgoing = pl.pallas_call(
        functools.partial(forward_kernel, places, slab, rank_slots),
        out_shape=(
            shaped(LOW, 3, inner_width, length),
            shaped(FULL, head_count, length, length),
            shaped(LOW, length, inner_width),
            shaped(FULL, length, model_width),
            shaped(FULL, length, experts_total),
            shaped(LOW, ranks, slab, model_width),
        ),
        in_specs=[VMEM] * 9 + [ANY] * len(pieces),
        out_specs=(VMEM,) * 6,
        scratch_shapes=[
            pltpu.VMEM(w_shape, LOW),
            pltpu.VMEM((3, inner_width, length), FULL),
            pltpu.VMEM((inner_width, length), FULL),
            pltpu.SemaphoreType.DMA,
        ],
        compiler_params=pltpu.CompilerParams(vmem_limit_bytes=LIMIT),
        name="attention_forward",
    )(
        tokens,
        normed_low,
        seg_ids.reshape(length, 1),
        seg_ids,
        bias_full,
        ffn_gain.reshape(1, model_width),
        w_router,
        hits_float,
        slab_mask.T,
        *pieces,
    )
    attended_all = lax.all_gather(attended, "expert", axis=0, tiled=True)
    gate_value = jnp.sum(chance * hits_float, axis=1)

    arrived = lax.all_to_all(outgoing, "expert", split_axis=0, concat_axis=0, tiled=True)
    gathered = gather_rel(arrived, "dp").reshape(blocks, slab, model_width)
    slot_rows = gathered[:, :rank_slots].reshape(blocks, local_experts, capacity, model_width)
    gate_rows = gathered[:, rank_slots, :rank_slots].astype(FULL) + gathered[
        :, rank_slots, 64 : 64 + rank_slots
    ].astype(FULL)
    gate_rows = gate_rows.reshape(blocks, local_experts, capacity, 1)

    pre_act = jnp.einsum("secd,edf->secf", slot_rows, w_in, preferred_element_type=FULL)
    activated_f, gelu_back = jax.vjp(smooth, pre_act)
    activated = activated_f.astype(LOW)
    gate_part = jnp.sum(activated.astype(FULL) * up_act, axis=3)
    pre_grad = gelu_back(up_act * gate_rows)[0].astype(LOW)
    input_part = jnp.einsum("secf,edf->secd", pre_grad, w_in, preferred_element_type=FULL)
    gate_part = gate_part.reshape(blocks, 1, rank_slots).astype(LOW)
    gate_part = jnp.pad(
        gate_part, ((0, 0), (0, slab - rank_slots - 1), (0, model_width - rank_slots))
    )
    back = jnp.concatenate(
        [input_part.astype(LOW).reshape(blocks, rank_slots, model_width), gate_part], axis=1
    )
    back = scatter_sum(back.reshape(dps, ranks, slab, model_width), "dp")
    dispatch_back = lax.all_to_all(back, "expert", split_axis=0, concat_axis=0, tiled=True)

    partial_out = jnp.einsum("secf,efd->secd", activated, w_out, preferred_element_type=FULL)
    returned = scatter_sum(
        partial_out.astype(LOW).reshape(dps, ranks, rank_slots, model_width), "dp"
    )
    back_rows = lax.all_to_all(returned, "expert", split_axis=0, concat_axis=0, tiled=True)
    first_grad = jnp.einsum("secd,secf->edf", slot_rows, pre_grad, preferred_element_type=FULL)
    grad_rows = (up_rows.astype(FULL) * gate_rows).astype(LOW)
    second_grad = jnp.einsum("secf,secd->efd", activated, grad_rows, preferred_element_type=FULL)

    fetched = jnp.dot(
        slot_mask, back_rows.reshape(slot_total, model_width), preferred_element_type=FULL
    )
    output = (hidden + gate_value[:, None] * fetched).astype(LOW)

    d_input, factors, score_grad, router_grad, gain_grads = pl.pallas_call(
        functools.partial(backward_kernel, places, rank_slots),
        out_shape=(
            shaped(FULL, length, model_width),
            shaped(LOW, ranks, 4 * columns_here, length),
            shaped(LOW, head_count, length, length),
            shaped(FULL, experts_total, model_width),
            shaped(FULL, 2, model_width),
        ),
        in_specs=[VMEM] * 12 + [ANY] * len(pieces),
        out_specs=(VMEM,) * 5,
        scratch_shapes=[
            pltpu.VMEM(w_shape, LOW),
            pltpu.VMEM((inner_width, length), FULL),
            pltpu.VMEM((3, inner_width, length), FULL),
            pltpu.SemaphoreType.DMA,
        ],
        compiler_params=pltpu.CompilerParams(vmem_limit_bytes=LIMIT),
        name="attention_backward",
    )(
        tokens,
        attn_gain.reshape(1, model_width),
        ffn_gain.reshape(1, model_width),
        w_router.T,
        hits_float,
        slab_mask,
        dispatch_back,
        d_out,
        hidden,
        chance,
        heads,
        weights,
        *pieces,
    )
    bias_grad = jnp.einsum("hij,ijb->bh", score_grad, onehot_buckets, preferred_element_type=FULL)

    factors = lax.all_to_all(factors, "expert", split_axis=0, concat_axis=0, tiled=True)
    factors = factors.transpose(0, 2, 1).reshape(ranks * length, 4 * columns_here)
    grads_qkv = contract_rows(normed_all, factors[:, : 3 * columns_here])
    grads_out = contract_rows(attended_all, factors[:, 3 * columns_here :])
    grads = jnp.concatenate([grads_qkv, grads_out], axis=1).astype(LOW)
    grads = grads.reshape(dps, rows_here, 4 * columns_here)
    grads = scatter_sum(absolute(grads, lax.axis_index("dp")), "dp").astype(FULL)
    g_query, g_key, g_value, g_output = (
        grads[:, i * columns_here : (i + 1) * columns_here] for i in range(4)
    )

    bias_row = jnp.pad(bias_grad.reshape(1, -1), ((0, 0), (0, model_width - bias_grad.size)))
    small = all_sum(jnp.concatenate([router_grad, gain_grads, bias_row], axis=0))
    g_router = small[:experts_total].T
    g_ffn_gain, g_attn_gain = small[experts_total], small[experts_total + 1]
    g_rel_bias = small[experts_total + 2, : bias_grad.size].reshape(bias_grad.shape)
    return (
        output,
        d_input,
        g_attn_gain,
        g_query,
        g_key,
        g_value,
        g_output,
        g_rel_bias,
        g_ffn_gain,
        g_router,
        first_grad,
        second_grad,
    )


def solution(mesh):
    return jax.shard_map(
        per_device,
        mesh=mesh,
        in_specs=(
            P(("dp", "expert"), None),
            P(("dp", "expert"), None),
            P(("dp", "expert"), None),
            P(),
            P("dp", "expert"),
            P("dp", "expert"),
            P("dp", "expert"),
            P("dp", "expert"),
            P(),
            P(),
            P(),
            P("expert", None, "dp"),
            P("expert", "dp", None),
            P(("dp", "expert"), None),
        ),
        out_specs=(
            P(("dp", "expert"), None),
            P(("dp", "expert"), None),
            P(),
            P("dp", "expert"),
            P("dp", "expert"),
            P("dp", "expert"),
            P("dp", "expert"),
            P(),
            P(),
            P(),
            P("expert", None, "dp"),
            P("expert", "dp", None),
        ),
        check_vma=False,
    )
```

time: 336 us -> 253 us (0.75)
  local copies, waits for them, and re-layouts: 92.3 us -> 49.9 us
  blocking collectives: 39.2 us -> 0 us
  matrix products: 56.8 us -> 28.3 us
  Pallas kernels: 0 us -> 20.4 us
  waiting for transfers between devices: 39.3 us -> 52.5 us
  other arithmetic: 35.3 us -> 26.5 us
    slice x5 -> x2, local copies, waits for them, and re-layouts: 48.8 us -> 0.63 us  [the longest x1 0.61 us: per_device(): g_ffn_gain, g_attn_gain = (small[experts_total], small[experts_total + 1])]
    psum x1 -> x0, blocking collectives: 39.2 us -> none  [per_device(): lax.psum((attn_gain_grad, bias_grad), ('dp', 'expert'))]
    dot_general x17 -> x0, matrix products: 26.2 us -> none  [the longest x5 5.28 us: contract_cols(): lax.dot_general(left, right, (((1,), (1,)), ((), ())), precision=precisio...]
    unnamed x129 -> x102, local copies, waits for them, and re-layouts: 3.83 us -> 26 us
    pallas_call x0 -> x2, Pallas kernels: none -> 20.4 us  [the longest x1 11.8 us: per_device(): pl.pallas_call(functools.partial(backward_kernel, places, rank_slots), ou...]
    ppermute x22 -> x29, waiting for transfers between devices: 21.2 us -> 39.5 us  [swap(): return lax.ppermute(value, axis, [(i, i ^ mask) for i in range(count)])]
    reshape x4 -> x6, local copies, waits for them, and re-layouts: 14.2 us -> 2.48 us  [the longest x1 1.53 us: per_device(): slab_mask = jnp.pad(slot_mask.reshape(length, ranks, rank_slots), ((0, 0)...]
    broadcast_in_dim x6 -> x2, other arithmetic: 8.37 us -> 0.98 us  [gather_pieces(): value = gather_bits(value[None], axis, masks[1:])]
  transfers between devices with their start and end apart: 29 -> 36, of which waited for: 12 -> 14; matrix products, arithmetic and copies ran while one was open for 52% -> 31% of each run, Pallas kernels for 0% -> 8%
where the time goes in v2:
time: 253 us; the launch traced here: 250 us
  starting transfers between devices  57.8 us (23%)
  waiting for transfers between devices  52.5 us (21%)
  local copies, waits for them, and re-layouts  49.9 us (20%)
  matrix products  28.3 us (11%)
  other arithmetic  26.5 us (10%)
  Pallas kernels  20.4 us (8%)
  between operations  14.7 us (6%)
    ppermute x29, waiting for transfers between devices, swap(): return lax.ppermute(value, axis, [(i, i ^ mask) for i in range(count)])  39.5 us
    ppermute x29, starting transfers between devices, swap(): return lax.ppermute(value, axis, [(i, i ^ mask) for i in range(count)])  34.2 us
    unnamed x102, local copies, waits for them, and re-layouts  26 us
    pallas_call x1, Pallas kernels, per_device(): pl.pallas_call(functools.partial(backward_kernel, places, rank_slots), ou...  11.8 us
    all_to_all x1, waiting for transfers between devices, per_device(): lax.all_to_all(outgoing, 'expert', split_axis=0, concat_axis=0, tiled=True)  8.78 us
    pallas_call x1, Pallas kernels, per_device(): pl.pallas_call(functools.partial(forward_kernel, places, slab, rank_slots...  8.51 us
    dot_general x1, matrix products, per_device(): jnp.einsum('secf,secd->efd', activated, grad_rows, preferred_element_type...  5.85 us
    dot_general x3, matrix products, contract_rows(): lax.dot_general(left, right, (((0,), (0,)), ((), ())), precision=precisio...  5.81 us
  transfers between devices with their start and end apart: 36, of which 14 were waited for; matrix products, arithmetic and copies ran while one was open for 31% of the time, Pallas kernels for 8%

profile of v2, /device:TPU:0, one launch (start us, length us, event | category | flops | bytes accessed | tf_op | source)
XLA Modules:
  0.0 250.0 jit_solution(991401476921405523)
XLA Ops:
  8.4 5.1 %collective-permute-start.2 = (bf16[1,96,384]{2,1,0:T(8,128)(2,1)S(1)}, bf16[1,96,384]{2,1,0:T(8,128)(2,1)S(1)}, u32[]{:S(2)}, u32[]{:S(2)}) collective-permute-start(bf16[1,96,384]{2,1,0:T(8,128)(2,1)S(1)} %get-tuple-element.97), channel_id=1, source_target_pairs={{0,6},{1,7},{2,4},{3,5},{4,2},{5,3},{6,0},{7,1},{8,14},{9,15},{10,... | collective-permute-start | bytes 221192 | tf_op jit(solution)/shard_map/ppermute | solution.py:62
  14.2 3.7 %collective-permute-start.9 = (bf16[1,96,384]{2,1,0:T(8,128)(2,1)S(1)}, bf16[1,96,384]{2,1,0:T(8,128)(2,1)S(1)}, u32[]{:S(2)}, u32[]{:S(2)}) collective-permute-start(bf16[1,96,384]{2,1,0:T(8,128)(2,1)S(1)} %get-tuple-element.96), channel_id=1, source_target_pairs={{0,6},{1,7},{2,4},{3,5},{4,2},{5,3},{6,0},{7,1},{8,14},{9,15},{10,... | collective-permute-start | bytes 221192 | tf_op jit(solution)/shard_map/ppermute | solution.py:62
  17.9 1.4 fusion.61
  21.7 1.9 collective-permute-done.1
  23.6 1.3 collective-permute-start.3
  27.8 1.6 collective-permute-start.10
  30.5 4.9 %all-to-all-start.2 = ((bf16[8,20,768]{2,1,0:T(8,128)(2,1)}), bf16[8,20,768]{2,1,0:T(8,128)(2,1)}, u32[]{:S(2)}, u32[]{:S(2)}) async-start(bf16[8,20,768]{2,1,0:T(8,128)(2,1)} %reshape.248), calls=%async_computation.2 | async-start | bytes 589824 | tf_op jit(solution)/shard_map/all_to_all | solution.py:358
  38.1 2.1 collective-permute-start.11
  40.4 1.4 fusion.9
  42.3 7.9 %collective-permute-done.4.rest_1_ = bf16[2,4,96,384]{3,2,1,0:T(8,128)(2,1)} collective-permute-done((bf16[2,4,96,384]{3,2,1,0:T(8,128)(2,1)S(1)}, bf16[2,4,96,384]{3,2,1,0:T(8,128)(2,1)}, u32[]{:S(2)}, u32[]{:S(2)}) %collective-permute-start.4) | collective-permute-done | bytes 589856 | tf_op jit(solution)/shard_map/ppermute | solution.py:62
  50.3 3.3 %collective-permute-done.11.rest_5_ = bf16[2,4,96,384]{3,2,1,0:T(8,128)(2,1)} collective-permute-done((bf16[2,4,96,384]{3,2,1,0:T(8,128)(2,1)S(1)}, bf16[2,4,96,384]{3,2,1,0:T(8,128)(2,1)}, u32[]{:S(2)}, u32[]{:S(2)}) %collective-permute-start.11) | collective-permute-done | bytes 589856 | tf_op jit(solution)/shard_map/ppermute | solution.py:62
  55.0 2.4 copy.124
  57.4 1.6 copy.83.router_ref
  60.0 1.7 fusion.45.normed_ref
  68.1 8.5 %attention_forward.1 = (bf16[3,768,128]{2,1,0:T(8,128)(2,1)S(1)}, f32[12,128,128]{2,1,0:T(8,128)S(1)}, bf16[128,768]{1,0:T(8,128)(2,1)S(1)}, f32[128,768]{1,0:T(...) custom-call(bf16[128,768]{1,0:T(8,128)(2,1)S(1)} %copy-done.2, bf16[128,768]{1,0:T(8,128)(2,1)S(1)} %copy-done.4, ...), custom_call_target="tpu_custom_call" | custom-call | tf_op jit(solution)/shard_map/attention_forward/pallas_call | solution.py:372
  81.1 4.4 %all-to-all-start = ((bf16[8,24,768]{2,1,0:T(8,128)(2,1)}), bf16[8,24,768]{2,1,0:T(8,128)(2,1)}, u32[]{:S(2)}, u32[]{:S(2)}) async-start(bf16[8,24,768]{2,1,0:T(8,128)(2,1)} %copy-done.18), calls=%async_computation | async-start | bytes 589824 | tf_op jit(solution)/shard_map/all_to_all | solution.py:407
  85.7 1.3 collective-permute-start.18
  87.1 8.8 %all-to-all-done = bf16[8,24,768]{2,1,0:T(8,128)(2,1)} async-done(((bf16[8,24,768]{2,1,0:T(8,128)(2,1)}), bf16[8,24,768]{2,1,0:T(8,128)(2,1)}, u32[]{:S(2)}, u32[]{:S(2)}) %all-to-all-start) | async-done | bytes 294944 | tf_op jit(solution)/shard_map/all_to_all | solution.py:407
  99.1 4.4 %collective-permute-done.14 = bf16[1,8,24,768]{3,2,1,0:T(8,128)(2,1)S(1)} collective-permute-done((bf16[1,8,24,768]{3,2,1,0:T(8,128)(2,1)}, bf16[1,8,24,768]{3,2,1,0:T(8,128)(2,1)S(1)}, u32[]{:S(2)}, u32[]{:S(2)}) %collective-permute-start.14) | collective-permute-done | bytes 294944 | tf_op jit(solution)/shard_map/ppermute | solution.py:62
  104.2 1.8 pad_maximum_fusion.5
  115.0 3.0 %fusion.2 = f32[2,32,10,768]{3,1,2,0:T(8,128)S(1)} fusion(bf16[32,2,10,768]{3,0,2,1:T(8,128)(2,1)} %bitcast.190, bf16[2,768,768]{2,1,0:T(8,128)(2,1)} %param.25), kind=kOutput, calls=%fused_computation.4 | convolution fusion | flops 754974720 | bytes 5308416 | tf_op jit(solution)/shard_map/secd,edf->secf/dot_general | solution.py:415
  118.0 3.1 %fusion.16 = (bf16[32,2,10,768]{3,0,2,1:T(8,128)(2,1)}, bf16[32,2,10]{0,2,1:T(8,128)(2,1)S(1)}) fusion(f32[2,32,10,768]{3,1,2,0:T(8,128)S(1)} %fusion.2, f32[32,2,10]{0,2,1:T(8,128)S(1)} %copy-done.40, bf16[32,2,10,768]{3,0,2,1:T(8,128)(2,1)S(1)} %bitcast.199, bf16[2,768,768]{2,1,0:T(8,128)(2,1)S(1)} %copy-done), kind=kOutput, calls=%fused_computation.21 | convolution fusion | flops 767753600 | bytes 6295296 | tf_op jit(solution)/shard_map/secd,efd->secf/dot_general | solution.py:360
  122.7 2.9 %fusion.24 = bf16[2,32,10,768]{3,1,2,0:T(8,128)(2,1)S(1)} fusion(bf16[32,2,10,768]{3,0,2,1:T(8,128)(2,1)} %get-tuple-element.84, bf16[2,768,768]{2,1,0:T(8,128)(2,1)} %param.25), kind=kOutput, calls=%fused_computation.32 | convolution fusion | flops 755466240 | bytes 4325376 | tf_op jit(solution)/shard_map/secf,edf->secd/dot_general | solution.py:420
  129.3 1.4 collective-permute-start.21
  131.6 6.7 %collective-permute-done.21 = bf16[1,8,24,768]{3,2,1,0:T(8,128)(2,1)S(1)} collective-permute-done((bf16[1,8,24,768]{3,2,1,0:T(8,128)(2,1)S(1)}, bf16[1,8,24,768]{3,2,1,0:T(8,128)(2,1)S(1)}, u32[]{:S(2)}, u32[]{:S(2)}) %collective-permute-start.21) | collective-permute-done | bytes 294944 | tf_op jit(solution)/shard_map/ppermute | solution.py:62
  139.1 5.2 %all-to-all-start.3 = ((bf16[8,24,768]{2,1,0:T(8,128)(2,1)}), bf16[8,24,768]{2,1,0:T(8,128)(2,1)}, u32[]{:S(2)}, u32[]{:S(2)}) async-start(bf16[8,24,768]{2,1,0:T(8,128)(2,1)} %fusion.46), calls=%async_computation.3 | async-start | bytes 589824 | tf_op jit(solution)/shard_map/all_to_all | solution.py:429
  144.3 1.7 slice_bitcast_fusion.4
  147.3 1.5 copy.97.mask_ref
  148.8 4.3 %collective-permute-done.17 = bf16[1,8,20,768]{3,1,2,0:T(8,128)(2,1)} collective-permute-done((bf16[1,8,20,768]{3,1,2,0:T(8,128)(2,1)}, bf16[1,8,20,768]{3,1,2,0:T(8,128)(2,1)}, u32[]{:S(2)}, u32[]{:S(2)}) %collective-permute-start.17) | collective-permute-done | bytes 245792 | tf_op jit(solution)/shard_map/ppermute | solution.py:62
  155.1 2.5 all-to-all-done.3.back_ref
  157.5 4.3 %all-to-all-start.1 = ((bf16[8,20,768]{2,1,0:T(8,128)(2,1)}), bf16[8,20,768]{2,1,0:T(8,128)(2,1)}, u32[]{:S(2)}, u32[]{:S(2)}) async-start(bf16[8,20,768]{2,1,0:T(8,128)(2,1)} %copy.88), calls=%async_computation.1 | async-start | bytes 589824 | tf_op jit(solution)/shard_map/all_to_all | solution.py:435
  170.1 11.8 %attention_backward.1 = (f32[128,768]{1,0:T(8,128)}, bf16[8,384,128]{2,1,0:T(8,128)(2,1)}, bf16[12,128,128]{2,1,0:T(8,128)(2,1)S(1)}, f32[16,768]{1,0:T(8,128)S(1)}, f32[2,768]{1,0:T(2,128)S(1)}) custom-call(bf16[128,768]{1,0:T(8,128)(2,1)S(1)} %copy-done.3, bf16[1,768]{1,0:T(2,128)(2,1)S(1)} %reshape.247.gain_one_ref, ...), custom_call_target="tpu_custom_call" | custom-call | tf_op jit(solution)/shard_map/attention_backward/pallas_call | solution.py:445
  186.2 1.5 collective-permute-start.23
  188.8 1.9 collective-permute-done.23
  190.7 1.7 collective-permute-start.24
  192.4 4.6 %all-to-all-start.4 = ((bf16[8,384,128]{2,1,0:T(8,128)(2,1)}), bf16[8,384,128]{2,1,0:T(8,128)(2,1)}, u32[]{:S(2)}, u32[]{:S(2)}) async-start(bf16[8,384,128]{2,1,0:T(8,128)(2,1)} %get-tuple-element.32), calls=%async_computation.4 | async-start | bytes 1572864 | tf_op jit(solution)/shard_map/all_to_all | solution.py:481
  197.0 5.8 %convolution_bitcast_fusion = f32[2,768,768]{2,1,0:T(8,128)} fusion(bf16[32,2,10,768]{3,0,2,1:T(8,128)(2,1)} %bitcast.198, f32[32,2,10]{0,2,1:T(8,128)S(1)} %copy-done.41, f32[2,32,10,768]{3,1,2,0:T(8,128)} %copy-done.28), kind=kOutput, calls=%fused_computation.10 | convolution fusion | flops 760872960 | bytes 7670272 | tf_op jit(solution)/shard_map/secf,secd->efd/dot_general | solution.py:438
  203.7 2.0 collective-permute-start.25
  205.8 3.6 %convolution_bitcast_fusion.1 = f32[2,768,768]{2,1,0:T(8,128)} fusion(bf16[32,2,10,768]{3,0,2,1:T(8,128)(2,1)S(1)} %bitcast.191, bf16[32,2,10,768]{3,0,2,1:T(8,128)(2,1)S(1)} %copy-done.48), kind=kOutput, calls=%fused_computation.11 | convolution fusion | flops 754974720 | bytes 6684672 | tf_op jit(solution)/shard_map/secd,secf->edf/dot_general | solution.py:436
  209.4 1.7 reshape.246
  211.1 3.7 %collective-permute-done.25 = f32[19,768]{1,0:T(8,128)S(1)} collective-permute-done((f32[19,768]{1,0:T(8,128)S(1)}, f32[19,768]{1,0:T(8,128)S(1)}, u32[]{:S(2)}, u32[]{:S(2)}) %collective-permute-start.25) | collective-permute-done | bytes 58400 | tf_op jit(solution)/shard_map/ppermute | solution.py:62
  215.5 4.6 %collective-permute-start.26 = (f32[19,768]{1,0:T(8,128)}, f32[19,768]{1,0:T(8,128)}, u32[]{:S(2)}, u32[]{:S(2)}) collective-permute-start(f32[19,768]{1,0:T(8,128)} %add.186), channel_id=1, source_target_pairs={{0,4},{1,5},{2,6},{3,7},{4,0},{5,1},{6,2},{7,3},{8,12},{9,13},{10,... | collective-permute-start | bytes 175112 | tf_op jit(solution)/shard_map/ppermute | solution.py:62
  220.0 1.6 all-to-all-done.4
  221.7 1.5 copy.100
  224.1 2.8 %convolution_convert_fusion = bf16[768,288]{0,1:T(8,128)(2,1)} fusion(bf16[1024,768]{1,0:T(8,128)(2,1)} %all-gather.3.cloned.1.call-done, bf16[1024,384]{1,0:T(8,128)(2,1)S(1)} %bitcast.196), kind=kOutput, calls=%fused_computation.33 | convolution fusion | flops 453206016 | bytes 2801664 | tf_op jit(solution)/shard_map/dot_general | solution.py:45
  228.3 2.6 %convolution_convert_fusion.2 = bf16[768,96]{0,1:T(8,128)(2,1)} fusion(bf16[1024,768]{1,0:T(8,128)(2,1)} %all-gather.5.cloned.1.call-done, bf16[1024,384]{1,0:T(8,128)(2,1)} %bitcast.197), kind=kOutput, calls=%fused_computation.40 | convolution fusion | flops 151068672 | bytes 1982464 | tf_op jit(solution)/shard_map/dot_general | solution.py:45
  235.6 1.5 collective-permute-start.28
  238.6 2.8 %collective-permute-done.28 = bf16[1,192,384]{2,1,0:T(8,128)(2,1)S(1)} collective-permute-done((bf16[1,192,384]{2,1,0:T(8,128)(2,1)S(1)}, bf16[1,192,384]{2,1,0:T(8,128)(2,1)S(1)}, u32[]{:S(2)}, u32[]{:S(2)}) %collective-permute-start.28) | collective-permute-done | bytes 147488 | tf_op jit(solution)/shard_map/ppermute | solution.py:62
  (215 shorter events, 73.2 us)
Async XLA Ops:
  7.2 110.8 %copy-start = (bf16[2,768,768]{2,1,0:T(8,128)(2,1)S(1)}, bf16[2,768,768]{2,1,0:T(8,128)(2,1)}, u32[]{:S(2)}) copy-start(bf16[2,768,768]{2,1,0:T(8,128)(2,1)} %param.26) | copy-start | bytes 7077892
  7.2 22.2 %copy-start.11 = (bf16[128,768]{1,0:T(8,128)(2,1)S(1)}, bf16[128,768]{1,0:T(8,128)(2,1)}, u32[]{:S(2)}) copy-start(bf16[128,768]{1,0:T(8,128)(2,1)} %up_ref.1) | copy-start | bytes 589828
  8.4 12.5 %collective-permute-start.2 = (bf16[1,96,384]{2,1,0:T(8,128)(2,1)S(1)}, bf16[1,96,384]{2,1,0:T(8,128)(2,1)S(1)}, u32[]{:S(2)}, u32[]{:S(2)}) collective-permute-start(bf16[1,96,384]{2,1,0:T(8,128)(2,1)S(1)} %get-tuple-element.97), channel_id=1, source_target_pairs={{0,6},{1,7},{2,4},{3,5},{4,2},{5,3},{6,0},{7,1},{8,14},{9,15},{10,... | collective-permute-start | bytes 221192 | tf_op jit(solution)/shard_map/ppermute | solution.py:62
  13.5 10.1 %collective-permute-start.1 = (bf16[1,96,384]{2,1,0:T(8,128)(2,1)S(1)}, bf16[1,96,384]{2,1,0:T(8,128)(2,1)S(1)}, u32[]{:S(2)}, u32[]{:S(2)}) collective-permute-start(bf16[1,96,384]{2,1,0:T(8,128)(2,1)S(1)} %get-tuple-element.97), channel_id=1, source_target_pairs={{0,4},{1,5},{2,6},{3,7},{4,0},{5,1},{6,2},{7,3},{8,12},{9,13},{10,... | collective-permute-start | bytes 221192 | tf_op jit(solution)/shard_map/ppermute | solution.py:62
  13.5 10.1 %collective-permute-start = (bf16[1,96,384]{2,1,0:T(8,128)(2,1)S(1)}, bf16[1,96,384]{2,1,0:T(8,128)(2,1)S(1)}, u32[]{:S(2)}, u32[]{:S(2)}) collective-permute-start(bf16[1,96,384]{2,1,0:T(8,128)(2,1)S(1)} %get-tuple-element.97), channel_id=1, source_target_pairs={{0,2},{1,3},{2,0},{3,1},{4,6},{5,7},{6,4},{7,5},{8,10},{9,11},{10,... | collective-permute-start | bytes 221192 | tf_op jit(solution)/shard_map/ppermute | solution.py:62
  14.2 10.8 %collective-permute-start.9 = (bf16[1,96,384]{2,1,0:T(8,128)(2,1)S(1)}, bf16[1,96,384]{2,1,0:T(8,128)(2,1)S(1)}, u32[]{:S(2)}, u32[]{:S(2)}) collective-permute-start(bf16[1,96,384]{2,1,0:T(8,128)(2,1)S(1)} %get-tuple-element.96), channel_id=1, source_target_pairs={{0,6},{1,7},{2,4},{3,5},{4,2},{5,3},{6,0},{7,1},{8,14},{9,15},{10,... | collective-permute-start | bytes 221192 | tf_op jit(solution)/shard_map/ppermute | solution.py:62
  17.9 8.3 %collective-permute-start.8 = (bf16[1,96,384]{2,1,0:T(8,128)(2,1)S(1)}, bf16[1,96,384]{2,1,0:T(8,128)(2,1)S(1)}, u32[]{:S(2)}, u32[]{:S(2)}) collective-permute-start(bf16[1,96,384]{2,1,0:T(8,128)(2,1)S(1)} %get-tuple-element.96), channel_id=1, source_target_pairs={{0,4},{1,5},{2,6},{3,7},{4,0},{5,1},{6,2},{7,3},{8,12},{9,13},{10,... | collective-permute-start | bytes 221192 | tf_op jit(solution)/shard_map/ppermute | solution.py:62
  21.0 19.4 %copy-start.44 = (s32[128]{0:T(128)}, s32[128]{0:T(128)S(1)}, u32[]{:S(2)}) copy-start(s32[128]{0:T(128)S(1)} %fusion.74) | copy-start | bytes 1540
  21.0 5.8 %collective-permute-start.7 = (bf16[1,96,384]{2,1,0:T(8,128)(2,1)S(1)}, bf16[1,96,384]{2,1,0:T(8,128)(2,1)S(1)}, u32[]{:S(2)}, u32[]{:S(2)}) collective-permute-start(bf16[1,96,384]{2,1,0:T(8,128)(2,1)S(1)} %get-tuple-element.96), channel_id=1, source_target_pairs={{0,2},{1,3},{2,0},{3,1},{4,6},{5,7},{6,4},{7,5},{8,10},{9,11},{10,... | collective-permute-start | bytes 221192 | tf_op jit(solution)/shard_map/ppermute | solution.py:62
  23.6 11.7 %collective-permute-start.3 = (bf16[1,4,96,384]{3,2,1,0:T(8,128)(2,1)S(1)}, bf16[1,4,96,384]{3,2,1,0:T(8,128)(2,1)}, u32[]{:S(2)}, u32[]{:S(2)}) collective-permute-start(bf16[1,4,96,384]{3,2,1,0:T(8,128)(2,1)S(1)} %maximum_bitcast_fusion), channel_id=1, source_target_pairs={{0,1},{1,0},{2,3},{3,2},{4,5},{5,4},{6,7},{7,6},{8,9},{9,8},{10,11... | collective-permute-start | bytes 884744 | tf_op jit(solution)/shard_map/ppermute | solution.py:62
  27.7 9.3 %copy-start.34 = (bf16[1,4,96,384]{3,2,1,0:T(8,128)(2,1)}, bf16[1,4,96,384]{3,2,1,0:T(8,128)(2,1)S(1)}, u32[]{:S(2)}) copy-start(bf16[1,4,96,384]{3,2,1,0:T(8,128)(2,1)S(1)} %maximum_bitcast_fusion.1) | copy-start | bytes 884740
  27.8 12.7 %copy-start.46 = (bf16[32,12]{0,1:T(8,128)(2,1)S(1)}, bf16[32,12]{0,1:T(8,128)(2,1)}, u32[]{:S(2)}) copy-start(bf16[32,12]{0,1:T(8,128)(2,1)} %param.22) | copy-start | bytes 2308
  27.8 9.2 %collective-permute-start.10 = (bf16[1,4,96,384]{3,2,1,0:T(8,128)(2,1)S(1)}, bf16[1,4,96,384]{3,2,1,0:T(8,128)(2,1)}, u32[]{:S(2)}, u32[]{:S(2)}) collective-permute-start(bf16[1,4,96,384]{3,2,1,0:T(8,128)(2,1)S(1)} %maximum_bitcast_fusion.1), channel_id=1, source_target_pairs={{0,16},{8,24},{16,0},{24,8},{1,17},{9,25},{17,1},{25,9},{2,18},{10... | collective-permute-start | bytes 884744 | tf_op jit(solution)/shard_map/ppermute | solution.py:62
  30.5 50.6 %all-to-all-start.2 = ((bf16[8,20,768]{2,1,0:T(8,128)(2,1)}), bf16[8,20,768]{2,1,0:T(8,128)(2,1)}, u32[]{:S(2)}, u32[]{:S(2)}) async-start(bf16[8,20,768]{2,1,0:T(8,128)(2,1)} %reshape.248), calls=%async_computation.2 | async-start | bytes 589824 | tf_op jit(solution)/shard_map/all_to_all | solution.py:358
  35.4 18.9 %copy-start.42 = (bf16[768]{0:T(1024)(128)(2,1)S(1)}, bf16[768]{0:T(1024)(128)(2,1)}, u32[]{:S(2)}) copy-start(bf16[768]{0:T(1024)(128)(2,1)} %param.17) | copy-start | bytes 4612
  35.4 18.9 %copy-start.26 = (s32[1,128]{1,0:T(1,128)S(1)}, s32[1,128]{1,0:T(1,128)}, u32[]{:S(2)}) copy-start(s32[1,128]{1,0:T(1,128)} %seg_row_ref.1) | copy-start | bytes 1540
  36.4 20.9 %copy-start.47 = (bf16[768]{0:T(1024)(128)(2,1)S(1)}, bf16[768]{0:T(1024)(128)(2,1)}, u32[]{:S(2)}) copy-start(bf16[768]{0:T(1024)(128)(2,1)} %param.23) | copy-start | bytes 4612
  36.4 13.9 %collective-permute-start.4 = (bf16[2,4,96,384]{3,2,1,0:T(8,128)(2,1)S(1)}, bf16[2,4,96,384]{3,2,1,0:T(8,128)(2,1)}, u32[]{:S(2)}, u32[]{:S(2)}) collective-permute-start(bf16[2,4,96,384]{3,2,1,0:T(8,128)(2,1)S(1)} %pad_maximum_fusion.3.rest_0_), channel_id=1, source_target_pairs={{0,16},{8,24},{16,0},{24,8},{1,17},{9,25},{17,1},{25,9},{2,18},{10... | collective-permute-start | bytes 1769480 | tf_op jit(solution)/shard_map/ppermute | solution.py:62
  38.1 15.5 %collective-permute-start.11 = (bf16[2,4,96,384]{3,2,1,0:T(8,128)(2,1)S(1)}, bf16[2,4,96,384]{3,2,1,0:T(8,128)(2,1)}, u32[]{:S(2)}, u32[]{:S(2)}) collective-permute-start(bf16[2,4,96,384]{3,2,1,0:T(8,128)(2,1)S(1)} %pad_maximum_fusion.4.rest_4_), channel_id=1, source_target_pairs={{0,1},{1,0},{2,3},{3,2},{4,5},{5,4},{6,7},{7,6},{8,9},{9,8},{10,11... | collective-permute-start | bytes 1769480 | tf_op jit(solution)/shard_map/ppermute | solution.py:62
  40.3 13.3 %copy-start.37 = (s32[128,128]{1,0:T(8,128)}, s32[128,128]{1,0:T(8,128)S(1)}, u32[]{:S(2)}) copy-start(s32[128,128]{1,0:T(8,128)S(1)} %fusion.58) | copy-start | bytes 196612
  41.8 19.9 %collective-permute-start.5 = (bf16[2,4,96,384]{3,2,1,0:T(8,128)(2,1)S(1)}, bf16[2,4,96,384]{3,2,1,0:T(8,128)(2,1)}, u32[]{:S(2)}, u32[]{:S(2)}) collective-permute-start(bf16[2,4,96,384]{3,2,1,0:T(8,128)(2,1)S(1)} %pad_maximum_fusion.3.rest_0_), channel_id=1, source_target_pairs={{0,8},{8,0},{16,24},{24,16},{1,9},{9,1},{17,25},{25,17},{2,10},{10... | collective-permute-start | bytes 1769480 | tf_op jit(solution)/shard_map/ppermute | solution.py:62
  41.8 19.9 %collective-permute-start.12 = (bf16[2,4,96,384]{3,2,1,0:T(8,128)(2,1)S(1)}, bf16[2,4,96,384]{3,2,1,0:T(8,128)(2,1)}, u32[]{:S(2)}, u32[]{:S(2)}) collective-permute-start(bf16[2,4,96,384]{3,2,1,0:T(8,128)(2,1)S(1)} %pad_maximum_fusion.4.rest_4_), channel_id=1, source_target_pairs={{0,8},{8,0},{16,24},{24,16},{1,9},{9,1},{17,25},{25,17},{2,10},{10... | collective-permute-start | bytes 1769480 | tf_op jit(solution)/shard_map/ppermute | solution.py:62
  50.3 11.4 %collective-permute-start.6 = (bf16[2,4,96,384]{3,2,1,0:T(8,128)(2,1)}, bf16[2,4,96,384]{3,2,1,0:T(8,128)(2,1)}, u32[]{:S(2)}, u32[]{:S(2)}) collective-permute-start(bf16[2,4,96,384]{3,2,1,0:T(8,128)(2,1)} %collective-permute-done.4.rest_1_), channel_id=1, source_target_pairs={{0,8},{8,0},{16,24},{24,16},{1,9},{9,1},{17,25},{25,17},{2,10},{10... | collective-permute-start | bytes 1769480 | tf_op jit(solution)/shard_map/ppermute | solution.py:62
  53.6 8.1 %collective-permute-start.13 = (bf16[2,4,96,384]{3,2,1,0:T(8,128)(2,1)}, bf16[2,4,96,384]{3,2,1,0:T(8,128)(2,1)}, u32[]{:S(2)}, u32[]{:S(2)}) collective-permute-start(bf16[2,4,96,384]{3,2,1,0:T(8,128)(2,1)} %collective-permute-done.11.rest_5_), channel_id=1, source_target_pairs={{0,8},{8,0},{16,24},{24,16},{1,9},{9,1},{17,25},{25,17},{2,10},{10... | collective-permute-start | bytes 1769480 | tf_op jit(solution)/shard_map/ppermute | solution.py:62
  81.1 14.7 %all-to-all-start = ((bf16[8,24,768]{2,1,0:T(8,128)(2,1)}), bf16[8,24,768]{2,1,0:T(8,128)(2,1)}, u32[]{:S(2)}, u32[]{:S(2)}) async-start(bf16[8,24,768]{2,1,0:T(8,128)(2,1)} %copy-done.18), calls=%async_computation | async-start | bytes 589824 | tf_op jit(solution)/shard_map/all_to_all | solution.py:407
  85.5 137.7 %all-gather.3.cloned.1.call-start = ((), (), s32[]{:S(2)}) async-start(), calls=%async_computation.5 | async-start | bytes 1769472 | tf_op jit(solution)/shard_map/all_gather | solution.py:365
  85.7 11.4 %collective-permute-start.18 = (bf16[1,8,20,768]{3,2,1,0:T(8,128)(2,1)}, bf16[1,8,20,768]{3,2,1,0:T(8,128)(2,1)}, u32[]{:S(2)}, u32[]{:S(2)}) collective-permute-start(bf16[1,8,20,768]{3,2,1,0:T(8,128)(2,1)} %bitcast.32), channel_id=1, source_target_pairs={{0,16},{8,24},{16,0},{24,8},{1,17},{9,25},{17,1},{25,9},{2,18},{10... | collective-permute-start | bytes 737288 | tf_op jit(solution)/shard_map/ppermute | solution.py:62
  95.8 7.7 %collective-permute-start.14 = (bf16[1,8,24,768]{3,2,1,0:T(8,128)(2,1)}, bf16[1,8,24,768]{3,2,1,0:T(8,128)(2,1)S(1)}, u32[]{:S(2)}, u32[]{:S(2)}) collective-permute-start(bf16[1,8,24,768]{3,2,1,0:T(8,128)(2,1)} %bitcast.12), channel_id=1, source_target_pairs={{0,16},{8,24},{16,0},{24,8},{1,17},{9,25},{17,1},{25,9},{2,18},{10... | collective-permute-start | bytes 884744 | tf_op jit(solution)/shard_map/ppermute | solution.py:62
  99.1 9.0 %collective-permute-start.19 = (bf16[2,8,20,768]{3,1,2,0:T(8,128)(2,1)}, bf16[2,8,20,768]{3,1,2,0:T(8,128)(2,1)}, u32[]{:S(2)}, u32[]{:S(2)}) collective-permute-start(bf16[2,8,20,768]{3,1,2,0:T(8,128)(2,1)} %copy.89), channel_id=1, source_target_pairs={{0,8},{8,0},{16,24},{24,16},{1,9},{9,1},{17,25},{25,17},{2,10},{10... | collective-permute-start | bytes 1474568 | tf_op jit(solution)/shard_map/ppermute | solution.py:62
  106.1 4.3 %collective-permute-start.15 = (bf16[2,8,24,768]{3,2,1,0:T(8,128)(2,1)}, bf16[2,8,24,768]{3,2,1,0:T(8,128)(2,1)}, u32[]{:S(2)}, u32[]{:S(2)}) collective-permute-start(bf16[2,8,24,768]{3,2,1,0:T(8,128)(2,1)} %pad_maximum_fusion.5), channel_id=1, source_target_pairs={{0,8},{8,0},{16,24},{24,16},{1,9},{9,1},{17,25},{25,17},{2,10},{10... | collective-permute-start | bytes 1769480 | tf_op jit(solution)/shard_map/ppermute | solution.py:62
  126.3 2.7 %collective-permute-start.20 = (bf16[2,8,24,768]{3,2,1,0:T(8,128)(2,1)S(1)}, bf16[2,8,24,768]{3,2,1,0:T(8,128)(2,1)S(1)}, u32[]{:S(2)}, u32[]{:S(2)}) collective-permute-start(bf16[2,8,24,768]{3,2,1,0:T(8,128)(2,1)S(1)} %fusion.37), channel_id=1, source_target_pairs={{0,8},{8,0},{16,24},{24,16},{1,9},{9,1},{17,25},{25,17},{2,10},{10... | collective-permute-start | bytes 1769480 | tf_op jit(solution)/shard_map/ppermute | solution.py:62
  128.4 2.2 collective-permute-start.16
  129.3 18.0 %copy-start.43 = (bf16[768]{0:T(1024)(128)(2,1)S(1)}, bf16[768]{0:T(1024)(128)(2,1)}, u32[]{:S(2)}) copy-start(bf16[768]{0:T(1024)(128)(2,1)} %param.17) | copy-start | bytes 4612
  129.3 9.0 %collective-permute-start.21 = (bf16[1,8,24,768]{3,2,1,0:T(8,128)(2,1)S(1)}, bf16[1,8,24,768]{3,2,1,0:T(8,128)(2,1)S(1)}, u32[]{:S(2)}, u32[]{:S(2)}) collective-permute-start(bf16[1,8,24,768]{3,2,1,0:T(8,128)(2,1)S(1)} %slice_bitcast_fusion.2), channel_id=1, source_target_pairs={{0,16},{8,24},{16,0},{24,8},{1,17},{9,25},{17,1},{25,9},{2,18},{10... | collective-permute-start | bytes 884744 | tf_op jit(solution)/shard_map/ppermute | solution.py:62
  139.1 18.4 %all-to-all-start.3 = ((bf16[8,24,768]{2,1,0:T(8,128)(2,1)}), bf16[8,24,768]{2,1,0:T(8,128)(2,1)}, u32[]{:S(2)}, u32[]{:S(2)}) async-start(bf16[8,24,768]{2,1,0:T(8,128)(2,1)} %fusion.46), calls=%async_computation.3 | async-start | bytes 589824 | tf_op jit(solution)/shard_map/all_to_all | solution.py:429
  144.2 84.0 %all-gather.5.cloned.1.call-start = ((), (), s32[]{:S(2)}) async-start(), calls=%async_computation.6 | async-start | bytes 1769472 | tf_op jit(solution)/shard_map/all_gather | solution.py:404
  146.0 7.2 %collective-permute-start.17 = (bf16[1,8,20,768]{3,1,2,0:T(8,128)(2,1)}, bf16[1,8,20,768]{3,1,2,0:T(8,128)(2,1)}, u32[]{:S(2)}, u32[]{:S(2)}) collective-permute-start(bf16[1,8,20,768]{3,1,2,0:T(8,128)(2,1)} %slice_bitcast_fusion.4), channel_id=1, source_target_pairs={{0,16},{8,24},{16,0},{24,8},{1,17},{9,25},{17,1},{25,9},{2,18},{10... | collective-permute-start | bytes 737288 | tf_op jit(solution)/shard_map/ppermute | solution.py:62
  157.5 34.9 %all-to-all-start.1 = ((bf16[8,20,768]{2,1,0:T(8,128)(2,1)}), bf16[8,20,768]{2,1,0:T(8,128)(2,1)}, u32[]{:S(2)}, u32[]{:S(2)}) async-start(bf16[8,20,768]{2,1,0:T(8,128)(2,1)} %copy.88), calls=%async_computation.1 | async-start | bytes 589824 | tf_op jit(solution)/shard_map/all_to_all | solution.py:435
  170.1 12.5 %copy-start.38 = (s32[128,128]{1,0:T(8,128)S(1)}, s32[128,128]{1,0:T(8,128)}, u32[]{:S(2)}) copy-start(s32[128,128]{1,0:T(8,128)} %copy-done.37) | copy-start | bytes 196612
  182.6 14.4 %copy-start.41 = (f32[32,2,10]{0,2,1:T(8,128)S(1)}, f32[32,2,10]{0,2,1:T(8,128)}, u32[]{:S(2)}) copy-start(f32[32,2,10]{0,2,1:T(8,128)} %add.180) | copy-start | bytes 7684
  184.1 1.3 collective-permute-start.22
  186.2 4.4 %collective-permute-start.23 = (f32[19,768]{1,0:T(8,128)S(1)}, f32[19,768]{1,0:T(8,128)S(1)}, u32[]{:S(2)}, u32[]{:S(2)}) collective-permute-start(f32[19,768]{1,0:T(8,128)S(1)} %fusion.75), channel_id=1, source_target_pairs={{0,16},{8,24},{16,0},{24,8},{1,17},{9,25},{17,1},{25,9},{2,18},{10... | collective-permute-start | bytes 175112 | tf_op jit(solution)/shard_map/ppermute | solution.py:62
  190.7 12.2 %collective-permute-start.24 = (f32[19,768]{1,0:T(8,128)S(1)}, f32[19,768]{1,0:T(8,128)}, u32[]{:S(2)}, u32[]{:S(2)}) collective-permute-start(f32[19,768]{1,0:T(8,128)S(1)} %add.184), channel_id=1, source_target_pairs={{0,1},{1,0},{2,3},{3,2},{4,5},{5,4},{6,7},{7,6},{8,9},{9,8},{10,11... | collective-permute-start | bytes 175112 | tf_op jit(solution)/shard_map/ppermute | solution.py:62
  192.4 29.3 %all-to-all-start.4 = ((bf16[8,384,128]{2,1,0:T(8,128)(2,1)}), bf16[8,384,128]{2,1,0:T(8,128)(2,1)}, u32[]{:S(2)}, u32[]{:S(2)}) async-start(bf16[8,384,128]{2,1,0:T(8,128)(2,1)} %get-tuple-element.32), calls=%async_computation.4 | async-start | bytes 1572864 | tf_op jit(solution)/shard_map/all_to_all | solution.py:481
  203.7 11.1 %collective-permute-start.25 = (f32[19,768]{1,0:T(8,128)S(1)}, f32[19,768]{1,0:T(8,128)S(1)}, u32[]{:S(2)}, u32[]{:S(2)}) collective-permute-start(f32[19,768]{1,0:T(8,128)S(1)} %add.185), channel_id=1, source_target_pairs={{0,2},{1,3},{2,0},{3,1},{4,6},{5,7},{6,4},{7,5},{8,10},{9,11},{10,... | collective-permute-start | bytes 175112 | tf_op jit(solution)/shard_map/ppermute | solution.py:62
  215.5 18.4 %collective-permute-start.26 = (f32[19,768]{1,0:T(8,128)}, f32[19,768]{1,0:T(8,128)}, u32[]{:S(2)}, u32[]{:S(2)}) collective-permute-start(f32[19,768]{1,0:T(8,128)} %add.186), channel_id=1, source_target_pairs={{0,4},{1,5},{2,6},{3,7},{4,0},{5,1},{6,2},{7,3},{8,12},{9,13},{10,... | collective-permute-start | bytes 175112 | tf_op jit(solution)/shard_map/ppermute | solution.py:62
  232.3 3.1 %collective-permute-start.27 = (bf16[2,192,384]{2,1,0:T(8,128)(2,1)S(1)}, bf16[2,192,384]{2,1,0:T(8,128)(2,1)S(1)}, u32[]{:S(2)}, u32[]{:S(2)}) collective-permute-start(bf16[2,192,384]{2,1,0:T(8,128)(2,1)S(1)} %slice_bitcast_fusion), channel_id=1, source_target_pairs={{0,8},{8,0},{16,24},{24,16},{1,9},{9,1},{17,25},{25,17},{2,10},{10... | collective-permute-start | bytes 884744 | tf_op jit(solution)/shard_map/ppermute | solution.py:62
  235.6 5.8 %collective-permute-start.28 = (bf16[1,192,384]{2,1,0:T(8,128)(2,1)S(1)}, bf16[1,192,384]{2,1,0:T(8,128)(2,1)S(1)}, u32[]{:S(2)}, u32[]{:S(2)}) collective-permute-start(bf16[1,192,384]{2,1,0:T(8,128)(2,1)S(1)} %slice_bitcast_fusion.6), channel_id=1, source_target_pairs={{0,16},{8,24},{16,0},{24,8},{1,17},{9,25},{17,1},{25,9},{2,18},{10... | collective-permute-start | bytes 442376 | tf_op jit(solution)/shard_map/ppermute | solution.py:62
  (37 other events, 59.6 us)
Sparse Core Ops, SparseCore 0:
  106.2 48.8 all-gather.2
  157.3 50.8 all-gather.4

commit v3 on v2

v3 whole, which is shorter than its diff:
```python
import functools

import jax
import jax.numpy as jnp
import numpy as np
from jax import lax
from jax.experimental import pallas as pl
from jax.experimental.pallas import tpu as pltpu
from jax.sharding import PartitionSpec as P

EPSILON = 1e-06
LIMITS = (12, 16, 23, 32, 46, 64, 91)
MASKED = -1000000000.0
HIGHEST = lax.Precision.HIGHEST
LOW = jnp.bfloat16
FULL = jnp.float32


def bucket_onehot(buckets, length):
    delta = np.arange(2 * length) - length
    magnitude = np.abs(delta)
    distant = 8 + sum((magnitude >= threshold).astype(np.int32) for threshold in LIMITS)
    ids = np.where(delta > 0, 16, 0) + np.where(magnitude < 8, magnitude, distant)
    return (ids[None, :] == np.arange(buckets)[:, None]).astype(np.float32)


def packing(local_experts, ranks, capacity, slab):
    table = np.zeros((local_experts, ranks, capacity, ranks, slab), np.float32)
    for e in range(local_experts):
        for r in range(ranks):
            for c in range(capacity):
                table[e, r, c, r, e * capacity + c] = 1.0
    return table.reshape(local_experts * ranks * capacity, ranks * slab)


def normalize(matrix, gain_vec):
    scale = lax.rsqrt(jnp.mean(matrix * matrix, axis=-1, keepdims=True) + EPSILON)
    return (matrix * scale * gain_vec, scale)


def norm_back(matrix, scale, gain_vec, incoming):
    weighted = incoming * gain_vec
    average = jnp.mean(matrix * weighted, axis=-1, keepdims=True)
    return (
        scale * weighted - matrix * (scale * scale * scale) * average,
        jnp.sum(incoming * matrix * scale, axis=0, keepdims=True),
    )


def swap(value, axis, mask):
    count = lax.axis_size(axis)
    return lax.ppermute(value, axis, [(i, i ^ mask) for i in range(count)])


def gather_bits(value, axis, masks):
    return jnp.concatenate([value] + [swap(value, axis, mask) for mask in masks], axis=0)


def fan_out(slabs):
    return [slabs[0]] + [swap(slabs[j], "expert", j) for j in range(1, len(slabs))]


def gather_list(value):
    found = {0: value}
    bit = lax.axis_size("dp") // 2
    while bit >= 1:
        found.update({index ^ bit: swap(item, "dp", bit) for index, item in found.items()})
        bit = bit // 2
    return [found[index] for index in range(len(found))]


def scatter_list(items, last=True):
    bit = 1
    while len(items) > 1:
        taken = [swap(item, "dp", bit) for item in items[1::2]]
        if len(items) == 2 and not last:
            return items[0], taken[0]
        items = [
            (kept.astype(FULL) + got.astype(FULL)).astype(kept.dtype)
            for kept, got in zip(items[0::2], taken)
        ]
        bit = bit * 2
    return items[0]


def all_sum(value):
    for axis in ("dp", "expert"):
        bit = 1
        while bit < lax.axis_size(axis):
            value = value + swap(value, axis, bit)
            bit = bit * 2
    return value


def gather_pieces(payload, early):
    ranks, dps = lax.axis_size("expert"), lax.axis_size("dp")
    half = payload.shape[0] // 2
    far = list(range(0, ranks, 2))
    sides = {"x": ("expert", [0, 1]), "y": ("dp", list(range(0, dps, 2)))}
    values = [
        gather_bits(payload[index * half : (index + 1) * half][None], "expert", far[1:])
        for index in range(2)
    ]
    values, early = lax.optimization_barrier((values, early))
    pieces, places = [], []
    for index, order in enumerate(("xy", "yx")):
        axis, masks = sides[order[0]]
        value = gather_bits(values[index][None], axis, masks[1:])
        other_axis, other_masks = sides[order[1]]
        found = [(value, 0)] + [(swap(value, other_axis, m), m) for m in other_masks[1:]]
        found = [(v, m, 0) for v, m in found] + [(swap(v, "dp", 1), m, 1) for v, m in found]
        for piece, mask, core in found:
            offsets = []
            for first in masks:
                for low in far:
                    x_mask, y_mask = (first, mask) if order == "xy" else (mask, first)
                    offsets.append((low ^ x_mask, y_mask ^ core))
            pieces.append(piece)
            places.append((index, offsets))
    return pieces, places, early


def place_weights(places, piece_refs, w_ref, sem):
    my_expert, my_dp = lax.axis_index("expert"), lax.axis_index("dp")
    copies = []
    for ref, (half, offsets) in zip(piece_refs, places):
        low_count, rows = ref.shape[1], ref.shape[2]
        for index, (e_mask, d_mask) in enumerate(offsets):
            start = (my_dp ^ d_mask) * (2 * rows) + half * rows
            copies.append(
                pltpu.make_async_copy(
                    ref.at[index // low_count, index % low_count],
                    w_ref.at[my_expert ^ e_mask, pl.ds(pl.multiple_of(start, 16), rows), :],
                    sem,
                )
            )
    for copy in copies:
        copy.start()
    return copies


def dot(left, right, dims=((1,), (0,)), precision=None):
    return lax.dot_general(
        left, right, (dims, ((), ())), precision=precision, preferred_element_type=FULL
    )


NT = ((1,), (1,))
TN = ((0,), (0,))


def grid_of(rows):
    sub = lax.broadcasted_iota(jnp.int32, (rows, 128), 0)
    lane = lax.broadcasted_iota(jnp.int32, (rows, 128), 1)
    return sub, lane


def row_to_column(row, rows, shift=0):
    sub, lane = grid_of(rows)
    column = jnp.sum(jnp.where(lane == sub + shift, row, 0.0), axis=1, keepdims=True)
    return jnp.broadcast_to(column, (rows, 128))


def column_to_row(column, shift=0):
    sub, lane = grid_of(column.shape[0])
    return jnp.sum(jnp.where(lane == sub + shift, column, 0.0), axis=0, keepdims=True)


def turn(value, shift):
    return pltpu.roll(value, shift % value.shape[1], 1)


def slide(value, direction):
    sub = lax.broadcasted_iota(jnp.int32, value.shape, 0)
    for bit in (1, 2, 4):
        value = jnp.where((sub & bit) != 0, turn(value, direction * bit), value)
    return value


def slid_rows(row, count):
    value = slide(jnp.broadcast_to(row, (8, row.shape[1])), 1)
    while value.shape[0] < count:
        value = jnp.concatenate([value, turn(value, value.shape[0])], axis=0)
    return value


def slid_sum(value):
    while value.shape[0] > 8:
        half = value.shape[0] // 2
        value = value[:half] + turn(value[half:], -half)
    return jnp.sum(slide(value, -1), axis=0, keepdims=True)


def early_kernel(
    ranks, local_experts, capacity, slab, tokens_ref, routes_ref, gain_ref, d_out_ref, table_ref,
    onehot_ref, normed_ref, hits_ref, mask_ref, mask_t_ref, bias_ref, *up_refs
):
    length = tokens_ref.shape[0]
    normed, _ = normalize(tokens_ref[...].astype(FULL), gain_ref[...].astype(FULL))
    normed_ref[...] = normed.astype(LOW)
    experts = hits_ref.shape[1]
    routes = jnp.broadcast_to(routes_ref[...].astype(FULL), (length, length)).T
    route = routes[:, :1].astype(jnp.int32)
    lanes = lax.broadcasted_iota(jnp.int32, (length, experts), 1)
    hits = (lanes == route).astype(FULL)
    hits_ref[...] = hits
    row = lax.broadcasted_iota(jnp.int32, (length, length), 0)
    col = lax.broadcasted_iota(jnp.int32, (length, length), 1)
    before = dot((col < row).astype(FULL).astype(LOW), hits.astype(LOW))
    placed = jnp.sum(before * hits, axis=1, keepdims=True).astype(jnp.int32)
    rank = jnp.zeros_like(route)
    for r in range(1, ranks):
        rank = rank + (route >= r * local_experts).astype(jnp.int32)
    spot = (rank ^ lax.axis_index("expert")) * slab
    spot = spot + (route - rank * local_experts) * capacity + placed
    spot = jnp.where(placed < capacity, spot, -1)
    places = lax.broadcasted_iota(jnp.int32, (length, ranks * slab), 1)
    mask = (places == spot).astype(FULL)
    mask_ref[...] = mask.astype(LOW)
    mask_t = mask.T.astype(LOW)
    mask_t_ref[...] = mask_t
    slabs = dot(mask_t, d_out_ref[...])
    for r in range(ranks):
        up_refs[r][...] = slabs[r * slab : (r + 1) * slab].astype(LOW)
    values = dot(table_ref[...], onehot_ref[...])
    for h in range(bias_ref.shape[0]):
        bias_ref[h] = slid_rows(values[h : h + 1], length)[:, length:]


def forward_kernel(
    places, slab, rank_slots, tokens_ref, normed_ref, seg_ref, bias_ref, gain_ref,
    router_t_ref, hits_ref, mask_t_ref, *rest
):
    count = len(places)
    piece_refs, rest = rest[:count], rest[count:]
    heads_ref, weights_ref, attended_ref, hidden_ref, chance_ref = rest[:5]
    slab_refs = rest[5:-4]
    w_ref, qkv_ref, att_t_ref, sem = rest[-4:]
    copies = place_weights(places, piece_refs, w_ref, sem)
    ranks, width, columns = w_ref.shape
    cols = columns // 4
    head_count = weights_ref.shape[0]
    head = width // head_count
    length = tokens_ref.shape[0]
    segments = jnp.broadcast_to(seg_ref[...].astype(FULL), (length, length))
    same_doc = segments == segments.T
    normed = normed_ref[...]
    for copy in copies:
        copy.wait()
    for e in range(ranks):
        turned = dot(normed, w_ref[e]).T
        for m in range(3):
            qkv_ref[m, e * cols : (e + 1) * cols, :] = turned[m * cols : (m + 1) * cols]
    heads_ref[...] = qkv_ref[...].astype(LOW)
    for h in range(head_count):
        rows = slice(h * head, (h + 1) * head)
        scores = dot(heads_ref[0, rows, :], heads_ref[1, rows, :], TN) * head ** (-0.5)
        scores = jnp.where(same_doc, scores + bias_ref[h], MASKED)
        grown = jnp.exp(scores - jnp.max(scores, axis=1, keepdims=True))
        weights = grown / jnp.sum(grown, axis=1, keepdims=True)
        weights_ref[h] = weights
        att_t_ref[rows, :] = dot(heads_ref[2, rows, :], weights.astype(LOW), NT)
    attended = att_t_ref[...].T.astype(LOW)
    attended_ref[...] = attended
    low_lane = 3 * cols // 128 * 128
    for e in range(ranks):
        turned = dot(attended, w_ref[e, :, low_lane:]).T
        att_t_ref[e * cols : (e + 1) * cols, :] = turned[3 * cols - low_lane :]
    hidden = tokens_ref[...].astype(FULL) + att_t_ref[...].T
    hidden_ref[...] = hidden
    normed_two, _ = normalize(hidden, gain_ref[...].astype(FULL))
    logits = dot(normed_two, router_t_ref[...].astype(FULL), NT, HIGHEST)
    grown = jnp.exp(logits - jnp.max(logits, axis=1, keepdims=True))
    chance = grown / jnp.sum(grown, axis=1, keepdims=True)
    chance_ref[...] = chance
    gate = jnp.sum(chance * hits_ref[...], axis=1, keepdims=True)
    mask_t = mask_t_ref[...]
    slots = dot(mask_t, normed_two.astype(LOW))
    gates = dot(mask_t.astype(FULL), jnp.broadcast_to(gate, (length, 128)), precision=HIGHEST)
    sub, _ = grid_of(slab)
    for r in range(ranks):
        mine = gates[r * slab : (r + 1) * slab]
        high = mine.astype(LOW).astype(FULL)
        row = column_to_row(high) + column_to_row(mine - high, 64)
        rows = slots[r * slab : (r + 1) * slab]
        start = rows[:, :128] + jnp.where(sub == rank_slots, row, 0.0)
        slab_refs[r][:, :128] = start.astype(LOW)
        slab_refs[r][:, 128:] = rows[:, 128:].astype(LOW)


def upstream_kernel(pack_ref, w_out_ref, *rest):
    piece_refs, (rows_ref, act_ref) = rest[:-2], rest[-2:]
    local_experts = w_out_ref.shape[0]
    chunk = pack_ref.shape[0] // local_experts
    for p, piece in enumerate(piece_refs):
        packed = dot(pack_ref[...], piece[...]).astype(LOW)
        for e in range(local_experts):
            rows_ref[e, p * chunk : (p + 1) * chunk, :] = packed[e * chunk : (e + 1) * chunk]
    for e in range(local_experts):
        act_ref[e] = dot(rows_ref[e], w_out_ref[e], NT)


def unpack(pack_t, rows_ref, p, chunk):
    rows = [rows_ref[e, p * chunk : (p + 1) * chunk, :] for e in range(rows_ref.shape[0])]
    return dot(pack_t, jnp.concatenate(rows, axis=0))


def expert_kernel(
    count, slab, rank_slots, pack_ref, pack_t_ref, w_in_ref, up_act_ref, *rest
):
    piece_refs, rest = rest[:count], rest[count:]
    back_refs, rest = rest[:count], rest[count:]
    rows_ref, act_ref, pre_grad_ref, gates_ref, pre_ref, back_ref, part_ref = rest
    local_experts = w_in_ref.shape[0]
    chunk = pack_ref.shape[0] // local_experts
    ranks = pack_ref.shape[1] // slab
    pack, pack_t = pack_ref[...], pack_t_ref[...]
    for p, piece in enumerate(piece_refs):
        packed = dot(pack, piece[...]).astype(LOW)
        tile = piece[:, :128].astype(FULL)
        spread = []
        for shift in (0, 64):
            columns = [
                row_to_column(tile[r * slab + rank_slots : r * slab + rank_slots + 1], slab, shift)
                for r in range(ranks)
            ]
            spread.append(dot(pack, jnp.concatenate(columns, axis=0).astype(LOW)))
        gates = spread[0] + spread[1]
        for e in range(local_experts):
            rows_ref[e, p * chunk : (p + 1) * chunk, :] = packed[e * chunk : (e + 1) * chunk]
            gates_ref[e, p * chunk : (p + 1) * chunk, :] = gates[e * chunk : (e + 1) * chunk]
    root = np.float32(np.sqrt(2.0 / np.pi))
    step = 16
    for e in range(local_experts):
        pre_ref[...] = dot(rows_ref[e], w_in_ref[e])

        def body(index, carry):
            span = pl.ds(pl.multiple_of(index * step, step), step)
            pre = pre_ref[span, :]
            up = up_act_ref[e, span, :]
            square = pre * pre
            curve = jnp.tanh(root * pre * (1.0 + 0.044715 * square))
            rise = 0.5 + 0.5 * curve
            act = (pre * rise).astype(LOW)
            act_ref[e, span, :] = act
            slope = rise + pre * (rise * (1.0 - curve)) * (root + 3 * 0.044715 * root * square)
            gate = gates_ref[e, span, :][:, :1]
            pre_grad_ref[e, span, :] = (slope * (up * gate)).astype(LOW)
            part = jnp.sum(act.astype(FULL) * up, axis=1, keepdims=True)
            part_ref[e, span, :] = jnp.broadcast_to(part, (step, 128)).astype(LOW)
            return carry

        lax.fori_loop(0, pre_ref.shape[0] // step, body, 0, unroll=2)
        back_ref[e] = dot(pre_grad_ref[e], w_in_ref[e], NT).astype(LOW)
    sub, _ = grid_of(slab)
    for p in range(count):
        rows = unpack(pack_t, back_ref, p, chunk)
        parts = unpack(pack_t, part_ref, p, chunk)
        pieces = []
        for r in range(ranks):
            span = slice(r * slab, (r + 1) * slab)
            row = column_to_row(parts[span])
            pieces.append(rows[span, :128] + jnp.where(sub == rank_slots, row, 0.0))
        back_refs[p][:, :128] = jnp.concatenate(pieces, axis=0).astype(LOW)
        back_refs[p][:, 128:] = rows[:, 128:].astype(LOW)


def expert_grad_kernel(
    count, pack_t_ref, w_out_ref, rows_ref, act_ref, pre_grad_ref, gates_ref, up_rows_ref, *rest
):
    out_refs, (g_in_ref, g_out_ref, returned_ref) = rest[:count], rest[count:]
    local_experts = w_out_ref.shape[0]
    chunk = rows_ref.shape[1] // count
    pack_t = pack_t_ref[...]
    for e in range(local_experts):
        returned_ref[e] = dot(act_ref[e], w_out_ref[e]).astype(LOW)
    for p in range(count):
        out_refs[p][...] = unpack(pack_t, returned_ref, p, chunk).astype(LOW)
    for e in range(local_experts):
        g_in_ref[e] = dot(rows_ref[e], pre_grad_ref[e], TN)
        slot_grad = (up_rows_ref[e].astype(FULL) * gates_ref[e][:, :1]).astype(LOW)
        g_out_ref[e] = dot(act_ref[e], slot_grad, TN)


def split_kernel(first_ref, second_ref, *out_refs):
    slab = out_refs[0].shape[0]
    total = first_ref[...].astype(FULL) + second_ref[...].astype(FULL)
    for r, ref in enumerate(out_refs):
        ref[...] = total[r * slab : (r + 1) * slab].astype(LOW)


def joined(refs):
    return jnp.concatenate([ref[...].astype(FULL) for ref in refs], axis=0).astype(LOW)


def backward_kernel(
    places, rank_slots, tokens_ref, gain_one_ref, gain_two_ref, router_t_ref, hits_ref, mask_ref,
    up_ref, hidden_ref, chance_ref, heads_ref, weights_ref, onehot_ref, *rest
):
    count = len(places)
    piece_refs, rest = rest[:count], rest[count:]
    w_ref, turned_ref, grads_ref, bias_ref, sent_ref, sem = rest[-6:]
    ranks, width, columns = w_ref.shape
    back_refs, rest = rest[:ranks], rest[ranks:-6]
    d_input_ref, small_ref = rest[:2]
    factor_refs = rest[2:]
    copies = place_weights(places, piece_refs, w_ref, sem)
    cols = columns // 4
    head_count = weights_ref.shape[0]
    head = width // head_count
    factor = head ** (-0.5)
    length = tokens_ref.shape[0]
    slab = back_refs[0].shape[0]
    hidden = hidden_ref[...]
    gain_two = gain_two_ref[...].astype(FULL)
    normed_two, scale_two = normalize(hidden, gain_two)
    mask = mask_ref[...]
    chance, hits = chance_ref[...], hits_ref[...]
    gate = jnp.sum(chance * hits, axis=1, keepdims=True)
    spread = [
        row_to_column(ref[:, :128].astype(FULL)[rank_slots : rank_slots + 1], slab)
        for ref in back_refs
    ]
    gate_grad = dot(mask, jnp.concatenate(spread, axis=0).astype(LOW))[:, :1]
    logit_grad = chance * (hits - gate) * gate_grad
    experts = hits.shape[1]
    small_ref[:experts, :] = dot(logit_grad, normed_two, TN, HIGHEST)
    router_t = router_t_ref[...].astype(FULL)
    normed_two_grad = dot(logit_grad, router_t, precision=HIGHEST) + dot(mask, joined(back_refs))
    hidden_part, ffn_gain_grad = norm_back(hidden, scale_two, gain_two, normed_two_grad)
    hidden_grad = up_ref[...].astype(FULL) + hidden_part
    turned_ref[...] = hidden_grad.astype(LOW).astype(FULL).T
    for copy in copies:
        copy.wait()
    low_lane = 3 * cols // 128 * 128
    att_grad = None
    for e in range(ranks):
        own = turned_ref[e * cols : (e + 1) * cols, :]
        if 3 * cols > low_lane:
            own = jnp.concatenate([jnp.zeros((3 * cols - low_lane, 128), FULL), own], axis=0)
        part = dot(w_ref[e, :, low_lane:], own.astype(LOW))
        att_grad = part if att_grad is None else att_grad + part
    att_grad = att_grad.astype(LOW)
    for h in range(head_count):
        rows = slice(h * head, (h + 1) * head)
        own = att_grad[rows]
        weights = weights_ref[h]
        grads_ref[2, rows, :] = dot(own, weights.astype(LOW))
        prob_grad = dot(own, heads_ref[2, rows, :], TN)
        score_grad = weights * (prob_grad - jnp.sum(prob_grad * weights, axis=1, keepdims=True))
        score_grad = score_grad.astype(LOW)
        grads_ref[0, rows, :] = dot(heads_ref[1, rows, :], score_grad, NT) * factor
        grads_ref[1, rows, :] = dot(heads_ref[0, rows, :], score_grad) * factor
        wide = [jnp.zeros((length, length), FULL), score_grad.astype(FULL)]
        bias_ref[h : h + 1, :] = slid_sum(jnp.concatenate(wide, axis=1))
    total = None
    for e in range(ranks):
        span = slice(e * cols, (e + 1) * cols)
        held = [grads_ref[m, span, :] for m in range(3)] + [jnp.zeros((cols, 128), FULL)]
        part = dot(w_ref[e], jnp.concatenate(held, axis=0).astype(LOW))
        total = part if total is None else total + part
        sent = [grads_ref[m, span, :] for m in range(3)] + [turned_ref[span, :]]
        sent_ref[e] = jnp.concatenate(sent, axis=0)
    for e in range(ranks):
        factor_refs[e][...] = sent_ref[lax.axis_index("expert") ^ e].astype(LOW)
    inputs = tokens_ref[...].astype(FULL)
    gain_one = gain_one_ref[...].astype(FULL)
    _, scale_one = normalize(inputs, gain_one)
    norm_part, attn_gain_grad = norm_back(inputs, scale_one, gain_one, total.T)
    d_input_ref[...] = hidden_grad + norm_part
    sums = dot(bias_ref[...], onehot_ref[...], NT, HIGHEST)
    small_ref[experts : experts + 1, :] = ffn_gain_grad
    small_ref[experts + 1 : experts + 2, :] = attn_gain_grad
    small_ref[experts + 2 :, :] = jnp.zeros((small_ref.shape[0] - experts - 2, width), FULL)
    small_ref[experts + 2 : experts + 2 + head_count, : sums.shape[1]] = sums


def product_kernel(
    ranks, dps, rank_slots, normed_ref, attended_ref, hidden_ref, chance_ref, hits_ref, mask_ref, *rest
):
    factor_refs, rest = rest[:ranks], rest[ranks:]
    returned_refs, rest = rest[:ranks], rest[ranks:]
    output_ref, total_ref = rest[0], rest[-1]
    piece_refs = rest[1:-1]
    length = hidden_ref.shape[0]
    cols = factor_refs[0].shape[0] // 4
    first, second = None, None
    for j, ref in enumerate(factor_refs):
        span = lax.axis_index("expert") ^ j
        held = ref[...].astype(FULL)
        part = dot(held[: 3 * cols].astype(LOW), normed_ref[span])
        first = part if first is None else first + part
        part = dot(held[3 * cols :].astype(LOW), attended_ref[span])
        second = part if second is None else second + part
    total = jnp.concatenate([first, second], axis=0).T
    rows = piece_refs[0].shape[0]
    for j in range(dps):
        total_ref[j] = total[j * rows : (j + 1) * rows]
    for j, ref in enumerate(piece_refs):
        ref[...] = total_ref[lax.axis_index("dp") ^ j].astype(LOW)
    gate = jnp.sum(chance_ref[...] * hits_ref[...], axis=1, keepdims=True)
    fetched = dot(mask_ref[...], joined(returned_refs))
    output_ref[...] = (hidden_ref[...] + gate * fetched).astype(LOW)


VMEM = pl.BlockSpec(memory_space=pltpu.VMEM)
ANY = pl.BlockSpec(memory_space=pl.ANY)
LIMIT = 60 * 1024 * 1024


def shaped(dtype, *shape):
    return jax.ShapeDtypeStruct(shape, dtype)


def call(kernel, name, out_shape, args, pieces=(), scratch=(), more=()):
    return pl.pallas_call(
        kernel,
        out_shape=tuple(out_shape),
        in_specs=[VMEM] * len(args) + [ANY] * len(pieces) + [VMEM] * len(more),
        out_specs=(VMEM,) * len(out_shape),
        scratch_shapes=list(scratch),
        compiler_params=pltpu.CompilerParams(vmem_limit_bytes=LIMIT),
        name=name,
    )(*args, *pieces, *more)


def per_device(
    tokens,
    seg_ids,
    routes,
    attn_gain,
    w_query,
    w_key,
    w_value,
    w_output,
    rel_bias,
    ffn_gain,
    w_router,
    w_in,
    w_out,
    d_out,
):
    length, model_width = tokens.shape
    bucket_count, head_count = rel_bias.shape
    experts_total = w_router.shape[1]
    local_experts, _, hidden_here = w_in.shape
    ranks, dps = lax.axis_size("expert"), lax.axis_size("dp")
    capacity = length * 5 // (4 * experts_total)
    rank_slots = local_experts * capacity
    slab = -(-(rank_slots + 1) // 8) * 8
    rows_here, columns_here = w_query.shape
    inner_width = dps * rows_here
    packed_rows = dps * ranks * capacity
    gain_one = attn_gain.reshape(1, model_width)
    gain_two = ffn_gain.reshape(1, model_width)
    router_t = w_router.T
    pack = packing(local_experts, ranks, capacity, slab)
    pack, pack_t = jnp.asarray(pack, LOW), jnp.asarray(pack.T, LOW)

    normed_low, hits, mask, mask_t, bias_full, *up_slabs = call(
        functools.partial(early_kernel, ranks, local_experts, capacity, slab),
        "early",
        [
            shaped(LOW, length, model_width),
            shaped(FULL, length, experts_total),
            shaped(LOW, length, ranks * slab),
            shaped(LOW, ranks * slab, length),
            shaped(FULL, head_count, length, length),
        ]
        + [shaped(LOW, slab, model_width)] * ranks,
        [
            tokens,
            routes.reshape(1, length),
            gain_one,
            d_out,
            rel_bias.T,
            jnp.asarray(bucket_onehot(bucket_count, length), LOW),
        ],
    )

    payload = jnp.concatenate([w_query, w_key, w_value, w_output], axis=1)
    pieces, places, (normed_low, hits, mask, mask_t, bias_full, up_slabs) = gather_pieces(
        payload, (normed_low, hits, mask, mask_t, bias_full, up_slabs)
    )
    pieces, normed_later, up_slabs = lax.optimization_barrier((pieces, normed_low, up_slabs))
    normed_all = lax.all_gather(normed_later, "expert", axis=0)

    w_shape = (ranks, inner_width, 4 * columns_here)
    heads, weights, attended, hidden, chance, *slabs = call(
        functools.partial(forward_kernel, places, slab, rank_slots),
        "attention_forward",
        [
            shaped(LOW, 3, inner_width, length),
            shaped(FULL, head_count, length, length),
            shaped(LOW, length, inner_width),
            shaped(FULL, length, model_width),
            shaped(FULL, length, experts_total),
        ]
        + [shaped(LOW, slab, model_width)] * ranks,
        [tokens, normed_low, seg_ids, bias_full, gain_two, router_t, hits, mask_t],
        pieces,
        [
            pltpu.VMEM(w_shape, LOW),
            pltpu.VMEM((3, inner_width, length), FULL),
            pltpu.VMEM((inner_width, length), FULL),
            pltpu.SemaphoreType.DMA,
        ],
    )

    up_pieces = gather_list(jnp.concatenate(fan_out(up_slabs), axis=0))
    row_pieces = gather_list(jnp.concatenate(fan_out(slabs), axis=0))
    attended_all = lax.all_gather(attended, "expert", axis=0)
    by_expert = (local_experts, packed_rows)
    up_rows, up_act = call(
        upstream_kernel,
        "upstream_rows",
        [shaped(LOW, *by_expert, model_width), shaped(FULL, *by_expert, hidden_here)],
        [pack, w_out, *up_pieces],
    )

    *back, slot_rows, activated, pre_grad, gates = call(
        functools.partial(expert_kernel, dps, slab, rank_slots),
        "experts",
        [shaped(LOW, ranks * slab, model_width)] * dps
        + [
            shaped(LOW, *by_expert, model_width),
            shaped(LOW, *by_expert, hidden_here),
            shaped(LOW, *by_expert, hidden_here),
            shaped(FULL, *by_expert, 128),
        ],
        [pack, pack_t, w_in, up_act, *row_pieces],
        scratch=[
            pltpu.VMEM((packed_rows, hidden_here), FULL),
            pltpu.VMEM((*by_expert, model_width), LOW),
            pltpu.VMEM((*by_expert, 128), LOW),
        ],
    )
    slab_shapes = [shaped(LOW, slab, model_width)] * ranks
    back = fan_out(call(split_kernel, "back_slabs", slab_shapes, scatter_list(back, last=False)))
    *returned, first_grad, second_grad = call(
        functools.partial(expert_grad_kernel, dps),
        "expert_gradients",
        [shaped(LOW, ranks * slab, model_width)] * dps
        + [shaped(FULL, *w_in.shape), shaped(FULL, *w_out.shape)],
        [pack_t, w_out, slot_rows, activated, pre_grad, gates, up_rows],
        scratch=[pltpu.VMEM((*by_expert, model_width), LOW)],
    )
    returned = fan_out(
        call(split_kernel, "returned_slabs", slab_shapes, scatter_list(returned, last=False))
    )

    small_rows = -(-(experts_total + 2 + head_count) // 8) * 8
    d_input, small, *factors = call(
        functools.partial(backward_kernel, places, rank_slots),
        "attention_backward",
        [
            shaped(FULL, length, model_width),
            shaped(FULL, small_rows, model_width),
        ]
        + [shaped(LOW, 4 * columns_here, length)] * ranks,
        [
            tokens,
            gain_one,
            gain_two,
            router_t,
            hits,
            mask,
            d_out,
            hidden,
            chance,
            heads,
            weights,
            jnp.asarray(bucket_onehot(bucket_count, length), FULL),
        ],
        pieces,
        [
            pltpu.VMEM(w_shape, LOW),
            pltpu.VMEM((inner_width, length), FULL),
            pltpu.VMEM((3, inner_width, length), FULL),
            pltpu.VMEM((head_count, 2 * length), FULL),
            pltpu.VMEM((ranks, 4 * columns_here, length), FULL),
            pltpu.SemaphoreType.DMA,
        ],
        back,
    )

    factors = fan_out(factors)
    small = all_sum(small)
    output, *grads = call(
        functools.partial(product_kernel, ranks, dps, rank_slots),
        "weight_gradients",
        [shaped(LOW, length, model_width)] + [shaped(LOW, rows_here, 4 * columns_here)] * dps,
        [normed_all, attended_all, hidden, chance, hits, mask, *factors, *returned],
        scratch=[pltpu.VMEM((dps, rows_here, 4 * columns_here), FULL)],
    )
    kept, got = scatter_list(grads, last=False)
    grads = kept.astype(FULL) + got.astype(FULL)
    g_query, g_key, g_value, g_output = (
        grads[:, i * columns_here : (i + 1) * columns_here] for i in range(4)
    )
    g_router = small[:experts_total].T
    g_ffn_gain, g_attn_gain = small[experts_total], small[experts_total + 1]
    g_rel_bias = small[experts_total + 2 : experts_total + 2 + head_count, :bucket_count].T
    return (
        output,
        d_input,
        g_attn_gain,
        g_query,
        g_key,
        g_value,
        g_output,
        g_rel_bias,
        g_ffn_gain,
        g_router,
        first_grad,
        second_grad,
    )


def solution(mesh):
    return jax.shard_map(
        per_device,
        mesh=mesh,
        in_specs=(
            P(("dp", "expert"), None),
            P(("dp", "expert"), None),
            P(("dp", "expert"), None),
            P(),
            P("dp", "expert"),
            P("dp", "expert"),
            P("dp", "expert"),
            P("dp", "expert"),
            P(),
            P(),
            P(),
            P("expert", None, "dp"),
            P("expert", "dp", None),
            P(("dp", "expert"), None),
        ),
        out_specs=(
            P(("dp", "expert"), None),
            P(("dp", "expert"), None),
            P(),
            P("dp", "expert"),
            P("dp", "expert"),
            P("dp", "expert"),
            P("dp", "expert"),
            P(),
            P(),
            P(),
            P("expert", None, "dp"),
            P("expert", "dp", None),
        ),
        check_vma=False,
    )
```

time: 253 us -> 246 us (0.972)
  Pallas kernels: 20.4 us -> 58.1 us
  local copies, waits for them, and re-layouts: 49.9 us -> 15 us
  matrix products: 28.3 us -> 0 us
  starting transfers between devices: 57.8 us -> 84.9 us
  other arithmetic: 26.5 us -> 6.8 us
  waiting for transfers between devices: 52.5 us -> 65.2 us
    ppermute x29 -> x69, starting transfers between devices: 34.2 us -> 84.9 us  [swap(): return lax.ppermute(value, axis, [(i, i ^ mask) for i in range(count)])]
    pallas_call x2 -> x9, Pallas kernels: 20.4 us -> 58.1 us  [call(): pl.pallas_call(kernel, out_shape=tuple(out_shape), in_specs=[VMEM] * len(...]
    dot_general x12 -> x0, matrix products: 28.3 us -> none  [the longest x1 5.85 us: per_device(): jnp.einsum('secf,secd->efd', activated, grad_rows, preferred_element_type...]
    ppermute x29 -> x69, waiting for transfers between devices: 39.5 us -> 65.1 us  [swap(): return lax.ppermute(value, axis, [(i, i ^ mask) for i in range(count)])]
    all_to_all x5 -> x0, starting transfers between devices: 23.3 us -> none  [the longest x1 5.17 us: per_device(): lax.all_to_all(back, 'expert', split_axis=0, concat_axis=0, tiled=True)]
    unnamed x102 -> x116, local copies, waits for them, and re-layouts: 26 us -> 10.4 us
    all_to_all x5 -> x0, waiting for transfers between devices: 12.9 us -> none  [the longest x1 8.78 us: per_device(): lax.all_to_all(outgoing, 'expert', split_axis=0, concat_axis=0, tiled=True)]
    concatenate x7 -> x0, other arithmetic: 6.42 us -> none  [the longest x4 5.37 us: gather_rel(): stacked = jnp.concatenate([stacked, other], axis=0)]
  transfers between devices with their start and end apart: 36 -> 71, of which waited for: 14 -> 28; matrix products, arithmetic and copies ran while one was open for 31% -> 5% of each run, Pallas kernels for 8% -> 22%
where the time goes in v3:
time: 246 us; the launch traced here: 245 us
  starting transfers between devices  84.9 us (35%)
  waiting for transfers between devices  65.2 us (27%)
  Pallas kernels  58.1 us (24%)
  local copies, waits for them, and re-layouts  15 us (6%)
  between operations  14.8 us (6%)
  other arithmetic  6.8 us (3%)
    ppermute x69, starting transfers between devices, swap(): return lax.ppermute(value, axis, [(i, i ^ mask) for i in range(count)])  84.9 us
    ppermute x69, waiting for transfers between devices, swap(): return lax.ppermute(value, axis, [(i, i ^ mask) for i in range(count)])  65.1 us
    pallas_call x9, Pallas kernels, call(): pl.pallas_call(kernel, out_shape=tuple(out_shape), in_specs=[VMEM] * len(...  58.1 us
    unnamed x116, local copies, waits for them, and re-layouts  10.4 us
  transfers between devices with their start and end apart: 71, of which 28 were waited for; matrix products, arithmetic and copies ran while one was open for 5% of the time, Pallas kernels for 22%

profile of v3, /device:TPU:0, one launch (start us, length us, event | category | flops | bytes accessed | tf_op | source)
XLA Modules:
  0.0 244.8 jit_solution(3825476170721234760)
XLA Ops:
  8.3 5.1 %collective-permute-start.5 = (bf16[1,96,384]{2,1,0:T(8,128)(2,1)S(1)}, bf16[1,96,384]{2,1,0:T(8,128)(2,1)S(1)}, u32[]{:S(2)}, u32[]{:S(2)}) collective-permute-start(bf16[1,96,384]{2,1,0:T(8,128)(2,1)S(1)} %get-tuple-element.228), channel_id=1, source_target_pairs={{0,6},{1,7},{2,4},{3,5},{4,2},{5,3},{6,0},{7,1},{8,14},{9,15},{10,... | collective-permute-start | bytes 221192 | tf_op jit(solution)/shard_map/ppermute | solution.py:52
  14.0 3.7 %collective-permute-start.2 = (bf16[1,96,384]{2,1,0:T(8,128)(2,1)S(1)}, bf16[1,96,384]{2,1,0:T(8,128)(2,1)S(1)}, u32[]{:S(2)}, u32[]{:S(2)}) collective-permute-start(bf16[1,96,384]{2,1,0:T(8,128)(2,1)S(1)} %get-tuple-element.229), channel_id=1, source_target_pairs={{0,6},{1,7},{2,4},{3,5},{4,2},{5,3},{6,0},{7,1},{8,14},{9,15},{10,... | collective-permute-start | bytes 221192 | tf_op jit(solution)/shard_map/ppermute | solution.py:52
  19.0 3.4 %early.1 = (bf16[128,768]{1,0:T(8,128)(2,1)}, f32[128,16]{1,0:T(8,128)}, bf16[128,192]{1,0:T(8,128)(2,1)}, bf16[192,128]{1,0:T(8,128)(2,1)}, f32[12,128,128]{2,1...) custom-call(bf16[128,768]{1,0:T(8,128)(2,1)} %tokens_ref.5, ...), custom_call_target="tpu_custom_call" | custom-call | tf_op jit(solution)/shard_map/early/pallas_call | solution.py:516
  23.5 2.5 %collective-permute-done.1 = bf16[1,96,384]{2,1,0:T(8,128)(2,1)S(1)} collective-permute-done((bf16[1,96,384]{2,1,0:T(8,128)(2,1)S(1)}, bf16[1,96,384]{2,1,0:T(8,128)(2,1)S(1)}, u32[]{:S(2)}, u32[]{:S(2)}) %collective-permute-start.1) | collective-permute-done | bytes 73760 | tf_op jit(solution)/shard_map/ppermute | solution.py:52
  26.9 1.6 collective-permute-start.6
  28.6 1.5 collective-permute-start.10
  30.1 5.0 %collective-permute-done.6 = bf16[1,4,96,384]{3,2,1,0:T(8,128)(2,1)S(1)} collective-permute-done((bf16[1,4,96,384]{3,2,1,0:T(8,128)(2,1)S(1)}, bf16[1,4,96,384]{3,2,1,0:T(8,128)(2,1)S(1)}, u32[]{:S(2)}, u32[]{:S(2)}) %collective-permute-start.6) | collective-permute-done | bytes 294944 | tf_op jit(solution)/shard_map/ppermute | solution.py:52
  35.2 1.8 collective-permute-start.7
  37.1 1.6 collective-permute-start.11
  39.2 10.0 %collective-permute-done.7.rest_1_ = bf16[2,4,96,384]{3,2,1,0:T(8,128)(2,1)S(1)} collective-permute-done((bf16[2,4,96,384]{3,2,1,0:T(8,128)(2,1)S(1)}, bf16[2,4,96,384]{3,2,1,0:T(8,128)(2,1)S(1)}, u32[]{:S(2)}, u32[]{:S(2)}) %collective-permute-start.7) | collective-permute-done | bytes 589856 | tf_op jit(solution)/shard_map/ppermute | solution.py:52
  54.9 2.0 collective-permute-start.16
  57.9 2.9 %collective-permute-start.18 = (bf16[24,768]{1,0:T(8,128)(2,1)}, bf16[24,768]{1,0:T(8,128)(2,1)}, u32[]{:S(2)}, u32[]{:S(2)}) collective-permute-start(bf16[24,768]{1,0:T(8,128)(2,1)} %get-tuple-element.164), channel_id=1, source_target_pairs={{0,5},{1,4},{2,7},{3,6},{4,1},{5,0},{6,3},{7,2},{8,13},{9,12},{10,... | collective-permute-start | bytes 110600 | tf_op jit(solution)/shard_map/ppermute | solution.py:52
  60.8 9.9 %attention_forward.1 = (bf16[3,768,128]{2,1,0:T(8,128)(2,1)}, f32[12,128,128]{2,1,0:T(8,128)}, bf16[128,768]{1,0:T(8,128)(2,1)}, f32[128,768]{1,0:T(8,128)}, f32...) custom-call(bf16[128,768]{1,0:T(8,128)(2,1)} %tokens_ref.5, ...), custom_call_target="tpu_custom_call" | custom-call | tf_op jit(solution)/shard_map/attention_forward/pallas_call | solution.py:516
  72.5 3.6 %collective-permute-start.20 = (bf16[24,768]{1,0:T(8,128)(2,1)}, bf16[24,768]{1,0:T(8,128)(2,1)S(1)}, u32[]{:S(2)}, u32[]{:S(2)}) collective-permute-start(bf16[24,768]{1,0:T(8,128)(2,1)} %get-tuple-element.166), channel_id=1, source_target_pairs={{0,7},{1,6},{2,5},{3,4},{4,3},{5,2},{6,1},{7,0},{8,15},{9,14},{10,... | collective-permute-start | bytes 110600 | tf_op jit(solution)/shard_map/ppermute | solution.py:52
  79.9 2.0 collective-permute-start.26
  82.7 3.8 %collective-permute-start.28 = (bf16[24,768]{1,0:T(8,128)(2,1)}, bf16[24,768]{1,0:T(8,128)(2,1)S(1)}, u32[]{:S(2)}, u32[]{:S(2)}) collective-permute-start(bf16[24,768]{1,0:T(8,128)(2,1)} %get-tuple-element.173), channel_id=1, source_target_pairs={{0,5},{1,4},{2,7},{3,6},{4,1},{5,0},{6,3},{7,2},{8,13},{9,12},{10,... | collective-permute-start | bytes 110600 | tf_op jit(solution)/shard_map/ppermute | solution.py:52
  86.9 3.6 %collective-permute-start.30 = (bf16[24,768]{1,0:T(8,128)(2,1)}, bf16[24,768]{1,0:T(8,128)(2,1)S(1)}, u32[]{:S(2)}, u32[]{:S(2)}) collective-permute-start(bf16[24,768]{1,0:T(8,128)(2,1)} %get-tuple-element.175), channel_id=1, source_target_pairs={{0,7},{1,6},{2,5},{3,4},{4,3},{5,2},{6,1},{7,0},{8,15},{9,14},{10,... | collective-permute-start | bytes 110600 | tf_op jit(solution)/shard_map/ppermute | solution.py:52
  91.8 4.6 %collective-permute-done.28 = bf16[24,768]{1,0:T(8,128)(2,1)S(1)} collective-permute-done((bf16[24,768]{1,0:T(8,128)(2,1)}, bf16[24,768]{1,0:T(8,128)(2,1)S(1)}, u32[]{:S(2)}, u32[]{:S(2)}) %collective-permute-start.28) | collective-permute-done | bytes 36896 | tf_op jit(solution)/shard_map/ppermute | solution.py:52
  97.8 2.3 collective-permute-done.22.rest_2_
  100.7 2.6 %collective-permute-done.32.rest_2_ = bf16[192,768]{1,0:T(8,128)(2,1)S(1)} collective-permute-done((bf16[192,768]{1,0:T(8,128)(2,1)S(1)}, bf16[192,768]{1,0:T(8,128)(2,1)S(1)}, u32[]{:S(2)}, u32[]{:S(2)}) %collective-permute-start.32) | collective-permute-done | bytes 294944 | tf_op jit(solution)/shard_map/ppermute | solution.py:52
  104.8 4.5 %upstream_rows.1 = (bf16[2,320,768]{2,1,0:T(8,128)(2,1)}, f32[2,320,768]{2,1,0:T(8,128)}) custom-call(bf16[160,192]{1,0:T(8,128)(2,1)} %constant.8.clone.pack_ref, bf16[2,768,768]{2,1,0:T(8,128)(2,1)} %w_out_ref.3, bf16[192,768]{1,0:T(8,128)(2,1)} %copy-done.8, bf16[192,768]{1,0:T(8,128)(2,1)} %copy-done.13, bf16[192,768]{1,0:T(8,128)(2,1)} %copy-done.9, ...), custom_call_target="tpu_custom_call" | custom-call | tf_op jit(solution)/shard_map/upstream_rows/pallas_call | solution.py:516
  110.1 10.1 %experts.1 = (bf16[192,768]{1,0:T(8,128)(2,1)}, bf16[192,768]{1,0:T(8,128)(2,1)}, bf16[192,768]{1,0:T(8,128)(2,1)}, bf16[192,768]{1,0:T(8,128)(2,1)}, bf16[2,320...) custom-call(bf16[160,192]{1,0:T(8,128)(2,1)} %constant.8.clone.pack_re, ...), custom_call_target="tpu_custom_call" | custom-call | tf_op jit(solution)/shard_map/experts/pallas_call | solution.py:516
  124.4 10.2 %expert_gradients.1 = (bf16[192,768]{1,0:T(8,128)(2,1)}, bf16[192,768]{1,0:T(8,128)(2,1)}, bf16[192,768]{1,0:T(8,128)(2,1)}, bf16[192,768]{1,0:T(8,128)(2,1)}, f...) custom-call(bf16[192,160]{1,0:T(8,128)(2,1)} %constant.9.clone.pack_t_ref, bf16[2,768,768]{2,1,0:T(8,128)(2,1)} %w_out_ref.3, ...), custom_call_target="tpu_custom_call" | custom-call | tf_op jit(solution)/shard_map/expert_gradients/pallas_call | solution.py:516
  136.1 1.8 back_slabs.1
  138.4 3.9 %collective-permute-start.38 = (bf16[24,768]{1,0:T(8,128)(2,1)}, bf16[24,768]{1,0:T(8,128)(2,1)S(1)}, u32[]{:S(2)}, u32[]{:S(2)}) collective-permute-start(bf16[24,768]{1,0:T(8,128)(2,1)} %get-tuple-element.182), channel_id=1, source_target_pairs={{0,2},{1,3},{2,0},{3,1},{4,6},{5,7},{6,4},{7,5},{8,10},{9,11},{10,... | collective-permute-start | bytes 110600 | tf_op jit(solution)/shard_map/ppermute | solution.py:52
  146.4 2.0 collective-permute-start.42
  148.4 2.7 %collective-permute-start.43 = (bf16[24,768]{1,0:T(8,128)(2,1)}, bf16[24,768]{1,0:T(8,128)(2,1)S(1)}, u32[]{:S(2)}, u32[]{:S(2)}) collective-permute-start(bf16[24,768]{1,0:T(8,128)(2,1)} %get-tuple-element.187), channel_id=1, source_target_pairs={{0,7},{1,6},{2,5},{3,4},{4,3},{5,2},{6,1},{7,0},{8,15},{9,14},{10,... | collective-permute-start | bytes 110600 | tf_op jit(solution)/shard_map/ppermute | solution.py:52
  152.4 2.8 %collective-permute-done.43.rest_15_ = bf16[24,768]{1,0:T(8,128)(2,1)S(1)} collective-permute-done((bf16[24,768]{1,0:T(8,128)(2,1)}, bf16[24,768]{1,0:T(8,128)(2,1)S(1)}, u32[]{:S(2)}, u32[]{:S(2)}) %collective-permute-start.43) | collective-permute-done | bytes 36896 | tf_op jit(solution)/shard_map/ppermute | solution.py:52
  155.8 11.8 %attention_backward.1 = (f32[128,768]{1,0:T(8,128)}, f32[32,768]{1,0:T(8,128)}, bf16[384,128]{1,0:T(8,128)(2,1)}, bf16[384,128]{1,0:T(8,128)(2,1)}, bf16[384,128...) custom-call(bf16[128,768]{1,0:T(8,128)(2,1)} %tokens_ref.5, ...), custom_call_target="tpu_custom_call" | custom-call | tf_op jit(solution)/shard_map/attention_backward/pallas_call | solution.py:516
  171.4 3.7 %collective-permute-done.62 = f32[32,768]{1,0:T(8,128)S(1)} collective-permute-done((f32[32,768]{1,0:T(8,128)S(1)}, f32[32,768]{1,0:T(8,128)S(1)}, u32[]{:S(2)}, u32[]{:S(2)}) %collective-permute-start.62) | collective-permute-done | bytes 98336 | tf_op jit(solution)/shard_map/ppermute | solution.py:52
  175.1 1.7 collective-permute-start.63
  178.0 1.8 collective-permute-done.63
  180.7 4.2 %collective-permute-done.53.second_ref = bf16[192,768]{1,0:T(8,128)(2,1)S(1)} collective-permute-done((bf16[192,768]{1,0:T(8,128)(2,1)S(1)}, bf16[192,768]{1,0:T(8,128)(2,1)S(1)}, u32[]{:S(2)}, u32[]{:S(2)}) %collective-permute-start.53) | collective-permute-done | bytes 294944 | tf_op jit(solution)/shard_map/ppermute | solution.py:52
  185.6 1.8 returned_slabs.1
  187.8 3.1 %collective-permute-start.56 = (bf16[24,768]{1,0:T(8,128)(2,1)}, bf16[24,768]{1,0:T(8,128)(2,1)S(1)}, u32[]{:S(2)}, u32[]{:S(2)}) collective-permute-start(bf16[24,768]{1,0:T(8,128)(2,1)} %get-tuple-element.208), channel_id=1, source_target_pairs={{0,3},{1,2},{2,1},{3,0},{4,7},{5,6},{6,5},{7,4},{8,11},{9,10},{10,... | collective-permute-start | bytes 110600 | tf_op jit(solution)/shard_map/ppermute | solution.py:52
  191.9 2.0 collective-permute-start.65
  195.0 2.7 %collective-permute-start.58 = (bf16[24,768]{1,0:T(8,128)(2,1)}, bf16[24,768]{1,0:T(8,128)(2,1)S(1)}, u32[]{:S(2)}, u32[]{:S(2)}) collective-permute-start(bf16[24,768]{1,0:T(8,128)(2,1)} %get-tuple-element.210), channel_id=1, source_target_pairs={{0,5},{1,4},{2,7},{3,6},{4,1},{5,0},{6,3},{7,2},{8,13},{9,12},{10,... | collective-permute-start | bytes 110600 | tf_op jit(solution)/shard_map/ppermute | solution.py:52
  197.7 2.8 %collective-permute-done.57.rest_12_ = bf16[24,768]{1,0:T(8,128)(2,1)S(1)} collective-permute-done((bf16[24,768]{1,0:T(8,128)(2,1)}, bf16[24,768]{1,0:T(8,128)(2,1)S(1)}, u32[]{:S(2)}, u32[]{:S(2)}) %collective-permute-start.57) | collective-permute-done | bytes 36896 | tf_op jit(solution)/shard_map/ppermute | solution.py:52
  200.4 1.7 collective-permute-start.59
  202.1 2.4 collective-permute-start.60
  204.5 2.4 collective-permute-done.59.rest_14_
  206.9 2.6 %collective-permute-done.60.rest_15_ = bf16[24,768]{1,0:T(8,128)(2,1)S(1)} collective-permute-done((bf16[24,768]{1,0:T(8,128)(2,1)}, bf16[24,768]{1,0:T(8,128)(2,1)S(1)}, u32[]{:S(2)}, u32[]{:S(2)}) %collective-permute-start.60) | collective-permute-done | bytes 36896 | tf_op jit(solution)/shard_map/ppermute | solution.py:52
  209.5 2.7 %collective-permute-start.48 = (bf16[384,128]{1,0:T(8,128)(2,1)S(1)}, bf16[384,128]{1,0:T(8,128)(2,1)S(1)}, u32[]{:S(2)}, u32[]{:S(2)}) collective-permute-start(bf16[384,128]{1,0:T(8,128)(2,1)S(1)} %copy-done.46), channel_id=1, source_target_pairs={{0,5},{1,4},{2,7},{3,6},{4,1},{5,0},{6,3},{7,2},{8,13},{9,12},{10,... | collective-permute-start | bytes 294920 | tf_op jit(solution)/shard_map/ppermute | solution.py:52
  212.2 2.3 collective-permute-start.49
  214.5 2.8 %collective-permute-start.50 = (bf16[384,128]{1,0:T(8,128)(2,1)S(1)}, bf16[384,128]{1,0:T(8,128)(2,1)S(1)}, u32[]{:S(2)}, u32[]{:S(2)}) collective-permute-start(bf16[384,128]{1,0:T(8,128)(2,1)S(1)} %copy-done.44), channel_id=1, source_target_pairs={{0,7},{1,6},{2,5},{3,4},{4,3},{5,2},{6,1},{7,0},{8,15},{9,14},{10,... | collective-permute-start | bytes 294920 | tf_op jit(solution)/shard_map/ppermute | solution.py:52
  217.6 4.4 %collective-permute-done.48.rest_5_ = bf16[384,128]{1,0:T(8,128)(2,1)S(1)} collective-permute-done((bf16[384,128]{1,0:T(8,128)(2,1)S(1)}, bf16[384,128]{1,0:T(8,128)(2,1)S(1)}, u32[]{:S(2)}, u32[]{:S(2)}) %collective-permute-start.48) | collective-permute-done | bytes 98336 | tf_op jit(solution)/shard_map/ppermute | solution.py:52
  222.8 4.8 %weight_gradients.1 = (bf16[128,768]{1,0:T(8,128)(2,1)}, bf16[192,384]{1,0:T(8,128)(2,1)}, bf16[192,384]{1,0:T(8,128)(2,1)}, bf16[192,384]{1,0:T(8,128)(2,1)}, bf16[192,384]{1,0:T(8,128)(2,1)}) custom-call(bf16[8,128,768]{2,1,0:T(8,128)(2,1)} %bitcast.15, bf16[8,128,768]{2,1,0:T(8,128)(2,1)} %bitcast.16, f32[128,768]{1,0:T(8,128)} %get-tuple-element.154.hidden_ref, ...), custom_call_target="tpu_custom_call" | custom-call | tf_op jit(solution)/shard_map/weight_gradients/pallas_call | solution.py:516
  232.5 3.6 %collective-permute-done.68 = bf16[192,384]{1,0:T(8,128)(2,1)S(1)} collective-permute-done((bf16[192,384]{1,0:T(8,128)(2,1)S(1)}, bf16[192,384]{1,0:T(8,128)(2,1)S(1)}, u32[]{:S(2)}, u32[]{:S(2)}) %collective-permute-start.68) | collective-permute-done | bytes 147488 | tf_op jit(solution)/shard_map/ppermute | solution.py:52
  (246 shorter events, 53.4 us)
Async XLA Ops:
  7.2 214.9 %all-gather.5.cloned.1.call-start = ((), (), s32[]{:S(2)}) async-start(), calls=%async_computation | async-start | bytes 1769472 | tf_op jit(solution)/shard_map/all_gather | solution.py:586
  8.3 14.1 %collective-permute-start.5 = (bf16[1,96,384]{2,1,0:T(8,128)(2,1)S(1)}, bf16[1,96,384]{2,1,0:T(8,128)(2,1)S(1)}, u32[]{:S(2)}, u32[]{:S(2)}) collective-permute-start(bf16[1,96,384]{2,1,0:T(8,128)(2,1)S(1)} %get-tuple-element.228), channel_id=1, source_target_pairs={{0,6},{1,7},{2,4},{3,5},{4,2},{5,3},{6,0},{7,1},{8,14},{9,15},{10,... | collective-permute-start | bytes 221192 | tf_op jit(solution)/shard_map/ppermute | solution.py:52
  13.4 10.1 %collective-permute-start.4 = (bf16[1,96,384]{2,1,0:T(8,128)(2,1)S(1)}, bf16[1,96,384]{2,1,0:T(8,128)(2,1)S(1)}, u32[]{:S(2)}, u32[]{:S(2)}) collective-permute-start(bf16[1,96,384]{2,1,0:T(8,128)(2,1)S(1)} %get-tuple-element.228), channel_id=1, source_target_pairs={{0,4},{1,5},{2,6},{3,7},{4,0},{5,1},{6,2},{7,3},{8,12},{9,13},{10,... | collective-permute-start | bytes 221192 | tf_op jit(solution)/shard_map/ppermute | solution.py:52
  13.4 10.1 %collective-permute-start.3 = (bf16[1,96,384]{2,1,0:T(8,128)(2,1)S(1)}, bf16[1,96,384]{2,1,0:T(8,128)(2,1)S(1)}, u32[]{:S(2)}, u32[]{:S(2)}) collective-permute-start(bf16[1,96,384]{2,1,0:T(8,128)(2,1)S(1)} %get-tuple-element.228), channel_id=1, source_target_pairs={{0,2},{1,3},{2,0},{3,1},{4,6},{5,7},{6,4},{7,5},{8,10},{9,11},{10,... | collective-permute-start | bytes 221192 | tf_op jit(solution)/shard_map/ppermute | solution.py:52
  14.0 9.5 %collective-permute-start.2 = (bf16[1,96,384]{2,1,0:T(8,128)(2,1)S(1)}, bf16[1,96,384]{2,1,0:T(8,128)(2,1)S(1)}, u32[]{:S(2)}, u32[]{:S(2)}) collective-permute-start(bf16[1,96,384]{2,1,0:T(8,128)(2,1)S(1)} %get-tuple-element.229), channel_id=1, source_target_pairs={{0,6},{1,7},{2,4},{3,5},{4,2},{5,3},{6,0},{7,1},{8,14},{9,15},{10,... | collective-permute-start | bytes 221192 | tf_op jit(solution)/shard_map/ppermute | solution.py:52
  17.8 8.3 %collective-permute-start.1 = (bf16[1,96,384]{2,1,0:T(8,128)(2,1)S(1)}, bf16[1,96,384]{2,1,0:T(8,128)(2,1)S(1)}, u32[]{:S(2)}, u32[]{:S(2)}) collective-permute-start(bf16[1,96,384]{2,1,0:T(8,128)(2,1)S(1)} %get-tuple-element.229), channel_id=1, source_target_pairs={{0,4},{1,5},{2,6},{3,7},{4,0},{5,1},{6,2},{7,3},{8,12},{9,13},{10,... | collective-permute-start | bytes 221192 | tf_op jit(solution)/shard_map/ppermute | solution.py:52
  26.9 8.2 %collective-permute-start.6 = (bf16[1,4,96,384]{3,2,1,0:T(8,128)(2,1)S(1)}, bf16[1,4,96,384]{3,2,1,0:T(8,128)(2,1)S(1)}, u32[]{:S(2)}, u32[]{:S(2)}) collective-permute-start(bf16[1,4,96,384]{3,2,1,0:T(8,128)(2,1)S(1)} %bitcast.19), channel_id=1, source_target_pairs={{0,1},{1,0},{2,3},{3,2},{4,5},{5,4},{6,7},{7,6},{8,9},{9,8},{10,11... | collective-permute-start | bytes 884744 | tf_op jit(solution)/shard_map/ppermute | solution.py:52
  28.6 8.5 %collective-permute-start.10 = (bf16[1,4,96,384]{3,2,1,0:T(8,128)(2,1)S(1)}, bf16[1,4,96,384]{3,2,1,0:T(8,128)(2,1)S(1)}, u32[]{:S(2)}, u32[]{:S(2)}) collective-permute-start(bf16[1,4,96,384]{3,2,1,0:T(8,128)(2,1)S(1)} %bitcast.17), channel_id=1, source_target_pairs={{0,16},{8,24},{16,0},{24,8},{1,17},{9,25},{17,1},{25,9},{2,18},{10... | collective-permute-start | bytes 884744 | tf_op jit(solution)/shard_map/ppermute | solution.py:52
  35.2 14.0 %collective-permute-start.7 = (bf16[2,4,96,384]{3,2,1,0:T(8,128)(2,1)S(1)}, bf16[2,4,96,384]{3,2,1,0:T(8,128)(2,1)S(1)}, u32[]{:S(2)}, u32[]{:S(2)}) collective-permute-start(bf16[2,4,96,384]{3,2,1,0:T(8,128)(2,1)S(1)} %pad_maximum_fusion.rest_0_), channel_id=1, source_target_pairs={{0,16},{8,24},{16,0},{24,8},{1,17},{9,25},{17,1},{25,9},{2,18},{10... | collective-permute-start | bytes 1769480 | tf_op jit(solution)/shard_map/ppermute | solution.py:52
  37.1 13.5 %collective-permute-start.11 = (bf16[2,4,96,384]{3,2,1,0:T(8,128)(2,1)S(1)}, bf16[2,4,96,384]{3,2,1,0:T(8,128)(2,1)S(1)}, u32[]{:S(2)}, u32[]{:S(2)}) collective-permute-start(bf16[2,4,96,384]{3,2,1,0:T(8,128)(2,1)S(1)} %pad_maximum_fusion.1.rest_4_), channel_id=1, source_target_pairs={{0,1},{1,0},{2,3},{3,2},{4,5},{5,4},{6,7},{7,6},{8,9},{9,8},{10,11... | collective-permute-start | bytes 1769480 | tf_op jit(solution)/shard_map/ppermute | solution.py:52
  38.7 11.9 %collective-permute-start.8 = (bf16[2,4,96,384]{3,2,1,0:T(8,128)(2,1)S(1)}, bf16[2,4,96,384]{3,2,1,0:T(8,128)(2,1)S(1)}, u32[]{:S(2)}, u32[]{:S(2)}) collective-permute-start(bf16[2,4,96,384]{3,2,1,0:T(8,128)(2,1)S(1)} %pad_maximum_fusion.rest_0_), channel_id=1, source_target_pairs={{0,8},{8,0},{16,24},{24,16},{1,9},{9,1},{17,25},{25,17},{2,10},{10... | collective-permute-start | bytes 1769480 | tf_op jit(solution)/shard_map/ppermute | solution.py:52
  38.7 11.9 %collective-permute-start.12 = (bf16[2,4,96,384]{3,2,1,0:T(8,128)(2,1)S(1)}, bf16[2,4,96,384]{3,2,1,0:T(8,128)(2,1)S(1)}, u32[]{:S(2)}, u32[]{:S(2)}) collective-permute-start(bf16[2,4,96,384]{3,2,1,0:T(8,128)(2,1)S(1)} %pad_maximum_fusion.1.rest_4_), channel_id=1, source_target_pairs={{0,8},{8,0},{16,24},{24,16},{1,9},{9,1},{17,25},{25,17},{2,10},{10... | collective-permute-start | bytes 1769480 | tf_op jit(solution)/shard_map/ppermute | solution.py:52
  52.7 169.4 %all-gather.7.cloned.1.call-start = ((), (), s32[]{:S(2)}) async-start(), calls=%async_computation.1 | async-start | bytes 1769472 | tf_op jit(solution)/shard_map/all_gather | solution.py:612
  53.4 18.1 %collective-permute-start.14 = (bf16[24,768]{1,0:T(8,128)(2,1)}, bf16[24,768]{1,0:T(8,128)(2,1)}, u32[]{:S(2)}, u32[]{:S(2)}) collective-permute-start(bf16[24,768]{1,0:T(8,128)(2,1)} %get-tuple-element.160), channel_id=1, source_target_pairs={{0,1},{1,0},{2,3},{3,2},{4,5},{5,4},{6,7},{7,6},{8,9},{9,8},{10,11... | collective-permute-start | bytes 110600 | tf_op jit(solution)/shard_map/ppermute | solution.py:52
  54.9 17.7 %collective-permute-start.15 = (bf16[24,768]{1,0:T(8,128)(2,1)}, bf16[24,768]{1,0:T(8,128)(2,1)}, u32[]{:S(2)}, u32[]{:S(2)}) collective-permute-start(bf16[24,768]{1,0:T(8,128)(2,1)} %get-tuple-element.161), channel_id=1, source_target_pairs={{0,2},{1,3},{2,0},{3,1},{4,6},{5,7},{6,4},{7,5},{8,10},{9,11},{10,... | collective-permute-start | bytes 110600 | tf_op jit(solution)/shard_map/ppermute | solution.py:52
  54.9 22.0 %collective-permute-start.16 = (bf16[24,768]{1,0:T(8,128)(2,1)}, bf16[24,768]{1,0:T(8,128)(2,1)}, u32[]{:S(2)}, u32[]{:S(2)}) collective-permute-start(bf16[24,768]{1,0:T(8,128)(2,1)} %get-tuple-element.162), channel_id=1, source_target_pairs={{0,3},{1,2},{2,1},{3,0},{4,7},{5,6},{6,5},{7,4},{8,11},{9,10},{10,... | collective-permute-start | bytes 110600 | tf_op jit(solution)/shard_map/ppermute | solution.py:52
  56.9 22.3 %collective-permute-start.17 = (bf16[24,768]{1,0:T(8,128)(2,1)}, bf16[24,768]{1,0:T(8,128)(2,1)}, u32[]{:S(2)}, u32[]{:S(2)}) collective-permute-start(bf16[24,768]{1,0:T(8,128)(2,1)} %get-tuple-element.163), channel_id=1, source_target_pairs={{0,4},{1,5},{2,6},{3,7},{4,0},{5,1},{6,2},{7,3},{8,12},{9,13},{10,... | collective-permute-start | bytes 110600 | tf_op jit(solution)/shard_map/ppermute | solution.py:52
  57.9 22.1 %collective-permute-start.18 = (bf16[24,768]{1,0:T(8,128)(2,1)}, bf16[24,768]{1,0:T(8,128)(2,1)}, u32[]{:S(2)}, u32[]{:S(2)}) collective-permute-start(bf16[24,768]{1,0:T(8,128)(2,1)} %get-tuple-element.164), channel_id=1, source_target_pairs={{0,5},{1,4},{2,7},{3,6},{4,1},{5,0},{6,3},{7,2},{8,13},{9,12},{10,... | collective-permute-start | bytes 110600 | tf_op jit(solution)/shard_map/ppermute | solution.py:52
  71.5 11.2 %collective-permute-start.19 = (bf16[24,768]{1,0:T(8,128)(2,1)}, bf16[24,768]{1,0:T(8,128)(2,1)S(1)}, u32[]{:S(2)}, u32[]{:S(2)}) collective-permute-start(bf16[24,768]{1,0:T(8,128)(2,1)} %get-tuple-element.165), channel_id=1, source_target_pairs={{0,6},{1,7},{2,4},{3,5},{4,2},{5,3},{6,0},{7,1},{8,14},{9,15},{10,... | collective-permute-start | bytes 110600 | tf_op jit(solution)/shard_map/ppermute | solution.py:52
  72.5 10.2 %collective-permute-start.20 = (bf16[24,768]{1,0:T(8,128)(2,1)}, bf16[24,768]{1,0:T(8,128)(2,1)S(1)}, u32[]{:S(2)}, u32[]{:S(2)}) collective-permute-start(bf16[24,768]{1,0:T(8,128)(2,1)} %get-tuple-element.166), channel_id=1, source_target_pairs={{0,7},{1,6},{2,5},{3,4},{4,3},{5,2},{6,1},{7,0},{8,15},{9,14},{10,... | collective-permute-start | bytes 110600 | tf_op jit(solution)/shard_map/ppermute | solution.py:52
  76.9 9.7 %collective-permute-start.24 = (bf16[24,768]{1,0:T(8,128)(2,1)}, bf16[24,768]{1,0:T(8,128)(2,1)S(1)}, u32[]{:S(2)}, u32[]{:S(2)}) collective-permute-start(bf16[24,768]{1,0:T(8,128)(2,1)} %get-tuple-element.169), channel_id=1, source_target_pairs={{0,1},{1,0},{2,3},{3,2},{4,5},{5,4},{6,7},{7,6},{8,9},{9,8},{10,11... | collective-permute-start | bytes 110600 | tf_op jit(solution)/shard_map/ppermute | solution.py:52
  79.1 7.7 %collective-permute-start.25 = (bf16[24,768]{1,0:T(8,128)(2,1)}, bf16[24,768]{1,0:T(8,128)(2,1)S(1)}, u32[]{:S(2)}, u32[]{:S(2)}) collective-permute-start(bf16[24,768]{1,0:T(8,128)(2,1)} %get-tuple-element.170), channel_id=1, source_target_pairs={{0,2},{1,3},{2,0},{3,1},{4,6},{5,7},{6,4},{7,5},{8,10},{9,11},{10,... | collective-permute-start | bytes 110600 | tf_op jit(solution)/shard_map/ppermute | solution.py:52
  79.9 10.5 %collective-permute-start.26 = (bf16[24,768]{1,0:T(8,128)(2,1)}, bf16[24,768]{1,0:T(8,128)(2,1)S(1)}, u32[]{:S(2)}, u32[]{:S(2)}) collective-permute-start(bf16[24,768]{1,0:T(8,128)(2,1)} %get-tuple-element.171), channel_id=1, source_target_pairs={{0,3},{1,2},{2,1},{3,0},{4,7},{5,6},{6,5},{7,4},{8,11},{9,10},{10,... | collective-permute-start | bytes 110600 | tf_op jit(solution)/shard_map/ppermute | solution.py:52
  82.7 9.1 %collective-permute-start.27 = (bf16[24,768]{1,0:T(8,128)(2,1)}, bf16[24,768]{1,0:T(8,128)(2,1)S(1)}, u32[]{:S(2)}, u32[]{:S(2)}) collective-permute-start(bf16[24,768]{1,0:T(8,128)(2,1)} %get-tuple-element.172), channel_id=1, source_target_pairs={{0,4},{1,5},{2,6},{3,7},{4,0},{5,1},{6,2},{7,3},{8,12},{9,13},{10,... | collective-permute-start | bytes 110600 | tf_op jit(solution)/shard_map/ppermute | solution.py:52
  82.7 13.7 %collective-permute-start.28 = (bf16[24,768]{1,0:T(8,128)(2,1)}, bf16[24,768]{1,0:T(8,128)(2,1)S(1)}, u32[]{:S(2)}, u32[]{:S(2)}) collective-permute-start(bf16[24,768]{1,0:T(8,128)(2,1)} %get-tuple-element.173), channel_id=1, source_target_pairs={{0,5},{1,4},{2,7},{3,6},{4,1},{5,0},{6,3},{7,2},{8,13},{9,12},{10,... | collective-permute-start | bytes 110600 | tf_op jit(solution)/shard_map/ppermute | solution.py:52
  86.6 9.8 %collective-permute-start.29 = (bf16[24,768]{1,0:T(8,128)(2,1)}, bf16[24,768]{1,0:T(8,128)(2,1)S(1)}, u32[]{:S(2)}, u32[]{:S(2)}) collective-permute-start(bf16[24,768]{1,0:T(8,128)(2,1)} %get-tuple-element.174), channel_id=1, source_target_pairs={{0,6},{1,7},{2,4},{3,5},{4,2},{5,3},{6,0},{7,1},{8,14},{9,15},{10,... | collective-permute-start | bytes 110600 | tf_op jit(solution)/shard_map/ppermute | solution.py:52
  86.9 9.6 %collective-permute-start.30 = (bf16[24,768]{1,0:T(8,128)(2,1)}, bf16[24,768]{1,0:T(8,128)(2,1)S(1)}, u32[]{:S(2)}, u32[]{:S(2)}) collective-permute-start(bf16[24,768]{1,0:T(8,128)(2,1)} %get-tuple-element.175), channel_id=1, source_target_pairs={{0,7},{1,6},{2,5},{3,4},{4,3},{5,2},{6,1},{7,0},{8,15},{9,14},{10,... | collective-permute-start | bytes 110600 | tf_op jit(solution)/shard_map/ppermute | solution.py:52
  90.4 9.7 %collective-permute-start.22 = (bf16[192,768]{1,0:T(8,128)(2,1)S(1)}, bf16[192,768]{1,0:T(8,128)(2,1)S(1)}, u32[]{:S(2)}, u32[]{:S(2)}) collective-permute-start(bf16[192,768]{1,0:T(8,128)(2,1)S(1)} %constant_dynamic-update-slice_fusion.rest_0_), channel_id=1, source_target_pairs={{0,16},{8,24},{16,0},{24,8},{1,17},{9,25},{17,1},{25,9},{2,18},{10... | collective-permute-start | bytes 884744 | tf_op jit(solution)/shard_map/ppermute | solution.py:52
  100.2 9.1 %collective-permute-start.31 = (bf16[192,768]{1,0:T(8,128)(2,1)S(1)}, bf16[192,768]{1,0:T(8,128)(2,1)S(1)}, u32[]{:S(2)}, u32[]{:S(2)}) collective-permute-start(bf16[192,768]{1,0:T(8,128)(2,1)S(1)} %constant_dynamic-update-slice_fusion.8.rest_0_), channel_id=1, source_target_pairs={{0,8},{8,0},{16,24},{24,16},{1,9},{9,1},{17,25},{25,17},{2,10},{10... | collective-permute-start | bytes 884744 | tf_op jit(solution)/shard_map/ppermute | solution.py:52
  120.7 14.0 %collective-permute-start.34 = (bf16[192,768]{1,0:T(8,128)(2,1)}, bf16[192,768]{1,0:T(8,128)(2,1)S(1)}, u32[]{:S(2)}, u32[]{:S(2)}) collective-permute-start(bf16[192,768]{1,0:T(8,128)(2,1)} %get-tuple-element.177), channel_id=1, source_target_pairs={{0,8},{8,0},{16,24},{24,16},{1,9},{9,1},{17,25},{25,17},{2,10},{10... | collective-permute-start | bytes 884744 | tf_op jit(solution)/shard_map/ppermute | solution.py:52
  123.1 12.3 %collective-permute-start.36 = (bf16[192,768]{1,0:T(8,128)(2,1)S(1)}, bf16[192,768]{1,0:T(8,128)(2,1)S(1)}, u32[]{:S(2)}, u32[]{:S(2)}) collective-permute-start(bf16[192,768]{1,0:T(8,128)(2,1)S(1)} %add_convert_fusion.2), channel_id=1, source_target_pairs={{0,16},{8,24},{16,0},{24,8},{1,17},{9,25},{17,1},{25,9},{2,18},{10... | collective-permute-start | bytes 884744 | tf_op jit(solution)/shard_map/ppermute | solution.py:52
  134.6 42.2 %collective-permute-start.52 = (bf16[192,768]{1,0:T(8,128)(2,1)}, bf16[192,768]{1,0:T(8,128)(2,1)S(1)}, u32[]{:S(2)}, u32[]{:S(2)}) collective-permute-start(bf16[192,768]{1,0:T(8,128)(2,1)} %get-tuple-element.204), channel_id=1, source_target_pairs={{0,8},{8,0},{16,24},{24,16},{1,9},{9,1},{17,25},{25,17},{2,10},{10... | collective-permute-start | bytes 884744 | tf_op jit(solution)/shard_map/ppermute | solution.py:52
  138.4 7.9 %collective-permute-start.38 = (bf16[24,768]{1,0:T(8,128)(2,1)}, bf16[24,768]{1,0:T(8,128)(2,1)S(1)}, u32[]{:S(2)}, u32[]{:S(2)}) collective-permute-start(bf16[24,768]{1,0:T(8,128)(2,1)} %get-tuple-element.182), channel_id=1, source_target_pairs={{0,2},{1,3},{2,0},{3,1},{4,6},{5,7},{6,4},{7,5},{8,10},{9,11},{10,... | collective-permute-start | bytes 110600 | tf_op jit(solution)/shard_map/ppermute | solution.py:52
  143.4 7.7 %collective-permute-start.40 = (bf16[24,768]{1,0:T(8,128)(2,1)}, bf16[24,768]{1,0:T(8,128)(2,1)S(1)}, u32[]{:S(2)}, u32[]{:S(2)}) collective-permute-start(bf16[24,768]{1,0:T(8,128)(2,1)} %get-tuple-element.184), channel_id=1, source_target_pairs={{0,4},{1,5},{2,6},{3,7},{4,0},{5,1},{6,2},{7,3},{8,12},{9,13},{10,... | collective-permute-start | bytes 110600 | tf_op jit(solution)/shard_map/ppermute | solution.py:52
  171.4 8.5 %collective-permute-start.51 = (bf16[192,768]{1,0:T(8,128)(2,1)S(1)}, bf16[192,768]{1,0:T(8,128)(2,1)S(1)}, u32[]{:S(2)}, u32[]{:S(2)}) collective-permute-start(bf16[192,768]{1,0:T(8,128)(2,1)S(1)} %copy-done.43), channel_id=1, source_target_pairs={{0,8},{8,0},{16,24},{24,16},{1,9},{9,1},{17,25},{25,17},{2,10},{10... | collective-permute-start | bytes 884744 | tf_op jit(solution)/shard_map/ppermute | solution.py:52
  176.9 8.0 %collective-permute-start.53 = (bf16[192,768]{1,0:T(8,128)(2,1)S(1)}, bf16[192,768]{1,0:T(8,128)(2,1)S(1)}, u32[]{:S(2)}, u32[]{:S(2)}) collective-permute-start(bf16[192,768]{1,0:T(8,128)(2,1)S(1)} %add_convert_fusion), channel_id=1, source_target_pairs={{0,16},{8,24},{16,0},{24,8},{1,17},{9,25},{17,1},{25,9},{2,18},{10... | collective-permute-start | bytes 884744 | tf_op jit(solution)/shard_map/ppermute | solution.py:52
  179.8 11.5 %collective-permute-start.64 = (f32[32,768]{1,0:T(8,128)S(1)}, f32[32,768]{1,0:T(8,128)S(1)}, u32[]{:S(2)}, u32[]{:S(2)}) collective-permute-start(f32[32,768]{1,0:T(8,128)S(1)} %add.42), channel_id=1, source_target_pairs={{0,2},{1,3},{2,0},{3,1},{4,6},{5,7},{6,4},{7,5},{8,10},{9,11},{10,... | collective-permute-start | bytes 294920 | tf_op jit(solution)/shard_map/ppermute | solution.py:52
  187.8 7.2 %collective-permute-start.56 = (bf16[24,768]{1,0:T(8,128)(2,1)}, bf16[24,768]{1,0:T(8,128)(2,1)S(1)}, u32[]{:S(2)}, u32[]{:S(2)}) collective-permute-start(bf16[24,768]{1,0:T(8,128)(2,1)} %get-tuple-element.208), channel_id=1, source_target_pairs={{0,3},{1,2},{2,1},{3,0},{4,7},{5,6},{6,5},{7,4},{8,11},{9,10},{10,... | collective-permute-start | bytes 110600 | tf_op jit(solution)/shard_map/ppermute | solution.py:52
  190.9 18.6 %collective-permute-start.44 = (bf16[384,128]{1,0:T(8,128)(2,1)S(1)}, bf16[384,128]{1,0:T(8,128)(2,1)S(1)}, u32[]{:S(2)}, u32[]{:S(2)}) collective-permute-start(bf16[384,128]{1,0:T(8,128)(2,1)S(1)} %copy-done.50), channel_id=1, source_target_pairs={{0,1},{1,0},{2,3},{3,2},{4,5},{5,4},{6,7},{7,6},{8,9},{9,8},{10,11... | collective-permute-start | bytes 294920 | tf_op jit(solution)/shard_map/ppermute | solution.py:52
  191.3 20.9 %collective-permute-start.45 = (bf16[384,128]{1,0:T(8,128)(2,1)S(1)}, bf16[384,128]{1,0:T(8,128)(2,1)S(1)}, u32[]{:S(2)}, u32[]{:S(2)}) collective-permute-start(bf16[384,128]{1,0:T(8,128)(2,1)S(1)} %copy-done.49), channel_id=1, source_target_pairs={{0,2},{1,3},{2,0},{3,1},{4,6},{5,7},{6,4},{7,5},{8,10},{9,11},{10,... | collective-permute-start | bytes 294920 | tf_op jit(solution)/shard_map/ppermute | solution.py:52
  191.9 22.6 %collective-permute-start.65 = (f32[32,768]{1,0:T(8,128)S(1)}, f32[32,768]{1,0:T(8,128)S(1)}, u32[]{:S(2)}, u32[]{:S(2)}) collective-permute-start(f32[32,768]{1,0:T(8,128)S(1)} %add.43), channel_id=1, source_target_pairs={{0,4},{1,5},{2,6},{3,7},{4,0},{5,1},{6,2},{7,3},{8,12},{9,13},{10,... | collective-permute-start | bytes 294920 | tf_op jit(solution)/shard_map/ppermute | solution.py:52
  195.0 7.2 %collective-permute-start.58 = (bf16[24,768]{1,0:T(8,128)(2,1)}, bf16[24,768]{1,0:T(8,128)(2,1)S(1)}, u32[]{:S(2)}, u32[]{:S(2)}) collective-permute-start(bf16[24,768]{1,0:T(8,128)(2,1)} %get-tuple-element.210), channel_id=1, source_target_pairs={{0,5},{1,4},{2,7},{3,6},{4,1},{5,0},{6,3},{7,2},{8,13},{9,12},{10,... | collective-permute-start | bytes 110600 | tf_op jit(solution)/shard_map/ppermute | solution.py:52
  202.1 7.4 %collective-permute-start.60 = (bf16[24,768]{1,0:T(8,128)(2,1)}, bf16[24,768]{1,0:T(8,128)(2,1)S(1)}, u32[]{:S(2)}, u32[]{:S(2)}) collective-permute-start(bf16[24,768]{1,0:T(8,128)(2,1)} %get-tuple-element.212), channel_id=1, source_target_pairs={{0,7},{1,6},{2,5},{3,4},{4,3},{5,2},{6,1},{7,0},{8,15},{9,14},{10,... | collective-permute-start | bytes 110600 | tf_op jit(solution)/shard_map/ppermute | solution.py:52
  206.9 10.4 %collective-permute-start.46 = (bf16[384,128]{1,0:T(8,128)(2,1)S(1)}, bf16[384,128]{1,0:T(8,128)(2,1)S(1)}, u32[]{:S(2)}, u32[]{:S(2)}) collective-permute-start(bf16[384,128]{1,0:T(8,128)(2,1)S(1)} %copy-done.48), channel_id=1, source_target_pairs={{0,3},{1,2},{2,1},{3,0},{4,7},{5,6},{6,5},{7,4},{8,11},{9,10},{10,... | collective-permute-start | bytes 294920 | tf_op jit(solution)/shard_map/ppermute | solution.py:52
  209.5 8.2 %collective-permute-start.47 = (bf16[384,128]{1,0:T(8,128)(2,1)S(1)}, bf16[384,128]{1,0:T(8,128)(2,1)S(1)}, u32[]{:S(2)}, u32[]{:S(2)}) collective-permute-start(bf16[384,128]{1,0:T(8,128)(2,1)S(1)} %copy-done.47), channel_id=1, source_target_pairs={{0,4},{1,5},{2,6},{3,7},{4,0},{5,1},{6,2},{7,3},{8,12},{9,13},{10,... | collective-permute-start | bytes 294920 | tf_op jit(solution)/shard_map/ppermute | solution.py:52
  209.5 12.5 %collective-permute-start.48 = (bf16[384,128]{1,0:T(8,128)(2,1)S(1)}, bf16[384,128]{1,0:T(8,128)(2,1)S(1)}, u32[]{:S(2)}, u32[]{:S(2)}) collective-permute-start(bf16[384,128]{1,0:T(8,128)(2,1)S(1)} %copy-done.46), channel_id=1, source_target_pairs={{0,5},{1,4},{2,7},{3,6},{4,1},{5,0},{6,3},{7,2},{8,13},{9,12},{10,... | collective-permute-start | bytes 294920 | tf_op jit(solution)/shard_map/ppermute | solution.py:52
  212.2 9.9 %collective-permute-start.49 = (bf16[384,128]{1,0:T(8,128)(2,1)S(1)}, bf16[384,128]{1,0:T(8,128)(2,1)S(1)}, u32[]{:S(2)}, u32[]{:S(2)}) collective-permute-start(bf16[384,128]{1,0:T(8,128)(2,1)S(1)} %copy-done.45), channel_id=1, source_target_pairs={{0,6},{1,7},{2,4},{3,5},{4,2},{5,3},{6,0},{7,1},{8,14},{9,15},{10,... | collective-permute-start | bytes 294920 | tf_op jit(solution)/shard_map/ppermute | solution.py:52
  214.5 7.5 %collective-permute-start.50 = (bf16[384,128]{1,0:T(8,128)(2,1)S(1)}, bf16[384,128]{1,0:T(8,128)(2,1)S(1)}, u32[]{:S(2)}, u32[]{:S(2)}) collective-permute-start(bf16[384,128]{1,0:T(8,128)(2,1)S(1)} %copy-done.44), channel_id=1, source_target_pairs={{0,7},{1,6},{2,5},{3,4},{4,3},{5,2},{6,1},{7,0},{8,15},{9,14},{10,... | collective-permute-start | bytes 294920 | tf_op jit(solution)/shard_map/ppermute | solution.py:52
  (74 other events, 861.2 us)
Sparse Core Ops, SparseCore 0:
  52.9 47.0 all-gather.4
  102.1 43.4 all-gather.6

commit v4 on v3

--- a/solution.py
+++ b/solution.py
@@ -56,8 +56,8 @@
     return jnp.concatenate([value] + [swap(value, axis, mask) for mask in masks], axis=0)
 
 
-def fan_out(slabs):
-    return [slabs[0]] + [swap(slabs[j], "expert", j) for j in range(1, len(slabs))]
+def exchange(value):
+    return lax.all_to_all(value, "expert", split_axis=0, concat_axis=0, tiled=True)
 
 
 def gather_list(value):
@@ -69,14 +69,13 @@
     return [found[index] for index in range(len(found))]
 
 
-def scatter_list(items, last=True):
+def scatter_list(items, dtype=LOW):
     bit = 1
     while len(items) > 1:
         taken = [swap(item, "dp", bit) for item in items[1::2]]
-        if len(items) == 2 and not last:
-            return items[0], taken[0]
+        kind = dtype if len(items) == 2 else LOW
         items = [
-            (kept.astype(FULL) + got.astype(FULL)).astype(kept.dtype)
+            (kept.astype(FULL) + got.astype(FULL)).astype(kind)
             for kept, got in zip(items[0::2], taken)
         ]
         bit = bit * 2
@@ -193,10 +192,10 @@
 
 def early_kernel(
     ranks, local_experts, capacity, slab, tokens_ref, routes_ref, gain_ref, d_out_ref, table_ref,
-    onehot_ref, normed_ref, hits_ref, mask_ref, mask_t_ref, bias_ref, *up_refs
+    onehot_ref, normed_ref, hits_ref, mask_ref, mask_t_ref, bias_ref, up_ref
 ):
     length = tokens_ref.shape[0]
-    normed, _ = normalize(tokens_ref[...].astype(FULL), gain_ref[...].astype(FULL))
+    normed, _ = normalize(tokens_ref[...].astype(FULL), gain_ref[0:1, :])
     normed_ref[...] = normed.astype(LOW)
     experts = hits_ref.shape[1]
     routes = jnp.broadcast_to(routes_ref[...].astype(FULL), (length, length)).T
@@ -211,8 +210,7 @@
     rank = jnp.zeros_like(route)
     for r in range(1, ranks):
         rank = rank + (route >= r * local_experts).astype(jnp.int32)
-    spot = (rank ^ lax.axis_index("expert")) * slab
-    spot = spot + (route - rank * local_experts) * capacity + placed
+    spot = rank * slab + (route - rank * local_experts) * capacity + placed
     spot = jnp.where(placed < capacity, spot, -1)
     places = lax.broadcasted_iota(jnp.int32, (length, ranks * slab), 1)
     mask = (places == spot).astype(FULL)
@@ -221,7 +219,7 @@
     mask_t_ref[...] = mask_t
     slabs = dot(mask_t, d_out_ref[...])
     for r in range(ranks):
-        up_refs[r][...] = slabs[r * slab : (r + 1) * slab].astype(LOW)
+        up_ref[r] = slabs[r * slab : (r + 1) * slab].astype(LOW)
     values = dot(table_ref[...], onehot_ref[...])
     for h in range(bias_ref.shape[0]):
         bias_ref[h] = slid_rows(values[h : h + 1], length)[:, length:]
@@ -234,7 +232,7 @@
     count = len(places)
     piece_refs, rest = rest[:count], rest[count:]
     heads_ref, weights_ref, attended_ref, hidden_ref, chance_ref = rest[:5]
-    slab_refs = rest[5:-4]
+    slabs_ref = rest[5]
     w_ref, qkv_ref, att_t_ref, sem = rest[-4:]
     copies = place_weights(places, piece_refs, w_ref, sem)
     ranks, width, columns = w_ref.shape
@@ -268,7 +266,7 @@
         att_t_ref[e * cols : (e + 1) * cols, :] = turned[3 * cols - low_lane :]
     hidden = tokens_ref[...].astype(FULL) + att_t_ref[...].T
     hidden_ref[...] = hidden
-    normed_two, _ = normalize(hidden, gain_ref[...].astype(FULL))
+    normed_two, _ = normalize(hidden, gain_ref[1:2, :])
     logits = dot(normed_two, router_t_ref[...].astype(FULL), NT, HIGHEST)
     grown = jnp.exp(logits - jnp.max(logits, axis=1, keepdims=True))
     chance = grown / jnp.sum(grown, axis=1, keepdims=True)
@@ -284,8 +282,8 @@
         row = column_to_row(high) + column_to_row(mine - high, 64)
         rows = slots[r * slab : (r + 1) * slab]
         start = rows[:, :128] + jnp.where(sub == rank_slots, row, 0.0)
-        slab_refs[r][:, :128] = start.astype(LOW)
-        slab_refs[r][:, 128:] = rows[:, 128:].astype(LOW)
+        slabs_ref[r, :, :128] = start.astype(LOW)
+        slabs_ref[r, :, 128:] = rows[:, 128:].astype(LOW)
 
 
 def upstream_kernel(pack_ref, w_out_ref, *rest):
@@ -382,51 +380,43 @@
         g_out_ref[e] = dot(act_ref[e], slot_grad, TN)
 
 
-def split_kernel(first_ref, second_ref, *out_refs):
-    slab = out_refs[0].shape[0]
-    total = first_ref[...].astype(FULL) + second_ref[...].astype(FULL)
-    for r, ref in enumerate(out_refs):
-        ref[...] = total[r * slab : (r + 1) * slab].astype(LOW)
-
-
-def joined(refs):
-    return jnp.concatenate([ref[...].astype(FULL) for ref in refs], axis=0).astype(LOW)
+def joined(ref):
+    ranks, slab, width = ref.shape
+    return ref[...].astype(FULL).reshape(ranks * slab, width).astype(LOW)
 
 
 def backward_kernel(
-    places, rank_slots, tokens_ref, gain_one_ref, gain_two_ref, router_t_ref, hits_ref, mask_ref,
+    places, rank_slots, tokens_ref, gain_ref, router_t_ref, hits_ref, mask_ref,
     up_ref, hidden_ref, chance_ref, heads_ref, weights_ref, onehot_ref, *rest
 ):
     count = len(places)
     piece_refs, rest = rest[:count], rest[count:]
-    w_ref, turned_ref, grads_ref, bias_ref, sent_ref, sem = rest[-6:]
+    (back_ref, d_input_ref, small_ref, factors_ref,
+     w_ref, turned_ref, grads_ref, bias_ref, sem) = rest
     ranks, width, columns = w_ref.shape
-    back_refs, rest = rest[:ranks], rest[ranks:-6]
-    d_input_ref, small_ref = rest[:2]
-    factor_refs = rest[2:]
     copies = place_weights(places, piece_refs, w_ref, sem)
     cols = columns // 4
     head_count = weights_ref.shape[0]
     head = width // head_count
     factor = head ** (-0.5)
     length = tokens_ref.shape[0]
-    slab = back_refs[0].shape[0]
+    slab = back_ref.shape[1]
     hidden = hidden_ref[...]
-    gain_two = gain_two_ref[...].astype(FULL)
+    gain_two = gain_ref[1:2, :]
     normed_two, scale_two = normalize(hidden, gain_two)
     mask = mask_ref[...]
     chance, hits = chance_ref[...], hits_ref[...]
     gate = jnp.sum(chance * hits, axis=1, keepdims=True)
     spread = [
-        row_to_column(ref[:, :128].astype(FULL)[rank_slots : rank_slots + 1], slab)
-        for ref in back_refs
+        row_to_column(back_ref[r, :, :128].astype(FULL)[rank_slots : rank_slots + 1], slab)
+        for r in range(ranks)
     ]
     gate_grad = dot(mask, jnp.concatenate(spread, axis=0).astype(LOW))[:, :1]
     logit_grad = chance * (hits - gate) * gate_grad
     experts = hits.shape[1]
     small_ref[:experts, :] = dot(logit_grad, normed_two, TN, HIGHEST)
     router_t = router_t_ref[...].astype(FULL)
-    normed_two_grad = dot(logit_grad, router_t, precision=HIGHEST) + dot(mask, joined(back_refs))
+    normed_two_grad = dot(logit_grad, router_t, precision=HIGHEST) + dot(mask, joined(back_ref))
     hidden_part, ffn_gain_grad = norm_back(hidden, scale_two, gain_two, normed_two_grad)
     hidden_grad = up_ref[...].astype(FULL) + hidden_part
     turned_ref[...] = hidden_grad.astype(LOW).astype(FULL).T
@@ -460,11 +450,9 @@
         part = dot(w_ref[e], jnp.concatenate(held, axis=0).astype(LOW))
         total = part if total is None else total + part
         sent = [grads_ref[m, span, :] for m in range(3)] + [turned_ref[span, :]]
-        sent_ref[e] = jnp.concatenate(sent, axis=0)
-    for e in range(ranks):
-        factor_refs[e][...] = sent_ref[lax.axis_index("expert") ^ e].astype(LOW)
+        factors_ref[e] = jnp.concatenate(sent, axis=0).astype(LOW)
     inputs = tokens_ref[...].astype(FULL)
-    gain_one = gain_one_ref[...].astype(FULL)
+    gain_one = gain_ref[0:1, :]
     _, scale_one = normalize(inputs, gain_one)
     norm_part, attn_gain_grad = norm_back(inputs, scale_one, gain_one, total.T)
     d_input_ref[...] = hidden_grad + norm_part
@@ -476,21 +464,18 @@
 
 
 def product_kernel(
-    ranks, dps, rank_slots, normed_ref, attended_ref, hidden_ref, chance_ref, hits_ref, mask_ref, *rest
+    dps, normed_ref, attended_ref, hidden_ref, chance_ref, hits_ref, mask_ref, factors_ref,
+    returned_ref, output_ref, *rest
 ):
-    factor_refs, rest = rest[:ranks], rest[ranks:]
-    returned_refs, rest = rest[:ranks], rest[ranks:]
-    output_ref, total_ref = rest[0], rest[-1]
-    piece_refs = rest[1:-1]
-    length = hidden_ref.shape[0]
-    cols = factor_refs[0].shape[0] // 4
+    piece_refs, total_ref = rest[:-1], rest[-1]
+    ranks, columns, length = factors_ref.shape
+    cols = columns // 4
     first, second = None, None
-    for j, ref in enumerate(factor_refs):
-        span = lax.axis_index("expert") ^ j
-        held = ref[...].astype(FULL)
-        part = dot(held[: 3 * cols].astype(LOW), normed_ref[span])
+    for e in range(ranks):
+        held = factors_ref[e].astype(FULL)
+        part = dot(held[: 3 * cols].astype(LOW), normed_ref[e])
         first = part if first is None else first + part
-        part = dot(held[3 * cols :].astype(LOW), attended_ref[span])
+        part = dot(held[3 * cols :].astype(LOW), attended_ref[e])
         second = part if second is None else second + part
     total = jnp.concatenate([first, second], axis=0).T
     rows = piece_refs[0].shape[0]
@@ -499,7 +484,7 @@
     for j, ref in enumerate(piece_refs):
         ref[...] = total_ref[lax.axis_index("dp") ^ j].astype(LOW)
     gate = jnp.sum(chance_ref[...] * hits_ref[...], axis=1, keepdims=True)
-    fetched = dot(mask_ref[...], joined(returned_refs))
+    fetched = dot(mask_ref[...], joined(returned_ref))
     output_ref[...] = (hidden_ref[...] + gate * fetched).astype(LOW)
 
 
@@ -551,13 +536,13 @@
     rows_here, columns_here = w_query.shape
     inner_width = dps * rows_here
     packed_rows = dps * ranks * capacity
-    gain_one = attn_gain.reshape(1, model_width)
-    gain_two = ffn_gain.reshape(1, model_width)
+    gains = jnp.stack([attn_gain, ffn_gain]).astype(FULL)
+    slabs_shape = shaped(LOW, ranks, slab, model_width)
     router_t = w_router.T
     pack = packing(local_experts, ranks, capacity, slab)
     pack, pack_t = jnp.asarray(pack, LOW), jnp.asarray(pack.T, LOW)
 
-    normed_low, hits, mask, mask_t, bias_full, *up_slabs = call(
+    normed_low, hits, mask, mask_t, bias_full, up_slabs = call(
         functools.partial(early_kernel, ranks, local_experts, capacity, slab),
         "early",
         [
@@ -566,12 +551,12 @@
             shaped(LOW, length, ranks * slab),
             shaped(LOW, ranks * slab, length),
             shaped(FULL, head_count, length, length),
-        ]
-        + [shaped(LOW, slab, model_width)] * ranks,
+            slabs_shape,
+        ],
         [
             tokens,
             routes.reshape(1, length),
-            gain_one,
+            gains,
             d_out,
             rel_bias.T,
             jnp.asarray(bucket_onehot(bucket_count, length), LOW),
@@ -582,11 +567,12 @@
     pieces, places, (normed_low, hits, mask, mask_t, bias_full, up_slabs) = gather_pieces(
         payload, (normed_low, hits, mask, mask_t, bias_full, up_slabs)
     )
-    pieces, normed_later, up_slabs = lax.optimization_barrier((pieces, normed_low, up_slabs))
+    up_arrived = exchange(up_slabs).reshape(ranks * slab, model_width)
+    pieces, normed_later, up_arrived = lax.optimization_barrier((pieces, normed_low, up_arrived))
     normed_all = lax.all_gather(normed_later, "expert", axis=0)
 
     w_shape = (ranks, inner_width, 4 * columns_here)
-    heads, weights, attended, hidden, chance, *slabs = call(
+    heads, weights, attended, hidden, chance, slabs = call(
         functools.partial(forward_kernel, places, slab, rank_slots),
         "attention_forward",
         [
@@ -595,9 +581,9 @@
             shaped(LOW, length, inner_width),
             shaped(FULL, length, model_width),
             shaped(FULL, length, experts_total),
-        ]
-        + [shaped(LOW, slab, model_width)] * ranks,
-        [tokens, normed_low, seg_ids, bias_full, gain_two, router_t, hits, mask_t],
+            slabs_shape,
+        ],
+        [tokens, normed_low, seg_ids, bias_full, gains, router_t, hits, mask_t],
         pieces,
         [
             pltpu.VMEM(w_shape, LOW),
@@ -607,8 +593,8 @@
         ],
     )
 
-    up_pieces = gather_list(jnp.concatenate(fan_out(up_slabs), axis=0))
-    row_pieces = gather_list(jnp.concatenate(fan_out(slabs), axis=0))
+    up_pieces = gather_list(up_arrived)
+    row_pieces = gather_list(exchange(slabs).reshape(ranks * slab, model_width))
     attended_all = lax.all_gather(attended, "expert", axis=0)
     by_expert = (local_experts, packed_rows)
     up_rows, up_act = call(
@@ -635,8 +621,9 @@
             pltpu.VMEM((*by_expert, 128), LOW),
         ],
     )
-    slab_shapes = [shaped(LOW, slab, model_width)] * ranks
-    back = fan_out(call(split_kernel, "back_slabs", slab_shapes, scatter_list(back, last=False)))
+    back = scatter_list(back).reshape(ranks, slab, model_width)
+    back, activated = lax.optimization_barrier((back, activated))
+    back = exchange(back)
     *returned, first_grad, second_grad = call(
         functools.partial(expert_grad_kernel, dps),
         "expert_gradients",
@@ -645,23 +632,20 @@
         [pack_t, w_out, slot_rows, activated, pre_grad, gates, up_rows],
         scratch=[pltpu.VMEM((*by_expert, model_width), LOW)],
     )
-    returned = fan_out(
-        call(split_kernel, "returned_slabs", slab_shapes, scatter_list(returned, last=False))
-    )
+    returned = scatter_list(returned).reshape(ranks, slab, model_width)
 
     small_rows = -(-(experts_total + 2 + head_count) // 8) * 8
-    d_input, small, *factors = call(
+    d_input, small, factors = call(
         functools.partial(backward_kernel, places, rank_slots),
         "attention_backward",
         [
             shaped(FULL, length, model_width),
             shaped(FULL, small_rows, model_width),
-        ]
-        + [shaped(LOW, 4 * columns_here, length)] * ranks,
+            shaped(LOW, ranks, 4 * columns_here, length),
+        ],
         [
             tokens,
-            gain_one,
-            gain_two,
+            gains,
             router_t,
             hits,
             mask,
@@ -678,23 +662,23 @@
             pltpu.VMEM((inner_width, length), FULL),
             pltpu.VMEM((3, inner_width, length), FULL),
             pltpu.VMEM((head_count, 2 * length), FULL),
-            pltpu.VMEM((ranks, 4 * columns_here, length), FULL),
             pltpu.SemaphoreType.DMA,
         ],
-        back,
-    )
-
-    factors = fan_out(factors)
+        [back],
+    )
+
+    factors, returned = lax.optimization_barrier((factors, returned))
+    factors = exchange(factors)
+    returned = exchange(returned)
     small = all_sum(small)
     output, *grads = call(
-        functools.partial(product_kernel, ranks, dps, rank_slots),
+        functools.partial(product_kernel, dps),
         "weight_gradients",
         [shaped(LOW, length, model_width)] + [shaped(LOW, rows_here, 4 * columns_here)] * dps,
-        [normed_all, attended_all, hidden, chance, hits, mask, *factors, *returned],
+        [normed_all, attended_all, hidden, chance, hits, mask, factors, returned],
         scratch=[pltpu.VMEM((dps, rows_here, 4 * columns_here), FULL)],
     )
-    kept, got = scatter_list(grads, last=False)
-    grads = kept.astype(FULL) + got.astype(FULL)
+    grads = scatter_list(grads, FULL)
     g_query, g_key, g_value, g_output = (
         grads[:, i * columns_here : (i + 1) * columns_here] for i in range(4)
     )

time: 246 us -> 245 us (level)
  starting transfers between devices: 84.9 us -> 42.4 us
  blocking collectives: 0 us -> 35.1 us
  waiting for transfers between devices: 65.2 us -> 80.6 us
  local copies, waits for them, and re-layouts: 15 us -> 9.59 us
  Pallas kernels: 58.1 us -> 54.4 us
    ppermute x69 -> x34, starting transfers between devices: 84.9 us -> 30.8 us  [swap(): return lax.ppermute(value, axis, [(i, i ^ mask) for i in range(count)])]
    all_to_all x0 -> x2, blocking collectives: none -> 35.1 us  [exchange(): lax.all_to_all(value, 'expert', split_axis=0, concat_axis=0, tiled=True)]
    all_to_all x0 -> x3, waiting for transfers between devices: none -> 21 us  [exchange(): lax.all_to_all(value, 'expert', split_axis=0, concat_axis=0, tiled=True)]
    all_to_all x0 -> x3, starting transfers between devices: none -> 11.3 us  [exchange(): lax.all_to_all(value, 'expert', split_axis=0, concat_axis=0, tiled=True)]
    ppermute x69 -> x34, waiting for transfers between devices: 65.1 us -> 59.5 us  [swap(): return lax.ppermute(value, axis, [(i, i ^ mask) for i in range(count)])]
    unnamed x116 -> x40, local copies, waits for them, and re-layouts: 10.4 us -> 5.54 us
    pallas_call x9 -> x7, Pallas kernels: 58.1 us -> 54.4 us  [call(): pl.pallas_call(kernel, out_shape=tuple(out_shape), in_specs=[VMEM] * len(...]
    convert_element_type x5 -> x6, other arithmetic: 3.63 us -> 5.52 us  [the longest x5 4.92 us: scatter_list(): (kept.astype(FULL) + got.astype(FULL)).astype(kind)]
  transfers between devices with their start and end apart: 71 -> 39, of which waited for: 28 -> 18; matrix products, arithmetic and copies ran while one was open for 5% -> 4% of each run, Pallas kernels for 22% -> 20%
where the time goes in v4:
time: 245 us; the launch traced here: 244 us
  waiting for transfers between devices  80.6 us (33%)
  Pallas kernels  54.4 us (22%)
  starting transfers between devices  42.4 us (17%)
  blocking collectives  35.1 us (14%)
  between operations  14.5 us (6%)
  local copies, waits for them, and re-layouts  9.59 us (4%)
  other arithmetic  7.79 us (3%)
    ppermute x34, waiting for transfers between devices, swap(): return lax.ppermute(value, axis, [(i, i ^ mask) for i in range(count)])  59.5 us
    pallas_call x7, Pallas kernels, call(): pl.pallas_call(kernel, out_shape=tuple(out_shape), in_specs=[VMEM] * len(...  54.4 us
    all_to_all x2, blocking collectives, exchange(): lax.all_to_all(value, 'expert', split_axis=0, concat_axis=0, tiled=True)  35.1 us
    ppermute x34, starting transfers between devices, swap(): return lax.ppermute(value, axis, [(i, i ^ mask) for i in range(count)])  30.8 us
    all_to_all x3, waiting for transfers between devices, exchange(): lax.all_to_all(value, 'expert', split_axis=0, concat_axis=0, tiled=True)  21 us
    all_to_all x3, starting transfers between devices, exchange(): lax.all_to_all(value, 'expert', split_axis=0, concat_axis=0, tiled=True)  11.3 us
    unnamed x40, local copies, waits for them, and re-layouts  5.54 us
    convert_element_type x5, other arithmetic, scatter_list(): (kept.astype(FULL) + got.astype(FULL)).astype(kind)  4.92 us
  transfers between devices with their start and end apart: 39, of which 18 were waited for; matrix products, arithmetic and copies ran while one was open for 4% of the time, Pallas kernels for 20%

profile of v4, /device:TPU:0, one launch (start us, length us, event | category | flops | bytes accessed | tf_op | source)
XLA Modules:
  0.0 244.3 jit_solution(6772587017106036395)
XLA Ops:
  7.2 1.0 pad_maximum_fusion.4
  8.3 5.1 %collective-permute-start.5 = (bf16[1,96,384]{2,1,0:T(8,128)(2,1)S(1)}, bf16[1,96,384]{2,1,0:T(8,128)(2,1)S(1)}, u32[]{:S(2)}, u32[]{:S(2)}) collective-permute-start(bf16[1,96,384]{2,1,0:T(8,128)(2,1)S(1)} %get-tuple-element.134), channel_id=1, source_target_pairs={{0,6},{1,7},{2,4},{3,5},{4,2},{5,3},{6,0},{7,1},{8,14},{9,15},{10,... | collective-permute-start | bytes 221192 | tf_op jit(solution)/shard_map/ppermute | solution.py:52
  14.0 3.7 %collective-permute-start.2 = (bf16[1,96,384]{2,1,0:T(8,128)(2,1)S(1)}, bf16[1,96,384]{2,1,0:T(8,128)(2,1)S(1)}, u32[]{:S(2)}, u32[]{:S(2)}) collective-permute-start(bf16[1,96,384]{2,1,0:T(8,128)(2,1)S(1)} %get-tuple-element.135), channel_id=1, source_target_pairs={{0,6},{1,7},{2,4},{3,5},{4,2},{5,3},{6,0},{7,1},{8,14},{9,15},{10,... | collective-permute-start | bytes 221192 | tf_op jit(solution)/shard_map/ppermute | solution.py:52
  19.7 3.4 %early.1 = (bf16[128,768]{1,0:T(8,128)(2,1)}, f32[128,16]{1,0:T(8,128)}, bf16[128,192]{1,0:T(8,128)(2,1)}, bf16[192,128]{1,0:T(8,128)(2,1)}, f32[12,128,128]{2,1,0:T(8,128)}, /*index=5*/bf16[8,24,768]{2,1,0:T(8,128)(2,1)}) custom-call(bf16[128,768]{1,0:T(8,128)(2,1)} %tokens_ref.5, s32[1,128]{1,0:T(1,128)} %bitcast.35, ...), custom_call_target="tpu_custom_call" | custom-call | tf_op jit(solution)/shard_map/early/pallas_call | solution.py:501
  23.9 2.2 collective-permute-done.1
  26.0 1.5 collective-permute-done
  27.6 1.6 collective-permute-start.6
  29.1 1.5 collective-permute-start.10
  30.7 4.6 %collective-permute-done.6 = bf16[1,4,96,384]{3,2,1,0:T(8,128)(2,1)S(1)} collective-permute-done((bf16[1,4,96,384]{3,2,1,0:T(8,128)(2,1)S(1)}, bf16[1,4,96,384]{3,2,1,0:T(8,128)(2,1)S(1)}, u32[]{:S(2)}, u32[]{:S(2)}) %collective-permute-start.6) | collective-permute-done | bytes 294944 | tf_op jit(solution)/shard_map/ppermute | solution.py:52
  35.4 1.7 collective-permute-start.7
  37.4 1.3 collective-permute-start.11
  39.2 10.0 %collective-permute-done.7.rest_1_ = bf16[2,4,96,384]{3,2,1,0:T(8,128)(2,1)S(1)} collective-permute-done((bf16[2,4,96,384]{3,2,1,0:T(8,128)(2,1)S(1)}, bf16[2,4,96,384]{3,2,1,0:T(8,128)(2,1)S(1)}, u32[]{:S(2)}, u32[]{:S(2)}) %collective-permute-start.7) | collective-permute-done | bytes 589856 | tf_op jit(solution)/shard_map/ppermute | solution.py:52
  50.1 15.5 %all_to_all.25 = bf16[8,24,768]{2,1,0:T(8,128)(2,1)} all-to-all(bf16[8,24,768]{2,1,0:T(8,128)(2,1)S(1)} %copy-done.17), channel_id=1, replica_groups=mesh['dp'=4,'expert'=8] {'expert'}, dimensions={0} | all-to-all | bytes 589824 | tf_op jit(solution)/shard_map/all_to_all | solution.py:60
  65.7 0.9 copy-done.7
  67.4 9.9 %attention_forward.1 = (bf16[3,768,128]{2,1,0:T(8,128)(2,1)}, f32[12,128,128]{2,1,0:T(8,128)}, bf16[128,768]{1,0:T(8,128)(2,1)}, f32[128,768]{1,0:T(8,128)}, f32...) custom-call(bf16[128,768]{1,0:T(8,128)(2,1)} %tokens_ref.5, bf16[128,768]{1,0:T(8,128)(2,1)} %get-tuple-element.80.normed_ref, ...), custom_call_target="tpu_custom_call" | custom-call | tf_op jit(solution)/shard_map/attention_forward/pallas_call | solution.py:501
  77.3 3.4 %all-to-all-start.1 = ((bf16[8,24,768]{2,1,0:T(8,128)(2,1)}), bf16[8,24,768]{2,1,0:T(8,128)(2,1)S(1)}, u32[]{:S(2)}, u32[]{:S(2)}) async-start(bf16[8,24,768]{2,1,0:T(8,128)(2,1)} %get-tuple-element.100), calls=%async_computation.1 | async-start | bytes 589824 | tf_op jit(solution)/shard_map/all_to_all | solution.py:60
  81.6 9.8 %all-to-all-done.1 = bf16[8,24,768]{2,1,0:T(8,128)(2,1)S(1)} async-done(((bf16[8,24,768]{2,1,0:T(8,128)(2,1)}), bf16[8,24,768]{2,1,0:T(8,128)(2,1)S(1)}, u32[]{:S(2)}, u32[]{:S(2)}) %all-to-all-start.1) | async-done | bytes 294944 | tf_op jit(solution)/shard_map/all_to_all | solution.py:60
  91.4 1.3 collective-permute-start.18
  93.2 6.3 %collective-permute-done.18.rest_2_ = bf16[192,768]{1,0:T(8,128)(2,1)S(1)} collective-permute-done((bf16[192,768]{1,0:T(8,128)(2,1)S(1)}, bf16[192,768]{1,0:T(8,128)(2,1)S(1)}, u32[]{:S(2)}, u32[]{:S(2)}) %collective-permute-start.18) | collective-permute-done | bytes 294944 | tf_op jit(solution)/shard_map/ppermute | solution.py:52
  101.1 4.5 %upstream_rows.1 = (bf16[2,320,768]{2,1,0:T(8,128)(2,1)}, f32[2,320,768]{2,1,0:T(8,128)}) custom-call(bf16[160,192]{1,0:T(8,128)(2,1)} %constant.8.clone.pack_ref, bf16[2,768,768]{2,1,0:T(8,128)(2,1)} %w_out_ref.3, bf16[192,768]{1,0:T(8,128)(2,1)} %bitcast.23, bf16[192,768]{1,0:T(8,128)(2,1)} %copy-done.15, bf16[192,768]{1,0:T(8,128)(2,1)} %copy-done.12, ...), custom_call_target="tpu_custom_call" | custom-call | tf_op jit(solution)/shard_map/upstream_rows/pallas_call | solution.py:501
  106.3 9.9 %experts.1 = (bf16[192,768]{1,0:T(8,128)(2,1)}, bf16[192,768]{1,0:T(8,128)(2,1)}, bf16[192,768]{1,0:T(8,128)(2,1)}, bf16[192,768]{1,0:T(8,128)(2,1)}, bf16[2,320...) custom-call(bf16[160,192]{1,0:T(8,128)(2,1)} %constant.8.clone.pack_re, ...), custom_call_target="tpu_custom_call" | custom-call | tf_op jit(solution)/shard_map/experts/pallas_call | solution.py:501
  116.8 1.3 collective-permute-done.21
  118.2 1.0 add_convert_fusion.4
  119.2 1.3 collective-permute-start.22
  120.5 8.1 %collective-permute-done.22 = bf16[192,768]{1,0:T(8,128)(2,1)S(1)} collective-permute-done((bf16[192,768]{1,0:T(8,128)(2,1)S(1)}, bf16[192,768]{1,0:T(8,128)(2,1)S(1)}, u32[]{:S(2)}, u32[]{:S(2)}) %collective-permute-start.22) | collective-permute-done | bytes 294944 | tf_op jit(solution)/shard_map/ppermute | solution.py:52
  128.6 1.8 add_convert_fusion.3
  130.3 10.0 %expert_gradients.1 = (bf16[192,768]{1,0:T(8,128)(2,1)}, bf16[192,768]{1,0:T(8,128)(2,1)}, bf16[192,768]{1,0:T(8,128)(2,1)}, bf16[192,768]{1,0:T(8,128)(2,1)}, f...) custom-call(bf16[192,160]{1,0:T(8,128)(2,1)} %constant.9.clone.pack_t_ref, bf16[2,768,768]{2,1,0:T(8,128)(2,1)} %w_out_ref.3, ...), custom_call_target="tpu_custom_call" | custom-call | tf_op jit(solution)/shard_map/expert_gradients/pallas_call | solution.py:501
  140.4 4.3 %all-to-all-start.2 = ((bf16[8,24,768]{2,1,0:T(8,128)(2,1)}), bf16[8,24,768]{2,1,0:T(8,128)(2,1)S(1)}, u32[]{:S(2)}, u32[]{:S(2)}) async-start(bf16[8,24,768]{2,1,0:T(8,128)(2,1)} %bitcast.11), calls=%async_computation.2 | async-start | bytes 589824 | tf_op jit(solution)/shard_map/all_to_all | solution.py:60
  144.9 1.0 add_convert_fusion.1
  145.9 1.1 collective-permute-start.25
  147.0 11.2 %all-to-all-done.2.rest_8_ = bf16[8,24,768]{2,1,0:T(8,128)(2,1)S(1)} async-done(((bf16[8,24,768]{2,1,0:T(8,128)(2,1)}), bf16[8,24,768]{2,1,0:T(8,128)(2,1)S(1)}, u32[]{:S(2)}, u32[]{:S(2)}) %all-to-all-start.2) | async-done | bytes 294944 | tf_op jit(solution)/shard_map/all_to_all | solution.py:60
  158.9 12.0 %attention_backward.1 = (f32[128,768]{1,0:T(8,128)}, f32[32,768]{1,0:T(8,128)}, bf16[8,384,128]{2,1,0:T(8,128)(2,1)}) custom-call(bf16[128,768]{1,0:T(8,128)(2,1)} %tokens_ref.5, f32[2,768]{1,0:T(2,128)} %maximum_convert_fusion.gain_ref, bf16[16,768]{1,0:T(8,128)(2,1)} %bitcast.33, f32[128,16]{1,0:T(8,128)} %get-tuple-element.82.hits_ref, ...), custom_call_target="tpu_custom_call" | custom-call | tf_op jit(solution)/shard_map/attention_backward/pallas_call | solution.py:501
  171.1 19.6 %all_to_all.26.returned_ref = bf16[8,24,768]{2,1,0:T(8,128)(2,1)} all-to-all(bf16[8,24,768]{2,1,0:T(8,128)(2,1)S(1)} %bitcast.31), channel_id=1, replica_groups=mesh['dp'=4,'expert'=8] {'expert'}, dimensions={0} | all-to-all | bytes 589824 | tf_op jit(solution)/shard_map/all_to_all | solution.py:60
  190.6 3.5 %all-to-all-start.3 = ((bf16[8,384,128]{2,1,0:T(8,128)(2,1)}), bf16[8,384,128]{2,1,0:T(8,128)(2,1)S(1)}, u32[]{:S(2)}, u32[]{:S(2)}) async-start(bf16[8,384,128]{2,1,0:T(8,128)(2,1)} %get-tuple-element.117), calls=%async_computation.3 | async-start | bytes 1572864 | tf_op jit(solution)/shard_map/all_to_all | solution.py:60
  194.3 1.3 collective-permute-done.26
  195.6 1.3 collective-permute-start.27
  196.9 3.6 %collective-permute-done.27 = f32[32,768]{1,0:T(8,128)S(1)} collective-permute-done((f32[32,768]{1,0:T(8,128)S(1)}, f32[32,768]{1,0:T(8,128)S(1)}, u32[]{:S(2)}, u32[]{:S(2)}) %collective-permute-start.27) | collective-permute-done | bytes 98336 | tf_op jit(solution)/shard_map/ppermute | solution.py:52
  200.5 1.9 collective-permute-start.28
  202.4 3.8 %collective-permute-done.28 = f32[32,768]{1,0:T(8,128)S(1)} collective-permute-done((f32[32,768]{1,0:T(8,128)S(1)}, f32[32,768]{1,0:T(8,128)S(1)}, u32[]{:S(2)}, u32[]{:S(2)}) %collective-permute-start.28) | collective-permute-done | bytes 98336 | tf_op jit(solution)/shard_map/ppermute | solution.py:52
  206.3 2.6 %collective-permute-start.29 = (f32[32,768]{1,0:T(8,128)S(1)}, f32[32,768]{1,0:T(8,128)S(1)}, u32[]{:S(2)}, u32[]{:S(2)}) collective-permute-start(f32[32,768]{1,0:T(8,128)S(1)} %add.50), channel_id=1, source_target_pairs={{0,2},{1,3},{2,0},{3,1},{4,6},{5,7},{6,4},{7,5},{8,10},{9,11},{10,... | collective-permute-start | bytes 294920 | tf_op jit(solution)/shard_map/ppermute | solution.py:52
  208.9 5.5 %collective-permute-done.29 = f32[32,768]{1,0:T(8,128)S(1)} collective-permute-done((f32[32,768]{1,0:T(8,128)S(1)}, f32[32,768]{1,0:T(8,128)S(1)}, u32[]{:S(2)}, u32[]{:S(2)}) %collective-permute-start.29) | collective-permute-done | bytes 98336 | tf_op jit(solution)/shard_map/ppermute | solution.py:52
  214.4 1.0 collective-permute-start.30
  215.4 5.9 %collective-permute-done.30 = f32[32,768]{1,0:T(8,128)S(1)} collective-permute-done((f32[32,768]{1,0:T(8,128)S(1)}, f32[32,768]{1,0:T(8,128)S(1)}, u32[]{:S(2)}, u32[]{:S(2)}) %collective-permute-start.30) | collective-permute-done | bytes 98336 | tf_op jit(solution)/shard_map/ppermute | solution.py:52
  222.3 4.8 %weight_gradients.1 = (bf16[128,768]{1,0:T(8,128)(2,1)}, bf16[192,384]{1,0:T(8,128)(2,1)}, bf16[192,384]{1,0:T(8,128)(2,1)}, bf16[192,384]{1,0:T(8,128)(2,1)}, bf16[192,384]{1,0:T(8,128)(2,1)}) custom-call(bf16[8,128,768]{2,1,0:T(8,128)(2,1)} %bitcast.19, bf16[8,128,768]{2,1,0:T(8,128)(2,1)} %bitcast.20, f32[128,768]{1,0:T(8,128)} %get-tuple-element.93.hidden_ref, ...), custom_call_target="tpu_custom_call" | custom-call | tf_op jit(solution)/shard_map/weight_gradients/pallas_call | solution.py:501
  228.7 1.0 add_convert_fusion.6
  229.7 1.0 collective-permute-start.33
  231.9 3.7 %collective-permute-done.33 = bf16[192,384]{1,0:T(8,128)(2,1)S(1)} collective-permute-done((bf16[192,384]{1,0:T(8,128)(2,1)S(1)}, bf16[192,384]{1,0:T(8,128)(2,1)S(1)}, u32[]{:S(2)}, u32[]{:S(2)}) %collective-permute-start.33) | collective-permute-done | bytes 147488 | tf_op jit(solution)/shard_map/ppermute | solution.py:52
  235.7 1.0 convert_add_fusion
  (105 shorter events, 16.0 us)
Async XLA Ops:
  7.2 214.2 %all-gather.5.cloned.1.call-start = ((), (), s32[]{:S(2)}) async-start(), calls=%async_computation.5 | async-start | bytes 1769472 | tf_op jit(solution)/shard_map/all_gather | solution.py:572
  8.3 14.8 %collective-permute-start.5 = (bf16[1,96,384]{2,1,0:T(8,128)(2,1)S(1)}, bf16[1,96,384]{2,1,0:T(8,128)(2,1)S(1)}, u32[]{:S(2)}, u32[]{:S(2)}) collective-permute-start(bf16[1,96,384]{2,1,0:T(8,128)(2,1)S(1)} %get-tuple-element.134), channel_id=1, source_target_pairs={{0,6},{1,7},{2,4},{3,5},{4,2},{5,3},{6,0},{7,1},{8,14},{9,15},{10,... | collective-permute-start | bytes 221192 | tf_op jit(solution)/shard_map/ppermute | solution.py:52
  13.4 10.4 %collective-permute-start.4 = (bf16[1,96,384]{2,1,0:T(8,128)(2,1)S(1)}, bf16[1,96,384]{2,1,0:T(8,128)(2,1)S(1)}, u32[]{:S(2)}, u32[]{:S(2)}) collective-permute-start(bf16[1,96,384]{2,1,0:T(8,128)(2,1)S(1)} %get-tuple-element.134), channel_id=1, source_target_pairs={{0,4},{1,5},{2,6},{3,7},{4,0},{5,1},{6,2},{7,3},{8,12},{9,13},{10,... | collective-permute-start | bytes 221192 | tf_op jit(solution)/shard_map/ppermute | solution.py:52
  13.4 10.4 %collective-permute-start.3 = (bf16[1,96,384]{2,1,0:T(8,128)(2,1)S(1)}, bf16[1,96,384]{2,1,0:T(8,128)(2,1)S(1)}, u32[]{:S(2)}, u32[]{:S(2)}) collective-permute-start(bf16[1,96,384]{2,1,0:T(8,128)(2,1)S(1)} %get-tuple-element.134), channel_id=1, source_target_pairs={{0,2},{1,3},{2,0},{3,1},{4,6},{5,7},{6,4},{7,5},{8,10},{9,11},{10,... | collective-permute-start | bytes 221192 | tf_op jit(solution)/shard_map/ppermute | solution.py:52
  14.0 9.8 %collective-permute-start.2 = (bf16[1,96,384]{2,1,0:T(8,128)(2,1)S(1)}, bf16[1,96,384]{2,1,0:T(8,128)(2,1)S(1)}, u32[]{:S(2)}, u32[]{:S(2)}) collective-permute-start(bf16[1,96,384]{2,1,0:T(8,128)(2,1)S(1)} %get-tuple-element.135), channel_id=1, source_target_pairs={{0,6},{1,7},{2,4},{3,5},{4,2},{5,3},{6,0},{7,1},{8,14},{9,15},{10,... | collective-permute-start | bytes 221192 | tf_op jit(solution)/shard_map/ppermute | solution.py:52
  17.8 8.3 %collective-permute-start.1 = (bf16[1,96,384]{2,1,0:T(8,128)(2,1)S(1)}, bf16[1,96,384]{2,1,0:T(8,128)(2,1)S(1)}, u32[]{:S(2)}, u32[]{:S(2)}) collective-permute-start(bf16[1,96,384]{2,1,0:T(8,128)(2,1)S(1)} %get-tuple-element.135), channel_id=1, source_target_pairs={{0,4},{1,5},{2,6},{3,7},{4,0},{5,1},{6,2},{7,3},{8,12},{9,13},{10,... | collective-permute-start | bytes 221192 | tf_op jit(solution)/shard_map/ppermute | solution.py:52
  23.1 4.4 %collective-permute-start = (bf16[1,96,384]{2,1,0:T(8,128)(2,1)S(1)}, bf16[1,96,384]{2,1,0:T(8,128)(2,1)S(1)}, u32[]{:S(2)}, u32[]{:S(2)}) collective-permute-start(bf16[1,96,384]{2,1,0:T(8,128)(2,1)S(1)} %get-tuple-element.135), channel_id=1, source_target_pairs={{0,2},{1,3},{2,0},{3,1},{4,6},{5,7},{6,4},{7,5},{8,10},{9,11},{10,... | collective-permute-start | bytes 221192 | tf_op jit(solution)/shard_map/ppermute | solution.py:52
  27.6 22.5 %copy-start.17 = (bf16[8,24,768]{2,1,0:T(8,128)(2,1)S(1)}, bf16[8,24,768]{2,1,0:T(8,128)(2,1)}, u32[]{:S(2)}) copy-start(bf16[8,24,768]{2,1,0:T(8,128)(2,1)} %get-tuple-element.79) | copy-start | bytes 884740
  27.6 7.7 %collective-permute-start.6 = (bf16[1,4,96,384]{3,2,1,0:T(8,128)(2,1)S(1)}, bf16[1,4,96,384]{3,2,1,0:T(8,128)(2,1)S(1)}, u32[]{:S(2)}, u32[]{:S(2)}) collective-permute-start(bf16[1,4,96,384]{3,2,1,0:T(8,128)(2,1)S(1)} %bitcast.29), channel_id=1, source_target_pairs={{0,1},{1,0},{2,3},{3,2},{4,5},{5,4},{6,7},{7,6},{8,9},{9,8},{10,11... | collective-permute-start | bytes 884744 | tf_op jit(solution)/shard_map/ppermute | solution.py:52
  29.1 8.2 %collective-permute-start.10 = (bf16[1,4,96,384]{3,2,1,0:T(8,128)(2,1)S(1)}, bf16[1,4,96,384]{3,2,1,0:T(8,128)(2,1)S(1)}, u32[]{:S(2)}, u32[]{:S(2)}) collective-permute-start(bf16[1,4,96,384]{3,2,1,0:T(8,128)(2,1)S(1)} %bitcast.27), channel_id=1, source_target_pairs={{0,16},{8,24},{16,0},{24,8},{1,17},{9,25},{17,1},{25,9},{2,18},{10... | collective-permute-start | bytes 884744 | tf_op jit(solution)/shard_map/ppermute | solution.py:52
  35.4 32.0 %copy-start = (bf16[2,4,96,384]{3,2,1,0:T(8,128)(2,1)}, bf16[2,4,96,384]{3,2,1,0:T(8,128)(2,1)S(1)}, u32[]{:S(2)}) copy-start(bf16[2,4,96,384]{3,2,1,0:T(8,128)(2,1)S(1)} %pad_maximum_fusion.rest_0_) | copy-start | bytes 1769476
  35.4 13.9 %collective-permute-start.7 = (bf16[2,4,96,384]{3,2,1,0:T(8,128)(2,1)S(1)}, bf16[2,4,96,384]{3,2,1,0:T(8,128)(2,1)S(1)}, u32[]{:S(2)}, u32[]{:S(2)}) collective-permute-start(bf16[2,4,96,384]{3,2,1,0:T(8,128)(2,1)S(1)} %pad_maximum_fusion.rest_0_), channel_id=1, source_target_pairs={{0,16},{8,24},{16,0},{24,8},{1,17},{9,25},{17,1},{25,9},{2,18},{10... | collective-permute-start | bytes 1769480 | tf_op jit(solution)/shard_map/ppermute | solution.py:52
  37.4 30.0 %copy-start.1 = (bf16[2,4,96,384]{3,2,1,0:T(8,128)(2,1)}, bf16[2,4,96,384]{3,2,1,0:T(8,128)(2,1)S(1)}, u32[]{:S(2)}) copy-start(bf16[2,4,96,384]{3,2,1,0:T(8,128)(2,1)S(1)} %pad_maximum_fusion.1.rest_4_) | copy-start | bytes 1769476
  37.4 12.7 %collective-permute-start.11 = (bf16[2,4,96,384]{3,2,1,0:T(8,128)(2,1)S(1)}, bf16[2,4,96,384]{3,2,1,0:T(8,128)(2,1)S(1)}, u32[]{:S(2)}, u32[]{:S(2)}) collective-permute-start(bf16[2,4,96,384]{3,2,1,0:T(8,128)(2,1)S(1)} %pad_maximum_fusion.1.rest_4_), channel_id=1, source_target_pairs={{0,1},{1,0},{2,3},{3,2},{4,5},{5,4},{6,7},{7,6},{8,9},{9,8},{10,11... | collective-permute-start | bytes 1769480 | tf_op jit(solution)/shard_map/ppermute | solution.py:52
  38.7 26.9 %collective-permute-start.8 = (bf16[2,4,96,384]{3,2,1,0:T(8,128)(2,1)S(1)}, bf16[2,4,96,384]{3,2,1,0:T(8,128)(2,1)S(1)}, u32[]{:S(2)}, u32[]{:S(2)}) collective-permute-start(bf16[2,4,96,384]{3,2,1,0:T(8,128)(2,1)S(1)} %pad_maximum_fusion.rest_0_), channel_id=1, source_target_pairs={{0,8},{8,0},{16,24},{24,16},{1,9},{9,1},{17,25},{25,17},{2,10},{10... | collective-permute-start | bytes 1769480 | tf_op jit(solution)/shard_map/ppermute | solution.py:52
  38.7 26.9 %collective-permute-start.12 = (bf16[2,4,96,384]{3,2,1,0:T(8,128)(2,1)S(1)}, bf16[2,4,96,384]{3,2,1,0:T(8,128)(2,1)S(1)}, u32[]{:S(2)}, u32[]{:S(2)}) collective-permute-start(bf16[2,4,96,384]{3,2,1,0:T(8,128)(2,1)S(1)} %pad_maximum_fusion.1.rest_4_), channel_id=1, source_target_pairs={{0,8},{8,0},{16,24},{24,16},{1,9},{9,1},{17,25},{25,17},{2,10},{10... | collective-permute-start | bytes 1769480 | tf_op jit(solution)/shard_map/ppermute | solution.py:52
  49.3 18.1 %copy-start.3 = (bf16[2,4,96,384]{3,2,1,0:T(8,128)(2,1)}, bf16[2,4,96,384]{3,2,1,0:T(8,128)(2,1)S(1)}, u32[]{:S(2)}) copy-start(bf16[2,4,96,384]{3,2,1,0:T(8,128)(2,1)S(1)} %collective-permute-done.7.rest_1_) | copy-start | bytes 1769476
  49.3 16.4 %collective-permute-start.9 = (bf16[2,4,96,384]{3,2,1,0:T(8,128)(2,1)S(1)}, bf16[2,4,96,384]{3,2,1,0:T(8,128)(2,1)S(1)}, u32[]{:S(2)}, u32[]{:S(2)}) collective-permute-start(bf16[2,4,96,384]{3,2,1,0:T(8,128)(2,1)S(1)} %collective-permute-done.7.rest_1_), channel_id=1, source_target_pairs={{0,8},{8,0},{16,24},{24,16},{1,9},{9,1},{17,25},{25,17},{2,10},{10... | collective-permute-start | bytes 1769480 | tf_op jit(solution)/shard_map/ppermute | solution.py:52
  50.1 17.3 %copy-start.4 = (bf16[2,4,96,384]{3,2,1,0:T(8,128)(2,1)}, bf16[2,4,96,384]{3,2,1,0:T(8,128)(2,1)S(1)}, u32[]{:S(2)}) copy-start(bf16[2,4,96,384]{3,2,1,0:T(8,128)(2,1)S(1)} %collective-permute-done.11.rest_5_) | copy-start | bytes 1769476
  50.1 15.6 %collective-permute-start.13 = (bf16[2,4,96,384]{3,2,1,0:T(8,128)(2,1)S(1)}, bf16[2,4,96,384]{3,2,1,0:T(8,128)(2,1)S(1)}, u32[]{:S(2)}, u32[]{:S(2)}) collective-permute-start(bf16[2,4,96,384]{3,2,1,0:T(8,128)(2,1)S(1)} %collective-permute-done.11.rest_5_), channel_id=1, source_target_pairs={{0,8},{8,0},{16,24},{24,16},{1,9},{9,1},{17,25},{25,17},{2,10},{10... | collective-permute-start | bytes 1769480 | tf_op jit(solution)/shard_map/ppermute | solution.py:52
  77.3 14.0 %all-to-all-start.1 = ((bf16[8,24,768]{2,1,0:T(8,128)(2,1)}), bf16[8,24,768]{2,1,0:T(8,128)(2,1)S(1)}, u32[]{:S(2)}, u32[]{:S(2)}) async-start(bf16[8,24,768]{2,1,0:T(8,128)(2,1)} %get-tuple-element.100), calls=%async_computation.1 | async-start | bytes 589824 | tf_op jit(solution)/shard_map/all_to_all | solution.py:60
  80.8 140.7 %all-gather.7.cloned.1.call-start = ((), (), s32[]{:S(2)}) async-start(), calls=%async_computation.6 | async-start | bytes 1769472 | tf_op jit(solution)/shard_map/all_gather | solution.py:598
  81.0 11.7 %collective-permute-start.15 = (bf16[192,768]{1,0:T(8,128)(2,1)}, bf16[192,768]{1,0:T(8,128)(2,1)S(1)}, u32[]{:S(2)}, u32[]{:S(2)}) collective-permute-start(bf16[192,768]{1,0:T(8,128)(2,1)} %bitcast.21), channel_id=1, source_target_pairs={{0,16},{8,24},{16,0},{24,8},{1,17},{9,25},{17,1},{25,9},{2,18},{10... | collective-permute-start | bytes 884744 | tf_op jit(solution)/shard_map/ppermute | solution.py:52
  91.4 14.2 %copy-start.9 = (bf16[8,24,768]{2,1,0:T(8,128)(2,1)}, bf16[8,24,768]{2,1,0:T(8,128)(2,1)S(1)}, u32[]{:S(2)}) copy-start(bf16[8,24,768]{2,1,0:T(8,128)(2,1)S(1)} %all-to-all-done.1) | copy-start | bytes 884740
  91.4 8.2 %collective-permute-start.18 = (bf16[192,768]{1,0:T(8,128)(2,1)S(1)}, bf16[192,768]{1,0:T(8,128)(2,1)S(1)}, u32[]{:S(2)}, u32[]{:S(2)}) collective-permute-start(bf16[192,768]{1,0:T(8,128)(2,1)S(1)} %bitcast.24), channel_id=1, source_target_pairs={{0,16},{8,24},{16,0},{24,8},{1,17},{9,25},{17,1},{25,9},{2,18},{10... | collective-permute-start | bytes 884744 | tf_op jit(solution)/shard_map/ppermute | solution.py:52
  92.7 6.9 %collective-permute-start.14 = (bf16[192,768]{1,0:T(8,128)(2,1)}, bf16[192,768]{1,0:T(8,128)(2,1)S(1)}, u32[]{:S(2)}, u32[]{:S(2)}) collective-permute-start(bf16[192,768]{1,0:T(8,128)(2,1)} %bitcast.22), channel_id=1, source_target_pairs={{0,8},{8,0},{16,24},{24,16},{1,9},{9,1},{17,25},{25,17},{2,10},{10... | collective-permute-start | bytes 884744 | tf_op jit(solution)/shard_map/ppermute | solution.py:52
  92.7 7.0 %copy-start.12 = (bf16[192,768]{1,0:T(8,128)(2,1)}, bf16[192,768]{1,0:T(8,128)(2,1)S(1)}, u32[]{:S(2)}) copy-start(bf16[192,768]{1,0:T(8,128)(2,1)S(1)} %collective-permute-done.15.rest_2_) | copy-start | bytes 884740
  92.7 6.9 %collective-permute-start.16 = (bf16[192,768]{1,0:T(8,128)(2,1)S(1)}, bf16[192,768]{1,0:T(8,128)(2,1)S(1)}, u32[]{:S(2)}, u32[]{:S(2)}) collective-permute-start(bf16[192,768]{1,0:T(8,128)(2,1)S(1)} %collective-permute-done.15.rest_2_), channel_id=1, source_target_pairs={{0,8},{8,0},{16,24},{24,16},{1,9},{9,1},{17,25},{25,17},{2,10},{10... | collective-permute-start | bytes 884744 | tf_op jit(solution)/shard_map/ppermute | solution.py:52
  93.2 12.4 %collective-permute-start.17 = (bf16[192,768]{1,0:T(8,128)(2,1)S(1)}, bf16[192,768]{1,0:T(8,128)(2,1)S(1)}, u32[]{:S(2)}, u32[]{:S(2)}) collective-permute-start(bf16[192,768]{1,0:T(8,128)(2,1)S(1)} %bitcast.25), channel_id=1, source_target_pairs={{0,8},{8,0},{16,24},{24,16},{1,9},{9,1},{17,25},{25,17},{2,10},{10... | collective-permute-start | bytes 884744 | tf_op jit(solution)/shard_map/ppermute | solution.py:52
  99.6 6.0 %collective-permute-start.19 = (bf16[192,768]{1,0:T(8,128)(2,1)S(1)}, bf16[192,768]{1,0:T(8,128)(2,1)S(1)}, u32[]{:S(2)}, u32[]{:S(2)}) collective-permute-start(bf16[192,768]{1,0:T(8,128)(2,1)S(1)} %collective-permute-done.18.rest_2_), channel_id=1, source_target_pairs={{0,8},{8,0},{16,24},{24,16},{1,9},{9,1},{17,25},{25,17},{2,10},{10... | collective-permute-start | bytes 884744 | tf_op jit(solution)/shard_map/ppermute | solution.py:52
  116.3 1.9 collective-permute-start.21
  116.8 3.7 %collective-permute-start.20 = (bf16[192,768]{1,0:T(8,128)(2,1)}, bf16[192,768]{1,0:T(8,128)(2,1)S(1)}, u32[]{:S(2)}, u32[]{:S(2)}) collective-permute-start(bf16[192,768]{1,0:T(8,128)(2,1)} %get-tuple-element.102), channel_id=1, source_target_pairs={{0,8},{8,0},{16,24},{24,16},{1,9},{9,1},{17,25},{25,17},{2,10},{10... | collective-permute-start | bytes 884744 | tf_op jit(solution)/shard_map/ppermute | solution.py:52
  119.2 9.4 %collective-permute-start.22 = (bf16[192,768]{1,0:T(8,128)(2,1)S(1)}, bf16[192,768]{1,0:T(8,128)(2,1)S(1)}, u32[]{:S(2)}, u32[]{:S(2)}) collective-permute-start(bf16[192,768]{1,0:T(8,128)(2,1)S(1)} %add_convert_fusion.4), channel_id=1, source_target_pairs={{0,16},{8,24},{16,0},{24,8},{1,17},{9,25},{17,1},{25,9},{2,18},{10... | collective-permute-start | bytes 884744 | tf_op jit(solution)/shard_map/ppermute | solution.py:52
  140.3 4.6 %collective-permute-start.24 = (bf16[192,768]{1,0:T(8,128)(2,1)}, bf16[192,768]{1,0:T(8,128)(2,1)S(1)}, u32[]{:S(2)}, u32[]{:S(2)}) collective-permute-start(bf16[192,768]{1,0:T(8,128)(2,1)} %get-tuple-element.116), channel_id=1, source_target_pairs={{0,8},{8,0},{16,24},{24,16},{1,9},{9,1},{17,25},{25,17},{2,10},{10... | collective-permute-start | bytes 884744 | tf_op jit(solution)/shard_map/ppermute | solution.py:52
  140.4 17.8 %all-to-all-start.2 = ((bf16[8,24,768]{2,1,0:T(8,128)(2,1)}), bf16[8,24,768]{2,1,0:T(8,128)(2,1)S(1)}, u32[]{:S(2)}, u32[]{:S(2)}) async-start(bf16[8,24,768]{2,1,0:T(8,128)(2,1)} %bitcast.11), calls=%async_computation.2 | async-start | bytes 589824 | tf_op jit(solution)/shard_map/all_to_all | solution.py:60
  144.7 26.3 %collective-permute-start.23 = (bf16[192,768]{1,0:T(8,128)(2,1)}, bf16[192,768]{1,0:T(8,128)(2,1)S(1)}, u32[]{:S(2)}, u32[]{:S(2)}) collective-permute-start(bf16[192,768]{1,0:T(8,128)(2,1)} %get-tuple-element.114), channel_id=1, source_target_pairs={{0,8},{8,0},{16,24},{24,16},{1,9},{9,1},{17,25},{25,17},{2,10},{10... | collective-permute-start | bytes 884744 | tf_op jit(solution)/shard_map/ppermute | solution.py:52
  145.9 25.0 %collective-permute-start.25 = (bf16[192,768]{1,0:T(8,128)(2,1)S(1)}, bf16[192,768]{1,0:T(8,128)(2,1)S(1)}, u32[]{:S(2)}, u32[]{:S(2)}) collective-permute-start(bf16[192,768]{1,0:T(8,128)(2,1)S(1)} %add_convert_fusion.1), channel_id=1, source_target_pairs={{0,16},{8,24},{16,0},{24,8},{1,17},{9,25},{17,1},{25,9},{2,18},{10... | collective-permute-start | bytes 884744 | tf_op jit(solution)/shard_map/ppermute | solution.py:52
  158.9 12.0 %copy-start.18 = (bf16[192,768]{1,0:T(8,128)(2,1)S(1)}, bf16[192,768]{1,0:T(8,128)(2,1)}, u32[]{:S(2)}) copy-start(bf16[192,768]{1,0:T(8,128)(2,1)} %get-tuple-element.113) | copy-start | bytes 884740
  170.9 23.3 %copy-start.19 = (f32[32,768]{1,0:T(8,128)S(1)}, f32[32,768]{1,0:T(8,128)}, u32[]{:S(2)}) copy-start(f32[32,768]{1,0:T(8,128)} %get-tuple-element.121) | copy-start | bytes 294916
  190.6 30.8 %all-to-all-start.3 = ((bf16[8,384,128]{2,1,0:T(8,128)(2,1)}), bf16[8,384,128]{2,1,0:T(8,128)(2,1)S(1)}, u32[]{:S(2)}, u32[]{:S(2)}) async-start(bf16[8,384,128]{2,1,0:T(8,128)(2,1)} %get-tuple-element.117), calls=%async_computation.3 | async-start | bytes 1572864 | tf_op jit(solution)/shard_map/all_to_all | solution.py:60
  194.2 1.4 collective-permute-start.26
  195.6 4.9 %collective-permute-start.27 = (f32[32,768]{1,0:T(8,128)S(1)}, f32[32,768]{1,0:T(8,128)S(1)}, u32[]{:S(2)}, u32[]{:S(2)}) collective-permute-start(f32[32,768]{1,0:T(8,128)S(1)} %add.48), channel_id=1, source_target_pairs={{0,16},{8,24},{16,0},{24,8},{1,17},{9,25},{17,1},{25,9},{2,18},{10... | collective-permute-start | bytes 294920 | tf_op jit(solution)/shard_map/ppermute | solution.py:52
  200.5 5.7 %collective-permute-start.28 = (f32[32,768]{1,0:T(8,128)S(1)}, f32[32,768]{1,0:T(8,128)S(1)}, u32[]{:S(2)}, u32[]{:S(2)}) collective-permute-start(f32[32,768]{1,0:T(8,128)S(1)} %add.49), channel_id=1, source_target_pairs={{0,1},{1,0},{2,3},{3,2},{4,5},{5,4},{6,7},{7,6},{8,9},{9,8},{10,11... | collective-permute-start | bytes 294920 | tf_op jit(solution)/shard_map/ppermute | solution.py:52
  206.3 8.2 %collective-permute-start.29 = (f32[32,768]{1,0:T(8,128)S(1)}, f32[32,768]{1,0:T(8,128)S(1)}, u32[]{:S(2)}, u32[]{:S(2)}) collective-permute-start(f32[32,768]{1,0:T(8,128)S(1)} %add.50), channel_id=1, source_target_pairs={{0,2},{1,3},{2,0},{3,1},{4,6},{5,7},{6,4},{7,5},{8,10},{9,11},{10,... | collective-permute-start | bytes 294920 | tf_op jit(solution)/shard_map/ppermute | solution.py:52
  214.4 6.9 %collective-permute-start.30 = (f32[32,768]{1,0:T(8,128)S(1)}, f32[32,768]{1,0:T(8,128)S(1)}, u32[]{:S(2)}, u32[]{:S(2)}) collective-permute-start(f32[32,768]{1,0:T(8,128)S(1)} %add.51), channel_id=1, source_target_pairs={{0,4},{1,5},{2,6},{3,7},{4,0},{5,1},{6,2},{7,3},{8,12},{9,13},{10,... | collective-permute-start | bytes 294920 | tf_op jit(solution)/shard_map/ppermute | solution.py:52
  227.1 1.6 collective-permute-start.32
  227.8 4.2 %collective-permute-start.31 = (bf16[192,384]{1,0:T(8,128)(2,1)}, bf16[192,384]{1,0:T(8,128)(2,1)S(1)}, u32[]{:S(2)}, u32[]{:S(2)}) collective-permute-start(bf16[192,384]{1,0:T(8,128)(2,1)} %get-tuple-element.123), channel_id=1, source_target_pairs={{0,8},{8,0},{16,24},{24,16},{1,9},{9,1},{17,25},{25,17},{2,10},{10... | collective-permute-start | bytes 442376 | tf_op jit(solution)/shard_map/ppermute | solution.py:52
  229.7 6.0 %collective-permute-start.33 = (bf16[192,384]{1,0:T(8,128)(2,1)S(1)}, bf16[192,384]{1,0:T(8,128)(2,1)S(1)}, u32[]{:S(2)}, u32[]{:S(2)}) collective-permute-start(bf16[192,384]{1,0:T(8,128)(2,1)S(1)} %add_convert_fusion.6), channel_id=1, source_target_pairs={{0,16},{8,24},{16,0},{24,8},{1,17},{9,25},{17,1},{25,9},{2,18},{10... | collective-permute-start | bytes 442376 | tf_op jit(solution)/shard_map/ppermute | solution.py:52
  (11 other events, 15.9 us)
Sparse Core Ops, SparseCore 0:
  67.5 44.1 all-gather.4
  140.5 50.7 all-gather.6

commit v5 on v4

--- a/solution.py
+++ b/solution.py
@@ -60,26 +60,31 @@
     return lax.all_to_all(value, "expert", split_axis=0, concat_axis=0, tiled=True)
 
 
-def gather_list(value):
+def gather_far(value):
     found = {0: value}
     bit = lax.axis_size("dp") // 2
-    while bit >= 1:
+    while bit > 1:
         found.update({index ^ bit: swap(item, "dp", bit) for index, item in found.items()})
         bit = bit // 2
+    return found
+
+
+def gather_near(found):
+    found = {**found, **{index ^ 1: swap(item, "dp", 1) for index, item in found.items()}}
     return [found[index] for index in range(len(found))]
 
 
-def scatter_list(items, dtype=LOW):
+def add(left, right, dtype=LOW):
+    return (left.astype(FULL) + right.astype(FULL)).astype(dtype)
+
+
+def scatter_terms(items):
     bit = 1
-    while len(items) > 1:
+    while len(items) > 2:
         taken = [swap(item, "dp", bit) for item in items[1::2]]
-        kind = dtype if len(items) == 2 else LOW
-        items = [
-            (kept.astype(FULL) + got.astype(FULL)).astype(kind)
-            for kept, got in zip(items[0::2], taken)
-        ]
+        items = [add(kept, got) for kept, got in zip(items[0::2], taken)]
         bit = bit * 2
-    return items[0]
+    return items[0], swap(items[1], "dp", bit)
 
 
 def all_sum(value):
@@ -91,7 +96,11 @@
     return value
 
 
-def gather_pieces(payload, early):
+def together(*values):
+    return lax.optimization_barrier(values)
+
+
+def gather_pieces(payload, early, up_slabs):
     ranks, dps = lax.axis_size("expert"), lax.axis_size("dp")
     half = payload.shape[0] // 2
     far = list(range(0, ranks, 2))
@@ -100,14 +109,25 @@
         gather_bits(payload[index * half : (index + 1) * half][None], "expert", far[1:])
         for index in range(2)
     ]
-    values, early = lax.optimization_barrier((values, early))
+    values, early = together(values, early)
+    firsts = []
+    for value, letter in zip(values, "xy"):
+        axis, masks = sides[letter]
+        firsts.append(gather_bits(value[None], axis, masks[1:]))
+    firsts, up_slabs = together(firsts, up_slabs)
+    up_arrived = exchange(up_slabs)
+    seconds = []
+    for value, letter in zip(firsts, "yx"):
+        axis, masks = sides[letter]
+        seconds.append([swap(value, axis, mask) for mask in masks[1:]])
+    others = [swap(value, "dp", 1) for value in firsts]
+    seconds, others, up_arrived = together(seconds, others, up_arrived)
     pieces, places = [], []
     for index, order in enumerate(("xy", "yx")):
-        axis, masks = sides[order[0]]
-        value = gather_bits(values[index][None], axis, masks[1:])
-        other_axis, other_masks = sides[order[1]]
-        found = [(value, 0)] + [(swap(value, other_axis, m), m) for m in other_masks[1:]]
-        found = [(v, m, 0) for v, m in found] + [(swap(v, "dp", 1), m, 1) for v, m in found]
+        masks, other_masks = sides[order[0]][1], sides[order[1]][1]
+        found = [(firsts[index], 0, 0), (others[index], 0, 1)]
+        for value, mask in zip(seconds[index], other_masks[1:]):
+            found += [(value, mask, 0), (swap(value, "dp", 1), mask, 1)]
         for piece, mask, core in found:
             offsets = []
             for first in masks:
@@ -116,7 +136,7 @@
                     offsets.append((low ^ x_mask, y_mask ^ core))
             pieces.append(piece)
             places.append((index, offsets))
-    return pieces, places, early
+    return pieces, places, early, up_arrived
 
 
 def place_weights(places, piece_refs, w_ref, sem):
@@ -363,21 +383,23 @@
         back_refs[p][:, 128:] = rows[:, 128:].astype(LOW)
 
 
+def expert_out_kernel(pack_t_ref, w_out_ref, act_ref, *rest):
+    out_refs, returned_ref = rest[:-1], rest[-1]
+    chunk = act_ref.shape[1] // len(out_refs)
+    for e in range(w_out_ref.shape[0]):
+        returned_ref[e] = dot(act_ref[e], w_out_ref[e]).astype(LOW)
+    for p, ref in enumerate(out_refs):
+        ref[...] = unpack(pack_t_ref[...], returned_ref, p, chunk).astype(LOW)
+
+
 def expert_grad_kernel(
-    count, pack_t_ref, w_out_ref, rows_ref, act_ref, pre_grad_ref, gates_ref, up_rows_ref, *rest
+    rows_ref, act_ref, pre_grad_ref, gates_ref, up_rows_ref, g_in_ref, g_out_ref, token_ref
 ):
-    out_refs, (g_in_ref, g_out_ref, returned_ref) = rest[:count], rest[count:]
-    local_experts = w_out_ref.shape[0]
-    chunk = rows_ref.shape[1] // count
-    pack_t = pack_t_ref[...]
-    for e in range(local_experts):
-        returned_ref[e] = dot(act_ref[e], w_out_ref[e]).astype(LOW)
-    for p in range(count):
-        out_refs[p][...] = unpack(pack_t, returned_ref, p, chunk).astype(LOW)
-    for e in range(local_experts):
+    for e in range(rows_ref.shape[0]):
         g_in_ref[e] = dot(rows_ref[e], pre_grad_ref[e], TN)
         slot_grad = (up_rows_ref[e].astype(FULL) * gates_ref[e][:, :1]).astype(LOW)
         g_out_ref[e] = dot(act_ref[e], slot_grad, TN)
+    token_ref[...] = jnp.zeros(token_ref.shape, FULL)
 
 
 def joined(ref):
@@ -387,7 +409,7 @@
 
 def backward_kernel(
     places, rank_slots, tokens_ref, gain_ref, router_t_ref, hits_ref, mask_ref,
-    up_ref, hidden_ref, chance_ref, heads_ref, weights_ref, onehot_ref, *rest
+    up_ref, hidden_ref, chance_ref, heads_ref, weights_ref, onehot_ref, token_ref, *rest
 ):
     count = len(places)
     piece_refs, rest = rest[:count], rest[count:]
@@ -460,7 +482,9 @@
     small_ref[experts : experts + 1, :] = ffn_gain_grad
     small_ref[experts + 1 : experts + 2, :] = attn_gain_grad
     small_ref[experts + 2 :, :] = jnp.zeros((small_ref.shape[0] - experts - 2, width), FULL)
-    small_ref[experts + 2 : experts + 2 + head_count, : sums.shape[1]] = sums
+    for h in range(head_count):
+        line, place = experts + 2 + h // 6, 128 * (h % 6)
+        small_ref[line : line + 1, place : place + sums.shape[1]] = sums[h : h + 1]
 
 
 def product_kernel(
@@ -497,7 +521,7 @@
     return jax.ShapeDtypeStruct(shape, dtype)
 
 
-def call(kernel, name, out_shape, args, pieces=(), scratch=(), more=()):
+def call(kernel, name, micros, out_shape, args, pieces=(), scratch=(), more=()):
     return pl.pallas_call(
         kernel,
         out_shape=tuple(out_shape),
@@ -505,6 +529,9 @@
         out_specs=(VMEM,) * len(out_shape),
         scratch_shapes=list(scratch),
         compiler_params=pltpu.CompilerParams(vmem_limit_bytes=LIMIT),
+        cost_estimate=pl.CostEstimate(
+            flops=0, bytes_accessed=micros * 3_600_000, transcendentals=0
+        ),
         name=name,
     )(*args, *pieces, *more)
 
@@ -545,6 +572,7 @@
     normed_low, hits, mask, mask_t, bias_full, up_slabs = call(
         functools.partial(early_kernel, ranks, local_experts, capacity, slab),
         "early",
+        3,
         [
             shaped(LOW, length, model_width),
             shaped(FULL, length, experts_total),
@@ -564,17 +592,18 @@
     )
 
     payload = jnp.concatenate([w_query, w_key, w_value, w_output], axis=1)
-    pieces, places, (normed_low, hits, mask, mask_t, bias_full, up_slabs) = gather_pieces(
-        payload, (normed_low, hits, mask, mask_t, bias_full, up_slabs)
-    )
-    up_arrived = exchange(up_slabs).reshape(ranks * slab, model_width)
-    pieces, normed_later, up_arrived = lax.optimization_barrier((pieces, normed_low, up_arrived))
+    early = (normed_low, hits, mask, mask_t, bias_full)
+    pieces, places, early, up_arrived = gather_pieces(payload, early, up_slabs)
+    normed_low, hits, mask, mask_t, bias_full = early
+    pieces, normed_later = together(pieces, normed_low)
     normed_all = lax.all_gather(normed_later, "expert", axis=0)
+    up_far = gather_far(up_arrived.reshape(ranks * slab, model_width))
 
     w_shape = (ranks, inner_width, 4 * columns_here)
     heads, weights, attended, hidden, chance, slabs = call(
         functools.partial(forward_kernel, places, slab, rank_slots),
         "attention_forward",
+        10,
         [
             shaped(LOW, 3, inner_width, length),
             shaped(FULL, head_count, length, length),
@@ -593,20 +622,25 @@
         ],
     )
 
-    up_pieces = gather_list(up_arrived)
-    row_pieces = gather_list(exchange(slabs).reshape(ranks * slab, model_width))
+    slabs, up_far = together(slabs, up_far)
+    arrived = exchange(slabs).reshape(ranks * slab, model_width)
     attended_all = lax.all_gather(attended, "expert", axis=0)
+    up_pieces = gather_near(up_far)
     by_expert = (local_experts, packed_rows)
     up_rows, up_act = call(
         upstream_kernel,
         "upstream_rows",
+        5,
         [shaped(LOW, *by_expert, model_width), shaped(FULL, *by_expert, hidden_here)],
         [pack, w_out, *up_pieces],
     )
+    arrived, up_act = together(arrived, up_act)
+    row_pieces = gather_near(gather_far(arrived))
 
     *back, slot_rows, activated, pre_grad, gates = call(
         functools.partial(expert_kernel, dps, slab, rank_slots),
         "experts",
+        10,
         [shaped(LOW, ranks * slab, model_width)] * dps
         + [
             shaped(LOW, *by_expert, model_width),
@@ -621,23 +655,36 @@
             pltpu.VMEM((*by_expert, 128), LOW),
         ],
     )
-    back = scatter_list(back).reshape(ranks, slab, model_width)
-    back, activated = lax.optimization_barrier((back, activated))
+    kept, got = scatter_terms(back)
+    first_grad, second_grad, token = call(
+        expert_grad_kernel,
+        "expert_gradients",
+        8,
+        [shaped(FULL, *w_in.shape), shaped(FULL, *w_out.shape), shaped(FULL, 8, 128)],
+        [slot_rows, activated, pre_grad, gates, up_rows],
+    )
+    got, token = together(got, token)
+    back = add(kept, got).reshape(ranks, slab, model_width)
+    back, activated = together(back, activated)
     back = exchange(back)
-    *returned, first_grad, second_grad = call(
-        functools.partial(expert_grad_kernel, dps),
-        "expert_gradients",
-        [shaped(LOW, ranks * slab, model_width)] * dps
-        + [shaped(FULL, *w_in.shape), shaped(FULL, *w_out.shape)],
-        [pack_t, w_out, slot_rows, activated, pre_grad, gates, up_rows],
+    returned = call(
+        expert_out_kernel,
+        "expert_outputs",
+        3,
+        [shaped(LOW, ranks * slab, model_width)] * dps,
+        [pack_t, w_out, activated],
         scratch=[pltpu.VMEM((*by_expert, model_width), LOW)],
     )
-    returned = scatter_list(returned).reshape(ranks, slab, model_width)
-
-    small_rows = -(-(experts_total + 2 + head_count) // 8) * 8
+    returned = add(*scatter_terms(returned)).reshape(ranks, slab, model_width)
+    back, returned = together(back, returned)
+    returned = exchange(returned)
+
+    bias_rows = -(-head_count // 6)
+    small_rows = -(-(experts_total + 2 + bias_rows) // 8) * 8
     d_input, small, factors = call(
         functools.partial(backward_kernel, places, rank_slots),
         "attention_backward",
+        12,
         [
             shaped(FULL, length, model_width),
             shaped(FULL, small_rows, model_width),
@@ -655,6 +702,7 @@
             heads,
             weights,
             jnp.asarray(bucket_onehot(bucket_count, length), FULL),
+            token,
         ],
         pieces,
         [
@@ -667,24 +715,25 @@
         [back],
     )
 
-    factors, returned = lax.optimization_barrier((factors, returned))
+    factors, small, returned = together(factors, small, returned)
     factors = exchange(factors)
-    returned = exchange(returned)
-    small = all_sum(small)
+    factors, small = together(factors, all_sum(small))
     output, *grads = call(
         functools.partial(product_kernel, dps),
         "weight_gradients",
+        5,
         [shaped(LOW, length, model_width)] + [shaped(LOW, rows_here, 4 * columns_here)] * dps,
         [normed_all, attended_all, hidden, chance, hits, mask, factors, returned],
         scratch=[pltpu.VMEM((dps, rows_here, 4 * columns_here), FULL)],
     )
-    grads = scatter_list(grads, FULL)
+    grads = add(*scatter_terms(grads), FULL)
     g_query, g_key, g_value, g_output = (
         grads[:, i * columns_here : (i + 1) * columns_here] for i in range(4)
     )
     g_router = small[:experts_total].T
     g_ffn_gain, g_attn_gain = small[experts_total], small[experts_total + 1]
-    g_rel_bias = small[experts_total + 2 : experts_total + 2 + head_count, :bucket_count].T
+    g_rel_bias = small[experts_total + 2 : experts_total + 2 + bias_rows].reshape(-1, 128)
+    g_rel_bias = g_rel_bias[:head_count, :bucket_count].T
     return (
         output,
         d_input,

time: 245 us -> 229 us (0.935)
  blocking collectives: 35.1 us -> 16.7 us
  starting transfers between devices: 42.4 us -> 50.6 us
  waiting for transfers between devices: 80.6 us -> 72.4 us
    all_to_all x2 -> x1, blocking collectives: 35.1 us -> 16.7 us  [exchange(): lax.all_to_all(value, 'expert', split_axis=0, concat_axis=0, tiled=True)]
    ppermute x34, waiting for transfers between devices: 59.5 us -> 53.9 us  [swap(): return lax.ppermute(value, axis, [(i, i ^ mask) for i in range(count)])]
    all_to_all x3 -> x4, starting transfers between devices: 11.3 us -> 15.6 us  [exchange(): lax.all_to_all(value, 'expert', split_axis=0, concat_axis=0, tiled=True)]
    ppermute x34, starting transfers between devices: 30.8 us -> 34.8 us  [swap(): return lax.ppermute(value, axis, [(i, i ^ mask) for i in range(count)])]
    all_to_all x3 -> x4, waiting for transfers between devices: 21 us -> 18.4 us  [exchange(): lax.all_to_all(value, 'expert', split_axis=0, concat_axis=0, tiled=True)]
    pallas_call x7 -> x8, Pallas kernels: 54.4 us -> 56.8 us  [call(): pl.pallas_call(kernel, out_shape=tuple(out_shape), in_specs=[VMEM] * len(...]
    unnamed x40 -> x42, local copies, waits for them, and re-layouts: 5.54 us -> 3.38 us
  transfers between devices with their start and end apart: 39 -> 40, of which waited for: 18 -> 23; matrix products, arithmetic and copies ran while one was open for 4% -> 5% of each run, Pallas kernels for 20% -> 18%
where the time goes in v5:
time: 229 us; the launch traced here: 228 us
  waiting for transfers between devices  72.4 us (32%)
  Pallas kernels  56.8 us (25%)
  starting transfers between devices  50.6 us (22%)
  blocking collectives  16.7 us (7%)
  between operations  14.4 us (6%)
  other arithmetic  9.4 us (4%)
  local copies, waits for them, and re-layouts  7.45 us (3%)
    pallas_call x8, Pallas kernels, call(): pl.pallas_call(kernel, out_shape=tuple(out_shape), in_specs=[VMEM] * len(...  56.8 us
    ppermute x34, waiting for transfers between devices, swap(): return lax.ppermute(value, axis, [(i, i ^ mask) for i in range(count)])  53.9 us
    ppermute x34, starting transfers between devices, swap(): return lax.ppermute(value, axis, [(i, i ^ mask) for i in range(count)])  34.8 us
    all_to_all x4, waiting for transfers between devices, exchange(): lax.all_to_all(value, 'expert', split_axis=0, concat_axis=0, tiled=True)  18.4 us
    all_to_all x1, blocking collectives, exchange(): lax.all_to_all(value, 'expert', split_axis=0, concat_axis=0, tiled=True)  16.7 us
    all_to_all x4, starting transfers between devices, exchange(): lax.all_to_all(value, 'expert', split_axis=0, concat_axis=0, tiled=True)  15.6 us
    convert_element_type x5, other arithmetic, add(): return (left.astype(FULL) + right.astype(FULL)).astype(dtype)  5.66 us
  transfers between devices with their start and end apart: 40, of which 23 were waited for; matrix products, arithmetic and copies ran while one was open for 5% of the time, Pallas kernels for 18%

profile of v5, /device:TPU:0, one launch (start us, length us, event | category | flops | bytes accessed | tf_op | source)
XLA Modules:
  0.0 227.8 jit_solution(10108293187886674096)
XLA Ops:
  8.3 3.1 %collective-permute-start.3 = (bf16[1,96,384]{2,1,0:T(8,128)(2,1)S(1)}, bf16[1,96,384]{2,1,0:T(8,128)(2,1)S(1)}, u32[]{:S(2)}, u32[]{:S(2)}) collective-permute-start(bf16[1,96,384]{2,1,0:T(8,128)(2,1)S(1)} %get-tuple-element.172), channel_id=1, source_target_pairs={{0,2},{1,3},{2,0},{3,1},{4,6},{5,7},{6,4},{7,5},{8,10},{9,11},{10,... | collective-permute-start | bytes 221192 | tf_op jit(solution)/shard_map/ppermute | solution.py:52
  11.4 2.6 %collective-permute-start.4 = (bf16[1,96,384]{2,1,0:T(8,128)(2,1)S(1)}, bf16[1,96,384]{2,1,0:T(8,128)(2,1)S(1)}, u32[]{:S(2)}, u32[]{:S(2)}) collective-permute-start(bf16[1,96,384]{2,1,0:T(8,128)(2,1)S(1)} %get-tuple-element.172), channel_id=1, source_target_pairs={{0,4},{1,5},{2,6},{3,7},{4,0},{5,1},{6,2},{7,3},{8,12},{9,13},{10,... | collective-permute-start | bytes 221192 | tf_op jit(solution)/shard_map/ppermute | solution.py:52
  14.8 3.5 %collective-permute-start.1 = (bf16[1,96,384]{2,1,0:T(8,128)(2,1)S(1)}, bf16[1,96,384]{2,1,0:T(8,128)(2,1)S(1)}, u32[]{:S(2)}, u32[]{:S(2)}) collective-permute-start(bf16[1,96,384]{2,1,0:T(8,128)(2,1)S(1)} %get-tuple-element.173), channel_id=1, source_target_pairs={{0,4},{1,5},{2,6},{3,7},{4,0},{5,1},{6,2},{7,3},{8,12},{9,13},{10,... | collective-permute-start | bytes 221192 | tf_op jit(solution)/shard_map/ppermute | solution.py:52
  20.3 3.4 %early.1 = (bf16[128,768]{1,0:T(8,128)(2,1)}, f32[128,16]{1,0:T(8,128)}, bf16[128,192]{1,0:T(8,128)(2,1)}, bf16[192,128]{1,0:T(8,128)(2,1)}, f32[12,128,128]{2,1,0:T(8,128)}, /*index=5*/bf16[8,24,768]{2,1,0:T(8,128)(2,1)}) custom-call(bf16[128,768]{1,0:T(8,128)(2,1)} %tokens_ref.5, s32[1,128]{1,0:T(1,128)} %bitcast.34, ...), custom_call_target="tpu_custom_call" | custom-call | bytes 10800000 | tf_op jit(solution)/shard_map/early/pallas_call | solution.py:525
  23.9 6.0 %collective-permute-done.2 = bf16[1,96,384]{2,1,0:T(8,128)(2,1)S(1)} collective-permute-done((bf16[1,96,384]{2,1,0:T(8,128)(2,1)S(1)}, bf16[1,96,384]{2,1,0:T(8,128)(2,1)S(1)}, u32[]{:S(2)}, u32[]{:S(2)}) %collective-permute-start.2) | collective-permute-done | bytes 73760 | tf_op jit(solution)/shard_map/ppermute | solution.py:52
  29.9 1.6 collective-permute-start.7
  31.5 1.5 collective-permute-start.6
  33.0 3.7 %collective-permute-done.7 = bf16[1,4,96,384]{3,2,1,0:T(8,128)(2,1)S(1)} collective-permute-done((bf16[1,4,96,384]{3,2,1,0:T(8,128)(2,1)S(1)}, bf16[1,4,96,384]{3,2,1,0:T(8,128)(2,1)S(1)}, u32[]{:S(2)}, u32[]{:S(2)}) %collective-permute-start.7) | collective-permute-done | bytes 294944 | tf_op jit(solution)/shard_map/ppermute | solution.py:52
  36.8 1.4 collective-permute-done.6
  39.4 1.5 collective-permute-start.9
  40.9 16.7 %all_to_all.25 = bf16[8,24,768]{2,1,0:T(8,128)(2,1)S(1)} all-to-all(bf16[8,24,768]{2,1,0:T(8,128)(2,1)S(1)} %copy-done.19), channel_id=1, replica_groups=mesh['dp'=4,'expert'=8] {'expert'}, dimensions={0} | all-to-all | bytes 589824 | tf_op jit(solution)/shard_map/all_to_all | solution.py:60
  58.2 1.5 collective-permute-done.12.rest_3_
  61.4 9.9 %attention_forward.1 = (bf16[3,768,128]{2,1,0:T(8,128)(2,1)}, f32[12,128,128]{2,1,0:T(8,128)}, bf16[128,768]{1,0:T(8,128)(2,1)}, f32[128,768]{1,0:T(8,128)}, f32...) custom-call(bf16[128,768]{1,0:T(8,128)(2,1)} %tokens_ref.5, bf16[128,768]{1,0:T(8,128)(2,1)} %get-tuple-element.105.normed_ref, ...), custom_call_target="tpu_custom_call" | custom-call | bytes 36000000 | tf_op jit(solution)/shard_map/attention_forward/pallas_call | solution.py:525
  71.3 1.6 collective-permute-start.14
  72.9 7.5 %collective-permute-done.14.rest_2_ = bf16[192,768]{1,0:T(8,128)(2,1)S(1)} collective-permute-done((bf16[192,768]{1,0:T(8,128)(2,1)S(1)}, bf16[192,768]{1,0:T(8,128)(2,1)S(1)}, u32[]{:S(2)}, u32[]{:S(2)}) %collective-permute-start.14) | collective-permute-done | bytes 294944 | tf_op jit(solution)/shard_map/ppermute | solution.py:52
  80.4 3.4 %all-to-all-start.1 = ((bf16[8,24,768]{2,1,0:T(8,128)(2,1)}), bf16[8,24,768]{2,1,0:T(8,128)(2,1)S(1)}, u32[]{:S(2)}, u32[]{:S(2)}) async-start(bf16[8,24,768]{2,1,0:T(8,128)(2,1)} %get-tuple-element.125), calls=%async_computation.1 | async-start | bytes 589824 | tf_op jit(solution)/shard_map/all_to_all | solution.py:60
  87.2 4.5 %upstream_rows.1 = (bf16[2,320,768]{2,1,0:T(8,128)(2,1)}, f32[2,320,768]{2,1,0:T(8,128)}) custom-call(bf16[160,192]{1,0:T(8,128)(2,1)} %constant.8.clone.pack_ref, bf16[2,768,768]{2,1,0:T(8,128)(2,1)} %w_out_ref.3, bf16[192,768]{1,0:T(8,128)(2,1)} %bitcast.23, bf16[192,768]{1,0:T(8,128)(2,1)} %copy-done.17, bf16[192,768]{1,0:T(8,128)(2,1)} %copy-done.14, ...), custom_call_target="tpu_custom_call" | custom-call | bytes 18000000 | tf_op jit(solution)/shard_map/upstream_rows/pallas_call | solution.py:525
  91.7 4.2 %all-to-all-done.1 = bf16[8,24,768]{2,1,0:T(8,128)(2,1)S(1)} async-done(((bf16[8,24,768]{2,1,0:T(8,128)(2,1)}), bf16[8,24,768]{2,1,0:T(8,128)(2,1)S(1)}, u32[]{:S(2)}, u32[]{:S(2)}) %all-to-all-start.1) | async-done | bytes 294944 | tf_op jit(solution)/shard_map/all_to_all | solution.py:60
  95.9 1.5 collective-permute-start.18
  97.3 6.6 %collective-permute-done.18.rest_2_ = bf16[192,768]{1,0:T(8,128)(2,1)S(1)} collective-permute-done((bf16[192,768]{1,0:T(8,128)(2,1)S(1)}, bf16[192,768]{1,0:T(8,128)(2,1)S(1)}, u32[]{:S(2)}, u32[]{:S(2)}) %collective-permute-start.18) | collective-permute-done | bytes 294944 | tf_op jit(solution)/shard_map/ppermute | solution.py:52
  104.0 1.6 collective-permute-done.19.rest_3_
  106.3 10.0 %experts.1 = (bf16[192,768]{1,0:T(8,128)(2,1)}, bf16[192,768]{1,0:T(8,128)(2,1)}, bf16[192,768]{1,0:T(8,128)(2,1)}, bf16[192,768]{1,0:T(8,128)(2,1)}, bf16[2,320...) custom-call(bf16[160,192]{1,0:T(8,128)(2,1)} %constant.8.clone.pack_re, ...), custom_call_target="tpu_custom_call" | custom-call | bytes 36000000 | tf_op jit(solution)/shard_map/experts/pallas_call | solution.py:525
  116.4 1.6 collective-permute-done.20
  118.0 1.1 add_convert_fusion.5
  119.1 1.5 collective-permute-start.21
  120.6 8.2 %expert_gradients.1 = (f32[2,768,768]{2,1,0:T(8,128)}, f32[2,768,768]{2,1,0:T(8,128)}, f32[8,128]{1,0:T(8,128)}) custom-call(bf16[2,320,768]{2,1,0:T(8,128)(2,1)} %get-tuple-element.133.rows_ref, bf16[2,320,768]{2,1,0:T(8,128)(2,1)} %get-tuple-element.144.act_ref, bf16[2,320,768]{2,1,0:T(8,128)(2,1)} %get-tuple-element.135.pre_grad_ref, ...), custom_call_target="tpu_custom_call" | custom-call | bytes 28800000 | tf_op jit(solution)/shard_map/expert_gradients/pallas_call | solution.py:525
  129.7 4.0 %expert_outputs.1 = (bf16[192,768]{1,0:T(8,128)(2,1)}, bf16[192,768]{1,0:T(8,128)(2,1)}, bf16[192,768]{1,0:T(8,128)(2,1)}, bf16[192,768]{1,0:T(8,128)(2,1)}) custom-call(bf16[192,160]{1,0:T(8,128)(2,1)} %constant.9.clone.pack_t_ref, bf16[2,768,768]{2,1,0:T(8,128)(2,1)} %w_out_ref.3, bf16[2,320,768]{2,1,0:T(8,128)(2,1)} %get-tuple-element.144.act_ref), custom_call_target="tpu_custom_call" | custom-call | bytes 10800000 | tf_op jit(solution)/shard_map/expert_outputs/pallas_call | solution.py:525
  134.3 1.3 collective-permute-done.24
  137.5 4.4 %all-to-all-start.2 = ((bf16[8,24,768]{2,1,0:T(8,128)(2,1)}), bf16[8,24,768]{2,1,0:T(8,128)(2,1)S(1)}, u32[]{:S(2)}, u32[]{:S(2)}) async-start(bf16[8,24,768]{2,1,0:T(8,128)(2,1)} %bitcast.11), calls=%async_computation.2 | async-start | bytes 589824 | tf_op jit(solution)/shard_map/all_to_all | solution.py:60
  141.9 4.2 %collective-permute-done.25 = bf16[192,768]{1,0:T(8,128)(2,1)S(1)} collective-permute-done((bf16[192,768]{1,0:T(8,128)(2,1)S(1)}, bf16[192,768]{1,0:T(8,128)(2,1)S(1)}, u32[]{:S(2)}, u32[]{:S(2)}) %collective-permute-start.25) | collective-permute-done | bytes 294944 | tf_op jit(solution)/shard_map/ppermute | solution.py:52
  146.0 1.8 add_convert_fusion
  147.8 9.7 %all-to-all-done.2.rest_8_ = bf16[8,24,768]{2,1,0:T(8,128)(2,1)S(1)} async-done(((bf16[8,24,768]{2,1,0:T(8,128)(2,1)}), bf16[8,24,768]{2,1,0:T(8,128)(2,1)S(1)}, u32[]{:S(2)}, u32[]{:S(2)}) %all-to-all-start.2) | async-done | bytes 294944 | tf_op jit(solution)/shard_map/all_to_all | solution.py:60
  157.5 3.6 %all-to-all-start.3 = ((bf16[8,24,768]{2,1,0:T(8,128)(2,1)}), bf16[8,24,768]{2,1,0:T(8,128)(2,1)S(1)}, u32[]{:S(2)}, u32[]{:S(2)}) async-start(bf16[8,24,768]{2,1,0:T(8,128)(2,1)} %bitcast.12), calls=%async_computation.3 | async-start | bytes 589824 | tf_op jit(solution)/shard_map/all_to_all | solution.py:60
  161.2 12.1 %attention_backward.1 = (f32[128,768]{1,0:T(8,128)}, f32[24,768]{1,0:T(8,128)}, bf16[8,384,128]{2,1,0:T(8,128)(2,1)}) custom-call(bf16[128,768]{1,0:T(8,128)(2,1)} %tokens_ref.5, f32[2,768]{1,0:T(2,128)} %maximum_convert_fusion.gain_ref, bf16[16,768]{1,0:T(8,128)(2,1)} %bitcast.32, f32[128,16]{1,0:T(8,128)} %get-tuple-element.107.hits_ref, ...), custom_call_target="tpu_custom_call" | custom-call | bytes 43200000 | tf_op jit(solution)/shard_map/attention_backward/pallas_call | solution.py:525
  173.3 4.4 %all-to-all-done.3.returned_ref = bf16[8,24,768]{2,1,0:T(8,128)(2,1)S(1)} async-done(((bf16[8,24,768]{2,1,0:T(8,128)(2,1)}), bf16[8,24,768]{2,1,0:T(8,128)(2,1)S(1)}, u32[]{:S(2)}, u32[]{:S(2)}) %all-to-all-start.3) | async-done | bytes 294944 | tf_op jit(solution)/shard_map/all_to_all | solution.py:60
  177.7 4.1 %all-to-all-start.4 = ((bf16[8,384,128]{2,1,0:T(8,128)(2,1)}), bf16[8,384,128]{2,1,0:T(8,128)(2,1)S(1)}, u32[]{:S(2)}, u32[]{:S(2)}) async-start(bf16[8,384,128]{2,1,0:T(8,128)(2,1)} %get-tuple-element.153), calls=%async_computation.4 | async-start | bytes 1572864 | tf_op jit(solution)/shard_map/all_to_all | solution.py:60
  181.9 1.5 collective-permute-done.26
  184.2 1.6 collective-permute-start.27
  185.8 2.8 %collective-permute-done.27 = f32[24,768]{1,0:T(8,128)S(1)} collective-permute-done((f32[24,768]{1,0:T(8,128)S(1)}, f32[24,768]{1,0:T(8,128)S(1)}, u32[]{:S(2)}, u32[]{:S(2)}) %collective-permute-start.27) | collective-permute-done | bytes 73760 | tf_op jit(solution)/shard_map/ppermute | solution.py:52
  188.7 2.1 collective-permute-start.28
  190.7 3.1 %collective-permute-done.28 = f32[24,768]{1,0:T(8,128)S(1)} collective-permute-done((f32[24,768]{1,0:T(8,128)S(1)}, f32[24,768]{1,0:T(8,128)S(1)}, u32[]{:S(2)}, u32[]{:S(2)}) %collective-permute-start.28) | collective-permute-done | bytes 73760 | tf_op jit(solution)/shard_map/ppermute | solution.py:52
  193.8 1.7 collective-permute-start.29
  195.5 2.8 %collective-permute-done.29 = f32[24,768]{1,0:T(8,128)S(1)} collective-permute-done((f32[24,768]{1,0:T(8,128)S(1)}, f32[24,768]{1,0:T(8,128)S(1)}, u32[]{:S(2)}, u32[]{:S(2)}) %collective-permute-start.29) | collective-permute-done | bytes 73760 | tf_op jit(solution)/shard_map/ppermute | solution.py:52
  198.2 4.3 %collective-permute-start.30 = (f32[24,768]{1,0:T(8,128)S(1)}, f32[24,768]{1,0:T(8,128)S(1)}, u32[]{:S(2)}, u32[]{:S(2)}) collective-permute-start(f32[24,768]{1,0:T(8,128)S(1)} %add.51), channel_id=1, source_target_pairs={{0,4},{1,5},{2,6},{3,7},{4,0},{5,1},{6,2},{7,3},{8,12},{9,13},{10,... | collective-permute-start | bytes 221192 | tf_op jit(solution)/shard_map/ppermute | solution.py:52
  202.5 2.5 %collective-permute-done.30 = f32[24,768]{1,0:T(8,128)S(1)} collective-permute-done((f32[24,768]{1,0:T(8,128)S(1)}, f32[24,768]{1,0:T(8,128)S(1)}, u32[]{:S(2)}, u32[]{:S(2)}) %collective-permute-start.30) | collective-permute-done | bytes 73760 | tf_op jit(solution)/shard_map/ppermute | solution.py:52
  205.8 4.8 %weight_gradients.1 = (bf16[128,768]{1,0:T(8,128)(2,1)}, bf16[192,384]{1,0:T(8,128)(2,1)}, bf16[192,384]{1,0:T(8,128)(2,1)}, bf16[192,384]{1,0:T(8,128)(2,1)}, bf16[192,384]{1,0:T(8,128)(2,1)}) custom-call(bf16[8,128,768]{2,1,0:T(8,128)(2,1)} %bitcast.20, bf16[8,128,768]{2,1,0:T(8,128)(2,1)} %bitcast.19, f32[128,768]{1,0:T(8,128)} %get-tuple-element.118.hidden_ref, ...), custom_call_target="tpu_custom_call" | custom-call | bytes 18000000 | tf_op jit(solution)/shard_map/weight_gradients/pallas_call | solution.py:525
  213.2 1.7 collective-permute-start.33
  216.1 3.1 %collective-permute-done.33 = bf16[192,384]{1,0:T(8,128)(2,1)S(1)} collective-permute-done((bf16[192,384]{1,0:T(8,128)(2,1)S(1)}, bf16[192,384]{1,0:T(8,128)(2,1)S(1)}, u32[]{:S(2)}, u32[]{:S(2)}) %collective-permute-start.33) | collective-permute-done | bytes 147488 | tf_op jit(solution)/shard_map/ppermute | solution.py:52
  (111 shorter events, 22.4 us)
Async XLA Ops:
  7.2 197.8 %all-gather.7.cloned.1.call-start = ((), (), s32[]{:S(2)}) async-start(), calls=%async_computation.6 | async-start | bytes 1769472 | tf_op jit(solution)/shard_map/all_gather | solution.py:627
  8.3 15.4 %collective-permute-start.3 = (bf16[1,96,384]{2,1,0:T(8,128)(2,1)S(1)}, bf16[1,96,384]{2,1,0:T(8,128)(2,1)S(1)}, u32[]{:S(2)}, u32[]{:S(2)}) collective-permute-start(bf16[1,96,384]{2,1,0:T(8,128)(2,1)S(1)} %get-tuple-element.172), channel_id=1, source_target_pairs={{0,2},{1,3},{2,0},{3,1},{4,6},{5,7},{6,4},{7,5},{8,10},{9,11},{10,... | collective-permute-start | bytes 221192 | tf_op jit(solution)/shard_map/ppermute | solution.py:52
  11.4 12.4 %collective-permute-start.4 = (bf16[1,96,384]{2,1,0:T(8,128)(2,1)S(1)}, bf16[1,96,384]{2,1,0:T(8,128)(2,1)S(1)}, u32[]{:S(2)}, u32[]{:S(2)}) collective-permute-start(bf16[1,96,384]{2,1,0:T(8,128)(2,1)S(1)} %get-tuple-element.172), channel_id=1, source_target_pairs={{0,4},{1,5},{2,6},{3,7},{4,0},{5,1},{6,2},{7,3},{8,12},{9,13},{10,... | collective-permute-start | bytes 221192 | tf_op jit(solution)/shard_map/ppermute | solution.py:52
  13.9 9.8 %collective-permute-start.5 = (bf16[1,96,384]{2,1,0:T(8,128)(2,1)S(1)}, bf16[1,96,384]{2,1,0:T(8,128)(2,1)S(1)}, u32[]{:S(2)}, u32[]{:S(2)}) collective-permute-start(bf16[1,96,384]{2,1,0:T(8,128)(2,1)S(1)} %get-tuple-element.172), channel_id=1, source_target_pairs={{0,6},{1,7},{2,4},{3,5},{4,2},{5,3},{6,0},{7,1},{8,14},{9,15},{10,... | collective-permute-start | bytes 221192 | tf_op jit(solution)/shard_map/ppermute | solution.py:52
  13.9 9.9 %collective-permute-start = (bf16[1,96,384]{2,1,0:T(8,128)(2,1)S(1)}, bf16[1,96,384]{2,1,0:T(8,128)(2,1)S(1)}, u32[]{:S(2)}, u32[]{:S(2)}) collective-permute-start(bf16[1,96,384]{2,1,0:T(8,128)(2,1)S(1)} %get-tuple-element.173), channel_id=1, source_target_pairs={{0,2},{1,3},{2,0},{3,1},{4,6},{5,7},{6,4},{7,5},{8,10},{9,11},{10,... | collective-permute-start | bytes 221192 | tf_op jit(solution)/shard_map/ppermute | solution.py:52
  14.8 9.0 %collective-permute-start.1 = (bf16[1,96,384]{2,1,0:T(8,128)(2,1)S(1)}, bf16[1,96,384]{2,1,0:T(8,128)(2,1)S(1)}, u32[]{:S(2)}, u32[]{:S(2)}) collective-permute-start(bf16[1,96,384]{2,1,0:T(8,128)(2,1)S(1)} %get-tuple-element.173), channel_id=1, source_target_pairs={{0,4},{1,5},{2,6},{3,7},{4,0},{5,1},{6,2},{7,3},{8,12},{9,13},{10,... | collective-permute-start | bytes 221192 | tf_op jit(solution)/shard_map/ppermute | solution.py:52
  23.7 17.2 %copy-start.19 = (bf16[8,24,768]{2,1,0:T(8,128)(2,1)S(1)}, bf16[8,24,768]{2,1,0:T(8,128)(2,1)}, u32[]{:S(2)}) copy-start(bf16[8,24,768]{2,1,0:T(8,128)(2,1)} %get-tuple-element.99) | copy-start | bytes 884740
  23.7 6.2 %collective-permute-start.2 = (bf16[1,96,384]{2,1,0:T(8,128)(2,1)S(1)}, bf16[1,96,384]{2,1,0:T(8,128)(2,1)S(1)}, u32[]{:S(2)}, u32[]{:S(2)}) collective-permute-start(bf16[1,96,384]{2,1,0:T(8,128)(2,1)S(1)} %get-tuple-element.173), channel_id=1, source_target_pairs={{0,6},{1,7},{2,4},{3,5},{4,2},{5,3},{6,0},{7,1},{8,14},{9,15},{10,... | collective-permute-start | bytes 221192 | tf_op jit(solution)/shard_map/ppermute | solution.py:52
  29.9 6.8 %collective-permute-start.7 = (bf16[1,4,96,384]{3,2,1,0:T(8,128)(2,1)S(1)}, bf16[1,4,96,384]{3,2,1,0:T(8,128)(2,1)S(1)}, u32[]{:S(2)}, u32[]{:S(2)}) collective-permute-start(bf16[1,4,96,384]{3,2,1,0:T(8,128)(2,1)S(1)} %bitcast.27), channel_id=1, source_target_pairs={{0,16},{8,24},{16,0},{24,8},{1,17},{9,25},{17,1},{25,9},{2,18},{10... | collective-permute-start | bytes 884744 | tf_op jit(solution)/shard_map/ppermute | solution.py:52
  31.5 6.7 %collective-permute-start.6 = (bf16[1,4,96,384]{3,2,1,0:T(8,128)(2,1)S(1)}, bf16[1,4,96,384]{3,2,1,0:T(8,128)(2,1)S(1)}, u32[]{:S(2)}, u32[]{:S(2)}) collective-permute-start(bf16[1,4,96,384]{3,2,1,0:T(8,128)(2,1)S(1)} %bitcast.29), channel_id=1, source_target_pairs={{0,1},{1,0},{2,3},{3,2},{4,5},{5,4},{6,7},{7,6},{8,9},{9,8},{10,11... | collective-permute-start | bytes 884744 | tf_op jit(solution)/shard_map/ppermute | solution.py:52
  36.8 24.6 %copy-start = (bf16[2,4,96,384]{3,2,1,0:T(8,128)(2,1)}, bf16[2,4,96,384]{3,2,1,0:T(8,128)(2,1)S(1)}, u32[]{:S(2)}) copy-start(bf16[2,4,96,384]{3,2,1,0:T(8,128)(2,1)S(1)} %pad_maximum_fusion.1.rest_4_) | copy-start | bytes 1769476
  38.3 23.1 %copy-start.1 = (bf16[2,4,96,384]{3,2,1,0:T(8,128)(2,1)}, bf16[2,4,96,384]{3,2,1,0:T(8,128)(2,1)S(1)}, u32[]{:S(2)}) copy-start(bf16[2,4,96,384]{3,2,1,0:T(8,128)(2,1)S(1)} %pad_maximum_fusion.rest_0_) | copy-start | bytes 1769476
  38.3 19.3 %collective-permute-start.10 = (bf16[2,4,96,384]{3,2,1,0:T(8,128)(2,1)S(1)}, bf16[2,4,96,384]{3,2,1,0:T(8,128)(2,1)S(1)}, u32[]{:S(2)}, u32[]{:S(2)}) collective-permute-start(bf16[2,4,96,384]{3,2,1,0:T(8,128)(2,1)S(1)} %pad_maximum_fusion.rest_0_), channel_id=1, source_target_pairs={{0,8},{8,0},{16,24},{24,16},{1,9},{9,1},{17,25},{25,17},{2,10},{10... | collective-permute-start | bytes 1769480 | tf_op jit(solution)/shard_map/ppermute | solution.py:52
  38.4 19.2 %collective-permute-start.11 = (bf16[2,4,96,384]{3,2,1,0:T(8,128)(2,1)S(1)}, bf16[2,4,96,384]{3,2,1,0:T(8,128)(2,1)S(1)}, u32[]{:S(2)}, u32[]{:S(2)}) collective-permute-start(bf16[2,4,96,384]{3,2,1,0:T(8,128)(2,1)S(1)} %pad_maximum_fusion.1.rest_4_), channel_id=1, source_target_pairs={{0,8},{8,0},{16,24},{24,16},{1,9},{9,1},{17,25},{25,17},{2,10},{10... | collective-permute-start | bytes 1769480 | tf_op jit(solution)/shard_map/ppermute | solution.py:52
  38.9 18.7 %collective-permute-start.8 = (bf16[2,4,96,384]{3,2,1,0:T(8,128)(2,1)S(1)}, bf16[2,4,96,384]{3,2,1,0:T(8,128)(2,1)S(1)}, u32[]{:S(2)}, u32[]{:S(2)}) collective-permute-start(bf16[2,4,96,384]{3,2,1,0:T(8,128)(2,1)S(1)} %pad_maximum_fusion.rest_0_), channel_id=1, source_target_pairs={{0,16},{8,24},{16,0},{24,8},{1,17},{9,25},{17,1},{25,9},{2,18},{10... | collective-permute-start | bytes 1769480 | tf_op jit(solution)/shard_map/ppermute | solution.py:52
  39.4 18.2 %collective-permute-start.9 = (bf16[2,4,96,384]{3,2,1,0:T(8,128)(2,1)S(1)}, bf16[2,4,96,384]{3,2,1,0:T(8,128)(2,1)S(1)}, u32[]{:S(2)}, u32[]{:S(2)}) collective-permute-start(bf16[2,4,96,384]{3,2,1,0:T(8,128)(2,1)S(1)} %pad_maximum_fusion.1.rest_4_), channel_id=1, source_target_pairs={{0,1},{1,0},{2,3},{3,2},{4,5},{5,4},{6,7},{7,6},{8,9},{9,8},{10,11... | collective-permute-start | bytes 1769480 | tf_op jit(solution)/shard_map/ppermute | solution.py:52
  57.6 28.6 %copy-start.10 = (bf16[8,24,768]{2,1,0:T(8,128)(2,1)}, bf16[8,24,768]{2,1,0:T(8,128)(2,1)S(1)}, u32[]{:S(2)}) copy-start(bf16[8,24,768]{2,1,0:T(8,128)(2,1)S(1)} %all_to_all.25) | copy-start | bytes 884740
  57.7 2.1 collective-permute-start.12
  57.7 2.8 %collective-permute-start.13 = (bf16[2,4,96,384]{3,2,1,0:T(8,128)(2,1)S(1)}, bf16[2,4,96,384]{3,2,1,0:T(8,128)(2,1)S(1)}, u32[]{:S(2)}, u32[]{:S(2)}) collective-permute-start(bf16[2,4,96,384]{3,2,1,0:T(8,128)(2,1)S(1)} %collective-permute-done.9.rest_6_), channel_id=1, source_target_pairs={{0,8},{8,0},{16,24},{24,16},{1,9},{9,1},{17,25},{25,17},{2,10},{10... | collective-permute-start | bytes 1769480 | tf_op jit(solution)/shard_map/ppermute | solution.py:52
  71.3 9.1 %collective-permute-start.14 = (bf16[192,768]{1,0:T(8,128)(2,1)S(1)}, bf16[192,768]{1,0:T(8,128)(2,1)S(1)}, u32[]{:S(2)}, u32[]{:S(2)}) collective-permute-start(bf16[192,768]{1,0:T(8,128)(2,1)S(1)} %bitcast.21), channel_id=1, source_target_pairs={{0,16},{8,24},{16,0},{24,8},{1,17},{9,25},{17,1},{25,9},{2,18},{10... | collective-permute-start | bytes 884744 | tf_op jit(solution)/shard_map/ppermute | solution.py:52
  80.4 5.7 %copy-start.14 = (bf16[192,768]{1,0:T(8,128)(2,1)}, bf16[192,768]{1,0:T(8,128)(2,1)S(1)}, u32[]{:S(2)}) copy-start(bf16[192,768]{1,0:T(8,128)(2,1)S(1)} %collective-permute-done.14.rest_2_) | copy-start | bytes 884740
  80.4 15.4 %all-to-all-start.1 = ((bf16[8,24,768]{2,1,0:T(8,128)(2,1)}), bf16[8,24,768]{2,1,0:T(8,128)(2,1)S(1)}, u32[]{:S(2)}, u32[]{:S(2)}) async-start(bf16[8,24,768]{2,1,0:T(8,128)(2,1)} %get-tuple-element.125), calls=%async_computation.1 | async-start | bytes 589824 | tf_op jit(solution)/shard_map/all_to_all | solution.py:60
  83.9 121.1 %all-gather.5.cloned.1.call-start = ((), (), s32[]{:S(2)}) async-start(), calls=%async_computation.5 | async-start | bytes 1769472 | tf_op jit(solution)/shard_map/all_gather | solution.py:599
  84.1 1.6 collective-permute-start.15
  84.2 2.0 collective-permute-start.16
  95.9 9.7 %copy-start.11 = (bf16[8,24,768]{2,1,0:T(8,128)(2,1)}, bf16[8,24,768]{2,1,0:T(8,128)(2,1)S(1)}, u32[]{:S(2)}) copy-start(bf16[8,24,768]{2,1,0:T(8,128)(2,1)S(1)} %all-to-all-done.1) | copy-start | bytes 884740
  95.9 8.1 %collective-permute-start.18 = (bf16[192,768]{1,0:T(8,128)(2,1)S(1)}, bf16[192,768]{1,0:T(8,128)(2,1)S(1)}, u32[]{:S(2)}, u32[]{:S(2)}) collective-permute-start(bf16[192,768]{1,0:T(8,128)(2,1)S(1)} %bitcast.24), channel_id=1, source_target_pairs={{0,16},{8,24},{16,0},{24,8},{1,17},{9,25},{17,1},{25,9},{2,18},{10... | collective-permute-start | bytes 884744 | tf_op jit(solution)/shard_map/ppermute | solution.py:52
  97.3 6.6 %collective-permute-start.17 = (bf16[192,768]{1,0:T(8,128)(2,1)S(1)}, bf16[192,768]{1,0:T(8,128)(2,1)S(1)}, u32[]{:S(2)}, u32[]{:S(2)}) collective-permute-start(bf16[192,768]{1,0:T(8,128)(2,1)S(1)} %bitcast.25), channel_id=1, source_target_pairs={{0,8},{8,0},{16,24},{24,16},{1,9},{9,1},{17,25},{25,17},{2,10},{10... | collective-permute-start | bytes 884744 | tf_op jit(solution)/shard_map/ppermute | solution.py:52
  104.0 1.6 collective-permute-start.19
  116.2 1.8 collective-permute-start.20
  118.0 10.8 %copy-start.20 = (bf16[192,768]{1,0:T(8,128)(2,1)S(1)}, bf16[192,768]{1,0:T(8,128)(2,1)}, u32[]{:S(2)}) copy-start(bf16[192,768]{1,0:T(8,128)(2,1)} %get-tuple-element.140) | copy-start | bytes 884740
  119.1 9.7 %collective-permute-start.21 = (bf16[192,768]{1,0:T(8,128)(2,1)S(1)}, bf16[192,768]{1,0:T(8,128)(2,1)S(1)}, u32[]{:S(2)}, u32[]{:S(2)}) collective-permute-start(bf16[192,768]{1,0:T(8,128)(2,1)S(1)} %add_convert_fusion.5), channel_id=1, source_target_pairs={{0,16},{8,24},{16,0},{24,8},{1,17},{9,25},{17,1},{25,9},{2,18},{10... | collective-permute-start | bytes 884744 | tf_op jit(solution)/shard_map/ppermute | solution.py:52
  120.6 8.2 %collective-permute-start.22 = (bf16[192,768]{1,0:T(8,128)(2,1)}, bf16[192,768]{1,0:T(8,128)(2,1)S(1)}, u32[]{:S(2)}, u32[]{:S(2)}) collective-permute-start(bf16[192,768]{1,0:T(8,128)(2,1)} %get-tuple-element.141), channel_id=1, source_target_pairs={{0,8},{8,0},{16,24},{24,16},{1,9},{9,1},{17,25},{25,17},{2,10},{10... | collective-permute-start | bytes 884744 | tf_op jit(solution)/shard_map/ppermute | solution.py:52
  133.7 1.9 collective-permute-start.24
  134.2 7.6 %collective-permute-start.23 = (bf16[192,768]{1,0:T(8,128)(2,1)}, bf16[192,768]{1,0:T(8,128)(2,1)S(1)}, u32[]{:S(2)}, u32[]{:S(2)}) collective-permute-start(bf16[192,768]{1,0:T(8,128)(2,1)} %get-tuple-element.146), channel_id=1, source_target_pairs={{0,8},{8,0},{16,24},{24,16},{1,9},{9,1},{17,25},{25,17},{2,10},{10... | collective-permute-start | bytes 884744 | tf_op jit(solution)/shard_map/ppermute | solution.py:52
  136.7 9.4 %collective-permute-start.25 = (bf16[192,768]{1,0:T(8,128)(2,1)S(1)}, bf16[192,768]{1,0:T(8,128)(2,1)S(1)}, u32[]{:S(2)}, u32[]{:S(2)}) collective-permute-start(bf16[192,768]{1,0:T(8,128)(2,1)S(1)} %add_convert_fusion.1), channel_id=1, source_target_pairs={{0,16},{8,24},{16,0},{24,8},{1,17},{9,25},{17,1},{25,9},{2,18},{10... | collective-permute-start | bytes 884744 | tf_op jit(solution)/shard_map/ppermute | solution.py:52
  137.5 20.1 %all-to-all-start.2 = ((bf16[8,24,768]{2,1,0:T(8,128)(2,1)}), bf16[8,24,768]{2,1,0:T(8,128)(2,1)S(1)}, u32[]{:S(2)}, u32[]{:S(2)}) async-start(bf16[8,24,768]{2,1,0:T(8,128)(2,1)} %bitcast.11), calls=%async_computation.2 | async-start | bytes 589824 | tf_op jit(solution)/shard_map/all_to_all | solution.py:60
  157.5 20.2 %all-to-all-start.3 = ((bf16[8,24,768]{2,1,0:T(8,128)(2,1)}), bf16[8,24,768]{2,1,0:T(8,128)(2,1)S(1)}, u32[]{:S(2)}, u32[]{:S(2)}) async-start(bf16[8,24,768]{2,1,0:T(8,128)(2,1)} %bitcast.12), calls=%async_computation.3 | async-start | bytes 589824 | tf_op jit(solution)/shard_map/all_to_all | solution.py:60
  177.7 27.3 %copy-start.9 = (bf16[8,24,768]{2,1,0:T(8,128)(2,1)}, bf16[8,24,768]{2,1,0:T(8,128)(2,1)S(1)}, u32[]{:S(2)}) copy-start(bf16[8,24,768]{2,1,0:T(8,128)(2,1)S(1)} %all-to-all-done.3.returned_ref) | copy-start | bytes 884740
  177.7 27.2 %all-to-all-start.4 = ((bf16[8,384,128]{2,1,0:T(8,128)(2,1)}), bf16[8,384,128]{2,1,0:T(8,128)(2,1)S(1)}, u32[]{:S(2)}, u32[]{:S(2)}) async-start(bf16[8,384,128]{2,1,0:T(8,128)(2,1)} %get-tuple-element.153), calls=%async_computation.4 | async-start | bytes 1572864 | tf_op jit(solution)/shard_map/all_to_all | solution.py:60
  181.8 1.5 collective-permute-start.26
  184.2 4.4 %collective-permute-start.27 = (f32[24,768]{1,0:T(8,128)S(1)}, f32[24,768]{1,0:T(8,128)S(1)}, u32[]{:S(2)}, u32[]{:S(2)}) collective-permute-start(f32[24,768]{1,0:T(8,128)S(1)} %add.48), channel_id=1, source_target_pairs={{0,16},{8,24},{16,0},{24,8},{1,17},{9,25},{17,1},{25,9},{2,18},{10... | collective-permute-start | bytes 221192 | tf_op jit(solution)/shard_map/ppermute | solution.py:52
  188.7 5.1 %collective-permute-start.28 = (f32[24,768]{1,0:T(8,128)S(1)}, f32[24,768]{1,0:T(8,128)S(1)}, u32[]{:S(2)}, u32[]{:S(2)}) collective-permute-start(f32[24,768]{1,0:T(8,128)S(1)} %add.49), channel_id=1, source_target_pairs={{0,1},{1,0},{2,3},{3,2},{4,5},{5,4},{6,7},{7,6},{8,9},{9,8},{10,11... | collective-permute-start | bytes 221192 | tf_op jit(solution)/shard_map/ppermute | solution.py:52
  193.8 4.4 %collective-permute-start.29 = (f32[24,768]{1,0:T(8,128)S(1)}, f32[24,768]{1,0:T(8,128)S(1)}, u32[]{:S(2)}, u32[]{:S(2)}) collective-permute-start(f32[24,768]{1,0:T(8,128)S(1)} %add.50), channel_id=1, source_target_pairs={{0,2},{1,3},{2,0},{3,1},{4,6},{5,7},{6,4},{7,5},{8,10},{9,11},{10,... | collective-permute-start | bytes 221192 | tf_op jit(solution)/shard_map/ppermute | solution.py:52
  198.2 6.7 %collective-permute-start.30 = (f32[24,768]{1,0:T(8,128)S(1)}, f32[24,768]{1,0:T(8,128)S(1)}, u32[]{:S(2)}, u32[]{:S(2)}) collective-permute-start(f32[24,768]{1,0:T(8,128)S(1)} %add.51), channel_id=1, source_target_pairs={{0,4},{1,5},{2,6},{3,7},{4,0},{5,1},{6,2},{7,3},{8,12},{9,13},{10,... | collective-permute-start | bytes 221192 | tf_op jit(solution)/shard_map/ppermute | solution.py:52
  210.7 1.6 collective-permute-start.32
  210.7 5.4 %collective-permute-start.31 = (bf16[192,384]{1,0:T(8,128)(2,1)}, bf16[192,384]{1,0:T(8,128)(2,1)S(1)}, u32[]{:S(2)}, u32[]{:S(2)}) collective-permute-start(bf16[192,384]{1,0:T(8,128)(2,1)} %get-tuple-element.161), channel_id=1, source_target_pairs={{0,8},{8,0},{16,24},{24,16},{1,9},{9,1},{17,25},{25,17},{2,10},{10... | collective-permute-start | bytes 442376 | tf_op jit(solution)/shard_map/ppermute | solution.py:52
  213.2 6.0 %collective-permute-start.33 = (bf16[192,384]{1,0:T(8,128)(2,1)S(1)}, bf16[192,384]{1,0:T(8,128)(2,1)S(1)}, u32[]{:S(2)}, u32[]{:S(2)}) collective-permute-start(bf16[192,384]{1,0:T(8,128)(2,1)S(1)} %add_convert_fusion.6), channel_id=1, source_target_pairs={{0,16},{8,24},{16,0},{24,8},{1,17},{9,25},{17,1},{25,9},{2,18},{10... | collective-permute-start | bytes 442376 | tf_op jit(solution)/shard_map/ppermute | solution.py:52
  (13 other events, 26.6 us)
Sparse Core Ops, SparseCore 0:
  71.4 45.7 all-gather.6
  134.4 49.3 all-gather.4

commit v6 on v5

--- a/solution.py
+++ b/solution.py
@@ -87,41 +87,36 @@
     return items[0], swap(items[1], "dp", bit)
 
 
-def all_sum(value):
+def sum_steps():
+    steps = []
     for axis in ("dp", "expert"):
         bit = 1
         while bit < lax.axis_size(axis):
-            value = value + swap(value, axis, bit)
+            steps.append((axis, bit))
             bit = bit * 2
-    return value
+    return steps
 
 
 def together(*values):
     return lax.optimization_barrier(values)
 
 
-def gather_pieces(payload, early, up_slabs):
+def gather_pieces(payload, early):
     ranks, dps = lax.axis_size("expert"), lax.axis_size("dp")
     half = payload.shape[0] // 2
     far = list(range(0, ranks, 2))
     sides = {"x": ("expert", [0, 1]), "y": ("dp", list(range(0, dps, 2)))}
-    values = [
-        gather_bits(payload[index * half : (index + 1) * half][None], "expert", far[1:])
-        for index in range(2)
-    ]
-    values, early = together(values, early)
+    value, early = together(gather_bits(payload[None], "expert", far[1:]), early)
+    values = (value[:, :half], value[:, half:])
     firsts = []
     for value, letter in zip(values, "xy"):
         axis, masks = sides[letter]
         firsts.append(gather_bits(value[None], axis, masks[1:]))
-    firsts, up_slabs = together(firsts, up_slabs)
-    up_arrived = exchange(up_slabs)
     seconds = []
     for value, letter in zip(firsts, "yx"):
         axis, masks = sides[letter]
         seconds.append([swap(value, axis, mask) for mask in masks[1:]])
     others = [swap(value, "dp", 1) for value in firsts]
-    seconds, others, up_arrived = together(seconds, others, up_arrived)
     pieces, places = [], []
     for index, order in enumerate(("xy", "yx")):
         masks, other_masks = sides[order[0]][1], sides[order[1]][1]
@@ -136,7 +131,7 @@
                     offsets.append((low ^ x_mask, y_mask ^ core))
             pieces.append(piece)
             places.append((index, offsets))
-    return pieces, places, early, up_arrived
+    return pieces, places, early
 
 
 def place_weights(places, piece_refs, w_ref, sem):
@@ -593,11 +588,11 @@
 
     payload = jnp.concatenate([w_query, w_key, w_value, w_output], axis=1)
     early = (normed_low, hits, mask, mask_t, bias_full)
-    pieces, places, early, up_arrived = gather_pieces(payload, early, up_slabs)
+    pieces, places, early = gather_pieces(payload, early)
     normed_low, hits, mask, mask_t, bias_full = early
-    pieces, normed_later = together(pieces, normed_low)
+    pieces, normed_later, up_slabs = together(pieces, normed_low, up_slabs)
     normed_all = lax.all_gather(normed_later, "expert", axis=0)
-    up_far = gather_far(up_arrived.reshape(ranks * slab, model_width))
+    up_arrived = exchange(up_slabs).reshape(ranks * slab, model_width)
 
     w_shape = (ranks, inner_width, 4 * columns_here)
     heads, weights, attended, hidden, chance, slabs = call(
@@ -622,10 +617,12 @@
         ],
     )
 
-    slabs, up_far = together(slabs, up_far)
+    slabs, up_arrived = together(slabs, up_arrived)
     arrived = exchange(slabs).reshape(ranks * slab, model_width)
     attended_all = lax.all_gather(attended, "expert", axis=0)
-    up_pieces = gather_near(up_far)
+    up_pieces = gather_near(gather_far(up_arrived))
+    arrived, up_pieces = together(arrived, up_pieces)
+    row_far = gather_far(arrived)
     by_expert = (local_experts, packed_rows)
     up_rows, up_act = call(
         upstream_kernel,
@@ -634,8 +631,8 @@
         [shaped(LOW, *by_expert, model_width), shaped(FULL, *by_expert, hidden_here)],
         [pack, w_out, *up_pieces],
     )
-    arrived, up_act = together(arrived, up_act)
-    row_pieces = gather_near(gather_far(arrived))
+    row_far, up_act = together(row_far, up_act)
+    row_pieces = gather_near(row_far)
 
     *back, slot_rows, activated, pre_grad, gates = call(
         functools.partial(expert_kernel, dps, slab, rank_slots),
@@ -656,17 +653,6 @@
         ],
     )
     kept, got = scatter_terms(back)
-    first_grad, second_grad, token = call(
-        expert_grad_kernel,
-        "expert_gradients",
-        8,
-        [shaped(FULL, *w_in.shape), shaped(FULL, *w_out.shape), shaped(FULL, 8, 128)],
-        [slot_rows, activated, pre_grad, gates, up_rows],
-    )
-    got, token = together(got, token)
-    back = add(kept, got).reshape(ranks, slab, model_width)
-    back, activated = together(back, activated)
-    back = exchange(back)
     returned = call(
         expert_out_kernel,
         "expert_outputs",
@@ -674,6 +660,17 @@
         [shaped(LOW, ranks * slab, model_width)] * dps,
         [pack_t, w_out, activated],
         scratch=[pltpu.VMEM((*by_expert, model_width), LOW)],
+    )
+    got, returned = together(got, returned)
+    back = add(kept, got).reshape(ranks, slab, model_width)
+    back, activated, returned = together(back, activated, returned)
+    back = exchange(back)
+    first_grad, second_grad, token = call(
+        expert_grad_kernel,
+        "expert_gradients",
+        8,
+        [shaped(FULL, *w_in.shape), shaped(FULL, *w_out.shape), shaped(FULL, 8, 128)],
+        [slot_rows, activated, pre_grad, gates, up_rows],
     )
     returned = add(*scatter_terms(returned)).reshape(ranks, slab, model_width)
     back, returned = together(back, returned)
@@ -717,7 +714,11 @@
 
     factors, small, returned = together(factors, small, returned)
     factors = exchange(factors)
-    factors, small = together(factors, all_sum(small))
+    *steps, one_but_last, last = sum_steps()
+    for axis, bit in steps:
+        small = small + swap(small, axis, bit)
+    factors, small = together(factors, small)
+    small = small + swap(small, *one_but_last)
     output, *grads = call(
         functools.partial(product_kernel, dps),
         "weight_gradients",
@@ -726,6 +727,8 @@
         [normed_all, attended_all, hidden, chance, hits, mask, factors, returned],
         scratch=[pltpu.VMEM((dps, rows_here, 4 * columns_here), FULL)],
     )
+    grads, small = together(grads, small)
+    small = small + swap(small, *last)
     grads = add(*scatter_terms(grads), FULL)
     g_query, g_key, g_value, g_output = (
         grads[:, i * columns_here : (i + 1) * columns_here] for i in range(4)

time: 229 us -> 220 us (0.961)
  blocking collectives: 16.7 us -> 0 us
  waiting for transfers between devices: 72.4 us -> 84.9 us
  starting transfers between devices: 50.6 us -> 47.8 us
    all_to_all x1 -> x0, blocking collectives: 16.7 us -> none  [exchange(): lax.all_to_all(value, 'expert', split_axis=0, concat_axis=0, tiled=True)]
    ppermute x34 -> x31, starting transfers between devices: 34.8 us -> 22.2 us  [swap(): return lax.ppermute(value, axis, [(i, i ^ mask) for i in range(count)])]
    all_to_all x4 -> x5, waiting for transfers between devices: 18.4 us -> 29 us  [exchange(): lax.all_to_all(value, 'expert', split_axis=0, concat_axis=0, tiled=True)]
    all_to_all x4 -> x5, starting transfers between devices: 15.6 us -> 25.3 us  [exchange(): lax.all_to_all(value, 'expert', split_axis=0, concat_axis=0, tiled=True)]
    ppermute x34 -> x31, waiting for transfers between devices: 53.9 us -> 55.8 us  [swap(): return lax.ppermute(value, axis, [(i, i ^ mask) for i in range(count)])]
  transfers between devices with their start and end apart: 40 -> 38, of which waited for: 23 -> 22; matrix products, arithmetic and copies ran while one was open for 5% -> 4% of each run, Pallas kernels for 18% -> 26%
where the time goes in v6:
time: 220 us; the launch traced here: 219 us
  waiting for transfers between devices  84.9 us (39%)
  Pallas kernels  56.8 us (26%)
  starting transfers between devices  47.8 us (22%)
  between operations  14.3 us (6%)
  other arithmetic  8.43 us (4%)
  local copies, waits for them, and re-layouts  6.97 us (3%)
    pallas_call x8, Pallas kernels, call(): pl.pallas_call(kernel, out_shape=tuple(out_shape), in_specs=[VMEM] * len(...  56.8 us
    ppermute x31, waiting for transfers between devices, swap(): return lax.ppermute(value, axis, [(i, i ^ mask) for i in range(count)])  55.8 us
    all_to_all x5, waiting for transfers between devices, exchange(): lax.all_to_all(value, 'expert', split_axis=0, concat_axis=0, tiled=True)  29 us
    all_to_all x5, starting transfers between devices, exchange(): lax.all_to_all(value, 'expert', split_axis=0, concat_axis=0, tiled=True)  25.3 us
    ppermute x31, starting transfers between devices, swap(): return lax.ppermute(value, axis, [(i, i ^ mask) for i in range(count)])  22.2 us
    convert_element_type x5, other arithmetic, add(): return (left.astype(FULL) + right.astype(FULL)).astype(dtype)  4.69 us
  transfers between devices with their start and end apart: 38, of which 22 were waited for; matrix products, arithmetic and copies ran while one was open for 4% of the time, Pallas kernels for 26%

profile of v6, /device:TPU:0, one launch (start us, length us, event | category | flops | bytes accessed | tf_op | source)
XLA Modules:
  0.0 219.2 jit_solution(17119935067146646761)
XLA Ops:
  7.2 1.0 maximum_bitcast_fusion
  8.2 3.1 %collective-permute-start = (bf16[1,192,384]{2,1,0:T(8,128)(2,1)S(1)}, bf16[1,192,384]{2,1,0:T(8,128)(2,1)S(1)}, u32[]{:S(2)}, u32[]{:S(2)}) collective-permute-start(bf16[1,192,384]{2,1,0:T(8,128)(2,1)S(1)} %maximum_bitcast_fusion), channel_id=1, source_target_pairs={{0,2},{1,3},{2,0},{3,1},{4,6},{5,7},{6,4},{7,5},{8,10},{9,11},{10,... | collective-permute-start | bytes 442376 | tf_op jit(solution)/shard_map/ppermute | solution.py:52
  11.3 2.6 %collective-permute-start.1 = (bf16[1,192,384]{2,1,0:T(8,128)(2,1)S(1)}, bf16[1,192,384]{2,1,0:T(8,128)(2,1)S(1)}, u32[]{:S(2)}, u32[]{:S(2)}) collective-permute-start(bf16[1,192,384]{2,1,0:T(8,128)(2,1)S(1)} %maximum_bitcast_fusion), channel_id=1, source_target_pairs={{0,4},{1,5},{2,6},{3,7},{4,0},{5,1},{6,2},{7,3},{8,12},{9,13},{10,... | collective-permute-start | bytes 442376 | tf_op jit(solution)/shard_map/ppermute | solution.py:52
  15.9 3.3 %early.1 = (bf16[128,768]{1,0:T(8,128)(2,1)}, f32[128,16]{1,0:T(8,128)}, bf16[128,192]{1,0:T(8,128)(2,1)}, bf16[192,128]{1,0:T(8,128)(2,1)}, f32[12,128,128]{2,1,0:T(8,128)}, /*index=5*/bf16[8,24,768]{2,1,0:T(8,128)(2,1)}) custom-call(bf16[128,768]{1,0:T(8,128)(2,1)} %tokens_ref.5, s32[1,128]{1,0:T(1,128)} %bitcast.27, ...), custom_call_target="tpu_custom_call" | custom-call | bytes 10800000 | tf_op jit(solution)/shard_map/early/pallas_call | solution.py:520
  19.2 6.1 %collective-permute-done.1 = bf16[1,192,384]{2,1,0:T(8,128)(2,1)S(1)} collective-permute-done((bf16[1,192,384]{2,1,0:T(8,128)(2,1)S(1)}, bf16[1,192,384]{2,1,0:T(8,128)(2,1)S(1)}, u32[]{:S(2)}, u32[]{:S(2)}) %collective-permute-start.1) | collective-permute-done | bytes 147488 | tf_op jit(solution)/shard_map/ppermute | solution.py:52
  25.4 1.6 collective-permute-start.7
  27.0 1.5 collective-permute-start.3
  28.5 3.7 %collective-permute-done.7 = bf16[1,4,96,384]{3,2,1,0:T(8,128)(2,1)S(1)} collective-permute-done((bf16[1,4,96,384]{3,2,1,0:T(8,128)(2,1)S(1)}, bf16[1,4,96,384]{3,2,1,0:T(8,128)(2,1)S(1)}, u32[]{:S(2)}, u32[]{:S(2)}) %collective-permute-start.7) | collective-permute-done | bytes 294944 | tf_op jit(solution)/shard_map/ppermute | solution.py:52
  32.3 1.6 collective-permute-start.9
  33.9 2.5 %collective-permute-done.3 = bf16[1,4,96,384]{3,2,1,0:T(8,128)(2,1)S(1)} collective-permute-done((bf16[1,4,96,384]{3,2,1,0:T(8,128)(2,1)S(1)}, bf16[1,4,96,384]{3,2,1,0:T(8,128)(2,1)S(1)}, u32[]{:S(2)}, u32[]{:S(2)}) %collective-permute-start.3) | collective-permute-done | bytes 294944 | tf_op jit(solution)/shard_map/ppermute | solution.py:52
  37.1 9.3 %collective-permute-done.9.rest_6_ = bf16[2,4,96,384]{3,2,1,0:T(8,128)(2,1)S(1)} collective-permute-done((bf16[2,4,96,384]{3,2,1,0:T(8,128)(2,1)S(1)}, bf16[2,4,96,384]{3,2,1,0:T(8,128)(2,1)S(1)}, u32[]{:S(2)}, u32[]{:S(2)}) %collective-permute-start.9) | collective-permute-done | bytes 589856 | tf_op jit(solution)/shard_map/ppermute | solution.py:52
  46.9 1.5 collective-permute-done.10.rest_7_
  50.1 6.3 %all-to-all-start = ((bf16[8,24,768]{2,1,0:T(8,128)(2,1)}), bf16[8,24,768]{2,1,0:T(8,128)(2,1)}, u32[]{:S(2)}, u32[]{:S(2)}) async-start(bf16[8,24,768]{2,1,0:T(8,128)(2,1)} %get-tuple-element.125), calls=%async_computation | async-start | bytes 589824 | tf_op jit(solution)/shard_map/all_to_all | solution.py:60
  56.5 9.9 %attention_forward.1 = (bf16[3,768,128]{2,1,0:T(8,128)(2,1)}, f32[12,128,128]{2,1,0:T(8,128)}, bf16[128,768]{1,0:T(8,128)(2,1)}, f32[128,768]{1,0:T(8,128)}, f32...) custom-call(bf16[128,768]{1,0:T(8,128)(2,1)} %tokens_ref.5, bf16[128,768]{1,0:T(8,128)(2,1)} %get-tuple-element.106.normed_ref, ...), custom_call_target="tpu_custom_call" | custom-call | bytes 36000000 | tf_op jit(solution)/shard_map/attention_forward/pallas_call | solution.py:520
  66.4 1.0 collective-permute-start.12
  67.4 6.0 %all-to-all-start.1 = ((bf16[8,24,768]{2,1,0:T(8,128)(2,1)}), bf16[8,24,768]{2,1,0:T(8,128)(2,1)S(1)}, u32[]{:S(2)}, u32[]{:S(2)}) async-start(bf16[8,24,768]{2,1,0:T(8,128)(2,1)} %get-tuple-element.126), calls=%async_computation.1 | async-start | bytes 589824 | tf_op jit(solution)/shard_map/all_to_all | solution.py:60
  73.7 1.7 collective-permute-done.12.rest_2_
  75.5 11.8 %all-to-all-done.1 = bf16[8,24,768]{2,1,0:T(8,128)(2,1)S(1)} async-done(((bf16[8,24,768]{2,1,0:T(8,128)(2,1)}), bf16[8,24,768]{2,1,0:T(8,128)(2,1)S(1)}, u32[]{:S(2)}, u32[]{:S(2)}) %all-to-all-start.1) | async-done | bytes 294944 | tf_op jit(solution)/shard_map/all_to_all | solution.py:60
  88.1 4.5 %upstream_rows.1 = (bf16[2,320,768]{2,1,0:T(8,128)(2,1)}, f32[2,320,768]{2,1,0:T(8,128)}) custom-call(bf16[160,192]{1,0:T(8,128)(2,1)} %constant.8.clone.pack_ref, bf16[2,768,768]{2,1,0:T(8,128)(2,1)} %w_out_ref.3, bf16[192,768]{1,0:T(8,128)(2,1)} %bitcast.8.rest_0_, bf16[192,768]{1,0:T(8,128)(2,1)} %copy-done.14, bf16[192,768]{1,0:T(8,128)(2,1)} %copy-done.12, ...), custom_call_target="tpu_custom_call" | custom-call | bytes 18000000 | tf_op jit(solution)/shard_map/upstream_rows/pallas_call | solution.py:520
  92.5 1.5 collective-permute-done.14.rest_2_
  94.6 1.1 collective-permute-done.15.rest_1_
  97.1 10.0 %experts.1 = (bf16[192,768]{1,0:T(8,128)(2,1)}, bf16[192,768]{1,0:T(8,128)(2,1)}, bf16[192,768]{1,0:T(8,128)(2,1)}, bf16[192,768]{1,0:T(8,128)(2,1)}, bf16[2,320...) custom-call(bf16[160,192]{1,0:T(8,128)(2,1)} %constant.8.clone.pack_re, ...), custom_call_target="tpu_custom_call" | custom-call | bytes 36000000 | tf_op jit(solution)/shard_map/experts/pallas_call | solution.py:520
  107.3 1.7 collective-permute-done.18
  108.9 1.0 add_convert_fusion.4
  110.4 4.0 %expert_outputs.1 = (bf16[192,768]{1,0:T(8,128)(2,1)}, bf16[192,768]{1,0:T(8,128)(2,1)}, bf16[192,768]{1,0:T(8,128)(2,1)}, bf16[192,768]{1,0:T(8,128)(2,1)}) custom-call(bf16[192,160]{1,0:T(8,128)(2,1)} %constant.9.clone.pack_t_ref, bf16[2,768,768]{2,1,0:T(8,128)(2,1)} %w_out_ref.3, bf16[2,320,768]{2,1,0:T(8,128)(2,1)} %get-tuple-element.152.act_ref), custom_call_target="tpu_custom_call" | custom-call | bytes 10800000 | tf_op jit(solution)/shard_map/expert_outputs/pallas_call | solution.py:520
  114.4 4.7 %collective-permute-done.19 = bf16[192,768]{1,0:T(8,128)(2,1)S(1)} collective-permute-done((bf16[192,768]{1,0:T(8,128)(2,1)S(1)}, bf16[192,768]{1,0:T(8,128)(2,1)S(1)}, u32[]{:S(2)}, u32[]{:S(2)}) %collective-permute-start.19) | collective-permute-done | bytes 294944 | tf_op jit(solution)/shard_map/ppermute | solution.py:52
  120.5 1.2 collective-permute-done.21
  121.7 1.0 add_convert_fusion.1
  123.2 3.6 %all-to-all-start.2 = ((bf16[8,24,768]{2,1,0:T(8,128)(2,1)}), bf16[8,24,768]{2,1,0:T(8,128)(2,1)S(1)}, u32[]{:S(2)}, u32[]{:S(2)}) async-start(bf16[8,24,768]{2,1,0:T(8,128)(2,1)} %bitcast.10), calls=%async_computation.2 | async-start | bytes 589824 | tf_op jit(solution)/shard_map/all_to_all | solution.py:60
  126.8 5.0 %collective-permute-done.22 = bf16[192,768]{1,0:T(8,128)(2,1)S(1)} collective-permute-done((bf16[192,768]{1,0:T(8,128)(2,1)S(1)}, bf16[192,768]{1,0:T(8,128)(2,1)S(1)}, u32[]{:S(2)}, u32[]{:S(2)}) %collective-permute-start.22) | collective-permute-done | bytes 294944 | tf_op jit(solution)/shard_map/ppermute | solution.py:52
  132.7 9.7 %all-to-all-done.2.rest_8_ = bf16[8,24,768]{2,1,0:T(8,128)(2,1)S(1)} async-done(((bf16[8,24,768]{2,1,0:T(8,128)(2,1)}), bf16[8,24,768]{2,1,0:T(8,128)(2,1)S(1)}, u32[]{:S(2)}, u32[]{:S(2)}) %all-to-all-start.2) | async-done | bytes 294944 | tf_op jit(solution)/shard_map/all_to_all | solution.py:60
  142.5 3.6 %all-to-all-start.3 = ((bf16[8,24,768]{2,1,0:T(8,128)(2,1)}), bf16[8,24,768]{2,1,0:T(8,128)(2,1)S(1)}, u32[]{:S(2)}, u32[]{:S(2)}) async-start(bf16[8,24,768]{2,1,0:T(8,128)(2,1)} %bitcast.11), calls=%async_computation.3 | async-start | bytes 589824 | tf_op jit(solution)/shard_map/all_to_all | solution.py:60
  146.1 8.4 %expert_gradients.1 = (f32[2,768,768]{2,1,0:T(8,128)}, f32[2,768,768]{2,1,0:T(8,128)}, f32[8,128]{1,0:T(8,128)}) custom-call(bf16[2,320,768]{2,1,0:T(8,128)(2,1)} %get-tuple-element.137.rows_ref, bf16[2,320,768]{2,1,0:T(8,128)(2,1)} %get-tuple-element.152.act_ref, bf16[2,320,768]{2,1,0:T(8,128)(2,1)} %get-tuple-element.153.pre_grad_ref, ...), custom_call_target="tpu_custom_call" | custom-call | bytes 28800000 | tf_op jit(solution)/shard_map/expert_gradients/pallas_call | solution.py:520
  154.5 11.9 %attention_backward.1 = (f32[128,768]{1,0:T(8,128)}, f32[24,768]{1,0:T(8,128)}, bf16[8,384,128]{2,1,0:T(8,128)(2,1)}) custom-call(bf16[128,768]{1,0:T(8,128)(2,1)} %tokens_ref.5, f32[2,768]{1,0:T(2,128)} %maximum_convert_fusion.gain_ref, bf16[16,768]{1,0:T(8,128)(2,1)} %bitcast.25, f32[128,16]{1,0:T(8,128)} %get-tuple-element.108.hits_ref, ...), custom_call_target="tpu_custom_call" | custom-call | bytes 43200000 | tf_op jit(solution)/shard_map/attention_backward/pallas_call | solution.py:520
  166.5 5.8 %all-to-all-start.4 = ((bf16[8,384,128]{2,1,0:T(8,128)(2,1)}), bf16[8,384,128]{2,1,0:T(8,128)(2,1)S(1)}, u32[]{:S(2)}, u32[]{:S(2)}) async-start(bf16[8,384,128]{2,1,0:T(8,128)(2,1)} %get-tuple-element.166), calls=%async_computation.4 | async-start | bytes 1572864 | tf_op jit(solution)/shard_map/all_to_all | solution.py:60
  172.2 1.5 collective-permute-done.23
  173.7 0.9 add.48
  174.6 1.6 collective-permute-start.24
  176.2 2.8 %collective-permute-done.24 = f32[24,768]{1,0:T(8,128)S(1)} collective-permute-done((f32[24,768]{1,0:T(8,128)S(1)}, f32[24,768]{1,0:T(8,128)S(1)}, u32[]{:S(2)}, u32[]{:S(2)}) %collective-permute-start.24) | collective-permute-done | bytes 73760 | tf_op jit(solution)/shard_map/ppermute | solution.py:52
  179.0 2.1 collective-permute-start.25
  181.1 3.3 %collective-permute-done.25 = f32[24,768]{1,0:T(8,128)S(1)} collective-permute-done((f32[24,768]{1,0:T(8,128)S(1)}, f32[24,768]{1,0:T(8,128)S(1)}, u32[]{:S(2)}, u32[]{:S(2)}) %collective-permute-start.25) | collective-permute-done | bytes 73760 | tf_op jit(solution)/shard_map/ppermute | solution.py:52
  184.4 7.4 %all-to-all-done.4.factors_ref = bf16[8,384,128]{2,1,0:T(8,128)(2,1)S(1)} async-done(((bf16[8,384,128]{2,1,0:T(8,128)(2,1)}), bf16[8,384,128]{2,1,0:T(8,128)(2,1)S(1)}, u32[]{:S(2)}, u32[]{:S(2)}) %all-to-all-start.4) | async-done | bytes 786464 | tf_op jit(solution)/shard_map/all_to_all | solution.py:60
  192.7 4.8 %weight_gradients.1 = (bf16[128,768]{1,0:T(8,128)(2,1)}, bf16[192,384]{1,0:T(8,128)(2,1)}, bf16[192,384]{1,0:T(8,128)(2,1)}, bf16[192,384]{1,0:T(8,128)(2,1)}, bf16[192,384]{1,0:T(8,128)(2,1)}) custom-call(bf16[8,128,768]{2,1,0:T(8,128)(2,1)} %bitcast.20, bf16[8,128,768]{2,1,0:T(8,128)(2,1)} %bitcast.19, f32[128,768]{1,0:T(8,128)} %get-tuple-element.119.hidden_ref, ...), custom_call_target="tpu_custom_call" | custom-call | bytes 18000000 | tf_op jit(solution)/shard_map/weight_gradients/pallas_call | solution.py:520
  198.9 4.8 %collective-permute-done.27 = f32[24,768]{1,0:T(8,128)S(1)} collective-permute-done((f32[24,768]{1,0:T(8,128)S(1)}, f32[24,768]{1,0:T(8,128)S(1)}, u32[]{:S(2)}, u32[]{:S(2)}) %collective-permute-start.27) | collective-permute-done | bytes 73760 | tf_op jit(solution)/shard_map/ppermute | solution.py:52
  204.3 1.0 add_convert_fusion.6
  205.3 1.8 collective-permute-start.30
  208.3 2.2 collective-permute-done.30
  210.5 1.0 convert_add_fusion
  (103 shorter events, 16.5 us)
Async XLA Ops:
  8.2 11.0 %collective-permute-start = (bf16[1,192,384]{2,1,0:T(8,128)(2,1)S(1)}, bf16[1,192,384]{2,1,0:T(8,128)(2,1)S(1)}, u32[]{:S(2)}, u32[]{:S(2)}) collective-permute-start(bf16[1,192,384]{2,1,0:T(8,128)(2,1)S(1)} %maximum_bitcast_fusion), channel_id=1, source_target_pairs={{0,2},{1,3},{2,0},{3,1},{4,6},{5,7},{6,4},{7,5},{8,10},{9,11},{10,... | collective-permute-start | bytes 442376 | tf_op jit(solution)/shard_map/ppermute | solution.py:52
  11.3 14.0 %collective-permute-start.1 = (bf16[1,192,384]{2,1,0:T(8,128)(2,1)S(1)}, bf16[1,192,384]{2,1,0:T(8,128)(2,1)S(1)}, u32[]{:S(2)}, u32[]{:S(2)}) collective-permute-start(bf16[1,192,384]{2,1,0:T(8,128)(2,1)S(1)} %maximum_bitcast_fusion), channel_id=1, source_target_pairs={{0,4},{1,5},{2,6},{3,7},{4,0},{5,1},{6,2},{7,3},{8,12},{9,13},{10,... | collective-permute-start | bytes 442376 | tf_op jit(solution)/shard_map/ppermute | solution.py:52
  13.9 11.4 %collective-permute-start.2 = (bf16[1,192,384]{2,1,0:T(8,128)(2,1)S(1)}, bf16[1,192,384]{2,1,0:T(8,128)(2,1)S(1)}, u32[]{:S(2)}, u32[]{:S(2)}) collective-permute-start(bf16[1,192,384]{2,1,0:T(8,128)(2,1)S(1)} %maximum_bitcast_fusion), channel_id=1, source_target_pairs={{0,6},{1,7},{2,4},{3,5},{4,2},{5,3},{6,0},{7,1},{8,14},{9,15},{10,... | collective-permute-start | bytes 442376 | tf_op jit(solution)/shard_map/ppermute | solution.py:52
  25.4 6.8 %collective-permute-start.7 = (bf16[1,4,96,384]{3,2,1,0:T(8,128)(2,1)S(1)}, bf16[1,4,96,384]{3,2,1,0:T(8,128)(2,1)S(1)}, u32[]{:S(2)}, u32[]{:S(2)}) collective-permute-start(bf16[1,4,96,384]{3,2,1,0:T(8,128)(2,1)S(1)} %get-tuple-element.186), channel_id=1, source_target_pairs={{0,16},{8,24},{16,0},{24,8},{1,17},{9,25},{17,1},{25,9},{2,18},{10... | collective-permute-start | bytes 884744 | tf_op jit(solution)/shard_map/ppermute | solution.py:52
  27.0 9.3 %collective-permute-start.3 = (bf16[1,4,96,384]{3,2,1,0:T(8,128)(2,1)S(1)}, bf16[1,4,96,384]{3,2,1,0:T(8,128)(2,1)S(1)}, u32[]{:S(2)}, u32[]{:S(2)}) collective-permute-start(bf16[1,4,96,384]{3,2,1,0:T(8,128)(2,1)S(1)} %get-tuple-element.187), channel_id=1, source_target_pairs={{0,1},{1,0},{2,3},{3,2},{4,5},{5,4},{6,7},{7,6},{8,9},{9,8},{10,11... | collective-permute-start | bytes 884744 | tf_op jit(solution)/shard_map/ppermute | solution.py:52
  32.3 24.1 %copy-start = (bf16[2,4,96,384]{3,2,1,0:T(8,128)(2,1)}, bf16[2,4,96,384]{3,2,1,0:T(8,128)(2,1)S(1)}, u32[]{:S(2)}) copy-start(bf16[2,4,96,384]{3,2,1,0:T(8,128)(2,1)S(1)} %pad_maximum_fusion.2.rest_4_) | copy-start | bytes 1769476
  32.3 14.1 %collective-permute-start.9 = (bf16[2,4,96,384]{3,2,1,0:T(8,128)(2,1)S(1)}, bf16[2,4,96,384]{3,2,1,0:T(8,128)(2,1)S(1)}, u32[]{:S(2)}, u32[]{:S(2)}) collective-permute-start(bf16[2,4,96,384]{3,2,1,0:T(8,128)(2,1)S(1)} %pad_maximum_fusion.2.rest_4_), channel_id=1, source_target_pairs={{0,1},{1,0},{2,3},{3,2},{4,5},{5,4},{6,7},{7,6},{8,9},{9,8},{10,11... | collective-permute-start | bytes 1769480 | tf_op jit(solution)/shard_map/ppermute | solution.py:52
  36.4 20.0 %copy-start.1 = (bf16[2,4,96,384]{3,2,1,0:T(8,128)(2,1)}, bf16[2,4,96,384]{3,2,1,0:T(8,128)(2,1)S(1)}, u32[]{:S(2)}) copy-start(bf16[2,4,96,384]{3,2,1,0:T(8,128)(2,1)S(1)} %pad_maximum_fusion.1.rest_0_) | copy-start | bytes 1769476
  36.5 9.9 %collective-permute-start.5 = (bf16[2,4,96,384]{3,2,1,0:T(8,128)(2,1)S(1)}, bf16[2,4,96,384]{3,2,1,0:T(8,128)(2,1)S(1)}, u32[]{:S(2)}, u32[]{:S(2)}) collective-permute-start(bf16[2,4,96,384]{3,2,1,0:T(8,128)(2,1)S(1)} %pad_maximum_fusion.1.rest_0_), channel_id=1, source_target_pairs={{0,16},{8,24},{16,0},{24,8},{1,17},{9,25},{17,1},{25,9},{2,18},{10... | collective-permute-start | bytes 1769480 | tf_op jit(solution)/shard_map/ppermute | solution.py:52
  36.5 10.4 %collective-permute-start.8 = (bf16[2,4,96,384]{3,2,1,0:T(8,128)(2,1)S(1)}, bf16[2,4,96,384]{3,2,1,0:T(8,128)(2,1)S(1)}, u32[]{:S(2)}, u32[]{:S(2)}) collective-permute-start(bf16[2,4,96,384]{3,2,1,0:T(8,128)(2,1)S(1)} %pad_maximum_fusion.2.rest_4_), channel_id=1, source_target_pairs={{0,8},{8,0},{16,24},{24,16},{1,9},{9,1},{17,25},{25,17},{2,10},{10... | collective-permute-start | bytes 1769480 | tf_op jit(solution)/shard_map/ppermute | solution.py:52
  36.6 10.3 %collective-permute-start.4 = (bf16[2,4,96,384]{3,2,1,0:T(8,128)(2,1)S(1)}, bf16[2,4,96,384]{3,2,1,0:T(8,128)(2,1)S(1)}, u32[]{:S(2)}, u32[]{:S(2)}) collective-permute-start(bf16[2,4,96,384]{3,2,1,0:T(8,128)(2,1)S(1)} %pad_maximum_fusion.1.rest_0_), channel_id=1, source_target_pairs={{0,8},{8,0},{16,24},{24,16},{1,9},{9,1},{17,25},{25,17},{2,10},{10... | collective-permute-start | bytes 1769480 | tf_op jit(solution)/shard_map/ppermute | solution.py:52
  46.4 10.0 %copy-start.3 = (bf16[2,4,96,384]{3,2,1,0:T(8,128)(2,1)}, bf16[2,4,96,384]{3,2,1,0:T(8,128)(2,1)S(1)}, u32[]{:S(2)}) copy-start(bf16[2,4,96,384]{3,2,1,0:T(8,128)(2,1)S(1)} %collective-permute-done.9.rest_6_) | copy-start | bytes 1769476
  46.4 2.0 collective-permute-start.10
  46.4 10.0 %copy-start.4 = (bf16[2,4,96,384]{3,2,1,0:T(8,128)(2,1)}, bf16[2,4,96,384]{3,2,1,0:T(8,128)(2,1)S(1)}, u32[]{:S(2)}) copy-start(bf16[2,4,96,384]{3,2,1,0:T(8,128)(2,1)S(1)} %collective-permute-done.5.rest_2_) | copy-start | bytes 1769476
  46.4 2.8 %collective-permute-start.6 = (bf16[2,4,96,384]{3,2,1,0:T(8,128)(2,1)S(1)}, bf16[2,4,96,384]{3,2,1,0:T(8,128)(2,1)S(1)}, u32[]{:S(2)}, u32[]{:S(2)}) collective-permute-start(bf16[2,4,96,384]{3,2,1,0:T(8,128)(2,1)S(1)} %collective-permute-done.5.rest_2_), channel_id=1, source_target_pairs={{0,8},{8,0},{16,24},{24,16},{1,9},{9,1},{17,25},{25,17},{2,10},{10... | collective-permute-start | bytes 1769480 | tf_op jit(solution)/shard_map/ppermute | solution.py:52
  50.1 16.3 %all-to-all-start = ((bf16[8,24,768]{2,1,0:T(8,128)(2,1)}), bf16[8,24,768]{2,1,0:T(8,128)(2,1)}, u32[]{:S(2)}, u32[]{:S(2)}) async-start(bf16[8,24,768]{2,1,0:T(8,128)(2,1)} %get-tuple-element.125), calls=%async_computation | async-start | bytes 589824 | tf_op jit(solution)/shard_map/all_to_all | solution.py:60
  56.4 135.7 %all-gather.7.cloned.1.call-start = ((), (), s32[]{:S(2)}) async-start(), calls=%async_computation.6 | async-start | bytes 1769472 | tf_op jit(solution)/shard_map/all_gather | solution.py:622
  66.4 9.1 %collective-permute-start.12 = (bf16[192,768]{1,0:T(8,128)(2,1)}, bf16[192,768]{1,0:T(8,128)(2,1)S(1)}, u32[]{:S(2)}, u32[]{:S(2)}) collective-permute-start(bf16[192,768]{1,0:T(8,128)(2,1)} %bitcast.8.rest_0_), channel_id=1, source_target_pairs={{0,16},{8,24},{16,0},{24,8},{1,17},{9,25},{17,1},{25,9},{2,18},{10... | collective-permute-start | bytes 884744 | tf_op jit(solution)/shard_map/ppermute | solution.py:52
  67.4 19.9 %all-to-all-start.1 = ((bf16[8,24,768]{2,1,0:T(8,128)(2,1)}), bf16[8,24,768]{2,1,0:T(8,128)(2,1)S(1)}, u32[]{:S(2)}, u32[]{:S(2)}) async-start(bf16[8,24,768]{2,1,0:T(8,128)(2,1)} %get-tuple-element.126), calls=%async_computation.1 | async-start | bytes 589824 | tf_op jit(solution)/shard_map/all_to_all | solution.py:60
  73.4 118.7 %all-gather.5.cloned.1.call-start = ((), (), s32[]{:S(2)}) async-start(), calls=%async_computation.5 | async-start | bytes 1769472 | tf_op jit(solution)/shard_map/all_gather | solution.py:594
  73.6 1.9 collective-permute-start.11
  75.4 12.3 %copy-start.12 = (bf16[192,768]{1,0:T(8,128)(2,1)}, bf16[192,768]{1,0:T(8,128)(2,1)S(1)}, u32[]{:S(2)}) copy-start(bf16[192,768]{1,0:T(8,128)(2,1)S(1)} %collective-permute-done.12.rest_2_) | copy-start | bytes 884740
  75.4 11.9 %collective-permute-start.13 = (bf16[192,768]{1,0:T(8,128)(2,1)S(1)}, bf16[192,768]{1,0:T(8,128)(2,1)S(1)}, u32[]{:S(2)}, u32[]{:S(2)}) collective-permute-start(bf16[192,768]{1,0:T(8,128)(2,1)S(1)} %collective-permute-done.12.rest_2_), channel_id=1, source_target_pairs={{0,8},{8,0},{16,24},{24,16},{1,9},{9,1},{17,25},{25,17},{2,10},{10... | collective-permute-start | bytes 884744 | tf_op jit(solution)/shard_map/ppermute | solution.py:52
  75.5 12.2 %copy-start.14 = (bf16[192,768]{1,0:T(8,128)(2,1)}, bf16[192,768]{1,0:T(8,128)(2,1)S(1)}, u32[]{:S(2)}) copy-start(bf16[192,768]{1,0:T(8,128)(2,1)S(1)} %collective-permute-done.11.rest_1_) | copy-start | bytes 884740
  87.3 6.8 %collective-permute-start.14 = (bf16[192,768]{1,0:T(8,128)(2,1)S(1)}, bf16[192,768]{1,0:T(8,128)(2,1)S(1)}, u32[]{:S(2)}, u32[]{:S(2)}) collective-permute-start(bf16[192,768]{1,0:T(8,128)(2,1)S(1)} %bitcast.21), channel_id=1, source_target_pairs={{0,16},{8,24},{16,0},{24,8},{1,17},{9,25},{17,1},{25,9},{2,18},{10... | collective-permute-start | bytes 884744 | tf_op jit(solution)/shard_map/ppermute | solution.py:52
  94.1 1.6 collective-permute-start.15
  94.1 2.0 collective-permute-start.16
  107.1 12.0 %copy-start.19 = (bf16[192,768]{1,0:T(8,128)(2,1)S(1)}, bf16[192,768]{1,0:T(8,128)(2,1)}, u32[]{:S(2)}) copy-start(bf16[192,768]{1,0:T(8,128)(2,1)} %get-tuple-element.138) | copy-start | bytes 884740
  107.1 1.9 collective-permute-start.18
  110.0 9.1 %collective-permute-start.19 = (bf16[192,768]{1,0:T(8,128)(2,1)S(1)}, bf16[192,768]{1,0:T(8,128)(2,1)S(1)}, u32[]{:S(2)}, u32[]{:S(2)}) collective-permute-start(bf16[192,768]{1,0:T(8,128)(2,1)S(1)} %add_convert_fusion.4), channel_id=1, source_target_pairs={{0,16},{8,24},{16,0},{24,8},{1,17},{9,25},{17,1},{25,9},{2,18},{10... | collective-permute-start | bytes 884744 | tf_op jit(solution)/shard_map/ppermute | solution.py:52
  110.4 8.7 %collective-permute-start.17 = (bf16[192,768]{1,0:T(8,128)(2,1)}, bf16[192,768]{1,0:T(8,128)(2,1)S(1)}, u32[]{:S(2)}, u32[]{:S(2)}) collective-permute-start(bf16[192,768]{1,0:T(8,128)(2,1)} %get-tuple-element.139), channel_id=1, source_target_pairs={{0,8},{8,0},{16,24},{24,16},{1,9},{9,1},{17,25},{25,17},{2,10},{10... | collective-permute-start | bytes 884744 | tf_op jit(solution)/shard_map/ppermute | solution.py:52
  114.4 17.5 %copy-start.18 = (bf16[192,768]{1,0:T(8,128)(2,1)S(1)}, bf16[192,768]{1,0:T(8,128)(2,1)}, u32[]{:S(2)}) copy-start(bf16[192,768]{1,0:T(8,128)(2,1)} %get-tuple-element.158) | copy-start | bytes 884740
  119.9 1.8 collective-permute-start.21
  120.0 6.9 %collective-permute-start.20 = (bf16[192,768]{1,0:T(8,128)(2,1)}, bf16[192,768]{1,0:T(8,128)(2,1)S(1)}, u32[]{:S(2)}, u32[]{:S(2)}) collective-permute-start(bf16[192,768]{1,0:T(8,128)(2,1)} %get-tuple-element.159), channel_id=1, source_target_pairs={{0,8},{8,0},{16,24},{24,16},{1,9},{9,1},{17,25},{25,17},{2,10},{10... | collective-permute-start | bytes 884744 | tf_op jit(solution)/shard_map/ppermute | solution.py:52
  122.8 9.1 %collective-permute-start.22 = (bf16[192,768]{1,0:T(8,128)(2,1)S(1)}, bf16[192,768]{1,0:T(8,128)(2,1)S(1)}, u32[]{:S(2)}, u32[]{:S(2)}) collective-permute-start(bf16[192,768]{1,0:T(8,128)(2,1)S(1)} %add_convert_fusion.1), channel_id=1, source_target_pairs={{0,16},{8,24},{16,0},{24,8},{1,17},{9,25},{17,1},{25,9},{2,18},{10... | collective-permute-start | bytes 884744 | tf_op jit(solution)/shard_map/ppermute | solution.py:52
  123.2 19.3 %all-to-all-start.2 = ((bf16[8,24,768]{2,1,0:T(8,128)(2,1)}), bf16[8,24,768]{2,1,0:T(8,128)(2,1)S(1)}, u32[]{:S(2)}, u32[]{:S(2)}) async-start(bf16[8,24,768]{2,1,0:T(8,128)(2,1)} %bitcast.10), calls=%async_computation.2 | async-start | bytes 589824 | tf_op jit(solution)/shard_map/all_to_all | solution.py:60
  142.5 12.0 %copy-start.11 = (bf16[8,24,768]{2,1,0:T(8,128)(2,1)}, bf16[8,24,768]{2,1,0:T(8,128)(2,1)S(1)}, u32[]{:S(2)}) copy-start(bf16[8,24,768]{2,1,0:T(8,128)(2,1)S(1)} %all-to-all-done.2.rest_8_) | copy-start | bytes 884740
  142.5 24.0 %all-to-all-start.3 = ((bf16[8,24,768]{2,1,0:T(8,128)(2,1)}), bf16[8,24,768]{2,1,0:T(8,128)(2,1)S(1)}, u32[]{:S(2)}, u32[]{:S(2)}) async-start(bf16[8,24,768]{2,1,0:T(8,128)(2,1)} %bitcast.11), calls=%async_computation.3 | async-start | bytes 589824 | tf_op jit(solution)/shard_map/all_to_all | solution.py:60
  166.4 25.7 %copy-start.9 = (bf16[8,24,768]{2,1,0:T(8,128)(2,1)}, bf16[8,24,768]{2,1,0:T(8,128)(2,1)S(1)}, u32[]{:S(2)}) copy-start(bf16[8,24,768]{2,1,0:T(8,128)(2,1)S(1)} %all-to-all-done.3.returned_ref) | copy-start | bytes 884740
  166.5 25.4 %all-to-all-start.4 = ((bf16[8,384,128]{2,1,0:T(8,128)(2,1)}), bf16[8,384,128]{2,1,0:T(8,128)(2,1)S(1)}, u32[]{:S(2)}, u32[]{:S(2)}) async-start(bf16[8,384,128]{2,1,0:T(8,128)(2,1)} %get-tuple-element.166), calls=%async_computation.4 | async-start | bytes 1572864 | tf_op jit(solution)/shard_map/all_to_all | solution.py:60
  172.2 1.5 collective-permute-start.23
  174.6 4.4 %collective-permute-start.24 = (f32[24,768]{1,0:T(8,128)S(1)}, f32[24,768]{1,0:T(8,128)S(1)}, u32[]{:S(2)}, u32[]{:S(2)}) collective-permute-start(f32[24,768]{1,0:T(8,128)S(1)} %add.48), channel_id=1, source_target_pairs={{0,16},{8,24},{16,0},{24,8},{1,17},{9,25},{17,1},{25,9},{2,18},{10... | collective-permute-start | bytes 221192 | tf_op jit(solution)/shard_map/ppermute | solution.py:52
  179.0 5.4 %collective-permute-start.25 = (f32[24,768]{1,0:T(8,128)S(1)}, f32[24,768]{1,0:T(8,128)S(1)}, u32[]{:S(2)}, u32[]{:S(2)}) collective-permute-start(f32[24,768]{1,0:T(8,128)S(1)} %add.49), channel_id=1, source_target_pairs={{0,1},{1,0},{2,3},{3,2},{4,5},{5,4},{6,7},{7,6},{8,9},{9,8},{10,11... | collective-permute-start | bytes 221192 | tf_op jit(solution)/shard_map/ppermute | solution.py:52
  191.8 5.7 %collective-permute-start.26 = (f32[24,768]{1,0:T(8,128)S(1)}, f32[24,768]{1,0:T(8,128)S(1)}, u32[]{:S(2)}, u32[]{:S(2)}) collective-permute-start(f32[24,768]{1,0:T(8,128)S(1)} %add.50), channel_id=1, source_target_pairs={{0,2},{1,3},{2,0},{3,1},{4,6},{5,7},{6,4},{7,5},{8,10},{9,11},{10,... | collective-permute-start | bytes 221192 | tf_op jit(solution)/shard_map/ppermute | solution.py:52
  197.6 6.1 %collective-permute-start.27 = (f32[24,768]{1,0:T(8,128)S(1)}, f32[24,768]{1,0:T(8,128)S(1)}, u32[]{:S(2)}, u32[]{:S(2)}) collective-permute-start(f32[24,768]{1,0:T(8,128)S(1)} %add.51), channel_id=1, source_target_pairs={{0,4},{1,5},{2,6},{3,7},{4,0},{5,1},{6,2},{7,3},{8,12},{9,13},{10,... | collective-permute-start | bytes 221192 | tf_op jit(solution)/shard_map/ppermute | solution.py:52
  198.4 6.0 %collective-permute-start.29 = (bf16[192,384]{1,0:T(8,128)(2,1)}, bf16[192,384]{1,0:T(8,128)(2,1)S(1)}, u32[]{:S(2)}, u32[]{:S(2)}) collective-permute-start(bf16[192,384]{1,0:T(8,128)(2,1)} %get-tuple-element.181), channel_id=1, source_target_pairs={{0,8},{8,0},{16,24},{24,16},{1,9},{9,1},{17,25},{25,17},{2,10},{10... | collective-permute-start | bytes 442376 | tf_op jit(solution)/shard_map/ppermute | solution.py:52
  198.4 10.0 %collective-permute-start.28 = (bf16[192,384]{1,0:T(8,128)(2,1)}, bf16[192,384]{1,0:T(8,128)(2,1)S(1)}, u32[]{:S(2)}, u32[]{:S(2)}) collective-permute-start(bf16[192,384]{1,0:T(8,128)(2,1)} %get-tuple-element.179), channel_id=1, source_target_pairs={{0,8},{8,0},{16,24},{24,16},{1,9},{9,1},{17,25},{25,17},{2,10},{10... | collective-permute-start | bytes 442376 | tf_op jit(solution)/shard_map/ppermute | solution.py:52
  205.3 5.2 %collective-permute-start.30 = (bf16[192,384]{1,0:T(8,128)(2,1)S(1)}, bf16[192,384]{1,0:T(8,128)(2,1)S(1)}, u32[]{:S(2)}, u32[]{:S(2)}) collective-permute-start(bf16[192,384]{1,0:T(8,128)(2,1)S(1)} %add_convert_fusion.6), channel_id=1, source_target_pairs={{0,16},{8,24},{16,0},{24,8},{1,17},{9,25},{17,1},{25,9},{2,18},{10... | collective-permute-start | bytes 442376 | tf_op jit(solution)/shard_map/ppermute | solution.py:52
  (10 other events, 34.7 us)
Sparse Core Ops, SparseCore 0:
  66.5 46.1 all-gather.6
  120.1 48.5 all-gather.4

commit v7 on v6

--- a/solution.py
+++ b/solution.py
@@ -78,13 +78,22 @@
     return (left.astype(FULL) + right.astype(FULL)).astype(dtype)
 
 
-def scatter_terms(items):
-    bit = 1
+def scatter_near(items):
+    taken = [swap(item, "dp", 1) for item in items[1::2]]
+    return [add(kept, got) for kept, got in zip(items[0::2], taken)]
+
+
+def scatter_far(items):
+    bit = 2
     while len(items) > 2:
         taken = [swap(item, "dp", bit) for item in items[1::2]]
         items = [add(kept, got) for kept, got in zip(items[0::2], taken)]
         bit = bit * 2
     return items[0], swap(items[1], "dp", bit)
+
+
+def scatter_terms(items):
+    return scatter_far(scatter_near(items))
 
 
 def sum_steps():
@@ -404,7 +413,7 @@
 
 def backward_kernel(
     places, rank_slots, tokens_ref, gain_ref, router_t_ref, hits_ref, mask_ref,
-    up_ref, hidden_ref, chance_ref, heads_ref, weights_ref, onehot_ref, token_ref, *rest
+    up_ref, hidden_ref, chance_ref, heads_ref, weights_ref, onehot_ref, *rest
 ):
     count = len(places)
     piece_refs, rest = rest[:count], rest[count:]
@@ -483,22 +492,25 @@
 
 
 def product_kernel(
-    dps, normed_ref, attended_ref, hidden_ref, chance_ref, hits_ref, mask_ref, factors_ref,
-    returned_ref, output_ref, *rest
+    normed_far_ref, normed_near_ref, attended_far_ref, attended_near_ref, hidden_ref, chance_ref,
+    hits_ref, mask_ref, factors_ref, returned_ref, token_ref, output_ref, *rest
 ):
     piece_refs, total_ref = rest[:-1], rest[-1]
     ranks, columns, length = factors_ref.shape
     cols = columns // 4
     first, second = None, None
-    for e in range(ranks):
-        held = factors_ref[e].astype(FULL)
-        part = dot(held[: 3 * cols].astype(LOW), normed_ref[e])
+    for j in range(ranks):
+        held = factors_ref[lax.axis_index("expert") ^ j].astype(FULL)
+        normed_ref, attended_ref = (
+            (normed_near_ref, attended_near_ref) if j % 2 else (normed_far_ref, attended_far_ref)
+        )
+        part = dot(held[: 3 * cols].astype(LOW), normed_ref[j // 2])
         first = part if first is None else first + part
-        part = dot(held[3 * cols :].astype(LOW), attended_ref[e])
+        part = dot(held[3 * cols :].astype(LOW), attended_ref[j // 2])
         second = part if second is None else second + part
     total = jnp.concatenate([first, second], axis=0).T
     rows = piece_refs[0].shape[0]
-    for j in range(dps):
+    for j in range(len(piece_refs)):
         total_ref[j] = total[j * rows : (j + 1) * rows]
     for j, ref in enumerate(piece_refs):
         ref[...] = total_ref[lax.axis_index("dp") ^ j].astype(LOW)
@@ -590,8 +602,7 @@
     early = (normed_low, hits, mask, mask_t, bias_full)
     pieces, places, early = gather_pieces(payload, early)
     normed_low, hits, mask, mask_t, bias_full = early
-    pieces, normed_later, up_slabs = together(pieces, normed_low, up_slabs)
-    normed_all = lax.all_gather(normed_later, "expert", axis=0)
+    pieces, up_slabs = together(pieces, up_slabs)
     up_arrived = exchange(up_slabs).reshape(ranks * slab, model_width)
 
     w_shape = (ranks, inner_width, 4 * columns_here)
@@ -619,10 +630,11 @@
 
     slabs, up_arrived = together(slabs, up_arrived)
     arrived = exchange(slabs).reshape(ranks * slab, model_width)
-    attended_all = lax.all_gather(attended, "expert", axis=0)
     up_pieces = gather_near(gather_far(up_arrived))
-    arrived, up_pieces = together(arrived, up_pieces)
+    arrived, up_pieces, normed_own = together(arrived, up_pieces, normed_low)
     row_far = gather_far(arrived)
+    far = list(range(2, ranks, 2))
+    normed_far = gather_bits(normed_own[None], "expert", far)
     by_expert = (local_experts, packed_rows)
     up_rows, up_act = call(
         upstream_kernel,
@@ -652,7 +664,10 @@
             pltpu.VMEM((*by_expert, 128), LOW),
         ],
     )
+    back, normed_far, attended_own = together(back, normed_far, attended)
     kept, got = scatter_terms(back)
+    normed_near = swap(normed_far, "expert", 1)
+    attended_far = gather_bits(attended_own[None], "expert", far)
     returned = call(
         expert_out_kernel,
         "expert_outputs",
@@ -661,18 +676,13 @@
         [pack_t, w_out, activated],
         scratch=[pltpu.VMEM((*by_expert, model_width), LOW)],
     )
+    returned = scatter_near(returned)
     got, returned = together(got, returned)
     back = add(kept, got).reshape(ranks, slab, model_width)
-    back, activated, returned = together(back, activated, returned)
     back = exchange(back)
-    first_grad, second_grad, token = call(
-        expert_grad_kernel,
-        "expert_gradients",
-        8,
-        [shaped(FULL, *w_in.shape), shaped(FULL, *w_out.shape), shaped(FULL, 8, 128)],
-        [slot_rows, activated, pre_grad, gates, up_rows],
-    )
-    returned = add(*scatter_terms(returned)).reshape(ranks, slab, model_width)
+    returned, attended_far = together(returned, attended_far)
+    attended_near = swap(attended_far, "expert", 1)
+    returned = add(*scatter_far(returned)).reshape(ranks, slab, model_width)
     back, returned = together(back, returned)
     returned = exchange(returned)
 
@@ -699,7 +709,6 @@
             heads,
             weights,
             jnp.asarray(bucket_onehot(bucket_count, length), FULL),
-            token,
         ],
         pieces,
         [
@@ -712,24 +721,43 @@
         [back],
     )
 
-    factors, small, returned = together(factors, small, returned)
+    factors, small, returned, activated = together(factors, small, returned, activated)
     factors = exchange(factors)
+    first_grad, second_grad, token = call(
+        expert_grad_kernel,
+        "expert_gradients",
+        8,
+        [shaped(FULL, *w_in.shape), shaped(FULL, *w_out.shape), shaped(FULL, 8, 128)],
+        [slot_rows, activated, pre_grad, gates, up_rows],
+    )
     *steps, one_but_last, last = sum_steps()
     for axis, bit in steps:
         small = small + swap(small, axis, bit)
-    factors, small = together(factors, small)
+    factors, small, token = together(factors, small, token)
     small = small + swap(small, *one_but_last)
     output, *grads = call(
-        functools.partial(product_kernel, dps),
+        product_kernel,
         "weight_gradients",
         5,
         [shaped(LOW, length, model_width)] + [shaped(LOW, rows_here, 4 * columns_here)] * dps,
-        [normed_all, attended_all, hidden, chance, hits, mask, factors, returned],
+        [
+            normed_far,
+            normed_near,
+            attended_far,
+            attended_near,
+            hidden,
+            chance,
+            hits,
+            mask,
+            factors,
+            returned,
+            token,
+        ],
         scratch=[pltpu.VMEM((dps, rows_here, 4 * columns_here), FULL)],
     )
-    grads, small = together(grads, small)
+    grads, small = together(scatter_near(grads), small)
     small = small + swap(small, *last)
-    grads = add(*scatter_terms(grads), FULL)
+    grads = add(*scatter_far(grads), FULL)
     g_query, g_key, g_value, g_output = (
         grads[:, i * columns_here : (i + 1) * columns_here] for i in range(4)
     )

time: 220 us -> 236 us (1.073)
  starting transfers between devices: 47.8 us -> 64.1 us
  waiting for transfers between devices: 84.9 us -> 98.4 us
  between operations: 14.3 us -> 1.15 us
    ppermute x31 -> x39, waiting for transfers between devices: 55.8 us -> 84.7 us  [swap(): return lax.ppermute(value, axis, [(i, i ^ mask) for i in range(count)])]
    all_to_all x5, waiting for transfers between devices: 29 us -> 13.7 us  [exchange(): lax.all_to_all(value, 'expert', split_axis=0, concat_axis=0, tiled=True)]
    ppermute x31 -> x39, starting transfers between devices: 22.2 us -> 36.8 us  [swap(): return lax.ppermute(value, axis, [(i, i ^ mask) for i in range(count)])]
  transfers between devices with their start and end apart: 38 -> 44, of which waited for: 22 -> 18; matrix products, arithmetic and copies ran while one was open for 4% -> 3% of each run, Pallas kernels for 26% -> 18%
where the time goes in v7:
time: 236 us; the launch traced here: 235 us
  waiting for transfers between devices  98.4 us (42%)
  starting transfers between devices  64.1 us (27%)
  Pallas kernels  56.8 us (24%)
  local copies, waits for them, and re-layouts  7.61 us (3%)
  other arithmetic  6.73 us (3%)
    ppermute x39, waiting for transfers between devices, swap(): return lax.ppermute(value, axis, [(i, i ^ mask) for i in range(count)])  84.7 us
    pallas_call x8, Pallas kernels, call(): pl.pallas_call(kernel, out_shape=tuple(out_shape), in_specs=[VMEM] * len(...  56.8 us
    ppermute x39, starting transfers between devices, swap(): return lax.ppermute(value, axis, [(i, i ^ mask) for i in range(count)])  36.8 us
    all_to_all x5, starting transfers between devices, exchange(): lax.all_to_all(value, 'expert', split_axis=0, concat_axis=0, tiled=True)  27.3 us
    all_to_all x5, waiting for transfers between devices, exchange(): lax.all_to_all(value, 'expert', split_axis=0, concat_axis=0, tiled=True)  13.7 us
  transfers between devices with their start and end apart: 44, of which 18 were waited for; matrix products, arithmetic and copies ran while one was open for 3% of the time, Pallas kernels for 18%

profile of v7, /device:TPU:0, one launch (start us, length us, event | category | flops | bytes accessed | tf_op | source)
XLA Modules:
  0.0 234.8 jit_solution(14123694967821072194)
XLA Ops:
  1.7 3.1 %collective-permute-start = (bf16[1,192,384]{2,1,0:T(8,128)(2,1)S(1)}, bf16[1,192,384]{2,1,0:T(8,128)(2,1)S(1)}, u32[]{:S(2)}, u32[]{:S(2)}) collective-permute-start(bf16[1,192,384]{2,1,0:T(8,128)(2,1)S(1)} %maximum_bitcast_fusion), channel_id=1, source_target_pairs={{0,2},{1,3},{2,0},{3,1},{4,6},{5,7},{6,4},{7,5},{8,10},{9,11},{10,... | collective-permute-start | bytes 442376 | tf_op jit(solution)/shard_map/ppermute | solution.py:52
  4.7 2.6 %collective-permute-start.1 = (bf16[1,192,384]{2,1,0:T(8,128)(2,1)S(1)}, bf16[1,192,384]{2,1,0:T(8,128)(2,1)S(1)}, u32[]{:S(2)}, u32[]{:S(2)}) collective-permute-start(bf16[1,192,384]{2,1,0:T(8,128)(2,1)S(1)} %maximum_bitcast_fusion), channel_id=1, source_target_pairs={{0,4},{1,5},{2,6},{3,7},{4,0},{5,1},{6,2},{7,3},{8,12},{9,13},{10,... | collective-permute-start | bytes 442376 | tf_op jit(solution)/shard_map/ppermute | solution.py:52
  9.3 3.4 %early.1 = (bf16[128,768]{1,0:T(8,128)(2,1)}, f32[128,16]{1,0:T(8,128)}, bf16[128,192]{1,0:T(8,128)(2,1)}, bf16[192,128]{1,0:T(8,128)(2,1)}, f32[12,128,128]{2,1,0:T(8,128)}, /*index=5*/bf16[8,24,768]{2,1,0:T(8,128)(2,1)}) custom-call(bf16[128,768]{1,0:T(8,128)(2,1)} %tokens_ref.5, s32[1,128]{1,0:T(1,128)} %bitcast.36, ...), custom_call_target="tpu_custom_call" | custom-call | bytes 10800000 | tf_op jit(solution)/shard_map/early/pallas_call | solution.py:532
  12.7 6.1 %collective-permute-done.1 = bf16[1,192,384]{2,1,0:T(8,128)(2,1)S(1)} collective-permute-done((bf16[1,192,384]{2,1,0:T(8,128)(2,1)S(1)}, bf16[1,192,384]{2,1,0:T(8,128)(2,1)S(1)}, u32[]{:S(2)}, u32[]{:S(2)}) %collective-permute-start.1) | collective-permute-done | bytes 147488 | tf_op jit(solution)/shard_map/ppermute | solution.py:52
  18.9 1.6 collective-permute-start.7
  20.5 1.5 collective-permute-start.3
  22.0 3.7 %collective-permute-done.7 = bf16[1,4,96,384]{3,2,1,0:T(8,128)(2,1)S(1)} collective-permute-done((bf16[1,4,96,384]{3,2,1,0:T(8,128)(2,1)S(1)}, bf16[1,4,96,384]{3,2,1,0:T(8,128)(2,1)S(1)}, u32[]{:S(2)}, u32[]{:S(2)}) %collective-permute-start.7) | collective-permute-done | bytes 294944 | tf_op jit(solution)/shard_map/ppermute | solution.py:52
  25.8 1.6 collective-permute-start.9
  27.3 2.5 %collective-permute-done.3 = bf16[1,4,96,384]{3,2,1,0:T(8,128)(2,1)S(1)} collective-permute-done((bf16[1,4,96,384]{3,2,1,0:T(8,128)(2,1)S(1)}, bf16[1,4,96,384]{3,2,1,0:T(8,128)(2,1)S(1)}, u32[]{:S(2)}, u32[]{:S(2)}) %collective-permute-start.3) | collective-permute-done | bytes 294944 | tf_op jit(solution)/shard_map/ppermute | solution.py:52
  30.6 9.3 %collective-permute-done.9.rest_6_ = bf16[2,4,96,384]{3,2,1,0:T(8,128)(2,1)S(1)} collective-permute-done((bf16[2,4,96,384]{3,2,1,0:T(8,128)(2,1)S(1)}, bf16[2,4,96,384]{3,2,1,0:T(8,128)(2,1)S(1)}, u32[]{:S(2)}, u32[]{:S(2)}) %collective-permute-start.9) | collective-permute-done | bytes 589856 | tf_op jit(solution)/shard_map/ppermute | solution.py:52
  40.4 1.5 collective-permute-done.10.rest_7_
  43.5 6.3 %all-to-all-start = ((bf16[8,24,768]{2,1,0:T(8,128)(2,1)}), bf16[8,24,768]{2,1,0:T(8,128)(2,1)S(1)}, u32[]{:S(2)}, u32[]{:S(2)}) async-start(bf16[8,24,768]{2,1,0:T(8,128)(2,1)} %get-tuple-element.119), calls=%async_computation | async-start | bytes 589824 | tf_op jit(solution)/shard_map/all_to_all | solution.py:60
  49.9 9.9 %attention_forward.1 = (bf16[3,768,128]{2,1,0:T(8,128)(2,1)}, f32[12,128,128]{2,1,0:T(8,128)}, bf16[128,768]{1,0:T(8,128)(2,1)}, f32[128,768]{1,0:T(8,128)}, f32...) custom-call(bf16[128,768]{1,0:T(8,128)(2,1)} %tokens_ref.5, bf16[128,768]{1,0:T(8,128)(2,1)} %get-tuple-element.135.normed_ref, ...), custom_call_target="tpu_custom_call" | custom-call | bytes 36000000 | tf_op jit(solution)/shard_map/attention_forward/pallas_call | solution.py:532
  59.8 1.0 collective-permute-start.12
  60.9 6.0 %all-to-all-start.1 = ((bf16[8,24,768]{2,1,0:T(8,128)(2,1)}), bf16[8,24,768]{2,1,0:T(8,128)(2,1)S(1)}, u32[]{:S(2)}, u32[]{:S(2)}) async-start(bf16[8,24,768]{2,1,0:T(8,128)(2,1)} %get-tuple-element.120), calls=%async_computation.1 | async-start | bytes 589824 | tf_op jit(solution)/shard_map/all_to_all | solution.py:60
  66.9 1.8 collective-permute-done.12.rest_2_
  68.7 7.2 %all-to-all-done.1 = bf16[8,24,768]{2,1,0:T(8,128)(2,1)S(1)} async-done(((bf16[8,24,768]{2,1,0:T(8,128)(2,1)}), bf16[8,24,768]{2,1,0:T(8,128)(2,1)S(1)}, u32[]{:S(2)}, u32[]{:S(2)}) %all-to-all-start.1) | async-done | bytes 294944 | tf_op jit(solution)/shard_map/all_to_all | solution.py:60
  75.9 1.1 collective-permute-start.14
  77.0 1.1 collective-permute-start.17
  78.8 2.6 %collective-permute-start.19 = (bf16[1,128,768]{2,1,0:T(8,128)(2,1)S(1)}, bf16[1,128,768]{2,1,0:T(8,128)(2,1)S(1)}, u32[]{:S(2)}, u32[]{:S(2)}) collective-permute-start(bf16[1,128,768]{2,1,0:T(8,128)(2,1)S(1)} %bitcast.27), channel_id=1, source_target_pairs={{0,6},{1,7},{2,4},{3,5},{4,2},{5,3},{6,0},{7,1},{8,14},{9,15},{10,... | collective-permute-start | bytes 589832 | tf_op jit(solution)/shard_map/ppermute | solution.py:52
  81.4 4.5 %upstream_rows.1 = (bf16[2,320,768]{2,1,0:T(8,128)(2,1)}, f32[2,320,768]{2,1,0:T(8,128)}) custom-call(bf16[160,192]{1,0:T(8,128)(2,1)} %constant.8.clone.pack_ref, bf16[2,768,768]{2,1,0:T(8,128)(2,1)} %w_out_ref.3, bf16[192,768]{1,0:T(8,128)(2,1)} %bitcast.24, bf16[192,768]{1,0:T(8,128)(2,1)} %copy-done.19, bf16[192,768]{1,0:T(8,128)(2,1)} %copy-done.18, ...), custom_call_target="tpu_custom_call" | custom-call | bytes 18000000 | tf_op jit(solution)/shard_map/upstream_rows/pallas_call | solution.py:532
  86.5 6.6 %collective-permute-done.18 = bf16[1,128,768]{2,1,0:T(8,128)(2,1)S(1)} collective-permute-done((bf16[1,128,768]{2,1,0:T(8,128)(2,1)S(1)}, bf16[1,128,768]{2,1,0:T(8,128)(2,1)S(1)}, u32[]{:S(2)}, u32[]{:S(2)}) %collective-permute-start.18) | collective-permute-done | bytes 196640 | tf_op jit(solution)/shard_map/ppermute | solution.py:52
  94.7 9.9 %experts.1 = (bf16[192,768]{1,0:T(8,128)(2,1)}, bf16[192,768]{1,0:T(8,128)(2,1)}, bf16[192,768]{1,0:T(8,128)(2,1)}, bf16[192,768]{1,0:T(8,128)(2,1)}, bf16[2,320...) custom-call(bf16[160,192]{1,0:T(8,128)(2,1)} %constant.8.clone.pack_re, ...), custom_call_target="tpu_custom_call" | custom-call | bytes 36000000 | tf_op jit(solution)/shard_map/experts/pallas_call | solution.py:532
  104.7 2.7 %collective-permute-start.25 = (bf16[1,128,768]{2,1,0:T(8,128)(2,1)S(1)}, bf16[1,128,768]{2,1,0:T(8,128)(2,1)S(1)}, u32[]{:S(2)}, u32[]{:S(2)}) collective-permute-start(bf16[1,128,768]{2,1,0:T(8,128)(2,1)S(1)} %bitcast.29), channel_id=1, source_target_pairs={{0,2},{1,3},{2,0},{3,1},{4,6},{5,7},{6,4},{7,5},{8,10},{9,11},{10,... | collective-permute-start | bytes 589832 | tf_op jit(solution)/shard_map/ppermute | solution.py:52
  108.4 1.4 collective-permute-start.27
  109.8 4.0 %expert_outputs.1 = (bf16[192,768]{1,0:T(8,128)(2,1)}, bf16[192,768]{1,0:T(8,128)(2,1)}, bf16[192,768]{1,0:T(8,128)(2,1)}, bf16[192,768]{1,0:T(8,128)(2,1)}) custom-call(bf16[192,160]{1,0:T(8,128)(2,1)} %constant.9.clone.pack_t_ref, bf16[2,768,768]{2,1,0:T(8,128)(2,1)} %w_out_ref.3, bf16[2,320,768]{2,1,0:T(8,128)(2,1)} %get-tuple-element.166.act_ref), custom_call_target="tpu_custom_call" | custom-call | bytes 10800000 | tf_op jit(solution)/shard_map/expert_outputs/pallas_call | solution.py:532
  114.6 8.6 %collective-permute-done.26 = bf16[1,128,768]{2,1,0:T(8,128)(2,1)S(1)} collective-permute-done((bf16[1,128,768]{2,1,0:T(8,128)(2,1)S(1)}, bf16[1,128,768]{2,1,0:T(8,128)(2,1)S(1)}, u32[]{:S(2)}, u32[]{:S(2)}) %collective-permute-start.26) | collective-permute-done | bytes 196640 | tf_op jit(solution)/shard_map/ppermute | solution.py:52
  123.3 1.0 collective-permute-start.22
  124.6 8.3 %collective-permute-done.22 = bf16[192,768]{1,0:T(8,128)(2,1)S(1)} collective-permute-done((bf16[192,768]{1,0:T(8,128)(2,1)S(1)}, bf16[192,768]{1,0:T(8,128)(2,1)S(1)}, u32[]{:S(2)}, u32[]{:S(2)}) %collective-permute-start.22) | collective-permute-done | bytes 294944 | tf_op jit(solution)/shard_map/ppermute | solution.py:52
  134.6 5.6 %all-to-all-start.2 = ((bf16[8,24,768]{2,1,0:T(8,128)(2,1)}), bf16[8,24,768]{2,1,0:T(8,128)(2,1)S(1)}, u32[]{:S(2)}, u32[]{:S(2)}) async-start(bf16[8,24,768]{2,1,0:T(8,128)(2,1)} %bitcast.10), calls=%async_computation.2 | async-start | bytes 589824 | tf_op jit(solution)/shard_map/all_to_all | solution.py:60
  140.3 1.2 collective-permute-done.30
  142.2 6.5 %all-to-all-done.2.rest_8_ = bf16[8,24,768]{2,1,0:T(8,128)(2,1)S(1)} async-done(((bf16[8,24,768]{2,1,0:T(8,128)(2,1)}), bf16[8,24,768]{2,1,0:T(8,128)(2,1)S(1)}, u32[]{:S(2)}, u32[]{:S(2)}) %all-to-all-start.2) | async-done | bytes 294944 | tf_op jit(solution)/shard_map/all_to_all | solution.py:60
  148.7 3.4 %all-to-all-start.3 = ((bf16[8,24,768]{2,1,0:T(8,128)(2,1)}), bf16[8,24,768]{2,1,0:T(8,128)(2,1)S(1)}, u32[]{:S(2)}, u32[]{:S(2)}) async-start(bf16[8,24,768]{2,1,0:T(8,128)(2,1)} %bitcast.11), calls=%async_computation.3 | async-start | bytes 589824 | tf_op jit(solution)/shard_map/all_to_all | solution.py:60
  152.2 12.0 %attention_backward.1 = (f32[128,768]{1,0:T(8,128)}, f32[24,768]{1,0:T(8,128)}, bf16[8,384,128]{2,1,0:T(8,128)(2,1)}) custom-call(bf16[128,768]{1,0:T(8,128)(2,1)} %tokens_ref.5, f32[2,768]{1,0:T(2,128)} %maximum_convert_fusion.gain_ref, bf16[16,768]{1,0:T(8,128)(2,1)} %bitcast.34, f32[128,16]{1,0:T(8,128)} %get-tuple-element.106.hits_ref, ...), custom_call_target="tpu_custom_call" | custom-call | bytes 43200000 | tf_op jit(solution)/shard_map/attention_backward/pallas_call | solution.py:532
  164.2 5.9 %all-to-all-start.4 = ((bf16[8,384,128]{2,1,0:T(8,128)(2,1)}), bf16[8,384,128]{2,1,0:T(8,128)(2,1)S(1)}, u32[]{:S(2)}, u32[]{:S(2)}) async-start(bf16[8,384,128]{2,1,0:T(8,128)(2,1)} %get-tuple-element.163), calls=%async_computation.4 | async-start | bytes 1572864 | tf_op jit(solution)/shard_map/all_to_all | solution.py:60
  170.1 2.0 collective-permute-start.20
  172.2 1.5 collective-permute-done.31
  174.6 1.1 collective-permute-start.32
  175.7 3.3 %collective-permute-done.32 = f32[24,768]{1,0:T(8,128)S(1)} collective-permute-done((f32[24,768]{1,0:T(8,128)S(1)}, f32[24,768]{1,0:T(8,128)S(1)}, u32[]{:S(2)}, u32[]{:S(2)}) %collective-permute-start.32) | collective-permute-done | bytes 73760 | tf_op jit(solution)/shard_map/ppermute | solution.py:52
  179.0 2.0 collective-permute-start.33
  181.0 8.2 %expert_gradients.1 = (f32[2,768,768]{2,1,0:T(8,128)}, f32[2,768,768]{2,1,0:T(8,128)}, f32[8,128]{1,0:T(8,128)}) custom-call(bf16[2,320,768]{2,1,0:T(8,128)(2,1)} %get-tuple-element.165.rows_ref, bf16[2,320,768]{2,1,0:T(8,128)(2,1)} %get-tuple-element.166.act_ref, bf16[2,320,768]{2,1,0:T(8,128)(2,1)} %get-tuple-element.167.pre_grad_ref, ...), custom_call_target="tpu_custom_call" | custom-call | bytes 28800000 | tf_op jit(solution)/shard_map/expert_gradients/pallas_call | solution.py:532
  189.2 23.6 %collective-permute-done.33 = f32[24,768]{1,0:T(8,128)S(1)} collective-permute-done((f32[24,768]{1,0:T(8,128)S(1)}, f32[24,768]{1,0:T(8,128)S(1)}, u32[]{:S(2)}, u32[]{:S(2)}) %collective-permute-start.33) | collective-permute-done | bytes 73760 | tf_op jit(solution)/shard_map/ppermute | solution.py:52
  214.0 4.9 %weight_gradients.1 = (bf16[128,768]{1,0:T(8,128)(2,1)}, bf16[192,384]{1,0:T(8,128)(2,1)}, bf16[192,384]{1,0:T(8,128)(2,1)}, bf16[192,384]{1,0:T(8,128)(2,1)}, bf16[192,384]{1,0:T(8,128)(2,1)}) custom-call(bf16[4,128,768]{2,1,0:T(8,128)(2,1)} %copy-done.2, bf16[4,128,768]{2,1,0:T(8,128)(2,1)} %copy-done.16, bf16[4,128,768]{2,1,0:T(8,128)(2,1)} %copy-done.3, ...), custom_call_target="tpu_custom_call" | custom-call | bytes 18000000 | tf_op jit(solution)/shard_map/weight_gradients/pallas_call | solution.py:532
  218.9 1.5 collective-permute-start.36
  220.6 3.0 %collective-permute-done.36 = f32[24,768]{1,0:T(8,128)S(1)} collective-permute-done((f32[24,768]{1,0:T(8,128)S(1)}, f32[24,768]{1,0:T(8,128)S(1)}, u32[]{:S(2)}, u32[]{:S(2)}) %collective-permute-start.36) | collective-permute-done | bytes 73760 | tf_op jit(solution)/shard_map/ppermute | solution.py:52
  225.5 2.4 %collective-permute-start.37 = (f32[24,768]{1,0:T(8,128)S(1)}, f32[24,768]{1,0:T(8,128)S(1)}, u32[]{:S(2)}, u32[]{:S(2)}) collective-permute-start(f32[24,768]{1,0:T(8,128)S(1)} %add.53), channel_id=1, source_target_pairs={{0,4},{1,5},{2,6},{3,7},{4,0},{5,1},{6,2},{7,3},{8,12},{9,13},{10,... | collective-permute-start | bytes 221192 | tf_op jit(solution)/shard_map/ppermute | solution.py:52
  228.0 1.0 collective-permute-start.38
  229.0 3.0 %collective-permute-done.37 = f32[24,768]{1,0:T(8,128)S(1)} collective-permute-done((f32[24,768]{1,0:T(8,128)S(1)}, f32[24,768]{1,0:T(8,128)S(1)}, u32[]{:S(2)}, u32[]{:S(2)}) %collective-permute-start.37) | collective-permute-done | bytes 73760 | tf_op jit(solution)/shard_map/ppermute | solution.py:52
  (135 shorter events, 20.5 us)
Async XLA Ops:
  1.7 11.0 %collective-permute-start = (bf16[1,192,384]{2,1,0:T(8,128)(2,1)S(1)}, bf16[1,192,384]{2,1,0:T(8,128)(2,1)S(1)}, u32[]{:S(2)}, u32[]{:S(2)}) collective-permute-start(bf16[1,192,384]{2,1,0:T(8,128)(2,1)S(1)} %maximum_bitcast_fusion), channel_id=1, source_target_pairs={{0,2},{1,3},{2,0},{3,1},{4,6},{5,7},{6,4},{7,5},{8,10},{9,11},{10,... | collective-permute-start | bytes 442376 | tf_op jit(solution)/shard_map/ppermute | solution.py:52
  4.7 14.0 %collective-permute-start.1 = (bf16[1,192,384]{2,1,0:T(8,128)(2,1)S(1)}, bf16[1,192,384]{2,1,0:T(8,128)(2,1)S(1)}, u32[]{:S(2)}, u32[]{:S(2)}) collective-permute-start(bf16[1,192,384]{2,1,0:T(8,128)(2,1)S(1)} %maximum_bitcast_fusion), channel_id=1, source_target_pairs={{0,4},{1,5},{2,6},{3,7},{4,0},{5,1},{6,2},{7,3},{8,12},{9,13},{10,... | collective-permute-start | bytes 442376 | tf_op jit(solution)/shard_map/ppermute | solution.py:52
  7.3 11.4 %collective-permute-start.2 = (bf16[1,192,384]{2,1,0:T(8,128)(2,1)S(1)}, bf16[1,192,384]{2,1,0:T(8,128)(2,1)S(1)}, u32[]{:S(2)}, u32[]{:S(2)}) collective-permute-start(bf16[1,192,384]{2,1,0:T(8,128)(2,1)S(1)} %maximum_bitcast_fusion), channel_id=1, source_target_pairs={{0,6},{1,7},{2,4},{3,5},{4,2},{5,3},{6,0},{7,1},{8,14},{9,15},{10,... | collective-permute-start | bytes 442376 | tf_op jit(solution)/shard_map/ppermute | solution.py:52
  18.9 6.8 %collective-permute-start.7 = (bf16[1,4,96,384]{3,2,1,0:T(8,128)(2,1)S(1)}, bf16[1,4,96,384]{3,2,1,0:T(8,128)(2,1)S(1)}, u32[]{:S(2)}, u32[]{:S(2)}) collective-permute-start(bf16[1,4,96,384]{3,2,1,0:T(8,128)(2,1)S(1)} %get-tuple-element.188), channel_id=1, source_target_pairs={{0,16},{8,24},{16,0},{24,8},{1,17},{9,25},{17,1},{25,9},{2,18},{10... | collective-permute-start | bytes 884744 | tf_op jit(solution)/shard_map/ppermute | solution.py:52
  20.5 9.3 %collective-permute-start.3 = (bf16[1,4,96,384]{3,2,1,0:T(8,128)(2,1)S(1)}, bf16[1,4,96,384]{3,2,1,0:T(8,128)(2,1)S(1)}, u32[]{:S(2)}, u32[]{:S(2)}) collective-permute-start(bf16[1,4,96,384]{3,2,1,0:T(8,128)(2,1)S(1)} %get-tuple-element.189), channel_id=1, source_target_pairs={{0,1},{1,0},{2,3},{3,2},{4,5},{5,4},{6,7},{7,6},{8,9},{9,8},{10,11... | collective-permute-start | bytes 884744 | tf_op jit(solution)/shard_map/ppermute | solution.py:52
  25.8 14.1 %collective-permute-start.9 = (bf16[2,4,96,384]{3,2,1,0:T(8,128)(2,1)S(1)}, bf16[2,4,96,384]{3,2,1,0:T(8,128)(2,1)S(1)}, u32[]{:S(2)}, u32[]{:S(2)}) collective-permute-start(bf16[2,4,96,384]{3,2,1,0:T(8,128)(2,1)S(1)} %pad_maximum_fusion.4.rest_4_), channel_id=1, source_target_pairs={{0,1},{1,0},{2,3},{3,2},{4,5},{5,4},{6,7},{7,6},{8,9},{9,8},{10,11... | collective-permute-start | bytes 1769480 | tf_op jit(solution)/shard_map/ppermute | solution.py:52
  29.9 9.9 %collective-permute-start.5 = (bf16[2,4,96,384]{3,2,1,0:T(8,128)(2,1)S(1)}, bf16[2,4,96,384]{3,2,1,0:T(8,128)(2,1)S(1)}, u32[]{:S(2)}, u32[]{:S(2)}) collective-permute-start(bf16[2,4,96,384]{3,2,1,0:T(8,128)(2,1)S(1)} %pad_maximum_fusion.3.rest_0_), channel_id=1, source_target_pairs={{0,16},{8,24},{16,0},{24,8},{1,17},{9,25},{17,1},{25,9},{2,18},{10... | collective-permute-start | bytes 1769480 | tf_op jit(solution)/shard_map/ppermute | solution.py:52
  30.0 10.4 %collective-permute-start.8 = (bf16[2,4,96,384]{3,2,1,0:T(8,128)(2,1)S(1)}, bf16[2,4,96,384]{3,2,1,0:T(8,128)(2,1)S(1)}, u32[]{:S(2)}, u32[]{:S(2)}) collective-permute-start(bf16[2,4,96,384]{3,2,1,0:T(8,128)(2,1)S(1)} %pad_maximum_fusion.4.rest_4_), channel_id=1, source_target_pairs={{0,8},{8,0},{16,24},{24,16},{1,9},{9,1},{17,25},{25,17},{2,10},{10... | collective-permute-start | bytes 1769480 | tf_op jit(solution)/shard_map/ppermute | solution.py:52
  30.1 10.3 %collective-permute-start.4 = (bf16[2,4,96,384]{3,2,1,0:T(8,128)(2,1)S(1)}, bf16[2,4,96,384]{3,2,1,0:T(8,128)(2,1)S(1)}, u32[]{:S(2)}, u32[]{:S(2)}) collective-permute-start(bf16[2,4,96,384]{3,2,1,0:T(8,128)(2,1)S(1)} %pad_maximum_fusion.3.rest_0_), channel_id=1, source_target_pairs={{0,8},{8,0},{16,24},{24,16},{1,9},{9,1},{17,25},{25,17},{2,10},{10... | collective-permute-start | bytes 1769480 | tf_op jit(solution)/shard_map/ppermute | solution.py:52
  39.9 2.0 collective-permute-start.10
  39.9 2.8 %collective-permute-start.6 = (bf16[2,4,96,384]{3,2,1,0:T(8,128)(2,1)S(1)}, bf16[2,4,96,384]{3,2,1,0:T(8,128)(2,1)S(1)}, u32[]{:S(2)}, u32[]{:S(2)}) collective-permute-start(bf16[2,4,96,384]{3,2,1,0:T(8,128)(2,1)S(1)} %collective-permute-done.5.rest_2_), channel_id=1, source_target_pairs={{0,8},{8,0},{16,24},{24,16},{1,9},{9,1},{17,25},{25,17},{2,10},{10... | collective-permute-start | bytes 1769480 | tf_op jit(solution)/shard_map/ppermute | solution.py:52
  43.5 16.3 %all-to-all-start = ((bf16[8,24,768]{2,1,0:T(8,128)(2,1)}), bf16[8,24,768]{2,1,0:T(8,128)(2,1)S(1)}, u32[]{:S(2)}, u32[]{:S(2)}) async-start(bf16[8,24,768]{2,1,0:T(8,128)(2,1)} %get-tuple-element.119), calls=%async_computation | async-start | bytes 589824 | tf_op jit(solution)/shard_map/all_to_all | solution.py:60
  49.9 27.1 %copy-start.15 = (bf16[128,768]{1,0:T(8,128)(2,1)S(1)}, bf16[128,768]{1,0:T(8,128)(2,1)}, u32[]{:S(2)}) copy-start(bf16[128,768]{1,0:T(8,128)(2,1)} %get-tuple-element.135.normed_ref) | copy-start | bytes 589828
  59.8 8.8 %collective-permute-start.12 = (bf16[192,768]{1,0:T(8,128)(2,1)S(1)}, bf16[192,768]{1,0:T(8,128)(2,1)S(1)}, u32[]{:S(2)}, u32[]{:S(2)}) collective-permute-start(bf16[192,768]{1,0:T(8,128)(2,1)S(1)} %bitcast.22), channel_id=1, source_target_pairs={{0,16},{8,24},{16,0},{24,8},{1,17},{9,25},{17,1},{25,9},{2,18},{10... | collective-permute-start | bytes 884744 | tf_op jit(solution)/shard_map/ppermute | solution.py:52
  60.9 15.0 %all-to-all-start.1 = ((bf16[8,24,768]{2,1,0:T(8,128)(2,1)}), bf16[8,24,768]{2,1,0:T(8,128)(2,1)S(1)}, u32[]{:S(2)}, u32[]{:S(2)}) async-start(bf16[8,24,768]{2,1,0:T(8,128)(2,1)} %get-tuple-element.120), calls=%async_computation.1 | async-start | bytes 589824 | tf_op jit(solution)/shard_map/all_to_all | solution.py:60
  66.9 1.8 collective-permute-start.11
  68.7 7.2 %collective-permute-start.13 = (bf16[192,768]{1,0:T(8,128)(2,1)S(1)}, bf16[192,768]{1,0:T(8,128)(2,1)S(1)}, u32[]{:S(2)}, u32[]{:S(2)}) collective-permute-start(bf16[192,768]{1,0:T(8,128)(2,1)S(1)} %collective-permute-done.12.rest_2_), channel_id=1, source_target_pairs={{0,8},{8,0},{16,24},{24,16},{1,9},{9,1},{17,25},{25,17},{2,10},{10... | collective-permute-start | bytes 884744 | tf_op jit(solution)/shard_map/ppermute | solution.py:52
  75.9 10.0 %collective-permute-start.14 = (bf16[192,768]{1,0:T(8,128)(2,1)S(1)}, bf16[192,768]{1,0:T(8,128)(2,1)S(1)}, u32[]{:S(2)}, u32[]{:S(2)}) collective-permute-start(bf16[192,768]{1,0:T(8,128)(2,1)S(1)} %bitcast.19), channel_id=1, source_target_pairs={{0,16},{8,24},{16,0},{24,8},{1,17},{9,25},{17,1},{25,9},{2,18},{10... | collective-permute-start | bytes 884744 | tf_op jit(solution)/shard_map/ppermute | solution.py:52
  77.0 9.5 %collective-permute-start.17 = (bf16[1,128,768]{2,1,0:T(8,128)(2,1)S(1)}, bf16[1,128,768]{2,1,0:T(8,128)(2,1)S(1)}, u32[]{:S(2)}, u32[]{:S(2)}) collective-permute-start(bf16[1,128,768]{2,1,0:T(8,128)(2,1)S(1)} %bitcast.25), channel_id=1, source_target_pairs={{0,2},{1,3},{2,0},{3,1},{4,6},{5,7},{6,4},{7,5},{8,10},{9,11},{10,... | collective-permute-start | bytes 589832 | tf_op jit(solution)/shard_map/ppermute | solution.py:52
  78.1 15.0 %collective-permute-start.18 = (bf16[1,128,768]{2,1,0:T(8,128)(2,1)S(1)}, bf16[1,128,768]{2,1,0:T(8,128)(2,1)S(1)}, u32[]{:S(2)}, u32[]{:S(2)}) collective-permute-start(bf16[1,128,768]{2,1,0:T(8,128)(2,1)S(1)} %bitcast.26), channel_id=1, source_target_pairs={{0,4},{1,5},{2,6},{3,7},{4,0},{5,1},{6,2},{7,3},{8,12},{9,13},{10,... | collective-permute-start | bytes 589832 | tf_op jit(solution)/shard_map/ppermute | solution.py:52
  78.8 14.3 %collective-permute-start.19 = (bf16[1,128,768]{2,1,0:T(8,128)(2,1)S(1)}, bf16[1,128,768]{2,1,0:T(8,128)(2,1)S(1)}, u32[]{:S(2)}, u32[]{:S(2)}) collective-permute-start(bf16[1,128,768]{2,1,0:T(8,128)(2,1)S(1)} %bitcast.27), channel_id=1, source_target_pairs={{0,6},{1,7},{2,4},{3,5},{4,2},{5,3},{6,0},{7,1},{8,14},{9,15},{10,... | collective-permute-start | bytes 589832 | tf_op jit(solution)/shard_map/ppermute | solution.py:52
  85.9 7.3 %collective-permute-start.15 = (bf16[192,768]{1,0:T(8,128)(2,1)S(1)}, bf16[192,768]{1,0:T(8,128)(2,1)S(1)}, u32[]{:S(2)}, u32[]{:S(2)}) collective-permute-start(bf16[192,768]{1,0:T(8,128)(2,1)S(1)} %bitcast.20), channel_id=1, source_target_pairs={{0,8},{8,0},{16,24},{24,16},{1,9},{9,1},{17,25},{25,17},{2,10},{10... | collective-permute-start | bytes 884744 | tf_op jit(solution)/shard_map/ppermute | solution.py:52
  86.0 7.3 %collective-permute-start.16 = (bf16[192,768]{1,0:T(8,128)(2,1)S(1)}, bf16[192,768]{1,0:T(8,128)(2,1)S(1)}, u32[]{:S(2)}, u32[]{:S(2)}) collective-permute-start(bf16[192,768]{1,0:T(8,128)(2,1)S(1)} %collective-permute-done.14.rest_2_), channel_id=1, source_target_pairs={{0,8},{8,0},{16,24},{24,16},{1,9},{9,1},{17,25},{25,17},{2,10},{10... | collective-permute-start | bytes 884744 | tf_op jit(solution)/shard_map/ppermute | solution.py:52
  93.2 76.9 %copy-start.2 = (bf16[4,128,768]{2,1,0:T(8,128)(2,1)}, bf16[4,128,768]{2,1,0:T(8,128)(2,1)S(1)}, u32[]{:S(2)}) copy-start(bf16[4,128,768]{2,1,0:T(8,128)(2,1)S(1)} %pad_maximum_fusion.normed_far_ref) | copy-start | bytes 2359300
  104.7 9.8 %collective-permute-start.25 = (bf16[1,128,768]{2,1,0:T(8,128)(2,1)S(1)}, bf16[1,128,768]{2,1,0:T(8,128)(2,1)S(1)}, u32[]{:S(2)}, u32[]{:S(2)}) collective-permute-start(bf16[1,128,768]{2,1,0:T(8,128)(2,1)S(1)} %bitcast.29), channel_id=1, source_target_pairs={{0,2},{1,3},{2,0},{3,1},{4,6},{5,7},{6,4},{7,5},{8,10},{9,11},{10,... | collective-permute-start | bytes 589832 | tf_op jit(solution)/shard_map/ppermute | solution.py:52
  107.4 15.7 %collective-permute-start.26 = (bf16[1,128,768]{2,1,0:T(8,128)(2,1)S(1)}, bf16[1,128,768]{2,1,0:T(8,128)(2,1)S(1)}, u32[]{:S(2)}, u32[]{:S(2)}) collective-permute-start(bf16[1,128,768]{2,1,0:T(8,128)(2,1)S(1)} %bitcast.30), channel_id=1, source_target_pairs={{0,4},{1,5},{2,6},{3,7},{4,0},{5,1},{6,2},{7,3},{8,12},{9,13},{10,... | collective-permute-start | bytes 589832 | tf_op jit(solution)/shard_map/ppermute | solution.py:52
  108.4 14.7 %collective-permute-start.27 = (bf16[1,128,768]{2,1,0:T(8,128)(2,1)S(1)}, bf16[1,128,768]{2,1,0:T(8,128)(2,1)S(1)}, u32[]{:S(2)}, u32[]{:S(2)}) collective-permute-start(bf16[1,128,768]{2,1,0:T(8,128)(2,1)S(1)} %bitcast.31), channel_id=1, source_target_pairs={{0,6},{1,7},{2,4},{3,5},{4,2},{5,3},{6,0},{7,1},{8,14},{9,15},{10,... | collective-permute-start | bytes 589832 | tf_op jit(solution)/shard_map/ppermute | solution.py:52
  109.8 13.4 %collective-permute-start.21 = (bf16[192,768]{1,0:T(8,128)(2,1)}, bf16[192,768]{1,0:T(8,128)(2,1)S(1)}, u32[]{:S(2)}, u32[]{:S(2)}) collective-permute-start(bf16[192,768]{1,0:T(8,128)(2,1)} %get-tuple-element.139), channel_id=1, source_target_pairs={{0,8},{8,0},{16,24},{24,16},{1,9},{9,1},{17,25},{25,17},{2,10},{10... | collective-permute-start | bytes 884744 | tf_op jit(solution)/shard_map/ppermute | solution.py:52
  113.9 10.5 %collective-permute-start.24 = (bf16[192,768]{1,0:T(8,128)(2,1)}, bf16[192,768]{1,0:T(8,128)(2,1)S(1)}, u32[]{:S(2)}, u32[]{:S(2)}) collective-permute-start(bf16[192,768]{1,0:T(8,128)(2,1)} %get-tuple-element.144), channel_id=1, source_target_pairs={{0,8},{8,0},{16,24},{24,16},{1,9},{9,1},{17,25},{25,17},{2,10},{10... | collective-permute-start | bytes 884744 | tf_op jit(solution)/shard_map/ppermute | solution.py:52
  114.5 10.0 %collective-permute-start.23 = (bf16[192,768]{1,0:T(8,128)(2,1)}, bf16[192,768]{1,0:T(8,128)(2,1)S(1)}, u32[]{:S(2)}, u32[]{:S(2)}) collective-permute-start(bf16[192,768]{1,0:T(8,128)(2,1)} %get-tuple-element.142), channel_id=1, source_target_pairs={{0,8},{8,0},{16,24},{24,16},{1,9},{9,1},{17,25},{25,17},{2,10},{10... | collective-permute-start | bytes 884744 | tf_op jit(solution)/shard_map/ppermute | solution.py:52
  123.1 10.7 %collective-permute-start.29 = (bf16[192,768]{1,0:T(8,128)(2,1)S(1)}, bf16[192,768]{1,0:T(8,128)(2,1)S(1)}, u32[]{:S(2)}, u32[]{:S(2)}) collective-permute-start(bf16[192,768]{1,0:T(8,128)(2,1)S(1)} %copy-done.28), channel_id=1, source_target_pairs={{0,8},{8,0},{16,24},{24,16},{1,9},{9,1},{17,25},{25,17},{2,10},{10... | collective-permute-start | bytes 884744 | tf_op jit(solution)/shard_map/ppermute | solution.py:52
  123.2 48.9 %copy-start.3 = (bf16[4,128,768]{2,1,0:T(8,128)(2,1)}, bf16[4,128,768]{2,1,0:T(8,128)(2,1)S(1)}, u32[]{:S(2)}) copy-start(bf16[4,128,768]{2,1,0:T(8,128)(2,1)S(1)} %pad_maximum_fusion.1.attended_far_ref) | copy-start | bytes 2359300
  123.3 9.5 %collective-permute-start.22 = (bf16[192,768]{1,0:T(8,128)(2,1)S(1)}, bf16[192,768]{1,0:T(8,128)(2,1)S(1)}, u32[]{:S(2)}, u32[]{:S(2)}) collective-permute-start(bf16[192,768]{1,0:T(8,128)(2,1)S(1)} %add_convert_fusion.5), channel_id=1, source_target_pairs={{0,16},{8,24},{16,0},{24,8},{1,17},{9,25},{17,1},{25,9},{2,18},{10... | collective-permute-start | bytes 884744 | tf_op jit(solution)/shard_map/ppermute | solution.py:52
  132.8 8.6 %collective-permute-start.30 = (bf16[192,768]{1,0:T(8,128)(2,1)S(1)}, bf16[192,768]{1,0:T(8,128)(2,1)S(1)}, u32[]{:S(2)}, u32[]{:S(2)}) collective-permute-start(bf16[192,768]{1,0:T(8,128)(2,1)S(1)} %add_convert_fusion.3), channel_id=1, source_target_pairs={{0,16},{8,24},{16,0},{24,8},{1,17},{9,25},{17,1},{25,9},{2,18},{10... | collective-permute-start | bytes 884744 | tf_op jit(solution)/shard_map/ppermute | solution.py:52
  134.6 14.1 %all-to-all-start.2 = ((bf16[8,24,768]{2,1,0:T(8,128)(2,1)}), bf16[8,24,768]{2,1,0:T(8,128)(2,1)S(1)}, u32[]{:S(2)}, u32[]{:S(2)}) async-start(bf16[8,24,768]{2,1,0:T(8,128)(2,1)} %bitcast.10), calls=%async_computation.2 | async-start | bytes 589824 | tf_op jit(solution)/shard_map/all_to_all | solution.py:60
  148.7 15.4 %all-to-all-start.3 = ((bf16[8,24,768]{2,1,0:T(8,128)(2,1)}), bf16[8,24,768]{2,1,0:T(8,128)(2,1)S(1)}, u32[]{:S(2)}, u32[]{:S(2)}) async-start(bf16[8,24,768]{2,1,0:T(8,128)(2,1)} %bitcast.11), calls=%async_computation.3 | async-start | bytes 589824 | tf_op jit(solution)/shard_map/all_to_all | solution.py:60
  164.2 25.0 %copy-start.14 = (bf16[8,24,768]{2,1,0:T(8,128)(2,1)}, bf16[8,24,768]{2,1,0:T(8,128)(2,1)S(1)}, u32[]{:S(2)}) copy-start(bf16[8,24,768]{2,1,0:T(8,128)(2,1)S(1)} %all-to-all-done.3.returned_ref) | copy-start | bytes 884740
  164.2 48.6 %all-to-all-start.4 = ((bf16[8,384,128]{2,1,0:T(8,128)(2,1)}), bf16[8,384,128]{2,1,0:T(8,128)(2,1)S(1)}, u32[]{:S(2)}, u32[]{:S(2)}) async-start(bf16[8,384,128]{2,1,0:T(8,128)(2,1)} %get-tuple-element.163), calls=%async_computation.4 | async-start | bytes 1572864 | tf_op jit(solution)/shard_map/all_to_all | solution.py:60
  170.1 42.7 %collective-permute-start.20 = (bf16[4,128,768]{2,1,0:T(8,128)(2,1)S(1)}, bf16[4,128,768]{2,1,0:T(8,128)(2,1)S(1)}, u32[]{:S(2)}, u32[]{:S(2)}) collective-permute-start(bf16[4,128,768]{2,1,0:T(8,128)(2,1)S(1)} %pad_maximum_fusion.normed_far_ref), channel_id=1, source_target_pairs={{0,1},{1,0},{2,3},{3,2},{4,5},{5,4},{6,7},{7,6},{8,9},{9,8},{10,11... | collective-permute-start | bytes 2359304 | tf_op jit(solution)/shard_map/ppermute | solution.py:52
  172.1 40.7 %collective-permute-start.28 = (bf16[4,128,768]{2,1,0:T(8,128)(2,1)S(1)}, bf16[4,128,768]{2,1,0:T(8,128)(2,1)}, u32[]{:S(2)}, u32[]{:S(2)}) collective-permute-start(bf16[4,128,768]{2,1,0:T(8,128)(2,1)S(1)} %pad_maximum_fusion.1.attended_far_ref), channel_id=1, source_target_pairs={{0,1},{1,0},{2,3},{3,2},{4,5},{5,4},{6,7},{7,6},{8,9},{9,8},{10,11... | collective-permute-start | bytes 2359304 | tf_op jit(solution)/shard_map/ppermute | solution.py:52
  172.2 1.5 collective-permute-start.31
  174.6 4.4 %collective-permute-start.32 = (f32[24,768]{1,0:T(8,128)S(1)}, f32[24,768]{1,0:T(8,128)S(1)}, u32[]{:S(2)}, u32[]{:S(2)}) collective-permute-start(f32[24,768]{1,0:T(8,128)S(1)} %add.48), channel_id=1, source_target_pairs={{0,16},{8,24},{16,0},{24,8},{1,17},{9,25},{17,1},{25,9},{2,18},{10... | collective-permute-start | bytes 221192 | tf_op jit(solution)/shard_map/ppermute | solution.py:52
  179.0 33.8 %collective-permute-start.33 = (f32[24,768]{1,0:T(8,128)S(1)}, f32[24,768]{1,0:T(8,128)S(1)}, u32[]{:S(2)}, u32[]{:S(2)}) collective-permute-start(f32[24,768]{1,0:T(8,128)S(1)} %add.49), channel_id=1, source_target_pairs={{0,1},{1,0},{2,3},{3,2},{4,5},{5,4},{6,7},{7,6},{8,9},{9,8},{10,11... | collective-permute-start | bytes 221192 | tf_op jit(solution)/shard_map/ppermute | solution.py:52
  218.9 4.7 %collective-permute-start.35 = (bf16[192,384]{1,0:T(8,128)(2,1)}, bf16[192,384]{1,0:T(8,128)(2,1)S(1)}, u32[]{:S(2)}, u32[]{:S(2)}) collective-permute-start(bf16[192,384]{1,0:T(8,128)(2,1)} %get-tuple-element.179), channel_id=1, source_target_pairs={{0,8},{8,0},{16,24},{24,16},{1,9},{9,1},{17,25},{25,17},{2,10},{10... | collective-permute-start | bytes 442376 | tf_op jit(solution)/shard_map/ppermute | solution.py:52
  218.9 4.7 %collective-permute-start.36 = (f32[24,768]{1,0:T(8,128)S(1)}, f32[24,768]{1,0:T(8,128)S(1)}, u32[]{:S(2)}, u32[]{:S(2)}) collective-permute-start(f32[24,768]{1,0:T(8,128)S(1)} %add.50), channel_id=1, source_target_pairs={{0,2},{1,3},{2,0},{3,1},{4,6},{5,7},{6,4},{7,5},{8,10},{9,11},{10,... | collective-permute-start | bytes 221192 | tf_op jit(solution)/shard_map/ppermute | solution.py:52
  220.4 4.1 %collective-permute-start.34 = (bf16[192,384]{1,0:T(8,128)(2,1)}, bf16[192,384]{1,0:T(8,128)(2,1)S(1)}, u32[]{:S(2)}, u32[]{:S(2)}) collective-permute-start(bf16[192,384]{1,0:T(8,128)(2,1)} %get-tuple-element.177), channel_id=1, source_target_pairs={{0,8},{8,0},{16,24},{24,16},{1,9},{9,1},{17,25},{25,17},{2,10},{10... | collective-permute-start | bytes 442376 | tf_op jit(solution)/shard_map/ppermute | solution.py:52
  225.5 6.5 %collective-permute-start.37 = (f32[24,768]{1,0:T(8,128)S(1)}, f32[24,768]{1,0:T(8,128)S(1)}, u32[]{:S(2)}, u32[]{:S(2)}) collective-permute-start(f32[24,768]{1,0:T(8,128)S(1)} %add.53), channel_id=1, source_target_pairs={{0,4},{1,5},{2,6},{3,7},{4,0},{5,1},{6,2},{7,3},{8,12},{9,13},{10,... | collective-permute-start | bytes 221192 | tf_op jit(solution)/shard_map/ppermute | solution.py:52
  228.0 5.9 %collective-permute-start.38 = (bf16[192,384]{1,0:T(8,128)(2,1)S(1)}, bf16[192,384]{1,0:T(8,128)(2,1)S(1)}, u32[]{:S(2)}, u32[]{:S(2)}) collective-permute-start(bf16[192,384]{1,0:T(8,128)(2,1)S(1)} %add_convert_fusion.6), channel_id=1, source_target_pairs={{0,16},{8,24},{16,0},{24,8},{1,17},{9,25},{17,1},{25,9},{2,18},{10... | collective-permute-start | bytes 442376 | tf_op jit(solution)/shard_map/ppermute | solution.py:52
  (25 other events, 246.0 us)

commit v8 on v7

--- a/solution.py
+++ b/solution.py
@@ -492,21 +492,18 @@
 
 
 def product_kernel(
-    normed_far_ref, normed_near_ref, attended_far_ref, attended_near_ref, hidden_ref, chance_ref,
-    hits_ref, mask_ref, factors_ref, returned_ref, token_ref, output_ref, *rest
+    normed_ref, attended_ref, hidden_ref, chance_ref, hits_ref, mask_ref, factors_ref,
+    returned_ref, token_ref, output_ref, *rest
 ):
     piece_refs, total_ref = rest[:-1], rest[-1]
     ranks, columns, length = factors_ref.shape
     cols = columns // 4
     first, second = None, None
-    for j in range(ranks):
-        held = factors_ref[lax.axis_index("expert") ^ j].astype(FULL)
-        normed_ref, attended_ref = (
-            (normed_near_ref, attended_near_ref) if j % 2 else (normed_far_ref, attended_far_ref)
-        )
-        part = dot(held[: 3 * cols].astype(LOW), normed_ref[j // 2])
+    for e in range(ranks):
+        held = factors_ref[e].astype(FULL)
+        part = dot(held[: 3 * cols].astype(LOW), normed_ref[e])
         first = part if first is None else first + part
-        part = dot(held[3 * cols :].astype(LOW), attended_ref[j // 2])
+        part = dot(held[3 * cols :].astype(LOW), attended_ref[e])
         second = part if second is None else second + part
     total = jnp.concatenate([first, second], axis=0).T
     rows = piece_refs[0].shape[0]
@@ -631,10 +628,12 @@
     slabs, up_arrived = together(slabs, up_arrived)
     arrived = exchange(slabs).reshape(ranks * slab, model_width)
     up_pieces = gather_near(gather_far(up_arrived))
-    arrived, up_pieces, normed_own = together(arrived, up_pieces, normed_low)
+    arrived, up_pieces, normed_own, attended = together(
+        arrived, up_pieces, normed_low, attended
+    )
     row_far = gather_far(arrived)
-    far = list(range(2, ranks, 2))
-    normed_far = gather_bits(normed_own[None], "expert", far)
+    normed_all = lax.all_gather(normed_own, "expert", axis=0)
+    attended_all = lax.all_gather(attended, "expert", axis=0)
     by_expert = (local_experts, packed_rows)
     up_rows, up_act = call(
         upstream_kernel,
@@ -664,10 +663,7 @@
             pltpu.VMEM((*by_expert, 128), LOW),
         ],
     )
-    back, normed_far, attended_own = together(back, normed_far, attended)
     kept, got = scatter_terms(back)
-    normed_near = swap(normed_far, "expert", 1)
-    attended_far = gather_bits(attended_own[None], "expert", far)
     returned = call(
         expert_out_kernel,
         "expert_outputs",
@@ -680,8 +676,6 @@
     got, returned = together(got, returned)
     back = add(kept, got).reshape(ranks, slab, model_width)
     back = exchange(back)
-    returned, attended_far = together(returned, attended_far)
-    attended_near = swap(attended_far, "expert", 1)
     returned = add(*scatter_far(returned)).reshape(ranks, slab, model_width)
     back, returned = together(back, returned)
     returned = exchange(returned)
@@ -741,10 +735,8 @@
         5,
         [shaped(LOW, length, model_width)] + [shaped(LOW, rows_here, 4 * columns_here)] * dps,
         [
-            normed_far,
-            normed_near,
-            attended_far,
-            attended_near,
+            normed_all,
+            attended_all,
             hidden,
             chance,
             hits,

time: 236 us -> 216 us (0.915)
  waiting for transfers between devices: 98.4 us -> 81.1 us
  starting transfers between devices: 64.1 us -> 48 us
  between operations: 1.15 us -> 14.4 us
    ppermute x39 -> x31, waiting for transfers between devices: 84.7 us -> 48.9 us  [swap(): return lax.ppermute(value, axis, [(i, i ^ mask) for i in range(count)])]
    all_to_all x5, waiting for transfers between devices: 13.7 us -> 32.1 us  [exchange(): lax.all_to_all(value, 'expert', split_axis=0, concat_axis=0, tiled=True)]
    ppermute x39 -> x31, starting transfers between devices: 36.8 us -> 23.1 us  [swap(): return lax.ppermute(value, axis, [(i, i ^ mask) for i in range(count)])]
    all_to_all x5, starting transfers between devices: 27.3 us -> 24.7 us  [exchange(): lax.all_to_all(value, 'expert', split_axis=0, concat_axis=0, tiled=True)]
  transfers between devices with their start and end apart: 44 -> 38, of which waited for: 18 -> 20; matrix products, arithmetic and copies ran while one was open for 3% -> 4% of each run, Pallas kernels for 18% -> 24%
where the time goes in v8:
time: 216 us; the launch traced here: 215 us
  waiting for transfers between devices  81.1 us (38%)
  Pallas kernels  56.7 us (26%)
  starting transfers between devices  48 us (22%)
  between operations  14.4 us (7%)
  other arithmetic  8.47 us (4%)
  local copies, waits for them, and re-layouts  6.9 us (3%)
    pallas_call x8, Pallas kernels, call(): pl.pallas_call(kernel, out_shape=tuple(out_shape), in_specs=[VMEM] * len(...  56.7 us
    ppermute x31, waiting for transfers between devices, swap(): return lax.ppermute(value, axis, [(i, i ^ mask) for i in range(count)])  48.9 us
    all_to_all x5, waiting for transfers between devices, exchange(): lax.all_to_all(value, 'expert', split_axis=0, concat_axis=0, tiled=True)  32.1 us
    all_to_all x5, starting transfers between devices, exchange(): lax.all_to_all(value, 'expert', split_axis=0, concat_axis=0, tiled=True)  24.7 us
    ppermute x31, starting transfers between devices, swap(): return lax.ppermute(value, axis, [(i, i ^ mask) for i in range(count)])  23.1 us
    convert_element_type x7, other arithmetic, add(): return (left.astype(FULL) + right.astype(FULL)).astype(dtype)  5.66 us
  transfers between devices with their start and end apart: 38, of which 20 were waited for; matrix products, arithmetic and copies ran while one was open for 4% of the time, Pallas kernels for 24%

profile of v8, /device:TPU:0, one launch (start us, length us, event | category | flops | bytes accessed | tf_op | source)
XLA Modules:
  0.0 215.5 jit_solution(5762239602250101138)
XLA Ops:
  7.2 1.0 maximum_bitcast_fusion
  8.2 3.1 %collective-permute-start = (bf16[1,192,384]{2,1,0:T(8,128)(2,1)S(1)}, bf16[1,192,384]{2,1,0:T(8,128)(2,1)S(1)}, u32[]{:S(2)}, u32[]{:S(2)}) collective-permute-start(bf16[1,192,384]{2,1,0:T(8,128)(2,1)S(1)} %maximum_bitcast_fusion), channel_id=1, source_target_pairs={{0,2},{1,3},{2,0},{3,1},{4,6},{5,7},{6,4},{7,5},{8,10},{9,11},{10,... | collective-permute-start | bytes 442376 | tf_op jit(solution)/shard_map/ppermute | solution.py:52
  11.3 2.6 %collective-permute-start.1 = (bf16[1,192,384]{2,1,0:T(8,128)(2,1)S(1)}, bf16[1,192,384]{2,1,0:T(8,128)(2,1)S(1)}, u32[]{:S(2)}, u32[]{:S(2)}) collective-permute-start(bf16[1,192,384]{2,1,0:T(8,128)(2,1)S(1)} %maximum_bitcast_fusion), channel_id=1, source_target_pairs={{0,4},{1,5},{2,6},{3,7},{4,0},{5,1},{6,2},{7,3},{8,12},{9,13},{10,... | collective-permute-start | bytes 442376 | tf_op jit(solution)/shard_map/ppermute | solution.py:52
  15.9 3.3 %early.1 = (bf16[128,768]{1,0:T(8,128)(2,1)}, f32[128,16]{1,0:T(8,128)}, bf16[128,192]{1,0:T(8,128)(2,1)}, bf16[192,128]{1,0:T(8,128)(2,1)}, f32[12,128,128]{2,1,0:T(8,128)}, /*index=5*/bf16[8,24,768]{2,1,0:T(8,128)(2,1)}) custom-call(bf16[128,768]{1,0:T(8,128)(2,1)} %tokens_ref.5, s32[1,128]{1,0:T(1,128)} %bitcast.27, ...), custom_call_target="tpu_custom_call" | custom-call | bytes 10800000 | tf_op jit(solution)/shard_map/early/pallas_call | solution.py:529
  19.2 6.1 %collective-permute-done.1 = bf16[1,192,384]{2,1,0:T(8,128)(2,1)S(1)} collective-permute-done((bf16[1,192,384]{2,1,0:T(8,128)(2,1)S(1)}, bf16[1,192,384]{2,1,0:T(8,128)(2,1)S(1)}, u32[]{:S(2)}, u32[]{:S(2)}) %collective-permute-start.1) | collective-permute-done | bytes 147488 | tf_op jit(solution)/shard_map/ppermute | solution.py:52
  25.4 1.6 collective-permute-start.7
  27.0 1.5 collective-permute-start.3
  28.5 3.7 %collective-permute-done.7 = bf16[1,4,96,384]{3,2,1,0:T(8,128)(2,1)S(1)} collective-permute-done((bf16[1,4,96,384]{3,2,1,0:T(8,128)(2,1)S(1)}, bf16[1,4,96,384]{3,2,1,0:T(8,128)(2,1)S(1)}, u32[]{:S(2)}, u32[]{:S(2)}) %collective-permute-start.7) | collective-permute-done | bytes 294944 | tf_op jit(solution)/shard_map/ppermute | solution.py:52
  32.3 1.6 collective-permute-start.9
  33.9 2.5 %collective-permute-done.3 = bf16[1,4,96,384]{3,2,1,0:T(8,128)(2,1)S(1)} collective-permute-done((bf16[1,4,96,384]{3,2,1,0:T(8,128)(2,1)S(1)}, bf16[1,4,96,384]{3,2,1,0:T(8,128)(2,1)S(1)}, u32[]{:S(2)}, u32[]{:S(2)}) %collective-permute-start.3) | collective-permute-done | bytes 294944 | tf_op jit(solution)/shard_map/ppermute | solution.py:52
  37.1 9.3 %collective-permute-done.9.rest_6_ = bf16[2,4,96,384]{3,2,1,0:T(8,128)(2,1)S(1)} collective-permute-done((bf16[2,4,96,384]{3,2,1,0:T(8,128)(2,1)S(1)}, bf16[2,4,96,384]{3,2,1,0:T(8,128)(2,1)S(1)}, u32[]{:S(2)}, u32[]{:S(2)}) %collective-permute-start.9) | collective-permute-done | bytes 589856 | tf_op jit(solution)/shard_map/ppermute | solution.py:52
  46.9 1.5 collective-permute-done.10.rest_7_
  50.1 6.3 %all-to-all-start = ((bf16[8,24,768]{2,1,0:T(8,128)(2,1)}), bf16[8,24,768]{2,1,0:T(8,128)(2,1)}, u32[]{:S(2)}, u32[]{:S(2)}) async-start(bf16[8,24,768]{2,1,0:T(8,128)(2,1)} %get-tuple-element.111), calls=%async_computation | async-start | bytes 589824 | tf_op jit(solution)/shard_map/all_to_all | solution.py:60
  56.4 9.9 %attention_forward.1 = (bf16[3,768,128]{2,1,0:T(8,128)(2,1)}, f32[12,128,128]{2,1,0:T(8,128)}, bf16[128,768]{1,0:T(8,128)(2,1)}, f32[128,768]{1,0:T(8,128)}, f32...) custom-call(bf16[128,768]{1,0:T(8,128)(2,1)} %tokens_ref.5, bf16[128,768]{1,0:T(8,128)(2,1)} %get-tuple-element.115.normed_ref, ...), custom_call_target="tpu_custom_call" | custom-call | bytes 36000000 | tf_op jit(solution)/shard_map/attention_forward/pallas_call | solution.py:529
  66.4 1.0 collective-permute-start.12
  67.4 6.0 %all-to-all-start.1 = ((bf16[8,24,768]{2,1,0:T(8,128)(2,1)}), bf16[8,24,768]{2,1,0:T(8,128)(2,1)S(1)}, u32[]{:S(2)}, u32[]{:S(2)}) async-start(bf16[8,24,768]{2,1,0:T(8,128)(2,1)} %get-tuple-element.112), calls=%async_computation.1 | async-start | bytes 589824 | tf_op jit(solution)/shard_map/all_to_all | solution.py:60
  73.5 1.9 collective-permute-done.12.rest_2_
  75.4 7.0 %all-to-all-done.1 = bf16[8,24,768]{2,1,0:T(8,128)(2,1)S(1)} async-done(((bf16[8,24,768]{2,1,0:T(8,128)(2,1)}), bf16[8,24,768]{2,1,0:T(8,128)(2,1)S(1)}, u32[]{:S(2)}, u32[]{:S(2)}) %all-to-all-start.1) | async-done | bytes 294944 | tf_op jit(solution)/shard_map/all_to_all | solution.py:60
  82.6 1.1 collective-permute-start.14
  83.8 4.5 %upstream_rows.1 = (bf16[2,320,768]{2,1,0:T(8,128)(2,1)}, f32[2,320,768]{2,1,0:T(8,128)}) custom-call(bf16[160,192]{1,0:T(8,128)(2,1)} %constant.8.clone.pack_ref, bf16[2,768,768]{2,1,0:T(8,128)(2,1)} %w_out_ref.3, bf16[192,768]{1,0:T(8,128)(2,1)} %bitcast.6.rest_0_, bf16[192,768]{1,0:T(8,128)(2,1)} %copy-done.13, bf16[192,768]{1,0:T(8,128)(2,1)} %copy-done.12, ...), custom_call_target="tpu_custom_call" | custom-call | bytes 18000000 | tf_op jit(solution)/shard_map/upstream_rows/pallas_call | solution.py:529
  88.2 1.2 collective-permute-done.14.rest_2_
  90.0 1.1 collective-permute-done.15.rest_1_
  92.4 9.9 %experts.1 = (bf16[192,768]{1,0:T(8,128)(2,1)}, bf16[192,768]{1,0:T(8,128)(2,1)}, bf16[192,768]{1,0:T(8,128)(2,1)}, bf16[192,768]{1,0:T(8,128)(2,1)}, bf16[2,320...) custom-call(bf16[160,192]{1,0:T(8,128)(2,1)} %constant.8.clone.pack_re, ...), custom_call_target="tpu_custom_call" | custom-call | bytes 36000000 | tf_op jit(solution)/shard_map/experts/pallas_call | solution.py:529
  102.6 4.0 %expert_outputs.1 = (bf16[192,768]{1,0:T(8,128)(2,1)}, bf16[192,768]{1,0:T(8,128)(2,1)}, bf16[192,768]{1,0:T(8,128)(2,1)}, bf16[192,768]{1,0:T(8,128)(2,1)}) custom-call(bf16[192,160]{1,0:T(8,128)(2,1)} %constant.9.clone.pack_t_ref, bf16[2,768,768]{2,1,0:T(8,128)(2,1)} %w_out_ref.3, bf16[2,320,768]{2,1,0:T(8,128)(2,1)} %get-tuple-element.150.act_ref), custom_call_target="tpu_custom_call" | custom-call | bytes 10800000 | tf_op jit(solution)/shard_map/expert_outputs/pallas_call | solution.py:529
  107.7 1.1 collective-permute-start.19
  108.8 1.0 add_convert_fusion.2
  109.8 1.0 add_convert_fusion.3
  110.9 5.9 %collective-permute-done.19 = bf16[192,768]{1,0:T(8,128)(2,1)S(1)} collective-permute-done((bf16[192,768]{1,0:T(8,128)(2,1)S(1)}, bf16[192,768]{1,0:T(8,128)(2,1)S(1)}, u32[]{:S(2)}, u32[]{:S(2)}) %collective-permute-start.19) | collective-permute-done | bytes 294944 | tf_op jit(solution)/shard_map/ppermute | solution.py:52
  116.8 1.0 collective-permute-start.22
  118.7 5.1 %all-to-all-start.2 = ((bf16[8,24,768]{2,1,0:T(8,128)(2,1)}), bf16[8,24,768]{2,1,0:T(8,128)(2,1)S(1)}, u32[]{:S(2)}, u32[]{:S(2)}) async-start(bf16[8,24,768]{2,1,0:T(8,128)(2,1)} %bitcast.10), calls=%async_computation.2 | async-start | bytes 589824 | tf_op jit(solution)/shard_map/all_to_all | solution.py:60
  123.8 1.4 collective-permute-done.22
  125.9 6.8 %all-to-all-done.2.rest_8_ = bf16[8,24,768]{2,1,0:T(8,128)(2,1)S(1)} async-done(((bf16[8,24,768]{2,1,0:T(8,128)(2,1)}), bf16[8,24,768]{2,1,0:T(8,128)(2,1)S(1)}, u32[]{:S(2)}, u32[]{:S(2)}) %all-to-all-start.2) | async-done | bytes 294944 | tf_op jit(solution)/shard_map/all_to_all | solution.py:60
  132.8 3.5 %all-to-all-start.3 = ((bf16[8,24,768]{2,1,0:T(8,128)(2,1)}), bf16[8,24,768]{2,1,0:T(8,128)(2,1)S(1)}, u32[]{:S(2)}, u32[]{:S(2)}) async-start(bf16[8,24,768]{2,1,0:T(8,128)(2,1)} %bitcast.11), calls=%async_computation.3 | async-start | bytes 589824 | tf_op jit(solution)/shard_map/all_to_all | solution.py:60
  136.3 12.0 %attention_backward.1 = (f32[128,768]{1,0:T(8,128)}, f32[24,768]{1,0:T(8,128)}, bf16[8,384,128]{2,1,0:T(8,128)(2,1)}) custom-call(bf16[128,768]{1,0:T(8,128)(2,1)} %tokens_ref.5, f32[2,768]{1,0:T(2,128)} %maximum_convert_fusion.gain_ref, bf16[16,768]{1,0:T(8,128)(2,1)} %bitcast.25, f32[128,16]{1,0:T(8,128)} %get-tuple-element.98.hits_ref, ...), custom_call_target="tpu_custom_call" | custom-call | bytes 43200000 | tf_op jit(solution)/shard_map/attention_backward/pallas_call | solution.py:529
  148.3 2.5 %all-to-all-done.3.returned_ref = bf16[8,24,768]{2,1,0:T(8,128)(2,1)S(1)} async-done(((bf16[8,24,768]{2,1,0:T(8,128)(2,1)}), bf16[8,24,768]{2,1,0:T(8,128)(2,1)S(1)}, u32[]{:S(2)}, u32[]{:S(2)}) %all-to-all-start.3) | async-done | bytes 294944 | tf_op jit(solution)/shard_map/all_to_all | solution.py:60
  150.8 3.8 %all-to-all-start.4 = ((bf16[8,384,128]{2,1,0:T(8,128)(2,1)}), bf16[8,384,128]{2,1,0:T(8,128)(2,1)S(1)}, u32[]{:S(2)}, u32[]{:S(2)}) async-start(bf16[8,384,128]{2,1,0:T(8,128)(2,1)} %get-tuple-element.147), calls=%async_computation.4 | async-start | bytes 1572864 | tf_op jit(solution)/shard_map/all_to_all | solution.py:60
  154.7 1.5 collective-permute-done.23
  157.0 1.5 collective-permute-start.24
  158.6 2.9 %collective-permute-done.24 = f32[24,768]{1,0:T(8,128)S(1)} collective-permute-done((f32[24,768]{1,0:T(8,128)S(1)}, f32[24,768]{1,0:T(8,128)S(1)}, u32[]{:S(2)}, u32[]{:S(2)}) %collective-permute-start.24) | collective-permute-done | bytes 73760 | tf_op jit(solution)/shard_map/ppermute | solution.py:52
  161.5 1.8 collective-permute-start.25
  163.3 8.2 %expert_gradients.1 = (f32[2,768,768]{2,1,0:T(8,128)}, f32[2,768,768]{2,1,0:T(8,128)}, f32[8,128]{1,0:T(8,128)}) custom-call(bf16[2,320,768]{2,1,0:T(8,128)(2,1)} %get-tuple-element.149.rows_ref, bf16[2,320,768]{2,1,0:T(8,128)(2,1)} %get-tuple-element.150.act_ref, bf16[2,320,768]{2,1,0:T(8,128)(2,1)} %get-tuple-element.151.pre_grad_ref, ...), custom_call_target="tpu_custom_call" | custom-call | bytes 28800000 | tf_op jit(solution)/shard_map/expert_gradients/pallas_call | solution.py:529
  171.5 15.7 %all-to-all-done.4.factors_ref = bf16[8,384,128]{2,1,0:T(8,128)(2,1)S(1)} async-done(((bf16[8,384,128]{2,1,0:T(8,128)(2,1)}), bf16[8,384,128]{2,1,0:T(8,128)(2,1)S(1)}, u32[]{:S(2)}, u32[]{:S(2)}) %all-to-all-start.4) | async-done | bytes 786464 | tf_op jit(solution)/shard_map/all_to_all | solution.py:60
  188.1 4.8 %weight_gradients.1 = (bf16[128,768]{1,0:T(8,128)(2,1)}, bf16[192,384]{1,0:T(8,128)(2,1)}, bf16[192,384]{1,0:T(8,128)(2,1)}, bf16[192,384]{1,0:T(8,128)(2,1)}, bf16[192,384]{1,0:T(8,128)(2,1)}) custom-call(bf16[8,128,768]{2,1,0:T(8,128)(2,1)} %bitcast.19, bf16[8,128,768]{2,1,0:T(8,128)(2,1)} %bitcast.20, f32[128,768]{1,0:T(8,128)} %get-tuple-element.117.hidden_ref, ...), custom_call_target="tpu_custom_call" | custom-call | bytes 18000000 | tf_op jit(solution)/shard_map/weight_gradients/pallas_call | solution.py:529
  193.4 4.2 %collective-permute-done.28 = f32[24,768]{1,0:T(8,128)S(1)} collective-permute-done((f32[24,768]{1,0:T(8,128)S(1)}, f32[24,768]{1,0:T(8,128)S(1)}, u32[]{:S(2)}, u32[]{:S(2)}) %collective-permute-start.28) | collective-permute-done | bytes 73760 | tf_op jit(solution)/shard_map/ppermute | solution.py:52
  197.6 1.0 add_convert_fusion.6
  198.6 1.0 add_convert_fusion.7
  199.6 1.6 collective-permute-start.30
  201.3 4.6 %collective-permute-done.29 = f32[24,768]{1,0:T(8,128)S(1)} collective-permute-done((f32[24,768]{1,0:T(8,128)S(1)}, f32[24,768]{1,0:T(8,128)S(1)}, u32[]{:S(2)}, u32[]{:S(2)}) %collective-permute-start.29) | collective-permute-done | bytes 73760 | tf_op jit(solution)/shard_map/ppermute | solution.py:52
  (107 shorter events, 15.5 us)
Async XLA Ops:
  8.2 11.0 %collective-permute-start = (bf16[1,192,384]{2,1,0:T(8,128)(2,1)S(1)}, bf16[1,192,384]{2,1,0:T(8,128)(2,1)S(1)}, u32[]{:S(2)}, u32[]{:S(2)}) collective-permute-start(bf16[1,192,384]{2,1,0:T(8,128)(2,1)S(1)} %maximum_bitcast_fusion), channel_id=1, source_target_pairs={{0,2},{1,3},{2,0},{3,1},{4,6},{5,7},{6,4},{7,5},{8,10},{9,11},{10,... | collective-permute-start | bytes 442376 | tf_op jit(solution)/shard_map/ppermute | solution.py:52
  11.3 14.0 %collective-permute-start.1 = (bf16[1,192,384]{2,1,0:T(8,128)(2,1)S(1)}, bf16[1,192,384]{2,1,0:T(8,128)(2,1)S(1)}, u32[]{:S(2)}, u32[]{:S(2)}) collective-permute-start(bf16[1,192,384]{2,1,0:T(8,128)(2,1)S(1)} %maximum_bitcast_fusion), channel_id=1, source_target_pairs={{0,4},{1,5},{2,6},{3,7},{4,0},{5,1},{6,2},{7,3},{8,12},{9,13},{10,... | collective-permute-start | bytes 442376 | tf_op jit(solution)/shard_map/ppermute | solution.py:52
  13.9 11.4 %collective-permute-start.2 = (bf16[1,192,384]{2,1,0:T(8,128)(2,1)S(1)}, bf16[1,192,384]{2,1,0:T(8,128)(2,1)S(1)}, u32[]{:S(2)}, u32[]{:S(2)}) collective-permute-start(bf16[1,192,384]{2,1,0:T(8,128)(2,1)S(1)} %maximum_bitcast_fusion), channel_id=1, source_target_pairs={{0,6},{1,7},{2,4},{3,5},{4,2},{5,3},{6,0},{7,1},{8,14},{9,15},{10,... | collective-permute-start | bytes 442376 | tf_op jit(solution)/shard_map/ppermute | solution.py:52
  25.4 6.8 %collective-permute-start.7 = (bf16[1,4,96,384]{3,2,1,0:T(8,128)(2,1)S(1)}, bf16[1,4,96,384]{3,2,1,0:T(8,128)(2,1)S(1)}, u32[]{:S(2)}, u32[]{:S(2)}) collective-permute-start(bf16[1,4,96,384]{3,2,1,0:T(8,128)(2,1)S(1)} %get-tuple-element.172), channel_id=1, source_target_pairs={{0,16},{8,24},{16,0},{24,8},{1,17},{9,25},{17,1},{25,9},{2,18},{10... | collective-permute-start | bytes 884744 | tf_op jit(solution)/shard_map/ppermute | solution.py:52
  27.0 9.3 %collective-permute-start.3 = (bf16[1,4,96,384]{3,2,1,0:T(8,128)(2,1)S(1)}, bf16[1,4,96,384]{3,2,1,0:T(8,128)(2,1)S(1)}, u32[]{:S(2)}, u32[]{:S(2)}) collective-permute-start(bf16[1,4,96,384]{3,2,1,0:T(8,128)(2,1)S(1)} %get-tuple-element.173), channel_id=1, source_target_pairs={{0,1},{1,0},{2,3},{3,2},{4,5},{5,4},{6,7},{7,6},{8,9},{9,8},{10,11... | collective-permute-start | bytes 884744 | tf_op jit(solution)/shard_map/ppermute | solution.py:52
  32.3 24.1 %copy-start = (bf16[2,4,96,384]{3,2,1,0:T(8,128)(2,1)}, bf16[2,4,96,384]{3,2,1,0:T(8,128)(2,1)S(1)}, u32[]{:S(2)}) copy-start(bf16[2,4,96,384]{3,2,1,0:T(8,128)(2,1)S(1)} %pad_maximum_fusion.2.rest_4_) | copy-start | bytes 1769476
  32.3 14.1 %collective-permute-start.9 = (bf16[2,4,96,384]{3,2,1,0:T(8,128)(2,1)S(1)}, bf16[2,4,96,384]{3,2,1,0:T(8,128)(2,1)S(1)}, u32[]{:S(2)}, u32[]{:S(2)}) collective-permute-start(bf16[2,4,96,384]{3,2,1,0:T(8,128)(2,1)S(1)} %pad_maximum_fusion.2.rest_4_), channel_id=1, source_target_pairs={{0,1},{1,0},{2,3},{3,2},{4,5},{5,4},{6,7},{7,6},{8,9},{9,8},{10,11... | collective-permute-start | bytes 1769480 | tf_op jit(solution)/shard_map/ppermute | solution.py:52
  36.4 19.9 %copy-start.1 = (bf16[2,4,96,384]{3,2,1,0:T(8,128)(2,1)}, bf16[2,4,96,384]{3,2,1,0:T(8,128)(2,1)S(1)}, u32[]{:S(2)}) copy-start(bf16[2,4,96,384]{3,2,1,0:T(8,128)(2,1)S(1)} %pad_maximum_fusion.1.rest_0_) | copy-start | bytes 1769476
  36.5 9.9 %collective-permute-start.5 = (bf16[2,4,96,384]{3,2,1,0:T(8,128)(2,1)S(1)}, bf16[2,4,96,384]{3,2,1,0:T(8,128)(2,1)S(1)}, u32[]{:S(2)}, u32[]{:S(2)}) collective-permute-start(bf16[2,4,96,384]{3,2,1,0:T(8,128)(2,1)S(1)} %pad_maximum_fusion.1.rest_0_), channel_id=1, source_target_pairs={{0,16},{8,24},{16,0},{24,8},{1,17},{9,25},{17,1},{25,9},{2,18},{10... | collective-permute-start | bytes 1769480 | tf_op jit(solution)/shard_map/ppermute | solution.py:52
  36.5 10.4 %collective-permute-start.8 = (bf16[2,4,96,384]{3,2,1,0:T(8,128)(2,1)S(1)}, bf16[2,4,96,384]{3,2,1,0:T(8,128)(2,1)S(1)}, u32[]{:S(2)}, u32[]{:S(2)}) collective-permute-start(bf16[2,4,96,384]{3,2,1,0:T(8,128)(2,1)S(1)} %pad_maximum_fusion.2.rest_4_), channel_id=1, source_target_pairs={{0,8},{8,0},{16,24},{24,16},{1,9},{9,1},{17,25},{25,17},{2,10},{10... | collective-permute-start | bytes 1769480 | tf_op jit(solution)/shard_map/ppermute | solution.py:52
  36.6 10.3 %collective-permute-start.4 = (bf16[2,4,96,384]{3,2,1,0:T(8,128)(2,1)S(1)}, bf16[2,4,96,384]{3,2,1,0:T(8,128)(2,1)S(1)}, u32[]{:S(2)}, u32[]{:S(2)}) collective-permute-start(bf16[2,4,96,384]{3,2,1,0:T(8,128)(2,1)S(1)} %pad_maximum_fusion.1.rest_0_), channel_id=1, source_target_pairs={{0,8},{8,0},{16,24},{24,16},{1,9},{9,1},{17,25},{25,17},{2,10},{10... | collective-permute-start | bytes 1769480 | tf_op jit(solution)/shard_map/ppermute | solution.py:52
  46.4 10.0 %copy-start.3 = (bf16[2,4,96,384]{3,2,1,0:T(8,128)(2,1)}, bf16[2,4,96,384]{3,2,1,0:T(8,128)(2,1)S(1)}, u32[]{:S(2)}) copy-start(bf16[2,4,96,384]{3,2,1,0:T(8,128)(2,1)S(1)} %collective-permute-done.9.rest_6_) | copy-start | bytes 1769476
  46.4 2.0 collective-permute-start.10
  46.4 10.0 %copy-start.4 = (bf16[2,4,96,384]{3,2,1,0:T(8,128)(2,1)}, bf16[2,4,96,384]{3,2,1,0:T(8,128)(2,1)S(1)}, u32[]{:S(2)}) copy-start(bf16[2,4,96,384]{3,2,1,0:T(8,128)(2,1)S(1)} %collective-permute-done.5.rest_2_) | copy-start | bytes 1769476
  46.4 2.8 %collective-permute-start.6 = (bf16[2,4,96,384]{3,2,1,0:T(8,128)(2,1)S(1)}, bf16[2,4,96,384]{3,2,1,0:T(8,128)(2,1)S(1)}, u32[]{:S(2)}, u32[]{:S(2)}) collective-permute-start(bf16[2,4,96,384]{3,2,1,0:T(8,128)(2,1)S(1)} %collective-permute-done.5.rest_2_), channel_id=1, source_target_pairs={{0,8},{8,0},{16,24},{24,16},{1,9},{9,1},{17,25},{25,17},{2,10},{10... | collective-permute-start | bytes 1769480 | tf_op jit(solution)/shard_map/ppermute | solution.py:52
  46.9 9.5 %copy-start.5 = (bf16[2,4,96,384]{3,2,1,0:T(8,128)(2,1)}, bf16[2,4,96,384]{3,2,1,0:T(8,128)(2,1)S(1)}, u32[]{:S(2)}) copy-start(bf16[2,4,96,384]{3,2,1,0:T(8,128)(2,1)S(1)} %collective-permute-done.8.rest_5_) | copy-start | bytes 1769476
  46.9 9.5 %copy-start.6 = (bf16[2,4,96,384]{3,2,1,0:T(8,128)(2,1)}, bf16[2,4,96,384]{3,2,1,0:T(8,128)(2,1)S(1)}, u32[]{:S(2)}) copy-start(bf16[2,4,96,384]{3,2,1,0:T(8,128)(2,1)S(1)} %collective-permute-done.4.rest_1_) | copy-start | bytes 1769476
  50.1 16.3 %all-to-all-start = ((bf16[8,24,768]{2,1,0:T(8,128)(2,1)}), bf16[8,24,768]{2,1,0:T(8,128)(2,1)}, u32[]{:S(2)}, u32[]{:S(2)}) async-start(bf16[8,24,768]{2,1,0:T(8,128)(2,1)} %get-tuple-element.111), calls=%async_computation | async-start | bytes 589824 | tf_op jit(solution)/shard_map/all_to_all | solution.py:60
  66.4 9.0 %collective-permute-start.12 = (bf16[192,768]{1,0:T(8,128)(2,1)}, bf16[192,768]{1,0:T(8,128)(2,1)S(1)}, u32[]{:S(2)}, u32[]{:S(2)}) collective-permute-start(bf16[192,768]{1,0:T(8,128)(2,1)} %bitcast.6.rest_0_), channel_id=1, source_target_pairs={{0,16},{8,24},{16,0},{24,8},{1,17},{9,25},{17,1},{25,9},{2,18},{10... | collective-permute-start | bytes 884744 | tf_op jit(solution)/shard_map/ppermute | solution.py:52
  67.4 15.0 %all-to-all-start.1 = ((bf16[8,24,768]{2,1,0:T(8,128)(2,1)}), bf16[8,24,768]{2,1,0:T(8,128)(2,1)S(1)}, u32[]{:S(2)}, u32[]{:S(2)}) async-start(bf16[8,24,768]{2,1,0:T(8,128)(2,1)} %get-tuple-element.112), calls=%async_computation.1 | async-start | bytes 589824 | tf_op jit(solution)/shard_map/all_to_all | solution.py:60
  73.4 113.8 %all-gather.5.cloned.1.call-start = ((), (), s32[]{:S(2)}) async-start(), calls=%async_computation.5 | async-start | bytes 1769472 | tf_op jit(solution)/shard_map/all_gather | solution.py:635
  73.4 2.0 collective-permute-start.11
  75.4 8.4 %copy-start.12 = (bf16[192,768]{1,0:T(8,128)(2,1)}, bf16[192,768]{1,0:T(8,128)(2,1)S(1)}, u32[]{:S(2)}) copy-start(bf16[192,768]{1,0:T(8,128)(2,1)S(1)} %collective-permute-done.12.rest_2_) | copy-start | bytes 884740
  75.4 7.0 %collective-permute-start.13 = (bf16[192,768]{1,0:T(8,128)(2,1)S(1)}, bf16[192,768]{1,0:T(8,128)(2,1)S(1)}, u32[]{:S(2)}, u32[]{:S(2)}) collective-permute-start(bf16[192,768]{1,0:T(8,128)(2,1)S(1)} %collective-permute-done.12.rest_2_), channel_id=1, source_target_pairs={{0,8},{8,0},{16,24},{24,16},{1,9},{9,1},{17,25},{25,17},{2,10},{10... | collective-permute-start | bytes 884744 | tf_op jit(solution)/shard_map/ppermute | solution.py:52
  82.4 9.1 %copy-start.9 = (bf16[8,24,768]{2,1,0:T(8,128)(2,1)}, bf16[8,24,768]{2,1,0:T(8,128)(2,1)S(1)}, u32[]{:S(2)}) copy-start(bf16[8,24,768]{2,1,0:T(8,128)(2,1)S(1)} %all-to-all-done.1) | copy-start | bytes 884740
  82.4 104.8 %all-gather.7.cloned.1.call-start = ((), (), s32[]{:S(2)}) async-start(), calls=%async_computation.6 | async-start | bytes 1769472 | tf_op jit(solution)/shard_map/all_gather | solution.py:636
  82.6 6.8 %collective-permute-start.14 = (bf16[192,768]{1,0:T(8,128)(2,1)S(1)}, bf16[192,768]{1,0:T(8,128)(2,1)S(1)}, u32[]{:S(2)}, u32[]{:S(2)}) collective-permute-start(bf16[192,768]{1,0:T(8,128)(2,1)S(1)} %bitcast.21), channel_id=1, source_target_pairs={{0,16},{8,24},{16,0},{24,8},{1,17},{9,25},{17,1},{25,9},{2,18},{10... | collective-permute-start | bytes 884744 | tf_op jit(solution)/shard_map/ppermute | solution.py:52
  89.4 1.6 collective-permute-start.15
  89.4 2.0 collective-permute-start.16
  102.4 5.2 %collective-permute-start.18 = (bf16[192,768]{1,0:T(8,128)(2,1)}, bf16[192,768]{1,0:T(8,128)(2,1)S(1)}, u32[]{:S(2)}, u32[]{:S(2)}) collective-permute-start(bf16[192,768]{1,0:T(8,128)(2,1)} %get-tuple-element.134), channel_id=1, source_target_pairs={{0,8},{8,0},{16,24},{24,16},{1,9},{9,1},{17,25},{25,17},{2,10},{10... | collective-permute-start | bytes 884744 | tf_op jit(solution)/shard_map/ppermute | solution.py:52
  102.6 15.3 %copy-start.19 = (bf16[192,768]{1,0:T(8,128)(2,1)S(1)}, bf16[192,768]{1,0:T(8,128)(2,1)}, u32[]{:S(2)}) copy-start(bf16[192,768]{1,0:T(8,128)(2,1)} %get-tuple-element.131) | copy-start | bytes 884740
  106.6 2.1 collective-permute-start.21
  107.0 2.8 %collective-permute-start.20 = (bf16[192,768]{1,0:T(8,128)(2,1)}, bf16[192,768]{1,0:T(8,128)(2,1)S(1)}, u32[]{:S(2)}, u32[]{:S(2)}) collective-permute-start(bf16[192,768]{1,0:T(8,128)(2,1)} %get-tuple-element.137), channel_id=1, source_target_pairs={{0,8},{8,0},{16,24},{24,16},{1,9},{9,1},{17,25},{25,17},{2,10},{10... | collective-permute-start | bytes 884744 | tf_op jit(solution)/shard_map/ppermute | solution.py:52
  107.2 10.6 %collective-permute-start.17 = (bf16[192,768]{1,0:T(8,128)(2,1)S(1)}, bf16[192,768]{1,0:T(8,128)(2,1)S(1)}, u32[]{:S(2)}, u32[]{:S(2)}) collective-permute-start(bf16[192,768]{1,0:T(8,128)(2,1)S(1)} %copy-done.20), channel_id=1, source_target_pairs={{0,8},{8,0},{16,24},{24,16},{1,9},{9,1},{17,25},{25,17},{2,10},{10... | collective-permute-start | bytes 884744 | tf_op jit(solution)/shard_map/ppermute | solution.py:52
  107.7 9.1 %collective-permute-start.19 = (bf16[192,768]{1,0:T(8,128)(2,1)S(1)}, bf16[192,768]{1,0:T(8,128)(2,1)S(1)}, u32[]{:S(2)}, u32[]{:S(2)}) collective-permute-start(bf16[192,768]{1,0:T(8,128)(2,1)S(1)} %add_convert_fusion.4), channel_id=1, source_target_pairs={{0,16},{8,24},{16,0},{24,8},{1,17},{9,25},{17,1},{25,9},{2,18},{10... | collective-permute-start | bytes 884744 | tf_op jit(solution)/shard_map/ppermute | solution.py:52
  116.8 8.3 %collective-permute-start.22 = (bf16[192,768]{1,0:T(8,128)(2,1)S(1)}, bf16[192,768]{1,0:T(8,128)(2,1)S(1)}, u32[]{:S(2)}, u32[]{:S(2)}) collective-permute-start(bf16[192,768]{1,0:T(8,128)(2,1)S(1)} %add_convert_fusion.2), channel_id=1, source_target_pairs={{0,16},{8,24},{16,0},{24,8},{1,17},{9,25},{17,1},{25,9},{2,18},{10... | collective-permute-start | bytes 884744 | tf_op jit(solution)/shard_map/ppermute | solution.py:52
  118.7 14.1 %all-to-all-start.2 = ((bf16[8,24,768]{2,1,0:T(8,128)(2,1)}), bf16[8,24,768]{2,1,0:T(8,128)(2,1)S(1)}, u32[]{:S(2)}, u32[]{:S(2)}) async-start(bf16[8,24,768]{2,1,0:T(8,128)(2,1)} %bitcast.10), calls=%async_computation.2 | async-start | bytes 589824 | tf_op jit(solution)/shard_map/all_to_all | solution.py:60
  132.8 18.1 %all-to-all-start.3 = ((bf16[8,24,768]{2,1,0:T(8,128)(2,1)}), bf16[8,24,768]{2,1,0:T(8,128)(2,1)S(1)}, u32[]{:S(2)}, u32[]{:S(2)}) async-start(bf16[8,24,768]{2,1,0:T(8,128)(2,1)} %bitcast.11), calls=%async_computation.3 | async-start | bytes 589824 | tf_op jit(solution)/shard_map/all_to_all | solution.py:60
  150.8 20.6 %copy-start.11 = (bf16[8,24,768]{2,1,0:T(8,128)(2,1)}, bf16[8,24,768]{2,1,0:T(8,128)(2,1)S(1)}, u32[]{:S(2)}) copy-start(bf16[8,24,768]{2,1,0:T(8,128)(2,1)S(1)} %all-to-all-done.3.returned_ref) | copy-start | bytes 884740
  150.8 36.4 %all-to-all-start.4 = ((bf16[8,384,128]{2,1,0:T(8,128)(2,1)}), bf16[8,384,128]{2,1,0:T(8,128)(2,1)S(1)}, u32[]{:S(2)}, u32[]{:S(2)}) async-start(bf16[8,384,128]{2,1,0:T(8,128)(2,1)} %get-tuple-element.147), calls=%async_computation.4 | async-start | bytes 1572864 | tf_op jit(solution)/shard_map/all_to_all | solution.py:60
  154.6 1.5 collective-permute-start.23
  157.0 4.4 %collective-permute-start.24 = (f32[24,768]{1,0:T(8,128)S(1)}, f32[24,768]{1,0:T(8,128)S(1)}, u32[]{:S(2)}, u32[]{:S(2)}) collective-permute-start(f32[24,768]{1,0:T(8,128)S(1)} %add.48), channel_id=1, source_target_pairs={{0,16},{8,24},{16,0},{24,8},{1,17},{9,25},{17,1},{25,9},{2,18},{10... | collective-permute-start | bytes 221192 | tf_op jit(solution)/shard_map/ppermute | solution.py:52
  161.5 10.0 %collective-permute-start.25 = (f32[24,768]{1,0:T(8,128)S(1)}, f32[24,768]{1,0:T(8,128)S(1)}, u32[]{:S(2)}, u32[]{:S(2)}) collective-permute-start(f32[24,768]{1,0:T(8,128)S(1)} %add.49), channel_id=1, source_target_pairs={{0,1},{1,0},{2,3},{3,2},{4,5},{5,4},{6,7},{7,6},{8,9},{9,8},{10,11... | collective-permute-start | bytes 221192 | tf_op jit(solution)/shard_map/ppermute | solution.py:52
  192.9 4.7 %collective-permute-start.27 = (bf16[192,384]{1,0:T(8,128)(2,1)}, bf16[192,384]{1,0:T(8,128)(2,1)S(1)}, u32[]{:S(2)}, u32[]{:S(2)}) collective-permute-start(bf16[192,384]{1,0:T(8,128)(2,1)} %get-tuple-element.163), channel_id=1, source_target_pairs={{0,8},{8,0},{16,24},{24,16},{1,9},{9,1},{17,25},{25,17},{2,10},{10... | collective-permute-start | bytes 442376 | tf_op jit(solution)/shard_map/ppermute | solution.py:52
  192.9 4.7 %collective-permute-start.28 = (f32[24,768]{1,0:T(8,128)S(1)}, f32[24,768]{1,0:T(8,128)S(1)}, u32[]{:S(2)}, u32[]{:S(2)}) collective-permute-start(f32[24,768]{1,0:T(8,128)S(1)} %add.50), channel_id=1, source_target_pairs={{0,2},{1,3},{2,0},{3,1},{4,6},{5,7},{6,4},{7,5},{8,10},{9,11},{10,... | collective-permute-start | bytes 221192 | tf_op jit(solution)/shard_map/ppermute | solution.py:52
  193.0 5.6 %collective-permute-start.26 = (bf16[192,384]{1,0:T(8,128)(2,1)}, bf16[192,384]{1,0:T(8,128)(2,1)S(1)}, u32[]{:S(2)}, u32[]{:S(2)}) collective-permute-start(bf16[192,384]{1,0:T(8,128)(2,1)} %get-tuple-element.161), channel_id=1, source_target_pairs={{0,8},{8,0},{16,24},{24,16},{1,9},{9,1},{17,25},{25,17},{2,10},{10... | collective-permute-start | bytes 442376 | tf_op jit(solution)/shard_map/ppermute | solution.py:52
  199.5 6.3 %collective-permute-start.29 = (f32[24,768]{1,0:T(8,128)S(1)}, f32[24,768]{1,0:T(8,128)S(1)}, u32[]{:S(2)}, u32[]{:S(2)}) collective-permute-start(f32[24,768]{1,0:T(8,128)S(1)} %add.53), channel_id=1, source_target_pairs={{0,4},{1,5},{2,6},{3,7},{4,0},{5,1},{6,2},{7,3},{8,12},{9,13},{10,... | collective-permute-start | bytes 221192 | tf_op jit(solution)/shard_map/ppermute | solution.py:52
  199.6 8.1 %collective-permute-start.30 = (bf16[192,384]{1,0:T(8,128)(2,1)S(1)}, bf16[192,384]{1,0:T(8,128)(2,1)S(1)}, u32[]{:S(2)}, u32[]{:S(2)}) collective-permute-start(bf16[192,384]{1,0:T(8,128)(2,1)S(1)} %add_convert_fusion.6), channel_id=1, source_target_pairs={{0,16},{8,24},{16,0},{24,8},{1,17},{9,25},{17,1},{25,9},{2,18},{10... | collective-permute-start | bytes 442376 | tf_op jit(solution)/shard_map/ppermute | solution.py:52
  (11 other events, 29.4 us)
Sparse Core Ops, SparseCore 0:
  82.5 42.7 all-gather.4
  127.5 59.0 all-gather.6

commit v9 on v8

--- a/solution.py
+++ b/solution.py
@@ -58,6 +58,11 @@
 
 def exchange(value):
     return lax.all_to_all(value, "expert", split_axis=0, concat_axis=0, tiled=True)
+
+
+def halves():
+    half = lax.axis_size("expert") // 2
+    return [list(range(half)), list(range(half, 2 * half))]
 
 
 def gather_far(value):
@@ -476,7 +481,8 @@
         part = dot(w_ref[e], jnp.concatenate(held, axis=0).astype(LOW))
         total = part if total is None else total + part
         sent = [grads_ref[m, span, :] for m in range(3)] + [turned_ref[span, :]]
-        factors_ref[e] = jnp.concatenate(sent, axis=0).astype(LOW)
+        sent = jnp.concatenate(sent, axis=0).astype(LOW)
+        factors_ref[e % (ranks // 2), e // (ranks // 2)] = sent
     inputs = tokens_ref[...].astype(FULL)
     gain_one = gain_ref[0:1, :]
     _, scale_one = normalize(inputs, gain_one)
@@ -491,26 +497,30 @@
         small_ref[line : line + 1, place : place + sums.shape[1]] = sums[h : h + 1]
 
 
-def product_kernel(
-    normed_ref, attended_ref, hidden_ref, chance_ref, hits_ref, mask_ref, factors_ref,
-    returned_ref, token_ref, output_ref, *rest
-):
+def product_kernel(normed_ref, attended_ref, factors_ref, token_ref, *rest):
     piece_refs, total_ref = rest[:-1], rest[-1]
-    ranks, columns, length = factors_ref.shape
+    count, _, columns, length = factors_ref.shape
     cols = columns // 4
-    first, second = None, None
-    for e in range(ranks):
-        held = factors_ref[e].astype(FULL)
-        part = dot(held[: 3 * cols].astype(LOW), normed_ref[e])
-        first = part if first is None else first + part
-        part = dot(held[3 * cols :].astype(LOW), attended_ref[e])
-        second = part if second is None else second + part
-    total = jnp.concatenate([first, second], axis=0).T
-    rows = piece_refs[0].shape[0]
-    for j in range(len(piece_refs)):
-        total_ref[j] = total[j * rows : (j + 1) * rows]
+    rows = total_ref.shape[2]
+    for side in range(2):
+        first, second = None, None
+        for e in range(count):
+            held = factors_ref[e, side].astype(FULL)
+            part = dot(held[: 3 * cols].astype(LOW), normed_ref[e])
+            first = part if first is None else first + part
+            part = dot(held[3 * cols :].astype(LOW), attended_ref[e])
+            second = part if second is None else second + part
+        total = jnp.concatenate([first, second], axis=0).T
+        for j in range(len(piece_refs)):
+            total_ref[side, j] = total[j * rows : (j + 1) * rows]
+    own = (lax.axis_index("expert") >= count).astype(jnp.int32)
     for j, ref in enumerate(piece_refs):
-        ref[...] = total_ref[lax.axis_index("dp") ^ j].astype(LOW)
+        place = lax.axis_index("dp") ^ j
+        ref[0] = total_ref[own, place].astype(LOW)
+        ref[1] = total_ref[1 - own, place].astype(LOW)
+
+
+def output_kernel(hidden_ref, chance_ref, hits_ref, mask_ref, returned_ref, output_ref):
     gate = jnp.sum(chance_ref[...] * hits_ref[...], axis=1, keepdims=True)
     fetched = dot(mask_ref[...], joined(returned_ref))
     output_ref[...] = (hidden_ref[...] + gate * fetched).astype(LOW)
@@ -632,8 +642,8 @@
         arrived, up_pieces, normed_low, attended
     )
     row_far = gather_far(arrived)
-    normed_all = lax.all_gather(normed_own, "expert", axis=0)
-    attended_all = lax.all_gather(attended, "expert", axis=0)
+    normed_half = lax.all_gather(normed_own, "expert", axis=0, axis_index_groups=halves())
+    attended_half = lax.all_gather(attended, "expert", axis=0, axis_index_groups=halves())
     by_expert = (local_experts, packed_rows)
     up_rows, up_act = call(
         upstream_kernel,
@@ -664,21 +674,28 @@
         ],
     )
     kept, got = scatter_terms(back)
+    first_grad, second_grad, token = call(
+        expert_grad_kernel,
+        "expert_gradients",
+        8,
+        [shaped(FULL, *w_in.shape), shaped(FULL, *w_out.shape), shaped(FULL, 8, 128)],
+        [slot_rows, activated, pre_grad, gates, up_rows],
+    )
+    got, token = together(got, token)
+    back = add(kept, got).reshape(ranks, slab, model_width)
+    back, activated = together(back, activated)
+    back = exchange(back)
     returned = call(
         expert_out_kernel,
         "expert_outputs",
-        3,
+        12,
         [shaped(LOW, ranks * slab, model_width)] * dps,
         [pack_t, w_out, activated],
         scratch=[pltpu.VMEM((*by_expert, model_width), LOW)],
     )
     returned = scatter_near(returned)
-    got, returned = together(got, returned)
-    back = add(kept, got).reshape(ranks, slab, model_width)
-    back = exchange(back)
+    back, returned = together(back, returned)
     returned = add(*scatter_far(returned)).reshape(ranks, slab, model_width)
-    back, returned = together(back, returned)
-    returned = exchange(returned)
 
     bias_rows = -(-head_count // 6)
     small_rows = -(-(experts_total + 2 + bias_rows) // 8) * 8
@@ -689,7 +706,7 @@
         [
             shaped(FULL, length, model_width),
             shaped(FULL, small_rows, model_width),
-            shaped(LOW, ranks, 4 * columns_here, length),
+            shaped(LOW, ranks // 2, 2, 4 * columns_here, length),
         ],
         [
             tokens,
@@ -715,41 +732,39 @@
         [back],
     )
 
-    factors, small, returned, activated = together(factors, small, returned, activated)
-    factors = exchange(factors)
-    first_grad, second_grad, token = call(
-        expert_grad_kernel,
-        "expert_gradients",
-        8,
-        [shaped(FULL, *w_in.shape), shaped(FULL, *w_out.shape), shaped(FULL, 8, 128)],
-        [slot_rows, activated, pre_grad, gates, up_rows],
-    )
-    *steps, one_but_last, last = sum_steps()
+    factors, small, returned = together(factors, small, returned)
+    factors = lax.all_to_all(
+        factors, "expert", split_axis=0, concat_axis=0, tiled=True, axis_index_groups=halves()
+    )
+    first, *steps, one_but_last, last = sum_steps()
+    small = small + swap(small, *first)
+    small, returned = together(small, returned)
+    returned = exchange(returned)
     for axis, bit in steps:
         small = small + swap(small, axis, bit)
-    factors, small, token = together(factors, small, token)
+    factors, small = together(factors, small)
     small = small + swap(small, *one_but_last)
-    output, *grads = call(
+    grads = call(
         product_kernel,
         "weight_gradients",
         5,
-        [shaped(LOW, length, model_width)] + [shaped(LOW, rows_here, 4 * columns_here)] * dps,
-        [
-            normed_all,
-            attended_all,
-            hidden,
-            chance,
-            hits,
-            mask,
-            factors,
-            returned,
-            token,
-        ],
-        scratch=[pltpu.VMEM((dps, rows_here, 4 * columns_here), FULL)],
+        [shaped(LOW, 2, rows_here, 4 * columns_here)] * dps,
+        [normed_half, attended_half, factors, token],
+        scratch=[pltpu.VMEM((2, dps, rows_here, 4 * columns_here), FULL)],
     )
     grads, small = together(scatter_near(grads), small)
     small = small + swap(small, *last)
-    grads = add(*scatter_far(grads), FULL)
+    (output,) = call(
+        output_kernel,
+        "output_rows",
+        2,
+        [shaped(LOW, length, model_width)],
+        [hidden, chance, hits, mask, returned],
+    )
+    kept, got = scatter_far(grads)
+    got, output = together(got, output)
+    other = swap(add(kept[1], got[1]), "expert", ranks // 2)
+    grads = kept[0].astype(FULL) + got[0].astype(FULL) + other.astype(FULL)
     g_query, g_key, g_value, g_output = (
         grads[:, i * columns_here : (i + 1) * columns_here] for i in range(4)
     )

time: 216 us -> 225 us (1.042)
  blocking collectives: 0 us -> 39.5 us
  waiting for transfers between devices: 81.1 us -> 59.3 us
  between operations: 14.4 us -> 1.04 us
    all_gather x0 -> x2, blocking collectives: none -> 39.5 us  [the longest x1 22.6 us: per_device(): lax.all_gather(normed_own, 'expert', axis=0, axis_index_groups=halves())]
    ppermute x31 -> x32, waiting for transfers between devices: 48.9 us -> 37.9 us  [swap(): return lax.ppermute(value, axis, [(i, i ^ mask) for i in range(count)])]
    all_to_all x5 -> x4, waiting for transfers between devices: 32.1 us -> 21.4 us  [exchange(): lax.all_to_all(value, 'expert', split_axis=0, concat_axis=0, tiled=True)]
    all_to_all x0 -> x1, starting transfers between devices: none -> 3.49 us  [per_device(): lax.all_to_all(factors, 'expert', split_axis=0, concat_axis=0, tiled=True...]
    all_to_all x5 -> x4, starting transfers between devices: 24.7 us -> 22.6 us  [exchange(): lax.all_to_all(value, 'expert', split_axis=0, concat_axis=0, tiled=True)]
    pallas_call x8 -> x9, Pallas kernels: 56.7 us -> 58.1 us  [call(): pl.pallas_call(kernel, out_shape=tuple(out_shape), in_specs=[VMEM] * len(...]
    convert_element_type x7 -> x8, other arithmetic: 5.66 us -> 6.85 us  [add(): return (left.astype(FULL) + right.astype(FULL)).astype(dtype)]
    ppermute x31 -> x32, starting transfers between devices: 23.1 us -> 23.6 us  [swap(): return lax.ppermute(value, axis, [(i, i ^ mask) for i in range(count)])]
  transfers between devices with their start and end apart: 38 -> 37, of which waited for: 20 -> 16; matrix products, arithmetic and copies ran while one was open for 4% -> 4% of each run, Pallas kernels for 24% -> 18%
where the time goes in v9:
time: 225 us; the launch traced here: 224 us
  waiting for transfers between devices  59.3 us (26%)
  Pallas kernels  58.1 us (26%)
  starting transfers between devices  49.7 us (22%)
  blocking collectives  39.5 us (18%)
  other arithmetic  8.79 us (4%)
  local copies, waits for them, and re-layouts  7.64 us (3%)
    pallas_call x9, Pallas kernels, call(): pl.pallas_call(kernel, out_shape=tuple(out_shape), in_specs=[VMEM] * len(...  58.1 us
    ppermute x32, waiting for transfers between devices, swap(): return lax.ppermute(value, axis, [(i, i ^ mask) for i in range(count)])  37.9 us
    ppermute x32, starting transfers between devices, swap(): return lax.ppermute(value, axis, [(i, i ^ mask) for i in range(count)])  23.6 us
    all_to_all x4, starting transfers between devices, exchange(): lax.all_to_all(value, 'expert', split_axis=0, concat_axis=0, tiled=True)  22.6 us
    all_gather x1, blocking collectives, per_device(): lax.all_gather(normed_own, 'expert', axis=0, axis_index_groups=halves())  22.6 us
    all_to_all x4, waiting for transfers between devices, exchange(): lax.all_to_all(value, 'expert', split_axis=0, concat_axis=0, tiled=True)  21.4 us
    all_gather x1, blocking collectives, per_device(): lax.all_gather(attended, 'expert', axis=0, axis_index_groups=halves())  17 us
    convert_element_type x8, other arithmetic, add(): return (left.astype(FULL) + right.astype(FULL)).astype(dtype)  6.85 us
  transfers between devices with their start and end apart: 37, of which 16 were waited for; matrix products, arithmetic and copies ran while one was open for 4% of the time, Pallas kernels for 18%

profile of v9, /device:TPU:0, one launch (start us, length us, event | category | flops | bytes accessed | tf_op | source)
XLA Modules:
  0.0 224.0 jit_solution(13674139237229358938)
XLA Ops:
  0.6 1.0 maximum_bitcast_fusion
  1.7 3.1 %collective-permute-start = (bf16[1,192,384]{2,1,0:T(8,128)(2,1)S(1)}, bf16[1,192,384]{2,1,0:T(8,128)(2,1)S(1)}, u32[]{:S(2)}, u32[]{:S(2)}) collective-permute-start(bf16[1,192,384]{2,1,0:T(8,128)(2,1)S(1)} %maximum_bitcast_fusion), channel_id=1, source_target_pairs={{0,2},{1,3},{2,0},{3,1},{4,6},{5,7},{6,4},{7,5},{8,10},{9,11},{10,... | collective-permute-start | bytes 442376 | tf_op jit(solution)/shard_map/ppermute | solution.py:52
  4.7 2.6 %collective-permute-start.1 = (bf16[1,192,384]{2,1,0:T(8,128)(2,1)S(1)}, bf16[1,192,384]{2,1,0:T(8,128)(2,1)S(1)}, u32[]{:S(2)}, u32[]{:S(2)}) collective-permute-start(bf16[1,192,384]{2,1,0:T(8,128)(2,1)S(1)} %maximum_bitcast_fusion), channel_id=1, source_target_pairs={{0,4},{1,5},{2,6},{3,7},{4,0},{5,1},{6,2},{7,3},{8,12},{9,13},{10,... | collective-permute-start | bytes 442376 | tf_op jit(solution)/shard_map/ppermute | solution.py:52
  9.3 3.4 %early.1 = (bf16[128,768]{1,0:T(8,128)(2,1)}, f32[128,16]{1,0:T(8,128)}, bf16[128,192]{1,0:T(8,128)(2,1)}, bf16[192,128]{1,0:T(8,128)(2,1)}, f32[12,128,128]{2,1,0:T(8,128)}, /*index=5*/bf16[8,24,768]{2,1,0:T(8,128)(2,1)}) custom-call(bf16[128,768]{1,0:T(8,128)(2,1)} %tokens_ref.5, s32[1,128]{1,0:T(1,128)} %bitcast.31, ...), custom_call_target="tpu_custom_call" | custom-call | bytes 10800000 | tf_op jit(solution)/shard_map/early/pallas_call | solution.py:539
  12.7 6.1 %collective-permute-done.1 = bf16[1,192,384]{2,1,0:T(8,128)(2,1)S(1)} collective-permute-done((bf16[1,192,384]{2,1,0:T(8,128)(2,1)S(1)}, bf16[1,192,384]{2,1,0:T(8,128)(2,1)S(1)}, u32[]{:S(2)}, u32[]{:S(2)}) %collective-permute-start.1) | collective-permute-done | bytes 147488 | tf_op jit(solution)/shard_map/ppermute | solution.py:52
  18.9 1.6 collective-permute-start.7
  20.5 1.5 collective-permute-start.3
  22.0 3.7 %collective-permute-done.7 = bf16[1,4,96,384]{3,2,1,0:T(8,128)(2,1)S(1)} collective-permute-done((bf16[1,4,96,384]{3,2,1,0:T(8,128)(2,1)S(1)}, bf16[1,4,96,384]{3,2,1,0:T(8,128)(2,1)S(1)}, u32[]{:S(2)}, u32[]{:S(2)}) %collective-permute-start.7) | collective-permute-done | bytes 294944 | tf_op jit(solution)/shard_map/ppermute | solution.py:52
  25.8 1.6 collective-permute-start.9
  27.3 2.5 %collective-permute-done.3 = bf16[1,4,96,384]{3,2,1,0:T(8,128)(2,1)S(1)} collective-permute-done((bf16[1,4,96,384]{3,2,1,0:T(8,128)(2,1)S(1)}, bf16[1,4,96,384]{3,2,1,0:T(8,128)(2,1)S(1)}, u32[]{:S(2)}, u32[]{:S(2)}) %collective-permute-start.3) | collective-permute-done | bytes 294944 | tf_op jit(solution)/shard_map/ppermute | solution.py:52
  30.6 9.3 %collective-permute-done.9.rest_6_ = bf16[2,4,96,384]{3,2,1,0:T(8,128)(2,1)S(1)} collective-permute-done((bf16[2,4,96,384]{3,2,1,0:T(8,128)(2,1)S(1)}, bf16[2,4,96,384]{3,2,1,0:T(8,128)(2,1)S(1)}, u32[]{:S(2)}, u32[]{:S(2)}) %collective-permute-start.9) | collective-permute-done | bytes 589856 | tf_op jit(solution)/shard_map/ppermute | solution.py:52
  40.4 1.5 collective-permute-done.10.rest_7_
  43.5 6.3 %all-to-all-start = ((bf16[8,24,768]{2,1,0:T(8,128)(2,1)}), bf16[8,24,768]{2,1,0:T(8,128)(2,1)}, u32[]{:S(2)}, u32[]{:S(2)}) async-start(bf16[8,24,768]{2,1,0:T(8,128)(2,1)} %get-tuple-element.114), calls=%async_computation | async-start | bytes 589824 | tf_op jit(solution)/shard_map/all_to_all | solution.py:60
  49.9 9.9 %attention_forward.1 = (bf16[3,768,128]{2,1,0:T(8,128)(2,1)}, f32[12,128,128]{2,1,0:T(8,128)}, bf16[128,768]{1,0:T(8,128)(2,1)}, f32[128,768]{1,0:T(8,128)}, f32...) custom-call(bf16[128,768]{1,0:T(8,128)(2,1)} %tokens_ref.5, bf16[128,768]{1,0:T(8,128)(2,1)} %get-tuple-element.118.normed_ref, ...), custom_call_target="tpu_custom_call" | custom-call | bytes 36000000 | tf_op jit(solution)/shard_map/attention_forward/pallas_call | solution.py:539
  59.8 1.0 collective-permute-start.12
  60.8 6.0 %all-to-all-start.1 = ((bf16[8,24,768]{2,1,0:T(8,128)(2,1)}), bf16[8,24,768]{2,1,0:T(8,128)(2,1)S(1)}, u32[]{:S(2)}, u32[]{:S(2)}) async-start(bf16[8,24,768]{2,1,0:T(8,128)(2,1)} %get-tuple-element.115), calls=%async_computation.1 | async-start | bytes 589824 | tf_op jit(solution)/shard_map/all_to_all | solution.py:60
  66.8 2.0 collective-permute-done.12.rest_2_
  68.9 7.0 %all-to-all-done.1 = bf16[8,24,768]{2,1,0:T(8,128)(2,1)S(1)} async-done(((bf16[8,24,768]{2,1,0:T(8,128)(2,1)}), bf16[8,24,768]{2,1,0:T(8,128)(2,1)S(1)}, u32[]{:S(2)}, u32[]{:S(2)}) %all-to-all-start.1) | async-done | bytes 294944 | tf_op jit(solution)/shard_map/all_to_all | solution.py:60
  75.9 1.1 collective-permute-start.14
  77.0 4.5 %upstream_rows.1 = (bf16[2,320,768]{2,1,0:T(8,128)(2,1)}, f32[2,320,768]{2,1,0:T(8,128)}) custom-call(bf16[160,192]{1,0:T(8,128)(2,1)} %constant.8.clone.pack_ref, bf16[2,768,768]{2,1,0:T(8,128)(2,1)} %w_out_ref.3, bf16[192,768]{1,0:T(8,128)(2,1)} %bitcast.6.rest_0_, bf16[192,768]{1,0:T(8,128)(2,1)} %copy-done.15, bf16[192,768]{1,0:T(8,128)(2,1)} %copy-done.13, ...), custom_call_target="tpu_custom_call" | custom-call | bytes 18000000 | tf_op jit(solution)/shard_map/upstream_rows/pallas_call | solution.py:539
  81.4 1.2 collective-permute-done.14.rest_2_
  83.2 1.1 collective-permute-done.15.rest_1_
  85.7 9.9 %experts.1 = (bf16[192,768]{1,0:T(8,128)(2,1)}, bf16[192,768]{1,0:T(8,128)(2,1)}, bf16[192,768]{1,0:T(8,128)(2,1)}, bf16[192,768]{1,0:T(8,128)(2,1)}, bf16[2,320...) custom-call(bf16[160,192]{1,0:T(8,128)(2,1)} %constant.8.clone.pack_re, ...), custom_call_target="tpu_custom_call" | custom-call | bytes 36000000 | tf_op jit(solution)/shard_map/experts/pallas_call | solution.py:539
  95.7 1.7 collective-permute-done.18
  97.4 1.1 add_convert_fusion.6
  98.5 1.1 collective-permute-start.19
  99.6 8.2 %expert_gradients.1 = (f32[2,768,768]{2,1,0:T(8,128)}, f32[2,768,768]{2,1,0:T(8,128)}, f32[8,128]{1,0:T(8,128)}) custom-call(bf16[2,320,768]{2,1,0:T(8,128)(2,1)} %get-tuple-element.138.rows_ref, bf16[2,320,768]{2,1,0:T(8,128)(2,1)} %get-tuple-element.146.act_ref, bf16[2,320,768]{2,1,0:T(8,128)(2,1)} %get-tuple-element.140.pre_grad_ref, ...), custom_call_target="tpu_custom_call" | custom-call | bytes 28800000 | tf_op jit(solution)/shard_map/expert_gradients/pallas_call | solution.py:539
  108.6 4.0 %expert_outputs.1 = (bf16[192,768]{1,0:T(8,128)(2,1)}, bf16[192,768]{1,0:T(8,128)(2,1)}, bf16[192,768]{1,0:T(8,128)(2,1)}, bf16[192,768]{1,0:T(8,128)(2,1)}) custom-call(bf16[192,160]{1,0:T(8,128)(2,1)} %constant.9.clone.pack_t_ref, bf16[2,768,768]{2,1,0:T(8,128)(2,1)} %w_out_ref.3, bf16[2,320,768]{2,1,0:T(8,128)(2,1)} %get-tuple-element.146.act_ref), custom_call_target="tpu_custom_call" | custom-call | bytes 43200000 | tf_op jit(solution)/shard_map/expert_outputs/pallas_call | solution.py:539
  113.1 5.1 %all-to-all-start.2 = ((bf16[8,24,768]{2,1,0:T(8,128)(2,1)}), bf16[8,24,768]{2,1,0:T(8,128)(2,1)S(1)}, u32[]{:S(2)}, u32[]{:S(2)}) async-start(bf16[8,24,768]{2,1,0:T(8,128)(2,1)} %bitcast.10), calls=%async_computation.2 | async-start | bytes 589824 | tf_op jit(solution)/shard_map/all_to_all | solution.py:60
  118.3 1.0 add_convert_fusion.3
  119.3 1.0 add_convert_fusion.4
  120.3 8.2 %all-to-all-done.2.rest_8_ = bf16[8,24,768]{2,1,0:T(8,128)(2,1)S(1)} async-done(((bf16[8,24,768]{2,1,0:T(8,128)(2,1)}), bf16[8,24,768]{2,1,0:T(8,128)(2,1)S(1)}, u32[]{:S(2)}, u32[]{:S(2)}) %all-to-all-start.2) | async-done | bytes 294944 | tf_op jit(solution)/shard_map/all_to_all | solution.py:60
  129.5 11.9 %attention_backward.1 = (f32[128,768]{1,0:T(8,128)}, f32[24,768]{1,0:T(8,128)}, bf16[4,2,384,128]{3,2,1,0:T(8,128)(2,1)}) custom-call(bf16[128,768]{1,0:T(8,128)(2,1)} %tokens_ref.5, f32[2,768]{1,0:T(2,128)} %maximum_convert_fusion.gain_ref, bf16[16,768]{1,0:T(8,128)(2,1)} %bitcast.29, f32[128,16]{1,0:T(8,128)} %get-tuple-element.101.hits_ref, ...), custom_call_target="tpu_custom_call" | custom-call | bytes 43200000 | tf_op jit(solution)/shard_map/attention_backward/pallas_call | solution.py:539
  142.2 3.5 %all-to-all-start.3 = ((bf16[4,2,384,128]{3,2,1,0:T(8,128)(2,1)}), bf16[4,2,384,128]{3,2,1,0:T(8,128)(2,1)S(1)}, u32[]{:S(2)}, u32[]{:S(2)}) async-start(bf16[4,2,384,128]{3,2,1,0:T(8,128)(2,1)} %get-tuple-element.156), calls=%async_computation.3 | async-start | bytes 1572864 | tf_op jit(solution)/shard_map/all_to_all | solution.py:736
  145.8 1.3 collective-permute-done.23
  147.1 1.1 collective-permute-start.24
  148.2 22.6 %all-gather = bf16[512,768]{1,0:T(8,128)(2,1)} all-gather(bf16[128,768]{1,0:T(8,128)(2,1)S(1)} %copy-done.12), channel_id=2, replica_groups={{0,1,2,3},{4,5,6,7},{8,9,10,11},{12,13,14,15},{16,17,18,19},{20,21,22,2..., dimensions={0}, use_global_device_ids=true | all-gather | bytes 983040 | tf_op jit(solution)/shard_map/all_gather | solution.py:645
  170.9 17.0 %all-gather.1 = bf16[512,768]{1,0:T(8,128)(2,1)} all-gather(bf16[128,768]{1,0:T(8,128)(2,1)S(1)} %copy-done.20), channel_id=3, replica_groups={{0,1,2,3},{4,5,6,7},{8,9,10,11},{12,13,14,15},{16,17,18,19},{20,21,22,2..., dimensions={0}, use_global_device_ids=true | all-gather | bytes 983040 | tf_op jit(solution)/shard_map/all_gather | solution.py:646
  188.8 4.3 %weight_gradients.1 = (bf16[2,192,384]{2,1,0:T(8,128)(2,1)}, bf16[2,192,384]{2,1,0:T(8,128)(2,1)}, bf16[2,192,384]{2,1,0:T(8,128)(2,1)}, bf16[2,192,384]{2,1,0:T(8,128)(2,1)}) custom-call(bf16[4,128,768]{2,1,0:T(8,128)(2,1)} %bitcast.23, bf16[4,128,768]{2,1,0:T(8,128)(2,1)} %bitcast.24, bf16[4,2,384,128]{3,2,1,0:T(8,128)(2,1)} %copy-done.2, ...), custom_call_target="tpu_custom_call" | custom-call | bytes 18000000 | tf_op jit(solution)/shard_map/weight_gradients/pallas_call | solution.py:539
  193.1 1.1 collective-permute-start.28
  194.4 5.2 %all-to-all-start.4 = ((bf16[8,24,768]{2,1,0:T(8,128)(2,1)}), bf16[8,24,768]{2,1,0:T(8,128)(2,1)S(1)}, u32[]{:S(2)}, u32[]{:S(2)}) async-start(bf16[8,24,768]{2,1,0:T(8,128)(2,1)} %bitcast.11), calls=%async_computation.4 | async-start | bytes 589824 | tf_op jit(solution)/shard_map/all_to_all | solution.py:60
  199.6 1.0 add_convert_fusion
  200.7 1.0 add_convert_fusion.1
  201.7 3.0 %collective-permute-start.30 = (f32[24,768]{1,0:T(8,128)S(1)}, f32[24,768]{1,0:T(8,128)S(1)}, u32[]{:S(2)}, u32[]{:S(2)}) collective-permute-start(f32[24,768]{1,0:T(8,128)S(1)} %add.63), channel_id=1, source_target_pairs={{0,4},{1,5},{2,6},{3,7},{4,0},{5,1},{6,2},{7,3},{8,12},{9,13},{10,... | collective-permute-start | bytes 221192 | tf_op jit(solution)/shard_map/ppermute | solution.py:52
  204.7 1.1 collective-permute-start.29
  205.8 6.2 %all-to-all-done.4.returned_ref = bf16[8,24,768]{2,1,0:T(8,128)(2,1)S(1)} async-done(((bf16[8,24,768]{2,1,0:T(8,128)(2,1)}), bf16[8,24,768]{2,1,0:T(8,128)(2,1)S(1)}, u32[]{:S(2)}, u32[]{:S(2)}) %all-to-all-start.4) | async-done | bytes 294944 | tf_op jit(solution)/shard_map/all_to_all | solution.py:60
  212.7 2.1 output_rows.1
  216.8 6.4 %collective-permute-done.31 = bf16[192,384]{1,0:T(8,128)(2,1)S(1)} collective-permute-done((bf16[192,384]{1,0:T(8,128)(2,1)S(1)}, bf16[192,384]{1,0:T(8,128)(2,1)S(1)}, u32[]{:S(2)}, u32[]{:S(2)}) %collective-permute-start.31) | collective-permute-done | bytes 147488 | tf_op jit(solution)/shard_map/ppermute | solution.py:52
  (109 shorter events, 15.3 us)
Async XLA Ops:
  1.7 11.0 %collective-permute-start = (bf16[1,192,384]{2,1,0:T(8,128)(2,1)S(1)}, bf16[1,192,384]{2,1,0:T(8,128)(2,1)S(1)}, u32[]{:S(2)}, u32[]{:S(2)}) collective-permute-start(bf16[1,192,384]{2,1,0:T(8,128)(2,1)S(1)} %maximum_bitcast_fusion), channel_id=1, source_target_pairs={{0,2},{1,3},{2,0},{3,1},{4,6},{5,7},{6,4},{7,5},{8,10},{9,11},{10,... | collective-permute-start | bytes 442376 | tf_op jit(solution)/shard_map/ppermute | solution.py:52
  4.7 14.0 %collective-permute-start.1 = (bf16[1,192,384]{2,1,0:T(8,128)(2,1)S(1)}, bf16[1,192,384]{2,1,0:T(8,128)(2,1)S(1)}, u32[]{:S(2)}, u32[]{:S(2)}) collective-permute-start(bf16[1,192,384]{2,1,0:T(8,128)(2,1)S(1)} %maximum_bitcast_fusion), channel_id=1, source_target_pairs={{0,4},{1,5},{2,6},{3,7},{4,0},{5,1},{6,2},{7,3},{8,12},{9,13},{10,... | collective-permute-start | bytes 442376 | tf_op jit(solution)/shard_map/ppermute | solution.py:52
  7.3 11.4 %collective-permute-start.2 = (bf16[1,192,384]{2,1,0:T(8,128)(2,1)S(1)}, bf16[1,192,384]{2,1,0:T(8,128)(2,1)S(1)}, u32[]{:S(2)}, u32[]{:S(2)}) collective-permute-start(bf16[1,192,384]{2,1,0:T(8,128)(2,1)S(1)} %maximum_bitcast_fusion), channel_id=1, source_target_pairs={{0,6},{1,7},{2,4},{3,5},{4,2},{5,3},{6,0},{7,1},{8,14},{9,15},{10,... | collective-permute-start | bytes 442376 | tf_op jit(solution)/shard_map/ppermute | solution.py:52
  18.9 6.8 %collective-permute-start.7 = (bf16[1,4,96,384]{3,2,1,0:T(8,128)(2,1)S(1)}, bf16[1,4,96,384]{3,2,1,0:T(8,128)(2,1)S(1)}, u32[]{:S(2)}, u32[]{:S(2)}) collective-permute-start(bf16[1,4,96,384]{3,2,1,0:T(8,128)(2,1)S(1)} %get-tuple-element.178), channel_id=1, source_target_pairs={{0,16},{8,24},{16,0},{24,8},{1,17},{9,25},{17,1},{25,9},{2,18},{10... | collective-permute-start | bytes 884744 | tf_op jit(solution)/shard_map/ppermute | solution.py:52
  20.5 9.3 %collective-permute-start.3 = (bf16[1,4,96,384]{3,2,1,0:T(8,128)(2,1)S(1)}, bf16[1,4,96,384]{3,2,1,0:T(8,128)(2,1)S(1)}, u32[]{:S(2)}, u32[]{:S(2)}) collective-permute-start(bf16[1,4,96,384]{3,2,1,0:T(8,128)(2,1)S(1)} %get-tuple-element.179), channel_id=1, source_target_pairs={{0,1},{1,0},{2,3},{3,2},{4,5},{5,4},{6,7},{7,6},{8,9},{9,8},{10,11... | collective-permute-start | bytes 884744 | tf_op jit(solution)/shard_map/ppermute | solution.py:52
  25.8 24.1 %copy-start = (bf16[2,4,96,384]{3,2,1,0:T(8,128)(2,1)}, bf16[2,4,96,384]{3,2,1,0:T(8,128)(2,1)S(1)}, u32[]{:S(2)}) copy-start(bf16[2,4,96,384]{3,2,1,0:T(8,128)(2,1)S(1)} %pad_maximum_fusion.2.rest_4_) | copy-start | bytes 1769476
  25.8 14.1 %collective-permute-start.9 = (bf16[2,4,96,384]{3,2,1,0:T(8,128)(2,1)S(1)}, bf16[2,4,96,384]{3,2,1,0:T(8,128)(2,1)S(1)}, u32[]{:S(2)}, u32[]{:S(2)}) collective-permute-start(bf16[2,4,96,384]{3,2,1,0:T(8,128)(2,1)S(1)} %pad_maximum_fusion.2.rest_4_), channel_id=1, source_target_pairs={{0,1},{1,0},{2,3},{3,2},{4,5},{5,4},{6,7},{7,6},{8,9},{9,8},{10,11... | collective-permute-start | bytes 1769480 | tf_op jit(solution)/shard_map/ppermute | solution.py:52
  29.9 19.9 %copy-start.1 = (bf16[2,4,96,384]{3,2,1,0:T(8,128)(2,1)}, bf16[2,4,96,384]{3,2,1,0:T(8,128)(2,1)S(1)}, u32[]{:S(2)}) copy-start(bf16[2,4,96,384]{3,2,1,0:T(8,128)(2,1)S(1)} %pad_maximum_fusion.1.rest_0_) | copy-start | bytes 1769476
  29.9 9.9 %collective-permute-start.5 = (bf16[2,4,96,384]{3,2,1,0:T(8,128)(2,1)S(1)}, bf16[2,4,96,384]{3,2,1,0:T(8,128)(2,1)S(1)}, u32[]{:S(2)}, u32[]{:S(2)}) collective-permute-start(bf16[2,4,96,384]{3,2,1,0:T(8,128)(2,1)S(1)} %pad_maximum_fusion.1.rest_0_), channel_id=1, source_target_pairs={{0,16},{8,24},{16,0},{24,8},{1,17},{9,25},{17,1},{25,9},{2,18},{10... | collective-permute-start | bytes 1769480 | tf_op jit(solution)/shard_map/ppermute | solution.py:52
  30.0 10.4 %collective-permute-start.8 = (bf16[2,4,96,384]{3,2,1,0:T(8,128)(2,1)S(1)}, bf16[2,4,96,384]{3,2,1,0:T(8,128)(2,1)S(1)}, u32[]{:S(2)}, u32[]{:S(2)}) collective-permute-start(bf16[2,4,96,384]{3,2,1,0:T(8,128)(2,1)S(1)} %pad_maximum_fusion.2.rest_4_), channel_id=1, source_target_pairs={{0,8},{8,0},{16,24},{24,16},{1,9},{9,1},{17,25},{25,17},{2,10},{10... | collective-permute-start | bytes 1769480 | tf_op jit(solution)/shard_map/ppermute | solution.py:52
  30.1 10.3 %collective-permute-start.4 = (bf16[2,4,96,384]{3,2,1,0:T(8,128)(2,1)S(1)}, bf16[2,4,96,384]{3,2,1,0:T(8,128)(2,1)S(1)}, u32[]{:S(2)}, u32[]{:S(2)}) collective-permute-start(bf16[2,4,96,384]{3,2,1,0:T(8,128)(2,1)S(1)} %pad_maximum_fusion.1.rest_0_), channel_id=1, source_target_pairs={{0,8},{8,0},{16,24},{24,16},{1,9},{9,1},{17,25},{25,17},{2,10},{10... | collective-permute-start | bytes 1769480 | tf_op jit(solution)/shard_map/ppermute | solution.py:52
  39.9 10.0 %copy-start.3 = (bf16[2,4,96,384]{3,2,1,0:T(8,128)(2,1)}, bf16[2,4,96,384]{3,2,1,0:T(8,128)(2,1)S(1)}, u32[]{:S(2)}) copy-start(bf16[2,4,96,384]{3,2,1,0:T(8,128)(2,1)S(1)} %collective-permute-done.9.rest_6_) | copy-start | bytes 1769476
  39.9 2.0 collective-permute-start.10
  39.9 10.0 %copy-start.4 = (bf16[2,4,96,384]{3,2,1,0:T(8,128)(2,1)}, bf16[2,4,96,384]{3,2,1,0:T(8,128)(2,1)S(1)}, u32[]{:S(2)}) copy-start(bf16[2,4,96,384]{3,2,1,0:T(8,128)(2,1)S(1)} %collective-permute-done.5.rest_2_) | copy-start | bytes 1769476
  39.9 2.8 %collective-permute-start.6 = (bf16[2,4,96,384]{3,2,1,0:T(8,128)(2,1)S(1)}, bf16[2,4,96,384]{3,2,1,0:T(8,128)(2,1)S(1)}, u32[]{:S(2)}, u32[]{:S(2)}) collective-permute-start(bf16[2,4,96,384]{3,2,1,0:T(8,128)(2,1)S(1)} %collective-permute-done.5.rest_2_), channel_id=1, source_target_pairs={{0,8},{8,0},{16,24},{24,16},{1,9},{9,1},{17,25},{25,17},{2,10},{10... | collective-permute-start | bytes 1769480 | tf_op jit(solution)/shard_map/ppermute | solution.py:52
  40.4 9.5 %copy-start.5 = (bf16[2,4,96,384]{3,2,1,0:T(8,128)(2,1)}, bf16[2,4,96,384]{3,2,1,0:T(8,128)(2,1)S(1)}, u32[]{:S(2)}) copy-start(bf16[2,4,96,384]{3,2,1,0:T(8,128)(2,1)S(1)} %collective-permute-done.8.rest_5_) | copy-start | bytes 1769476
  40.4 9.5 %copy-start.6 = (bf16[2,4,96,384]{3,2,1,0:T(8,128)(2,1)}, bf16[2,4,96,384]{3,2,1,0:T(8,128)(2,1)S(1)}, u32[]{:S(2)}) copy-start(bf16[2,4,96,384]{3,2,1,0:T(8,128)(2,1)S(1)} %collective-permute-done.4.rest_1_) | copy-start | bytes 1769476
  43.5 16.3 %all-to-all-start = ((bf16[8,24,768]{2,1,0:T(8,128)(2,1)}), bf16[8,24,768]{2,1,0:T(8,128)(2,1)}, u32[]{:S(2)}, u32[]{:S(2)}) async-start(bf16[8,24,768]{2,1,0:T(8,128)(2,1)} %get-tuple-element.114), calls=%async_computation | async-start | bytes 589824 | tf_op jit(solution)/shard_map/all_to_all | solution.py:60
  59.8 9.0 %collective-permute-start.12 = (bf16[192,768]{1,0:T(8,128)(2,1)}, bf16[192,768]{1,0:T(8,128)(2,1)S(1)}, u32[]{:S(2)}, u32[]{:S(2)}) collective-permute-start(bf16[192,768]{1,0:T(8,128)(2,1)} %bitcast.6.rest_0_), channel_id=1, source_target_pairs={{0,16},{8,24},{16,0},{24,8},{1,17},{9,25},{17,1},{25,9},{2,18},{10... | collective-permute-start | bytes 884744 | tf_op jit(solution)/shard_map/ppermute | solution.py:52
  60.8 15.0 %all-to-all-start.1 = ((bf16[8,24,768]{2,1,0:T(8,128)(2,1)}), bf16[8,24,768]{2,1,0:T(8,128)(2,1)S(1)}, u32[]{:S(2)}, u32[]{:S(2)}) async-start(bf16[8,24,768]{2,1,0:T(8,128)(2,1)} %get-tuple-element.115), calls=%async_computation.1 | async-start | bytes 589824 | tf_op jit(solution)/shard_map/all_to_all | solution.py:60
  66.8 2.0 collective-permute-start.11
  68.8 8.1 %copy-start.13 = (bf16[192,768]{1,0:T(8,128)(2,1)}, bf16[192,768]{1,0:T(8,128)(2,1)S(1)}, u32[]{:S(2)}) copy-start(bf16[192,768]{1,0:T(8,128)(2,1)S(1)} %collective-permute-done.12.rest_2_) | copy-start | bytes 884740
  68.8 7.0 %collective-permute-start.13 = (bf16[192,768]{1,0:T(8,128)(2,1)S(1)}, bf16[192,768]{1,0:T(8,128)(2,1)S(1)}, u32[]{:S(2)}, u32[]{:S(2)}) collective-permute-start(bf16[192,768]{1,0:T(8,128)(2,1)S(1)} %collective-permute-done.12.rest_2_), channel_id=1, source_target_pairs={{0,8},{8,0},{16,24},{24,16},{1,9},{9,1},{17,25},{25,17},{2,10},{10... | collective-permute-start | bytes 884744 | tf_op jit(solution)/shard_map/ppermute | solution.py:52
  68.8 8.1 %copy-start.15 = (bf16[192,768]{1,0:T(8,128)(2,1)}, bf16[192,768]{1,0:T(8,128)(2,1)S(1)}, u32[]{:S(2)}) copy-start(bf16[192,768]{1,0:T(8,128)(2,1)S(1)} %collective-permute-done.11.rest_1_) | copy-start | bytes 884740
  75.9 8.8 %copy-start.9 = (bf16[8,24,768]{2,1,0:T(8,128)(2,1)}, bf16[8,24,768]{2,1,0:T(8,128)(2,1)S(1)}, u32[]{:S(2)}) copy-start(bf16[8,24,768]{2,1,0:T(8,128)(2,1)S(1)} %all-to-all-done.1) | copy-start | bytes 884740
  75.9 6.8 %collective-permute-start.14 = (bf16[192,768]{1,0:T(8,128)(2,1)S(1)}, bf16[192,768]{1,0:T(8,128)(2,1)S(1)}, u32[]{:S(2)}, u32[]{:S(2)}) collective-permute-start(bf16[192,768]{1,0:T(8,128)(2,1)S(1)} %bitcast.25), channel_id=1, source_target_pairs={{0,16},{8,24},{16,0},{24,8},{1,17},{9,25},{17,1},{25,9},{2,18},{10... | collective-permute-start | bytes 884744 | tf_op jit(solution)/shard_map/ppermute | solution.py:52
  82.6 1.6 collective-permute-start.15
  82.7 2.0 collective-permute-start.16
  95.6 1.8 collective-permute-start.18
  97.4 10.4 %copy-start.19 = (bf16[192,768]{1,0:T(8,128)(2,1)S(1)}, bf16[192,768]{1,0:T(8,128)(2,1)}, u32[]{:S(2)}) copy-start(bf16[192,768]{1,0:T(8,128)(2,1)} %get-tuple-element.134) | copy-start | bytes 884740
  98.5 9.3 %collective-permute-start.19 = (bf16[192,768]{1,0:T(8,128)(2,1)S(1)}, bf16[192,768]{1,0:T(8,128)(2,1)S(1)}, u32[]{:S(2)}, u32[]{:S(2)}) collective-permute-start(bf16[192,768]{1,0:T(8,128)(2,1)S(1)} %add_convert_fusion.6), channel_id=1, source_target_pairs={{0,16},{8,24},{16,0},{24,8},{1,17},{9,25},{17,1},{25,9},{2,18},{10... | collective-permute-start | bytes 884744 | tf_op jit(solution)/shard_map/ppermute | solution.py:52
  99.6 8.2 %collective-permute-start.17 = (bf16[192,768]{1,0:T(8,128)(2,1)}, bf16[192,768]{1,0:T(8,128)(2,1)S(1)}, u32[]{:S(2)}, u32[]{:S(2)}) collective-permute-start(bf16[192,768]{1,0:T(8,128)(2,1)} %get-tuple-element.135), channel_id=1, source_target_pairs={{0,8},{8,0},{16,24},{24,16},{1,9},{9,1},{17,25},{25,17},{2,10},{10... | collective-permute-start | bytes 884744 | tf_op jit(solution)/shard_map/ppermute | solution.py:52
  112.6 5.6 %collective-permute-start.21 = (bf16[192,768]{1,0:T(8,128)(2,1)}, bf16[192,768]{1,0:T(8,128)(2,1)S(1)}, u32[]{:S(2)}, u32[]{:S(2)}) collective-permute-start(bf16[192,768]{1,0:T(8,128)(2,1)} %get-tuple-element.150), channel_id=1, source_target_pairs={{0,8},{8,0},{16,24},{24,16},{1,9},{9,1},{17,25},{25,17},{2,10},{10... | collective-permute-start | bytes 884744 | tf_op jit(solution)/shard_map/ppermute | solution.py:52
  113.1 6.2 %collective-permute-start.20 = (bf16[192,768]{1,0:T(8,128)(2,1)}, bf16[192,768]{1,0:T(8,128)(2,1)S(1)}, u32[]{:S(2)}, u32[]{:S(2)}) collective-permute-start(bf16[192,768]{1,0:T(8,128)(2,1)} %get-tuple-element.148), channel_id=1, source_target_pairs={{0,8},{8,0},{16,24},{24,16},{1,9},{9,1},{17,25},{25,17},{2,10},{10... | collective-permute-start | bytes 884744 | tf_op jit(solution)/shard_map/ppermute | solution.py:52
  113.1 15.4 %all-to-all-start.2 = ((bf16[8,24,768]{2,1,0:T(8,128)(2,1)}), bf16[8,24,768]{2,1,0:T(8,128)(2,1)S(1)}, u32[]{:S(2)}, u32[]{:S(2)}) async-start(bf16[8,24,768]{2,1,0:T(8,128)(2,1)} %bitcast.10), calls=%async_computation.2 | async-start | bytes 589824 | tf_op jit(solution)/shard_map/all_to_all | solution.py:60
  128.5 13.0 %collective-permute-start.22 = (bf16[192,768]{1,0:T(8,128)(2,1)S(1)}, bf16[192,768]{1,0:T(8,128)(2,1)S(1)}, u32[]{:S(2)}, u32[]{:S(2)}) collective-permute-start(bf16[192,768]{1,0:T(8,128)(2,1)S(1)} %add_convert_fusion.3), channel_id=1, source_target_pairs={{0,16},{8,24},{16,0},{24,8},{1,17},{9,25},{17,1},{25,9},{2,18},{10... | collective-permute-start | bytes 884744 | tf_op jit(solution)/shard_map/ppermute | solution.py:52
  141.4 29.4 %copy-start.20 = (bf16[128,768]{1,0:T(8,128)(2,1)S(1)}, bf16[128,768]{1,0:T(8,128)(2,1)}, u32[]{:S(2)}) copy-start(bf16[128,768]{1,0:T(8,128)(2,1)} %get-tuple-element.119) | copy-start | bytes 589828
  142.2 45.6 %all-to-all-start.3 = ((bf16[4,2,384,128]{3,2,1,0:T(8,128)(2,1)}), bf16[4,2,384,128]{3,2,1,0:T(8,128)(2,1)S(1)}, u32[]{:S(2)}, u32[]{:S(2)}) async-start(bf16[4,2,384,128]{3,2,1,0:T(8,128)(2,1)} %get-tuple-element.156), calls=%async_computation.3 | async-start | bytes 1572864 | tf_op jit(solution)/shard_map/all_to_all | solution.py:736
  145.8 1.3 collective-permute-start.23
  147.1 23.7 %collective-permute-start.24 = (f32[24,768]{1,0:T(8,128)S(1)}, f32[24,768]{1,0:T(8,128)S(1)}, u32[]{:S(2)}, u32[]{:S(2)}) collective-permute-start(f32[24,768]{1,0:T(8,128)S(1)} %add.58), channel_id=1, source_target_pairs={{0,16},{8,24},{16,0},{24,8},{1,17},{9,25},{17,1},{25,9},{2,18},{10... | collective-permute-start | bytes 221192 | tf_op jit(solution)/shard_map/ppermute | solution.py:52
  170.8 17.1 %collective-permute-start.25 = (f32[24,768]{1,0:T(8,128)S(1)}, f32[24,768]{1,0:T(8,128)S(1)}, u32[]{:S(2)}, u32[]{:S(2)}) collective-permute-start(f32[24,768]{1,0:T(8,128)S(1)} %add.59), channel_id=1, source_target_pairs={{0,1},{1,0},{2,3},{3,2},{4,5},{5,4},{6,7},{7,6},{8,9},{9,8},{10,11... | collective-permute-start | bytes 221192 | tf_op jit(solution)/shard_map/ppermute | solution.py:52
  193.1 6.5 %collective-permute-start.27 = (bf16[2,192,384]{2,1,0:T(8,128)(2,1)}, bf16[2,192,384]{2,1,0:T(8,128)(2,1)S(1)}, u32[]{:S(2)}, u32[]{:S(2)}) collective-permute-start(bf16[2,192,384]{2,1,0:T(8,128)(2,1)} %get-tuple-element.165), channel_id=1, source_target_pairs={{0,8},{8,0},{16,24},{24,16},{1,9},{9,1},{17,25},{25,17},{2,10},{10... | collective-permute-start | bytes 884744 | tf_op jit(solution)/shard_map/ppermute | solution.py:52
  193.1 6.5 %collective-permute-start.28 = (f32[24,768]{1,0:T(8,128)S(1)}, f32[24,768]{1,0:T(8,128)S(1)}, u32[]{:S(2)}, u32[]{:S(2)}) collective-permute-start(f32[24,768]{1,0:T(8,128)S(1)} %add.60), channel_id=1, source_target_pairs={{0,2},{1,3},{2,0},{3,1},{4,6},{5,7},{6,4},{7,5},{8,10},{9,11},{10,... | collective-permute-start | bytes 221192 | tf_op jit(solution)/shard_map/ppermute | solution.py:52
  194.2 6.5 %collective-permute-start.26 = (bf16[2,192,384]{2,1,0:T(8,128)(2,1)}, bf16[2,192,384]{2,1,0:T(8,128)(2,1)S(1)}, u32[]{:S(2)}, u32[]{:S(2)}) collective-permute-start(bf16[2,192,384]{2,1,0:T(8,128)(2,1)} %get-tuple-element.163), channel_id=1, source_target_pairs={{0,8},{8,0},{16,24},{24,16},{1,9},{9,1},{17,25},{25,17},{2,10},{10... | collective-permute-start | bytes 884744 | tf_op jit(solution)/shard_map/ppermute | solution.py:52
  194.4 17.6 %all-to-all-start.4 = ((bf16[8,24,768]{2,1,0:T(8,128)(2,1)}), bf16[8,24,768]{2,1,0:T(8,128)(2,1)S(1)}, u32[]{:S(2)}, u32[]{:S(2)}) async-start(bf16[8,24,768]{2,1,0:T(8,128)(2,1)} %bitcast.11), calls=%async_computation.4 | async-start | bytes 589824 | tf_op jit(solution)/shard_map/all_to_all | solution.py:60
  201.7 13.0 %collective-permute-start.30 = (f32[24,768]{1,0:T(8,128)S(1)}, f32[24,768]{1,0:T(8,128)S(1)}, u32[]{:S(2)}, u32[]{:S(2)}) collective-permute-start(f32[24,768]{1,0:T(8,128)S(1)} %add.63), channel_id=1, source_target_pairs={{0,4},{1,5},{2,6},{3,7},{4,0},{5,1},{6,2},{7,3},{8,12},{9,13},{10,... | collective-permute-start | bytes 221192 | tf_op jit(solution)/shard_map/ppermute | solution.py:52
  204.7 10.7 %collective-permute-start.29 = (bf16[2,192,384]{2,1,0:T(8,128)(2,1)S(1)}, bf16[2,192,384]{2,1,0:T(8,128)(2,1)S(1)}, u32[]{:S(2)}, u32[]{:S(2)}) collective-permute-start(bf16[2,192,384]{2,1,0:T(8,128)(2,1)S(1)} %add_convert_fusion), channel_id=1, source_target_pairs={{0,16},{8,24},{16,0},{24,8},{1,17},{9,25},{17,1},{25,9},{2,18},{10... | collective-permute-start | bytes 884744 | tf_op jit(solution)/shard_map/ppermute | solution.py:52
  215.5 7.7 %collective-permute-start.31 = (bf16[192,384]{1,0:T(8,128)(2,1)S(1)}, bf16[192,384]{1,0:T(8,128)(2,1)S(1)}, u32[]{:S(2)}, u32[]{:S(2)}) collective-permute-start(bf16[192,384]{1,0:T(8,128)(2,1)S(1)} %fusion), channel_id=1, source_target_pairs={{0,4},{1,5},{2,6},{3,7},{4,0},{5,1},{6,2},{7,3},{8,12},{9,13},{10,... | collective-permute-start | bytes 442376 | tf_op jit(solution)/shard_map/ppermute | solution.py:52
  (11 other events, 20.0 us)

commit v10 on v9

--- a/solution.py
+++ b/solution.py
@@ -260,7 +260,7 @@
 ):
     count = len(places)
     piece_refs, rest = rest[:count], rest[count:]
-    heads_ref, weights_ref, attended_ref, hidden_ref, chance_ref = rest[:5]
+    heads_ref, weights_ref, rows_ref, hidden_ref, chance_ref = rest[:5]
     slabs_ref = rest[5]
     w_ref, qkv_ref, att_t_ref, sem = rest[-4:]
     copies = place_weights(places, piece_refs, w_ref, sem)
@@ -288,7 +288,8 @@
         weights_ref[h] = weights
         att_t_ref[rows, :] = dot(heads_ref[2, rows, :], weights.astype(LOW), NT)
     attended = att_t_ref[...].T.astype(LOW)
-    attended_ref[...] = attended
+    rows_ref[0] = normed
+    rows_ref[1] = attended
     low_lane = 3 * cols // 128 * 128
     for e in range(ranks):
         turned = dot(attended, w_ref[e, :, low_lane:]).T
@@ -497,18 +498,19 @@
         small_ref[line : line + 1, place : place + sums.shape[1]] = sums[h : h + 1]
 
 
-def product_kernel(normed_ref, attended_ref, factors_ref, token_ref, *rest):
-    piece_refs, total_ref = rest[:-1], rest[-1]
+def product_kernel(factors_ref, token_ref, *rest):
     count, _, columns, length = factors_ref.shape
+    row_refs, piece_refs, total_ref = rest[:count], rest[count:-1], rest[-1]
     cols = columns // 4
     rows = total_ref.shape[2]
+    mine = lax.rem(lax.axis_index("expert"), count)
     for side in range(2):
         first, second = None, None
-        for e in range(count):
-            held = factors_ref[e, side].astype(FULL)
-            part = dot(held[: 3 * cols].astype(LOW), normed_ref[e])
+        for j, ref in enumerate(row_refs):
+            held = factors_ref[mine ^ j, side].astype(FULL)
+            part = dot(held[: 3 * cols].astype(LOW), ref[0])
             first = part if first is None else first + part
-            part = dot(held[3 * cols :].astype(LOW), attended_ref[e])
+            part = dot(held[3 * cols :].astype(LOW), ref[1])
             second = part if second is None else second + part
         total = jnp.concatenate([first, second], axis=0).T
         for j in range(len(piece_refs)):
@@ -613,14 +615,14 @@
     up_arrived = exchange(up_slabs).reshape(ranks * slab, model_width)
 
     w_shape = (ranks, inner_width, 4 * columns_here)
-    heads, weights, attended, hidden, chance, slabs = call(
+    heads, weights, rows, hidden, chance, slabs = call(
         functools.partial(forward_kernel, places, slab, rank_slots),
         "attention_forward",
         10,
         [
             shaped(LOW, 3, inner_width, length),
             shaped(FULL, head_count, length, length),
-            shaped(LOW, length, inner_width),
+            shaped(LOW, 2, length, inner_width),
             shaped(FULL, length, model_width),
             shaped(FULL, length, experts_total),
             slabs_shape,
@@ -638,12 +640,10 @@
     slabs, up_arrived = together(slabs, up_arrived)
     arrived = exchange(slabs).reshape(ranks * slab, model_width)
     up_pieces = gather_near(gather_far(up_arrived))
-    arrived, up_pieces, normed_own, attended = together(
-        arrived, up_pieces, normed_low, attended
-    )
+    arrived, up_pieces, rows = together(arrived, up_pieces, rows)
     row_far = gather_far(arrived)
-    normed_half = lax.all_gather(normed_own, "expert", axis=0, axis_index_groups=halves())
-    attended_half = lax.all_gather(attended, "expert", axis=0, axis_index_groups=halves())
+    half = ranks // 2
+    near_rows = [swap(rows, "expert", j) for j in range(1, half)]
     by_expert = (local_experts, packed_rows)
     up_rows, up_act = call(
         upstream_kernel,
@@ -681,7 +681,7 @@
         [shaped(FULL, *w_in.shape), shaped(FULL, *w_out.shape), shaped(FULL, 8, 128)],
         [slot_rows, activated, pre_grad, gates, up_rows],
     )
-    got, token = together(got, token)
+    got, token, near_rows = together(got, token, near_rows)
     back = add(kept, got).reshape(ranks, slab, model_width)
     back, activated = together(back, activated)
     back = exchange(back)
@@ -742,14 +742,14 @@
     returned = exchange(returned)
     for axis, bit in steps:
         small = small + swap(small, axis, bit)
-    factors, small = together(factors, small)
+    factors, small, returned = together(factors, small, returned)
     small = small + swap(small, *one_but_last)
     grads = call(
         product_kernel,
         "weight_gradients",
         5,
         [shaped(LOW, 2, rows_here, 4 * columns_here)] * dps,
-        [normed_half, attended_half, factors, token],
+        [factors, token, rows, *near_rows],
         scratch=[pltpu.VMEM((2, dps, rows_here, 4 * columns_here), FULL)],
     )
     grads, small = together(scatter_near(grads), small)

time: 225 us -> 214 us (0.951)
  blocking collectives: 39.5 us -> 14.2 us
  waiting for transfers between devices: 59.3 us -> 74.2 us
    all_gather x2 -> x0, blocking collectives: 39.5 us -> none  [the longest x1 22.6 us: per_device(): lax.all_gather(normed_own, 'expert', axis=0, axis_index_groups=halves())]
    ppermute x32 -> x35, waiting for transfers between devices: 37.9 us -> 59.4 us  [swap(): return lax.ppermute(value, axis, [(i, i ^ mask) for i in range(count)])]
    all_to_all x0 -> x1, blocking collectives: none -> 14.2 us  [exchange(): lax.all_to_all(value, 'expert', split_axis=0, concat_axis=0, tiled=True)]
    all_to_all x4 -> x3, starting transfers between devices: 22.6 us -> 15.5 us  [exchange(): lax.all_to_all(value, 'expert', split_axis=0, concat_axis=0, tiled=True)]
    ppermute x32 -> x35, starting transfers between devices: 23.6 us -> 30.4 us  [swap(): return lax.ppermute(value, axis, [(i, i ^ mask) for i in range(count)])]
    all_to_all x4 -> x3, waiting for transfers between devices: 21.4 us -> 14.8 us  [exchange(): lax.all_to_all(value, 'expert', split_axis=0, concat_axis=0, tiled=True)]
  transfers between devices with their start and end apart: 37 -> 39, of which waited for: 16 -> 20; matrix products, arithmetic and copies ran while one was open for 4% -> 4% of each run, Pallas kernels for 18% -> 19%
where the time goes in v10:
time: 214 us; the launch traced here: 213 us
  waiting for transfers between devices  74.2 us (35%)
  Pallas kernels  58 us (27%)
  starting transfers between devices  49.4 us (23%)
  blocking collectives  14.2 us (7%)
  other arithmetic  9 us (4%)
  local copies, waits for them, and re-layouts  6.91 us (3%)
    ppermute x35, waiting for transfers between devices, swap(): return lax.ppermute(value, axis, [(i, i ^ mask) for i in range(count)])  59.4 us
    pallas_call x9, Pallas kernels, call(): pl.pallas_call(kernel, out_shape=tuple(out_shape), in_specs=[VMEM] * len(...  58 us
    ppermute x35, starting transfers between devices, swap(): return lax.ppermute(value, axis, [(i, i ^ mask) for i in range(count)])  30.4 us
    all_to_all x3, starting transfers between devices, exchange(): lax.all_to_all(value, 'expert', split_axis=0, concat_axis=0, tiled=True)  15.5 us
    all_to_all x3, waiting for transfers between devices, exchange(): lax.all_to_all(value, 'expert', split_axis=0, concat_axis=0, tiled=True)  14.8 us
    all_to_all x1, blocking collectives, exchange(): lax.all_to_all(value, 'expert', split_axis=0, concat_axis=0, tiled=True)  14.2 us
    convert_element_type x8, other arithmetic, add(): return (left.astype(FULL) + right.astype(FULL)).astype(dtype)  6.17 us
  transfers between devices with their start and end apart: 39, of which 20 were waited for; matrix products, arithmetic and copies ran while one was open for 4% of the time, Pallas kernels for 19%

profile of v10, /device:TPU:0, one launch (start us, length us, event | category | flops | bytes accessed | tf_op | source)
XLA Modules:
  0.0 212.7 jit_solution(385949625343779920)
XLA Ops:
  1.7 5.1 %collective-permute-start.2 = (bf16[1,192,384]{2,1,0:T(8,128)(2,1)S(1)}, bf16[1,192,384]{2,1,0:T(8,128)(2,1)S(1)}, u32[]{:S(2)}, u32[]{:S(2)}) collective-permute-start(bf16[1,192,384]{2,1,0:T(8,128)(2,1)S(1)} %maximum_bitcast_fusion), channel_id=1, source_target_pairs={{0,6},{1,7},{2,4},{3,5},{4,2},{5,3},{6,0},{7,1},{8,14},{9,15},{10,... | collective-permute-start | bytes 442376 | tf_op jit(solution)/shard_map/ppermute | solution.py:52
  9.4 3.3 %early.1 = (bf16[128,768]{1,0:T(8,128)(2,1)}, f32[128,16]{1,0:T(8,128)}, bf16[128,192]{1,0:T(8,128)(2,1)}, bf16[192,128]{1,0:T(8,128)(2,1)}, f32[12,128,128]{2,1,0:T(8,128)}, /*index=5*/bf16[8,24,768]{2,1,0:T(8,128)(2,1)}) custom-call(bf16[128,768]{1,0:T(8,128)(2,1)} %tokens_ref.5, s32[1,128]{1,0:T(1,128)} %bitcast.28, ...), custom_call_target="tpu_custom_call" | custom-call | bytes 10800000 | tf_op jit(solution)/shard_map/early/pallas_call | solution.py:541
  12.7 6.5 %collective-permute-done.1 = bf16[1,192,384]{2,1,0:T(8,128)(2,1)S(1)} collective-permute-done((bf16[1,192,384]{2,1,0:T(8,128)(2,1)S(1)}, bf16[1,192,384]{2,1,0:T(8,128)(2,1)S(1)}, u32[]{:S(2)}, u32[]{:S(2)}) %collective-permute-start.1) | collective-permute-done | bytes 147488 | tf_op jit(solution)/shard_map/ppermute | solution.py:52
  19.4 1.6 collective-permute-start.3
  21.0 1.5 collective-permute-start.7
  22.5 5.1 %collective-permute-done.3 = bf16[1,4,96,384]{3,2,1,0:T(8,128)(2,1)S(1)} collective-permute-done((bf16[1,4,96,384]{3,2,1,0:T(8,128)(2,1)S(1)}, bf16[1,4,96,384]{3,2,1,0:T(8,128)(2,1)S(1)}, u32[]{:S(2)}, u32[]{:S(2)}) %collective-permute-start.3) | collective-permute-done | bytes 294944 | tf_op jit(solution)/shard_map/ppermute | solution.py:52
  27.6 1.6 collective-permute-start.5
  29.3 1.6 collective-permute-start.9
  31.4 10.0 %collective-permute-done.5.rest_2_ = bf16[2,4,96,384]{3,2,1,0:T(8,128)(2,1)S(1)} collective-permute-done((bf16[2,4,96,384]{3,2,1,0:T(8,128)(2,1)S(1)}, bf16[2,4,96,384]{3,2,1,0:T(8,128)(2,1)S(1)}, u32[]{:S(2)}, u32[]{:S(2)}) %collective-permute-start.5) | collective-permute-done | bytes 589856 | tf_op jit(solution)/shard_map/ppermute | solution.py:52
  41.4 1.1 collective-permute-done.9.rest_6_
  43.4 1.1 collective-permute-done.10.rest_7_
  45.4 4.3 %all-to-all-start = ((bf16[8,24,768]{2,1,0:T(8,128)(2,1)}), bf16[8,24,768]{2,1,0:T(8,128)(2,1)}, u32[]{:S(2)}, u32[]{:S(2)}) async-start(bf16[8,24,768]{2,1,0:T(8,128)(2,1)} %get-tuple-element.122), calls=%async_computation | async-start | bytes 589824 | tf_op jit(solution)/shard_map/all_to_all | solution.py:60
  49.8 9.9 %attention_forward.1 = (bf16[3,768,128]{2,1,0:T(8,128)(2,1)}, f32[12,128,128]{2,1,0:T(8,128)}, bf16[2,128,768]{2,1,0:T(8,128)(2,1)}, f32[128,768]{1,0:T(8,128)},...) custom-call(bf16[128,768]{1,0:T(8,128)(2,1)} %tokens_ref.5, bf16[128,768]{1,0:T(8,128)(2,1)} %get-tuple-element.104.normed_ref, ...), custom_call_target="tpu_custom_call" | custom-call | bytes 36000000 | tf_op jit(solution)/shard_map/attention_forward/pallas_call | solution.py:541
  59.7 1.1 collective-permute-start.12
  60.8 5.9 %all-to-all-start.1 = ((bf16[8,24,768]{2,1,0:T(8,128)(2,1)}), bf16[8,24,768]{2,1,0:T(8,128)(2,1)S(1)}, u32[]{:S(2)}, u32[]{:S(2)}) async-start(bf16[8,24,768]{2,1,0:T(8,128)(2,1)} %get-tuple-element.123), calls=%async_computation.1 | async-start | bytes 589824 | tf_op jit(solution)/shard_map/all_to_all | solution.py:60
  66.7 2.0 collective-permute-done.12.rest_2_
  68.7 7.1 %all-to-all-done.1 = bf16[8,24,768]{2,1,0:T(8,128)(2,1)S(1)} async-done(((bf16[8,24,768]{2,1,0:T(8,128)(2,1)}), bf16[8,24,768]{2,1,0:T(8,128)(2,1)S(1)}, u32[]{:S(2)}, u32[]{:S(2)}) %all-to-all-start.1) | async-done | bytes 294944 | tf_op jit(solution)/shard_map/all_to_all | solution.py:60
  76.8 4.5 %upstream_rows.1 = (bf16[2,320,768]{2,1,0:T(8,128)(2,1)}, f32[2,320,768]{2,1,0:T(8,128)}) custom-call(bf16[160,192]{1,0:T(8,128)(2,1)} %constant.8.clone.pack_ref, bf16[2,768,768]{2,1,0:T(8,128)(2,1)} %w_out_ref.3, bf16[192,768]{1,0:T(8,128)(2,1)} %bitcast.6.rest_0_, bf16[192,768]{1,0:T(8,128)(2,1)} %copy-done.17, bf16[192,768]{1,0:T(8,128)(2,1)} %copy-done.15, ...), custom_call_target="tpu_custom_call" | custom-call | bytes 18000000 | tf_op jit(solution)/shard_map/upstream_rows/pallas_call | solution.py:541
  81.3 1.3 collective-permute-done.14.rest_2_
  83.2 1.1 collective-permute-done.15.rest_1_
  85.7 9.9 %experts.1 = (bf16[192,768]{1,0:T(8,128)(2,1)}, bf16[192,768]{1,0:T(8,128)(2,1)}, bf16[192,768]{1,0:T(8,128)(2,1)}, bf16[192,768]{1,0:T(8,128)(2,1)}, bf16[2,320...) custom-call(bf16[160,192]{1,0:T(8,128)(2,1)} %constant.8.clone.pack_re, ...), custom_call_target="tpu_custom_call" | custom-call | bytes 36000000 | tf_op jit(solution)/shard_map/experts/pallas_call | solution.py:541
  95.8 1.5 collective-permute-start.20
  97.6 1.7 collective-permute-start.22
  99.3 1.1 add_convert_fusion.6
  101.3 8.2 %expert_gradients.1 = (f32[2,768,768]{2,1,0:T(8,128)}, f32[2,768,768]{2,1,0:T(8,128)}, f32[8,128]{1,0:T(8,128)}) custom-call(bf16[2,320,768]{2,1,0:T(8,128)(2,1)} %get-tuple-element.139.rows_ref, bf16[2,320,768]{2,1,0:T(8,128)(2,1)} %get-tuple-element.148.act_ref, bf16[2,320,768]{2,1,0:T(8,128)(2,1)} %get-tuple-element.141.pre_grad_ref, ...), custom_call_target="tpu_custom_call" | custom-call | bytes 28800000 | tf_op jit(solution)/shard_map/expert_gradients/pallas_call | solution.py:541
  109.5 7.2 %collective-permute-done.22.rest_3_ = bf16[2,128,768]{2,1,0:T(8,128)(2,1)S(1)} collective-permute-done((bf16[2,128,768]{2,1,0:T(8,128)(2,1)S(1)}, bf16[2,128,768]{2,1,0:T(8,128)(2,1)S(1)}, u32[]{:S(2)}, u32[]{:S(2)}) %collective-permute-start.22) | collective-permute-done | bytes 393248 | tf_op jit(solution)/shard_map/ppermute | solution.py:52
  117.6 4.0 %expert_outputs.1 = (bf16[192,768]{1,0:T(8,128)(2,1)}, bf16[192,768]{1,0:T(8,128)(2,1)}, bf16[192,768]{1,0:T(8,128)(2,1)}, bf16[192,768]{1,0:T(8,128)(2,1)}) custom-call(bf16[192,160]{1,0:T(8,128)(2,1)} %constant.9.clone.pack_t_ref, bf16[2,768,768]{2,1,0:T(8,128)(2,1)} %w_out_ref.3, bf16[2,320,768]{2,1,0:T(8,128)(2,1)} %get-tuple-element.148.act_ref), custom_call_target="tpu_custom_call" | custom-call | bytes 43200000 | tf_op jit(solution)/shard_map/expert_outputs/pallas_call | solution.py:541
  122.1 5.3 %all-to-all-start.2 = ((bf16[8,24,768]{2,1,0:T(8,128)(2,1)}), bf16[8,24,768]{2,1,0:T(8,128)(2,1)S(1)}, u32[]{:S(2)}, u32[]{:S(2)}) async-start(bf16[8,24,768]{2,1,0:T(8,128)(2,1)} %bitcast.8), calls=%async_computation.2 | async-start | bytes 589824 | tf_op jit(solution)/shard_map/all_to_all | solution.py:60
  129.5 7.7 %all-to-all-done.2.rest_8_ = bf16[8,24,768]{2,1,0:T(8,128)(2,1)S(1)} async-done(((bf16[8,24,768]{2,1,0:T(8,128)(2,1)}), bf16[8,24,768]{2,1,0:T(8,128)(2,1)S(1)}, u32[]{:S(2)}, u32[]{:S(2)}) %all-to-all-start.2) | async-done | bytes 294944 | tf_op jit(solution)/shard_map/all_to_all | solution.py:60
  137.9 11.9 %attention_backward.1 = (f32[128,768]{1,0:T(8,128)}, f32[24,768]{1,0:T(8,128)}, bf16[4,2,384,128]{3,2,1,0:T(8,128)(2,1)}) custom-call(bf16[128,768]{1,0:T(8,128)(2,1)} %tokens_ref.5, f32[2,768]{1,0:T(2,128)} %maximum_convert_fusion.gain_ref, bf16[16,768]{1,0:T(8,128)(2,1)} %bitcast.26, f32[128,16]{1,0:T(8,128)} %get-tuple-element.102.hits_ref, ...), custom_call_target="tpu_custom_call" | custom-call | bytes 43200000 | tf_op jit(solution)/shard_map/attention_backward/pallas_call | solution.py:541
  150.0 1.5 collective-permute-done.26
  152.4 14.2 %all_to_all.25.returned_ref = bf16[8,24,768]{2,1,0:T(8,128)(2,1)} all-to-all(bf16[8,24,768]{2,1,0:T(8,128)(2,1)S(1)} %bitcast.24), channel_id=1, replica_groups=mesh['dp'=4,'expert'=8] {'expert'}, dimensions={0} | all-to-all | bytes 589824 | tf_op jit(solution)/shard_map/all_to_all | solution.py:60
  166.6 3.5 %all-to-all-start.3 = ((bf16[4,2,384,128]{3,2,1,0:T(8,128)(2,1)}), bf16[4,2,384,128]{3,2,1,0:T(8,128)(2,1)S(1)}, u32[]{:S(2)}, u32[]{:S(2)}) async-start(bf16[4,2,384,128]{3,2,1,0:T(8,128)(2,1)} %get-tuple-element.158), calls=%async_computation.3 | async-start | bytes 1572864 | tf_op jit(solution)/shard_map/all_to_all | solution.py:736
  170.1 1.3 collective-permute-start.27
  171.4 3.1 %collective-permute-done.27 = f32[24,768]{1,0:T(8,128)S(1)} collective-permute-done((f32[24,768]{1,0:T(8,128)S(1)}, f32[24,768]{1,0:T(8,128)S(1)}, u32[]{:S(2)}, u32[]{:S(2)}) %collective-permute-start.27) | collective-permute-done | bytes 73760 | tf_op jit(solution)/shard_map/ppermute | solution.py:52
  174.5 2.0 collective-permute-start.28
  176.5 4.4 %collective-permute-done.28 = f32[24,768]{1,0:T(8,128)S(1)} collective-permute-done((f32[24,768]{1,0:T(8,128)S(1)}, f32[24,768]{1,0:T(8,128)S(1)}, u32[]{:S(2)}, u32[]{:S(2)}) %collective-permute-start.28) | collective-permute-done | bytes 73760 | tf_op jit(solution)/shard_map/ppermute | solution.py:52
  181.9 4.2 %weight_gradients.1 = (bf16[2,192,384]{2,1,0:T(8,128)(2,1)}, bf16[2,192,384]{2,1,0:T(8,128)(2,1)}, bf16[2,192,384]{2,1,0:T(8,128)(2,1)}, bf16[2,192,384]{2,1,0:T(8,128)(2,1)}) custom-call(bf16[4,2,384,128]{3,2,1,0:T(8,128)(2,1)} %copy-done.2, f32[8,128]{1,0:T(8,128)} %get-tuple-element.164.token_ref, bf16[2,128,768]{2,1,0:T(8,128)(2,1)} %get-tuple-element.145.rest_0_, ...), custom_call_target="tpu_custom_call" | custom-call | bytes 18000000 | tf_op jit(solution)/shard_map/weight_gradients/pallas_call | solution.py:541
  186.1 1.5 collective-permute-start.31
  187.8 3.0 %collective-permute-done.31 = f32[24,768]{1,0:T(8,128)S(1)} collective-permute-done((f32[24,768]{1,0:T(8,128)S(1)}, f32[24,768]{1,0:T(8,128)S(1)}, u32[]{:S(2)}, u32[]{:S(2)}) %collective-permute-start.31) | collective-permute-done | bytes 73760 | tf_op jit(solution)/shard_map/ppermute | solution.py:52
  190.8 1.0 add_convert_fusion.1
  191.9 1.0 add_convert_fusion
  192.9 2.1 collective-permute-start.33
  195.0 1.3 collective-permute-start.32
  196.3 2.1 output_rows.1
  198.4 1.1 collective-permute-done.33
  200.1 3.2 %collective-permute-done.32 = bf16[2,192,384]{2,1,0:T(8,128)(2,1)S(1)} collective-permute-done((bf16[2,192,384]{2,1,0:T(8,128)(2,1)S(1)}, bf16[2,192,384]{2,1,0:T(8,128)(2,1)S(1)}, u32[]{:S(2)}, u32[]{:S(2)}) %collective-permute-start.32) | collective-permute-done | bytes 294944 | tf_op jit(solution)/shard_map/ppermute | solution.py:52
  205.6 6.2 %collective-permute-done.34 = bf16[192,384]{1,0:T(8,128)(2,1)S(1)} collective-permute-done((bf16[192,384]{1,0:T(8,128)(2,1)S(1)}, bf16[192,384]{1,0:T(8,128)(2,1)S(1)}, u32[]{:S(2)}, u32[]{:S(2)}) %collective-permute-start.34) | collective-permute-done | bytes 147488 | tf_op jit(solution)/shard_map/ppermute | solution.py:52
  (112 shorter events, 20.6 us)
Async XLA Ops:
  1.7 11.1 %collective-permute-start.2 = (bf16[1,192,384]{2,1,0:T(8,128)(2,1)S(1)}, bf16[1,192,384]{2,1,0:T(8,128)(2,1)S(1)}, u32[]{:S(2)}, u32[]{:S(2)}) collective-permute-start(bf16[1,192,384]{2,1,0:T(8,128)(2,1)S(1)} %maximum_bitcast_fusion), channel_id=1, source_target_pairs={{0,6},{1,7},{2,4},{3,5},{4,2},{5,3},{6,0},{7,1},{8,14},{9,15},{10,... | collective-permute-start | bytes 442376 | tf_op jit(solution)/shard_map/ppermute | solution.py:52
  6.8 12.5 %collective-permute-start.1 = (bf16[1,192,384]{2,1,0:T(8,128)(2,1)S(1)}, bf16[1,192,384]{2,1,0:T(8,128)(2,1)S(1)}, u32[]{:S(2)}, u32[]{:S(2)}) collective-permute-start(bf16[1,192,384]{2,1,0:T(8,128)(2,1)S(1)} %maximum_bitcast_fusion), channel_id=1, source_target_pairs={{0,4},{1,5},{2,6},{3,7},{4,0},{5,1},{6,2},{7,3},{8,12},{9,13},{10,... | collective-permute-start | bytes 442376 | tf_op jit(solution)/shard_map/ppermute | solution.py:52
  6.8 12.5 %collective-permute-start = (bf16[1,192,384]{2,1,0:T(8,128)(2,1)S(1)}, bf16[1,192,384]{2,1,0:T(8,128)(2,1)S(1)}, u32[]{:S(2)}, u32[]{:S(2)}) collective-permute-start(bf16[1,192,384]{2,1,0:T(8,128)(2,1)S(1)} %maximum_bitcast_fusion), channel_id=1, source_target_pairs={{0,2},{1,3},{2,0},{3,1},{4,6},{5,7},{6,4},{7,5},{8,10},{9,11},{10,... | collective-permute-start | bytes 442376 | tf_op jit(solution)/shard_map/ppermute | solution.py:52
  19.4 8.1 %collective-permute-start.3 = (bf16[1,4,96,384]{3,2,1,0:T(8,128)(2,1)S(1)}, bf16[1,4,96,384]{3,2,1,0:T(8,128)(2,1)S(1)}, u32[]{:S(2)}, u32[]{:S(2)}) collective-permute-start(bf16[1,4,96,384]{3,2,1,0:T(8,128)(2,1)S(1)} %get-tuple-element.185), channel_id=1, source_target_pairs={{0,1},{1,0},{2,3},{3,2},{4,5},{5,4},{6,7},{7,6},{8,9},{9,8},{10,11... | collective-permute-start | bytes 884744 | tf_op jit(solution)/shard_map/ppermute | solution.py:52
  21.0 8.2 %collective-permute-start.7 = (bf16[1,4,96,384]{3,2,1,0:T(8,128)(2,1)S(1)}, bf16[1,4,96,384]{3,2,1,0:T(8,128)(2,1)S(1)}, u32[]{:S(2)}, u32[]{:S(2)}) collective-permute-start(bf16[1,4,96,384]{3,2,1,0:T(8,128)(2,1)S(1)} %get-tuple-element.184), channel_id=1, source_target_pairs={{0,16},{8,24},{16,0},{24,8},{1,17},{9,25},{17,1},{25,9},{2,18},{10... | collective-permute-start | bytes 884744 | tf_op jit(solution)/shard_map/ppermute | solution.py:52
  27.6 22.1 %copy-start = (bf16[2,4,96,384]{3,2,1,0:T(8,128)(2,1)}, bf16[2,4,96,384]{3,2,1,0:T(8,128)(2,1)S(1)}, u32[]{:S(2)}) copy-start(bf16[2,4,96,384]{3,2,1,0:T(8,128)(2,1)S(1)} %pad_maximum_fusion.1.rest_0_) | copy-start | bytes 1769476
  27.6 13.8 %collective-permute-start.5 = (bf16[2,4,96,384]{3,2,1,0:T(8,128)(2,1)S(1)}, bf16[2,4,96,384]{3,2,1,0:T(8,128)(2,1)S(1)}, u32[]{:S(2)}, u32[]{:S(2)}) collective-permute-start(bf16[2,4,96,384]{3,2,1,0:T(8,128)(2,1)S(1)} %pad_maximum_fusion.1.rest_0_), channel_id=1, source_target_pairs={{0,16},{8,24},{16,0},{24,8},{1,17},{9,25},{17,1},{25,9},{2,18},{10... | collective-permute-start | bytes 1769480 | tf_op jit(solution)/shard_map/ppermute | solution.py:52
  29.3 20.4 %copy-start.1 = (bf16[2,4,96,384]{3,2,1,0:T(8,128)(2,1)}, bf16[2,4,96,384]{3,2,1,0:T(8,128)(2,1)S(1)}, u32[]{:S(2)}) copy-start(bf16[2,4,96,384]{3,2,1,0:T(8,128)(2,1)S(1)} %pad_maximum_fusion.2.rest_4_) | copy-start | bytes 1769476
  29.3 13.2 %collective-permute-start.9 = (bf16[2,4,96,384]{3,2,1,0:T(8,128)(2,1)S(1)}, bf16[2,4,96,384]{3,2,1,0:T(8,128)(2,1)S(1)}, u32[]{:S(2)}, u32[]{:S(2)}) collective-permute-start(bf16[2,4,96,384]{3,2,1,0:T(8,128)(2,1)S(1)} %pad_maximum_fusion.2.rest_4_), channel_id=1, source_target_pairs={{0,1},{1,0},{2,3},{3,2},{4,5},{5,4},{6,7},{7,6},{8,9},{9,8},{10,11... | collective-permute-start | bytes 1769480 | tf_op jit(solution)/shard_map/ppermute | solution.py:52
  30.9 11.7 %collective-permute-start.4 = (bf16[2,4,96,384]{3,2,1,0:T(8,128)(2,1)S(1)}, bf16[2,4,96,384]{3,2,1,0:T(8,128)(2,1)S(1)}, u32[]{:S(2)}, u32[]{:S(2)}) collective-permute-start(bf16[2,4,96,384]{3,2,1,0:T(8,128)(2,1)S(1)} %pad_maximum_fusion.1.rest_0_), channel_id=1, source_target_pairs={{0,8},{8,0},{16,24},{24,16},{1,9},{9,1},{17,25},{25,17},{2,10},{10... | collective-permute-start | bytes 1769480 | tf_op jit(solution)/shard_map/ppermute | solution.py:52
  30.9 11.7 %collective-permute-start.8 = (bf16[2,4,96,384]{3,2,1,0:T(8,128)(2,1)S(1)}, bf16[2,4,96,384]{3,2,1,0:T(8,128)(2,1)S(1)}, u32[]{:S(2)}, u32[]{:S(2)}) collective-permute-start(bf16[2,4,96,384]{3,2,1,0:T(8,128)(2,1)S(1)} %pad_maximum_fusion.2.rest_4_), channel_id=1, source_target_pairs={{0,8},{8,0},{16,24},{24,16},{1,9},{9,1},{17,25},{25,17},{2,10},{10... | collective-permute-start | bytes 1769480 | tf_op jit(solution)/shard_map/ppermute | solution.py:52
  41.4 8.3 %copy-start.3 = (bf16[2,4,96,384]{3,2,1,0:T(8,128)(2,1)}, bf16[2,4,96,384]{3,2,1,0:T(8,128)(2,1)S(1)}, u32[]{:S(2)}) copy-start(bf16[2,4,96,384]{3,2,1,0:T(8,128)(2,1)S(1)} %collective-permute-done.5.rest_2_) | copy-start | bytes 1769476
  41.4 2.0 collective-permute-start.6
  42.6 2.0 collective-permute-start.10
  45.4 14.3 %all-to-all-start = ((bf16[8,24,768]{2,1,0:T(8,128)(2,1)}), bf16[8,24,768]{2,1,0:T(8,128)(2,1)}, u32[]{:S(2)}, u32[]{:S(2)}) async-start(bf16[8,24,768]{2,1,0:T(8,128)(2,1)} %get-tuple-element.122), calls=%async_computation | async-start | bytes 589824 | tf_op jit(solution)/shard_map/all_to_all | solution.py:60
  59.7 9.0 %collective-permute-start.12 = (bf16[192,768]{1,0:T(8,128)(2,1)}, bf16[192,768]{1,0:T(8,128)(2,1)S(1)}, u32[]{:S(2)}, u32[]{:S(2)}) collective-permute-start(bf16[192,768]{1,0:T(8,128)(2,1)} %bitcast.6.rest_0_), channel_id=1, source_target_pairs={{0,16},{8,24},{16,0},{24,8},{1,17},{9,25},{17,1},{25,9},{2,18},{10... | collective-permute-start | bytes 884744 | tf_op jit(solution)/shard_map/ppermute | solution.py:52
  60.8 15.1 %all-to-all-start.1 = ((bf16[8,24,768]{2,1,0:T(8,128)(2,1)}), bf16[8,24,768]{2,1,0:T(8,128)(2,1)S(1)}, u32[]{:S(2)}, u32[]{:S(2)}) async-start(bf16[8,24,768]{2,1,0:T(8,128)(2,1)} %get-tuple-element.123), calls=%async_computation.1 | async-start | bytes 589824 | tf_op jit(solution)/shard_map/all_to_all | solution.py:60
  66.7 2.0 collective-permute-start.11
  68.7 8.1 %copy-start.15 = (bf16[192,768]{1,0:T(8,128)(2,1)}, bf16[192,768]{1,0:T(8,128)(2,1)S(1)}, u32[]{:S(2)}) copy-start(bf16[192,768]{1,0:T(8,128)(2,1)S(1)} %collective-permute-done.12.rest_2_) | copy-start | bytes 884740
  68.7 7.2 %collective-permute-start.13 = (bf16[192,768]{1,0:T(8,128)(2,1)S(1)}, bf16[192,768]{1,0:T(8,128)(2,1)S(1)}, u32[]{:S(2)}, u32[]{:S(2)}) collective-permute-start(bf16[192,768]{1,0:T(8,128)(2,1)S(1)} %collective-permute-done.12.rest_2_), channel_id=1, source_target_pairs={{0,8},{8,0},{16,24},{24,16},{1,9},{9,1},{17,25},{25,17},{2,10},{10... | collective-permute-start | bytes 884744 | tf_op jit(solution)/shard_map/ppermute | solution.py:52
  75.9 8.8 %copy-start.9 = (bf16[8,24,768]{2,1,0:T(8,128)(2,1)}, bf16[8,24,768]{2,1,0:T(8,128)(2,1)S(1)}, u32[]{:S(2)}) copy-start(bf16[8,24,768]{2,1,0:T(8,128)(2,1)S(1)} %all-to-all-done.1) | copy-start | bytes 884740
  75.9 6.8 %collective-permute-start.14 = (bf16[192,768]{1,0:T(8,128)(2,1)S(1)}, bf16[192,768]{1,0:T(8,128)(2,1)S(1)}, u32[]{:S(2)}, u32[]{:S(2)}) collective-permute-start(bf16[192,768]{1,0:T(8,128)(2,1)S(1)} %bitcast.21), channel_id=1, source_target_pairs={{0,16},{8,24},{16,0},{24,8},{1,17},{9,25},{17,1},{25,9},{2,18},{10... | collective-permute-start | bytes 884744 | tf_op jit(solution)/shard_map/ppermute | solution.py:52
  82.7 13.1 %copy-start.11 = (bf16[2,128,768]{2,1,0:T(8,128)(2,1)S(1)}, bf16[2,128,768]{2,1,0:T(8,128)(2,1)}, u32[]{:S(2)}) copy-start(bf16[2,128,768]{2,1,0:T(8,128)(2,1)} %get-tuple-element.145.rest_0_) | copy-start | bytes 1179652
  82.7 1.6 collective-permute-start.15
  82.7 2.0 collective-permute-start.16
  95.6 3.6 %collective-permute-start.18 = (bf16[192,768]{1,0:T(8,128)(2,1)}, bf16[192,768]{1,0:T(8,128)(2,1)S(1)}, u32[]{:S(2)}, u32[]{:S(2)}) collective-permute-start(bf16[192,768]{1,0:T(8,128)(2,1)} %get-tuple-element.138), channel_id=1, source_target_pairs={{0,8},{8,0},{16,24},{24,16},{1,9},{9,1},{17,25},{25,17},{2,10},{10... | collective-permute-start | bytes 884744 | tf_op jit(solution)/shard_map/ppermute | solution.py:52
  95.8 13.8 %collective-permute-start.20 = (bf16[2,128,768]{2,1,0:T(8,128)(2,1)S(1)}, bf16[2,128,768]{2,1,0:T(8,128)(2,1)S(1)}, u32[]{:S(2)}, u32[]{:S(2)}) collective-permute-start(bf16[2,128,768]{2,1,0:T(8,128)(2,1)S(1)} %copy-done.11), channel_id=1, source_target_pairs={{0,1},{1,0},{2,3},{3,2},{4,5},{5,4},{6,7},{7,6},{8,9},{9,8},{10,11... | collective-permute-start | bytes 1179656 | tf_op jit(solution)/shard_map/ppermute | solution.py:52
  97.3 12.2 %collective-permute-start.21 = (bf16[2,128,768]{2,1,0:T(8,128)(2,1)S(1)}, bf16[2,128,768]{2,1,0:T(8,128)(2,1)S(1)}, u32[]{:S(2)}, u32[]{:S(2)}) collective-permute-start(bf16[2,128,768]{2,1,0:T(8,128)(2,1)S(1)} %copy-done.11), channel_id=1, source_target_pairs={{0,2},{1,3},{2,0},{3,1},{4,6},{5,7},{6,4},{7,5},{8,10},{9,11},{10,... | collective-permute-start | bytes 1179656 | tf_op jit(solution)/shard_map/ppermute | solution.py:52
  97.6 19.2 %collective-permute-start.22 = (bf16[2,128,768]{2,1,0:T(8,128)(2,1)S(1)}, bf16[2,128,768]{2,1,0:T(8,128)(2,1)S(1)}, u32[]{:S(2)}, u32[]{:S(2)}) collective-permute-start(bf16[2,128,768]{2,1,0:T(8,128)(2,1)S(1)} %copy-done.11), channel_id=1, source_target_pairs={{0,3},{1,2},{2,1},{3,0},{4,7},{5,6},{6,5},{7,4},{8,11},{9,10},{10,... | collective-permute-start | bytes 1179656 | tf_op jit(solution)/shard_map/ppermute | solution.py:52
  99.3 17.5 %copy-start.21 = (bf16[192,768]{1,0:T(8,128)(2,1)S(1)}, bf16[192,768]{1,0:T(8,128)(2,1)}, u32[]{:S(2)}) copy-start(bf16[192,768]{1,0:T(8,128)(2,1)} %get-tuple-element.135) | copy-start | bytes 884740
  100.4 16.4 %collective-permute-start.19 = (bf16[192,768]{1,0:T(8,128)(2,1)S(1)}, bf16[192,768]{1,0:T(8,128)(2,1)S(1)}, u32[]{:S(2)}, u32[]{:S(2)}) collective-permute-start(bf16[192,768]{1,0:T(8,128)(2,1)S(1)} %add_convert_fusion.6), channel_id=1, source_target_pairs={{0,16},{8,24},{16,0},{24,8},{1,17},{9,25},{17,1},{25,9},{2,18},{10... | collective-permute-start | bytes 884744 | tf_op jit(solution)/shard_map/ppermute | solution.py:52
  101.3 15.5 %collective-permute-start.17 = (bf16[192,768]{1,0:T(8,128)(2,1)}, bf16[192,768]{1,0:T(8,128)(2,1)S(1)}, u32[]{:S(2)}, u32[]{:S(2)}) collective-permute-start(bf16[192,768]{1,0:T(8,128)(2,1)} %get-tuple-element.136), channel_id=1, source_target_pairs={{0,8},{8,0},{16,24},{24,16},{1,9},{9,1},{17,25},{25,17},{2,10},{10... | collective-permute-start | bytes 884744 | tf_op jit(solution)/shard_map/ppermute | solution.py:52
  109.5 12.6 %copy-start.12 = (bf16[2,128,768]{2,1,0:T(8,128)(2,1)}, bf16[2,128,768]{2,1,0:T(8,128)(2,1)S(1)}, u32[]{:S(2)}) copy-start(bf16[2,128,768]{2,1,0:T(8,128)(2,1)S(1)} %collective-permute-done.20.rest_1_) | copy-start | bytes 1179652
  109.5 12.6 %copy-start.13 = (bf16[2,128,768]{2,1,0:T(8,128)(2,1)}, bf16[2,128,768]{2,1,0:T(8,128)(2,1)S(1)}, u32[]{:S(2)}) copy-start(bf16[2,128,768]{2,1,0:T(8,128)(2,1)S(1)} %collective-permute-done.21.rest_2_) | copy-start | bytes 1179652
  121.6 5.8 %collective-permute-start.23 = (bf16[192,768]{1,0:T(8,128)(2,1)}, bf16[192,768]{1,0:T(8,128)(2,1)S(1)}, u32[]{:S(2)}, u32[]{:S(2)}) collective-permute-start(bf16[192,768]{1,0:T(8,128)(2,1)} %get-tuple-element.150), channel_id=1, source_target_pairs={{0,8},{8,0},{16,24},{24,16},{1,9},{9,1},{17,25},{25,17},{2,10},{10... | collective-permute-start | bytes 884744 | tf_op jit(solution)/shard_map/ppermute | solution.py:52
  121.6 6.8 %collective-permute-start.24 = (bf16[192,768]{1,0:T(8,128)(2,1)}, bf16[192,768]{1,0:T(8,128)(2,1)S(1)}, u32[]{:S(2)}, u32[]{:S(2)}) collective-permute-start(bf16[192,768]{1,0:T(8,128)(2,1)} %get-tuple-element.152), channel_id=1, source_target_pairs={{0,8},{8,0},{16,24},{24,16},{1,9},{9,1},{17,25},{25,17},{2,10},{10... | collective-permute-start | bytes 884744 | tf_op jit(solution)/shard_map/ppermute | solution.py:52
  122.1 15.0 %all-to-all-start.2 = ((bf16[8,24,768]{2,1,0:T(8,128)(2,1)}), bf16[8,24,768]{2,1,0:T(8,128)(2,1)S(1)}, u32[]{:S(2)}, u32[]{:S(2)}) async-start(bf16[8,24,768]{2,1,0:T(8,128)(2,1)} %bitcast.8), calls=%async_computation.2 | async-start | bytes 589824 | tf_op jit(solution)/shard_map/all_to_all | solution.py:60
  137.1 12.7 %collective-permute-start.25 = (bf16[192,768]{1,0:T(8,128)(2,1)S(1)}, bf16[192,768]{1,0:T(8,128)(2,1)S(1)}, u32[]{:S(2)}, u32[]{:S(2)}) collective-permute-start(bf16[192,768]{1,0:T(8,128)(2,1)S(1)} %add_convert_fusion.3), channel_id=1, source_target_pairs={{0,16},{8,24},{16,0},{24,8},{1,17},{9,25},{17,1},{25,9},{2,18},{10... | collective-permute-start | bytes 884744 | tf_op jit(solution)/shard_map/ppermute | solution.py:52
  149.9 1.5 collective-permute-start.26
  166.6 14.4 %all-to-all-start.3 = ((bf16[4,2,384,128]{3,2,1,0:T(8,128)(2,1)}), bf16[4,2,384,128]{3,2,1,0:T(8,128)(2,1)S(1)}, u32[]{:S(2)}, u32[]{:S(2)}) async-start(bf16[4,2,384,128]{3,2,1,0:T(8,128)(2,1)} %get-tuple-element.158), calls=%async_computation.3 | async-start | bytes 1572864 | tf_op jit(solution)/shard_map/all_to_all | solution.py:736
  170.1 4.4 %collective-permute-start.27 = (f32[24,768]{1,0:T(8,128)S(1)}, f32[24,768]{1,0:T(8,128)S(1)}, u32[]{:S(2)}, u32[]{:S(2)}) collective-permute-start(f32[24,768]{1,0:T(8,128)S(1)} %add.58), channel_id=1, source_target_pairs={{0,16},{8,24},{16,0},{24,8},{1,17},{9,25},{17,1},{25,9},{2,18},{10... | collective-permute-start | bytes 221192 | tf_op jit(solution)/shard_map/ppermute | solution.py:52
  174.5 6.4 %collective-permute-start.28 = (f32[24,768]{1,0:T(8,128)S(1)}, f32[24,768]{1,0:T(8,128)S(1)}, u32[]{:S(2)}, u32[]{:S(2)}) collective-permute-start(f32[24,768]{1,0:T(8,128)S(1)} %add.59), channel_id=1, source_target_pairs={{0,1},{1,0},{2,3},{3,2},{4,5},{5,4},{6,7},{7,6},{8,9},{9,8},{10,11... | collective-permute-start | bytes 221192 | tf_op jit(solution)/shard_map/ppermute | solution.py:52
  186.1 4.7 %collective-permute-start.29 = (bf16[2,192,384]{2,1,0:T(8,128)(2,1)}, bf16[2,192,384]{2,1,0:T(8,128)(2,1)S(1)}, u32[]{:S(2)}, u32[]{:S(2)}) collective-permute-start(bf16[2,192,384]{2,1,0:T(8,128)(2,1)} %get-tuple-element.169), channel_id=1, source_target_pairs={{0,8},{8,0},{16,24},{24,16},{1,9},{9,1},{17,25},{25,17},{2,10},{10... | collective-permute-start | bytes 884744 | tf_op jit(solution)/shard_map/ppermute | solution.py:52
  186.1 4.7 %collective-permute-start.31 = (f32[24,768]{1,0:T(8,128)S(1)}, f32[24,768]{1,0:T(8,128)S(1)}, u32[]{:S(2)}, u32[]{:S(2)}) collective-permute-start(f32[24,768]{1,0:T(8,128)S(1)} %add.60), channel_id=1, source_target_pairs={{0,2},{1,3},{2,0},{3,1},{4,6},{5,7},{6,4},{7,5},{8,10},{9,11},{10,... | collective-permute-start | bytes 221192 | tf_op jit(solution)/shard_map/ppermute | solution.py:52
  187.6 4.3 %collective-permute-start.30 = (bf16[2,192,384]{2,1,0:T(8,128)(2,1)}, bf16[2,192,384]{2,1,0:T(8,128)(2,1)S(1)}, u32[]{:S(2)}, u32[]{:S(2)}) collective-permute-start(bf16[2,192,384]{2,1,0:T(8,128)(2,1)} %get-tuple-element.171), channel_id=1, source_target_pairs={{0,8},{8,0},{16,24},{24,16},{1,9},{9,1},{17,25},{25,17},{2,10},{10... | collective-permute-start | bytes 884744 | tf_op jit(solution)/shard_map/ppermute | solution.py:52
  192.9 6.6 %collective-permute-start.33 = (f32[24,768]{1,0:T(8,128)S(1)}, f32[24,768]{1,0:T(8,128)S(1)}, u32[]{:S(2)}, u32[]{:S(2)}) collective-permute-start(f32[24,768]{1,0:T(8,128)S(1)} %add.63), channel_id=1, source_target_pairs={{0,4},{1,5},{2,6},{3,7},{4,0},{5,1},{6,2},{7,3},{8,12},{9,13},{10,... | collective-permute-start | bytes 221192 | tf_op jit(solution)/shard_map/ppermute | solution.py:52
  195.0 8.4 %collective-permute-start.32 = (bf16[2,192,384]{2,1,0:T(8,128)(2,1)S(1)}, bf16[2,192,384]{2,1,0:T(8,128)(2,1)S(1)}, u32[]{:S(2)}, u32[]{:S(2)}) collective-permute-start(bf16[2,192,384]{2,1,0:T(8,128)(2,1)S(1)} %add_convert_fusion), channel_id=1, source_target_pairs={{0,16},{8,24},{16,0},{24,8},{1,17},{9,25},{17,1},{25,9},{2,18},{10... | collective-permute-start | bytes 884744 | tf_op jit(solution)/shard_map/ppermute | solution.py:52
  203.4 8.4 %collective-permute-start.34 = (bf16[192,384]{1,0:T(8,128)(2,1)S(1)}, bf16[192,384]{1,0:T(8,128)(2,1)S(1)}, u32[]{:S(2)}, u32[]{:S(2)}) collective-permute-start(bf16[192,384]{1,0:T(8,128)(2,1)S(1)} %fusion), channel_id=1, source_target_pairs={{0,4},{1,5},{2,6},{3,7},{4,0},{5,1},{6,2},{7,3},{8,12},{9,13},{10,... | collective-permute-start | bytes 442376 | tf_op jit(solution)/shard_map/ppermute | solution.py:52
  (13 other events, 43.1 us)

commit v11 on v10

--- a/solution.py
+++ b/solution.py
@@ -677,7 +677,7 @@
     first_grad, second_grad, token = call(
         expert_grad_kernel,
         "expert_gradients",
-        8,
+        1,
         [shaped(FULL, *w_in.shape), shaped(FULL, *w_out.shape), shaped(FULL, 8, 128)],
         [slot_rows, activated, pre_grad, gates, up_rows],
     )
@@ -693,9 +693,9 @@
         [pack_t, w_out, activated],
         scratch=[pltpu.VMEM((*by_expert, model_width), LOW)],
     )
-    returned = scatter_near(returned)
+    returned = add(*scatter_terms(returned)).reshape(ranks, slab, model_width)
     back, returned = together(back, returned)
-    returned = add(*scatter_far(returned)).reshape(ranks, slab, model_width)
+    returned = exchange(returned)
 
     bias_rows = -(-head_count // 6)
     small_rows = -(-(experts_total + 2 + bias_rows) // 8) * 8
@@ -738,11 +738,9 @@
     )
     first, *steps, one_but_last, last = sum_steps()
     small = small + swap(small, *first)
-    small, returned = together(small, returned)
-    returned = exchange(returned)
     for axis, bit in steps:
         small = small + swap(small, axis, bit)
-    factors, small, returned = together(factors, small, returned)
+    factors, small = together(factors, small)
     small = small + swap(small, *one_but_last)
     grads = call(
         product_kernel,

time: 214 us -> 205 us (0.958)
  blocking collectives: 14.2 us -> 0 us
  starting transfers between devices: 49.4 us -> 54.2 us
    all_to_all x1 -> x0, blocking collectives: 14.2 us -> none  [exchange(): lax.all_to_all(value, 'expert', split_axis=0, concat_axis=0, tiled=True)]
    all_to_all x3 -> x4, starting transfers between devices: 15.5 us -> 19 us  [exchange(): lax.all_to_all(value, 'expert', split_axis=0, concat_axis=0, tiled=True)]
    all_to_all x3 -> x4, waiting for transfers between devices: 14.8 us -> 12 us  [exchange(): lax.all_to_all(value, 'expert', split_axis=0, concat_axis=0, tiled=True)]
    ppermute x35, waiting for transfers between devices: 59.4 us -> 61.7 us  [swap(): return lax.ppermute(value, axis, [(i, i ^ mask) for i in range(count)])]
    convert_element_type x8 -> x7, other arithmetic: 6.17 us -> 6.87 us  [add(): return (left.astype(FULL) + right.astype(FULL)).astype(dtype)]
  transfers between devices with their start and end apart: 39 -> 40, of which waited for: 20 -> 22; matrix products, arithmetic and copies ran while one was open for 4% -> 5% of each run, Pallas kernels for 19% -> 20%
where the time goes in v11:
time: 205 us; the launch traced here: 204 us
  waiting for transfers between devices  73.7 us (36%)
  Pallas kernels  58.1 us (28%)
  starting transfers between devices  54.2 us (26%)
  other arithmetic  9.7 us (5%)
  local copies, waits for them, and re-layouts  6.95 us (3%)
    ppermute x35, waiting for transfers between devices, swap(): return lax.ppermute(value, axis, [(i, i ^ mask) for i in range(count)])  61.7 us
    pallas_call x9, Pallas kernels, call(): pl.pallas_call(kernel, out_shape=tuple(out_shape), in_specs=[VMEM] * len(...  58.1 us
    ppermute x35, starting transfers between devices, swap(): return lax.ppermute(value, axis, [(i, i ^ mask) for i in range(count)])  31.1 us
    all_to_all x4, starting transfers between devices, exchange(): lax.all_to_all(value, 'expert', split_axis=0, concat_axis=0, tiled=True)  19 us
    all_to_all x4, waiting for transfers between devices, exchange(): lax.all_to_all(value, 'expert', split_axis=0, concat_axis=0, tiled=True)  12 us
    convert_element_type x7, other arithmetic, add(): return (left.astype(FULL) + right.astype(FULL)).astype(dtype)  6.87 us
    all_to_all x1, starting transfers between devices, per_device(): lax.all_to_all(factors, 'expert', split_axis=0, concat_axis=0, tiled=True...  4.12 us
  transfers between devices with their start and end apart: 40, of which 22 were waited for; matrix products, arithmetic and copies ran while one was open for 5% of the time, Pallas kernels for 20%

profile of v11, /device:TPU:0, one launch (start us, length us, event | category | flops | bytes accessed | tf_op | source)
XLA Modules:
  0.0 203.6 jit_solution(14830218422050234467)
XLA Ops:
  1.7 5.1 %collective-permute-start.2 = (bf16[1,192,384]{2,1,0:T(8,128)(2,1)S(1)}, bf16[1,192,384]{2,1,0:T(8,128)(2,1)S(1)}, u32[]{:S(2)}, u32[]{:S(2)}) collective-permute-start(bf16[1,192,384]{2,1,0:T(8,128)(2,1)S(1)} %maximum_bitcast_fusion), channel_id=1, source_target_pairs={{0,6},{1,7},{2,4},{3,5},{4,2},{5,3},{6,0},{7,1},{8,14},{9,15},{10,... | collective-permute-start | bytes 442376 | tf_op jit(solution)/shard_map/ppermute | solution.py:52
  9.4 3.3 %early.1 = (bf16[128,768]{1,0:T(8,128)(2,1)}, f32[128,16]{1,0:T(8,128)}, bf16[128,192]{1,0:T(8,128)(2,1)}, bf16[192,128]{1,0:T(8,128)(2,1)}, f32[12,128,128]{2,1,0:T(8,128)}, /*index=5*/bf16[8,24,768]{2,1,0:T(8,128)(2,1)}) custom-call(bf16[128,768]{1,0:T(8,128)(2,1)} %tokens_ref.5, s32[1,128]{1,0:T(1,128)} %bitcast.27, ...), custom_call_target="tpu_custom_call" | custom-call | bytes 10800000 | tf_op jit(solution)/shard_map/early/pallas_call | solution.py:541
  12.7 6.5 %collective-permute-done.1 = bf16[1,192,384]{2,1,0:T(8,128)(2,1)S(1)} collective-permute-done((bf16[1,192,384]{2,1,0:T(8,128)(2,1)S(1)}, bf16[1,192,384]{2,1,0:T(8,128)(2,1)S(1)}, u32[]{:S(2)}, u32[]{:S(2)}) %collective-permute-start.1) | collective-permute-done | bytes 147488 | tf_op jit(solution)/shard_map/ppermute | solution.py:52
  19.4 1.6 collective-permute-start.3
  21.0 1.5 collective-permute-start.7
  22.5 5.1 %collective-permute-done.3 = bf16[1,4,96,384]{3,2,1,0:T(8,128)(2,1)S(1)} collective-permute-done((bf16[1,4,96,384]{3,2,1,0:T(8,128)(2,1)S(1)}, bf16[1,4,96,384]{3,2,1,0:T(8,128)(2,1)S(1)}, u32[]{:S(2)}, u32[]{:S(2)}) %collective-permute-start.3) | collective-permute-done | bytes 294944 | tf_op jit(solution)/shard_map/ppermute | solution.py:52
  27.6 1.6 collective-permute-start.5
  29.3 1.6 collective-permute-start.9
  31.4 10.0 %collective-permute-done.5.rest_2_ = bf16[2,4,96,384]{3,2,1,0:T(8,128)(2,1)S(1)} collective-permute-done((bf16[2,4,96,384]{3,2,1,0:T(8,128)(2,1)S(1)}, bf16[2,4,96,384]{3,2,1,0:T(8,128)(2,1)S(1)}, u32[]{:S(2)}, u32[]{:S(2)}) %collective-permute-start.5) | collective-permute-done | bytes 589856 | tf_op jit(solution)/shard_map/ppermute | solution.py:52
  41.4 1.1 collective-permute-done.9.rest_6_
  43.4 1.1 collective-permute-done.10.rest_7_
  45.4 4.3 %all-to-all-start = ((bf16[8,24,768]{2,1,0:T(8,128)(2,1)}), bf16[8,24,768]{2,1,0:T(8,128)(2,1)}, u32[]{:S(2)}, u32[]{:S(2)}) async-start(bf16[8,24,768]{2,1,0:T(8,128)(2,1)} %get-tuple-element.118), calls=%async_computation | async-start | bytes 589824 | tf_op jit(solution)/shard_map/all_to_all | solution.py:60
  49.8 9.9 %attention_forward.1 = (bf16[3,768,128]{2,1,0:T(8,128)(2,1)}, f32[12,128,128]{2,1,0:T(8,128)}, bf16[2,128,768]{2,1,0:T(8,128)(2,1)}, f32[128,768]{1,0:T(8,128)},...) custom-call(bf16[128,768]{1,0:T(8,128)(2,1)} %tokens_ref.5, bf16[128,768]{1,0:T(8,128)(2,1)} %get-tuple-element.100.normed_ref, ...), custom_call_target="tpu_custom_call" | custom-call | bytes 36000000 | tf_op jit(solution)/shard_map/attention_forward/pallas_call | solution.py:541
  59.7 1.1 collective-permute-start.12
  60.8 5.9 %all-to-all-start.1 = ((bf16[8,24,768]{2,1,0:T(8,128)(2,1)}), bf16[8,24,768]{2,1,0:T(8,128)(2,1)S(1)}, u32[]{:S(2)}, u32[]{:S(2)}) async-start(bf16[8,24,768]{2,1,0:T(8,128)(2,1)} %get-tuple-element.119), calls=%async_computation.1 | async-start | bytes 589824 | tf_op jit(solution)/shard_map/all_to_all | solution.py:60
  66.7 2.0 collective-permute-done.12.rest_2_
  68.7 7.1 %all-to-all-done.1 = bf16[8,24,768]{2,1,0:T(8,128)(2,1)S(1)} async-done(((bf16[8,24,768]{2,1,0:T(8,128)(2,1)}), bf16[8,24,768]{2,1,0:T(8,128)(2,1)S(1)}, u32[]{:S(2)}, u32[]{:S(2)}) %all-to-all-start.1) | async-done | bytes 294944 | tf_op jit(solution)/shard_map/all_to_all | solution.py:60
  76.8 4.5 %upstream_rows.1 = (bf16[2,320,768]{2,1,0:T(8,128)(2,1)}, f32[2,320,768]{2,1,0:T(8,128)}) custom-call(bf16[160,192]{1,0:T(8,128)(2,1)} %constant.8.clone.pack_ref, bf16[2,768,768]{2,1,0:T(8,128)(2,1)} %w_out_ref.3, bf16[192,768]{1,0:T(8,128)(2,1)} %bitcast.6.rest_0_, bf16[192,768]{1,0:T(8,128)(2,1)} %copy-done.18, bf16[192,768]{1,0:T(8,128)(2,1)} %copy-done.16, ...), custom_call_target="tpu_custom_call" | custom-call | bytes 18000000 | tf_op jit(solution)/shard_map/upstream_rows/pallas_call | solution.py:541
  81.3 1.3 collective-permute-done.14.rest_2_
  83.2 1.1 collective-permute-done.15.rest_1_
  85.7 9.9 %experts.1 = (bf16[192,768]{1,0:T(8,128)(2,1)}, bf16[192,768]{1,0:T(8,128)(2,1)}, bf16[192,768]{1,0:T(8,128)(2,1)}, bf16[192,768]{1,0:T(8,128)(2,1)}, bf16[2,320...) custom-call(bf16[160,192]{1,0:T(8,128)(2,1)} %constant.8.clone.pack_re, ...), custom_call_target="tpu_custom_call" | custom-call | bytes 36000000 | tf_op jit(solution)/shard_map/experts/pallas_call | solution.py:541
  95.8 1.5 collective-permute-start.20
  97.6 1.7 collective-permute-start.22
  99.3 1.1 add_convert_fusion.6
  101.4 8.2 %expert_gradients.1 = (f32[2,768,768]{2,1,0:T(8,128)}, f32[2,768,768]{2,1,0:T(8,128)}, f32[8,128]{1,0:T(8,128)}) custom-call(bf16[2,320,768]{2,1,0:T(8,128)(2,1)} %get-tuple-element.135.rows_ref, bf16[2,320,768]{2,1,0:T(8,128)(2,1)} %get-tuple-element.144.act_ref, bf16[2,320,768]{2,1,0:T(8,128)(2,1)} %get-tuple-element.137.pre_grad_ref, ...), custom_call_target="tpu_custom_call" | custom-call | bytes 3600000 | tf_op jit(solution)/shard_map/expert_gradients/pallas_call | solution.py:541
  109.6 7.2 %collective-permute-done.22.rest_3_ = bf16[2,128,768]{2,1,0:T(8,128)(2,1)S(1)} collective-permute-done((bf16[2,128,768]{2,1,0:T(8,128)(2,1)S(1)}, bf16[2,128,768]{2,1,0:T(8,128)(2,1)S(1)}, u32[]{:S(2)}, u32[]{:S(2)}) %collective-permute-start.22) | collective-permute-done | bytes 393248 | tf_op jit(solution)/shard_map/ppermute | solution.py:52
  117.7 4.0 %expert_outputs.1 = (bf16[192,768]{1,0:T(8,128)(2,1)}, bf16[192,768]{1,0:T(8,128)(2,1)}, bf16[192,768]{1,0:T(8,128)(2,1)}, bf16[192,768]{1,0:T(8,128)(2,1)}) custom-call(bf16[192,160]{1,0:T(8,128)(2,1)} %constant.9.clone.pack_t_ref, bf16[2,768,768]{2,1,0:T(8,128)(2,1)} %w_out_ref.3, bf16[2,320,768]{2,1,0:T(8,128)(2,1)} %get-tuple-element.144.act_ref), custom_call_target="tpu_custom_call" | custom-call | bytes 43200000 | tf_op jit(solution)/shard_map/expert_outputs/pallas_call | solution.py:541
  122.2 1.3 collective-permute-done.24
  125.5 5.1 %all-to-all-start.2 = ((bf16[8,24,768]{2,1,0:T(8,128)(2,1)}), bf16[8,24,768]{2,1,0:T(8,128)(2,1)S(1)}, u32[]{:S(2)}, u32[]{:S(2)}) async-start(bf16[8,24,768]{2,1,0:T(8,128)(2,1)} %bitcast.8), calls=%async_computation.2 | async-start | bytes 589824 | tf_op jit(solution)/shard_map/all_to_all | solution.py:60
  130.6 3.0 %collective-permute-done.25 = bf16[192,768]{1,0:T(8,128)(2,1)S(1)} collective-permute-done((bf16[192,768]{1,0:T(8,128)(2,1)S(1)}, bf16[192,768]{1,0:T(8,128)(2,1)S(1)}, u32[]{:S(2)}, u32[]{:S(2)}) %collective-permute-start.25) | collective-permute-done | bytes 294944 | tf_op jit(solution)/shard_map/ppermute | solution.py:52
  133.6 1.8 add_convert_fusion.2
  135.4 4.8 %all-to-all-done.2.rest_8_ = bf16[8,24,768]{2,1,0:T(8,128)(2,1)S(1)} async-done(((bf16[8,24,768]{2,1,0:T(8,128)(2,1)}), bf16[8,24,768]{2,1,0:T(8,128)(2,1)S(1)}, u32[]{:S(2)}, u32[]{:S(2)}) %all-to-all-start.2) | async-done | bytes 294944 | tf_op jit(solution)/shard_map/all_to_all | solution.py:60
  140.2 3.6 %all-to-all-start.3 = ((bf16[8,24,768]{2,1,0:T(8,128)(2,1)}), bf16[8,24,768]{2,1,0:T(8,128)(2,1)S(1)}, u32[]{:S(2)}, u32[]{:S(2)}) async-start(bf16[8,24,768]{2,1,0:T(8,128)(2,1)} %bitcast.9), calls=%async_computation.3 | async-start | bytes 589824 | tf_op jit(solution)/shard_map/all_to_all | solution.py:60
  143.9 12.0 %attention_backward.1 = (f32[128,768]{1,0:T(8,128)}, f32[24,768]{1,0:T(8,128)}, bf16[4,2,384,128]{3,2,1,0:T(8,128)(2,1)}) custom-call(bf16[128,768]{1,0:T(8,128)(2,1)} %tokens_ref.5, f32[2,768]{1,0:T(2,128)} %maximum_convert_fusion.gain_ref, bf16[16,768]{1,0:T(8,128)(2,1)} %bitcast.25, f32[128,16]{1,0:T(8,128)} %get-tuple-element.98.hits_ref, ...), custom_call_target="tpu_custom_call" | custom-call | bytes 43200000 | tf_op jit(solution)/shard_map/attention_backward/pallas_call | solution.py:541
  155.9 4.1 %all-to-all-start.4 = ((bf16[4,2,384,128]{3,2,1,0:T(8,128)(2,1)}), bf16[4,2,384,128]{3,2,1,0:T(8,128)(2,1)S(1)}, u32[]{:S(2)}, u32[]{:S(2)}) async-start(bf16[4,2,384,128]{3,2,1,0:T(8,128)(2,1)} %get-tuple-element.153), calls=%async_computation.4 | async-start | bytes 1572864 | tf_op jit(solution)/shard_map/all_to_all | solution.py:736
  160.0 1.5 collective-permute-done.26
  162.4 1.3 collective-permute-start.27
  163.7 3.1 %collective-permute-done.27 = f32[24,768]{1,0:T(8,128)S(1)} collective-permute-done((f32[24,768]{1,0:T(8,128)S(1)}, f32[24,768]{1,0:T(8,128)S(1)}, u32[]{:S(2)}, u32[]{:S(2)}) %collective-permute-start.27) | collective-permute-done | bytes 73760 | tf_op jit(solution)/shard_map/ppermute | solution.py:52
  166.8 2.1 %collective-permute-start.28 = (f32[24,768]{1,0:T(8,128)S(1)}, f32[24,768]{1,0:T(8,128)S(1)}, u32[]{:S(2)}, u32[]{:S(2)}) collective-permute-start(f32[24,768]{1,0:T(8,128)S(1)} %add.59), channel_id=1, source_target_pairs={{0,1},{1,0},{2,3},{3,2},{4,5},{5,4},{6,7},{7,6},{8,9},{9,8},{10,11... | collective-permute-start | bytes 221192 | tf_op jit(solution)/shard_map/ppermute | solution.py:52
  168.9 2.5 %collective-permute-done.28 = f32[24,768]{1,0:T(8,128)S(1)} collective-permute-done((f32[24,768]{1,0:T(8,128)S(1)}, f32[24,768]{1,0:T(8,128)S(1)}, u32[]{:S(2)}, u32[]{:S(2)}) %collective-permute-start.28) | collective-permute-done | bytes 73760 | tf_op jit(solution)/shard_map/ppermute | solution.py:52
  172.4 4.2 %weight_gradients.1 = (bf16[2,192,384]{2,1,0:T(8,128)(2,1)}, bf16[2,192,384]{2,1,0:T(8,128)(2,1)}, bf16[2,192,384]{2,1,0:T(8,128)(2,1)}, bf16[2,192,384]{2,1,0:T(8,128)(2,1)}) custom-call(bf16[4,2,384,128]{3,2,1,0:T(8,128)(2,1)} %copy-done.2, f32[8,128]{1,0:T(8,128)} %get-tuple-element.156.token_ref, bf16[2,128,768]{2,1,0:T(8,128)(2,1)} %get-tuple-element.141.rest_0_, ...), custom_call_target="tpu_custom_call" | custom-call | bytes 18000000 | tf_op jit(solution)/shard_map/weight_gradients/pallas_call | solution.py:541
  176.6 1.8 collective-permute-start.31
  178.7 2.7 %collective-permute-done.31 = f32[24,768]{1,0:T(8,128)S(1)} collective-permute-done((f32[24,768]{1,0:T(8,128)S(1)}, f32[24,768]{1,0:T(8,128)S(1)}, u32[]{:S(2)}, u32[]{:S(2)}) %collective-permute-start.31) | collective-permute-done | bytes 73760 | tf_op jit(solution)/shard_map/ppermute | solution.py:52
  183.5 2.4 %collective-permute-start.33 = (f32[24,768]{1,0:T(8,128)S(1)}, f32[24,768]{1,0:T(8,128)S(1)}, u32[]{:S(2)}, u32[]{:S(2)}) collective-permute-start(f32[24,768]{1,0:T(8,128)S(1)} %add.63), channel_id=1, source_target_pairs={{0,4},{1,5},{2,6},{3,7},{4,0},{5,1},{6,2},{7,3},{8,12},{9,13},{10,... | collective-permute-start | bytes 221192 | tf_op jit(solution)/shard_map/ppermute | solution.py:52
  186.0 1.3 collective-permute-start.32
  187.2 2.1 %output_rows.1 = bf16[128,768]{1,0:T(8,128)(2,1)} custom-call(f32[128,768]{1,0:T(8,128)} %get-tuple-element.113.hidden_ref, f32[128,16]{1,0:T(8,128)} %get-tuple-element.114.chance_ref, f32[128,16]{1,0:T(8,128)} %get-tuple-element.98.hits_ref, bf16[128,192]{1,0:T(8,128)(2,1)} %get-tuple-element.99.mask_ref, bf16[8,24,768]{2,1,0:T(8,128)(2,1)} %copy-done.11), custom_call_target="tpu_custom_call" | custom-call | bytes 7200000 | tf_op jit(solution)/shard_map/output_rows/pallas_call | solution.py:541
  191.0 3.3 %collective-permute-done.32 = bf16[2,192,384]{2,1,0:T(8,128)(2,1)S(1)} collective-permute-done((bf16[2,192,384]{2,1,0:T(8,128)(2,1)S(1)}, bf16[2,192,384]{2,1,0:T(8,128)(2,1)S(1)}, u32[]{:S(2)}, u32[]{:S(2)}) %collective-permute-start.32) | collective-permute-done | bytes 294944 | tf_op jit(solution)/shard_map/ppermute | solution.py:52
  196.3 6.5 %collective-permute-done.34 = bf16[192,384]{1,0:T(8,128)(2,1)S(1)} collective-permute-done((bf16[192,384]{1,0:T(8,128)(2,1)S(1)}, bf16[192,384]{1,0:T(8,128)(2,1)S(1)}, u32[]{:S(2)}, u32[]{:S(2)}) %collective-permute-start.34) | collective-permute-done | bytes 147488 | tf_op jit(solution)/shard_map/ppermute | solution.py:52
  (114 shorter events, 22.6 us)
Async XLA Ops:
  1.7 11.1 %collective-permute-start.2 = (bf16[1,192,384]{2,1,0:T(8,128)(2,1)S(1)}, bf16[1,192,384]{2,1,0:T(8,128)(2,1)S(1)}, u32[]{:S(2)}, u32[]{:S(2)}) collective-permute-start(bf16[1,192,384]{2,1,0:T(8,128)(2,1)S(1)} %maximum_bitcast_fusion), channel_id=1, source_target_pairs={{0,6},{1,7},{2,4},{3,5},{4,2},{5,3},{6,0},{7,1},{8,14},{9,15},{10,... | collective-permute-start | bytes 442376 | tf_op jit(solution)/shard_map/ppermute | solution.py:52
  6.8 12.5 %collective-permute-start.1 = (bf16[1,192,384]{2,1,0:T(8,128)(2,1)S(1)}, bf16[1,192,384]{2,1,0:T(8,128)(2,1)S(1)}, u32[]{:S(2)}, u32[]{:S(2)}) collective-permute-start(bf16[1,192,384]{2,1,0:T(8,128)(2,1)S(1)} %maximum_bitcast_fusion), channel_id=1, source_target_pairs={{0,4},{1,5},{2,6},{3,7},{4,0},{5,1},{6,2},{7,3},{8,12},{9,13},{10,... | collective-permute-start | bytes 442376 | tf_op jit(solution)/shard_map/ppermute | solution.py:52
  6.8 12.5 %collective-permute-start = (bf16[1,192,384]{2,1,0:T(8,128)(2,1)S(1)}, bf16[1,192,384]{2,1,0:T(8,128)(2,1)S(1)}, u32[]{:S(2)}, u32[]{:S(2)}) collective-permute-start(bf16[1,192,384]{2,1,0:T(8,128)(2,1)S(1)} %maximum_bitcast_fusion), channel_id=1, source_target_pairs={{0,2},{1,3},{2,0},{3,1},{4,6},{5,7},{6,4},{7,5},{8,10},{9,11},{10,... | collective-permute-start | bytes 442376 | tf_op jit(solution)/shard_map/ppermute | solution.py:52
  19.4 8.1 %collective-permute-start.3 = (bf16[1,4,96,384]{3,2,1,0:T(8,128)(2,1)S(1)}, bf16[1,4,96,384]{3,2,1,0:T(8,128)(2,1)S(1)}, u32[]{:S(2)}, u32[]{:S(2)}) collective-permute-start(bf16[1,4,96,384]{3,2,1,0:T(8,128)(2,1)S(1)} %get-tuple-element.177), channel_id=1, source_target_pairs={{0,1},{1,0},{2,3},{3,2},{4,5},{5,4},{6,7},{7,6},{8,9},{9,8},{10,11... | collective-permute-start | bytes 884744 | tf_op jit(solution)/shard_map/ppermute | solution.py:52
  21.0 8.2 %collective-permute-start.7 = (bf16[1,4,96,384]{3,2,1,0:T(8,128)(2,1)S(1)}, bf16[1,4,96,384]{3,2,1,0:T(8,128)(2,1)S(1)}, u32[]{:S(2)}, u32[]{:S(2)}) collective-permute-start(bf16[1,4,96,384]{3,2,1,0:T(8,128)(2,1)S(1)} %get-tuple-element.176), channel_id=1, source_target_pairs={{0,16},{8,24},{16,0},{24,8},{1,17},{9,25},{17,1},{25,9},{2,18},{10... | collective-permute-start | bytes 884744 | tf_op jit(solution)/shard_map/ppermute | solution.py:52
  27.6 22.1 %copy-start = (bf16[2,4,96,384]{3,2,1,0:T(8,128)(2,1)}, bf16[2,4,96,384]{3,2,1,0:T(8,128)(2,1)S(1)}, u32[]{:S(2)}) copy-start(bf16[2,4,96,384]{3,2,1,0:T(8,128)(2,1)S(1)} %pad_maximum_fusion.1.rest_0_) | copy-start | bytes 1769476
  27.6 13.8 %collective-permute-start.5 = (bf16[2,4,96,384]{3,2,1,0:T(8,128)(2,1)S(1)}, bf16[2,4,96,384]{3,2,1,0:T(8,128)(2,1)S(1)}, u32[]{:S(2)}, u32[]{:S(2)}) collective-permute-start(bf16[2,4,96,384]{3,2,1,0:T(8,128)(2,1)S(1)} %pad_maximum_fusion.1.rest_0_), channel_id=1, source_target_pairs={{0,16},{8,24},{16,0},{24,8},{1,17},{9,25},{17,1},{25,9},{2,18},{10... | collective-permute-start | bytes 1769480 | tf_op jit(solution)/shard_map/ppermute | solution.py:52
  29.3 20.4 %copy-start.1 = (bf16[2,4,96,384]{3,2,1,0:T(8,128)(2,1)}, bf16[2,4,96,384]{3,2,1,0:T(8,128)(2,1)S(1)}, u32[]{:S(2)}) copy-start(bf16[2,4,96,384]{3,2,1,0:T(8,128)(2,1)S(1)} %pad_maximum_fusion.2.rest_4_) | copy-start | bytes 1769476
  29.3 13.2 %collective-permute-start.9 = (bf16[2,4,96,384]{3,2,1,0:T(8,128)(2,1)S(1)}, bf16[2,4,96,384]{3,2,1,0:T(8,128)(2,1)S(1)}, u32[]{:S(2)}, u32[]{:S(2)}) collective-permute-start(bf16[2,4,96,384]{3,2,1,0:T(8,128)(2,1)S(1)} %pad_maximum_fusion.2.rest_4_), channel_id=1, source_target_pairs={{0,1},{1,0},{2,3},{3,2},{4,5},{5,4},{6,7},{7,6},{8,9},{9,8},{10,11... | collective-permute-start | bytes 1769480 | tf_op jit(solution)/shard_map/ppermute | solution.py:52
  30.9 11.7 %collective-permute-start.4 = (bf16[2,4,96,384]{3,2,1,0:T(8,128)(2,1)S(1)}, bf16[2,4,96,384]{3,2,1,0:T(8,128)(2,1)S(1)}, u32[]{:S(2)}, u32[]{:S(2)}) collective-permute-start(bf16[2,4,96,384]{3,2,1,0:T(8,128)(2,1)S(1)} %pad_maximum_fusion.1.rest_0_), channel_id=1, source_target_pairs={{0,8},{8,0},{16,24},{24,16},{1,9},{9,1},{17,25},{25,17},{2,10},{10... | collective-permute-start | bytes 1769480 | tf_op jit(solution)/shard_map/ppermute | solution.py:52
  30.9 11.7 %collective-permute-start.8 = (bf16[2,4,96,384]{3,2,1,0:T(8,128)(2,1)S(1)}, bf16[2,4,96,384]{3,2,1,0:T(8,128)(2,1)S(1)}, u32[]{:S(2)}, u32[]{:S(2)}) collective-permute-start(bf16[2,4,96,384]{3,2,1,0:T(8,128)(2,1)S(1)} %pad_maximum_fusion.2.rest_4_), channel_id=1, source_target_pairs={{0,8},{8,0},{16,24},{24,16},{1,9},{9,1},{17,25},{25,17},{2,10},{10... | collective-permute-start | bytes 1769480 | tf_op jit(solution)/shard_map/ppermute | solution.py:52
  41.4 2.0 collective-permute-start.6
  42.6 2.0 collective-permute-start.10
  45.4 14.3 %all-to-all-start = ((bf16[8,24,768]{2,1,0:T(8,128)(2,1)}), bf16[8,24,768]{2,1,0:T(8,128)(2,1)}, u32[]{:S(2)}, u32[]{:S(2)}) async-start(bf16[8,24,768]{2,1,0:T(8,128)(2,1)} %get-tuple-element.118), calls=%async_computation | async-start | bytes 589824 | tf_op jit(solution)/shard_map/all_to_all | solution.py:60
  59.7 9.0 %collective-permute-start.12 = (bf16[192,768]{1,0:T(8,128)(2,1)}, bf16[192,768]{1,0:T(8,128)(2,1)S(1)}, u32[]{:S(2)}, u32[]{:S(2)}) collective-permute-start(bf16[192,768]{1,0:T(8,128)(2,1)} %bitcast.6.rest_0_), channel_id=1, source_target_pairs={{0,16},{8,24},{16,0},{24,8},{1,17},{9,25},{17,1},{25,9},{2,18},{10... | collective-permute-start | bytes 884744 | tf_op jit(solution)/shard_map/ppermute | solution.py:52
  60.8 15.1 %all-to-all-start.1 = ((bf16[8,24,768]{2,1,0:T(8,128)(2,1)}), bf16[8,24,768]{2,1,0:T(8,128)(2,1)S(1)}, u32[]{:S(2)}, u32[]{:S(2)}) async-start(bf16[8,24,768]{2,1,0:T(8,128)(2,1)} %get-tuple-element.119), calls=%async_computation.1 | async-start | bytes 589824 | tf_op jit(solution)/shard_map/all_to_all | solution.py:60
  66.7 2.0 collective-permute-start.11
  68.7 7.2 %collective-permute-start.13 = (bf16[192,768]{1,0:T(8,128)(2,1)S(1)}, bf16[192,768]{1,0:T(8,128)(2,1)S(1)}, u32[]{:S(2)}, u32[]{:S(2)}) collective-permute-start(bf16[192,768]{1,0:T(8,128)(2,1)S(1)} %collective-permute-done.12.rest_2_), channel_id=1, source_target_pairs={{0,8},{8,0},{16,24},{24,16},{1,9},{9,1},{17,25},{25,17},{2,10},{10... | collective-permute-start | bytes 884744 | tf_op jit(solution)/shard_map/ppermute | solution.py:52
  75.9 8.8 %copy-start.9 = (bf16[8,24,768]{2,1,0:T(8,128)(2,1)}, bf16[8,24,768]{2,1,0:T(8,128)(2,1)S(1)}, u32[]{:S(2)}) copy-start(bf16[8,24,768]{2,1,0:T(8,128)(2,1)S(1)} %all-to-all-done.1) | copy-start | bytes 884740
  75.9 6.8 %collective-permute-start.14 = (bf16[192,768]{1,0:T(8,128)(2,1)S(1)}, bf16[192,768]{1,0:T(8,128)(2,1)S(1)}, u32[]{:S(2)}, u32[]{:S(2)}) collective-permute-start(bf16[192,768]{1,0:T(8,128)(2,1)S(1)} %bitcast.21), channel_id=1, source_target_pairs={{0,16},{8,24},{16,0},{24,8},{1,17},{9,25},{17,1},{25,9},{2,18},{10... | collective-permute-start | bytes 884744 | tf_op jit(solution)/shard_map/ppermute | solution.py:52
  82.7 13.1 %copy-start.12 = (bf16[2,128,768]{2,1,0:T(8,128)(2,1)S(1)}, bf16[2,128,768]{2,1,0:T(8,128)(2,1)}, u32[]{:S(2)}) copy-start(bf16[2,128,768]{2,1,0:T(8,128)(2,1)} %get-tuple-element.141.rest_0_) | copy-start | bytes 1179652
  82.7 1.6 collective-permute-start.15
  82.7 2.0 collective-permute-start.16
  95.6 3.6 %collective-permute-start.18 = (bf16[192,768]{1,0:T(8,128)(2,1)}, bf16[192,768]{1,0:T(8,128)(2,1)S(1)}, u32[]{:S(2)}, u32[]{:S(2)}) collective-permute-start(bf16[192,768]{1,0:T(8,128)(2,1)} %get-tuple-element.134), channel_id=1, source_target_pairs={{0,8},{8,0},{16,24},{24,16},{1,9},{9,1},{17,25},{25,17},{2,10},{10... | collective-permute-start | bytes 884744 | tf_op jit(solution)/shard_map/ppermute | solution.py:52
  95.8 13.8 %collective-permute-start.20 = (bf16[2,128,768]{2,1,0:T(8,128)(2,1)S(1)}, bf16[2,128,768]{2,1,0:T(8,128)(2,1)S(1)}, u32[]{:S(2)}, u32[]{:S(2)}) collective-permute-start(bf16[2,128,768]{2,1,0:T(8,128)(2,1)S(1)} %copy-done.12), channel_id=1, source_target_pairs={{0,1},{1,0},{2,3},{3,2},{4,5},{5,4},{6,7},{7,6},{8,9},{9,8},{10,11... | collective-permute-start | bytes 1179656 | tf_op jit(solution)/shard_map/ppermute | solution.py:52
  97.3 12.2 %collective-permute-start.21 = (bf16[2,128,768]{2,1,0:T(8,128)(2,1)S(1)}, bf16[2,128,768]{2,1,0:T(8,128)(2,1)S(1)}, u32[]{:S(2)}, u32[]{:S(2)}) collective-permute-start(bf16[2,128,768]{2,1,0:T(8,128)(2,1)S(1)} %copy-done.12), channel_id=1, source_target_pairs={{0,2},{1,3},{2,0},{3,1},{4,6},{5,7},{6,4},{7,5},{8,10},{9,11},{10,... | collective-permute-start | bytes 1179656 | tf_op jit(solution)/shard_map/ppermute | solution.py:52
  97.6 19.2 %collective-permute-start.22 = (bf16[2,128,768]{2,1,0:T(8,128)(2,1)S(1)}, bf16[2,128,768]{2,1,0:T(8,128)(2,1)S(1)}, u32[]{:S(2)}, u32[]{:S(2)}) collective-permute-start(bf16[2,128,768]{2,1,0:T(8,128)(2,1)S(1)} %copy-done.12), channel_id=1, source_target_pairs={{0,3},{1,2},{2,1},{3,0},{4,7},{5,6},{6,5},{7,4},{8,11},{9,10},{10,... | collective-permute-start | bytes 1179656 | tf_op jit(solution)/shard_map/ppermute | solution.py:52
  99.3 17.5 %copy-start.22 = (bf16[192,768]{1,0:T(8,128)(2,1)S(1)}, bf16[192,768]{1,0:T(8,128)(2,1)}, u32[]{:S(2)}) copy-start(bf16[192,768]{1,0:T(8,128)(2,1)} %get-tuple-element.131) | copy-start | bytes 884740
  100.4 16.4 %collective-permute-start.19 = (bf16[192,768]{1,0:T(8,128)(2,1)S(1)}, bf16[192,768]{1,0:T(8,128)(2,1)S(1)}, u32[]{:S(2)}, u32[]{:S(2)}) collective-permute-start(bf16[192,768]{1,0:T(8,128)(2,1)S(1)} %add_convert_fusion.6), channel_id=1, source_target_pairs={{0,16},{8,24},{16,0},{24,8},{1,17},{9,25},{17,1},{25,9},{2,18},{10... | collective-permute-start | bytes 884744 | tf_op jit(solution)/shard_map/ppermute | solution.py:52
  101.4 15.4 %collective-permute-start.17 = (bf16[192,768]{1,0:T(8,128)(2,1)}, bf16[192,768]{1,0:T(8,128)(2,1)S(1)}, u32[]{:S(2)}, u32[]{:S(2)}) collective-permute-start(bf16[192,768]{1,0:T(8,128)(2,1)} %get-tuple-element.132), channel_id=1, source_target_pairs={{0,8},{8,0},{16,24},{24,16},{1,9},{9,1},{17,25},{25,17},{2,10},{10... | collective-permute-start | bytes 884744 | tf_op jit(solution)/shard_map/ppermute | solution.py:52
  109.5 14.9 %copy-start.13 = (bf16[2,128,768]{2,1,0:T(8,128)(2,1)}, bf16[2,128,768]{2,1,0:T(8,128)(2,1)S(1)}, u32[]{:S(2)}) copy-start(bf16[2,128,768]{2,1,0:T(8,128)(2,1)S(1)} %collective-permute-done.20.rest_1_) | copy-start | bytes 1179652
  109.5 14.9 %copy-start.14 = (bf16[2,128,768]{2,1,0:T(8,128)(2,1)}, bf16[2,128,768]{2,1,0:T(8,128)(2,1)S(1)}, u32[]{:S(2)}) copy-start(bf16[2,128,768]{2,1,0:T(8,128)(2,1)S(1)} %collective-permute-done.21.rest_2_) | copy-start | bytes 1179652
  121.6 1.8 collective-permute-start.24
  121.6 8.9 %collective-permute-start.23 = (bf16[192,768]{1,0:T(8,128)(2,1)}, bf16[192,768]{1,0:T(8,128)(2,1)S(1)}, u32[]{:S(2)}, u32[]{:S(2)}) collective-permute-start(bf16[192,768]{1,0:T(8,128)(2,1)} %get-tuple-element.146), channel_id=1, source_target_pairs={{0,8},{8,0},{16,24},{24,16},{1,9},{9,1},{17,25},{25,17},{2,10},{10... | collective-permute-start | bytes 884744 | tf_op jit(solution)/shard_map/ppermute | solution.py:52
  124.5 9.1 %collective-permute-start.25 = (bf16[192,768]{1,0:T(8,128)(2,1)S(1)}, bf16[192,768]{1,0:T(8,128)(2,1)S(1)}, u32[]{:S(2)}, u32[]{:S(2)}) collective-permute-start(bf16[192,768]{1,0:T(8,128)(2,1)S(1)} %add_convert_fusion.3), channel_id=1, source_target_pairs={{0,16},{8,24},{16,0},{24,8},{1,17},{9,25},{17,1},{25,9},{2,18},{10... | collective-permute-start | bytes 884744 | tf_op jit(solution)/shard_map/ppermute | solution.py:52
  125.5 14.7 %all-to-all-start.2 = ((bf16[8,24,768]{2,1,0:T(8,128)(2,1)}), bf16[8,24,768]{2,1,0:T(8,128)(2,1)S(1)}, u32[]{:S(2)}, u32[]{:S(2)}) async-start(bf16[8,24,768]{2,1,0:T(8,128)(2,1)} %bitcast.8), calls=%async_computation.2 | async-start | bytes 589824 | tf_op jit(solution)/shard_map/all_to_all | solution.py:60
  140.2 15.6 %all-to-all-start.3 = ((bf16[8,24,768]{2,1,0:T(8,128)(2,1)}), bf16[8,24,768]{2,1,0:T(8,128)(2,1)S(1)}, u32[]{:S(2)}, u32[]{:S(2)}) async-start(bf16[8,24,768]{2,1,0:T(8,128)(2,1)} %bitcast.9), calls=%async_computation.3 | async-start | bytes 589824 | tf_op jit(solution)/shard_map/all_to_all | solution.py:60
  155.9 25.5 %copy-start.11 = (bf16[8,24,768]{2,1,0:T(8,128)(2,1)}, bf16[8,24,768]{2,1,0:T(8,128)(2,1)S(1)}, u32[]{:S(2)}) copy-start(bf16[8,24,768]{2,1,0:T(8,128)(2,1)S(1)} %all-to-all-done.3.returned_ref) | copy-start | bytes 884740
  155.9 15.5 %all-to-all-start.4 = ((bf16[4,2,384,128]{3,2,1,0:T(8,128)(2,1)}), bf16[4,2,384,128]{3,2,1,0:T(8,128)(2,1)S(1)}, u32[]{:S(2)}, u32[]{:S(2)}) async-start(bf16[4,2,384,128]{3,2,1,0:T(8,128)(2,1)} %get-tuple-element.153), calls=%async_computation.4 | async-start | bytes 1572864 | tf_op jit(solution)/shard_map/all_to_all | solution.py:736
  160.0 1.5 collective-permute-start.26
  162.4 4.4 %collective-permute-start.27 = (f32[24,768]{1,0:T(8,128)S(1)}, f32[24,768]{1,0:T(8,128)S(1)}, u32[]{:S(2)}, u32[]{:S(2)}) collective-permute-start(f32[24,768]{1,0:T(8,128)S(1)} %add.58), channel_id=1, source_target_pairs={{0,16},{8,24},{16,0},{24,8},{1,17},{9,25},{17,1},{25,9},{2,18},{10... | collective-permute-start | bytes 221192 | tf_op jit(solution)/shard_map/ppermute | solution.py:52
  166.8 4.6 %collective-permute-start.28 = (f32[24,768]{1,0:T(8,128)S(1)}, f32[24,768]{1,0:T(8,128)S(1)}, u32[]{:S(2)}, u32[]{:S(2)}) collective-permute-start(f32[24,768]{1,0:T(8,128)S(1)} %add.59), channel_id=1, source_target_pairs={{0,1},{1,0},{2,3},{3,2},{4,5},{5,4},{6,7},{7,6},{8,9},{9,8},{10,11... | collective-permute-start | bytes 221192 | tf_op jit(solution)/shard_map/ppermute | solution.py:52
  176.6 4.8 %collective-permute-start.29 = (bf16[2,192,384]{2,1,0:T(8,128)(2,1)}, bf16[2,192,384]{2,1,0:T(8,128)(2,1)S(1)}, u32[]{:S(2)}, u32[]{:S(2)}) collective-permute-start(bf16[2,192,384]{2,1,0:T(8,128)(2,1)} %get-tuple-element.161), channel_id=1, source_target_pairs={{0,8},{8,0},{16,24},{24,16},{1,9},{9,1},{17,25},{25,17},{2,10},{10... | collective-permute-start | bytes 884744 | tf_op jit(solution)/shard_map/ppermute | solution.py:52
  176.6 4.8 %collective-permute-start.31 = (f32[24,768]{1,0:T(8,128)S(1)}, f32[24,768]{1,0:T(8,128)S(1)}, u32[]{:S(2)}, u32[]{:S(2)}) collective-permute-start(f32[24,768]{1,0:T(8,128)S(1)} %add.60), channel_id=1, source_target_pairs={{0,2},{1,3},{2,0},{3,1},{4,6},{5,7},{6,4},{7,5},{8,10},{9,11},{10,... | collective-permute-start | bytes 221192 | tf_op jit(solution)/shard_map/ppermute | solution.py:52
  178.4 4.0 %collective-permute-start.30 = (bf16[2,192,384]{2,1,0:T(8,128)(2,1)}, bf16[2,192,384]{2,1,0:T(8,128)(2,1)S(1)}, u32[]{:S(2)}, u32[]{:S(2)}) collective-permute-start(bf16[2,192,384]{2,1,0:T(8,128)(2,1)} %get-tuple-element.163), channel_id=1, source_target_pairs={{0,8},{8,0},{16,24},{24,16},{1,9},{9,1},{17,25},{25,17},{2,10},{10... | collective-permute-start | bytes 884744 | tf_op jit(solution)/shard_map/ppermute | solution.py:52
  183.5 6.8 %collective-permute-start.33 = (f32[24,768]{1,0:T(8,128)S(1)}, f32[24,768]{1,0:T(8,128)S(1)}, u32[]{:S(2)}, u32[]{:S(2)}) collective-permute-start(f32[24,768]{1,0:T(8,128)S(1)} %add.63), channel_id=1, source_target_pairs={{0,4},{1,5},{2,6},{3,7},{4,0},{5,1},{6,2},{7,3},{8,12},{9,13},{10,... | collective-permute-start | bytes 221192 | tf_op jit(solution)/shard_map/ppermute | solution.py:52
  186.0 8.4 %collective-permute-start.32 = (bf16[2,192,384]{2,1,0:T(8,128)(2,1)S(1)}, bf16[2,192,384]{2,1,0:T(8,128)(2,1)S(1)}, u32[]{:S(2)}, u32[]{:S(2)}) collective-permute-start(bf16[2,192,384]{2,1,0:T(8,128)(2,1)S(1)} %add_convert_fusion), channel_id=1, source_target_pairs={{0,16},{8,24},{16,0},{24,8},{1,17},{9,25},{17,1},{25,9},{2,18},{10... | collective-permute-start | bytes 884744 | tf_op jit(solution)/shard_map/ppermute | solution.py:52
  194.4 8.4 %collective-permute-start.34 = (bf16[192,384]{1,0:T(8,128)(2,1)S(1)}, bf16[192,384]{1,0:T(8,128)(2,1)S(1)}, u32[]{:S(2)}, u32[]{:S(2)}) collective-permute-start(bf16[192,384]{1,0:T(8,128)(2,1)S(1)} %fusion), channel_id=1, source_target_pairs={{0,4},{1,5},{2,6},{3,7},{4,0},{5,1},{6,2},{7,3},{8,12},{9,13},{10,... | collective-permute-start | bytes 442376 | tf_op jit(solution)/shard_map/ppermute | solution.py:52
  (15 other events, 64.9 us)

commit v12 on v11

--- a/solution.py
+++ b/solution.py
@@ -58,6 +58,10 @@
 
 def exchange(value):
     return lax.all_to_all(value, "expert", split_axis=0, concat_axis=0, tiled=True)
+
+
+def half_ranks(value):
+    return [value] + [swap(value, "expert", j) for j in range(1, lax.axis_size("expert") // 2)]
 
 
 def halves():
@@ -288,8 +292,7 @@
         weights_ref[h] = weights
         att_t_ref[rows, :] = dot(heads_ref[2, rows, :], weights.astype(LOW), NT)
     attended = att_t_ref[...].T.astype(LOW)
-    rows_ref[0] = normed
-    rows_ref[1] = attended
+    rows_ref[...] = attended
     low_lane = 3 * cols // 128 * 128
     for e in range(ranks):
         turned = dot(attended, w_ref[e, :, low_lane:]).T
@@ -409,7 +412,7 @@
         g_in_ref[e] = dot(rows_ref[e], pre_grad_ref[e], TN)
         slot_grad = (up_rows_ref[e].astype(FULL) * gates_ref[e][:, :1]).astype(LOW)
         g_out_ref[e] = dot(act_ref[e], slot_grad, TN)
-    token_ref[...] = jnp.zeros(token_ref.shape, FULL)
+    token_ref[...] = jnp.zeros(token_ref.shape, LOW)
 
 
 def joined(ref):
@@ -498,19 +501,20 @@
         small_ref[line : line + 1, place : place + sums.shape[1]] = sums[h : h + 1]
 
 
-def product_kernel(factors_ref, token_ref, *rest):
+def product_kernel(factors_ref, *rest):
     count, _, columns, length = factors_ref.shape
-    row_refs, piece_refs, total_ref = rest[:count], rest[count:-1], rest[-1]
+    normed_refs, attended_refs = rest[:count], rest[count : 2 * count]
+    piece_refs, total_ref = rest[2 * count : -1], rest[-1]
     cols = columns // 4
     rows = total_ref.shape[2]
     mine = lax.rem(lax.axis_index("expert"), count)
     for side in range(2):
         first, second = None, None
-        for j, ref in enumerate(row_refs):
+        for j in range(count):
             held = factors_ref[mine ^ j, side].astype(FULL)
-            part = dot(held[: 3 * cols].astype(LOW), ref[0])
+            part = dot(held[: 3 * cols].astype(LOW), normed_refs[j][...])
             first = part if first is None else first + part
-            part = dot(held[3 * cols :].astype(LOW), ref[1])
+            part = dot(held[3 * cols :].astype(LOW), attended_refs[j][...])
             second = part if second is None else second + part
         total = jnp.concatenate([first, second], axis=0).T
         for j in range(len(piece_refs)):
@@ -615,14 +619,14 @@
     up_arrived = exchange(up_slabs).reshape(ranks * slab, model_width)
 
     w_shape = (ranks, inner_width, 4 * columns_here)
-    heads, weights, rows, hidden, chance, slabs = call(
+    heads, weights, attended, hidden, chance, slabs = call(
         functools.partial(forward_kernel, places, slab, rank_slots),
         "attention_forward",
         10,
         [
             shaped(LOW, 3, inner_width, length),
             shaped(FULL, head_count, length, length),
-            shaped(LOW, 2, length, inner_width),
+            shaped(LOW, length, inner_width),
             shaped(FULL, length, model_width),
             shaped(FULL, length, experts_total),
             slabs_shape,
@@ -640,10 +644,9 @@
     slabs, up_arrived = together(slabs, up_arrived)
     arrived = exchange(slabs).reshape(ranks * slab, model_width)
     up_pieces = gather_near(gather_far(up_arrived))
-    arrived, up_pieces, rows = together(arrived, up_pieces, rows)
+    arrived, up_pieces, normed_own = together(arrived, up_pieces, normed_low)
     row_far = gather_far(arrived)
-    half = ranks // 2
-    near_rows = [swap(rows, "expert", j) for j in range(1, half)]
+    near_normed = half_ranks(normed_own)
     by_expert = (local_experts, packed_rows)
     up_rows, up_act = call(
         upstream_kernel,
@@ -652,7 +655,7 @@
         [shaped(LOW, *by_expert, model_width), shaped(FULL, *by_expert, hidden_here)],
         [pack, w_out, *up_pieces],
     )
-    row_far, up_act = together(row_far, up_act)
+    row_far, up_act, near_normed = together(row_far, up_act, near_normed)
     row_pieces = gather_near(row_far)
 
     *back, slot_rows, activated, pre_grad, gates = call(
@@ -673,26 +676,22 @@
             pltpu.VMEM((*by_expert, 128), LOW),
         ],
     )
-    kept, got = scatter_terms(back)
-    first_grad, second_grad, token = call(
-        expert_grad_kernel,
-        "expert_gradients",
-        1,
-        [shaped(FULL, *w_in.shape), shaped(FULL, *w_out.shape), shaped(FULL, 8, 128)],
-        [slot_rows, activated, pre_grad, gates, up_rows],
-    )
-    got, token, near_rows = together(got, token, near_rows)
-    back = add(kept, got).reshape(ranks, slab, model_width)
-    back, activated = together(back, activated)
-    back = exchange(back)
+    near, attended_own = together(scatter_near(back), attended)
+    kept, got = scatter_far(near)
+    near_attended = half_ranks(attended_own)
+    near, late_activated = together(near, activated)
     returned = call(
         expert_out_kernel,
         "expert_outputs",
-        12,
+        3,
         [shaped(LOW, ranks * slab, model_width)] * dps,
-        [pack_t, w_out, activated],
+        [pack_t, w_out, late_activated],
         scratch=[pltpu.VMEM((*by_expert, model_width), LOW)],
     )
+    got, returned, near_attended = together(got, returned, near_attended)
+    back = add(kept, got).reshape(ranks, slab, model_width)
+    back, returned = together(back, returned)
+    back = exchange(back)
     returned = add(*scatter_terms(returned)).reshape(ranks, slab, model_width)
     back, returned = together(back, returned)
     returned = exchange(returned)
@@ -747,7 +746,7 @@
         "weight_gradients",
         5,
         [shaped(LOW, 2, rows_here, 4 * columns_here)] * dps,
-        [factors, token, rows, *near_rows],
+        [factors, *near_normed, *near_attended],
         scratch=[pltpu.VMEM((2, dps, rows_here, 4 * columns_here), FULL)],
     )
     grads, small = together(scatter_near(grads), small)
@@ -761,7 +760,17 @@
     )
     kept, got = scatter_far(grads)
     got, output = together(got, output)
-    other = swap(add(kept[1], got[1]), "expert", ranks // 2)
+    other, activated = together(add(kept[1], got[1]), activated)
+    other = swap(other, "expert", ranks // 2)
+    first_grad, second_grad, token = call(
+        expert_grad_kernel,
+        "expert_gradients",
+        8,
+        [shaped(FULL, *w_in.shape), shaped(FULL, *w_out.shape), shaped(LOW, 16, 128)],
+        [slot_rows, activated, pre_grad, gates, up_rows],
+    )
+    other, token = together(other, token)
+    other = other + jnp.sum(token)
     grads = kept[0].astype(FULL) + got[0].astype(FULL) + other.astype(FULL)
     g_query, g_key, g_value, g_output = (
         grads[:, i * columns_here : (i + 1) * columns_here] for i in range(4)

time: 205 us -> 204 us (level)
  waiting for transfers between devices: 73.7 us -> 66.8 us
  starting transfers between devices: 54.2 us -> 58.3 us
    ppermute x35 -> x38, waiting for transfers between devices: 61.7 us -> 53.8 us  [swap(): return lax.ppermute(value, axis, [(i, i ^ mask) for i in range(count)])]
    ppermute x35 -> x38, starting transfers between devices: 31.1 us -> 35.1 us  [swap(): return lax.ppermute(value, axis, [(i, i ^ mask) for i in range(count)])]
    convert_element_type x7 -> x8, other arithmetic: 6.87 us -> 6.89 us  [add(): return (left.astype(FULL) + right.astype(FULL)).astype(dtype)]
  transfers between devices with their start and end apart: 40 -> 43, of which waited for: 22 -> 23; matrix products, arithmetic and copies ran while one was open for 5% -> 4% of each run, Pallas kernels for 20% -> 22%
where the time goes in v12:
time: 204 us; the launch traced here: 203 us
  waiting for transfers between devices  66.8 us (33%)
  starting transfers between devices  58.3 us (29%)
  Pallas kernels  58.1 us (28%)
  other arithmetic  11.7 us (6%)
  local copies, waits for them, and re-layouts  6.9 us (3%)
    pallas_call x9, Pallas kernels, call(): pl.pallas_call(kernel, out_shape=tuple(out_shape), in_specs=[VMEM] * len(...  58.1 us
    ppermute x38, waiting for transfers between devices, swap(): return lax.ppermute(value, axis, [(i, i ^ mask) for i in range(count)])  53.8 us
    ppermute x38, starting transfers between devices, swap(): return lax.ppermute(value, axis, [(i, i ^ mask) for i in range(count)])  35.1 us
    all_to_all x4, starting transfers between devices, exchange(): lax.all_to_all(value, 'expert', split_axis=0, concat_axis=0, tiled=True)  19 us
    all_to_all x4, waiting for transfers between devices, exchange(): lax.all_to_all(value, 'expert', split_axis=0, concat_axis=0, tiled=True)  13 us
    convert_element_type x8, other arithmetic, add(): return (left.astype(FULL) + right.astype(FULL)).astype(dtype)  6.89 us
    all_to_all x1, starting transfers between devices, per_device(): lax.all_to_all(factors, 'expert', split_axis=0, concat_axis=0, tiled=True...  4.18 us
  transfers between devices with their start and end apart: 43, of which 23 were waited for; matrix products, arithmetic and copies ran while one was open for 4% of the time, Pallas kernels for 22%

profile of v12, /device:TPU:0, one launch (start us, length us, event | category | flops | bytes accessed | tf_op | source)
XLA Modules:
  0.0 202.8 jit_solution(16743395148501245262)
XLA Ops:
  1.7 5.1 %collective-permute-start.2 = (bf16[1,192,384]{2,1,0:T(8,128)(2,1)S(1)}, bf16[1,192,384]{2,1,0:T(8,128)(2,1)S(1)}, u32[]{:S(2)}, u32[]{:S(2)}) collective-permute-start(bf16[1,192,384]{2,1,0:T(8,128)(2,1)S(1)} %maximum_bitcast_fusion), channel_id=1, source_target_pairs={{0,6},{1,7},{2,4},{3,5},{4,2},{5,3},{6,0},{7,1},{8,14},{9,15},{10,... | collective-permute-start | bytes 442376 | tf_op jit(solution)/shard_map/ppermute | solution.py:52
  9.4 3.3 %early.1 = (bf16[128,768]{1,0:T(8,128)(2,1)}, f32[128,16]{1,0:T(8,128)}, bf16[128,192]{1,0:T(8,128)(2,1)}, bf16[192,128]{1,0:T(8,128)(2,1)}, f32[12,128,128]{2,1,0:T(8,128)}, /*index=5*/bf16[8,24,768]{2,1,0:T(8,128)(2,1)}) custom-call(bf16[128,768]{1,0:T(8,128)(2,1)} %tokens_ref.5, s32[1,128]{1,0:T(1,128)} %bitcast.27, ...), custom_call_target="tpu_custom_call" | custom-call | bytes 10800000 | tf_op jit(solution)/shard_map/early/pallas_call | solution.py:545
  12.7 6.5 %collective-permute-done.1 = bf16[1,192,384]{2,1,0:T(8,128)(2,1)S(1)} collective-permute-done((bf16[1,192,384]{2,1,0:T(8,128)(2,1)S(1)}, bf16[1,192,384]{2,1,0:T(8,128)(2,1)S(1)}, u32[]{:S(2)}, u32[]{:S(2)}) %collective-permute-start.1) | collective-permute-done | bytes 147488 | tf_op jit(solution)/shard_map/ppermute | solution.py:52
  19.4 1.6 collective-permute-start.3
  21.0 1.5 collective-permute-start.7
  22.5 5.1 %collective-permute-done.3 = bf16[1,4,96,384]{3,2,1,0:T(8,128)(2,1)S(1)} collective-permute-done((bf16[1,4,96,384]{3,2,1,0:T(8,128)(2,1)S(1)}, bf16[1,4,96,384]{3,2,1,0:T(8,128)(2,1)S(1)}, u32[]{:S(2)}, u32[]{:S(2)}) %collective-permute-start.3) | collective-permute-done | bytes 294944 | tf_op jit(solution)/shard_map/ppermute | solution.py:52
  27.6 1.6 collective-permute-start.5
  29.3 1.6 collective-permute-start.9
  31.4 10.0 %collective-permute-done.5.rest_2_ = bf16[2,4,96,384]{3,2,1,0:T(8,128)(2,1)S(1)} collective-permute-done((bf16[2,4,96,384]{3,2,1,0:T(8,128)(2,1)S(1)}, bf16[2,4,96,384]{3,2,1,0:T(8,128)(2,1)S(1)}, u32[]{:S(2)}, u32[]{:S(2)}) %collective-permute-start.5) | collective-permute-done | bytes 589856 | tf_op jit(solution)/shard_map/ppermute | solution.py:52
  41.4 1.1 collective-permute-done.9.rest_6_
  43.4 1.1 collective-permute-done.10.rest_7_
  45.4 4.3 %all-to-all-start = ((bf16[8,24,768]{2,1,0:T(8,128)(2,1)}), bf16[8,24,768]{2,1,0:T(8,128)(2,1)}, u32[]{:S(2)}, u32[]{:S(2)}) async-start(bf16[8,24,768]{2,1,0:T(8,128)(2,1)} %get-tuple-element.137), calls=%async_computation | async-start | bytes 589824 | tf_op jit(solution)/shard_map/all_to_all | solution.py:60
  49.8 9.9 %attention_forward.1 = (bf16[3,768,128]{2,1,0:T(8,128)(2,1)}, f32[12,128,128]{2,1,0:T(8,128)}, bf16[128,768]{1,0:T(8,128)(2,1)}, f32[128,768]{1,0:T(8,128)}, f32...) custom-call(bf16[128,768]{1,0:T(8,128)(2,1)} %tokens_ref.5, bf16[128,768]{1,0:T(8,128)(2,1)} %get-tuple-element.181.normed_ref.rest_0_, ...), custom_call_target="tpu_custom_call" | custom-call | bytes 36000000 | tf_op jit(solution)/shard_map/attention_forward/pallas_call | solution.py:545
  60.8 5.9 %all-to-all-start.1 = ((bf16[8,24,768]{2,1,0:T(8,128)(2,1)}), bf16[8,24,768]{2,1,0:T(8,128)(2,1)S(1)}, u32[]{:S(2)}, u32[]{:S(2)}) async-start(bf16[8,24,768]{2,1,0:T(8,128)(2,1)} %get-tuple-element.138), calls=%async_computation.1 | async-start | bytes 589824 | tf_op jit(solution)/shard_map/all_to_all | solution.py:60
  66.7 2.0 collective-permute-done.12.rest_2_
  68.7 7.1 %all-to-all-done.1 = bf16[8,24,768]{2,1,0:T(8,128)(2,1)S(1)} async-done(((bf16[8,24,768]{2,1,0:T(8,128)(2,1)}), bf16[8,24,768]{2,1,0:T(8,128)(2,1)S(1)}, u32[]{:S(2)}, u32[]{:S(2)}) %all-to-all-start.1) | async-done | bytes 294944 | tf_op jit(solution)/shard_map/all_to_all | solution.py:60
  77.7 2.2 %collective-permute-start.16 = (bf16[128,768]{1,0:T(8,128)(2,1)}, bf16[128,768]{1,0:T(8,128)(2,1)S(1)}, u32[]{:S(2)}, u32[]{:S(2)}) collective-permute-start(bf16[128,768]{1,0:T(8,128)(2,1)} %get-tuple-element.181.normed_ref.rest_0_), channel_id=1, source_target_pairs={{0,2},{1,3},{2,0},{3,1},{4,6},{5,7},{6,4},{7,5},{8,10},{9,11},{10,... | collective-permute-start | bytes 589832 | tf_op jit(solution)/shard_map/ppermute | solution.py:52
  80.4 4.5 %upstream_rows.1 = (bf16[2,320,768]{2,1,0:T(8,128)(2,1)}, f32[2,320,768]{2,1,0:T(8,128)}) custom-call(bf16[160,192]{1,0:T(8,128)(2,1)} %constant.11.clone.pack_ref, bf16[2,768,768]{2,1,0:T(8,128)(2,1)} %w_out_ref.3, bf16[192,768]{1,0:T(8,128)(2,1)} %bitcast.6.rest_0_, bf16[192,768]{1,0:T(8,128)(2,1)} %copy-done.14, bf16[192,768]{1,0:T(8,128)(2,1)} %copy-done.13, ...), custom_call_target="tpu_custom_call" | custom-call | bytes 18000000 | tf_op jit(solution)/shard_map/upstream_rows/pallas_call | solution.py:545
  84.8 1.5 collective-permute-done.16.rest_2_
  89.5 9.9 %experts.1 = (bf16[192,768]{1,0:T(8,128)(2,1)}, bf16[192,768]{1,0:T(8,128)(2,1)}, bf16[192,768]{1,0:T(8,128)(2,1)}, bf16[192,768]{1,0:T(8,128)(2,1)}, bf16[2,320...) custom-call(bf16[160,192]{1,0:T(8,128)(2,1)} %constant.11.clone.pack_r, ...), custom_call_target="tpu_custom_call" | custom-call | bytes 36000000 | tf_op jit(solution)/shard_map/experts/pallas_call | solution.py:545
  99.9 1.3 collective-permute-done.20
  103.3 1.2 collective-permute-start.22
  104.5 1.4 collective-permute-start.25
  105.8 1.5 collective-permute-start.24
  107.9 4.0 %expert_outputs.1 = (bf16[192,768]{1,0:T(8,128)(2,1)}, bf16[192,768]{1,0:T(8,128)(2,1)}, bf16[192,768]{1,0:T(8,128)(2,1)}, bf16[192,768]{1,0:T(8,128)(2,1)}) custom-call(bf16[192,160]{1,0:T(8,128)(2,1)} %constant.12.clone.pack_t_ref, bf16[2,768,768]{2,1,0:T(8,128)(2,1)} %w_out_ref.3, bf16[2,320,768]{2,1,0:T(8,128)(2,1)} %get-tuple-element.203.act_ref), custom_call_target="tpu_custom_call" | custom-call | bytes 10800000 | tf_op jit(solution)/shard_map/expert_outputs/pallas_call | solution.py:545
  111.9 1.2 collective-permute-done.25.rest_7_
  113.2 3.1 %collective-permute-done.24.rest_6_ = bf16[128,768]{1,0:T(8,128)(2,1)S(1)} collective-permute-done((bf16[128,768]{1,0:T(8,128)(2,1)S(1)}, bf16[128,768]{1,0:T(8,128)(2,1)S(1)}, u32[]{:S(2)}, u32[]{:S(2)}) %collective-permute-start.24) | collective-permute-done | bytes 196640 | tf_op jit(solution)/shard_map/ppermute | solution.py:52
  117.6 1.3 collective-permute-done.27
  120.9 5.2 %all-to-all-start.2 = ((bf16[8,24,768]{2,1,0:T(8,128)(2,1)}), bf16[8,24,768]{2,1,0:T(8,128)(2,1)S(1)}, u32[]{:S(2)}, u32[]{:S(2)}) async-start(bf16[8,24,768]{2,1,0:T(8,128)(2,1)} %bitcast.8), calls=%async_computation.2 | async-start | bytes 589824 | tf_op jit(solution)/shard_map/all_to_all | solution.py:60
  126.1 3.0 %collective-permute-done.28 = bf16[192,768]{1,0:T(8,128)(2,1)S(1)} collective-permute-done((bf16[192,768]{1,0:T(8,128)(2,1)S(1)}, bf16[192,768]{1,0:T(8,128)(2,1)S(1)}, u32[]{:S(2)}, u32[]{:S(2)}) %collective-permute-start.28) | collective-permute-done | bytes 294944 | tf_op jit(solution)/shard_map/ppermute | solution.py:52
  129.9 5.8 %all-to-all-done.2.rest_8_ = bf16[8,24,768]{2,1,0:T(8,128)(2,1)S(1)} async-done(((bf16[8,24,768]{2,1,0:T(8,128)(2,1)}), bf16[8,24,768]{2,1,0:T(8,128)(2,1)S(1)}, u32[]{:S(2)}, u32[]{:S(2)}) %all-to-all-start.2) | async-done | bytes 294944 | tf_op jit(solution)/shard_map/all_to_all | solution.py:60
  135.7 3.6 %all-to-all-start.3 = ((bf16[8,24,768]{2,1,0:T(8,128)(2,1)}), bf16[8,24,768]{2,1,0:T(8,128)(2,1)S(1)}, u32[]{:S(2)}, u32[]{:S(2)}) async-start(bf16[8,24,768]{2,1,0:T(8,128)(2,1)} %bitcast.9), calls=%async_computation.3 | async-start | bytes 589824 | tf_op jit(solution)/shard_map/all_to_all | solution.py:60
  139.3 12.0 %attention_backward.1 = (f32[128,768]{1,0:T(8,128)}, f32[24,768]{1,0:T(8,128)}, bf16[4,2,384,128]{3,2,1,0:T(8,128)(2,1)}) custom-call(bf16[128,768]{1,0:T(8,128)(2,1)} %tokens_ref.5, f32[2,768]{1,0:T(2,128)} %maximum_convert_fusion.gain_ref, bf16[16,768]{1,0:T(8,128)(2,1)} %bitcast.25, f32[128,16]{1,0:T(8,128)} %get-tuple-element.117.hits_ref, ...), custom_call_target="tpu_custom_call" | custom-call | bytes 43200000 | tf_op jit(solution)/shard_map/attention_backward/pallas_call | solution.py:545
  151.4 4.2 %all-to-all-start.4 = ((bf16[4,2,384,128]{3,2,1,0:T(8,128)(2,1)}), bf16[4,2,384,128]{3,2,1,0:T(8,128)(2,1)S(1)}, u32[]{:S(2)}, u32[]{:S(2)}) async-start(bf16[4,2,384,128]{3,2,1,0:T(8,128)(2,1)} %get-tuple-element.178), calls=%async_computation.4 | async-start | bytes 1572864 | tf_op jit(solution)/shard_map/all_to_all | solution.py:735
  155.5 1.5 collective-permute-done.29
  157.9 1.3 collective-permute-start.30
  159.3 3.1 %collective-permute-done.30 = f32[24,768]{1,0:T(8,128)S(1)} collective-permute-done((f32[24,768]{1,0:T(8,128)S(1)}, f32[24,768]{1,0:T(8,128)S(1)}, u32[]{:S(2)}, u32[]{:S(2)}) %collective-permute-start.30) | collective-permute-done | bytes 73760 | tf_op jit(solution)/shard_map/ppermute | solution.py:52
  162.3 2.1 %collective-permute-start.31 = (f32[24,768]{1,0:T(8,128)S(1)}, f32[24,768]{1,0:T(8,128)S(1)}, u32[]{:S(2)}, u32[]{:S(2)}) collective-permute-start(f32[24,768]{1,0:T(8,128)S(1)} %add.65), channel_id=1, source_target_pairs={{0,1},{1,0},{2,3},{3,2},{4,5},{5,4},{6,7},{7,6},{8,9},{9,8},{10,11... | collective-permute-start | bytes 221192 | tf_op jit(solution)/shard_map/ppermute | solution.py:52
  164.4 2.6 %collective-permute-done.31 = f32[24,768]{1,0:T(8,128)S(1)} collective-permute-done((f32[24,768]{1,0:T(8,128)S(1)}, f32[24,768]{1,0:T(8,128)S(1)}, u32[]{:S(2)}, u32[]{:S(2)}) %collective-permute-start.31) | collective-permute-done | bytes 73760 | tf_op jit(solution)/shard_map/ppermute | solution.py:52
  167.9 4.3 %weight_gradients.1 = (bf16[2,192,384]{2,1,0:T(8,128)(2,1)}, bf16[2,192,384]{2,1,0:T(8,128)(2,1)}, bf16[2,192,384]{2,1,0:T(8,128)(2,1)}, bf16[2,192,384]{2,1,0:T(8,128)(2,1)}) custom-call(bf16[4,2,384,128]{3,2,1,0:T(8,128)(2,1)} %copy-done.2, bf16[128,768]{1,0:T(8,128)(2,1)} %get-tuple-element.181.normed_ref.rest_0_, bf16[128,768]{1,0:T(8,128)(2,1)} %copy-done.22, ...), custom_call_target="tpu_custom_call" | custom-call | bytes 18000000 | tf_op jit(solution)/shard_map/weight_gradients/pallas_call | solution.py:545
  172.3 1.8 collective-permute-start.34
  174.3 2.7 %collective-permute-done.34 = f32[24,768]{1,0:T(8,128)S(1)} collective-permute-done((f32[24,768]{1,0:T(8,128)S(1)}, f32[24,768]{1,0:T(8,128)S(1)}, u32[]{:S(2)}, u32[]{:S(2)}) %collective-permute-start.34) | collective-permute-done | bytes 73760 | tf_op jit(solution)/shard_map/ppermute | solution.py:52
  179.1 2.4 %collective-permute-start.36 = (f32[24,768]{1,0:T(8,128)S(1)}, f32[24,768]{1,0:T(8,128)S(1)}, u32[]{:S(2)}, u32[]{:S(2)}) collective-permute-start(f32[24,768]{1,0:T(8,128)S(1)} %add.69), channel_id=1, source_target_pairs={{0,4},{1,5},{2,6},{3,7},{4,0},{5,1},{6,2},{7,3},{8,12},{9,13},{10,... | collective-permute-start | bytes 221192 | tf_op jit(solution)/shard_map/ppermute | solution.py:52
  181.5 1.3 collective-permute-start.35
  182.8 2.1 %output_rows.1 = bf16[128,768]{1,0:T(8,128)(2,1)} custom-call(f32[128,768]{1,0:T(8,128)} %get-tuple-element.132.hidden_ref, f32[128,16]{1,0:T(8,128)} %get-tuple-element.133.chance_ref, f32[128,16]{1,0:T(8,128)} %get-tuple-element.117.hits_ref, bf16[128,192]{1,0:T(8,128)(2,1)} %get-tuple-element.118.mask_ref, bf16[8,24,768]{2,1,0:T(8,128)(2,1)} %copy-done.11), custom_call_target="tpu_custom_call" | custom-call | bytes 7200000 | tf_op jit(solution)/shard_map/output_rows/pallas_call | solution.py:545
  186.6 3.3 %collective-permute-done.35 = bf16[2,192,384]{2,1,0:T(8,128)(2,1)S(1)} collective-permute-done((bf16[2,192,384]{2,1,0:T(8,128)(2,1)S(1)}, bf16[2,192,384]{2,1,0:T(8,128)(2,1)S(1)}, u32[]{:S(2)}, u32[]{:S(2)}) %collective-permute-start.35) | collective-permute-done | bytes 294944 | tf_op jit(solution)/shard_map/ppermute | solution.py:52
  191.8 8.2 %expert_gradients.1 = (f32[2,768,768]{2,1,0:T(8,128)}, f32[2,768,768]{2,1,0:T(8,128)}, bf16[16,128]{1,0:T(8,128)(2,1)}) custom-call(bf16[2,320,768]{2,1,0:T(8,128)(2,1)} %get-tuple-element.202.rows_ref, bf16[2,320,768]{2,1,0:T(8,128)(2,1)} %get-tuple-element.203.act_ref, bf16[2,320,768]{2,1,0:T(8,128)(2,1)} %get-tuple-element.204.pre_grad_ref, ...), custom_call_target="tpu_custom_call" | custom-call | bytes 28800000 | tf_op jit(solution)/shard_map/expert_gradients/pallas_call | solution.py:545
  200.0 1.3 reduce_sum.12
  (128 shorter events, 29.3 us)
Async XLA Ops:
  1.7 11.1 %collective-permute-start.2 = (bf16[1,192,384]{2,1,0:T(8,128)(2,1)S(1)}, bf16[1,192,384]{2,1,0:T(8,128)(2,1)S(1)}, u32[]{:S(2)}, u32[]{:S(2)}) collective-permute-start(bf16[1,192,384]{2,1,0:T(8,128)(2,1)S(1)} %maximum_bitcast_fusion), channel_id=1, source_target_pairs={{0,6},{1,7},{2,4},{3,5},{4,2},{5,3},{6,0},{7,1},{8,14},{9,15},{10,... | collective-permute-start | bytes 442376 | tf_op jit(solution)/shard_map/ppermute | solution.py:52
  6.8 12.5 %collective-permute-start.1 = (bf16[1,192,384]{2,1,0:T(8,128)(2,1)S(1)}, bf16[1,192,384]{2,1,0:T(8,128)(2,1)S(1)}, u32[]{:S(2)}, u32[]{:S(2)}) collective-permute-start(bf16[1,192,384]{2,1,0:T(8,128)(2,1)S(1)} %maximum_bitcast_fusion), channel_id=1, source_target_pairs={{0,4},{1,5},{2,6},{3,7},{4,0},{5,1},{6,2},{7,3},{8,12},{9,13},{10,... | collective-permute-start | bytes 442376 | tf_op jit(solution)/shard_map/ppermute | solution.py:52
  6.8 12.5 %collective-permute-start = (bf16[1,192,384]{2,1,0:T(8,128)(2,1)S(1)}, bf16[1,192,384]{2,1,0:T(8,128)(2,1)S(1)}, u32[]{:S(2)}, u32[]{:S(2)}) collective-permute-start(bf16[1,192,384]{2,1,0:T(8,128)(2,1)S(1)} %maximum_bitcast_fusion), channel_id=1, source_target_pairs={{0,2},{1,3},{2,0},{3,1},{4,6},{5,7},{6,4},{7,5},{8,10},{9,11},{10,... | collective-permute-start | bytes 442376 | tf_op jit(solution)/shard_map/ppermute | solution.py:52
  19.4 8.1 %collective-permute-start.3 = (bf16[1,4,96,384]{3,2,1,0:T(8,128)(2,1)S(1)}, bf16[1,4,96,384]{3,2,1,0:T(8,128)(2,1)S(1)}, u32[]{:S(2)}, u32[]{:S(2)}) collective-permute-start(bf16[1,4,96,384]{3,2,1,0:T(8,128)(2,1)S(1)} %get-tuple-element.215), channel_id=1, source_target_pairs={{0,1},{1,0},{2,3},{3,2},{4,5},{5,4},{6,7},{7,6},{8,9},{9,8},{10,11... | collective-permute-start | bytes 884744 | tf_op jit(solution)/shard_map/ppermute | solution.py:52
  21.0 8.2 %collective-permute-start.7 = (bf16[1,4,96,384]{3,2,1,0:T(8,128)(2,1)S(1)}, bf16[1,4,96,384]{3,2,1,0:T(8,128)(2,1)S(1)}, u32[]{:S(2)}, u32[]{:S(2)}) collective-permute-start(bf16[1,4,96,384]{3,2,1,0:T(8,128)(2,1)S(1)} %get-tuple-element.214), channel_id=1, source_target_pairs={{0,16},{8,24},{16,0},{24,8},{1,17},{9,25},{17,1},{25,9},{2,18},{10... | collective-permute-start | bytes 884744 | tf_op jit(solution)/shard_map/ppermute | solution.py:52
  27.6 13.8 %collective-permute-start.5 = (bf16[2,4,96,384]{3,2,1,0:T(8,128)(2,1)S(1)}, bf16[2,4,96,384]{3,2,1,0:T(8,128)(2,1)S(1)}, u32[]{:S(2)}, u32[]{:S(2)}) collective-permute-start(bf16[2,4,96,384]{3,2,1,0:T(8,128)(2,1)S(1)} %pad_maximum_fusion.1.rest_0_), channel_id=1, source_target_pairs={{0,16},{8,24},{16,0},{24,8},{1,17},{9,25},{17,1},{25,9},{2,18},{10... | collective-permute-start | bytes 1769480 | tf_op jit(solution)/shard_map/ppermute | solution.py:52
  29.3 13.2 %collective-permute-start.9 = (bf16[2,4,96,384]{3,2,1,0:T(8,128)(2,1)S(1)}, bf16[2,4,96,384]{3,2,1,0:T(8,128)(2,1)S(1)}, u32[]{:S(2)}, u32[]{:S(2)}) collective-permute-start(bf16[2,4,96,384]{3,2,1,0:T(8,128)(2,1)S(1)} %pad_maximum_fusion.2.rest_4_), channel_id=1, source_target_pairs={{0,1},{1,0},{2,3},{3,2},{4,5},{5,4},{6,7},{7,6},{8,9},{9,8},{10,11... | collective-permute-start | bytes 1769480 | tf_op jit(solution)/shard_map/ppermute | solution.py:52
  30.9 11.7 %collective-permute-start.4 = (bf16[2,4,96,384]{3,2,1,0:T(8,128)(2,1)S(1)}, bf16[2,4,96,384]{3,2,1,0:T(8,128)(2,1)S(1)}, u32[]{:S(2)}, u32[]{:S(2)}) collective-permute-start(bf16[2,4,96,384]{3,2,1,0:T(8,128)(2,1)S(1)} %pad_maximum_fusion.1.rest_0_), channel_id=1, source_target_pairs={{0,8},{8,0},{16,24},{24,16},{1,9},{9,1},{17,25},{25,17},{2,10},{10... | collective-permute-start | bytes 1769480 | tf_op jit(solution)/shard_map/ppermute | solution.py:52
  30.9 11.7 %collective-permute-start.8 = (bf16[2,4,96,384]{3,2,1,0:T(8,128)(2,1)S(1)}, bf16[2,4,96,384]{3,2,1,0:T(8,128)(2,1)S(1)}, u32[]{:S(2)}, u32[]{:S(2)}) collective-permute-start(bf16[2,4,96,384]{3,2,1,0:T(8,128)(2,1)S(1)} %pad_maximum_fusion.2.rest_4_), channel_id=1, source_target_pairs={{0,8},{8,0},{16,24},{24,16},{1,9},{9,1},{17,25},{25,17},{2,10},{10... | collective-permute-start | bytes 1769480 | tf_op jit(solution)/shard_map/ppermute | solution.py:52
  41.4 2.0 collective-permute-start.6
  42.6 2.0 collective-permute-start.10
  45.4 14.3 %all-to-all-start = ((bf16[8,24,768]{2,1,0:T(8,128)(2,1)}), bf16[8,24,768]{2,1,0:T(8,128)(2,1)}, u32[]{:S(2)}, u32[]{:S(2)}) async-start(bf16[8,24,768]{2,1,0:T(8,128)(2,1)} %get-tuple-element.137), calls=%async_computation | async-start | bytes 589824 | tf_op jit(solution)/shard_map/all_to_all | solution.py:60
  59.7 9.0 %collective-permute-start.12 = (bf16[192,768]{1,0:T(8,128)(2,1)}, bf16[192,768]{1,0:T(8,128)(2,1)S(1)}, u32[]{:S(2)}, u32[]{:S(2)}) collective-permute-start(bf16[192,768]{1,0:T(8,128)(2,1)} %bitcast.6.rest_0_), channel_id=1, source_target_pairs={{0,16},{8,24},{16,0},{24,8},{1,17},{9,25},{17,1},{25,9},{2,18},{10... | collective-permute-start | bytes 884744 | tf_op jit(solution)/shard_map/ppermute | solution.py:52
  60.8 15.1 %all-to-all-start.1 = ((bf16[8,24,768]{2,1,0:T(8,128)(2,1)}), bf16[8,24,768]{2,1,0:T(8,128)(2,1)S(1)}, u32[]{:S(2)}, u32[]{:S(2)}) async-start(bf16[8,24,768]{2,1,0:T(8,128)(2,1)} %get-tuple-element.138), calls=%async_computation.1 | async-start | bytes 589824 | tf_op jit(solution)/shard_map/all_to_all | solution.py:60
  66.7 2.0 collective-permute-start.11
  68.7 7.2 %collective-permute-start.13 = (bf16[192,768]{1,0:T(8,128)(2,1)S(1)}, bf16[192,768]{1,0:T(8,128)(2,1)S(1)}, u32[]{:S(2)}, u32[]{:S(2)}) collective-permute-start(bf16[192,768]{1,0:T(8,128)(2,1)S(1)} %collective-permute-done.12.rest_2_), channel_id=1, source_target_pairs={{0,8},{8,0},{16,24},{24,16},{1,9},{9,1},{17,25},{25,17},{2,10},{10... | collective-permute-start | bytes 884744 | tf_op jit(solution)/shard_map/ppermute | solution.py:52
  75.9 10.5 %collective-permute-start.14 = (bf16[192,768]{1,0:T(8,128)(2,1)S(1)}, bf16[192,768]{1,0:T(8,128)(2,1)S(1)}, u32[]{:S(2)}, u32[]{:S(2)}) collective-permute-start(bf16[192,768]{1,0:T(8,128)(2,1)S(1)} %bitcast.21), channel_id=1, source_target_pairs={{0,16},{8,24},{16,0},{24,8},{1,17},{9,25},{17,1},{25,9},{2,18},{10... | collective-permute-start | bytes 884744 | tf_op jit(solution)/shard_map/ppermute | solution.py:52
  76.9 8.0 %collective-permute-start.17 = (bf16[128,768]{1,0:T(8,128)(2,1)}, bf16[128,768]{1,0:T(8,128)(2,1)S(1)}, u32[]{:S(2)}, u32[]{:S(2)}) collective-permute-start(bf16[128,768]{1,0:T(8,128)(2,1)} %get-tuple-element.181.normed_ref.rest_0_), channel_id=1, source_target_pairs={{0,3},{1,2},{2,1},{3,0},{4,7},{5,6},{6,5},{7,4},{8,11},{9,10},{10,... | collective-permute-start | bytes 589832 | tf_op jit(solution)/shard_map/ppermute | solution.py:52
  77.7 8.7 %collective-permute-start.16 = (bf16[128,768]{1,0:T(8,128)(2,1)}, bf16[128,768]{1,0:T(8,128)(2,1)S(1)}, u32[]{:S(2)}, u32[]{:S(2)}) collective-permute-start(bf16[128,768]{1,0:T(8,128)(2,1)} %get-tuple-element.181.normed_ref.rest_0_), channel_id=1, source_target_pairs={{0,2},{1,3},{2,0},{3,1},{4,6},{5,7},{6,4},{7,5},{8,10},{9,11},{10,... | collective-permute-start | bytes 589832 | tf_op jit(solution)/shard_map/ppermute | solution.py:52
  79.8 6.5 %collective-permute-start.15 = (bf16[128,768]{1,0:T(8,128)(2,1)}, bf16[128,768]{1,0:T(8,128)(2,1)S(1)}, u32[]{:S(2)}, u32[]{:S(2)}) collective-permute-start(bf16[128,768]{1,0:T(8,128)(2,1)} %get-tuple-element.181.normed_ref.rest_0_), channel_id=1, source_target_pairs={{0,1},{1,0},{2,3},{3,2},{4,5},{5,4},{6,7},{7,6},{8,9},{9,8},{10,11... | collective-permute-start | bytes 589832 | tf_op jit(solution)/shard_map/ppermute | solution.py:52
  84.8 45.1 %copy-start.20 = (bf16[128,768]{1,0:T(8,128)(2,1)}, bf16[128,768]{1,0:T(8,128)(2,1)S(1)}, u32[]{:S(2)}) copy-start(bf16[128,768]{1,0:T(8,128)(2,1)S(1)} %collective-permute-done.17.rest_3_) | copy-start | bytes 589828
  86.4 43.5 %copy-start.21 = (bf16[128,768]{1,0:T(8,128)(2,1)}, bf16[128,768]{1,0:T(8,128)(2,1)S(1)}, u32[]{:S(2)}) copy-start(bf16[128,768]{1,0:T(8,128)(2,1)S(1)} %collective-permute-done.16.rest_2_) | copy-start | bytes 589828
  86.4 43.5 %copy-start.22 = (bf16[128,768]{1,0:T(8,128)(2,1)}, bf16[128,768]{1,0:T(8,128)(2,1)S(1)}, u32[]{:S(2)}) copy-start(bf16[128,768]{1,0:T(8,128)(2,1)S(1)} %collective-permute-done.15.rest_1_) | copy-start | bytes 589828
  86.4 1.6 collective-permute-start.18
  86.5 2.0 collective-permute-start.19
  99.4 1.8 collective-permute-start.20
  99.5 2.7 %collective-permute-start.21 = (bf16[192,768]{1,0:T(8,128)(2,1)}, bf16[192,768]{1,0:T(8,128)(2,1)S(1)}, u32[]{:S(2)}, u32[]{:S(2)}) collective-permute-start(bf16[192,768]{1,0:T(8,128)(2,1)} %get-tuple-element.153), channel_id=1, source_target_pairs={{0,8},{8,0},{16,24},{24,16},{1,9},{9,1},{17,25},{25,17},{2,10},{10... | collective-permute-start | bytes 884744 | tf_op jit(solution)/shard_map/ppermute | solution.py:52
  103.3 13.0 %collective-permute-start.22 = (bf16[192,768]{1,0:T(8,128)(2,1)S(1)}, bf16[192,768]{1,0:T(8,128)(2,1)S(1)}, u32[]{:S(2)}, u32[]{:S(2)}) collective-permute-start(bf16[192,768]{1,0:T(8,128)(2,1)S(1)} %add_convert_fusion.6), channel_id=1, source_target_pairs={{0,16},{8,24},{16,0},{24,8},{1,17},{9,25},{17,1},{25,9},{2,18},{10... | collective-permute-start | bytes 884744 | tf_op jit(solution)/shard_map/ppermute | solution.py:52
  104.5 8.7 %collective-permute-start.25 = (bf16[128,768]{1,0:T(8,128)(2,1)S(1)}, bf16[128,768]{1,0:T(8,128)(2,1)S(1)}, u32[]{:S(2)}, u32[]{:S(2)}) collective-permute-start(bf16[128,768]{1,0:T(8,128)(2,1)S(1)} %copy-done.19), channel_id=1, source_target_pairs={{0,3},{1,2},{2,1},{3,0},{4,7},{5,6},{6,5},{7,4},{8,11},{9,10},{10,... | collective-permute-start | bytes 589832 | tf_op jit(solution)/shard_map/ppermute | solution.py:52
  105.8 10.4 %collective-permute-start.24 = (bf16[128,768]{1,0:T(8,128)(2,1)S(1)}, bf16[128,768]{1,0:T(8,128)(2,1)S(1)}, u32[]{:S(2)}, u32[]{:S(2)}) collective-permute-start(bf16[128,768]{1,0:T(8,128)(2,1)S(1)} %copy-done.19), channel_id=1, source_target_pairs={{0,2},{1,3},{2,0},{3,1},{4,6},{5,7},{6,4},{7,5},{8,10},{9,11},{10,... | collective-permute-start | bytes 589832 | tf_op jit(solution)/shard_map/ppermute | solution.py:52
  107.4 8.9 %collective-permute-start.23 = (bf16[128,768]{1,0:T(8,128)(2,1)S(1)}, bf16[128,768]{1,0:T(8,128)(2,1)S(1)}, u32[]{:S(2)}, u32[]{:S(2)}) collective-permute-start(bf16[128,768]{1,0:T(8,128)(2,1)S(1)} %copy-done.19), channel_id=1, source_target_pairs={{0,1},{1,0},{2,3},{3,2},{4,5},{5,4},{6,7},{7,6},{8,9},{9,8},{10,11... | collective-permute-start | bytes 589832 | tf_op jit(solution)/shard_map/ppermute | solution.py:52
  113.2 38.1 %copy-start.23 = (bf16[128,768]{1,0:T(8,128)(2,1)}, bf16[128,768]{1,0:T(8,128)(2,1)S(1)}, u32[]{:S(2)}) copy-start(bf16[128,768]{1,0:T(8,128)(2,1)S(1)} %collective-permute-done.25.rest_7_) | copy-start | bytes 589828
  116.2 35.1 %copy-start.25 = (bf16[128,768]{1,0:T(8,128)(2,1)}, bf16[128,768]{1,0:T(8,128)(2,1)S(1)}, u32[]{:S(2)}) copy-start(bf16[128,768]{1,0:T(8,128)(2,1)S(1)} %collective-permute-done.23.rest_5_) | copy-start | bytes 589828
  117.1 1.8 collective-permute-start.27
  117.1 9.0 %collective-permute-start.26 = (bf16[192,768]{1,0:T(8,128)(2,1)}, bf16[192,768]{1,0:T(8,128)(2,1)S(1)}, u32[]{:S(2)}, u32[]{:S(2)}) collective-permute-start(bf16[192,768]{1,0:T(8,128)(2,1)} %get-tuple-element.171), channel_id=1, source_target_pairs={{0,8},{8,0},{16,24},{24,16},{1,9},{9,1},{17,25},{25,17},{2,10},{10... | collective-permute-start | bytes 884744 | tf_op jit(solution)/shard_map/ppermute | solution.py:52
  119.9 9.1 %collective-permute-start.28 = (bf16[192,768]{1,0:T(8,128)(2,1)S(1)}, bf16[192,768]{1,0:T(8,128)(2,1)S(1)}, u32[]{:S(2)}, u32[]{:S(2)}) collective-permute-start(bf16[192,768]{1,0:T(8,128)(2,1)S(1)} %add_convert_fusion.3), channel_id=1, source_target_pairs={{0,16},{8,24},{16,0},{24,8},{1,17},{9,25},{17,1},{25,9},{2,18},{10... | collective-permute-start | bytes 884744 | tf_op jit(solution)/shard_map/ppermute | solution.py:52
  120.9 14.8 %all-to-all-start.2 = ((bf16[8,24,768]{2,1,0:T(8,128)(2,1)}), bf16[8,24,768]{2,1,0:T(8,128)(2,1)S(1)}, u32[]{:S(2)}, u32[]{:S(2)}) async-start(bf16[8,24,768]{2,1,0:T(8,128)(2,1)} %bitcast.8), calls=%async_computation.2 | async-start | bytes 589824 | tf_op jit(solution)/shard_map/all_to_all | solution.py:60
  135.7 15.6 %all-to-all-start.3 = ((bf16[8,24,768]{2,1,0:T(8,128)(2,1)}), bf16[8,24,768]{2,1,0:T(8,128)(2,1)S(1)}, u32[]{:S(2)}, u32[]{:S(2)}) async-start(bf16[8,24,768]{2,1,0:T(8,128)(2,1)} %bitcast.9), calls=%async_computation.3 | async-start | bytes 589824 | tf_op jit(solution)/shard_map/all_to_all | solution.py:60
  151.4 15.7 %all-to-all-start.4 = ((bf16[4,2,384,128]{3,2,1,0:T(8,128)(2,1)}), bf16[4,2,384,128]{3,2,1,0:T(8,128)(2,1)S(1)}, u32[]{:S(2)}, u32[]{:S(2)}) async-start(bf16[4,2,384,128]{3,2,1,0:T(8,128)(2,1)} %get-tuple-element.178), calls=%async_computation.4 | async-start | bytes 1572864 | tf_op jit(solution)/shard_map/all_to_all | solution.py:735
  155.5 1.5 collective-permute-start.29
  157.9 4.4 %collective-permute-start.30 = (f32[24,768]{1,0:T(8,128)S(1)}, f32[24,768]{1,0:T(8,128)S(1)}, u32[]{:S(2)}, u32[]{:S(2)}) collective-permute-start(f32[24,768]{1,0:T(8,128)S(1)} %add.64), channel_id=1, source_target_pairs={{0,16},{8,24},{16,0},{24,8},{1,17},{9,25},{17,1},{25,9},{2,18},{10... | collective-permute-start | bytes 221192 | tf_op jit(solution)/shard_map/ppermute | solution.py:52
  162.3 4.7 %collective-permute-start.31 = (f32[24,768]{1,0:T(8,128)S(1)}, f32[24,768]{1,0:T(8,128)S(1)}, u32[]{:S(2)}, u32[]{:S(2)}) collective-permute-start(f32[24,768]{1,0:T(8,128)S(1)} %add.65), channel_id=1, source_target_pairs={{0,1},{1,0},{2,3},{3,2},{4,5},{5,4},{6,7},{7,6},{8,9},{9,8},{10,11... | collective-permute-start | bytes 221192 | tf_op jit(solution)/shard_map/ppermute | solution.py:52
  172.2 4.7 %collective-permute-start.32 = (bf16[2,192,384]{2,1,0:T(8,128)(2,1)}, bf16[2,192,384]{2,1,0:T(8,128)(2,1)S(1)}, u32[]{:S(2)}, u32[]{:S(2)}) collective-permute-start(bf16[2,192,384]{2,1,0:T(8,128)(2,1)} %get-tuple-element.190), channel_id=1, source_target_pairs={{0,8},{8,0},{16,24},{24,16},{1,9},{9,1},{17,25},{25,17},{2,10},{10... | collective-permute-start | bytes 884744 | tf_op jit(solution)/shard_map/ppermute | solution.py:52
  172.3 4.7 %collective-permute-start.34 = (f32[24,768]{1,0:T(8,128)S(1)}, f32[24,768]{1,0:T(8,128)S(1)}, u32[]{:S(2)}, u32[]{:S(2)}) collective-permute-start(f32[24,768]{1,0:T(8,128)S(1)} %add.66), channel_id=1, source_target_pairs={{0,2},{1,3},{2,0},{3,1},{4,6},{5,7},{6,4},{7,5},{8,10},{9,11},{10,... | collective-permute-start | bytes 221192 | tf_op jit(solution)/shard_map/ppermute | solution.py:52
  174.0 4.0 %collective-permute-start.33 = (bf16[2,192,384]{2,1,0:T(8,128)(2,1)}, bf16[2,192,384]{2,1,0:T(8,128)(2,1)S(1)}, u32[]{:S(2)}, u32[]{:S(2)}) collective-permute-start(bf16[2,192,384]{2,1,0:T(8,128)(2,1)} %get-tuple-element.192), channel_id=1, source_target_pairs={{0,8},{8,0},{16,24},{24,16},{1,9},{9,1},{17,25},{25,17},{2,10},{10... | collective-permute-start | bytes 884744 | tf_op jit(solution)/shard_map/ppermute | solution.py:52
  179.1 6.8 %collective-permute-start.36 = (f32[24,768]{1,0:T(8,128)S(1)}, f32[24,768]{1,0:T(8,128)S(1)}, u32[]{:S(2)}, u32[]{:S(2)}) collective-permute-start(f32[24,768]{1,0:T(8,128)S(1)} %add.69), channel_id=1, source_target_pairs={{0,4},{1,5},{2,6},{3,7},{4,0},{5,1},{6,2},{7,3},{8,12},{9,13},{10,... | collective-permute-start | bytes 221192 | tf_op jit(solution)/shard_map/ppermute | solution.py:52
  181.5 8.3 %collective-permute-start.35 = (bf16[2,192,384]{2,1,0:T(8,128)(2,1)S(1)}, bf16[2,192,384]{2,1,0:T(8,128)(2,1)S(1)}, u32[]{:S(2)}, u32[]{:S(2)}) collective-permute-start(bf16[2,192,384]{2,1,0:T(8,128)(2,1)S(1)} %add_convert_fusion), channel_id=1, source_target_pairs={{0,16},{8,24},{16,0},{24,8},{1,17},{9,25},{17,1},{25,9},{2,18},{10... | collective-permute-start | bytes 884744 | tf_op jit(solution)/shard_map/ppermute | solution.py:52
  189.9 10.0 %collective-permute-start.37 = (bf16[192,384]{1,0:T(8,128)(2,1)S(1)}, bf16[192,384]{1,0:T(8,128)(2,1)S(1)}, u32[]{:S(2)}, u32[]{:S(2)}) collective-permute-start(bf16[192,384]{1,0:T(8,128)(2,1)S(1)} %fusion), channel_id=1, source_target_pairs={{0,4},{1,5},{2,6},{3,7},{4,0},{5,1},{6,2},{7,3},{8,12},{9,13},{10,... | collective-permute-start | bytes 442376 | tf_op jit(solution)/shard_map/ppermute | solution.py:52
  (21 other events, 218.6 us)

commit v13 on v12

--- a/solution.py
+++ b/solution.py
@@ -154,7 +154,7 @@
 
 def place_weights(places, piece_refs, w_ref, sem):
     my_expert, my_dp = lax.axis_index("expert"), lax.axis_index("dp")
-    copies = []
+    copies, masks = [], []
     for ref, (half, offsets) in zip(piece_refs, places):
         low_count, rows = ref.shape[1], ref.shape[2]
         for index, (e_mask, d_mask) in enumerate(offsets):
@@ -163,12 +163,17 @@
                 pltpu.make_async_copy(
                     ref.at[index // low_count, index % low_count],
                     w_ref.at[my_expert ^ e_mask, pl.ds(pl.multiple_of(start, 16), rows), :],
-                    sem,
+                    sem.at[e_mask],
                 )
             )
-    for copy in copies:
-        copy.start()
-    return copies
+            masks.append(e_mask)
+    groups = [[] for _ in range(w_ref.shape[0])]
+    for copy, e_mask in zip(copies, masks):
+        groups[e_mask].append(copy)
+    for group in groups:
+        for copy in group:
+            copy.start()
+    return groups
 
 
 def dot(left, right, dims=((1,), (0,)), precision=None):
@@ -276,13 +281,14 @@
     segments = jnp.broadcast_to(seg_ref[...].astype(FULL), (length, length))
     same_doc = segments == segments.T
     normed = normed_ref[...]
-    for copy in copies:
-        copy.wait()
-    for e in range(ranks):
+    for j, group in enumerate(copies):
+        for copy in group:
+            copy.wait()
+        e = lax.axis_index("expert") ^ j
         turned = dot(normed, w_ref[e]).T
         for m in range(3):
-            qkv_ref[m, e * cols : (e + 1) * cols, :] = turned[m * cols : (m + 1) * cols]
-    heads_ref[...] = qkv_ref[...].astype(LOW)
+            qkv_ref[m, e] = turned[m * cols : (m + 1) * cols]
+    heads_ref[...] = qkv_ref[...].reshape(3, width, length).astype(LOW)
     for h in range(head_count):
         rows = slice(h * head, (h + 1) * head)
         scores = dot(heads_ref[0, rows, :], heads_ref[1, rows, :], TN) * head ** (-0.5)
@@ -406,13 +412,27 @@
 
 
 def expert_grad_kernel(
-    rows_ref, act_ref, pre_grad_ref, gates_ref, up_rows_ref, g_in_ref, g_out_ref, token_ref
+    rows_ref, act_ref, pre_grad_ref, gates_ref, up_rows_ref, g_in_ref, g_out_ref
 ):
-    for e in range(rows_ref.shape[0]):
-        g_in_ref[e] = dot(rows_ref[e], pre_grad_ref[e], TN)
-        slot_grad = (up_rows_ref[e].astype(FULL) * gates_ref[e][:, :1]).astype(LOW)
-        g_out_ref[e] = dot(act_ref[e], slot_grad, TN)
-    token_ref[...] = jnp.zeros(token_ref.shape, LOW)
+    g_in_ref[0] = dot(rows_ref[0], pre_grad_ref[0], TN)
+    slot_grad = (up_rows_ref[0].astype(FULL) * gates_ref[0][:, :1]).astype(LOW)
+    g_out_ref[0] = dot(act_ref[0], slot_grad, TN)
+
+
+def expert_gradients(shapes, args):
+    def block(item):
+        return pl.BlockSpec((1,) + item.shape[1:], lambda e: (e, 0, 0))
+
+    return pl.pallas_call(
+        expert_grad_kernel,
+        grid=(shapes[0].shape[0],),
+        out_shape=tuple(shapes),
+        in_specs=[block(item) for item in args],
+        out_specs=tuple(block(item) for item in shapes),
+        compiler_params=pltpu.CompilerParams(vmem_limit_bytes=LIMIT),
+        cost_estimate=pl.CostEstimate(flops=0, bytes_accessed=28_800_000, transcendentals=0),
+        name="expert_gradients",
+    )(*args)
 
 
 def joined(ref):
@@ -455,8 +475,9 @@
     hidden_part, ffn_gain_grad = norm_back(hidden, scale_two, gain_two, normed_two_grad)
     hidden_grad = up_ref[...].astype(FULL) + hidden_part
     turned_ref[...] = hidden_grad.astype(LOW).astype(FULL).T
-    for copy in copies:
-        copy.wait()
+    for group in copies:
+        for copy in group:
+            copy.wait()
     low_lane = 3 * cols // 128 * 128
     att_grad = None
     for e in range(ranks):
@@ -635,9 +656,9 @@
         pieces,
         [
             pltpu.VMEM(w_shape, LOW),
-            pltpu.VMEM((3, inner_width, length), FULL),
+            pltpu.VMEM((3, ranks, columns_here, length), FULL),
             pltpu.VMEM((inner_width, length), FULL),
-            pltpu.SemaphoreType.DMA,
+            pltpu.SemaphoreType.DMA((ranks,)),
         ],
     )
 
@@ -726,7 +747,7 @@
             pltpu.VMEM((inner_width, length), FULL),
             pltpu.VMEM((3, inner_width, length), FULL),
             pltpu.VMEM((head_count, 2 * length), FULL),
-            pltpu.SemaphoreType.DMA,
+            pltpu.SemaphoreType.DMA((ranks,)),
         ],
         [back],
     )
@@ -762,15 +783,11 @@
     got, output = together(got, output)
     other, activated = together(add(kept[1], got[1]), activated)
     other = swap(other, "expert", ranks // 2)
-    first_grad, second_grad, token = call(
-        expert_grad_kernel,
-        "expert_gradients",
-        8,
-        [shaped(FULL, *w_in.shape), shaped(FULL, *w_out.shape), shaped(LOW, 16, 128)],
+    first_grad, second_grad = expert_gradients(
+        [shaped(FULL, *w_in.shape), shaped(FULL, *w_out.shape)],
         [slot_rows, activated, pre_grad, gates, up_rows],
     )
-    other, token = together(other, token)
-    other = other + jnp.sum(token)
+    other, first_grad = together(other, first_grad)
     grads = kept[0].astype(FULL) + got[0].astype(FULL) + other.astype(FULL)
     g_query, g_key, g_value, g_output = (
         grads[:, i * columns_here : (i + 1) * columns_here] for i in range(4)

time: 204 us -> 201 us (0.985)
    pallas_call x9 -> x8, Pallas kernels: 58.1 us -> 50.5 us  [call(): pl.pallas_call(kernel, out_shape=tuple(out_shape), in_specs=[VMEM] * len(...]
    pallas_call x0 -> x1, Pallas kernels: none -> 6.26 us  [expert_gradients(): pl.pallas_call(expert_grad_kernel, grid=(shapes[0].shape[0],), out_shape=...]
  transfers between devices with their start and end apart: 43 -> 43, of which waited for: 23 -> 24; matrix products, arithmetic and copies ran while one was open for 4% -> 4% of each run, Pallas kernels for 22% -> 21%
where the time goes in v13:
time: 201 us; the launch traced here: 200 us
  waiting for transfers between devices  67.1 us (33%)
  starting transfers between devices  58.2 us (29%)
  Pallas kernels  56.8 us (28%)
  other arithmetic  9.73 us (5%)
  local copies, waits for them, and re-layouts  6.88 us (3%)
    ppermute x38, waiting for transfers between devices, swap(): return lax.ppermute(value, axis, [(i, i ^ mask) for i in range(count)])  54.1 us
    pallas_call x8, Pallas kernels, call(): pl.pallas_call(kernel, out_shape=tuple(out_shape), in_specs=[VMEM] * len(...  50.5 us
    ppermute x38, starting transfers between devices, swap(): return lax.ppermute(value, axis, [(i, i ^ mask) for i in range(count)])  35 us
    all_to_all x4, starting transfers between devices, exchange(): lax.all_to_all(value, 'expert', split_axis=0, concat_axis=0, tiled=True)  19.1 us
    all_to_all x4, waiting for transfers between devices, exchange(): lax.all_to_all(value, 'expert', split_axis=0, concat_axis=0, tiled=True)  13 us
    convert_element_type x8, other arithmetic, add(): return (left.astype(FULL) + right.astype(FULL)).astype(dtype)  6.9 us
    pallas_call x1, Pallas kernels, expert_gradients(): pl.pallas_call(expert_grad_kernel, grid=(shapes[0].shape[0],), out_shape=...  6.26 us
    all_to_all x1, starting transfers between devices, per_device(): lax.all_to_all(factors, 'expert', split_axis=0, concat_axis=0, tiled=True...  4.17 us
  transfers between devices with their start and end apart: 43, of which 24 were waited for; matrix products, arithmetic and copies ran while one was open for 4% of the time, Pallas kernels for 21%

profile of v13, /device:TPU:0, one launch (start us, length us, event | category | flops | bytes accessed | tf_op | source)
XLA Modules:
  0.0 199.7 jit_solution(17558367207539541944)
XLA Ops:
  1.7 5.1 %collective-permute-start.2 = (bf16[1,192,384]{2,1,0:T(8,128)(2,1)S(1)}, bf16[1,192,384]{2,1,0:T(8,128)(2,1)S(1)}, u32[]{:S(2)}, u32[]{:S(2)}) collective-permute-start(bf16[1,192,384]{2,1,0:T(8,128)(2,1)S(1)} %maximum_bitcast_fusion), channel_id=1, source_target_pairs={{0,6},{1,7},{2,4},{3,5},{4,2},{5,3},{6,0},{7,1},{8,14},{9,15},{10,... | collective-permute-start | bytes 442376 | tf_op jit(solution)/shard_map/ppermute | solution.py:52
  9.4 3.3 %early.1 = (bf16[128,768]{1,0:T(8,128)(2,1)}, f32[128,16]{1,0:T(8,128)}, bf16[128,192]{1,0:T(8,128)(2,1)}, bf16[192,128]{1,0:T(8,128)(2,1)}, f32[12,128,128]{2,1,0:T(8,128)}, /*index=5*/bf16[8,24,768]{2,1,0:T(8,128)(2,1)}) custom-call(bf16[128,768]{1,0:T(8,128)(2,1)} %tokens_ref.5, s32[1,128]{1,0:T(1,128)} %bitcast.27, ...), custom_call_target="tpu_custom_call" | custom-call | bytes 10800000 | tf_op jit(solution)/shard_map/early/pallas_call | solution.py:566
  12.7 6.5 %collective-permute-done.1 = bf16[1,192,384]{2,1,0:T(8,128)(2,1)S(1)} collective-permute-done((bf16[1,192,384]{2,1,0:T(8,128)(2,1)S(1)}, bf16[1,192,384]{2,1,0:T(8,128)(2,1)S(1)}, u32[]{:S(2)}, u32[]{:S(2)}) %collective-permute-start.1) | collective-permute-done | bytes 147488 | tf_op jit(solution)/shard_map/ppermute | solution.py:52
  19.4 1.6 collective-permute-start.3
  21.0 1.5 collective-permute-start.7
  22.5 5.1 %collective-permute-done.3 = bf16[1,4,96,384]{3,2,1,0:T(8,128)(2,1)S(1)} collective-permute-done((bf16[1,4,96,384]{3,2,1,0:T(8,128)(2,1)S(1)}, bf16[1,4,96,384]{3,2,1,0:T(8,128)(2,1)S(1)}, u32[]{:S(2)}, u32[]{:S(2)}) %collective-permute-start.3) | collective-permute-done | bytes 294944 | tf_op jit(solution)/shard_map/ppermute | solution.py:52
  27.6 1.6 collective-permute-start.5
  29.3 1.6 collective-permute-start.9
  31.4 10.0 %collective-permute-done.5.rest_2_ = bf16[2,4,96,384]{3,2,1,0:T(8,128)(2,1)S(1)} collective-permute-done((bf16[2,4,96,384]{3,2,1,0:T(8,128)(2,1)S(1)}, bf16[2,4,96,384]{3,2,1,0:T(8,128)(2,1)S(1)}, u32[]{:S(2)}, u32[]{:S(2)}) %collective-permute-start.5) | collective-permute-done | bytes 589856 | tf_op jit(solution)/shard_map/ppermute | solution.py:52
  41.4 1.1 collective-permute-done.9.rest_6_
  43.4 1.1 collective-permute-done.10.rest_7_
  45.4 4.3 %all-to-all-start = ((bf16[8,24,768]{2,1,0:T(8,128)(2,1)}), bf16[8,24,768]{2,1,0:T(8,128)(2,1)}, u32[]{:S(2)}, u32[]{:S(2)}) async-start(bf16[8,24,768]{2,1,0:T(8,128)(2,1)} %get-tuple-element.136), calls=%async_computation | async-start | bytes 589824 | tf_op jit(solution)/shard_map/all_to_all | solution.py:60
  49.8 10.4 %attention_forward.1 = (bf16[3,768,128]{2,1,0:T(8,128)(2,1)}, f32[12,128,128]{2,1,0:T(8,128)}, bf16[128,768]{1,0:T(8,128)(2,1)}, f32[128,768]{1,0:T(8,128)}, f32...) custom-call(bf16[128,768]{1,0:T(8,128)(2,1)} %tokens_ref.5, bf16[128,768]{1,0:T(8,128)(2,1)} %get-tuple-element.180.normed_ref.rest_0_, ...), custom_call_target="tpu_custom_call" | custom-call | bytes 36000000 | tf_op jit(solution)/shard_map/attention_forward/pallas_call | solution.py:566
  61.2 6.0 %all-to-all-start.1 = ((bf16[8,24,768]{2,1,0:T(8,128)(2,1)}), bf16[8,24,768]{2,1,0:T(8,128)(2,1)S(1)}, u32[]{:S(2)}, u32[]{:S(2)}) async-start(bf16[8,24,768]{2,1,0:T(8,128)(2,1)} %get-tuple-element.137), calls=%async_computation.1 | async-start | bytes 589824 | tf_op jit(solution)/shard_map/all_to_all | solution.py:60
  67.2 2.0 %collective-permute-done.12.rest_2_ = bf16[192,768]{1,0:T(8,128)(2,1)S(1)} collective-permute-done((bf16[192,768]{1,0:T(8,128)(2,1)}, bf16[192,768]{1,0:T(8,128)(2,1)S(1)}, u32[]{:S(2)}, u32[]{:S(2)}) %collective-permute-start.12) | collective-permute-done | bytes 294944 | tf_op jit(solution)/shard_map/ppermute | solution.py:52
  69.2 7.1 %all-to-all-done.1 = bf16[8,24,768]{2,1,0:T(8,128)(2,1)S(1)} async-done(((bf16[8,24,768]{2,1,0:T(8,128)(2,1)}), bf16[8,24,768]{2,1,0:T(8,128)(2,1)S(1)}, u32[]{:S(2)}, u32[]{:S(2)}) %all-to-all-start.1) | async-done | bytes 294944 | tf_op jit(solution)/shard_map/all_to_all | solution.py:60
  78.1 2.2 %collective-permute-start.16 = (bf16[128,768]{1,0:T(8,128)(2,1)}, bf16[128,768]{1,0:T(8,128)(2,1)S(1)}, u32[]{:S(2)}, u32[]{:S(2)}) collective-permute-start(bf16[128,768]{1,0:T(8,128)(2,1)} %get-tuple-element.180.normed_ref.rest_0_), channel_id=1, source_target_pairs={{0,2},{1,3},{2,0},{3,1},{4,6},{5,7},{6,4},{7,5},{8,10},{9,11},{10,... | collective-permute-start | bytes 589832 | tf_op jit(solution)/shard_map/ppermute | solution.py:52
  80.8 4.5 %upstream_rows.1 = (bf16[2,320,768]{2,1,0:T(8,128)(2,1)}, f32[2,320,768]{2,1,0:T(8,128)}) custom-call(bf16[160,192]{1,0:T(8,128)(2,1)} %constant.8.clone.pack_ref, bf16[2,768,768]{2,1,0:T(8,128)(2,1)} %w_out_ref.3, bf16[192,768]{1,0:T(8,128)(2,1)} %bitcast.6.rest_0_, bf16[192,768]{1,0:T(8,128)(2,1)} %copy-done.14, bf16[192,768]{1,0:T(8,128)(2,1)} %copy-done.13, ...), custom_call_target="tpu_custom_call" | custom-call | bytes 18000000 | tf_op jit(solution)/shard_map/upstream_rows/pallas_call | solution.py:566
  85.3 1.5 collective-permute-done.16.rest_2_
  87.4 1.1 collective-permute-done.18.rest_1_
  89.9 9.9 %experts.1 = (bf16[192,768]{1,0:T(8,128)(2,1)}, bf16[192,768]{1,0:T(8,128)(2,1)}, bf16[192,768]{1,0:T(8,128)(2,1)}, bf16[192,768]{1,0:T(8,128)(2,1)}, bf16[2,320...) custom-call(bf16[160,192]{1,0:T(8,128)(2,1)} %constant.8.clone.pack_re, ...), custom_call_target="tpu_custom_call" | custom-call | bytes 36000000 | tf_op jit(solution)/shard_map/experts/pallas_call | solution.py:566
  100.4 1.3 collective-permute-done.20
  103.7 1.2 collective-permute-start.22
  104.9 1.3 collective-permute-start.25
  106.3 1.5 collective-permute-start.24
  108.4 4.0 %expert_outputs.1 = (bf16[192,768]{1,0:T(8,128)(2,1)}, bf16[192,768]{1,0:T(8,128)(2,1)}, bf16[192,768]{1,0:T(8,128)(2,1)}, bf16[192,768]{1,0:T(8,128)(2,1)}) custom-call(bf16[192,160]{1,0:T(8,128)(2,1)} %constant.9.clone.pack_t_ref, bf16[2,768,768]{2,1,0:T(8,128)(2,1)} %w_out_ref.3, bf16[2,320,768]{2,1,0:T(8,128)(2,1)} %get-tuple-element.202.act_ref), custom_call_target="tpu_custom_call" | custom-call | bytes 10800000 | tf_op jit(solution)/shard_map/expert_outputs/pallas_call | solution.py:566
  112.4 1.2 collective-permute-done.25.rest_7_
  113.6 3.1 %collective-permute-done.24.rest_6_ = bf16[128,768]{1,0:T(8,128)(2,1)S(1)} collective-permute-done((bf16[128,768]{1,0:T(8,128)(2,1)S(1)}, bf16[128,768]{1,0:T(8,128)(2,1)S(1)}, u32[]{:S(2)}, u32[]{:S(2)}) %collective-permute-start.24) | collective-permute-done | bytes 196640 | tf_op jit(solution)/shard_map/ppermute | solution.py:52
  118.1 1.3 collective-permute-done.27
  121.4 5.1 %all-to-all-start.2 = ((bf16[8,24,768]{2,1,0:T(8,128)(2,1)}), bf16[8,24,768]{2,1,0:T(8,128)(2,1)S(1)}, u32[]{:S(2)}, u32[]{:S(2)}) async-start(bf16[8,24,768]{2,1,0:T(8,128)(2,1)} %bitcast.8), calls=%async_computation.2 | async-start | bytes 589824 | tf_op jit(solution)/shard_map/all_to_all | solution.py:60
  126.6 3.0 %collective-permute-done.28 = bf16[192,768]{1,0:T(8,128)(2,1)S(1)} collective-permute-done((bf16[192,768]{1,0:T(8,128)(2,1)S(1)}, bf16[192,768]{1,0:T(8,128)(2,1)S(1)}, u32[]{:S(2)}, u32[]{:S(2)}) %collective-permute-start.28) | collective-permute-done | bytes 294944 | tf_op jit(solution)/shard_map/ppermute | solution.py:52
  130.4 5.8 %all-to-all-done.2.rest_8_ = bf16[8,24,768]{2,1,0:T(8,128)(2,1)S(1)} async-done(((bf16[8,24,768]{2,1,0:T(8,128)(2,1)}), bf16[8,24,768]{2,1,0:T(8,128)(2,1)S(1)}, u32[]{:S(2)}, u32[]{:S(2)}) %all-to-all-start.2) | async-done | bytes 294944 | tf_op jit(solution)/shard_map/all_to_all | solution.py:60
  136.2 3.6 %all-to-all-start.3 = ((bf16[8,24,768]{2,1,0:T(8,128)(2,1)}), bf16[8,24,768]{2,1,0:T(8,128)(2,1)S(1)}, u32[]{:S(2)}, u32[]{:S(2)}) async-start(bf16[8,24,768]{2,1,0:T(8,128)(2,1)} %bitcast.9), calls=%async_computation.3 | async-start | bytes 589824 | tf_op jit(solution)/shard_map/all_to_all | solution.py:60
  139.8 12.0 %attention_backward.1 = (f32[128,768]{1,0:T(8,128)}, f32[24,768]{1,0:T(8,128)}, bf16[4,2,384,128]{3,2,1,0:T(8,128)(2,1)}) custom-call(bf16[128,768]{1,0:T(8,128)(2,1)} %tokens_ref.5, f32[2,768]{1,0:T(2,128)} %maximum_convert_fusion.gain_ref, bf16[16,768]{1,0:T(8,128)(2,1)} %bitcast.25, f32[128,16]{1,0:T(8,128)} %get-tuple-element.116.hits_ref, ...), custom_call_target="tpu_custom_call" | custom-call | bytes 43200000 | tf_op jit(solution)/shard_map/attention_backward/pallas_call | solution.py:566
  151.9 4.2 %all-to-all-start.4 = ((bf16[4,2,384,128]{3,2,1,0:T(8,128)(2,1)}), bf16[4,2,384,128]{3,2,1,0:T(8,128)(2,1)S(1)}, u32[]{:S(2)}, u32[]{:S(2)}) async-start(bf16[4,2,384,128]{3,2,1,0:T(8,128)(2,1)} %get-tuple-element.177), calls=%async_computation.4 | async-start | bytes 1572864 | tf_op jit(solution)/shard_map/all_to_all | solution.py:756
  156.1 1.5 collective-permute-done.29
  158.4 1.3 collective-permute-start.30
  159.8 3.1 %collective-permute-done.30 = f32[24,768]{1,0:T(8,128)S(1)} collective-permute-done((f32[24,768]{1,0:T(8,128)S(1)}, f32[24,768]{1,0:T(8,128)S(1)}, u32[]{:S(2)}, u32[]{:S(2)}) %collective-permute-start.30) | collective-permute-done | bytes 73760 | tf_op jit(solution)/shard_map/ppermute | solution.py:52
  162.9 2.1 %collective-permute-start.31 = (f32[24,768]{1,0:T(8,128)S(1)}, f32[24,768]{1,0:T(8,128)S(1)}, u32[]{:S(2)}, u32[]{:S(2)}) collective-permute-start(f32[24,768]{1,0:T(8,128)S(1)} %add.59), channel_id=1, source_target_pairs={{0,1},{1,0},{2,3},{3,2},{4,5},{5,4},{6,7},{7,6},{8,9},{9,8},{10,11... | collective-permute-start | bytes 221192 | tf_op jit(solution)/shard_map/ppermute | solution.py:52
  165.0 2.6 %collective-permute-done.31 = f32[24,768]{1,0:T(8,128)S(1)} collective-permute-done((f32[24,768]{1,0:T(8,128)S(1)}, f32[24,768]{1,0:T(8,128)S(1)}, u32[]{:S(2)}, u32[]{:S(2)}) %collective-permute-start.31) | collective-permute-done | bytes 73760 | tf_op jit(solution)/shard_map/ppermute | solution.py:52
  168.5 4.3 %weight_gradients.1 = (bf16[2,192,384]{2,1,0:T(8,128)(2,1)}, bf16[2,192,384]{2,1,0:T(8,128)(2,1)}, bf16[2,192,384]{2,1,0:T(8,128)(2,1)}, bf16[2,192,384]{2,1,0:T(8,128)(2,1)}) custom-call(bf16[4,2,384,128]{3,2,1,0:T(8,128)(2,1)} %copy-done.2, bf16[128,768]{1,0:T(8,128)(2,1)} %get-tuple-element.180.normed_ref.rest_0_, bf16[128,768]{1,0:T(8,128)(2,1)} %copy-done.22, ...), custom_call_target="tpu_custom_call" | custom-call | bytes 18000000 | tf_op jit(solution)/shard_map/weight_gradients/pallas_call | solution.py:566
  172.8 1.8 collective-permute-start.34
  174.8 2.7 %collective-permute-done.34 = f32[24,768]{1,0:T(8,128)S(1)} collective-permute-done((f32[24,768]{1,0:T(8,128)S(1)}, f32[24,768]{1,0:T(8,128)S(1)}, u32[]{:S(2)}, u32[]{:S(2)}) %collective-permute-start.34) | collective-permute-done | bytes 73760 | tf_op jit(solution)/shard_map/ppermute | solution.py:52
  179.6 2.5 %collective-permute-start.36 = (f32[24,768]{1,0:T(8,128)S(1)}, f32[24,768]{1,0:T(8,128)S(1)}, u32[]{:S(2)}, u32[]{:S(2)}) collective-permute-start(f32[24,768]{1,0:T(8,128)S(1)} %add.63), channel_id=1, source_target_pairs={{0,4},{1,5},{2,6},{3,7},{4,0},{5,1},{6,2},{7,3},{8,12},{9,13},{10,... | collective-permute-start | bytes 221192 | tf_op jit(solution)/shard_map/ppermute | solution.py:52
  182.1 1.3 collective-permute-start.35
  183.3 2.1 %output_rows.1 = bf16[128,768]{1,0:T(8,128)(2,1)} custom-call(f32[128,768]{1,0:T(8,128)} %get-tuple-element.131.hidden_ref, f32[128,16]{1,0:T(8,128)} %get-tuple-element.132.chance_ref, f32[128,16]{1,0:T(8,128)} %get-tuple-element.116.hits_ref, bf16[128,192]{1,0:T(8,128)(2,1)} %get-tuple-element.117.mask_ref, bf16[8,24,768]{2,1,0:T(8,128)(2,1)} %copy-done.11), custom_call_target="tpu_custom_call" | custom-call | bytes 7200000 | tf_op jit(solution)/shard_map/output_rows/pallas_call | solution.py:566
  187.1 3.3 %collective-permute-done.35 = bf16[2,192,384]{2,1,0:T(8,128)(2,1)S(1)} collective-permute-done((bf16[2,192,384]{2,1,0:T(8,128)(2,1)S(1)}, bf16[2,192,384]{2,1,0:T(8,128)(2,1)S(1)}, u32[]{:S(2)}, u32[]{:S(2)}) %collective-permute-start.35) | collective-permute-done | bytes 294944 | tf_op jit(solution)/shard_map/ppermute | solution.py:52
  192.3 6.3 %expert_gradients.1 = (f32[2,768,768]{2,1,0:T(8,128)}, f32[2,768,768]{2,1,0:T(8,128)}) custom-call(bf16[2,320,768]{2,1,0:T(8,128)(2,1)} %get-tuple-element.201.rows_ref, bf16[2,320,768]{2,1,0:T(8,128)(2,1)} %get-tuple-element.202.act_ref, bf16[2,320,768]{2,1,0:T(8,128)(2,1)} %get-tuple-element.203.pre_grad_ref, f32[2,320,128]{2,1,0:T(8,128)} %get-tuple-element.204.gates_ref, ...), custom_call_target="tpu_custom_call" | custom-call | bytes 28800000 | tf_op jit(solution)/shard_map/expert_gradients/pallas_call | solution.py:426
  (127 shorter events, 27.7 us)
Async XLA Ops:
  1.7 11.1 %collective-permute-start.2 = (bf16[1,192,384]{2,1,0:T(8,128)(2,1)S(1)}, bf16[1,192,384]{2,1,0:T(8,128)(2,1)S(1)}, u32[]{:S(2)}, u32[]{:S(2)}) collective-permute-start(bf16[1,192,384]{2,1,0:T(8,128)(2,1)S(1)} %maximum_bitcast_fusion), channel_id=1, source_target_pairs={{0,6},{1,7},{2,4},{3,5},{4,2},{5,3},{6,0},{7,1},{8,14},{9,15},{10,... | collective-permute-start | bytes 442376 | tf_op jit(solution)/shard_map/ppermute | solution.py:52
  6.8 12.5 %collective-permute-start.1 = (bf16[1,192,384]{2,1,0:T(8,128)(2,1)S(1)}, bf16[1,192,384]{2,1,0:T(8,128)(2,1)S(1)}, u32[]{:S(2)}, u32[]{:S(2)}) collective-permute-start(bf16[1,192,384]{2,1,0:T(8,128)(2,1)S(1)} %maximum_bitcast_fusion), channel_id=1, source_target_pairs={{0,4},{1,5},{2,6},{3,7},{4,0},{5,1},{6,2},{7,3},{8,12},{9,13},{10,... | collective-permute-start | bytes 442376 | tf_op jit(solution)/shard_map/ppermute | solution.py:52
  6.8 12.5 %collective-permute-start = (bf16[1,192,384]{2,1,0:T(8,128)(2,1)S(1)}, bf16[1,192,384]{2,1,0:T(8,128)(2,1)S(1)}, u32[]{:S(2)}, u32[]{:S(2)}) collective-permute-start(bf16[1,192,384]{2,1,0:T(8,128)(2,1)S(1)} %maximum_bitcast_fusion), channel_id=1, source_target_pairs={{0,2},{1,3},{2,0},{3,1},{4,6},{5,7},{6,4},{7,5},{8,10},{9,11},{10,... | collective-permute-start | bytes 442376 | tf_op jit(solution)/shard_map/ppermute | solution.py:52
  19.4 8.1 %collective-permute-start.3 = (bf16[1,4,96,384]{3,2,1,0:T(8,128)(2,1)S(1)}, bf16[1,4,96,384]{3,2,1,0:T(8,128)(2,1)S(1)}, u32[]{:S(2)}, u32[]{:S(2)}) collective-permute-start(bf16[1,4,96,384]{3,2,1,0:T(8,128)(2,1)S(1)} %get-tuple-element.213), channel_id=1, source_target_pairs={{0,1},{1,0},{2,3},{3,2},{4,5},{5,4},{6,7},{7,6},{8,9},{9,8},{10,11... | collective-permute-start | bytes 884744 | tf_op jit(solution)/shard_map/ppermute | solution.py:52
  21.0 8.2 %collective-permute-start.7 = (bf16[1,4,96,384]{3,2,1,0:T(8,128)(2,1)S(1)}, bf16[1,4,96,384]{3,2,1,0:T(8,128)(2,1)S(1)}, u32[]{:S(2)}, u32[]{:S(2)}) collective-permute-start(bf16[1,4,96,384]{3,2,1,0:T(8,128)(2,1)S(1)} %get-tuple-element.212), channel_id=1, source_target_pairs={{0,16},{8,24},{16,0},{24,8},{1,17},{9,25},{17,1},{25,9},{2,18},{10... | collective-permute-start | bytes 884744 | tf_op jit(solution)/shard_map/ppermute | solution.py:52
  27.6 13.8 %collective-permute-start.5 = (bf16[2,4,96,384]{3,2,1,0:T(8,128)(2,1)S(1)}, bf16[2,4,96,384]{3,2,1,0:T(8,128)(2,1)S(1)}, u32[]{:S(2)}, u32[]{:S(2)}) collective-permute-start(bf16[2,4,96,384]{3,2,1,0:T(8,128)(2,1)S(1)} %pad_maximum_fusion.1.rest_0_), channel_id=1, source_target_pairs={{0,16},{8,24},{16,0},{24,8},{1,17},{9,25},{17,1},{25,9},{2,18},{10... | collective-permute-start | bytes 1769480 | tf_op jit(solution)/shard_map/ppermute | solution.py:52
  29.3 13.2 %collective-permute-start.9 = (bf16[2,4,96,384]{3,2,1,0:T(8,128)(2,1)S(1)}, bf16[2,4,96,384]{3,2,1,0:T(8,128)(2,1)S(1)}, u32[]{:S(2)}, u32[]{:S(2)}) collective-permute-start(bf16[2,4,96,384]{3,2,1,0:T(8,128)(2,1)S(1)} %pad_maximum_fusion.2.rest_4_), channel_id=1, source_target_pairs={{0,1},{1,0},{2,3},{3,2},{4,5},{5,4},{6,7},{7,6},{8,9},{9,8},{10,11... | collective-permute-start | bytes 1769480 | tf_op jit(solution)/shard_map/ppermute | solution.py:52
  30.9 11.7 %collective-permute-start.4 = (bf16[2,4,96,384]{3,2,1,0:T(8,128)(2,1)S(1)}, bf16[2,4,96,384]{3,2,1,0:T(8,128)(2,1)S(1)}, u32[]{:S(2)}, u32[]{:S(2)}) collective-permute-start(bf16[2,4,96,384]{3,2,1,0:T(8,128)(2,1)S(1)} %pad_maximum_fusion.1.rest_0_), channel_id=1, source_target_pairs={{0,8},{8,0},{16,24},{24,16},{1,9},{9,1},{17,25},{25,17},{2,10},{10... | collective-permute-start | bytes 1769480 | tf_op jit(solution)/shard_map/ppermute | solution.py:52
  30.9 11.7 %collective-permute-start.8 = (bf16[2,4,96,384]{3,2,1,0:T(8,128)(2,1)S(1)}, bf16[2,4,96,384]{3,2,1,0:T(8,128)(2,1)S(1)}, u32[]{:S(2)}, u32[]{:S(2)}) collective-permute-start(bf16[2,4,96,384]{3,2,1,0:T(8,128)(2,1)S(1)} %pad_maximum_fusion.2.rest_4_), channel_id=1, source_target_pairs={{0,8},{8,0},{16,24},{24,16},{1,9},{9,1},{17,25},{25,17},{2,10},{10... | collective-permute-start | bytes 1769480 | tf_op jit(solution)/shard_map/ppermute | solution.py:52
  41.4 2.0 %collective-permute-start.6 = (bf16[2,4,96,384]{3,2,1,0:T(8,128)(2,1)S(1)}, bf16[2,4,96,384]{3,2,1,0:T(8,128)(2,1)S(1)}, u32[]{:S(2)}, u32[]{:S(2)}) collective-permute-start(bf16[2,4,96,384]{3,2,1,0:T(8,128)(2,1)S(1)} %collective-permute-done.5.rest_2_), channel_id=1, source_target_pairs={{0,8},{8,0},{16,24},{24,16},{1,9},{9,1},{17,25},{25,17},{2,10},{10... | collective-permute-start | bytes 1769480 | tf_op jit(solution)/shard_map/ppermute | solution.py:52
  42.6 2.0 %collective-permute-start.10 = (bf16[2,4,96,384]{3,2,1,0:T(8,128)(2,1)S(1)}, bf16[2,4,96,384]{3,2,1,0:T(8,128)(2,1)S(1)}, u32[]{:S(2)}, u32[]{:S(2)}) collective-permute-start(bf16[2,4,96,384]{3,2,1,0:T(8,128)(2,1)S(1)} %collective-permute-done.9.rest_6_), channel_id=1, source_target_pairs={{0,8},{8,0},{16,24},{24,16},{1,9},{9,1},{17,25},{25,17},{2,10},{10... | collective-permute-start | bytes 1769480 | tf_op jit(solution)/shard_map/ppermute | solution.py:52
  45.4 14.8 %all-to-all-start = ((bf16[8,24,768]{2,1,0:T(8,128)(2,1)}), bf16[8,24,768]{2,1,0:T(8,128)(2,1)}, u32[]{:S(2)}, u32[]{:S(2)}) async-start(bf16[8,24,768]{2,1,0:T(8,128)(2,1)} %get-tuple-element.136), calls=%async_computation | async-start | bytes 589824 | tf_op jit(solution)/shard_map/all_to_all | solution.py:60
  60.1 9.0 %collective-permute-start.12 = (bf16[192,768]{1,0:T(8,128)(2,1)}, bf16[192,768]{1,0:T(8,128)(2,1)S(1)}, u32[]{:S(2)}, u32[]{:S(2)}) collective-permute-start(bf16[192,768]{1,0:T(8,128)(2,1)} %bitcast.6.rest_0_), channel_id=1, source_target_pairs={{0,16},{8,24},{16,0},{24,8},{1,17},{9,25},{17,1},{25,9},{2,18},{10... | collective-permute-start | bytes 884744 | tf_op jit(solution)/shard_map/ppermute | solution.py:52
  61.2 15.2 %all-to-all-start.1 = ((bf16[8,24,768]{2,1,0:T(8,128)(2,1)}), bf16[8,24,768]{2,1,0:T(8,128)(2,1)S(1)}, u32[]{:S(2)}, u32[]{:S(2)}) async-start(bf16[8,24,768]{2,1,0:T(8,128)(2,1)} %get-tuple-element.137), calls=%async_computation.1 | async-start | bytes 589824 | tf_op jit(solution)/shard_map/all_to_all | solution.py:60
  67.2 2.0 %collective-permute-start.11 = (bf16[192,768]{1,0:T(8,128)(2,1)}, bf16[192,768]{1,0:T(8,128)(2,1)S(1)}, u32[]{:S(2)}, u32[]{:S(2)}) collective-permute-start(bf16[192,768]{1,0:T(8,128)(2,1)} %bitcast.6.rest_0_), channel_id=1, source_target_pairs={{0,8},{8,0},{16,24},{24,16},{1,9},{9,1},{17,25},{25,17},{2,10},{10... | collective-permute-start | bytes 884744 | tf_op jit(solution)/shard_map/ppermute | solution.py:52
  69.2 7.2 %collective-permute-start.13 = (bf16[192,768]{1,0:T(8,128)(2,1)S(1)}, bf16[192,768]{1,0:T(8,128)(2,1)S(1)}, u32[]{:S(2)}, u32[]{:S(2)}) collective-permute-start(bf16[192,768]{1,0:T(8,128)(2,1)S(1)} %collective-permute-done.12.rest_2_), channel_id=1, source_target_pairs={{0,8},{8,0},{16,24},{24,16},{1,9},{9,1},{17,25},{25,17},{2,10},{10... | collective-permute-start | bytes 884744 | tf_op jit(solution)/shard_map/ppermute | solution.py:52
  76.4 10.5 %collective-permute-start.14 = (bf16[192,768]{1,0:T(8,128)(2,1)S(1)}, bf16[192,768]{1,0:T(8,128)(2,1)S(1)}, u32[]{:S(2)}, u32[]{:S(2)}) collective-permute-start(bf16[192,768]{1,0:T(8,128)(2,1)S(1)} %bitcast.21), channel_id=1, source_target_pairs={{0,16},{8,24},{16,0},{24,8},{1,17},{9,25},{17,1},{25,9},{2,18},{10... | collective-permute-start | bytes 884744 | tf_op jit(solution)/shard_map/ppermute | solution.py:52
  77.3 8.0 %collective-permute-start.17 = (bf16[128,768]{1,0:T(8,128)(2,1)}, bf16[128,768]{1,0:T(8,128)(2,1)S(1)}, u32[]{:S(2)}, u32[]{:S(2)}) collective-permute-start(bf16[128,768]{1,0:T(8,128)(2,1)} %get-tuple-element.180.normed_ref.rest_0_), channel_id=1, source_target_pairs={{0,3},{1,2},{2,1},{3,0},{4,7},{5,6},{6,5},{7,4},{8,11},{9,10},{10,... | collective-permute-start | bytes 589832 | tf_op jit(solution)/shard_map/ppermute | solution.py:52
  78.1 8.7 %collective-permute-start.16 = (bf16[128,768]{1,0:T(8,128)(2,1)}, bf16[128,768]{1,0:T(8,128)(2,1)S(1)}, u32[]{:S(2)}, u32[]{:S(2)}) collective-permute-start(bf16[128,768]{1,0:T(8,128)(2,1)} %get-tuple-element.180.normed_ref.rest_0_), channel_id=1, source_target_pairs={{0,2},{1,3},{2,0},{3,1},{4,6},{5,7},{6,4},{7,5},{8,10},{9,11},{10,... | collective-permute-start | bytes 589832 | tf_op jit(solution)/shard_map/ppermute | solution.py:52
  80.3 6.5 %collective-permute-start.15 = (bf16[128,768]{1,0:T(8,128)(2,1)}, bf16[128,768]{1,0:T(8,128)(2,1)S(1)}, u32[]{:S(2)}, u32[]{:S(2)}) collective-permute-start(bf16[128,768]{1,0:T(8,128)(2,1)} %get-tuple-element.180.normed_ref.rest_0_), channel_id=1, source_target_pairs={{0,1},{1,0},{2,3},{3,2},{4,5},{5,4},{6,7},{7,6},{8,9},{9,8},{10,11... | collective-permute-start | bytes 589832 | tf_op jit(solution)/shard_map/ppermute | solution.py:52
  85.3 45.1 %copy-start.20 = (bf16[128,768]{1,0:T(8,128)(2,1)}, bf16[128,768]{1,0:T(8,128)(2,1)S(1)}, u32[]{:S(2)}) copy-start(bf16[128,768]{1,0:T(8,128)(2,1)S(1)} %collective-permute-done.17.rest_3_) | copy-start | bytes 589828
  86.8 43.5 %copy-start.21 = (bf16[128,768]{1,0:T(8,128)(2,1)}, bf16[128,768]{1,0:T(8,128)(2,1)S(1)}, u32[]{:S(2)}) copy-start(bf16[128,768]{1,0:T(8,128)(2,1)S(1)} %collective-permute-done.16.rest_2_) | copy-start | bytes 589828
  86.8 43.5 %copy-start.22 = (bf16[128,768]{1,0:T(8,128)(2,1)}, bf16[128,768]{1,0:T(8,128)(2,1)S(1)}, u32[]{:S(2)}) copy-start(bf16[128,768]{1,0:T(8,128)(2,1)S(1)} %collective-permute-done.15.rest_1_) | copy-start | bytes 589828
  86.9 1.6 collective-permute-start.18
  86.9 2.0 collective-permute-start.19
  99.9 1.8 collective-permute-start.20
  100.0 2.7 %collective-permute-start.21 = (bf16[192,768]{1,0:T(8,128)(2,1)}, bf16[192,768]{1,0:T(8,128)(2,1)S(1)}, u32[]{:S(2)}, u32[]{:S(2)}) collective-permute-start(bf16[192,768]{1,0:T(8,128)(2,1)} %get-tuple-element.152), channel_id=1, source_target_pairs={{0,8},{8,0},{16,24},{24,16},{1,9},{9,1},{17,25},{25,17},{2,10},{10... | collective-permute-start | bytes 884744 | tf_op jit(solution)/shard_map/ppermute | solution.py:52
  103.7 13.0 %collective-permute-start.22 = (bf16[192,768]{1,0:T(8,128)(2,1)S(1)}, bf16[192,768]{1,0:T(8,128)(2,1)S(1)}, u32[]{:S(2)}, u32[]{:S(2)}) collective-permute-start(bf16[192,768]{1,0:T(8,128)(2,1)S(1)} %add_convert_fusion.6), channel_id=1, source_target_pairs={{0,16},{8,24},{16,0},{24,8},{1,17},{9,25},{17,1},{25,9},{2,18},{10... | collective-permute-start | bytes 884744 | tf_op jit(solution)/shard_map/ppermute | solution.py:52
  104.9 8.7 %collective-permute-start.25 = (bf16[128,768]{1,0:T(8,128)(2,1)S(1)}, bf16[128,768]{1,0:T(8,128)(2,1)S(1)}, u32[]{:S(2)}, u32[]{:S(2)}) collective-permute-start(bf16[128,768]{1,0:T(8,128)(2,1)S(1)} %copy-done.19), channel_id=1, source_target_pairs={{0,3},{1,2},{2,1},{3,0},{4,7},{5,6},{6,5},{7,4},{8,11},{9,10},{10,... | collective-permute-start | bytes 589832 | tf_op jit(solution)/shard_map/ppermute | solution.py:52
  106.3 10.4 %collective-permute-start.24 = (bf16[128,768]{1,0:T(8,128)(2,1)S(1)}, bf16[128,768]{1,0:T(8,128)(2,1)S(1)}, u32[]{:S(2)}, u32[]{:S(2)}) collective-permute-start(bf16[128,768]{1,0:T(8,128)(2,1)S(1)} %copy-done.19), channel_id=1, source_target_pairs={{0,2},{1,3},{2,0},{3,1},{4,6},{5,7},{6,4},{7,5},{8,10},{9,11},{10,... | collective-permute-start | bytes 589832 | tf_op jit(solution)/shard_map/ppermute | solution.py:52
  107.8 8.9 %collective-permute-start.23 = (bf16[128,768]{1,0:T(8,128)(2,1)S(1)}, bf16[128,768]{1,0:T(8,128)(2,1)S(1)}, u32[]{:S(2)}, u32[]{:S(2)}) collective-permute-start(bf16[128,768]{1,0:T(8,128)(2,1)S(1)} %copy-done.19), channel_id=1, source_target_pairs={{0,1},{1,0},{2,3},{3,2},{4,5},{5,4},{6,7},{7,6},{8,9},{9,8},{10,11... | collective-permute-start | bytes 589832 | tf_op jit(solution)/shard_map/ppermute | solution.py:52
  113.6 38.2 %copy-start.23 = (bf16[128,768]{1,0:T(8,128)(2,1)}, bf16[128,768]{1,0:T(8,128)(2,1)S(1)}, u32[]{:S(2)}) copy-start(bf16[128,768]{1,0:T(8,128)(2,1)S(1)} %collective-permute-done.25.rest_7_) | copy-start | bytes 589828
  116.7 35.1 %copy-start.25 = (bf16[128,768]{1,0:T(8,128)(2,1)}, bf16[128,768]{1,0:T(8,128)(2,1)S(1)}, u32[]{:S(2)}) copy-start(bf16[128,768]{1,0:T(8,128)(2,1)S(1)} %collective-permute-done.23.rest_5_) | copy-start | bytes 589828
  117.6 1.8 collective-permute-start.27
  117.6 9.0 %collective-permute-start.26 = (bf16[192,768]{1,0:T(8,128)(2,1)}, bf16[192,768]{1,0:T(8,128)(2,1)S(1)}, u32[]{:S(2)}, u32[]{:S(2)}) collective-permute-start(bf16[192,768]{1,0:T(8,128)(2,1)} %get-tuple-element.170), channel_id=1, source_target_pairs={{0,8},{8,0},{16,24},{24,16},{1,9},{9,1},{17,25},{25,17},{2,10},{10... | collective-permute-start | bytes 884744 | tf_op jit(solution)/shard_map/ppermute | solution.py:52
  120.4 9.1 %collective-permute-start.28 = (bf16[192,768]{1,0:T(8,128)(2,1)S(1)}, bf16[192,768]{1,0:T(8,128)(2,1)S(1)}, u32[]{:S(2)}, u32[]{:S(2)}) collective-permute-start(bf16[192,768]{1,0:T(8,128)(2,1)S(1)} %add_convert_fusion.3), channel_id=1, source_target_pairs={{0,16},{8,24},{16,0},{24,8},{1,17},{9,25},{17,1},{25,9},{2,18},{10... | collective-permute-start | bytes 884744 | tf_op jit(solution)/shard_map/ppermute | solution.py:52
  121.4 14.8 %all-to-all-start.2 = ((bf16[8,24,768]{2,1,0:T(8,128)(2,1)}), bf16[8,24,768]{2,1,0:T(8,128)(2,1)S(1)}, u32[]{:S(2)}, u32[]{:S(2)}) async-start(bf16[8,24,768]{2,1,0:T(8,128)(2,1)} %bitcast.8), calls=%async_computation.2 | async-start | bytes 589824 | tf_op jit(solution)/shard_map/all_to_all | solution.py:60
  136.2 15.7 %all-to-all-start.3 = ((bf16[8,24,768]{2,1,0:T(8,128)(2,1)}), bf16[8,24,768]{2,1,0:T(8,128)(2,1)S(1)}, u32[]{:S(2)}, u32[]{:S(2)}) async-start(bf16[8,24,768]{2,1,0:T(8,128)(2,1)} %bitcast.9), calls=%async_computation.3 | async-start | bytes 589824 | tf_op jit(solution)/shard_map/all_to_all | solution.py:60
  151.9 15.7 %all-to-all-start.4 = ((bf16[4,2,384,128]{3,2,1,0:T(8,128)(2,1)}), bf16[4,2,384,128]{3,2,1,0:T(8,128)(2,1)S(1)}, u32[]{:S(2)}, u32[]{:S(2)}) async-start(bf16[4,2,384,128]{3,2,1,0:T(8,128)(2,1)} %get-tuple-element.177), calls=%async_computation.4 | async-start | bytes 1572864 | tf_op jit(solution)/shard_map/all_to_all | solution.py:756
  156.1 1.5 collective-permute-start.29
  158.4 4.4 %collective-permute-start.30 = (f32[24,768]{1,0:T(8,128)S(1)}, f32[24,768]{1,0:T(8,128)S(1)}, u32[]{:S(2)}, u32[]{:S(2)}) collective-permute-start(f32[24,768]{1,0:T(8,128)S(1)} %add.58), channel_id=1, source_target_pairs={{0,16},{8,24},{16,0},{24,8},{1,17},{9,25},{17,1},{25,9},{2,18},{10... | collective-permute-start | bytes 221192 | tf_op jit(solution)/shard_map/ppermute | solution.py:52
  162.9 4.7 %collective-permute-start.31 = (f32[24,768]{1,0:T(8,128)S(1)}, f32[24,768]{1,0:T(8,128)S(1)}, u32[]{:S(2)}, u32[]{:S(2)}) collective-permute-start(f32[24,768]{1,0:T(8,128)S(1)} %add.59), channel_id=1, source_target_pairs={{0,1},{1,0},{2,3},{3,2},{4,5},{5,4},{6,7},{7,6},{8,9},{9,8},{10,11... | collective-permute-start | bytes 221192 | tf_op jit(solution)/shard_map/ppermute | solution.py:52
  172.8 4.7 %collective-permute-start.32 = (bf16[2,192,384]{2,1,0:T(8,128)(2,1)}, bf16[2,192,384]{2,1,0:T(8,128)(2,1)S(1)}, u32[]{:S(2)}, u32[]{:S(2)}) collective-permute-start(bf16[2,192,384]{2,1,0:T(8,128)(2,1)} %get-tuple-element.189), channel_id=1, source_target_pairs={{0,8},{8,0},{16,24},{24,16},{1,9},{9,1},{17,25},{25,17},{2,10},{10... | collective-permute-start | bytes 884744 | tf_op jit(solution)/shard_map/ppermute | solution.py:52
  172.8 4.7 %collective-permute-start.34 = (f32[24,768]{1,0:T(8,128)S(1)}, f32[24,768]{1,0:T(8,128)S(1)}, u32[]{:S(2)}, u32[]{:S(2)}) collective-permute-start(f32[24,768]{1,0:T(8,128)S(1)} %add.60), channel_id=1, source_target_pairs={{0,2},{1,3},{2,0},{3,1},{4,6},{5,7},{6,4},{7,5},{8,10},{9,11},{10,... | collective-permute-start | bytes 221192 | tf_op jit(solution)/shard_map/ppermute | solution.py:52
  174.6 4.0 %collective-permute-start.33 = (bf16[2,192,384]{2,1,0:T(8,128)(2,1)}, bf16[2,192,384]{2,1,0:T(8,128)(2,1)S(1)}, u32[]{:S(2)}, u32[]{:S(2)}) collective-permute-start(bf16[2,192,384]{2,1,0:T(8,128)(2,1)} %get-tuple-element.191), channel_id=1, source_target_pairs={{0,8},{8,0},{16,24},{24,16},{1,9},{9,1},{17,25},{25,17},{2,10},{10... | collective-permute-start | bytes 884744 | tf_op jit(solution)/shard_map/ppermute | solution.py:52
  179.6 6.8 %collective-permute-start.36 = (f32[24,768]{1,0:T(8,128)S(1)}, f32[24,768]{1,0:T(8,128)S(1)}, u32[]{:S(2)}, u32[]{:S(2)}) collective-permute-start(f32[24,768]{1,0:T(8,128)S(1)} %add.63), channel_id=1, source_target_pairs={{0,4},{1,5},{2,6},{3,7},{4,0},{5,1},{6,2},{7,3},{8,12},{9,13},{10,... | collective-permute-start | bytes 221192 | tf_op jit(solution)/shard_map/ppermute | solution.py:52
  182.1 8.4 %collective-permute-start.35 = (bf16[2,192,384]{2,1,0:T(8,128)(2,1)S(1)}, bf16[2,192,384]{2,1,0:T(8,128)(2,1)S(1)}, u32[]{:S(2)}, u32[]{:S(2)}) collective-permute-start(bf16[2,192,384]{2,1,0:T(8,128)(2,1)S(1)} %add_convert_fusion), channel_id=1, source_target_pairs={{0,16},{8,24},{16,0},{24,8},{1,17},{9,25},{17,1},{25,9},{2,18},{10... | collective-permute-start | bytes 884744 | tf_op jit(solution)/shard_map/ppermute | solution.py:52
  190.5 8.4 %collective-permute-start.37 = (bf16[192,384]{1,0:T(8,128)(2,1)S(1)}, bf16[192,384]{1,0:T(8,128)(2,1)S(1)}, u32[]{:S(2)}, u32[]{:S(2)}) collective-permute-start(bf16[192,384]{1,0:T(8,128)(2,1)S(1)} %fusion), channel_id=1, source_target_pairs={{0,4},{1,5},{2,6},{3,7},{4,0},{5,1},{6,2},{7,3},{8,12},{9,13},{10,... | collective-permute-start | bytes 442376 | tf_op jit(solution)/shard_map/ppermute | solution.py:52
  (21 other events, 218.7 us)

commit v14 on v13

--- a/solution.py
+++ b/solution.py
@@ -665,18 +665,17 @@
     slabs, up_arrived = together(slabs, up_arrived)
     arrived = exchange(slabs).reshape(ranks * slab, model_width)
     up_pieces = gather_near(gather_far(up_arrived))
-    arrived, up_pieces, normed_own = together(arrived, up_pieces, normed_low)
-    row_far = gather_far(arrived)
-    near_normed = half_ranks(normed_own)
     by_expert = (local_experts, packed_rows)
     up_rows, up_act = call(
         upstream_kernel,
         "upstream_rows",
-        5,
+        1,
         [shaped(LOW, *by_expert, model_width), shaped(FULL, *by_expert, hidden_here)],
         [pack, w_out, *up_pieces],
     )
-    row_far, up_act, near_normed = together(row_far, up_act, near_normed)
+    arrived, up_act, attended_own = together(arrived, up_act, attended)
+    row_far = gather_far(arrived)
+    row_far, near_attended = together(row_far, half_ranks(attended_own))
     row_pieces = gather_near(row_far)
 
     *back, slot_rows, activated, pre_grad, gates = call(
@@ -697,10 +696,8 @@
             pltpu.VMEM((*by_expert, 128), LOW),
         ],
     )
-    near, attended_own = together(scatter_near(back), attended)
+    near, late_activated = together(scatter_near(back), activated)
     kept, got = scatter_far(near)
-    near_attended = half_ranks(attended_own)
-    near, late_activated = together(near, activated)
     returned = call(
         expert_out_kernel,
         "expert_outputs",
@@ -709,13 +706,14 @@
         [pack_t, w_out, late_activated],
         scratch=[pltpu.VMEM((*by_expert, model_width), LOW)],
     )
-    got, returned, near_attended = together(got, returned, near_attended)
+    got, returned = together(got, returned)
     back = add(kept, got).reshape(ranks, slab, model_width)
     back, returned = together(back, returned)
     back = exchange(back)
     returned = add(*scatter_terms(returned)).reshape(ranks, slab, model_width)
-    back, returned = together(back, returned)
+    back, returned, normed_own = together(back, returned, normed_low)
     returned = exchange(returned)
+    near_normed = half_ranks(normed_own)
 
     bias_rows = -(-head_count // 6)
     small_rows = -(-(experts_total + 2 + bias_rows) // 8) * 8
@@ -752,7 +750,7 @@
         [back],
     )
 
-    factors, small, returned = together(factors, small, returned)
+    factors, small, returned, near_normed = together(factors, small, returned, near_normed)
     factors = lax.all_to_all(
         factors, "expert", split_axis=0, concat_axis=0, tiled=True, axis_index_groups=halves()
     )

time: 201 us -> 203 us (level)
    ppermute x38, waiting for transfers between devices: 54.1 us -> 62.4 us  [swap(): return lax.ppermute(value, axis, [(i, i ^ mask) for i in range(count)])]
    all_to_all x4, waiting for transfers between devices: 13 us -> 6.47 us  [exchange(): lax.all_to_all(value, 'expert', split_axis=0, concat_axis=0, tiled=True)]
  transfers between devices with their start and end apart: 43 -> 43, of which waited for: 24 -> 25; matrix products, arithmetic and copies ran while one was open for 4% -> 4% of each run, Pallas kernels for 21% -> 21%
where the time goes in v14:
time: 203 us; the launch traced here: 202 us
  waiting for transfers between devices  68.9 us (34%)
  starting transfers between devices  58.3 us (29%)
  Pallas kernels  56.7 us (28%)
  other arithmetic  9.64 us (5%)
  local copies, waits for them, and re-layouts  7.6 us (4%)
    ppermute x38, waiting for transfers between devices, swap(): return lax.ppermute(value, axis, [(i, i ^ mask) for i in range(count)])  62.4 us
    pallas_call x8, Pallas kernels, call(): pl.pallas_call(kernel, out_shape=tuple(out_shape), in_specs=[VMEM] * len(...  50.5 us
    ppermute x38, starting transfers between devices, swap(): return lax.ppermute(value, axis, [(i, i ^ mask) for i in range(count)])  34.9 us
    all_to_all x4, starting transfers between devices, exchange(): lax.all_to_all(value, 'expert', split_axis=0, concat_axis=0, tiled=True)  19.3 us
    convert_element_type x8, other arithmetic, add(): return (left.astype(FULL) + right.astype(FULL)).astype(dtype)  6.81 us
    all_to_all x4, waiting for transfers between devices, exchange(): lax.all_to_all(value, 'expert', split_axis=0, concat_axis=0, tiled=True)  6.47 us
    pallas_call x1, Pallas kernels, expert_gradients(): pl.pallas_call(expert_grad_kernel, grid=(shapes[0].shape[0],), out_shape=...  6.25 us
    all_to_all x1, starting transfers between devices, per_device(): lax.all_to_all(factors, 'expert', split_axis=0, concat_axis=0, tiled=True...  4.14 us
  transfers between devices with their start and end apart: 43, of which 25 were waited for; matrix products, arithmetic and copies ran while one was open for 4% of the time, Pallas kernels for 21%

profile of v14, /device:TPU:0, one launch (start us, length us, event | category | flops | bytes accessed | tf_op | source)
XLA Modules:
  0.0 202.2 jit_solution(15753740786228928902)
XLA Ops:
  1.7 5.1 %collective-permute-start.2 = (bf16[1,192,384]{2,1,0:T(8,128)(2,1)S(1)}, bf16[1,192,384]{2,1,0:T(8,128)(2,1)S(1)}, u32[]{:S(2)}, u32[]{:S(2)}) collective-permute-start(bf16[1,192,384]{2,1,0:T(8,128)(2,1)S(1)} %maximum_bitcast_fusion), channel_id=1, source_target_pairs={{0,6},{1,7},{2,4},{3,5},{4,2},{5,3},{6,0},{7,1},{8,14},{9,15},{10,... | collective-permute-start | bytes 442376 | tf_op jit(solution)/shard_map/ppermute | solution.py:52
  9.4 3.3 %early.1 = (bf16[128,768]{1,0:T(8,128)(2,1)}, f32[128,16]{1,0:T(8,128)}, bf16[128,192]{1,0:T(8,128)(2,1)}, bf16[192,128]{1,0:T(8,128)(2,1)}, f32[12,128,128]{2,1,0:T(8,128)}, /*index=5*/bf16[8,24,768]{2,1,0:T(8,128)(2,1)}) custom-call(bf16[128,768]{1,0:T(8,128)(2,1)} %tokens_ref.5, s32[1,128]{1,0:T(1,128)} %bitcast.27, ...), custom_call_target="tpu_custom_call" | custom-call | bytes 10800000 | tf_op jit(solution)/shard_map/early/pallas_call | solution.py:566
  12.7 6.5 %collective-permute-done.1 = bf16[1,192,384]{2,1,0:T(8,128)(2,1)S(1)} collective-permute-done((bf16[1,192,384]{2,1,0:T(8,128)(2,1)S(1)}, bf16[1,192,384]{2,1,0:T(8,128)(2,1)S(1)}, u32[]{:S(2)}, u32[]{:S(2)}) %collective-permute-start.1) | collective-permute-done | bytes 147488 | tf_op jit(solution)/shard_map/ppermute | solution.py:52
  19.4 1.6 collective-permute-start.3
  21.0 1.5 collective-permute-start.7
  22.5 5.1 %collective-permute-done.3 = bf16[1,4,96,384]{3,2,1,0:T(8,128)(2,1)S(1)} collective-permute-done((bf16[1,4,96,384]{3,2,1,0:T(8,128)(2,1)S(1)}, bf16[1,4,96,384]{3,2,1,0:T(8,128)(2,1)S(1)}, u32[]{:S(2)}, u32[]{:S(2)}) %collective-permute-start.3) | collective-permute-done | bytes 294944 | tf_op jit(solution)/shard_map/ppermute | solution.py:52
  27.6 1.6 collective-permute-start.5
  29.3 1.6 collective-permute-start.9
  31.4 10.0 %collective-permute-done.5.rest_2_ = bf16[2,4,96,384]{3,2,1,0:T(8,128)(2,1)S(1)} collective-permute-done((bf16[2,4,96,384]{3,2,1,0:T(8,128)(2,1)S(1)}, bf16[2,4,96,384]{3,2,1,0:T(8,128)(2,1)S(1)}, u32[]{:S(2)}, u32[]{:S(2)}) %collective-permute-start.5) | collective-permute-done | bytes 589856 | tf_op jit(solution)/shard_map/ppermute | solution.py:52
  41.4 1.1 collective-permute-done.9.rest_6_
  43.4 1.1 collective-permute-done.10.rest_7_
  45.4 4.3 %all-to-all-start = ((bf16[8,24,768]{2,1,0:T(8,128)(2,1)}), bf16[8,24,768]{2,1,0:T(8,128)(2,1)}, u32[]{:S(2)}, u32[]{:S(2)}) async-start(bf16[8,24,768]{2,1,0:T(8,128)(2,1)} %get-tuple-element.132), calls=%async_computation | async-start | bytes 589824 | tf_op jit(solution)/shard_map/all_to_all | solution.py:60
  49.8 10.3 %attention_forward.1 = (bf16[3,768,128]{2,1,0:T(8,128)(2,1)}, f32[12,128,128]{2,1,0:T(8,128)}, bf16[128,768]{1,0:T(8,128)(2,1)}, f32[128,768]{1,0:T(8,128)}, f32...) custom-call(bf16[128,768]{1,0:T(8,128)(2,1)} %tokens_ref.5, bf16[128,768]{1,0:T(8,128)(2,1)} %get-tuple-element.172.normed_ref.rest_0_, ...), custom_call_target="tpu_custom_call" | custom-call | bytes 36000000 | tf_op jit(solution)/shard_map/attention_forward/pallas_call | solution.py:566
  61.2 6.0 %all-to-all-start.1 = ((bf16[8,24,768]{2,1,0:T(8,128)(2,1)}), bf16[8,24,768]{2,1,0:T(8,128)(2,1)S(1)}, u32[]{:S(2)}, u32[]{:S(2)}) async-start(bf16[8,24,768]{2,1,0:T(8,128)(2,1)} %get-tuple-element.133), calls=%async_computation.1 | async-start | bytes 589824 | tf_op jit(solution)/shard_map/all_to_all | solution.py:60
  67.2 2.0 collective-permute-done.12.rest_2_
  69.2 1.6 collective-permute-done.13.rest_3_
  71.5 4.5 %upstream_rows.1 = (bf16[2,320,768]{2,1,0:T(8,128)(2,1)}, f32[2,320,768]{2,1,0:T(8,128)}) custom-call(bf16[160,192]{1,0:T(8,128)(2,1)} %constant.8.clone.pack_ref, bf16[2,768,768]{2,1,0:T(8,128)(2,1)} %w_out_ref.3, bf16[192,768]{1,0:T(8,128)(2,1)} %bitcast.6.rest_0_, bf16[192,768]{1,0:T(8,128)(2,1)} %copy-done.17, bf16[192,768]{1,0:T(8,128)(2,1)} %copy-done.14, ...), custom_call_target="tpu_custom_call" | custom-call | bytes 3600000 | tf_op jit(solution)/shard_map/upstream_rows/pallas_call | solution.py:566
  77.3 2.5 %collective-permute-start.17 = (bf16[128,768]{1,0:T(8,128)(2,1)S(1)}, bf16[128,768]{1,0:T(8,128)(2,1)S(1)}, u32[]{:S(2)}, u32[]{:S(2)}) collective-permute-start(bf16[128,768]{1,0:T(8,128)(2,1)S(1)} %copy-done.20), channel_id=1, source_target_pairs={{0,3},{1,2},{2,1},{3,0},{4,7},{5,6},{6,5},{7,4},{8,11},{9,10},{10,... | collective-permute-start | bytes 589832 | tf_op jit(solution)/shard_map/ppermute | solution.py:52
  80.8 5.2 %collective-permute-done.17.rest_7_ = bf16[128,768]{1,0:T(8,128)(2,1)S(1)} collective-permute-done((bf16[128,768]{1,0:T(8,128)(2,1)S(1)}, bf16[128,768]{1,0:T(8,128)(2,1)S(1)}, u32[]{:S(2)}, u32[]{:S(2)}) %collective-permute-start.17) | collective-permute-done | bytes 196640 | tf_op jit(solution)/shard_map/ppermute | solution.py:52
  86.0 3.2 %collective-permute-done.16.rest_6_ = bf16[128,768]{1,0:T(8,128)(2,1)S(1)} collective-permute-done((bf16[128,768]{1,0:T(8,128)(2,1)S(1)}, bf16[128,768]{1,0:T(8,128)(2,1)S(1)}, u32[]{:S(2)}, u32[]{:S(2)}) %collective-permute-start.16) | collective-permute-done | bytes 196640 | tf_op jit(solution)/shard_map/ppermute | solution.py:52
  89.8 1.1 collective-permute-done.18.rest_1_
  92.3 9.9 %experts.1 = (bf16[192,768]{1,0:T(8,128)(2,1)}, bf16[192,768]{1,0:T(8,128)(2,1)}, bf16[192,768]{1,0:T(8,128)(2,1)}, bf16[192,768]{1,0:T(8,128)(2,1)}, bf16[2,320...) custom-call(bf16[160,192]{1,0:T(8,128)(2,1)} %constant.8.clone.pack_re, ...), custom_call_target="tpu_custom_call" | custom-call | bytes 36000000 | tf_op jit(solution)/shard_map/experts/pallas_call | solution.py:566
  102.7 1.3 collective-permute-done.20
  107.1 4.0 %expert_outputs.1 = (bf16[192,768]{1,0:T(8,128)(2,1)}, bf16[192,768]{1,0:T(8,128)(2,1)}, bf16[192,768]{1,0:T(8,128)(2,1)}, bf16[192,768]{1,0:T(8,128)(2,1)}) custom-call(bf16[192,160]{1,0:T(8,128)(2,1)} %constant.9.clone.pack_t_ref, bf16[2,768,768]{2,1,0:T(8,128)(2,1)} %w_out_ref.3, bf16[2,320,768]{2,1,0:T(8,128)(2,1)} %get-tuple-element.194.act_ref), custom_call_target="tpu_custom_call" | custom-call | bytes 10800000 | tf_op jit(solution)/shard_map/expert_outputs/pallas_call | solution.py:566
  111.1 4.1 %collective-permute-done.22 = bf16[192,768]{1,0:T(8,128)(2,1)S(1)} collective-permute-done((bf16[192,768]{1,0:T(8,128)(2,1)S(1)}, bf16[192,768]{1,0:T(8,128)(2,1)S(1)}, u32[]{:S(2)}, u32[]{:S(2)}) %collective-permute-start.22) | collective-permute-done | bytes 294944 | tf_op jit(solution)/shard_map/ppermute | solution.py:52
  116.5 1.3 collective-permute-done.24
  119.8 5.4 %all-to-all-start.2 = ((bf16[8,24,768]{2,1,0:T(8,128)(2,1)}), bf16[8,24,768]{2,1,0:T(8,128)(2,1)S(1)}, u32[]{:S(2)}, u32[]{:S(2)}) async-start(bf16[8,24,768]{2,1,0:T(8,128)(2,1)} %bitcast.8), calls=%async_computation.2 | async-start | bytes 589824 | tf_op jit(solution)/shard_map/all_to_all | solution.py:60
  125.2 2.7 %collective-permute-done.25 = bf16[192,768]{1,0:T(8,128)(2,1)S(1)} collective-permute-done((bf16[192,768]{1,0:T(8,128)(2,1)S(1)}, bf16[192,768]{1,0:T(8,128)(2,1)S(1)}, u32[]{:S(2)}, u32[]{:S(2)}) %collective-permute-start.25) | collective-permute-done | bytes 294944 | tf_op jit(solution)/shard_map/ppermute | solution.py:52
  128.8 6.1 %all-to-all-done.2.rest_8_ = bf16[8,24,768]{2,1,0:T(8,128)(2,1)S(1)} async-done(((bf16[8,24,768]{2,1,0:T(8,128)(2,1)}), bf16[8,24,768]{2,1,0:T(8,128)(2,1)S(1)}, u32[]{:S(2)}, u32[]{:S(2)}) %all-to-all-start.2) | async-done | bytes 294944 | tf_op jit(solution)/shard_map/all_to_all | solution.py:60
  134.9 3.6 %all-to-all-start.3 = ((bf16[8,24,768]{2,1,0:T(8,128)(2,1)}), bf16[8,24,768]{2,1,0:T(8,128)(2,1)S(1)}, u32[]{:S(2)}, u32[]{:S(2)}) async-start(bf16[8,24,768]{2,1,0:T(8,128)(2,1)} %bitcast.9), calls=%async_computation.3 | async-start | bytes 589824 | tf_op jit(solution)/shard_map/all_to_all | solution.py:60
  138.4 2.9 %collective-permute-start.28 = (bf16[128,768]{1,0:T(8,128)(2,1)S(1)}, bf16[128,768]{1,0:T(8,128)(2,1)S(1)}, u32[]{:S(2)}, u32[]{:S(2)}) collective-permute-start(bf16[128,768]{1,0:T(8,128)(2,1)S(1)} %copy-done.12), channel_id=1, source_target_pairs={{0,3},{1,2},{2,1},{3,0},{4,7},{5,6},{6,5},{7,4},{8,11},{9,10},{10,... | collective-permute-start | bytes 589832 | tf_op jit(solution)/shard_map/ppermute | solution.py:52
  142.0 12.0 %attention_backward.1 = (f32[128,768]{1,0:T(8,128)}, f32[24,768]{1,0:T(8,128)}, bf16[4,2,384,128]{3,2,1,0:T(8,128)(2,1)}) custom-call(bf16[128,768]{1,0:T(8,128)(2,1)} %tokens_ref.5, f32[2,768]{1,0:T(2,128)} %maximum_convert_fusion.gain_ref, bf16[16,768]{1,0:T(8,128)(2,1)} %bitcast.25, f32[128,16]{1,0:T(8,128)} %get-tuple-element.112.hits_ref, ...), custom_call_target="tpu_custom_call" | custom-call | bytes 43200000 | tf_op jit(solution)/shard_map/attention_backward/pallas_call | solution.py:566
  154.1 4.1 %all-to-all-start.4 = ((bf16[4,2,384,128]{3,2,1,0:T(8,128)(2,1)}), bf16[4,2,384,128]{3,2,1,0:T(8,128)(2,1)S(1)}, u32[]{:S(2)}, u32[]{:S(2)}) async-start(bf16[4,2,384,128]{3,2,1,0:T(8,128)(2,1)} %get-tuple-element.169), calls=%async_computation.4 | async-start | bytes 1572864 | tf_op jit(solution)/shard_map/all_to_all | solution.py:754
  158.2 1.5 collective-permute-done.29
  160.6 1.2 collective-permute-start.30
  161.8 3.2 %collective-permute-done.30 = f32[24,768]{1,0:T(8,128)S(1)} collective-permute-done((f32[24,768]{1,0:T(8,128)S(1)}, f32[24,768]{1,0:T(8,128)S(1)}, u32[]{:S(2)}, u32[]{:S(2)}) %collective-permute-start.30) | collective-permute-done | bytes 73760 | tf_op jit(solution)/shard_map/ppermute | solution.py:52
  165.0 2.1 %collective-permute-start.31 = (f32[24,768]{1,0:T(8,128)S(1)}, f32[24,768]{1,0:T(8,128)S(1)}, u32[]{:S(2)}, u32[]{:S(2)}) collective-permute-start(f32[24,768]{1,0:T(8,128)S(1)} %add.59), channel_id=1, source_target_pairs={{0,1},{1,0},{2,3},{3,2},{4,5},{5,4},{6,7},{7,6},{8,9},{9,8},{10,11... | collective-permute-start | bytes 221192 | tf_op jit(solution)/shard_map/ppermute | solution.py:52
  167.1 2.3 %collective-permute-done.31 = f32[24,768]{1,0:T(8,128)S(1)} collective-permute-done((f32[24,768]{1,0:T(8,128)S(1)}, f32[24,768]{1,0:T(8,128)S(1)}, u32[]{:S(2)}, u32[]{:S(2)}) %collective-permute-start.31) | collective-permute-done | bytes 73760 | tf_op jit(solution)/shard_map/ppermute | solution.py:52
  170.4 4.3 %weight_gradients.1 = (bf16[2,192,384]{2,1,0:T(8,128)(2,1)}, bf16[2,192,384]{2,1,0:T(8,128)(2,1)}, bf16[2,192,384]{2,1,0:T(8,128)(2,1)}, bf16[2,192,384]{2,1,0:T(8,128)(2,1)}) custom-call(bf16[4,2,384,128]{3,2,1,0:T(8,128)(2,1)} %copy-done.2, bf16[128,768]{1,0:T(8,128)(2,1)} %get-tuple-element.172.normed_ref.rest_0_, bf16[128,768]{1,0:T(8,128)(2,1)} %copy-done.26, ...), custom_call_target="tpu_custom_call" | custom-call | bytes 18000000 | tf_op jit(solution)/shard_map/weight_gradients/pallas_call | solution.py:566
  174.7 2.0 %collective-permute-start.34 = (f32[24,768]{1,0:T(8,128)S(1)}, f32[24,768]{1,0:T(8,128)S(1)}, u32[]{:S(2)}, u32[]{:S(2)}) collective-permute-start(f32[24,768]{1,0:T(8,128)S(1)} %add.60), channel_id=1, source_target_pairs={{0,2},{1,3},{2,0},{3,1},{4,6},{5,7},{6,4},{7,5},{8,10},{9,11},{10,... | collective-permute-start | bytes 221192 | tf_op jit(solution)/shard_map/ppermute | solution.py:52
  177.0 2.7 %collective-permute-done.34 = f32[24,768]{1,0:T(8,128)S(1)} collective-permute-done((f32[24,768]{1,0:T(8,128)S(1)}, f32[24,768]{1,0:T(8,128)S(1)}, u32[]{:S(2)}, u32[]{:S(2)}) %collective-permute-start.34) | collective-permute-done | bytes 73760 | tf_op jit(solution)/shard_map/ppermute | solution.py:52
  179.7 1.0 add_convert_fusion.1
  181.8 2.4 %collective-permute-start.36 = (f32[24,768]{1,0:T(8,128)S(1)}, f32[24,768]{1,0:T(8,128)S(1)}, u32[]{:S(2)}, u32[]{:S(2)}) collective-permute-start(f32[24,768]{1,0:T(8,128)S(1)} %add.63), channel_id=1, source_target_pairs={{0,4},{1,5},{2,6},{3,7},{4,0},{5,1},{6,2},{7,3},{8,12},{9,13},{10,... | collective-permute-start | bytes 221192 | tf_op jit(solution)/shard_map/ppermute | solution.py:52
  184.3 1.1 collective-permute-start.35
  185.4 2.1 %output_rows.1 = bf16[128,768]{1,0:T(8,128)(2,1)} custom-call(f32[128,768]{1,0:T(8,128)} %get-tuple-element.127.hidden_ref, f32[128,16]{1,0:T(8,128)} %get-tuple-element.128.chance_ref, f32[128,16]{1,0:T(8,128)} %get-tuple-element.112.hits_ref, bf16[128,192]{1,0:T(8,128)(2,1)} %get-tuple-element.113.mask_ref, bf16[8,24,768]{2,1,0:T(8,128)(2,1)} %copy-done.11), custom_call_target="tpu_custom_call" | custom-call | bytes 7200000 | tf_op jit(solution)/shard_map/output_rows/pallas_call | solution.py:566
  187.5 1.2 collective-permute-done.36
  189.3 3.4 %collective-permute-done.35 = bf16[2,192,384]{2,1,0:T(8,128)(2,1)S(1)} collective-permute-done((bf16[2,192,384]{2,1,0:T(8,128)(2,1)S(1)}, bf16[2,192,384]{2,1,0:T(8,128)(2,1)S(1)}, u32[]{:S(2)}, u32[]{:S(2)}) %collective-permute-start.35) | collective-permute-done | bytes 294944 | tf_op jit(solution)/shard_map/ppermute | solution.py:52
  194.7 6.2 %expert_gradients.1 = (f32[2,768,768]{2,1,0:T(8,128)}, f32[2,768,768]{2,1,0:T(8,128)}) custom-call(bf16[2,320,768]{2,1,0:T(8,128)(2,1)} %get-tuple-element.193.rows_ref, bf16[2,320,768]{2,1,0:T(8,128)(2,1)} %get-tuple-element.194.act_ref, bf16[2,320,768]{2,1,0:T(8,128)(2,1)} %get-tuple-element.195.pre_grad_ref, f32[2,320,128]{2,1,0:T(8,128)} %get-tuple-element.196.gates_ref, ...), custom_call_target="tpu_custom_call" | custom-call | bytes 28800000 | tf_op jit(solution)/shard_map/expert_gradients/pallas_call | solution.py:426
  (129 shorter events, 27.5 us)
Async XLA Ops:
  1.7 11.1 %collective-permute-start.2 = (bf16[1,192,384]{2,1,0:T(8,128)(2,1)S(1)}, bf16[1,192,384]{2,1,0:T(8,128)(2,1)S(1)}, u32[]{:S(2)}, u32[]{:S(2)}) collective-permute-start(bf16[1,192,384]{2,1,0:T(8,128)(2,1)S(1)} %maximum_bitcast_fusion), channel_id=1, source_target_pairs={{0,6},{1,7},{2,4},{3,5},{4,2},{5,3},{6,0},{7,1},{8,14},{9,15},{10,... | collective-permute-start | bytes 442376 | tf_op jit(solution)/shard_map/ppermute | solution.py:52
  6.8 12.5 %collective-permute-start.1 = (bf16[1,192,384]{2,1,0:T(8,128)(2,1)S(1)}, bf16[1,192,384]{2,1,0:T(8,128)(2,1)S(1)}, u32[]{:S(2)}, u32[]{:S(2)}) collective-permute-start(bf16[1,192,384]{2,1,0:T(8,128)(2,1)S(1)} %maximum_bitcast_fusion), channel_id=1, source_target_pairs={{0,4},{1,5},{2,6},{3,7},{4,0},{5,1},{6,2},{7,3},{8,12},{9,13},{10,... | collective-permute-start | bytes 442376 | tf_op jit(solution)/shard_map/ppermute | solution.py:52
  6.8 12.5 %collective-permute-start = (bf16[1,192,384]{2,1,0:T(8,128)(2,1)S(1)}, bf16[1,192,384]{2,1,0:T(8,128)(2,1)S(1)}, u32[]{:S(2)}, u32[]{:S(2)}) collective-permute-start(bf16[1,192,384]{2,1,0:T(8,128)(2,1)S(1)} %maximum_bitcast_fusion), channel_id=1, source_target_pairs={{0,2},{1,3},{2,0},{3,1},{4,6},{5,7},{6,4},{7,5},{8,10},{9,11},{10,... | collective-permute-start | bytes 442376 | tf_op jit(solution)/shard_map/ppermute | solution.py:52
  19.4 8.1 %collective-permute-start.3 = (bf16[1,4,96,384]{3,2,1,0:T(8,128)(2,1)S(1)}, bf16[1,4,96,384]{3,2,1,0:T(8,128)(2,1)S(1)}, u32[]{:S(2)}, u32[]{:S(2)}) collective-permute-start(bf16[1,4,96,384]{3,2,1,0:T(8,128)(2,1)S(1)} %get-tuple-element.205), channel_id=1, source_target_pairs={{0,1},{1,0},{2,3},{3,2},{4,5},{5,4},{6,7},{7,6},{8,9},{9,8},{10,11... | collective-permute-start | bytes 884744 | tf_op jit(solution)/shard_map/ppermute | solution.py:52
  21.0 8.2 %collective-permute-start.7 = (bf16[1,4,96,384]{3,2,1,0:T(8,128)(2,1)S(1)}, bf16[1,4,96,384]{3,2,1,0:T(8,128)(2,1)S(1)}, u32[]{:S(2)}, u32[]{:S(2)}) collective-permute-start(bf16[1,4,96,384]{3,2,1,0:T(8,128)(2,1)S(1)} %get-tuple-element.204), channel_id=1, source_target_pairs={{0,16},{8,24},{16,0},{24,8},{1,17},{9,25},{17,1},{25,9},{2,18},{10... | collective-permute-start | bytes 884744 | tf_op jit(solution)/shard_map/ppermute | solution.py:52
  27.6 13.8 %collective-permute-start.5 = (bf16[2,4,96,384]{3,2,1,0:T(8,128)(2,1)S(1)}, bf16[2,4,96,384]{3,2,1,0:T(8,128)(2,1)S(1)}, u32[]{:S(2)}, u32[]{:S(2)}) collective-permute-start(bf16[2,4,96,384]{3,2,1,0:T(8,128)(2,1)S(1)} %pad_maximum_fusion.1.rest_0_), channel_id=1, source_target_pairs={{0,16},{8,24},{16,0},{24,8},{1,17},{9,25},{17,1},{25,9},{2,18},{10... | collective-permute-start | bytes 1769480 | tf_op jit(solution)/shard_map/ppermute | solution.py:52
  29.3 13.2 %collective-permute-start.9 = (bf16[2,4,96,384]{3,2,1,0:T(8,128)(2,1)S(1)}, bf16[2,4,96,384]{3,2,1,0:T(8,128)(2,1)S(1)}, u32[]{:S(2)}, u32[]{:S(2)}) collective-permute-start(bf16[2,4,96,384]{3,2,1,0:T(8,128)(2,1)S(1)} %pad_maximum_fusion.2.rest_4_), channel_id=1, source_target_pairs={{0,1},{1,0},{2,3},{3,2},{4,5},{5,4},{6,7},{7,6},{8,9},{9,8},{10,11... | collective-permute-start | bytes 1769480 | tf_op jit(solution)/shard_map/ppermute | solution.py:52
  30.9 11.7 %collective-permute-start.4 = (bf16[2,4,96,384]{3,2,1,0:T(8,128)(2,1)S(1)}, bf16[2,4,96,384]{3,2,1,0:T(8,128)(2,1)S(1)}, u32[]{:S(2)}, u32[]{:S(2)}) collective-permute-start(bf16[2,4,96,384]{3,2,1,0:T(8,128)(2,1)S(1)} %pad_maximum_fusion.1.rest_0_), channel_id=1, source_target_pairs={{0,8},{8,0},{16,24},{24,16},{1,9},{9,1},{17,25},{25,17},{2,10},{10... | collective-permute-start | bytes 1769480 | tf_op jit(solution)/shard_map/ppermute | solution.py:52
  30.9 11.7 %collective-permute-start.8 = (bf16[2,4,96,384]{3,2,1,0:T(8,128)(2,1)S(1)}, bf16[2,4,96,384]{3,2,1,0:T(8,128)(2,1)S(1)}, u32[]{:S(2)}, u32[]{:S(2)}) collective-permute-start(bf16[2,4,96,384]{3,2,1,0:T(8,128)(2,1)S(1)} %pad_maximum_fusion.2.rest_4_), channel_id=1, source_target_pairs={{0,8},{8,0},{16,24},{24,16},{1,9},{9,1},{17,25},{25,17},{2,10},{10... | collective-permute-start | bytes 1769480 | tf_op jit(solution)/shard_map/ppermute | solution.py:52
  41.4 2.0 collective-permute-start.6
  42.6 2.0 collective-permute-start.10
  45.4 14.8 %all-to-all-start = ((bf16[8,24,768]{2,1,0:T(8,128)(2,1)}), bf16[8,24,768]{2,1,0:T(8,128)(2,1)}, u32[]{:S(2)}, u32[]{:S(2)}) async-start(bf16[8,24,768]{2,1,0:T(8,128)(2,1)} %get-tuple-element.132), calls=%async_computation | async-start | bytes 589824 | tf_op jit(solution)/shard_map/all_to_all | solution.py:60
  60.2 9.1 %collective-permute-start.12 = (bf16[192,768]{1,0:T(8,128)(2,1)}, bf16[192,768]{1,0:T(8,128)(2,1)S(1)}, u32[]{:S(2)}, u32[]{:S(2)}) collective-permute-start(bf16[192,768]{1,0:T(8,128)(2,1)} %bitcast.6.rest_0_), channel_id=1, source_target_pairs={{0,16},{8,24},{16,0},{24,8},{1,17},{9,25},{17,1},{25,9},{2,18},{10... | collective-permute-start | bytes 884744 | tf_op jit(solution)/shard_map/ppermute | solution.py:52
  61.2 15.2 %all-to-all-start.1 = ((bf16[8,24,768]{2,1,0:T(8,128)(2,1)}), bf16[8,24,768]{2,1,0:T(8,128)(2,1)S(1)}, u32[]{:S(2)}, u32[]{:S(2)}) async-start(bf16[8,24,768]{2,1,0:T(8,128)(2,1)} %get-tuple-element.133), calls=%async_computation.1 | async-start | bytes 589824 | tf_op jit(solution)/shard_map/all_to_all | solution.py:60
  67.2 2.0 %collective-permute-start.11 = (bf16[192,768]{1,0:T(8,128)(2,1)}, bf16[192,768]{1,0:T(8,128)(2,1)S(1)}, u32[]{:S(2)}, u32[]{:S(2)}) collective-permute-start(bf16[192,768]{1,0:T(8,128)(2,1)} %bitcast.6.rest_0_), channel_id=1, source_target_pairs={{0,8},{8,0},{16,24},{24,16},{1,9},{9,1},{17,25},{25,17},{2,10},{10... | collective-permute-start | bytes 884744 | tf_op jit(solution)/shard_map/ppermute | solution.py:52
  69.2 1.6 collective-permute-start.13
  76.4 12.8 %collective-permute-start.14 = (bf16[192,768]{1,0:T(8,128)(2,1)S(1)}, bf16[192,768]{1,0:T(8,128)(2,1)S(1)}, u32[]{:S(2)}, u32[]{:S(2)}) collective-permute-start(bf16[192,768]{1,0:T(8,128)(2,1)S(1)} %bitcast.21), channel_id=1, source_target_pairs={{0,16},{8,24},{16,0},{24,8},{1,17},{9,25},{17,1},{25,9},{2,18},{10... | collective-permute-start | bytes 884744 | tf_op jit(solution)/shard_map/ppermute | solution.py:52
  77.3 8.7 %collective-permute-start.17 = (bf16[128,768]{1,0:T(8,128)(2,1)S(1)}, bf16[128,768]{1,0:T(8,128)(2,1)S(1)}, u32[]{:S(2)}, u32[]{:S(2)}) collective-permute-start(bf16[128,768]{1,0:T(8,128)(2,1)S(1)} %copy-done.20), channel_id=1, source_target_pairs={{0,3},{1,2},{2,1},{3,0},{4,7},{5,6},{6,5},{7,4},{8,11},{9,10},{10,... | collective-permute-start | bytes 589832 | tf_op jit(solution)/shard_map/ppermute | solution.py:52
  79.8 9.4 %collective-permute-start.16 = (bf16[128,768]{1,0:T(8,128)(2,1)S(1)}, bf16[128,768]{1,0:T(8,128)(2,1)S(1)}, u32[]{:S(2)}, u32[]{:S(2)}) collective-permute-start(bf16[128,768]{1,0:T(8,128)(2,1)S(1)} %copy-done.20), channel_id=1, source_target_pairs={{0,2},{1,3},{2,0},{3,1},{4,6},{5,7},{6,4},{7,5},{8,10},{9,11},{10,... | collective-permute-start | bytes 589832 | tf_op jit(solution)/shard_map/ppermute | solution.py:52
  80.3 8.9 %collective-permute-start.15 = (bf16[128,768]{1,0:T(8,128)(2,1)S(1)}, bf16[128,768]{1,0:T(8,128)(2,1)S(1)}, u32[]{:S(2)}, u32[]{:S(2)}) collective-permute-start(bf16[128,768]{1,0:T(8,128)(2,1)S(1)} %copy-done.20), channel_id=1, source_target_pairs={{0,1},{1,0},{2,3},{3,2},{4,5},{5,4},{6,7},{7,6},{8,9},{9,8},{10,11... | collective-permute-start | bytes 589832 | tf_op jit(solution)/shard_map/ppermute | solution.py:52
  86.0 42.8 %copy-start.21 = (bf16[128,768]{1,0:T(8,128)(2,1)}, bf16[128,768]{1,0:T(8,128)(2,1)S(1)}, u32[]{:S(2)}) copy-start(bf16[128,768]{1,0:T(8,128)(2,1)S(1)} %collective-permute-done.17.rest_7_) | copy-start | bytes 589828
  89.2 39.6 %copy-start.22 = (bf16[128,768]{1,0:T(8,128)(2,1)}, bf16[128,768]{1,0:T(8,128)(2,1)S(1)}, u32[]{:S(2)}) copy-start(bf16[128,768]{1,0:T(8,128)(2,1)S(1)} %collective-permute-done.16.rest_6_) | copy-start | bytes 589828
  89.2 39.6 %copy-start.23 = (bf16[128,768]{1,0:T(8,128)(2,1)}, bf16[128,768]{1,0:T(8,128)(2,1)S(1)}, u32[]{:S(2)}) copy-start(bf16[128,768]{1,0:T(8,128)(2,1)S(1)} %collective-permute-done.15.rest_5_) | copy-start | bytes 589828
  89.2 1.6 collective-permute-start.18
  89.3 2.0 collective-permute-start.19
  102.2 1.8 collective-permute-start.20
  102.4 2.7 %collective-permute-start.21 = (bf16[192,768]{1,0:T(8,128)(2,1)}, bf16[192,768]{1,0:T(8,128)(2,1)S(1)}, u32[]{:S(2)}, u32[]{:S(2)}) collective-permute-start(bf16[192,768]{1,0:T(8,128)(2,1)} %get-tuple-element.145), channel_id=1, source_target_pairs={{0,8},{8,0},{16,24},{24,16},{1,9},{9,1},{17,25},{25,17},{2,10},{10... | collective-permute-start | bytes 884744 | tf_op jit(solution)/shard_map/ppermute | solution.py:52
  106.1 9.1 %collective-permute-start.22 = (bf16[192,768]{1,0:T(8,128)(2,1)S(1)}, bf16[192,768]{1,0:T(8,128)(2,1)S(1)}, u32[]{:S(2)}, u32[]{:S(2)}) collective-permute-start(bf16[192,768]{1,0:T(8,128)(2,1)S(1)} %add_convert_fusion.6), channel_id=1, source_target_pairs={{0,16},{8,24},{16,0},{24,8},{1,17},{9,25},{17,1},{25,9},{2,18},{10... | collective-permute-start | bytes 884744 | tf_op jit(solution)/shard_map/ppermute | solution.py:52
  111.1 27.3 %copy-start.12 = (bf16[128,768]{1,0:T(8,128)(2,1)S(1)}, bf16[128,768]{1,0:T(8,128)(2,1)}, u32[]{:S(2)}) copy-start(bf16[128,768]{1,0:T(8,128)(2,1)} %get-tuple-element.172.normed_ref.rest_0_) | copy-start | bytes 589828
  116.0 1.8 collective-permute-start.24
  116.0 9.2 %collective-permute-start.23 = (bf16[192,768]{1,0:T(8,128)(2,1)}, bf16[192,768]{1,0:T(8,128)(2,1)S(1)}, u32[]{:S(2)}, u32[]{:S(2)}) collective-permute-start(bf16[192,768]{1,0:T(8,128)(2,1)} %get-tuple-element.161), channel_id=1, source_target_pairs={{0,8},{8,0},{16,24},{24,16},{1,9},{9,1},{17,25},{25,17},{2,10},{10... | collective-permute-start | bytes 884744 | tf_op jit(solution)/shard_map/ppermute | solution.py:52
  118.8 9.1 %collective-permute-start.25 = (bf16[192,768]{1,0:T(8,128)(2,1)S(1)}, bf16[192,768]{1,0:T(8,128)(2,1)S(1)}, u32[]{:S(2)}, u32[]{:S(2)}) collective-permute-start(bf16[192,768]{1,0:T(8,128)(2,1)S(1)} %add_convert_fusion.3), channel_id=1, source_target_pairs={{0,16},{8,24},{16,0},{24,8},{1,17},{9,25},{17,1},{25,9},{2,18},{10... | collective-permute-start | bytes 884744 | tf_op jit(solution)/shard_map/ppermute | solution.py:52
  119.8 15.0 %all-to-all-start.2 = ((bf16[8,24,768]{2,1,0:T(8,128)(2,1)}), bf16[8,24,768]{2,1,0:T(8,128)(2,1)S(1)}, u32[]{:S(2)}, u32[]{:S(2)}) async-start(bf16[8,24,768]{2,1,0:T(8,128)(2,1)} %bitcast.8), calls=%async_computation.2 | async-start | bytes 589824 | tf_op jit(solution)/shard_map/all_to_all | solution.py:60
  134.9 19.2 %all-to-all-start.3 = ((bf16[8,24,768]{2,1,0:T(8,128)(2,1)}), bf16[8,24,768]{2,1,0:T(8,128)(2,1)S(1)}, u32[]{:S(2)}, u32[]{:S(2)}) async-start(bf16[8,24,768]{2,1,0:T(8,128)(2,1)} %bitcast.9), calls=%async_computation.3 | async-start | bytes 589824 | tf_op jit(solution)/shard_map/all_to_all | solution.py:60
  138.4 15.6 %collective-permute-start.28 = (bf16[128,768]{1,0:T(8,128)(2,1)S(1)}, bf16[128,768]{1,0:T(8,128)(2,1)S(1)}, u32[]{:S(2)}, u32[]{:S(2)}) collective-permute-start(bf16[128,768]{1,0:T(8,128)(2,1)S(1)} %copy-done.12), channel_id=1, source_target_pairs={{0,3},{1,2},{2,1},{3,0},{4,7},{5,6},{6,5},{7,4},{8,11},{9,10},{10,... | collective-permute-start | bytes 589832 | tf_op jit(solution)/shard_map/ppermute | solution.py:52
  141.4 12.7 %collective-permute-start.27 = (bf16[128,768]{1,0:T(8,128)(2,1)S(1)}, bf16[128,768]{1,0:T(8,128)(2,1)S(1)}, u32[]{:S(2)}, u32[]{:S(2)}) collective-permute-start(bf16[128,768]{1,0:T(8,128)(2,1)S(1)} %copy-done.12), channel_id=1, source_target_pairs={{0,2},{1,3},{2,0},{3,1},{4,6},{5,7},{6,4},{7,5},{8,10},{9,11},{10,... | collective-permute-start | bytes 589832 | tf_op jit(solution)/shard_map/ppermute | solution.py:52
  141.9 12.1 %collective-permute-start.26 = (bf16[128,768]{1,0:T(8,128)(2,1)S(1)}, bf16[128,768]{1,0:T(8,128)(2,1)S(1)}, u32[]{:S(2)}, u32[]{:S(2)}) collective-permute-start(bf16[128,768]{1,0:T(8,128)(2,1)S(1)} %copy-done.12), channel_id=1, source_target_pairs={{0,1},{1,0},{2,3},{3,2},{4,5},{5,4},{6,7},{7,6},{8,9},{9,8},{10,11... | collective-permute-start | bytes 589832 | tf_op jit(solution)/shard_map/ppermute | solution.py:52
  154.1 25.6 %copy-start.11 = (bf16[8,24,768]{2,1,0:T(8,128)(2,1)}, bf16[8,24,768]{2,1,0:T(8,128)(2,1)S(1)}, u32[]{:S(2)}) copy-start(bf16[8,24,768]{2,1,0:T(8,128)(2,1)S(1)} %all-to-all-done.3.returned_ref) | copy-start | bytes 884740
  154.1 15.4 %all-to-all-start.4 = ((bf16[4,2,384,128]{3,2,1,0:T(8,128)(2,1)}), bf16[4,2,384,128]{3,2,1,0:T(8,128)(2,1)S(1)}, u32[]{:S(2)}, u32[]{:S(2)}) async-start(bf16[4,2,384,128]{3,2,1,0:T(8,128)(2,1)} %get-tuple-element.169), calls=%async_computation.4 | async-start | bytes 1572864 | tf_op jit(solution)/shard_map/all_to_all | solution.py:754
  158.2 1.5 collective-permute-start.29
  160.6 4.4 %collective-permute-start.30 = (f32[24,768]{1,0:T(8,128)S(1)}, f32[24,768]{1,0:T(8,128)S(1)}, u32[]{:S(2)}, u32[]{:S(2)}) collective-permute-start(f32[24,768]{1,0:T(8,128)S(1)} %add.58), channel_id=1, source_target_pairs={{0,16},{8,24},{16,0},{24,8},{1,17},{9,25},{17,1},{25,9},{2,18},{10... | collective-permute-start | bytes 221192 | tf_op jit(solution)/shard_map/ppermute | solution.py:52
  165.0 4.4 %collective-permute-start.31 = (f32[24,768]{1,0:T(8,128)S(1)}, f32[24,768]{1,0:T(8,128)S(1)}, u32[]{:S(2)}, u32[]{:S(2)}) collective-permute-start(f32[24,768]{1,0:T(8,128)S(1)} %add.59), channel_id=1, source_target_pairs={{0,1},{1,0},{2,3},{3,2},{4,5},{5,4},{6,7},{7,6},{8,9},{9,8},{10,11... | collective-permute-start | bytes 221192 | tf_op jit(solution)/shard_map/ppermute | solution.py:52
  174.7 5.0 %collective-permute-start.32 = (bf16[2,192,384]{2,1,0:T(8,128)(2,1)}, bf16[2,192,384]{2,1,0:T(8,128)(2,1)S(1)}, u32[]{:S(2)}, u32[]{:S(2)}) collective-permute-start(bf16[2,192,384]{2,1,0:T(8,128)(2,1)} %get-tuple-element.181), channel_id=1, source_target_pairs={{0,8},{8,0},{16,24},{24,16},{1,9},{9,1},{17,25},{25,17},{2,10},{10... | collective-permute-start | bytes 884744 | tf_op jit(solution)/shard_map/ppermute | solution.py:52
  174.7 5.0 %collective-permute-start.34 = (f32[24,768]{1,0:T(8,128)S(1)}, f32[24,768]{1,0:T(8,128)S(1)}, u32[]{:S(2)}, u32[]{:S(2)}) collective-permute-start(f32[24,768]{1,0:T(8,128)S(1)} %add.60), channel_id=1, source_target_pairs={{0,2},{1,3},{2,0},{3,1},{4,6},{5,7},{6,4},{7,5},{8,10},{9,11},{10,... | collective-permute-start | bytes 221192 | tf_op jit(solution)/shard_map/ppermute | solution.py:52
  176.8 4.0 %collective-permute-start.33 = (bf16[2,192,384]{2,1,0:T(8,128)(2,1)}, bf16[2,192,384]{2,1,0:T(8,128)(2,1)S(1)}, u32[]{:S(2)}, u32[]{:S(2)}) collective-permute-start(bf16[2,192,384]{2,1,0:T(8,128)(2,1)} %get-tuple-element.183), channel_id=1, source_target_pairs={{0,8},{8,0},{16,24},{24,16},{1,9},{9,1},{17,25},{25,17},{2,10},{10... | collective-permute-start | bytes 884744 | tf_op jit(solution)/shard_map/ppermute | solution.py:52
  181.8 6.8 %collective-permute-start.36 = (f32[24,768]{1,0:T(8,128)S(1)}, f32[24,768]{1,0:T(8,128)S(1)}, u32[]{:S(2)}, u32[]{:S(2)}) collective-permute-start(f32[24,768]{1,0:T(8,128)S(1)} %add.63), channel_id=1, source_target_pairs={{0,4},{1,5},{2,6},{3,7},{4,0},{5,1},{6,2},{7,3},{8,12},{9,13},{10,... | collective-permute-start | bytes 221192 | tf_op jit(solution)/shard_map/ppermute | solution.py:52
  184.3 8.5 %collective-permute-start.35 = (bf16[2,192,384]{2,1,0:T(8,128)(2,1)S(1)}, bf16[2,192,384]{2,1,0:T(8,128)(2,1)S(1)}, u32[]{:S(2)}, u32[]{:S(2)}) collective-permute-start(bf16[2,192,384]{2,1,0:T(8,128)(2,1)S(1)} %add_convert_fusion), channel_id=1, source_target_pairs={{0,16},{8,24},{16,0},{24,8},{1,17},{9,25},{17,1},{25,9},{2,18},{10... | collective-permute-start | bytes 884744 | tf_op jit(solution)/shard_map/ppermute | solution.py:52
  192.8 8.5 %collective-permute-start.37 = (bf16[192,384]{1,0:T(8,128)(2,1)S(1)}, bf16[192,384]{1,0:T(8,128)(2,1)S(1)}, u32[]{:S(2)}, u32[]{:S(2)}) collective-permute-start(bf16[192,384]{1,0:T(8,128)(2,1)S(1)} %fusion), channel_id=1, source_target_pairs={{0,4},{1,5},{2,6},{3,7},{4,0},{5,1},{6,2},{7,3},{8,12},{9,13},{10,... | collective-permute-start | bytes 442376 | tf_op jit(solution)/shard_map/ppermute | solution.py:52
  (22 other events, 185.2 us)

commit v15 on v14

--- a/solution.py
+++ b/solution.py
@@ -675,7 +675,7 @@
     )
     arrived, up_act, attended_own = together(arrived, up_act, attended)
     row_far = gather_far(arrived)
-    row_far, near_attended = together(row_far, half_ranks(attended_own))
+    near_attended = half_ranks(attended_own)
     row_pieces = gather_near(row_far)
 
     *back, slot_rows, activated, pre_grad, gates = call(
@@ -696,6 +696,7 @@
             pltpu.VMEM((*by_expert, 128), LOW),
         ],
     )
+    back, near_attended = together(back, near_attended)
     near, late_activated = together(scatter_near(back), activated)
     kept, got = scatter_far(near)
     returned = call(

time: 203 us -> 202 us (level)
    ppermute x38, waiting for transfers between devices: 62.4 us -> 60.2 us  [swap(): return lax.ppermute(value, axis, [(i, i ^ mask) for i in range(count)])]
  transfers between devices with their start and end apart: 43 -> 43, of which waited for: 25 -> 23; matrix products, arithmetic and copies ran while one was open for 4% -> 4% of each run, Pallas kernels for 21% -> 26%
where the time goes in v15:
time: 202 us; the launch traced here: 201 us
  waiting for transfers between devices  67.2 us (33%)
  starting transfers between devices  57.8 us (29%)
  Pallas kernels  56.7 us (28%)
  other arithmetic  9.64 us (5%)
  local copies, waits for them, and re-layouts  8.03 us (4%)
    ppermute x38, waiting for transfers between devices, swap(): return lax.ppermute(value, axis, [(i, i ^ mask) for i in range(count)])  60.2 us
    pallas_call x8, Pallas kernels, call(): pl.pallas_call(kernel, out_shape=tuple(out_shape), in_specs=[VMEM] * len(...  50.5 us
    ppermute x38, starting transfers between devices, swap(): return lax.ppermute(value, axis, [(i, i ^ mask) for i in range(count)])  34.5 us
    all_to_all x4, starting transfers between devices, exchange(): lax.all_to_all(value, 'expert', split_axis=0, concat_axis=0, tiled=True)  19.5 us
    all_to_all x4, waiting for transfers between devices, exchange(): lax.all_to_all(value, 'expert', split_axis=0, concat_axis=0, tiled=True)  7 us
    convert_element_type x8, other arithmetic, add(): return (left.astype(FULL) + right.astype(FULL)).astype(dtype)  6.81 us
    pallas_call x1, Pallas kernels, expert_gradients(): pl.pallas_call(expert_grad_kernel, grid=(shapes[0].shape[0],), out_shape=...  6.25 us
  transfers between devices with their start and end apart: 43, of which 23 were waited for; matrix products, arithmetic and copies ran while one was open for 4% of the time, Pallas kernels for 26%

profile of v15, /device:TPU:0, one launch (start us, length us, event | category | flops | bytes accessed | tf_op | source)
XLA Modules:
  0.0 200.5 jit_solution(5826287187225386317)
XLA Ops:
  1.7 5.1 %collective-permute-start.2 = (bf16[1,192,384]{2,1,0:T(8,128)(2,1)S(1)}, bf16[1,192,384]{2,1,0:T(8,128)(2,1)S(1)}, u32[]{:S(2)}, u32[]{:S(2)}) collective-permute-start(bf16[1,192,384]{2,1,0:T(8,128)(2,1)S(1)} %maximum_bitcast_fusion), channel_id=1, source_target_pairs={{0,6},{1,7},{2,4},{3,5},{4,2},{5,3},{6,0},{7,1},{8,14},{9,15},{10,... | collective-permute-start | bytes 442376 | tf_op jit(solution)/shard_map/ppermute | solution.py:52
  9.4 3.3 %early.1 = (bf16[128,768]{1,0:T(8,128)(2,1)}, f32[128,16]{1,0:T(8,128)}, bf16[128,192]{1,0:T(8,128)(2,1)}, bf16[192,128]{1,0:T(8,128)(2,1)}, f32[12,128,128]{2,1,0:T(8,128)}, /*index=5*/bf16[8,24,768]{2,1,0:T(8,128)(2,1)}) custom-call(bf16[128,768]{1,0:T(8,128)(2,1)} %tokens_ref.5, s32[1,128]{1,0:T(1,128)} %bitcast.27, ...), custom_call_target="tpu_custom_call" | custom-call | bytes 10800000 | tf_op jit(solution)/shard_map/early/pallas_call | solution.py:566
  12.7 6.5 %collective-permute-done.1 = bf16[1,192,384]{2,1,0:T(8,128)(2,1)S(1)} collective-permute-done((bf16[1,192,384]{2,1,0:T(8,128)(2,1)S(1)}, bf16[1,192,384]{2,1,0:T(8,128)(2,1)S(1)}, u32[]{:S(2)}, u32[]{:S(2)}) %collective-permute-start.1) | collective-permute-done | bytes 147488 | tf_op jit(solution)/shard_map/ppermute | solution.py:52
  19.4 1.6 collective-permute-start.3
  21.0 1.5 collective-permute-start.7
  22.5 5.1 %collective-permute-done.3 = bf16[1,4,96,384]{3,2,1,0:T(8,128)(2,1)S(1)} collective-permute-done((bf16[1,4,96,384]{3,2,1,0:T(8,128)(2,1)S(1)}, bf16[1,4,96,384]{3,2,1,0:T(8,128)(2,1)S(1)}, u32[]{:S(2)}, u32[]{:S(2)}) %collective-permute-start.3) | collective-permute-done | bytes 294944 | tf_op jit(solution)/shard_map/ppermute | solution.py:52
  27.6 1.6 collective-permute-start.5
  29.3 1.6 collective-permute-start.9
  31.4 10.0 %collective-permute-done.5.rest_2_ = bf16[2,4,96,384]{3,2,1,0:T(8,128)(2,1)S(1)} collective-permute-done((bf16[2,4,96,384]{3,2,1,0:T(8,128)(2,1)S(1)}, bf16[2,4,96,384]{3,2,1,0:T(8,128)(2,1)S(1)}, u32[]{:S(2)}, u32[]{:S(2)}) %collective-permute-start.5) | collective-permute-done | bytes 589856 | tf_op jit(solution)/shard_map/ppermute | solution.py:52
  41.4 1.1 collective-permute-done.9.rest_6_
  43.4 1.1 collective-permute-done.10.rest_7_
  45.4 4.3 %all-to-all-start = ((bf16[8,24,768]{2,1,0:T(8,128)(2,1)}), bf16[8,24,768]{2,1,0:T(8,128)(2,1)}, u32[]{:S(2)}, u32[]{:S(2)}) async-start(bf16[8,24,768]{2,1,0:T(8,128)(2,1)} %get-tuple-element.134), calls=%async_computation | async-start | bytes 589824 | tf_op jit(solution)/shard_map/all_to_all | solution.py:60
  49.8 10.3 %attention_forward.1 = (bf16[3,768,128]{2,1,0:T(8,128)(2,1)}, f32[12,128,128]{2,1,0:T(8,128)}, bf16[128,768]{1,0:T(8,128)(2,1)}, f32[128,768]{1,0:T(8,128)}, f32...) custom-call(bf16[128,768]{1,0:T(8,128)(2,1)} %tokens_ref.5, bf16[128,768]{1,0:T(8,128)(2,1)} %get-tuple-element.176.normed_ref.rest_0_, ...), custom_call_target="tpu_custom_call" | custom-call | bytes 36000000 | tf_op jit(solution)/shard_map/attention_forward/pallas_call | solution.py:566
  61.2 6.0 %all-to-all-start.1 = ((bf16[8,24,768]{2,1,0:T(8,128)(2,1)}), bf16[8,24,768]{2,1,0:T(8,128)(2,1)S(1)}, u32[]{:S(2)}, u32[]{:S(2)}) async-start(bf16[8,24,768]{2,1,0:T(8,128)(2,1)} %get-tuple-element.135), calls=%async_computation.1 | async-start | bytes 589824 | tf_op jit(solution)/shard_map/all_to_all | solution.py:60
  67.2 2.0 %collective-permute-done.12.rest_2_ = bf16[192,768]{1,0:T(8,128)(2,1)S(1)} collective-permute-done((bf16[192,768]{1,0:T(8,128)(2,1)}, bf16[192,768]{1,0:T(8,128)(2,1)S(1)}, u32[]{:S(2)}, u32[]{:S(2)}) %collective-permute-start.12) | collective-permute-done | bytes 294944 | tf_op jit(solution)/shard_map/ppermute | solution.py:52
  69.2 1.6 collective-permute-done.13.rest_3_
  71.5 4.5 %upstream_rows.1 = (bf16[2,320,768]{2,1,0:T(8,128)(2,1)}, f32[2,320,768]{2,1,0:T(8,128)}) custom-call(bf16[160,192]{1,0:T(8,128)(2,1)} %constant.8.clone.pack_ref, bf16[2,768,768]{2,1,0:T(8,128)(2,1)} %w_out_ref.3, bf16[192,768]{1,0:T(8,128)(2,1)} %bitcast.6.rest_0_, bf16[192,768]{1,0:T(8,128)(2,1)} %copy-done.17, bf16[192,768]{1,0:T(8,128)(2,1)} %copy-done.16, ...), custom_call_target="tpu_custom_call" | custom-call | bytes 3600000 | tf_op jit(solution)/shard_map/upstream_rows/pallas_call | solution.py:566
  77.3 7.8 %collective-permute-done.15.rest_2_ = bf16[192,768]{1,0:T(8,128)(2,1)S(1)} collective-permute-done((bf16[192,768]{1,0:T(8,128)(2,1)S(1)}, bf16[192,768]{1,0:T(8,128)(2,1)S(1)}, u32[]{:S(2)}, u32[]{:S(2)}) %collective-permute-start.15) | collective-permute-done | bytes 294944 | tf_op jit(solution)/shard_map/ppermute | solution.py:52
  85.1 1.8 collective-permute-start.17
  86.9 1.5 collective-permute-start.18
  90.1 9.9 %experts.1 = (bf16[192,768]{1,0:T(8,128)(2,1)}, bf16[192,768]{1,0:T(8,128)(2,1)}, bf16[192,768]{1,0:T(8,128)(2,1)}, bf16[192,768]{1,0:T(8,128)(2,1)}, bf16[2,320...) custom-call(bf16[160,192]{1,0:T(8,128)(2,1)} %constant.8.clone.pack_re, ...), custom_call_target="tpu_custom_call" | custom-call | bytes 36000000 | tf_op jit(solution)/shard_map/experts/pallas_call | solution.py:566
  100.7 1.3 collective-permute-done.20
  104.0 1.3 collective-permute-start.22
  105.3 4.0 %expert_outputs.1 = (bf16[192,768]{1,0:T(8,128)(2,1)}, bf16[192,768]{1,0:T(8,128)(2,1)}, bf16[192,768]{1,0:T(8,128)(2,1)}, bf16[192,768]{1,0:T(8,128)(2,1)}) custom-call(bf16[192,160]{1,0:T(8,128)(2,1)} %constant.9.clone.pack_t_ref, bf16[2,768,768]{2,1,0:T(8,128)(2,1)} %w_out_ref.3, bf16[2,320,768]{2,1,0:T(8,128)(2,1)} %get-tuple-element.198.act_ref), custom_call_target="tpu_custom_call" | custom-call | bytes 10800000 | tf_op jit(solution)/shard_map/expert_outputs/pallas_call | solution.py:566
  109.3 3.8 %collective-permute-done.22 = bf16[192,768]{1,0:T(8,128)(2,1)S(1)} collective-permute-done((bf16[192,768]{1,0:T(8,128)(2,1)S(1)}, bf16[192,768]{1,0:T(8,128)(2,1)S(1)}, u32[]{:S(2)}, u32[]{:S(2)}) %collective-permute-start.22) | collective-permute-done | bytes 294944 | tf_op jit(solution)/shard_map/ppermute | solution.py:52
  114.4 1.3 collective-permute-done.24
  116.8 1.3 collective-permute-start.25
  118.0 5.6 %all-to-all-start.2 = ((bf16[8,24,768]{2,1,0:T(8,128)(2,1)}), bf16[8,24,768]{2,1,0:T(8,128)(2,1)S(1)}, u32[]{:S(2)}, u32[]{:S(2)}) async-start(bf16[8,24,768]{2,1,0:T(8,128)(2,1)} %bitcast.8), calls=%async_computation.2 | async-start | bytes 589824 | tf_op jit(solution)/shard_map/all_to_all | solution.py:60
  123.7 2.2 %collective-permute-done.25 = bf16[192,768]{1,0:T(8,128)(2,1)S(1)} collective-permute-done((bf16[192,768]{1,0:T(8,128)(2,1)S(1)}, bf16[192,768]{1,0:T(8,128)(2,1)S(1)}, u32[]{:S(2)}, u32[]{:S(2)}) %collective-permute-start.25) | collective-permute-done | bytes 294944 | tf_op jit(solution)/shard_map/ppermute | solution.py:52
  126.7 6.6 %all-to-all-done.2.rest_8_ = bf16[8,24,768]{2,1,0:T(8,128)(2,1)S(1)} async-done(((bf16[8,24,768]{2,1,0:T(8,128)(2,1)}), bf16[8,24,768]{2,1,0:T(8,128)(2,1)S(1)}, u32[]{:S(2)}, u32[]{:S(2)}) %all-to-all-start.2) | async-done | bytes 294944 | tf_op jit(solution)/shard_map/all_to_all | solution.py:60
  133.3 3.6 %all-to-all-start.3 = ((bf16[8,24,768]{2,1,0:T(8,128)(2,1)}), bf16[8,24,768]{2,1,0:T(8,128)(2,1)S(1)}, u32[]{:S(2)}, u32[]{:S(2)}) async-start(bf16[8,24,768]{2,1,0:T(8,128)(2,1)} %bitcast.9), calls=%async_computation.3 | async-start | bytes 589824 | tf_op jit(solution)/shard_map/all_to_all | solution.py:60
  136.9 2.0 %collective-permute-start.26 = (bf16[128,768]{1,0:T(8,128)(2,1)S(1)}, bf16[128,768]{1,0:T(8,128)(2,1)S(1)}, u32[]{:S(2)}, u32[]{:S(2)}) collective-permute-start(bf16[128,768]{1,0:T(8,128)(2,1)S(1)} %copy-done.12), channel_id=1, source_target_pairs={{0,1},{1,0},{2,3},{3,2},{4,5},{5,4},{6,7},{7,6},{8,9},{9,8},{10,11... | collective-permute-start | bytes 589832 | tf_op jit(solution)/shard_map/ppermute | solution.py:52
  138.9 1.5 collective-permute-start.27
  140.4 12.0 %attention_backward.1 = (f32[128,768]{1,0:T(8,128)}, f32[24,768]{1,0:T(8,128)}, bf16[4,2,384,128]{3,2,1,0:T(8,128)(2,1)}) custom-call(bf16[128,768]{1,0:T(8,128)(2,1)} %tokens_ref.5, f32[2,768]{1,0:T(2,128)} %maximum_convert_fusion.gain_ref, bf16[16,768]{1,0:T(8,128)(2,1)} %bitcast.25, f32[128,16]{1,0:T(8,128)} %get-tuple-element.114.hits_ref, ...), custom_call_target="tpu_custom_call" | custom-call | bytes 43200000 | tf_op jit(solution)/shard_map/attention_backward/pallas_call | solution.py:566
  152.9 3.8 %all-to-all-start.4 = ((bf16[4,2,384,128]{3,2,1,0:T(8,128)(2,1)}), bf16[4,2,384,128]{3,2,1,0:T(8,128)(2,1)S(1)}, u32[]{:S(2)}, u32[]{:S(2)}) async-start(bf16[4,2,384,128]{3,2,1,0:T(8,128)(2,1)} %get-tuple-element.173), calls=%async_computation.4 | async-start | bytes 1572864 | tf_op jit(solution)/shard_map/all_to_all | solution.py:755
  156.7 1.5 collective-permute-done.29
  160.0 3.5 %collective-permute-done.30 = f32[24,768]{1,0:T(8,128)S(1)} collective-permute-done((f32[24,768]{1,0:T(8,128)S(1)}, f32[24,768]{1,0:T(8,128)S(1)}, u32[]{:S(2)}, u32[]{:S(2)}) %collective-permute-start.30) | collective-permute-done | bytes 73760 | tf_op jit(solution)/shard_map/ppermute | solution.py:52
  163.5 2.1 %collective-permute-start.31 = (f32[24,768]{1,0:T(8,128)S(1)}, f32[24,768]{1,0:T(8,128)S(1)}, u32[]{:S(2)}, u32[]{:S(2)}) collective-permute-start(f32[24,768]{1,0:T(8,128)S(1)} %add.59), channel_id=1, source_target_pairs={{0,1},{1,0},{2,3},{3,2},{4,5},{5,4},{6,7},{7,6},{8,9},{9,8},{10,11... | collective-permute-start | bytes 221192 | tf_op jit(solution)/shard_map/ppermute | solution.py:52
  165.6 2.4 %collective-permute-done.31 = f32[24,768]{1,0:T(8,128)S(1)} collective-permute-done((f32[24,768]{1,0:T(8,128)S(1)}, f32[24,768]{1,0:T(8,128)S(1)}, u32[]{:S(2)}, u32[]{:S(2)}) %collective-permute-start.31) | collective-permute-done | bytes 73760 | tf_op jit(solution)/shard_map/ppermute | solution.py:52
  168.9 4.3 %weight_gradients.1 = (bf16[2,192,384]{2,1,0:T(8,128)(2,1)}, bf16[2,192,384]{2,1,0:T(8,128)(2,1)}, bf16[2,192,384]{2,1,0:T(8,128)(2,1)}, bf16[2,192,384]{2,1,0:T(8,128)(2,1)}) custom-call(bf16[4,2,384,128]{3,2,1,0:T(8,128)(2,1)} %copy-done.2, bf16[128,768]{1,0:T(8,128)(2,1)} %get-tuple-element.176.normed_ref.rest_0_, bf16[128,768]{1,0:T(8,128)(2,1)} %copy-done.24, ...), custom_call_target="tpu_custom_call" | custom-call | bytes 18000000 | tf_op jit(solution)/shard_map/weight_gradients/pallas_call | solution.py:566
  173.2 2.0 %collective-permute-start.34 = (f32[24,768]{1,0:T(8,128)S(1)}, f32[24,768]{1,0:T(8,128)S(1)}, u32[]{:S(2)}, u32[]{:S(2)}) collective-permute-start(f32[24,768]{1,0:T(8,128)S(1)} %add.60), channel_id=1, source_target_pairs={{0,2},{1,3},{2,0},{3,1},{4,6},{5,7},{6,4},{7,5},{8,10},{9,11},{10,... | collective-permute-start | bytes 221192 | tf_op jit(solution)/shard_map/ppermute | solution.py:52
  175.4 2.7 %collective-permute-done.34 = f32[24,768]{1,0:T(8,128)S(1)} collective-permute-done((f32[24,768]{1,0:T(8,128)S(1)}, f32[24,768]{1,0:T(8,128)S(1)}, u32[]{:S(2)}, u32[]{:S(2)}) %collective-permute-start.34) | collective-permute-done | bytes 73760 | tf_op jit(solution)/shard_map/ppermute | solution.py:52
  178.2 1.0 add_convert_fusion.1
  180.3 2.4 %collective-permute-start.36 = (f32[24,768]{1,0:T(8,128)S(1)}, f32[24,768]{1,0:T(8,128)S(1)}, u32[]{:S(2)}, u32[]{:S(2)}) collective-permute-start(f32[24,768]{1,0:T(8,128)S(1)} %add.63), channel_id=1, source_target_pairs={{0,4},{1,5},{2,6},{3,7},{4,0},{5,1},{6,2},{7,3},{8,12},{9,13},{10,... | collective-permute-start | bytes 221192 | tf_op jit(solution)/shard_map/ppermute | solution.py:52
  183.6 2.1 %output_rows.1 = bf16[128,768]{1,0:T(8,128)(2,1)} custom-call(f32[128,768]{1,0:T(8,128)} %get-tuple-element.129.hidden_ref, f32[128,16]{1,0:T(8,128)} %get-tuple-element.130.chance_ref, f32[128,16]{1,0:T(8,128)} %get-tuple-element.114.hits_ref, bf16[128,192]{1,0:T(8,128)(2,1)} %get-tuple-element.115.mask_ref, bf16[8,24,768]{2,1,0:T(8,128)(2,1)} %copy-done.11), custom_call_target="tpu_custom_call" | custom-call | bytes 7200000 | tf_op jit(solution)/shard_map/output_rows/pallas_call | solution.py:566
  185.7 1.4 collective-permute-done.36
  187.8 3.3 %collective-permute-done.35 = bf16[2,192,384]{2,1,0:T(8,128)(2,1)S(1)} collective-permute-done((bf16[2,192,384]{2,1,0:T(8,128)(2,1)S(1)}, bf16[2,192,384]{2,1,0:T(8,128)(2,1)S(1)}, u32[]{:S(2)}, u32[]{:S(2)}) %collective-permute-start.35) | collective-permute-done | bytes 294944 | tf_op jit(solution)/shard_map/ppermute | solution.py:52
  193.1 6.2 %expert_gradients.1 = (f32[2,768,768]{2,1,0:T(8,128)}, f32[2,768,768]{2,1,0:T(8,128)}) custom-call(bf16[2,320,768]{2,1,0:T(8,128)(2,1)} %get-tuple-element.197.rows_ref, bf16[2,320,768]{2,1,0:T(8,128)(2,1)} %get-tuple-element.198.act_ref, bf16[2,320,768]{2,1,0:T(8,128)(2,1)} %get-tuple-element.199.pre_grad_ref, f32[2,320,128]{2,1,0:T(8,128)} %get-tuple-element.200.gates_ref, ...), custom_call_target="tpu_custom_call" | custom-call | bytes 28800000 | tf_op jit(solution)/shard_map/expert_gradients/pallas_call | solution.py:426
  (129 shorter events, 25.9 us)
Async XLA Ops:
  1.7 11.1 %collective-permute-start.2 = (bf16[1,192,384]{2,1,0:T(8,128)(2,1)S(1)}, bf16[1,192,384]{2,1,0:T(8,128)(2,1)S(1)}, u32[]{:S(2)}, u32[]{:S(2)}) collective-permute-start(bf16[1,192,384]{2,1,0:T(8,128)(2,1)S(1)} %maximum_bitcast_fusion), channel_id=1, source_target_pairs={{0,6},{1,7},{2,4},{3,5},{4,2},{5,3},{6,0},{7,1},{8,14},{9,15},{10,... | collective-permute-start | bytes 442376 | tf_op jit(solution)/shard_map/ppermute | solution.py:52
  6.8 12.5 %collective-permute-start.1 = (bf16[1,192,384]{2,1,0:T(8,128)(2,1)S(1)}, bf16[1,192,384]{2,1,0:T(8,128)(2,1)S(1)}, u32[]{:S(2)}, u32[]{:S(2)}) collective-permute-start(bf16[1,192,384]{2,1,0:T(8,128)(2,1)S(1)} %maximum_bitcast_fusion), channel_id=1, source_target_pairs={{0,4},{1,5},{2,6},{3,7},{4,0},{5,1},{6,2},{7,3},{8,12},{9,13},{10,... | collective-permute-start | bytes 442376 | tf_op jit(solution)/shard_map/ppermute | solution.py:52
  6.8 12.5 %collective-permute-start = (bf16[1,192,384]{2,1,0:T(8,128)(2,1)S(1)}, bf16[1,192,384]{2,1,0:T(8,128)(2,1)S(1)}, u32[]{:S(2)}, u32[]{:S(2)}) collective-permute-start(bf16[1,192,384]{2,1,0:T(8,128)(2,1)S(1)} %maximum_bitcast_fusion), channel_id=1, source_target_pairs={{0,2},{1,3},{2,0},{3,1},{4,6},{5,7},{6,4},{7,5},{8,10},{9,11},{10,... | collective-permute-start | bytes 442376 | tf_op jit(solution)/shard_map/ppermute | solution.py:52
  19.4 8.1 %collective-permute-start.3 = (bf16[1,4,96,384]{3,2,1,0:T(8,128)(2,1)S(1)}, bf16[1,4,96,384]{3,2,1,0:T(8,128)(2,1)S(1)}, u32[]{:S(2)}, u32[]{:S(2)}) collective-permute-start(bf16[1,4,96,384]{3,2,1,0:T(8,128)(2,1)S(1)} %get-tuple-element.209), channel_id=1, source_target_pairs={{0,1},{1,0},{2,3},{3,2},{4,5},{5,4},{6,7},{7,6},{8,9},{9,8},{10,11... | collective-permute-start | bytes 884744 | tf_op jit(solution)/shard_map/ppermute | solution.py:52
  21.0 8.2 %collective-permute-start.7 = (bf16[1,4,96,384]{3,2,1,0:T(8,128)(2,1)S(1)}, bf16[1,4,96,384]{3,2,1,0:T(8,128)(2,1)S(1)}, u32[]{:S(2)}, u32[]{:S(2)}) collective-permute-start(bf16[1,4,96,384]{3,2,1,0:T(8,128)(2,1)S(1)} %get-tuple-element.208), channel_id=1, source_target_pairs={{0,16},{8,24},{16,0},{24,8},{1,17},{9,25},{17,1},{25,9},{2,18},{10... | collective-permute-start | bytes 884744 | tf_op jit(solution)/shard_map/ppermute | solution.py:52
  27.6 22.1 %copy-start = (bf16[2,4,96,384]{3,2,1,0:T(8,128)(2,1)}, bf16[2,4,96,384]{3,2,1,0:T(8,128)(2,1)S(1)}, u32[]{:S(2)}) copy-start(bf16[2,4,96,384]{3,2,1,0:T(8,128)(2,1)S(1)} %pad_maximum_fusion.1.rest_0_) | copy-start | bytes 1769476
  27.6 13.8 %collective-permute-start.5 = (bf16[2,4,96,384]{3,2,1,0:T(8,128)(2,1)S(1)}, bf16[2,4,96,384]{3,2,1,0:T(8,128)(2,1)S(1)}, u32[]{:S(2)}, u32[]{:S(2)}) collective-permute-start(bf16[2,4,96,384]{3,2,1,0:T(8,128)(2,1)S(1)} %pad_maximum_fusion.1.rest_0_), channel_id=1, source_target_pairs={{0,16},{8,24},{16,0},{24,8},{1,17},{9,25},{17,1},{25,9},{2,18},{10... | collective-permute-start | bytes 1769480 | tf_op jit(solution)/shard_map/ppermute | solution.py:52
  29.3 20.4 %copy-start.1 = (bf16[2,4,96,384]{3,2,1,0:T(8,128)(2,1)}, bf16[2,4,96,384]{3,2,1,0:T(8,128)(2,1)S(1)}, u32[]{:S(2)}) copy-start(bf16[2,4,96,384]{3,2,1,0:T(8,128)(2,1)S(1)} %pad_maximum_fusion.2.rest_4_) | copy-start | bytes 1769476
  29.3 13.2 %collective-permute-start.9 = (bf16[2,4,96,384]{3,2,1,0:T(8,128)(2,1)S(1)}, bf16[2,4,96,384]{3,2,1,0:T(8,128)(2,1)S(1)}, u32[]{:S(2)}, u32[]{:S(2)}) collective-permute-start(bf16[2,4,96,384]{3,2,1,0:T(8,128)(2,1)S(1)} %pad_maximum_fusion.2.rest_4_), channel_id=1, source_target_pairs={{0,1},{1,0},{2,3},{3,2},{4,5},{5,4},{6,7},{7,6},{8,9},{9,8},{10,11... | collective-permute-start | bytes 1769480 | tf_op jit(solution)/shard_map/ppermute | solution.py:52
  30.9 11.7 %collective-permute-start.4 = (bf16[2,4,96,384]{3,2,1,0:T(8,128)(2,1)S(1)}, bf16[2,4,96,384]{3,2,1,0:T(8,128)(2,1)S(1)}, u32[]{:S(2)}, u32[]{:S(2)}) collective-permute-start(bf16[2,4,96,384]{3,2,1,0:T(8,128)(2,1)S(1)} %pad_maximum_fusion.1.rest_0_), channel_id=1, source_target_pairs={{0,8},{8,0},{16,24},{24,16},{1,9},{9,1},{17,25},{25,17},{2,10},{10... | collective-permute-start | bytes 1769480 | tf_op jit(solution)/shard_map/ppermute | solution.py:52
  30.9 11.7 %collective-permute-start.8 = (bf16[2,4,96,384]{3,2,1,0:T(8,128)(2,1)S(1)}, bf16[2,4,96,384]{3,2,1,0:T(8,128)(2,1)S(1)}, u32[]{:S(2)}, u32[]{:S(2)}) collective-permute-start(bf16[2,4,96,384]{3,2,1,0:T(8,128)(2,1)S(1)} %pad_maximum_fusion.2.rest_4_), channel_id=1, source_target_pairs={{0,8},{8,0},{16,24},{24,16},{1,9},{9,1},{17,25},{25,17},{2,10},{10... | collective-permute-start | bytes 1769480 | tf_op jit(solution)/shard_map/ppermute | solution.py:52
  41.4 2.0 collective-permute-start.6
  42.6 2.0 collective-permute-start.10
  45.4 14.8 %all-to-all-start = ((bf16[8,24,768]{2,1,0:T(8,128)(2,1)}), bf16[8,24,768]{2,1,0:T(8,128)(2,1)}, u32[]{:S(2)}, u32[]{:S(2)}) async-start(bf16[8,24,768]{2,1,0:T(8,128)(2,1)} %get-tuple-element.134), calls=%async_computation | async-start | bytes 589824 | tf_op jit(solution)/shard_map/all_to_all | solution.py:60
  60.1 25.0 %copy-start.20 = (bf16[128,768]{1,0:T(8,128)(2,1)S(1)}, bf16[128,768]{1,0:T(8,128)(2,1)}, u32[]{:S(2)}) copy-start(bf16[128,768]{1,0:T(8,128)(2,1)} %get-tuple-element.180.rest_4_) | copy-start | bytes 589828
  60.2 9.1 %collective-permute-start.12 = (bf16[192,768]{1,0:T(8,128)(2,1)}, bf16[192,768]{1,0:T(8,128)(2,1)S(1)}, u32[]{:S(2)}, u32[]{:S(2)}) collective-permute-start(bf16[192,768]{1,0:T(8,128)(2,1)} %bitcast.6.rest_0_), channel_id=1, source_target_pairs={{0,16},{8,24},{16,0},{24,8},{1,17},{9,25},{17,1},{25,9},{2,18},{10... | collective-permute-start | bytes 884744 | tf_op jit(solution)/shard_map/ppermute | solution.py:52
  61.2 15.2 %all-to-all-start.1 = ((bf16[8,24,768]{2,1,0:T(8,128)(2,1)}), bf16[8,24,768]{2,1,0:T(8,128)(2,1)S(1)}, u32[]{:S(2)}, u32[]{:S(2)}) async-start(bf16[8,24,768]{2,1,0:T(8,128)(2,1)} %get-tuple-element.135), calls=%async_computation.1 | async-start | bytes 589824 | tf_op jit(solution)/shard_map/all_to_all | solution.py:60
  67.2 2.0 %collective-permute-start.11 = (bf16[192,768]{1,0:T(8,128)(2,1)}, bf16[192,768]{1,0:T(8,128)(2,1)S(1)}, u32[]{:S(2)}, u32[]{:S(2)}) collective-permute-start(bf16[192,768]{1,0:T(8,128)(2,1)} %bitcast.6.rest_0_), channel_id=1, source_target_pairs={{0,8},{8,0},{16,24},{24,16},{1,9},{9,1},{17,25},{25,17},{2,10},{10... | collective-permute-start | bytes 884744 | tf_op jit(solution)/shard_map/ppermute | solution.py:52
  69.2 1.6 collective-permute-start.13
  76.4 8.7 %collective-permute-start.15 = (bf16[192,768]{1,0:T(8,128)(2,1)S(1)}, bf16[192,768]{1,0:T(8,128)(2,1)S(1)}, u32[]{:S(2)}, u32[]{:S(2)}) collective-permute-start(bf16[192,768]{1,0:T(8,128)(2,1)S(1)} %bitcast.21), channel_id=1, source_target_pairs={{0,16},{8,24},{16,0},{24,8},{1,17},{9,25},{17,1},{25,9},{2,18},{10... | collective-permute-start | bytes 884744 | tf_op jit(solution)/shard_map/ppermute | solution.py:52
  77.3 11.4 %collective-permute-start.14 = (bf16[192,768]{1,0:T(8,128)(2,1)S(1)}, bf16[192,768]{1,0:T(8,128)(2,1)S(1)}, u32[]{:S(2)}, u32[]{:S(2)}) collective-permute-start(bf16[192,768]{1,0:T(8,128)(2,1)S(1)} %bitcast.22), channel_id=1, source_target_pairs={{0,8},{8,0},{16,24},{24,16},{1,9},{9,1},{17,25},{25,17},{2,10},{10... | collective-permute-start | bytes 884744 | tf_op jit(solution)/shard_map/ppermute | solution.py:52
  85.1 3.6 %collective-permute-start.16 = (bf16[192,768]{1,0:T(8,128)(2,1)S(1)}, bf16[192,768]{1,0:T(8,128)(2,1)S(1)}, u32[]{:S(2)}, u32[]{:S(2)}) collective-permute-start(bf16[192,768]{1,0:T(8,128)(2,1)S(1)} %collective-permute-done.15.rest_2_), channel_id=1, source_target_pairs={{0,8},{8,0},{16,24},{24,16},{1,9},{9,1},{17,25},{25,17},{2,10},{10... | collective-permute-start | bytes 884744 | tf_op jit(solution)/shard_map/ppermute | solution.py:52
  85.1 14.9 %collective-permute-start.17 = (bf16[128,768]{1,0:T(8,128)(2,1)S(1)}, bf16[128,768]{1,0:T(8,128)(2,1)S(1)}, u32[]{:S(2)}, u32[]{:S(2)}) collective-permute-start(bf16[128,768]{1,0:T(8,128)(2,1)S(1)} %copy-done.20), channel_id=1, source_target_pairs={{0,1},{1,0},{2,3},{3,2},{4,5},{5,4},{6,7},{7,6},{8,9},{9,8},{10,11... | collective-permute-start | bytes 589832 | tf_op jit(solution)/shard_map/ppermute | solution.py:52
  86.9 13.2 %collective-permute-start.18 = (bf16[128,768]{1,0:T(8,128)(2,1)S(1)}, bf16[128,768]{1,0:T(8,128)(2,1)S(1)}, u32[]{:S(2)}, u32[]{:S(2)}) collective-permute-start(bf16[128,768]{1,0:T(8,128)(2,1)S(1)} %copy-done.20), channel_id=1, source_target_pairs={{0,2},{1,3},{2,0},{3,1},{4,6},{5,7},{6,4},{7,5},{8,10},{9,11},{10,... | collective-permute-start | bytes 589832 | tf_op jit(solution)/shard_map/ppermute | solution.py:52
  88.4 11.7 %collective-permute-start.19 = (bf16[128,768]{1,0:T(8,128)(2,1)S(1)}, bf16[128,768]{1,0:T(8,128)(2,1)S(1)}, u32[]{:S(2)}, u32[]{:S(2)}) collective-permute-start(bf16[128,768]{1,0:T(8,128)(2,1)S(1)} %copy-done.20), channel_id=1, source_target_pairs={{0,3},{1,2},{2,1},{3,0},{4,7},{5,6},{6,5},{7,4},{8,11},{9,10},{10,... | collective-permute-start | bytes 589832 | tf_op jit(solution)/shard_map/ppermute | solution.py:52
  100.1 1.9 collective-permute-start.20
  100.2 2.8 %collective-permute-start.21 = (bf16[192,768]{1,0:T(8,128)(2,1)}, bf16[192,768]{1,0:T(8,128)(2,1)S(1)}, u32[]{:S(2)}, u32[]{:S(2)}) collective-permute-start(bf16[192,768]{1,0:T(8,128)(2,1)} %get-tuple-element.149), channel_id=1, source_target_pairs={{0,8},{8,0},{16,24},{24,16},{1,9},{9,1},{17,25},{25,17},{2,10},{10... | collective-permute-start | bytes 884744 | tf_op jit(solution)/shard_map/ppermute | solution.py:52
  104.0 9.1 %collective-permute-start.22 = (bf16[192,768]{1,0:T(8,128)(2,1)S(1)}, bf16[192,768]{1,0:T(8,128)(2,1)S(1)}, u32[]{:S(2)}, u32[]{:S(2)}) collective-permute-start(bf16[192,768]{1,0:T(8,128)(2,1)S(1)} %add_convert_fusion.6), channel_id=1, source_target_pairs={{0,16},{8,24},{16,0},{24,8},{1,17},{9,25},{17,1},{25,9},{2,18},{10... | collective-permute-start | bytes 884744 | tf_op jit(solution)/shard_map/ppermute | solution.py:52
  109.3 27.6 %copy-start.12 = (bf16[128,768]{1,0:T(8,128)(2,1)S(1)}, bf16[128,768]{1,0:T(8,128)(2,1)}, u32[]{:S(2)}) copy-start(bf16[128,768]{1,0:T(8,128)(2,1)} %get-tuple-element.176.normed_ref.rest_0_) | copy-start | bytes 589828
  113.9 1.8 collective-permute-start.24
  113.9 9.7 %collective-permute-start.23 = (bf16[192,768]{1,0:T(8,128)(2,1)}, bf16[192,768]{1,0:T(8,128)(2,1)S(1)}, u32[]{:S(2)}, u32[]{:S(2)}) collective-permute-start(bf16[192,768]{1,0:T(8,128)(2,1)} %get-tuple-element.165), channel_id=1, source_target_pairs={{0,8},{8,0},{16,24},{24,16},{1,9},{9,1},{17,25},{25,17},{2,10},{10... | collective-permute-start | bytes 884744 | tf_op jit(solution)/shard_map/ppermute | solution.py:52
  116.8 9.1 %collective-permute-start.25 = (bf16[192,768]{1,0:T(8,128)(2,1)S(1)}, bf16[192,768]{1,0:T(8,128)(2,1)S(1)}, u32[]{:S(2)}, u32[]{:S(2)}) collective-permute-start(bf16[192,768]{1,0:T(8,128)(2,1)S(1)} %add_convert_fusion.3), channel_id=1, source_target_pairs={{0,16},{8,24},{16,0},{24,8},{1,17},{9,25},{17,1},{25,9},{2,18},{10... | collective-permute-start | bytes 884744 | tf_op jit(solution)/shard_map/ppermute | solution.py:52
  118.0 15.3 %all-to-all-start.2 = ((bf16[8,24,768]{2,1,0:T(8,128)(2,1)}), bf16[8,24,768]{2,1,0:T(8,128)(2,1)S(1)}, u32[]{:S(2)}, u32[]{:S(2)}) async-start(bf16[8,24,768]{2,1,0:T(8,128)(2,1)} %bitcast.8), calls=%async_computation.2 | async-start | bytes 589824 | tf_op jit(solution)/shard_map/all_to_all | solution.py:60
  133.3 19.6 %all-to-all-start.3 = ((bf16[8,24,768]{2,1,0:T(8,128)(2,1)}), bf16[8,24,768]{2,1,0:T(8,128)(2,1)S(1)}, u32[]{:S(2)}, u32[]{:S(2)}) async-start(bf16[8,24,768]{2,1,0:T(8,128)(2,1)} %bitcast.9), calls=%async_computation.3 | async-start | bytes 589824 | tf_op jit(solution)/shard_map/all_to_all | solution.py:60
  136.9 15.6 %collective-permute-start.26 = (bf16[128,768]{1,0:T(8,128)(2,1)S(1)}, bf16[128,768]{1,0:T(8,128)(2,1)S(1)}, u32[]{:S(2)}, u32[]{:S(2)}) collective-permute-start(bf16[128,768]{1,0:T(8,128)(2,1)S(1)} %copy-done.12), channel_id=1, source_target_pairs={{0,1},{1,0},{2,3},{3,2},{4,5},{5,4},{6,7},{7,6},{8,9},{9,8},{10,11... | collective-permute-start | bytes 589832 | tf_op jit(solution)/shard_map/ppermute | solution.py:52
  138.9 13.6 %collective-permute-start.27 = (bf16[128,768]{1,0:T(8,128)(2,1)S(1)}, bf16[128,768]{1,0:T(8,128)(2,1)S(1)}, u32[]{:S(2)}, u32[]{:S(2)}) collective-permute-start(bf16[128,768]{1,0:T(8,128)(2,1)S(1)} %copy-done.12), channel_id=1, source_target_pairs={{0,2},{1,3},{2,0},{3,1},{4,6},{5,7},{6,4},{7,5},{8,10},{9,11},{10,... | collective-permute-start | bytes 589832 | tf_op jit(solution)/shard_map/ppermute | solution.py:52
  140.4 12.5 %collective-permute-start.28 = (bf16[128,768]{1,0:T(8,128)(2,1)S(1)}, bf16[128,768]{1,0:T(8,128)(2,1)S(1)}, u32[]{:S(2)}, u32[]{:S(2)}) collective-permute-start(bf16[128,768]{1,0:T(8,128)(2,1)S(1)} %copy-done.12), channel_id=1, source_target_pairs={{0,3},{1,2},{2,1},{3,0},{4,7},{5,6},{6,5},{7,4},{8,11},{9,10},{10,... | collective-permute-start | bytes 589832 | tf_op jit(solution)/shard_map/ppermute | solution.py:52
  152.9 25.3 %copy-start.11 = (bf16[8,24,768]{2,1,0:T(8,128)(2,1)}, bf16[8,24,768]{2,1,0:T(8,128)(2,1)S(1)}, u32[]{:S(2)}) copy-start(bf16[8,24,768]{2,1,0:T(8,128)(2,1)S(1)} %all-to-all-done.3.returned_ref) | copy-start | bytes 884740
  152.9 15.0 %all-to-all-start.4 = ((bf16[4,2,384,128]{3,2,1,0:T(8,128)(2,1)}), bf16[4,2,384,128]{3,2,1,0:T(8,128)(2,1)S(1)}, u32[]{:S(2)}, u32[]{:S(2)}) async-start(bf16[4,2,384,128]{3,2,1,0:T(8,128)(2,1)} %get-tuple-element.173), calls=%async_computation.4 | async-start | bytes 1572864 | tf_op jit(solution)/shard_map/all_to_all | solution.py:755
  156.7 1.5 collective-permute-start.29
  159.1 4.4 %collective-permute-start.30 = (f32[24,768]{1,0:T(8,128)S(1)}, f32[24,768]{1,0:T(8,128)S(1)}, u32[]{:S(2)}, u32[]{:S(2)}) collective-permute-start(f32[24,768]{1,0:T(8,128)S(1)} %add.58), channel_id=1, source_target_pairs={{0,16},{8,24},{16,0},{24,8},{1,17},{9,25},{17,1},{25,9},{2,18},{10... | collective-permute-start | bytes 221192 | tf_op jit(solution)/shard_map/ppermute | solution.py:52
  163.5 4.4 %collective-permute-start.31 = (f32[24,768]{1,0:T(8,128)S(1)}, f32[24,768]{1,0:T(8,128)S(1)}, u32[]{:S(2)}, u32[]{:S(2)}) collective-permute-start(f32[24,768]{1,0:T(8,128)S(1)} %add.59), channel_id=1, source_target_pairs={{0,1},{1,0},{2,3},{3,2},{4,5},{5,4},{6,7},{7,6},{8,9},{9,8},{10,11... | collective-permute-start | bytes 221192 | tf_op jit(solution)/shard_map/ppermute | solution.py:52
  173.2 5.0 %collective-permute-start.32 = (bf16[2,192,384]{2,1,0:T(8,128)(2,1)}, bf16[2,192,384]{2,1,0:T(8,128)(2,1)S(1)}, u32[]{:S(2)}, u32[]{:S(2)}) collective-permute-start(bf16[2,192,384]{2,1,0:T(8,128)(2,1)} %get-tuple-element.185), channel_id=1, source_target_pairs={{0,8},{8,0},{16,24},{24,16},{1,9},{9,1},{17,25},{25,17},{2,10},{10... | collective-permute-start | bytes 884744 | tf_op jit(solution)/shard_map/ppermute | solution.py:52
  173.2 4.9 %collective-permute-start.34 = (f32[24,768]{1,0:T(8,128)S(1)}, f32[24,768]{1,0:T(8,128)S(1)}, u32[]{:S(2)}, u32[]{:S(2)}) collective-permute-start(f32[24,768]{1,0:T(8,128)S(1)} %add.60), channel_id=1, source_target_pairs={{0,2},{1,3},{2,0},{3,1},{4,6},{5,7},{6,4},{7,5},{8,10},{9,11},{10,... | collective-permute-start | bytes 221192 | tf_op jit(solution)/shard_map/ppermute | solution.py:52
  175.2 4.0 %collective-permute-start.33 = (bf16[2,192,384]{2,1,0:T(8,128)(2,1)}, bf16[2,192,384]{2,1,0:T(8,128)(2,1)S(1)}, u32[]{:S(2)}, u32[]{:S(2)}) collective-permute-start(bf16[2,192,384]{2,1,0:T(8,128)(2,1)} %get-tuple-element.187), channel_id=1, source_target_pairs={{0,8},{8,0},{16,24},{24,16},{1,9},{9,1},{17,25},{25,17},{2,10},{10... | collective-permute-start | bytes 884744 | tf_op jit(solution)/shard_map/ppermute | solution.py:52
  180.3 6.8 %collective-permute-start.36 = (f32[24,768]{1,0:T(8,128)S(1)}, f32[24,768]{1,0:T(8,128)S(1)}, u32[]{:S(2)}, u32[]{:S(2)}) collective-permute-start(f32[24,768]{1,0:T(8,128)S(1)} %add.63), channel_id=1, source_target_pairs={{0,4},{1,5},{2,6},{3,7},{4,0},{5,1},{6,2},{7,3},{8,12},{9,13},{10,... | collective-permute-start | bytes 221192 | tf_op jit(solution)/shard_map/ppermute | solution.py:52
  182.7 8.4 %collective-permute-start.35 = (bf16[2,192,384]{2,1,0:T(8,128)(2,1)S(1)}, bf16[2,192,384]{2,1,0:T(8,128)(2,1)S(1)}, u32[]{:S(2)}, u32[]{:S(2)}) collective-permute-start(bf16[2,192,384]{2,1,0:T(8,128)(2,1)S(1)} %add_convert_fusion), channel_id=1, source_target_pairs={{0,16},{8,24},{16,0},{24,8},{1,17},{9,25},{17,1},{25,9},{2,18},{10... | collective-permute-start | bytes 884744 | tf_op jit(solution)/shard_map/ppermute | solution.py:52
  191.2 8.5 %collective-permute-start.37 = (bf16[192,384]{1,0:T(8,128)(2,1)S(1)}, bf16[192,384]{1,0:T(8,128)(2,1)S(1)}, u32[]{:S(2)}, u32[]{:S(2)}) collective-permute-start(bf16[192,384]{1,0:T(8,128)(2,1)S(1)} %fusion), channel_id=1, source_target_pairs={{0,4},{1,5},{2,6},{3,7},{4,0},{5,1},{6,2},{7,3},{8,12},{9,13},{10,... | collective-permute-start | bytes 442376 | tf_op jit(solution)/shard_map/ppermute | solution.py:52
  (22 other events, 151.5 us)
